TPU v7x, 32 devices: a whole 2x2x4 slice. The times are simulated.
32 devices in a mesh: page: 4 (over z), row: 8 (over y, x, core).
Axes of the slice: x: 2, y: 2, z: 4, core: 2. Of those that a mesh axis runs over, the one named last changes fastest.
Arguments:
- qkv_rows: bfloat16 [4, 512, 3840], P('page', 'row'), may hold values from -12 to 12
- residual: bfloat16 [4, 512, 1280], P('page', 'row'), may hold values from -40 to 40
- out_weight: bfloat16 [1280, 1280], P('page'), may hold values from -0.15625 to 0.15625
- norm_gain: float32 [1280], replicated, may hold values from 0.1 to 1.9
- merge_weight: bfloat16 [5120, 5120], P('row'), may hold values from -0.078125 to 0.078125
- merge_bias: float32 [5120], P('row'), may hold values from -3 to 3
- page_grid: int32 [4, 2], P('page'), may hold values from 2 to 64, as said below
Outputs:
- merged: bfloat16 [4, 5120, 128], P('page', 'row')
Inputs may be any that keep to these rules, and one draw needn't show every extreme that they name: `page_grid`: rows and columns are even; rows times columns is at most 512, and one page of every draw has exactly 512 live patches in 64 rows of 8 columns; columns are at least 8.
All inputs are finite; a program needn't handle non-finite values.
Results may differ from a plain program's by a relative error of at most 0.0049.
Values may be sent and summed in bfloat16 or wider, within the bound.
No kernel may reach another device: no remote copies, remote signals or barrier semaphores. Data moves between devices by JAX's collectives and lax.ppermute only.
A program may use at most 64 MiB of HBM per device.

v0:
```python
import math

import jax
import jax.numpy as jnp
from jax import lax
from jax.sharding import PartitionSpec as P

D = 1280
HEADS = 16
HDIM = 80


def local(qkv_rows, residual, out_weight, norm_gain, merge_weight, merge_bias, page_grid):
    row_count = lax.axis_size("row")
    q_split = max(1, row_count // HEADS)
    head_groups = row_count // q_split
    width = D // head_groups
    heads_per = width // HDIM
    band_len = qkv_rows.shape[1]
    part_len = band_len // q_split
    local_qkv = qkv_rows[0]
    queries = local_qkv[:, :D]
    key_vals = jnp.concatenate(
        [
            local_qkv[:, D : 2 * D].reshape(band_len, head_groups, width),
            local_qkv[:, 2 * D :].reshape(band_len, head_groups, width),
        ],
        axis=2,
    )
    q_send = (
        queries.reshape(q_split, part_len, head_groups, width)
        .transpose(2, 0, 1, 3)
        .reshape(row_count, part_len, width)
    )
    kv_send = jnp.broadcast_to(
        key_vals.transpose(1, 0, 2)[:, None], (head_groups, q_split, band_len, 2 * width)
    )
    kv_send = kv_send.reshape(row_count, band_len, 2 * width)
    q_recv, kv_recv = (
        lax.all_to_all(q_send, "row", split_axis=0, concat_axis=1, tiled=True),
        lax.all_to_all(kv_send, "row", split_axis=0, concat_axis=1, tiled=True),
    )
    kv_local = kv_recv[0]
    positions = jnp.arange(row_count * band_len, dtype=jnp.int32)
    valid_len = page_grid[0, 0] * page_grid[0, 1]
    key_valid = positions < valid_len
    key_total = kv_local.shape[0]
    key_heads = kv_local[:, :width].reshape(key_total, heads_per, HDIM)
    value_heads = kv_local[:, width:].reshape(key_total, heads_per, HDIM)
    query_total = row_count * part_len
    q_block = math.gcd(query_total, 512)
    q_blocks = q_recv[0].reshape(query_total // q_block, q_block, heads_per, HDIM)
    root_dim = math.sqrt(HDIM)

    def attend(q_span):
        scores = (
            jnp.einsum("qhd,khd->hqk", q_span, key_heads, preferred_element_type=jnp.float32)
            / root_dim
        )
        scores = jnp.where(key_valid[None, None, :], scores, -1e30)
        peak = jnp.max(scores, axis=2, keepdims=True)
        weights = jnp.exp(scores - peak)
        total = jnp.sum(weights, axis=2, keepdims=True)
        mixed = (
            jnp.einsum(
                "hqk,khd->hqd",
                weights.astype(jnp.bfloat16),
                value_heads,
                preferred_element_type=jnp.float32,
            )
            / total
        )
        return mixed.transpose(1, 0, 2).reshape(q_span.shape[0], width).astype(jnp.bfloat16)

    attn_heads = lax.map(attend, q_blocks).reshape(row_count, part_len, width)
    returned = lax.all_to_all(attn_heads, "row", split_axis=0, concat_axis=0, tiled=True)
    attn = (
        returned.reshape(head_groups, q_split, part_len, width)
        .transpose(1, 2, 0, 3)
        .reshape(band_len, D)
    )
    projected = jnp.dot(
        attn,
        lax.all_gather(out_weight, "page", axis=0, tiled=True),
        preferred_element_type=jnp.float32,
    )
    hidden = residual[0].astype(jnp.float32) + projected
    normed = (
        hidden * lax.rsqrt(jnp.mean(hidden * hidden, axis=1, keepdims=True) + 1e-06) * norm_gain
    ).astype(jnp.bfloat16)
    rows_n = page_grid[0, 0]
    cols_n = page_grid[0, 1]
    group_total = band_len * row_count // 4
    slots = jnp.arange(group_total, dtype=jnp.int32)
    half_cols = cols_n // 2
    live = slots < rows_n // 2 * half_cols
    first = jnp.where(live, 2 * (slots // half_cols) * cols_n + 2 * (slots % half_cols), 0)
    corners = [first, first + 1, first + cols_n, first + cols_n + 1]
    local_units = merge_weight.shape[0]
    page_all = lax.all_gather(normed, "row", axis=0, tiled=True)
    merged_sum = jnp.zeros((local_units, group_total), jnp.float32)
    for corner in range(4):
        picked = jnp.take(page_all, corners[corner], axis=0)
        merged_sum = merged_sum + jnp.einsum(
            "md,gd->mg",
            merge_weight[:, corner * D : (corner + 1) * D],
            picked,
            preferred_element_type=jnp.float32,
        )
    merged = jax.nn.gelu(merged_sum + merge_bias[:, None], approximate=False)
    merged = jnp.where(live[None, :], merged, 0.0).astype(jnp.bfloat16)
    return merged[None]


def solution(mesh):
    in_specs = (
        P("page", "row", None),
        P("page", "row", None),
        P("page", None),
        P(),
        P("row", None),
        P("row"),
        P("page", None),
    )
    out_specs = P("page", "row", None)
    return jax.shard_map(local, mesh=mesh, in_specs=in_specs, out_specs=out_specs, check_vma=False)
```

profile of v0, /device:TPU:0, one launch (start us, length us, event | category | flops | bytes accessed | tf_op | source)
XLA Modules:
  0.0 126.4 jit_solution(13824696844920702895)
XLA Ops:
  6.5 0.7 all-gather.3.cloned.1.call-update
  7.3 1.1 fusion.77
  8.7 0.8 copy.32
  9.5 5.3 %all-to-all-start.1 = ((bf16[8,64,160]{2,1,0:T(8,128)(2,1)}), bf16[8,64,160]{2,1,0:T(8,128)(2,1)S(1)}, u32[]{:S(2)}, u32[]{:S(2)}) async-start(bf16[8,64,160]{2,1,0:T(8,128)(2,1)} %copy.32), calls=%async_computation.1 | async-start | bytes 524288 | tf_op jit(solution)/shard_map/all_to_all | solution.py:40
  15.6 0.9 maximum_bitcast_fusion
  16.5 5.2 %all-to-all-done.1 = bf16[8,64,160]{2,1,0:T(8,128)(2,1)S(1)} async-done(((bf16[8,64,160]{2,1,0:T(8,128)(2,1)}), bf16[8,64,160]{2,1,0:T(8,128)(2,1)S(1)}, u32[]{:S(2)}, u32[]{:S(2)}) %all-to-all-start.1) | async-done | bytes 163872 | tf_op jit(solution)/shard_map/all_to_all | solution.py:40
  21.7 3.5 %all-to-all-start = ((bf16[8,64,320]{2,1,0:T(8,128)(2,1)}), bf16[8,64,320]{2,1,0:T(8,128)(2,1)S(1)}, u32[]{:S(2)}, u32[]{:S(2)}) async-start(bf16[8,64,320]{2,1,0:T(8,128)(2,1)} %maximum_bitcast_fusion), calls=%async_computation | async-start | bytes 786432 | tf_op jit(solution)/shard_map/all_to_all | solution.py:41
  25.2 0.6 fusion.79
  27.4 6.1 %all-to-all-done = bf16[8,64,320]{2,1,0:T(8,128)(2,1)S(1)} async-done(((bf16[8,64,320]{2,1,0:T(8,128)(2,1)}), bf16[8,64,320]{2,1,0:T(8,128)(2,1)S(1)}, u32[]{:S(2)}, u32[]{:S(2)}) %all-to-all-start) | async-done | bytes 327712 | tf_op jit(solution)/shard_map/all_to_all | solution.py:41
  34.9 0.7 fusion.24
  36.1 9.3 %all_to_all.23 = bf16[8,64,160]{2,1,0:T(8,128)(2,1)S(1)} all-to-all(bf16[8,64,160]{2,1,0:T(8,128)(2,1)S(1)} %copy.36), channel_id=1, replica_groups=mesh['page'=4,'row'=8] {'row'}, dimensions={0} | all-to-all | bytes 327680 | tf_op jit(solution)/shard_map/all_to_all | solution.py:76
  45.8 31.5 %all-gather.3.cloned.1.call-done = bf16[1280,1280]{1,0:T(8,128)(2,1)} async-done(((bf16[320,1280]{1,0:T(8,128)(2,1)}), bf16[1280,1280]{1,0:T(8,128)(2,1)}) %all-gather.3.cloned.1.call-update) | async-done | bytes 3276816 | tf_op jit(solution)/shard_map/all_gather | solution.py:84
  77.3 2.7 %multiply_reduce_fusion = (f32[64]{0:T(128)S(1)}, f32[64,1280]{1,0:T(8,128)S(1)}) fusion(bf16[64,1280]{1,0:T(8,128)(2,1)S(1)} %reshape.73, bf16[1280,1280]{1,0:T(8,128)(2,1)} %all-gather.3.cloned.1.call-done, bf16[1,64,1280]{2,1,0:T(8,128)(2,1)S(1)} %copy-done.1), kind=kOutput, calls=%fused_computation.61 | convolution fusion | flops 210042816 | bytes 3932416 | tf_op jit(solution)/shard_map/dot_general | solution.py:82
  80.1 0.8 multiply_convert_fusion
  87.6 16.7 %all-gather.5.cloned.1.call-done = bf16[512,1280]{1,0:T(8,128)(2,1)} async-done(((bf16[64,1280]{1,0:T(8,128)(2,1)}), bf16[512,1280]{1,0:T(8,128)(2,1)}) %all-gather.5.cloned.1.call-update) | async-done | bytes 1310736 | tf_op jit(solution)/shard_map/all_gather | solution.py:100
  104.3 2.6 %gather_fusion.1 = bf16[128,1280]{1,0:T(8,128)(2,1)S(1)} fusion(bf16[512,1280]{1,0:T(8,128)(2,1)} %all-gather.5.cloned.1.call-done, s32[1024]{0:T(1024)S(1)} %pad_clamp_fusion.2), kind=kCustom, calls=%fused_computation.1.clone | custom fusion | bytes 655872 | tf_op jit(solution)/shard_map/jit(_take)/gather | solution.py:103
  106.9 2.2 %fusion.5 = f32[128,640]{1,0:T(8,128)S(1)} fusion(bf16[640,5120]{1,0:T(8,128)(2,1)} %param.13, bf16[128,1280]{1,0:T(8,128)(2,1)S(1)} %gather_fusion.1, pred[128]{0:T(512)(128)(4,1)S(1)} %get-tuple-element.24), kind=kOutput, calls=%fused_computation.13 | convolution fusion | flops 209879040 | bytes 2293888 | tf_op jit(solution)/shard_map/md,gd->mg/dot_general | solution.py:104
  109.1 0.9 gather_fusion.2
  110.0 2.1 %fusion.3 = f32[128,640]{1,0:T(8,128)S(1)} fusion(bf16[640,5120]{1,0:T(8,128)(2,1)} %param.13, bf16[128,1280]{1,0:T(8,128)(2,1)S(1)} %gather_fusion.2, pred[128]{0:T(512)(128)(4,1)S(1)} %get-tuple-element.39), kind=kOutput, calls=%fused_computation.11 | convolution fusion | flops 209879040 | bytes 2293888 | tf_op jit(solution)/shard_map/md,gd->mg/dot_general | solution.py:104
  112.1 0.9 gather_fusion.3
  113.0 2.1 %fusion.1 = f32[128,640]{1,0:T(8,128)S(1)} fusion(bf16[640,5120]{1,0:T(8,128)(2,1)} %param.13, bf16[128,1280]{1,0:T(8,128)(2,1)S(1)} %gather_fusion.3, pred[128]{0:T(512)(128)(4,1)S(1)} %get-tuple-element.37), kind=kOutput, calls=%fused_computation.9 | convolution fusion | flops 209879040 | bytes 2293888 | tf_op jit(solution)/shard_map/md,gd->mg/dot_general | solution.py:104
  115.1 0.9 gather_fusion
  116.0 2.8 %fusion.56 = bf16[1,640,128]{1,2,0:T(8,128)(2,1)S(1)} fusion(f32[128,640]{1,0:T(8,128)S(1)} %fusion.1, f32[128,640]{1,0:T(8,128)S(1)} %fusion.3, f32[128,640]{1,0:T(8,128)S(1)} %fusion.5, bf16[640,5120]{1,0:T(8,128)(2,1)} %param.13, bf16[128,1280]{1,0:T(8,128)(2,1)S(1)} %gather_fusion, pred[128]{0:T(512)(128)(4,1)S(1)} %get-tuple-element.16, ...), kind=kOutput, calls=%fused_computation.59 | convolution fusion | flops 215613440 | bytes 3115776 | tf_op jit(solution)/shard_map/md,gd->mg/dot_general | solution.py:104
  118.8 0.8 copy.38
  (37 shorter events, 4.4 us)
Async XLA Ops:
  6.5 70.8 %all-gather.3.cloned.1.call-start = ((), (), s32[]{:S(2)}) async-start(), calls=%async_computation.3 | async-start | bytes 4096000 | tf_op jit(solution)/shard_map/all_gather | solution.py:84
  9.5 15.8 %copy-start.3 = (s32[1,2]{1,0:T(1,128)S(1)}, s32[1,2]{1,0:T(1,128)}, u32[]{:S(2)}) copy-start(s32[1,2]{1,0:T(1,128)} %param.15) | copy-start | bytes 28
  9.5 12.2 %all-to-all-start.1 = ((bf16[8,64,160]{2,1,0:T(8,128)(2,1)}), bf16[8,64,160]{2,1,0:T(8,128)(2,1)S(1)}, u32[]{:S(2)}, u32[]{:S(2)}) async-start(bf16[8,64,160]{2,1,0:T(8,128)(2,1)} %copy.32), calls=%async_computation.1 | async-start | bytes 524288 | tf_op jit(solution)/shard_map/all_to_all | solution.py:40
  21.7 11.7 %all-to-all-start = ((bf16[8,64,320]{2,1,0:T(8,128)(2,1)}), bf16[8,64,320]{2,1,0:T(8,128)(2,1)S(1)}, u32[]{:S(2)}, u32[]{:S(2)}) async-start(bf16[8,64,320]{2,1,0:T(8,128)(2,1)} %maximum_bitcast_fusion), calls=%async_computation | async-start | bytes 786432 | tf_op jit(solution)/shard_map/all_to_all | solution.py:41
  25.2 79.1 %all-gather.5.cloned.1.call-start = ((), (), s32[]{:S(2)}) async-start(), calls=%async_computation.4 | async-start | bytes 1474560 | tf_op jit(solution)/shard_map/all_gather | solution.py:100
  35.6 41.7 %copy-start.1 = (bf16[1,64,1280]{2,1,0:T(8,128)(2,1)S(1)}, bf16[1,64,1280]{2,1,0:T(8,128)(2,1)}, u32[]{:S(2)}) copy-start(bf16[1,64,1280]{2,1,0:T(8,128)(2,1)} %param.10) | copy-start | bytes 491524
  45.6 34.5 %copy-start.2 = (f32[1280]{0:T(1024)S(1)}, f32[1280]{0:T(1024)}, u32[]{:S(2)}) copy-start(f32[1280]{0:T(1024)} %param.12) | copy-start | bytes 15364
  106.9 2.2 %copy-start = (bf16[512,1280]{1,0:T(8,128)(2,1)S(1)}, bf16[512,1280]{1,0:T(8,128)(2,1)}, u32[]{:S(2)}) copy-start(bf16[512,1280]{1,0:T(8,128)(2,1)} %all-gather.5.cloned.1.call-done) | copy-start | bytes 3932164
  115.0 0.9 copy-start.4
Sparse Core Ops, SparseCore 0:
  8.9 68.3 all-gather.2
  81.0 23.2 all-gather.4
where the time goes:
time: 127 us; the launch traced here: 126 us
  waiting for transfers between devices  60.2 us (47%)
  between operations  20.8 us (16%)
  matrix products  13.1 us (10%)
  local copies, waits for them, and re-layouts  11.1 us (9%)
  blocking collectives  9.35 us (7%)
  starting transfers between devices  8.8 us (7%)
  other arithmetic  2.98 us (2%)
    all_gather x1, waiting for transfers between devices, local(): lax.all_gather(out_weight, 'page', axis=0, tiled=True)  31.5 us
    all_gather x1, waiting for transfers between devices, local(): page_all = lax.all_gather(normed, 'row', axis=0, tiled=True)  16.7 us
    all_to_all x1, blocking collectives, local(): lax.all_to_all(attn_heads, 'row', split_axis=0, concat_axis=0, tiled=True)  9.35 us
    dot_general x4, matrix products, local(): jnp.einsum('md,gd->mg', merge_weight[:, corner * D:(corner + 1) * D], pic...  9.11 us
    all_to_all x1, waiting for transfers between devices, local(): lax.all_to_all(kv_send, 'row', split_axis=0, concat_axis=1, tiled=True)  6.08 us
    gather x4, local copies, waits for them, and re-layouts, local(): picked = jnp.take(page_all, corners[corner], axis=0)  5.3 us
    all_to_all x1, starting transfers between devices, local(): lax.all_to_all(q_send, 'row', split_axis=0, concat_axis=1, tiled=True)  5.3 us
    all_to_all x1, waiting for transfers between devices, local(): lax.all_to_all(q_send, 'row', split_axis=0, concat_axis=1, tiled=True)  5.22 us
  transfers between devices with their start and end apart: 4, of which 4 were waited for; matrix products, arithmetic and copies ran while one was open for 7% of the time, Pallas kernels for 0%

commit v1 on v0

--- a/solution.py
+++ b/solution.py
@@ -1,8 +1,11 @@
+import functools
 import math
 
 import jax
 import jax.numpy as jnp
 from jax import lax
+from jax.experimental import pallas as pl
+from jax.experimental.pallas import tpu as pltpu
 from jax.sharding import PartitionSpec as P
 
 D = 1280
@@ -10,7 +13,7 @@
 HDIM = 80
 
 
-def local(qkv_rows, residual, out_weight, norm_gain, merge_weight, merge_bias, page_grid):
+def local_any(qkv_rows, residual, out_weight, norm_gain, merge_weight, merge_bias, page_grid):
     row_count = lax.axis_size("row")
     q_split = max(1, row_count // HEADS)
     head_groups = row_count // q_split
@@ -112,6 +115,248 @@
     return merged[None]
 
 
+ROWS = 8
+PAGES = 4
+HPAIR = 2 * HDIM
+KEEP = 128
+REST = HPAIR - KEEP
+
+
+def vmem(count):
+    return [pl.BlockSpec(memory_space=pltpu.VMEM)] * count
+
+
+def row_index():
+    return lax.axis_index("row")
+
+
+def spread_kernel(qkv_ref, *rest):
+    outs, held = rest[:ROWS], rest[ROWS]
+    me = row_index()
+    for dest in range(ROWS):
+        for part in range(3):
+            at = part * D + dest * HPAIR
+            held[dest, :, part * HPAIR : (part + 1) * HPAIR] = qkv_ref[0, :, at : at + HPAIR]
+    for step in range(ROWS):
+        outs[step][...] = held[me ^ step]
+
+
+def corner_rows(grid_ref, groups, corner):
+    rows_n, cols_n = grid_ref[0, 0], grid_ref[0, 1]
+    half = cols_n // 2
+    slots = lax.broadcasted_iota(jnp.int32, (groups, 1), 0)
+    line = jnp.floor((slots.astype(jnp.float32) + 0.5) / half.astype(jnp.float32)).astype(jnp.int32)
+    first = 2 * line * cols_n + 2 * (slots - line * half)
+    picked = first + (corner // 2) * cols_n + corner % 2
+    return jnp.where(slots < (rows_n // 2) * half, picked, -1)
+
+
+def select_rows(grid_ref, patches):
+    groups = patches // 4
+    wanted = jnp.concatenate([corner_rows(grid_ref, groups, corner) for corner in range(4)], axis=0)
+    at = lax.broadcasted_iota(jnp.int32, (patches, patches), 1)
+    return jnp.where(at == wanted, 1.0, 0.0).astype(jnp.bfloat16)
+
+
+def attend_kernel(grid_ref, *rest):
+    blocks = rest[:ROWS]
+    out_ref, q_all, k_all, v_all = rest[ROWS:]
+    me = row_index()
+    band = blocks[0].shape[0]
+    patches = band * ROWS
+    for step in range(ROWS):
+        at = pl.ds(pl.multiple_of((me ^ step) * band, band), band)
+        q_all[at, :] = blocks[step][:, :HPAIR]
+        k_all[at, :] = blocks[step][:, HPAIR : 2 * HPAIR]
+        v_all[at, :] = blocks[step][:, 2 * HPAIR :]
+    select = select_rows(grid_ref, patches)
+    queries = jnp.dot(select, q_all[...], preferred_element_type=jnp.float32).astype(jnp.bfloat16)
+    lane = lax.broadcasted_iota(jnp.int32, (1, HPAIR), 1)
+    live = lax.broadcasted_iota(jnp.int32, (1, patches), 1) < grid_ref[0, 0] * grid_ref[0, 1]
+    keys, values = k_all[...], v_all[...]
+    mixed = []
+    for head in range(2):
+        mine = (lane >= head * HDIM) & (lane < (head + 1) * HDIM)
+        asked = jnp.where(mine, queries, jnp.zeros_like(queries))
+        scores = lax.dot_general(asked, keys, (((1,), (1,)), ((), ())), preferred_element_type=jnp.float32)
+        scores = jnp.where(live, scores * (1.0 / math.sqrt(HDIM)), -1e30)
+        weights = jnp.exp(scores - jnp.max(scores, axis=1, keepdims=True))
+        total = jnp.sum(weights, axis=1, keepdims=True)
+        mixed.append(
+            jnp.dot(weights.astype(jnp.bfloat16), values, preferred_element_type=jnp.float32) / total
+        )
+    attn = jnp.where(lane < HDIM, mixed[0], mixed[1])
+    out_ref[:patches, :] = attn[:, :KEEP].astype(jnp.bfloat16)
+    groups = patches // 4
+    tail = [attn[corner * groups : (corner + 1) * groups, KEEP:] for corner in range(4)]
+    out_ref[patches:, :] = jnp.concatenate(tail, axis=1).astype(jnp.bfloat16)
+
+
+def residual_kernel(grid_ref, *rest):
+    blocks = rest[:ROWS]
+    out_ref, held = rest[ROWS:]
+    me = row_index()
+    band = blocks[0].shape[0]
+    for step in range(ROWS):
+        held[pl.ds(pl.multiple_of((me ^ step) * band, band), band), :] = blocks[step][...]
+    select = select_rows(grid_ref, band * ROWS)
+    out_ref[...] = jnp.dot(select, held[...], preferred_element_type=jnp.float32).astype(jnp.bfloat16)
+
+
+def weight_kernel(own_ref, *rest):
+    mine, theirs = rest[: PAGES - 1], rest[PAGES - 1 : 2 * PAGES - 2]
+    out_ref = rest[-1]
+    page, core = lax.axis_index("page"), row_index() % 2
+
+    def place(pair, block):
+        out_ref[pl.ds(pl.multiple_of(pair * KEEP, KEEP), KEEP), :] = block[:KEEP]
+        out_ref[pl.ds(pl.multiple_of(ROWS * KEEP + pair * REST, REST), REST), :] = block[KEEP:]
+
+    place(2 * page, own_ref[:HPAIR])
+    place(2 * page + 1, own_ref[HPAIR:])
+    for step in range(1, PAGES):
+        source = lax.rem(page + PAGES - step, PAGES)
+        place(2 * source + core, mine[step - 1][...])
+        place(2 * source + 1 - core, theirs[step - 1][...])
+
+
+def merge_kernel(grid_ref, *rest):
+    pieces = rest[:ROWS]
+    resid_ref, proj_ref, gain_ref, weight_hbm, bias_ref, out_ref, attn, hidden, weight, sem = rest[ROWS:]
+    fetch = pltpu.make_async_copy(weight_hbm, weight, sem)
+    fetch.start()
+    me = row_index()
+    patches = attn.shape[0]
+    groups = patches // 4
+    for step in range(ROWS):
+        pair = me ^ step
+        attn[:, pl.ds(pl.multiple_of(pair * KEEP, KEEP), KEEP)] = pieces[step][:patches]
+    lane = lax.broadcasted_iota(jnp.int32, (1, KEEP), 1) // REST
+    for half in range(2):
+        tails = []
+        for corner in range(4):
+            total = jnp.zeros((groups, KEEP), jnp.float32)
+            for step in range(ROWS):
+                pair = me ^ step
+                tail = pieces[step][patches:].astype(jnp.float32)
+                shift = lax.rem((pair + 4 - corner) * REST, KEEP)
+                turned = pltpu.roll(tail, shift, axis=1)
+                total = jnp.where((lane == lax.rem(pair, 4)) & (pair // 4 == half), turned, total)
+            tails.append(total.astype(jnp.bfloat16))
+        attn[:, ROWS * KEEP + half * KEEP : ROWS * KEEP + (half + 1) * KEEP] = jnp.concatenate(tails, axis=0)
+    squares = jnp.zeros((patches, 1), jnp.float32)
+    cols = 256
+    for at in range(0, D, cols):
+        part = jnp.dot(attn[...], proj_ref[:, at : at + cols], preferred_element_type=jnp.float32)
+        part = part + resid_ref[:, at : at + cols].astype(jnp.float32)
+        hidden[:, at : at + cols] = part
+        squares = squares + jnp.sum(part * part, axis=1, keepdims=True)
+    scale = lax.rsqrt(squares * (1.0 / D) + 1e-06)
+    fetch.wait()
+    total = jnp.zeros((weight.shape[0], groups), jnp.float32)
+    for corner in range(4):
+        span = slice(corner * groups, (corner + 1) * groups)
+        normed = (hidden[span, :] * scale[span] * gain_ref[...]).astype(jnp.bfloat16)
+        total = total + lax.dot_general(
+            weight[:, corner * D : (corner + 1) * D], normed, (((1,), (1,)), ((), ())), preferred_element_type=jnp.float32
+        )
+    total = total + bias_ref[...]
+    merged = 0.5 * total * (1.0 + lax.erf(total * math.sqrt(0.5)))
+    live = lax.broadcasted_iota(jnp.int32, (1, groups), 1) < (grid_ref[0, 0] // 2) * (grid_ref[0, 1] // 2)
+    out_ref[0] = jnp.where(live, merged, 0.0).astype(jnp.bfloat16)
+
+
+def params():
+    return pltpu.CompilerParams(vmem_limit_bytes=40 * 1024 * 1024)
+
+
+def cost(flops, moved):
+    return pl.CostEstimate(flops=flops, bytes_accessed=moved, transcendentals=0)
+
+
+def swap(value, step):
+    return lax.ppermute(value, "row", [(row, row ^ step) for row in range(ROWS)])
+
+
+def gather_rows(value):
+    far = [swap(value, step) for step in (2, 4, 6)]
+    near = [swap(piece, 1) for piece in [value] + far]
+    return [value, near[0], far[0], near[1], far[1], near[2], far[2], near[3]]
+
+
+def local_eight(qkv_rows, residual, out_weight, norm_gain, merge_weight, merge_bias, page_grid):
+    band = qkv_rows.shape[1]
+    patches = band * ROWS
+    units = merge_weight.shape[0]
+    smem = pl.BlockSpec(memory_space=pltpu.SMEM)
+    bf16, f32 = jnp.bfloat16, jnp.float32
+
+    core = row_index() % 2
+    moving = lax.dynamic_slice_in_dim(out_weight, core * HPAIR, HPAIR, 0)
+    mine = []
+    for _ in range(PAGES - 1):
+        moving = lax.ppermute(moving, "page", [(page, (page + 1) % PAGES) for page in range(PAGES)])
+        mine.append(moving)
+    theirs = [swap(piece, 1) for piece in mine]
+
+    sends = pl.pallas_call(
+        spread_kernel,
+        out_shape=[jax.ShapeDtypeStruct((band, 3 * HPAIR), bf16)] * ROWS,
+        in_specs=vmem(1),
+        out_specs=vmem(ROWS),
+        scratch_shapes=[pltpu.VMEM((ROWS, band, 3 * HPAIR), bf16)],
+        compiler_params=params(),
+        name="spread",
+    )(qkv_rows)
+    blocks = [sends[0]] + [swap(sends[step], step) for step in range(1, ROWS)]
+    attn = pl.pallas_call(
+        attend_kernel,
+        out_shape=jax.ShapeDtypeStruct((patches + patches // 4, KEEP), bf16),
+        in_specs=[smem] + vmem(ROWS),
+        out_specs=pl.BlockSpec(memory_space=pltpu.VMEM),
+        scratch_shapes=[pltpu.VMEM((patches, HPAIR), bf16)] * 3,
+        compiler_params=params(),
+        cost_estimate=cost(6 * patches * patches * 256, 1 << 20),
+        name="attend",
+    )(page_grid, *blocks)
+    resid = pl.pallas_call(
+        residual_kernel,
+        out_shape=jax.ShapeDtypeStruct((patches, D), bf16),
+        in_specs=[smem] + vmem(ROWS),
+        out_specs=pl.BlockSpec(memory_space=pltpu.VMEM),
+        scratch_shapes=[pltpu.VMEM((patches, D), bf16)],
+        compiler_params=params(),
+        cost_estimate=cost(2 * patches * patches * D, 4 * patches * D),
+        name="residual_rows",
+    )(page_grid, *gather_rows(residual[0]))
+    proj = pl.pallas_call(
+        weight_kernel,
+        out_shape=jax.ShapeDtypeStruct((D, D), bf16),
+        in_specs=vmem(2 * PAGES - 1),
+        out_specs=pl.BlockSpec(memory_space=pltpu.VMEM),
+        compiler_params=params(),
+        cost_estimate=cost(0, 4 * D * D),
+        name="projection_rows",
+    )(out_weight, *mine, *theirs)
+    pieces = gather_rows(attn)
+    merged = pl.pallas_call(
+        merge_kernel,
+        out_shape=jax.ShapeDtypeStruct((1, units, patches // 4), bf16),
+        in_specs=[smem] + vmem(ROWS + 3) + [pl.BlockSpec(memory_space=pl.ANY)] + vmem(1),
+        out_specs=pl.BlockSpec(memory_space=pltpu.VMEM),
+        scratch_shapes=[
+            pltpu.VMEM((patches, D), bf16),
+            pltpu.VMEM((patches, D), f32),
+            pltpu.VMEM((units, 4 * D), bf16),
+            pltpu.SemaphoreType.DMA,
+        ],
+        compiler_params=params(),
+        cost_estimate=cost(2 * patches * D * (D + units), 16 << 20),
+        name="merge",
+    )(page_grid, *pieces, resid, proj, norm_gain.reshape(1, D), merge_weight, merge_bias.reshape(units, 1))
+    return merged
+
+
 def solution(mesh):
     in_specs = (
         P("page", "row", None),
@@ -123,4 +368,5 @@
         P("page", None),
     )
     out_specs = P("page", "row", None)
+    local = local_eight if mesh.shape["row"] == 8 and mesh.shape["page"] == 4 else local_any
     return jax.shard_map(local, mesh=mesh, in_specs=in_specs, out_specs=out_specs, check_vma=False)

time: 127 us -> 71.4 us (0.56)
  waiting for transfers between devices: 60.2 us -> 33 us
  between operations: 20.8 us -> 0.17 us
  matrix products: 13.1 us -> 0 us
  Pallas kernels: 0 us -> 10.4 us
  starting transfers between devices: 8.8 us -> 19.1 us
  blocking collectives: 9.35 us -> 0 us
  other arithmetic: 2.98 us -> 0 us
  local copies, waits for them, and re-layouts: 11.1 us -> 8.43 us
    all_gather x2 -> x0, waiting for transfers between devices: 48.2 us -> none  [the longest x1 31.5 us: local(): lax.all_gather(out_weight, 'page', axis=0, tiled=True)]
    ppermute x0 -> x27, waiting for transfers between devices: none -> 33 us  [the longest x24 18.4 us: swap(): lax.ppermute(value, 'row', [(row, row ^ step) for row in range(ROWS)])]
    ppermute x0 -> x27, starting transfers between devices: none -> 19.1 us  [the longest x24 16 us: swap(): lax.ppermute(value, 'row', [(row, row ^ step) for row in range(ROWS)])]
    dot_general x7 -> x0, matrix products: 13.1 us -> none  [the longest x4 9.11 us: local(): jnp.einsum('md,gd->mg', merge_weight[:, corner * D:(corner + 1) * D], pic...]
    all_to_all x2 -> x0, waiting for transfers between devices: 11.3 us -> none  [the longest x1 6.08 us: local(): lax.all_to_all(kv_send, 'row', split_axis=0, concat_axis=1, tiled=True)]
    pallas_call x0 -> x5, Pallas kernels: none -> 10.4 us  [the longest x1 6.36 us: local_eight(): pl.pallas_call(merge_kernel, out_shape=jax.ShapeDtypeStruct((1, units, pa...]
    all_to_all x1 -> x0, blocking collectives: 9.35 us -> none  [local(): lax.all_to_all(attn_heads, 'row', split_axis=0, concat_axis=0, tiled=True)]
    all_to_all x2 -> x0, starting transfers between devices: 8.75 us -> none  [the longest x1 5.3 us: local(): lax.all_to_all(q_send, 'row', split_axis=0, concat_axis=1, tiled=True)]
  transfers between devices with their start and end apart: 4 -> 27, of which waited for: 4 -> 8; matrix products, arithmetic and copies ran while one was open for 7% -> 2% of each run, Pallas kernels for 0% -> 6%
where the time goes in v1:
time: 71.4 us; the launch traced here: 71 us
  waiting for transfers between devices  33 us (46%)
  starting transfers between devices  19.1 us (27%)
  Pallas kernels  10.4 us (15%)
  local copies, waits for them, and re-layouts  8.43 us (12%)
    ppermute x24, waiting for transfers between devices, swap(): lax.ppermute(value, 'row', [(row, row ^ step) for row in range(ROWS)])  18.4 us
    ppermute x24, starting transfers between devices, swap(): lax.ppermute(value, 'row', [(row, row ^ step) for row in range(ROWS)])  16 us
    ppermute x3, waiting for transfers between devices, local_eight(): lax.ppermute(moving, 'page', [(page, (page + 1) % PAGES) for page in rang...  14.6 us
    pallas_call x1, Pallas kernels, local_eight(): pl.pallas_call(merge_kernel, out_shape=jax.ShapeDtypeStruct((1, units, pa...  6.36 us
    unnamed x12, local copies, waits for them, and re-layouts  5.79 us
    ppermute x3, starting transfers between devices, local_eight(): lax.ppermute(moving, 'page', [(page, (page + 1) % PAGES) for page in rang...  3.08 us
    pallas_call x1, Pallas kernels, local_eight(): pl.pallas_call(attend_kernel, out_shape=jax.ShapeDtypeStruct((patches + p...  2.03 us
    pallas_call x1, Pallas kernels, local_eight(): pl.pallas_call(residual_kernel, out_shape=jax.ShapeDtypeStruct((patches,...  1.5 us
  transfers between devices with their start and end apart: 27, of which 8 were waited for; matrix products, arithmetic and copies ran while one was open for 2% of the time, Pallas kernels for 6%

profile of v1, /device:TPU:0, one launch (start us, length us, event | category | flops | bytes accessed | tf_op | source)
XLA Modules:
  0.0 71.0 jit_solution(13934544830635166476)
XLA Ops:
  0.0 1.1 %constant_dynamic-slice_fusion = bf16[160,1280]{1,0:T(8,128)(2,1)S(1)} fusion(bf16[320,1280]{1,0:T(8,128)(2,1)} %own_ref.1, s32[]{:T(128)S(6)} %select_n.11), kind=kLoop, calls=%fused_computation | loop fusion | bytes 819204 | tf_op jit(solution)/shard_map/dynamic_slice | solution.py:295
  1.1 3.1 %collective-permute-start.21 = (bf16[160,1280]{1,0:T(8,128)(2,1)S(1)}, bf16[160,1280]{1,0:T(8,128)(2,1)S(1)}, u32[]{:S(2)}, u32[]{:S(2)}) collective-permute-start(bf16[160,1280]{1,0:T(8,128)(2,1)S(1)} %constant_dynamic-slice_fusion), channel_id=1, source_target_pairs={{0,8},{8,16},{16,24},{24,0},{1,9},{9,17},{17,25},{25,1},{2,10},{10... | collective-permute-start | bytes 1228808 | tf_op jit(solution)/shard_map/ppermute | solution.py:298
  4.2 11.5 %collective-permute-done.21.rest_0_ = bf16[160,1280]{1,0:T(8,128)(2,1)S(1)} collective-permute-done((bf16[160,1280]{1,0:T(8,128)(2,1)S(1)}, bf16[160,1280]{1,0:T(8,128)(2,1)S(1)}, u32[]{:S(2)}, u32[]{:S(2)}) %collective-permute-start.21) | collective-permute-done | bytes 409632 | tf_op jit(solution)/shard_map/ppermute | solution.py:298
  15.7 1.0 %copy-done.2 = bf16[1,64,3840]{2,1,0:T(8,128)(2,1)S(1)} copy-done((bf16[1,64,3840]{2,1,0:T(8,128)(2,1)S(1)}, bf16[1,64,3840]{2,1,0:T(8,128)(2,1)}, u32[]{:S(2)}) %copy-start.2) | copy-done | bytes 491544
  17.0 1.6 %collective-permute-start.1 = (bf16[64,480]{1,0:T(8,128)(2,1)S(1)}, bf16[64,480]{1,0:T(8,128)(2,1)S(1)}, u32[]{:S(2)}, u32[]{:S(2)}) collective-permute-start(bf16[64,480]{1,0:T(8,128)(2,1)S(1)} %get-tuple-element.15), channel_id=1, source_target_pairs={{0,2},{1,3},{2,0},{3,1},{4,6},{5,7},{6,4},{7,5},{8,10},{9,11},{10,... | collective-permute-start | bytes 184328 | tf_op jit(solution)/shard_map/ppermute | solution.py:278
  18.9 1.5 %collective-permute-start.3 = (bf16[64,480]{1,0:T(8,128)(2,1)S(1)}, bf16[64,480]{1,0:T(8,128)(2,1)S(1)}, u32[]{:S(2)}, u32[]{:S(2)}) collective-permute-start(bf16[64,480]{1,0:T(8,128)(2,1)S(1)} %get-tuple-element.17), channel_id=1, source_target_pairs={{0,4},{1,5},{2,6},{3,7},{4,0},{5,1},{6,2},{7,3},{8,12},{9,13},{10,... | collective-permute-start | bytes 184328 | tf_op jit(solution)/shard_map/ppermute | solution.py:278
  20.6 0.9 %collective-permute-done.1.rest_2_ = bf16[64,480]{1,0:T(8,128)(2,1)S(1)} collective-permute-done((bf16[64,480]{1,0:T(8,128)(2,1)S(1)}, bf16[64,480]{1,0:T(8,128)(2,1)S(1)}, u32[]{:S(2)}, u32[]{:S(2)}) %collective-permute-start.1) | collective-permute-done | bytes 61472 | tf_op jit(solution)/shard_map/ppermute | solution.py:278
  21.6 1.9 %collective-permute-start.15 = (bf16[64,1280]{1,0:T(8,128)(2,1)}, bf16[64,1280]{1,0:T(8,128)(2,1)S(1)}, u32[]{:S(2)}, u32[]{:S(2)}) collective-permute-start(bf16[64,1280]{1,0:T(8,128)(2,1)} %bitcast.1), channel_id=1, source_target_pairs={{0,2},{1,3},{2,0},{3,1},{4,6},{5,7},{6,4},{7,5},{8,10},{9,11},{10,... | collective-permute-start | bytes 491528 | tf_op jit(solution)/shard_map/ppermute | solution.py:278
  23.5 1.5 %collective-permute-start.17 = (bf16[64,1280]{1,0:T(8,128)(2,1)}, bf16[64,1280]{1,0:T(8,128)(2,1)S(1)}, u32[]{:S(2)}, u32[]{:S(2)}) collective-permute-start(bf16[64,1280]{1,0:T(8,128)(2,1)} %bitcast.2), channel_id=1, source_target_pairs={{0,4},{1,5},{2,6},{3,7},{4,0},{5,1},{6,2},{7,3},{8,12},{9,13},{10,... | collective-permute-start | bytes 491528 | tf_op jit(solution)/shard_map/ppermute | solution.py:278
  25.0 3.1 %collective-permute-done.22.rest_1_ = bf16[160,1280]{1,0:T(8,128)(2,1)S(1)} collective-permute-done((bf16[160,1280]{1,0:T(8,128)(2,1)S(1)}, bf16[160,1280]{1,0:T(8,128)(2,1)S(1)}, u32[]{:S(2)}, u32[]{:S(2)}) %collective-permute-start.22) | collective-permute-done | bytes 409632 | tf_op jit(solution)/shard_map/ppermute | solution.py:298
  28.1 2.2 %collective-permute-start.5 = (bf16[64,480]{1,0:T(8,128)(2,1)S(1)}, bf16[64,480]{1,0:T(8,128)(2,1)S(1)}, u32[]{:S(2)}, u32[]{:S(2)}) collective-permute-start(bf16[64,480]{1,0:T(8,128)(2,1)S(1)} %get-tuple-element.19), channel_id=1, source_target_pairs={{0,6},{1,7},{2,4},{3,5},{4,2},{5,3},{6,0},{7,1},{8,14},{9,15},{10,... | collective-permute-start | bytes 184328 | tf_op jit(solution)/shard_map/ppermute | solution.py:278
  30.3 3.0 %collective-permute-done.5.rest_6_ = bf16[64,480]{1,0:T(8,128)(2,1)S(1)} collective-permute-done((bf16[64,480]{1,0:T(8,128)(2,1)S(1)}, bf16[64,480]{1,0:T(8,128)(2,1)S(1)}, u32[]{:S(2)}, u32[]{:S(2)}) %collective-permute-start.5) | collective-permute-done | bytes 61472 | tf_op jit(solution)/shard_map/ppermute | solution.py:278
  33.3 2.7 %collective-permute-start.19 = (bf16[64,1280]{1,0:T(8,128)(2,1)}, bf16[64,1280]{1,0:T(8,128)(2,1)S(1)}, u32[]{:S(2)}, u32[]{:S(2)}) collective-permute-start(bf16[64,1280]{1,0:T(8,128)(2,1)} %bitcast.3), channel_id=1, source_target_pairs={{0,6},{1,7},{2,4},{3,5},{4,2},{5,3},{6,0},{7,1},{8,14},{9,15},{10,... | collective-permute-start | bytes 491528 | tf_op jit(solution)/shard_map/ppermute | solution.py:278
  36.7 2.0 %attend.1.rest_0_ = bf16[640,128]{1,0:T(8,128)(2,1)S(1)} custom-call(s32[1,2]{1,0:T(1,128)S(1)} %copy-done.4, bf16[64,480]{1,0:T(8,128)(2,1)S(1)} %get-tuple-element.13.rest_0_, bf16[64,480]{1,0:T(8,128)(2,1)S(1)} %collective-permute-done.rest_1_, bf16[64,480]{1,0:T(8,128)(2,1)S(1)} %collective-permute-done.1.rest_2_, ...), custom_call_target="tpu_custom_call" | custom-call | flops 402653184 | bytes 1048576 | tf_op jit(solution)/shard_map/attend/pallas_call | solution.py:312
  38.8 1.4 %collective-permute-start.12 = (bf16[640,128]{1,0:T(8,128)(2,1)S(1)}, bf16[640,128]{1,0:T(8,128)(2,1)S(1)}, u32[]{:S(2)}, u32[]{:S(2)}) collective-permute-start(bf16[640,128]{1,0:T(8,128)(2,1)S(1)} %attend.1.rest_0_), channel_id=1, source_target_pairs={{0,6},{1,7},{2,4},{3,5},{4,2},{5,3},{6,0},{7,1},{8,14},{9,15},{10,... | collective-permute-start | bytes 491528 | tf_op jit(solution)/shard_map/ppermute | solution.py:278
  40.8 8.1 %collective-permute-done.10.rest_4_ = bf16[640,128]{1,0:T(8,128)(2,1)S(1)} collective-permute-done((bf16[640,128]{1,0:T(8,128)(2,1)S(1)}, bf16[640,128]{1,0:T(8,128)(2,1)S(1)}, u32[]{:S(2)}, u32[]{:S(2)}) %collective-permute-start.10) | collective-permute-done | bytes 163872 | tf_op jit(solution)/shard_map/ppermute | solution.py:278
  49.5 5.3 %collective-permute-done.8.rest_2_ = bf16[640,128]{1,0:T(8,128)(2,1)S(1)} collective-permute-done((bf16[640,128]{1,0:T(8,128)(2,1)S(1)}, bf16[640,128]{1,0:T(8,128)(2,1)S(1)}, u32[]{:S(2)}, u32[]{:S(2)}) %collective-permute-start.8) | collective-permute-done | bytes 163872 | tf_op jit(solution)/shard_map/ppermute | solution.py:278
  55.3 0.9 %collective-permute-done.18.rest_5_ = bf16[64,1280]{1,0:T(8,128)(2,1)S(1)} collective-permute-done((bf16[64,1280]{1,0:T(8,128)(2,1)S(1)}, bf16[64,1280]{1,0:T(8,128)(2,1)S(1)}, u32[]{:S(2)}, u32[]{:S(2)}) %collective-permute-start.18) | collective-permute-done | bytes 163872 | tf_op jit(solution)/shard_map/ppermute | solution.py:278
  57.2 0.8 %reshape.8.rest_12_ = f32[640,1]{1,0:T(8,128)S(1)} reshape(f32[640]{0:T(1024)} %param.12) | data formatting | bytes 5120 | tf_op jit(solution)/shard_map/reshape | solution.py:356
  58.0 0.7 reshape.6.rest_10_
  58.7 0.9 %copy-done.3 = bf16[1,64,1280]{2,1,0:T(8,128)(2,1)S(1)} copy-done((bf16[1,64,1280]{2,1,0:T(8,128)(2,1)S(1)}, bf16[1,64,1280]{2,1,0:T(8,128)(2,1)}, u32[]{:S(2)}) %copy-start.3) | copy-done | bytes 163864
  60.3 1.5 %residual_rows.1.rest_8_ = bf16[512,1280]{1,0:T(8,128)(2,1)S(1)} custom-call(s32[1,2]{1,0:T(1,128)S(1)} %copy-done.5, bf16[64,1280]{1,0:T(8,128)(2,1)S(1)} %bitcast.5, bf16[64,1280]{1,0:T(8,128)(2,1)S(1)} %collective-permute-done.14.rest_1_, bf16[64,1280]{1,0:T(8,128)(2,1)S(1)} %collective-permute-done.15.rest_2_, ...), custom_call_target="tpu_custom_call" | custom-call | flops 671088640 | bytes 2621440 | tf_op jit(solution)/shard_map/residual_rows/pallas_call | solution.py:322
  62.1 2.5 %copy-done = bf16[640,5120]{1,0:T(8,128)(2,1)S(1)} copy-done((bf16[640,5120]{1,0:T(8,128)(2,1)S(1)}, bf16[640,5120]{1,0:T(8,128)(2,1)}, u32[]{:S(2)}) %copy-start) | copy-done | bytes 6553624
  64.7 6.4 %merge.1 = bf16[1,640,128]{2,1,0:T(8,128)(2,1)} custom-call(s32[1,2]{1,0:T(1,128)S(1)} %copy-done.5, bf16[640,128]{1,0:T(8,128)(2,1)S(1)} %attend.1.rest_0_, bf16[640,128]{1,0:T(8,128)(2,1)S(1)} %collective-permute-done.7.rest_1_, bf16[640,128]{1,0:T(8,128)(2,1)S(1)} %collective-permute-done.8.rest_2_, bf16[640,128]{1,0:T(8,128)(2,1)S(1)} %collective-permute-done.9.rest_3_, ...), custom_call_target="tpu_custom_call" | custom-call | flops 2516582400 | bytes 16777216 | tf_op jit(solution)/shard_map/merge/pallas_call | solution.py:342
  (50 shorter events, 5.0 us)
Async XLA Ops:
  1.1 14.6 %collective-permute-start.21 = (bf16[160,1280]{1,0:T(8,128)(2,1)S(1)}, bf16[160,1280]{1,0:T(8,128)(2,1)S(1)}, u32[]{:S(2)}, u32[]{:S(2)}) collective-permute-start(bf16[160,1280]{1,0:T(8,128)(2,1)S(1)} %constant_dynamic-slice_fusion), channel_id=1, source_target_pairs={{0,8},{8,16},{16,24},{24,0},{1,9},{9,17},{17,25},{25,1},{2,10},{10... | collective-permute-start | bytes 1228808 | tf_op jit(solution)/shard_map/ppermute | solution.py:298
  15.7 12.5 %collective-permute-start.22 = (bf16[160,1280]{1,0:T(8,128)(2,1)S(1)}, bf16[160,1280]{1,0:T(8,128)(2,1)S(1)}, u32[]{:S(2)}, u32[]{:S(2)}) collective-permute-start(bf16[160,1280]{1,0:T(8,128)(2,1)S(1)} %collective-permute-done.21.rest_0_), channel_id=1, source_target_pairs={{0,8},{8,16},{16,24},{24,0},{1,9},{9,17},{17,25},{25,1},{2,10},{10... | collective-permute-start | bytes 1228808 | tf_op jit(solution)/shard_map/ppermute | solution.py:298
  17.0 4.5 %collective-permute-start.1 = (bf16[64,480]{1,0:T(8,128)(2,1)S(1)}, bf16[64,480]{1,0:T(8,128)(2,1)S(1)}, u32[]{:S(2)}, u32[]{:S(2)}) collective-permute-start(bf16[64,480]{1,0:T(8,128)(2,1)S(1)} %get-tuple-element.15), channel_id=1, source_target_pairs={{0,2},{1,3},{2,0},{3,1},{4,6},{5,7},{6,4},{7,5},{8,10},{9,11},{10,... | collective-permute-start | bytes 184328 | tf_op jit(solution)/shard_map/ppermute | solution.py:278
  18.6 4.9 %collective-permute-start.2 = (bf16[64,480]{1,0:T(8,128)(2,1)S(1)}, bf16[64,480]{1,0:T(8,128)(2,1)S(1)}, u32[]{:S(2)}, u32[]{:S(2)}) collective-permute-start(bf16[64,480]{1,0:T(8,128)(2,1)S(1)} %get-tuple-element.16), channel_id=1, source_target_pairs={{0,3},{1,2},{2,1},{3,0},{4,7},{5,6},{6,5},{7,4},{8,11},{9,10},{10,... | collective-permute-start | bytes 184328 | tf_op jit(solution)/shard_map/ppermute | solution.py:278
  18.9 9.2 %collective-permute-start.3 = (bf16[64,480]{1,0:T(8,128)(2,1)S(1)}, bf16[64,480]{1,0:T(8,128)(2,1)S(1)}, u32[]{:S(2)}, u32[]{:S(2)}) collective-permute-start(bf16[64,480]{1,0:T(8,128)(2,1)S(1)} %get-tuple-element.17), channel_id=1, source_target_pairs={{0,4},{1,5},{2,6},{3,7},{4,0},{5,1},{6,2},{7,3},{8,12},{9,13},{10,... | collective-permute-start | bytes 184328 | tf_op jit(solution)/shard_map/ppermute | solution.py:278
  20.4 9.9 %collective-permute-start.4 = (bf16[64,480]{1,0:T(8,128)(2,1)S(1)}, bf16[64,480]{1,0:T(8,128)(2,1)S(1)}, u32[]{:S(2)}, u32[]{:S(2)}) collective-permute-start(bf16[64,480]{1,0:T(8,128)(2,1)S(1)} %get-tuple-element.18), channel_id=1, source_target_pairs={{0,5},{1,4},{2,7},{3,6},{4,1},{5,0},{6,3},{7,2},{8,13},{9,12},{10,... | collective-permute-start | bytes 184328 | tf_op jit(solution)/shard_map/ppermute | solution.py:278
  21.6 17.2 %collective-permute-start.15 = (bf16[64,1280]{1,0:T(8,128)(2,1)}, bf16[64,1280]{1,0:T(8,128)(2,1)S(1)}, u32[]{:S(2)}, u32[]{:S(2)}) collective-permute-start(bf16[64,1280]{1,0:T(8,128)(2,1)} %bitcast.1), channel_id=1, source_target_pairs={{0,2},{1,3},{2,0},{3,1},{4,6},{5,7},{6,4},{7,5},{8,10},{9,11},{10,... | collective-permute-start | bytes 491528 | tf_op jit(solution)/shard_map/ppermute | solution.py:278
  23.5 15.3 %collective-permute-start.17 = (bf16[64,1280]{1,0:T(8,128)(2,1)}, bf16[64,1280]{1,0:T(8,128)(2,1)S(1)}, u32[]{:S(2)}, u32[]{:S(2)}) collective-permute-start(bf16[64,1280]{1,0:T(8,128)(2,1)} %bitcast.2), channel_id=1, source_target_pairs={{0,4},{1,5},{2,6},{3,7},{4,0},{5,1},{6,2},{7,3},{8,12},{9,13},{10,... | collective-permute-start | bytes 491528 | tf_op jit(solution)/shard_map/ppermute | solution.py:278
  28.1 20.8 %collective-permute-start.23 = (bf16[160,1280]{1,0:T(8,128)(2,1)S(1)}, bf16[160,1280]{1,0:T(8,128)(2,1)S(1)}, u32[]{:S(2)}, u32[]{:S(2)}) collective-permute-start(bf16[160,1280]{1,0:T(8,128)(2,1)S(1)} %collective-permute-done.22.rest_1_), channel_id=1, source_target_pairs={{0,8},{8,16},{16,24},{24,0},{1,9},{9,17},{17,25},{25,1},{2,10},{10... | collective-permute-start | bytes 1228808 | tf_op jit(solution)/shard_map/ppermute | solution.py:298
  28.1 5.2 %collective-permute-start.5 = (bf16[64,480]{1,0:T(8,128)(2,1)S(1)}, bf16[64,480]{1,0:T(8,128)(2,1)S(1)}, u32[]{:S(2)}, u32[]{:S(2)}) collective-permute-start(bf16[64,480]{1,0:T(8,128)(2,1)S(1)} %get-tuple-element.19), channel_id=1, source_target_pairs={{0,6},{1,7},{2,4},{3,5},{4,2},{5,3},{6,0},{7,1},{8,14},{9,15},{10,... | collective-permute-start | bytes 184328 | tf_op jit(solution)/shard_map/ppermute | solution.py:278
  30.3 5.7 %collective-permute-start.6 = (bf16[64,480]{1,0:T(8,128)(2,1)S(1)}, bf16[64,480]{1,0:T(8,128)(2,1)S(1)}, u32[]{:S(2)}, u32[]{:S(2)}) collective-permute-start(bf16[64,480]{1,0:T(8,128)(2,1)S(1)} %get-tuple-element.20), channel_id=1, source_target_pairs={{0,7},{1,6},{2,5},{3,4},{4,3},{5,2},{6,1},{7,0},{8,15},{9,14},{10,... | collective-permute-start | bytes 184328 | tf_op jit(solution)/shard_map/ppermute | solution.py:278
  33.3 7.0 %collective-permute-start.19 = (bf16[64,1280]{1,0:T(8,128)(2,1)}, bf16[64,1280]{1,0:T(8,128)(2,1)S(1)}, u32[]{:S(2)}, u32[]{:S(2)}) collective-permute-start(bf16[64,1280]{1,0:T(8,128)(2,1)} %bitcast.3), channel_id=1, source_target_pairs={{0,6},{1,7},{2,4},{3,5},{4,2},{5,3},{6,0},{7,1},{8,14},{9,15},{10,... | collective-permute-start | bytes 491528 | tf_op jit(solution)/shard_map/ppermute | solution.py:278
  36.0 4.2 %collective-permute-start.14 = (bf16[64,1280]{1,0:T(8,128)(2,1)}, bf16[64,1280]{1,0:T(8,128)(2,1)S(1)}, u32[]{:S(2)}, u32[]{:S(2)}) collective-permute-start(bf16[64,1280]{1,0:T(8,128)(2,1)} %bitcast.4), channel_id=1, source_target_pairs={{0,1},{1,0},{2,3},{3,2},{4,5},{5,4},{6,7},{7,6},{8,9},{9,8},{10,11... | collective-permute-start | bytes 491528 | tf_op jit(solution)/shard_map/ppermute | solution.py:278
  38.7 10.2 %collective-permute-start.10 = (bf16[640,128]{1,0:T(8,128)(2,1)S(1)}, bf16[640,128]{1,0:T(8,128)(2,1)S(1)}, u32[]{:S(2)}, u32[]{:S(2)}) collective-permute-start(bf16[640,128]{1,0:T(8,128)(2,1)S(1)} %attend.1.rest_0_), channel_id=1, source_target_pairs={{0,4},{1,5},{2,6},{3,7},{4,0},{5,1},{6,2},{7,3},{8,12},{9,13},{10,... | collective-permute-start | bytes 491528 | tf_op jit(solution)/shard_map/ppermute | solution.py:278
  38.8 10.1 %collective-permute-start.12 = (bf16[640,128]{1,0:T(8,128)(2,1)S(1)}, bf16[640,128]{1,0:T(8,128)(2,1)S(1)}, u32[]{:S(2)}, u32[]{:S(2)}) collective-permute-start(bf16[640,128]{1,0:T(8,128)(2,1)S(1)} %attend.1.rest_0_), channel_id=1, source_target_pairs={{0,6},{1,7},{2,4},{3,5},{4,2},{5,3},{6,0},{7,1},{8,14},{9,15},{10,... | collective-permute-start | bytes 491528 | tf_op jit(solution)/shard_map/ppermute | solution.py:278
  40.3 16.4 %collective-permute-start.24 = (bf16[160,1280]{1,0:T(8,128)(2,1)S(1)}, bf16[160,1280]{1,0:T(8,128)(2,1)S(1)}, u32[]{:S(2)}, u32[]{:S(2)}) collective-permute-start(bf16[160,1280]{1,0:T(8,128)(2,1)S(1)} %collective-permute-done.21.rest_0_), channel_id=1, source_target_pairs={{0,1},{1,0},{2,3},{3,2},{4,5},{5,4},{6,7},{7,6},{8,9},{9,8},{10,11... | collective-permute-start | bytes 1228808 | tf_op jit(solution)/shard_map/ppermute | solution.py:278
  40.3 16.6 %collective-permute-start.25 = (bf16[160,1280]{1,0:T(8,128)(2,1)S(1)}, bf16[160,1280]{1,0:T(8,128)(2,1)S(1)}, u32[]{:S(2)}, u32[]{:S(2)}) collective-permute-start(bf16[160,1280]{1,0:T(8,128)(2,1)S(1)} %collective-permute-done.22.rest_1_), channel_id=1, source_target_pairs={{0,1},{1,0},{2,3},{3,2},{4,5},{5,4},{6,7},{7,6},{8,9},{9,8},{10,11... | collective-permute-start | bytes 1228808 | tf_op jit(solution)/shard_map/ppermute | solution.py:278
  48.9 5.8 %collective-permute-start.8 = (bf16[640,128]{1,0:T(8,128)(2,1)S(1)}, bf16[640,128]{1,0:T(8,128)(2,1)S(1)}, u32[]{:S(2)}, u32[]{:S(2)}) collective-permute-start(bf16[640,128]{1,0:T(8,128)(2,1)S(1)} %attend.1.rest_0_), channel_id=1, source_target_pairs={{0,2},{1,3},{2,0},{3,1},{4,6},{5,7},{6,4},{7,5},{8,10},{9,11},{10,... | collective-permute-start | bytes 491528 | tf_op jit(solution)/shard_map/ppermute | solution.py:278
  48.9 5.8 %collective-permute-start.16 = (bf16[64,1280]{1,0:T(8,128)(2,1)S(1)}, bf16[64,1280]{1,0:T(8,128)(2,1)S(1)}, u32[]{:S(2)}, u32[]{:S(2)}) collective-permute-start(bf16[64,1280]{1,0:T(8,128)(2,1)S(1)} %collective-permute-done.15.rest_2_), channel_id=1, source_target_pairs={{0,1},{1,0},{2,3},{3,2},{4,5},{5,4},{6,7},{7,6},{8,9},{9,8},{10,11... | collective-permute-start | bytes 491528 | tf_op jit(solution)/shard_map/ppermute | solution.py:278
  49.0 12.9 %collective-permute-start.26 = (bf16[160,1280]{1,0:T(8,128)(2,1)S(1)}, bf16[160,1280]{1,0:T(8,128)(2,1)S(1)}, u32[]{:S(2)}, u32[]{:S(2)}) collective-permute-start(bf16[160,1280]{1,0:T(8,128)(2,1)S(1)} %collective-permute-done.23.rest_2_), channel_id=1, source_target_pairs={{0,1},{1,0},{2,3},{3,2},{4,5},{5,4},{6,7},{7,6},{8,9},{9,8},{10,11... | collective-permute-start | bytes 1228808 | tf_op jit(solution)/shard_map/ppermute | solution.py:278
  56.2 5.9 %collective-permute-start.7 = (bf16[640,128]{1,0:T(8,128)(2,1)S(1)}, bf16[640,128]{1,0:T(8,128)(2,1)S(1)}, u32[]{:S(2)}, u32[]{:S(2)}) collective-permute-start(bf16[640,128]{1,0:T(8,128)(2,1)S(1)} %attend.1.rest_0_), channel_id=1, source_target_pairs={{0,1},{1,0},{2,3},{3,2},{4,5},{5,4},{6,7},{7,6},{8,9},{9,8},{10,11... | collective-permute-start | bytes 491528 | tf_op jit(solution)/shard_map/ppermute | solution.py:278
  56.4 5.7 %collective-permute-start.11 = (bf16[640,128]{1,0:T(8,128)(2,1)S(1)}, bf16[640,128]{1,0:T(8,128)(2,1)S(1)}, u32[]{:S(2)}, u32[]{:S(2)}) collective-permute-start(bf16[640,128]{1,0:T(8,128)(2,1)S(1)} %collective-permute-done.10.rest_4_), channel_id=1, source_target_pairs={{0,1},{1,0},{2,3},{3,2},{4,5},{5,4},{6,7},{7,6},{8,9},{9,8},{10,11... | collective-permute-start | bytes 491528 | tf_op jit(solution)/shard_map/ppermute | solution.py:278
  56.7 5.5 %collective-permute-start.13 = (bf16[640,128]{1,0:T(8,128)(2,1)S(1)}, bf16[640,128]{1,0:T(8,128)(2,1)S(1)}, u32[]{:S(2)}, u32[]{:S(2)}) collective-permute-start(bf16[640,128]{1,0:T(8,128)(2,1)S(1)} %collective-permute-done.12.rest_6_), channel_id=1, source_target_pairs={{0,1},{1,0},{2,3},{3,2},{4,5},{5,4},{6,7},{7,6},{8,9},{9,8},{10,11... | collective-permute-start | bytes 491528 | tf_op jit(solution)/shard_map/ppermute | solution.py:278
  56.9 5.2 %collective-permute-start.9 = (bf16[640,128]{1,0:T(8,128)(2,1)S(1)}, bf16[640,128]{1,0:T(8,128)(2,1)S(1)}, u32[]{:S(2)}, u32[]{:S(2)}) collective-permute-start(bf16[640,128]{1,0:T(8,128)(2,1)S(1)} %collective-permute-done.8.rest_2_), channel_id=1, source_target_pairs={{0,1},{1,0},{2,3},{3,2},{4,5},{5,4},{6,7},{7,6},{8,9},{9,8},{10,11... | collective-permute-start | bytes 491528 | tf_op jit(solution)/shard_map/ppermute | solution.py:278
  (9 other events, 74.4 us)

commit v2 on v0

--- a/solution.py
+++ b/solution.py
@@ -1,8 +1,11 @@
+import functools
 import math
 
 import jax
 import jax.numpy as jnp
 from jax import lax
+from jax.experimental import pallas as pl
+from jax.experimental.pallas import tpu as pltpu
 from jax.sharding import PartitionSpec as P
 
 D = 1280
@@ -10,7 +13,7 @@
 HDIM = 80
 
 
-def local(qkv_rows, residual, out_weight, norm_gain, merge_weight, merge_bias, page_grid):
+def local_any(qkv_rows, residual, out_weight, norm_gain, merge_weight, merge_bias, page_grid):
     row_count = lax.axis_size("row")
     q_split = max(1, row_count // HEADS)
     head_groups = row_count // q_split
@@ -112,6 +115,312 @@
     return merged[None]
 
 
+ROWS = 8
+PAGES = 4
+HPAIR = 2 * HDIM
+WIDE = 128
+REST = HPAIR - WIDE
+MAIN = ROWS * WIDE
+ROOT = math.log2(math.e) / math.sqrt(HDIM)
+BF16 = jnp.bfloat16
+F32 = jnp.float32
+
+
+def row_index():
+    return lax.axis_index("row")
+
+
+def pack_tail(wide):
+    groups = wide.shape[0] // 4
+    return jnp.concatenate([wide[at * groups : (at + 1) * groups] for at in range(4)], axis=1)
+
+
+def spread_kernel(qkv_ref, resid_ref, *rest):
+    outs, held = rest[:ROWS], rest[ROWS]
+    me = row_index()
+    for dest in range(ROWS):
+        at = dest * HPAIR
+        resid = [resid_ref[0, :, dest * WIDE : (dest + 1) * WIDE]]
+        resid.append(resid_ref[0, :, MAIN + dest * REST : MAIN + (dest + 1) * REST])
+        parts = [qkv_ref[0, :, part * D + at : part * D + at + HPAIR] for part in range(3)]
+        held[dest] = jnp.concatenate(parts + resid, axis=1)
+    for step in range(ROWS):
+        outs[step][...] = held[me ^ step]
+
+
+def slice_kernel(weight_ref, token_ref, out_ref):
+    del token_ref
+    me = row_index()
+    depth = weight_ref.shape[0]
+    out_ref[:depth, :] = weight_ref[:, pl.ds(pl.multiple_of(me * WIDE, WIDE), WIDE)]
+    tile = weight_ref[:, pl.ds(pl.multiple_of(MAIN + me // 4 * WIDE, WIDE), WIDE)]
+    tail = tile[:, :REST]
+    for at in range(1, 4):
+        tail = jnp.where(lax.rem(me, 4) == at, tile[:, at * REST : (at + 1) * REST], tail)
+    out_ref[depth:, :] = pack_tail(tail)
+
+
+def layout_kernel(grid_ref, gain_ref, bias_ref, token_ref, select_ref, keys_ref, live_ref, gain_out, bias_out):
+    del token_ref
+    rows_n, cols_n = grid_ref[0, 0], grid_ref[0, 1]
+    patches = select_ref.shape[0]
+    groups = patches // 4
+    half = cols_n // 2
+    count = (rows_n // 2) * half
+    slots = lax.broadcasted_iota(jnp.int32, (groups, 1), 0)
+    line = jnp.floor((slots.astype(F32) + 0.5) / half.astype(F32)).astype(jnp.int32)
+    first = 2 * line * cols_n + 2 * (slots - line * half)
+    at = lax.broadcasted_iota(jnp.int32, (groups, patches), 1)
+    for corner in range(4):
+        wanted = jnp.where(slots < count, first + (corner // 2) * cols_n + corner % 2, -1)
+        select_ref[corner * groups : (corner + 1) * groups, :] = jnp.where(at == wanted, 1.0, 0.0).astype(BF16)
+    key = lax.broadcasted_iota(jnp.int32, keys_ref.shape, 1)
+    keys_ref[...] = jnp.where(key < rows_n * cols_n, 0.0, -1e30)
+    slot = lax.broadcasted_iota(jnp.int32, live_ref.shape, 1)
+    live_ref[...] = jnp.where(slot < count, 1.0, 0.0)
+    gain_out[...] = gain_ref[...]
+    bias_out[...] = bias_ref[...]
+
+
+def attend_kernel(select_ref, dead_ref, *rest):
+    blocks = rest[:ROWS]
+    out_ref, q_all, k_all, v_all = rest[ROWS:]
+    me = row_index()
+    band = blocks[0].shape[0]
+    patches = band * ROWS
+    for step in range(ROWS):
+        at = pl.ds(pl.multiple_of((me ^ step) * band, band), band)
+        q_all[at, :] = blocks[step][:, :HPAIR]
+        k_all[at, :] = blocks[step][:, HPAIR : 2 * HPAIR]
+        v_all[at, :] = blocks[step][:, 2 * HPAIR : 3 * HPAIR]
+    queries = jnp.dot(select_ref[...], q_all[...], preferred_element_type=F32).astype(BF16)
+    lane = lax.broadcasted_iota(jnp.int32, (1, HPAIR), 1)
+    keys, values, dead = k_all[...], v_all[...], dead_ref[...]
+    mixed = []
+    for head in range(2):
+        mine = (lane >= head * HDIM) & (lane < (head + 1) * HDIM)
+        asked = jnp.where(mine, queries, jnp.zeros_like(queries))
+        scores = lax.dot_general(asked, keys, (((1,), (1,)), ((), ())), preferred_element_type=F32) + dead
+        weights = jnp.exp2((scores - jnp.max(scores, axis=1, keepdims=True)) * ROOT)
+        total = jnp.sum(weights, axis=1, keepdims=True)
+        mixed.append(jnp.dot(weights.astype(BF16), values, preferred_element_type=F32) / total)
+    attn = jnp.where(lane < HDIM, mixed[0], mixed[1])
+    out_ref[:patches, :] = attn[:, :WIDE].astype(BF16)
+    out_ref[patches:, :] = pack_tail(attn[:, WIDE:]).astype(BF16)
+
+
+def ready_kernel(select_ref, token_ref, *rest):
+    del token_ref
+    blocks, slices = rest[:ROWS], rest[ROWS : ROWS + PAGES]
+    resid_ref, main_ref, tail_ref, held = rest[ROWS + PAGES :]
+    me = row_index()
+    page = lax.axis_index("page")
+    band = blocks[0].shape[0]
+    for step in range(ROWS):
+        at = pl.ds(pl.multiple_of((me ^ step) * band, band), band)
+        held[at, :] = blocks[step][:, 3 * HPAIR :]
+    resid_ref[...] = jnp.dot(select_ref[...], held[...], preferred_element_type=F32)
+    tail_ref[...] = jnp.zeros_like(tail_ref)
+    depth = 2 * HPAIR
+    for step in range(PAGES):
+        source = lax.rem(page + PAGES - step, PAGES)
+        packed = slices[step][depth:]
+        tail = jnp.concatenate([packed[:, at * REST : (at + 1) * REST] for at in range(4)], axis=0)
+        whole = jnp.concatenate([slices[step][:depth], tail], axis=1)
+        for core in range(2):
+            pair = 2 * source + core
+            rows = whole[core * HPAIR : (core + 1) * HPAIR]
+            main_ref[pl.ds(pl.multiple_of(pair * WIDE, WIDE), WIDE), :] = rows[:WIDE]
+            for corner in range(4):
+                spot = pl.multiple_of(pair * WIDE + corner * REST, REST)
+                tail_ref[corner, pl.ds(spot, REST), :] = rows[WIDE:]
+
+
+def collect(pieces, full):
+    me = row_index()
+    for step in range(ROWS):
+        full[:, pl.ds(pl.multiple_of((me ^ step) * WIDE, WIDE), WIDE)] = pieces[step][...]
+
+
+def project_kernel(*rest):
+    pieces = rest[:ROWS]
+    main_ref, tail_ref, resid_ref, out_ref, full = rest[ROWS:]
+    collect(pieces, full)
+    patches = resid_ref.shape[0]
+    groups = patches // 4
+    hidden = jnp.dot(full[:patches], main_ref[...], preferred_element_type=F32) + resid_ref[...]
+    ends = []
+    for corner in range(4):
+        span = slice(corner * groups, (corner + 1) * groups)
+        part = hidden[span] + jnp.dot(full[patches:], tail_ref[corner], preferred_element_type=F32)
+        out_ref[span, :] = part[:, :WIDE].astype(BF16)
+        ends.append(part[:, WIDE:])
+    out_ref[patches:, :] = jnp.concatenate(ends, axis=1).astype(BF16)
+
+
+def tail_kernel(weight_ref, token_ref, out_ref):
+    del token_ref
+    for pair in range(ROWS):
+        cut = [corner * D + MAIN + pair * REST for corner in range(4)]
+        out_ref[:, pair * WIDE : (pair + 1) * WIDE] = jnp.concatenate(
+            [weight_ref[:, at : at + REST] for at in cut], axis=1
+        )
+
+
+def merge_kernel(*rest):
+    pieces = rest[:ROWS]
+    weight_ref, tail_ref, gain_ref, bias_ref, live_ref, out_ref, full = rest[ROWS:]
+    collect(pieces, full)
+    groups = live_ref.shape[1]
+    patches = 4 * groups
+    gain = gain_ref[...]
+    ends = full[patches:].astype(F32)
+    squares = ends * ends
+    folded = squares[:, :WIDE]
+    for pair in range(1, ROWS):
+        folded = folded + squares[:, pair * WIDE : (pair + 1) * WIDE]
+    lane = lax.broadcasted_iota(jnp.int32, (1, WIDE), 1)
+    contract = (((1,), (1,)), ((), ()))
+    total = jnp.zeros((weight_ref.shape[0], groups), F32)
+    spread = jnp.zeros((groups, WIDE), F32)
+    for corner in range(4):
+        mine = (lane >= corner * REST) & (lane < (corner + 1) * REST)
+        rows = full[corner * groups : (corner + 1) * groups].astype(F32)
+        square = jnp.sum(rows * rows, axis=1, keepdims=True)
+        square = square + jnp.sum(jnp.where(mine, folded, 0.0), axis=1, keepdims=True)
+        scale = lax.rsqrt(square * (1.0 / D) + 1e-06)
+        spread = jnp.where(mine, scale, spread)
+        normed = (rows * scale * gain[:, :MAIN]).astype(BF16)
+        total = total + lax.dot_general(
+            weight_ref[:, corner * D : corner * D + MAIN], normed, contract, preferred_element_type=F32
+        )
+    normed = []
+    for pair in range(ROWS):
+        piece = gain[:, MAIN + pair * REST : MAIN + (pair + 1) * REST]
+        piece = jnp.concatenate([piece] * 4, axis=1)
+        normed.append((ends[:, pair * WIDE : (pair + 1) * WIDE] * spread * piece).astype(BF16))
+    total = total + lax.dot_general(
+        tail_ref[...], jnp.concatenate(normed, axis=1), contract, preferred_element_type=F32
+    )
+    total = total + bias_ref[...]
+    merged = 0.5 * total * (1.0 + lax.erf(total * math.sqrt(0.5)))
+    out_ref[0] = jnp.where(live_ref[...] > 0.0, merged, 0.0).astype(BF16)
+
+
+def kernel(body, name, out_shape, scratch=(), first="vmem", tokens=(), count=0, limit=24, flops=0, moved=0):
+    spaces = {"vmem": pltpu.VMEM, "smem": pltpu.SMEM, "any": pl.ANY}
+    specs = [pl.BlockSpec(memory_space=pltpu.VMEM) for _ in range(count)]
+    specs[0] = pl.BlockSpec(memory_space=spaces[first])
+    for at in tokens:
+        specs[at] = pl.BlockSpec(memory_space=pl.ANY)
+    return pl.pallas_call(
+        body,
+        out_shape=out_shape,
+        in_specs=specs,
+        out_specs=jax.tree.map(lambda _: pl.BlockSpec(memory_space=pltpu.VMEM), out_shape),
+        scratch_shapes=list(scratch),
+        compiler_params=pltpu.CompilerParams(vmem_limit_bytes=limit * 1024 * 1024),
+        cost_estimate=pl.CostEstimate(flops=flops, bytes_accessed=moved, transcendentals=0),
+        name=name,
+    )
+
+
+def shape(*dims, dtype=BF16):
+    return jax.ShapeDtypeStruct(dims, dtype)
+
+
+def swap(value, step):
+    return lax.ppermute(value, "row", [(row, row ^ step) for row in range(ROWS)])
+
+
+def gather_rows(value):
+    far = [swap(value, step) for step in (6, 2, 4)]
+    near = [swap(piece, 1) for piece in [value] + far]
+    return [value, near[0], far[1], near[2], far[2], near[3], far[0], near[1]]
+
+
+def local_eight(qkv_rows, residual, out_weight, norm_gain, merge_weight, merge_bias, page_grid):
+    band = qkv_rows.shape[1]
+    patches = band * ROWS
+    groups = patches // 4
+    units = merge_weight.shape[0]
+    depth = out_weight.shape[0]
+    piece = shape(patches + groups, WIDE)
+    assembled = pltpu.VMEM((patches + groups, MAIN), BF16)
+
+    sends = kernel(
+        spread_kernel,
+        "spread",
+        [shape(band, 4 * HPAIR)] * ROWS,
+        [pltpu.VMEM((ROWS, band, 4 * HPAIR), BF16)],
+        count=2,
+        moved=1 << 20,
+    )(qkv_rows, residual)
+    blocks = [None] * ROWS
+    blocks[0] = sends[0]
+    for step in (6, 7, 2, 4, 3, 5, 1):
+        blocks[step] = swap(sends[step], step)
+    own = kernel(slice_kernel, "weight_slice", shape(depth + depth // 4, WIDE), tokens=(1,), count=2, moved=1 << 20)(
+        out_weight, sends[0]
+    )
+    slices = [own]
+    for _ in range(PAGES - 1):
+        slices.append(lax.ppermute(slices[-1], "page", [(page, (page + 1) % PAGES) for page in range(PAGES)]))
+    select, dead, live, gain, bias = kernel(
+        layout_kernel,
+        "layout",
+        [
+            shape(patches, patches),
+            shape(1, patches, dtype=F32),
+            shape(1, groups, dtype=F32),
+            shape(1, D, dtype=F32),
+            shape(units, 1, dtype=F32),
+        ],
+        first="smem",
+        tokens=(3,),
+        count=4,
+        moved=1 << 20,
+    )(page_grid, norm_gain.reshape(1, D), merge_bias.reshape(units, 1), sends[0])
+    attn = kernel(
+        attend_kernel,
+        "attend",
+        piece,
+        [pltpu.VMEM((patches, HPAIR), BF16)] * 3,
+        count=2 + ROWS,
+        flops=6 * patches * patches * 256,
+        moved=1 << 20,
+    )(select, dead, *blocks)
+    resid, main, tail = kernel(
+        ready_kernel,
+        "ready",
+        [shape(patches, HPAIR, dtype=F32), shape(MAIN, HPAIR), shape(4, MAIN, HPAIR)],
+        [pltpu.VMEM((patches, HPAIR), BF16)],
+        tokens=(1,),
+        count=2 + ROWS + PAGES,
+        flops=2 * patches * patches * 256,
+        moved=4 << 20,
+    )(select, attn, *blocks, *slices)
+    hidden = kernel(
+        project_kernel,
+        "project",
+        piece,
+        [assembled],
+        count=ROWS + 3,
+        flops=4 * patches * MAIN * 256,
+        moved=4 << 20,
+    )(*gather_rows(attn), main, tail, resid)
+    ends = kernel(tail_kernel, "merge_tail", shape(units, MAIN), tokens=(1,), count=2, moved=4 << 20)(merge_weight, hidden)
+    return kernel(
+        merge_kernel,
+        "merge",
+        shape(1, units, groups),
+        [assembled],
+        count=ROWS + 5,
+        flops=10 * units * groups * MAIN,
+        moved=8 << 20,
+    )(*gather_rows(hidden), merge_weight, ends, gain, bias, live)
+
+
 def solution(mesh):
     in_specs = (
         P("page", "row", None),
@@ -123,4 +432,5 @@
         P("page", None),
     )
     out_specs = P("page", "row", None)
+    local = local_eight if mesh.shape["row"] == 8 and mesh.shape["page"] == 4 else local_any
     return jax.shard_map(local, mesh=mesh, in_specs=in_specs, out_specs=out_specs, check_vma=False)

time: 127 us -> 55.8 us (0.44)
  waiting for transfers between devices: 60.2 us -> 24.4 us
  between operations: 20.8 us -> 0.15 us
  matrix products: 13.1 us -> 0 us
  blocking collectives: 9.35 us -> 0 us
  starting transfers between devices: 8.8 us -> 17.8 us
  Pallas kernels: 0 us -> 8.92 us
  local copies, waits for them, and re-layouts: 11.1 us -> 4.21 us
  other arithmetic: 2.98 us -> 0 us
    all_gather x2 -> x0, waiting for transfers between devices: 48.2 us -> none  [the longest x1 31.5 us: local(): lax.all_gather(out_weight, 'page', axis=0, tiled=True)]
    ppermute x0 -> x24, waiting for transfers between devices: none -> 24.4 us  [the longest x3 16.7 us: local_eight(): lax.ppermute(slices[-1], 'page', [(page, (page + 1) % PAGES) for page in...]
    ppermute x0 -> x24, starting transfers between devices: none -> 17.8 us  [the longest x21 16.1 us: swap(): lax.ppermute(value, 'row', [(row, row ^ step) for row in range(ROWS)])]
    dot_general x7 -> x0, matrix products: 13.1 us -> none  [the longest x4 9.11 us: local(): jnp.einsum('md,gd->mg', merge_weight[:, corner * D:(corner + 1) * D], pic...]
    all_to_all x2 -> x0, waiting for transfers between devices: 11.3 us -> none  [the longest x1 6.08 us: local(): lax.all_to_all(kv_send, 'row', split_axis=0, concat_axis=1, tiled=True)]
    all_to_all x1 -> x0, blocking collectives: 9.35 us -> none  [local(): lax.all_to_all(attn_heads, 'row', split_axis=0, concat_axis=0, tiled=True)]
    pallas_call x0 -> x8, Pallas kernels: none -> 8.92 us  [the longest x1 3.3 us: local_eight(): kernel(merge_kernel, 'merge', shape(1, units, groups), [assembled], count...]
    all_to_all x2 -> x0, starting transfers between devices: 8.75 us -> none  [the longest x1 5.3 us: local(): lax.all_to_all(q_send, 'row', split_axis=0, concat_axis=1, tiled=True)]
  transfers between devices with their start and end apart: 4 -> 24, of which waited for: 4 -> 10; matrix products, arithmetic and copies ran while one was open for 7% -> 3% of each run, Pallas kernels for 0% -> 5%
where the time goes in v2:
time: 55.8 us; the launch traced here: 55.5 us
  waiting for transfers between devices  24.4 us (44%)
  starting transfers between devices  17.8 us (32%)
  Pallas kernels  8.92 us (16%)
  local copies, waits for them, and re-layouts  4.21 us (8%)
    ppermute x3, waiting for transfers between devices, local_eight(): lax.ppermute(slices[-1], 'page', [(page, (page + 1) % PAGES) for page in...  16.7 us
    ppermute x21, starting transfers between devices, swap(): lax.ppermute(value, 'row', [(row, row ^ step) for row in range(ROWS)])  16.1 us
    ppermute x21, waiting for transfers between devices, swap(): lax.ppermute(value, 'row', [(row, row ^ step) for row in range(ROWS)])  7.77 us
    pallas_call x1, Pallas kernels, local_eight(): kernel(merge_kernel, 'merge', shape(1, units, groups), [assembled], count...  3.3 us
    unnamed x10, local copies, waits for them, and re-layouts  2.68 us
    ppermute x3, starting transfers between devices, local_eight(): lax.ppermute(slices[-1], 'page', [(page, (page + 1) % PAGES) for page in...  1.74 us
    pallas_call x1, Pallas kernels, local_eight(): kernel(attend_kernel, 'attend', piece, [pltpu.VMEM((patches, HPAIR), BF16...  1.35 us
    pallas_call x1, Pallas kernels, local_eight(): kernel(tail_kernel, 'merge_tail', shape(units, MAIN), tokens=(1,), count=...  1.22 us
  transfers between devices with their start and end apart: 24, of which 10 were waited for; matrix products, arithmetic and copies ran while one was open for 3% of the time, Pallas kernels for 5%

profile of v2, /device:TPU:0, one launch (start us, length us, event | category | flops | bytes accessed | tf_op | source)
XLA Modules:
  0.0 55.5 jit_solution(12424200795986608861)
XLA Ops:
  0.0 1.1 %copy-done.2 = bf16[1,64,3840]{2,1,0:T(8,128)(2,1)S(1)} copy-done((bf16[1,64,3840]{2,1,0:T(8,128)(2,1)S(1)}, bf16[1,64,3840]{2,1,0:T(8,128)(2,1)}, u32[]{:S(2)}) %copy-start.2) | copy-done | bytes 491544
  1.1 0.9 %copy-done.3 = bf16[1,64,1280]{2,1,0:T(8,128)(2,1)S(1)} copy-done((bf16[1,64,1280]{2,1,0:T(8,128)(2,1)S(1)}, bf16[1,64,1280]{2,1,0:T(8,128)(2,1)}, u32[]{:S(2)}) %copy-start.3) | copy-done | bytes 163864
  2.9 2.6 %collective-permute-start.1 = (bf16[64,640]{1,0:T(8,128)(2,1)S(1)}, bf16[64,640]{1,0:T(8,128)(2,1)S(1)}, u32[]{:S(2)}, u32[]{:S(2)}) collective-permute-start(bf16[64,640]{1,0:T(8,128)(2,1)S(1)} %get-tuple-element.25), channel_id=1, source_target_pairs={{0,2},{1,3},{2,0},{3,1},{4,6},{5,7},{6,4},{7,5},{8,10},{9,11},{10,... | collective-permute-start | bytes 245768 | tf_op jit(solution)/shard_map/ppermute | solution.py:333
  5.5 1.8 %collective-permute-start.3 = (bf16[64,640]{1,0:T(8,128)(2,1)S(1)}, bf16[64,640]{1,0:T(8,128)(2,1)S(1)}, u32[]{:S(2)}, u32[]{:S(2)}) collective-permute-start(bf16[64,640]{1,0:T(8,128)(2,1)S(1)} %get-tuple-element.27), channel_id=1, source_target_pairs={{0,4},{1,5},{2,6},{3,7},{4,0},{5,1},{6,2},{7,3},{8,12},{9,13},{10,... | collective-permute-start | bytes 245768 | tf_op jit(solution)/shard_map/ppermute | solution.py:333
  7.3 2.6 %collective-permute-start.5 = (bf16[64,640]{1,0:T(8,128)(2,1)S(1)}, bf16[64,640]{1,0:T(8,128)(2,1)S(1)}, u32[]{:S(2)}, u32[]{:S(2)}) collective-permute-start(bf16[64,640]{1,0:T(8,128)(2,1)S(1)} %get-tuple-element.29), channel_id=1, source_target_pairs={{0,6},{1,7},{2,4},{3,5},{4,2},{5,3},{6,0},{7,1},{8,14},{9,15},{10,... | collective-permute-start | bytes 245768 | tf_op jit(solution)/shard_map/ppermute | solution.py:333
  10.5 0.8 %reshape.8.bias_ref = f32[640,1]{1,0:T(8,128)S(1)} reshape(f32[640]{0:T(1024)} %param.12) | data formatting | bytes 5120 | tf_op jit(solution)/shard_map/reshape | solution.py:383
  11.3 0.7 %reshape.6.gain_ref = f32[1,1280]{1,0:T(1,128)S(1)} reshape(f32[1280]{0:T(1024)} %param.10) | data formatting | bytes 10240 | tf_op jit(solution)/shard_map/reshape | solution.py:383
  12.7 0.7 %layout.1 = (bf16[512,512]{1,0:T(8,128)(2,1)S(1)}, f32[1,512]{1,0:T(1,128)S(1)}, f32[1,128]{1,0:T(1,128)S(1)}, f32[1,1280]{1,0:T(1,128)S(1)}, f32[640,1]{1,0:T(8,128)S(1)}) custom-call(s32[1,2]{1,0:T(1,128)S(1)} %copy-done.4, f32[1,1280]{1,0:T(1,128)S(1)} %reshape.6.gain_ref, f32[640,1]{1,0:T(8,128)S(1)} %reshape.8.bias_ref, ...), custom_call_target="tpu_custom_call" | custom-call | bytes 1048576 | tf_op jit(solution)/shard_map/layout/pallas_call | solution.py:369
  13.4 1.4 %collective-permute-done.4.rest_5_ = bf16[64,640]{1,0:T(8,128)(2,1)S(1)} collective-permute-done((bf16[64,640]{1,0:T(8,128)(2,1)S(1)}, bf16[64,640]{1,0:T(8,128)(2,1)S(1)}, u32[]{:S(2)}, u32[]{:S(2)}) %collective-permute-start.4) | collective-permute-done | bytes 81952 | tf_op jit(solution)/shard_map/ppermute | solution.py:333
  15.2 1.3 %attend.1.token_ref.rest_0_ = bf16[640,128]{1,0:T(8,128)(2,1)S(1)} custom-call(bf16[512,512]{1,0:T(8,128)(2,1)S(1)} %get-tuple-element.22.select_ref, f32[1,512]{1,0:T(1,128)S(1)} %get-tuple-element.23.dead_ref, bf16[64,640]{1,0:T(8,128)(2,1)S(1)} %get-tuple-element.21.token_ref.rest_0_, bf16[64,640]{1,0:T(8,128)(2,1)S(1)} %collective-permute-done.rest_1_, ...), custom_call_target="tpu_custom_call" | custom-call | flops 402653184 | bytes 1048576 | tf_op jit(solution)/shard_map/attend/pallas_call | solution.py:384
  16.6 1.5 %collective-permute-start.10 = (bf16[640,128]{1,0:T(8,128)(2,1)S(1)}, bf16[640,128]{1,0:T(8,128)(2,1)S(1)}, u32[]{:S(2)}, u32[]{:S(2)}) collective-permute-start(bf16[640,128]{1,0:T(8,128)(2,1)S(1)} %attend.1.token_ref.rest_0_), channel_id=1, source_target_pairs={{0,4},{1,5},{2,6},{3,7},{4,0},{5,1},{6,2},{7,3},{8,12},{9,13},{10,... | collective-permute-start | bytes 491528 | tf_op jit(solution)/shard_map/ppermute | solution.py:333
  18.1 1.8 %collective-permute-start.12 = (bf16[640,128]{1,0:T(8,128)(2,1)S(1)}, bf16[640,128]{1,0:T(8,128)(2,1)S(1)}, u32[]{:S(2)}, u32[]{:S(2)}) collective-permute-start(bf16[640,128]{1,0:T(8,128)(2,1)S(1)} %attend.1.token_ref.rest_0_), channel_id=1, source_target_pairs={{0,6},{1,7},{2,4},{3,5},{4,2},{5,3},{6,0},{7,1},{8,14},{9,15},{10,... | collective-permute-start | bytes 491528 | tf_op jit(solution)/shard_map/ppermute | solution.py:333
  20.4 1.7 %collective-permute-start.14 = (bf16[400,128]{1,0:T(8,128)(2,1)S(1)}, bf16[400,128]{1,0:T(8,128)(2,1)S(1)}, u32[]{:S(2)}, u32[]{:S(2)}) collective-permute-start(bf16[400,128]{1,0:T(8,128)(2,1)S(1)} %weight_slice.1.rest_8_), channel_id=1, source_target_pairs={{0,8},{8,16},{16,24},{24,0},{1,9},{9,17},{17,25},{25,1},{2,10},{10... | collective-permute-start | bytes 307208 | tf_op jit(solution)/shard_map/ppermute | solution.py:368
  22.2 4.8 %collective-permute-done.14.rest_9_ = bf16[400,128]{1,0:T(8,128)(2,1)S(1)} collective-permute-done((bf16[400,128]{1,0:T(8,128)(2,1)S(1)}, bf16[400,128]{1,0:T(8,128)(2,1)S(1)}, u32[]{:S(2)}, u32[]{:S(2)}) %collective-permute-start.14) | collective-permute-done | bytes 102432 | tf_op jit(solution)/shard_map/ppermute | solution.py:368
  28.0 5.4 %collective-permute-done.15.rest_10_ = bf16[400,128]{1,0:T(8,128)(2,1)S(1)} collective-permute-done((bf16[400,128]{1,0:T(8,128)(2,1)S(1)}, bf16[400,128]{1,0:T(8,128)(2,1)S(1)}, u32[]{:S(2)}, u32[]{:S(2)}) %collective-permute-start.15) | collective-permute-done | bytes 102432 | tf_op jit(solution)/shard_map/ppermute | solution.py:368
  33.4 6.5 %collective-permute-done.16.rest_11_ = bf16[400,128]{1,0:T(8,128)(2,1)S(1)} collective-permute-done((bf16[400,128]{1,0:T(8,128)(2,1)S(1)}, bf16[400,128]{1,0:T(8,128)(2,1)S(1)}, u32[]{:S(2)}, u32[]{:S(2)}) %collective-permute-start.16) | collective-permute-done | bytes 102432 | tf_op jit(solution)/shard_map/ppermute | solution.py:368
  40.4 1.2 %project.1.token_ref.rest_0_ = bf16[640,128]{1,0:T(8,128)(2,1)S(1)} custom-call(bf16[640,128]{1,0:T(8,128)(2,1)S(1)} %attend.1.token_ref.rest_0_, bf16[640,128]{1,0:T(8,128)(2,1)S(1)} %collective-permute-done.7.rest_1_, bf16[640,128]{1,0:T(8,128)(2,1)S(1)} %collective-permute-done.8.rest_2_, bf16[640,128]{1,0:T(8,128)(2,1)S(1)} %collective-permute-done.9.rest_3_, ...), custom_call_target="tpu_custom_call" | custom-call | flops 536870912 | bytes 4194304 | tf_op jit(solution)/shard_map/project/pallas_call | solution.py:403
  41.6 1.9 %collective-permute-start.18 = (bf16[640,128]{1,0:T(8,128)(2,1)S(1)}, bf16[640,128]{1,0:T(8,128)(2,1)S(1)}, u32[]{:S(2)}, u32[]{:S(2)}) collective-permute-start(bf16[640,128]{1,0:T(8,128)(2,1)S(1)} %project.1.token_ref.rest_0_), channel_id=1, source_target_pairs={{0,2},{1,3},{2,0},{3,1},{4,6},{5,7},{6,4},{7,5},{8,10},{9,11},{10,... | collective-permute-start | bytes 491528 | tf_op jit(solution)/shard_map/ppermute | solution.py:333
  43.5 1.1 %collective-permute-start.20 = (bf16[640,128]{1,0:T(8,128)(2,1)S(1)}, bf16[640,128]{1,0:T(8,128)(2,1)S(1)}, u32[]{:S(2)}, u32[]{:S(2)}) collective-permute-start(bf16[640,128]{1,0:T(8,128)(2,1)S(1)} %project.1.token_ref.rest_0_), channel_id=1, source_target_pairs={{0,4},{1,5},{2,6},{3,7},{4,0},{5,1},{6,2},{7,3},{8,12},{9,13},{10,... | collective-permute-start | bytes 491528 | tf_op jit(solution)/shard_map/ppermute | solution.py:333
  45.2 1.8 %collective-permute-done.18.rest_2_ = bf16[640,128]{1,0:T(8,128)(2,1)S(1)} collective-permute-done((bf16[640,128]{1,0:T(8,128)(2,1)S(1)}, bf16[640,128]{1,0:T(8,128)(2,1)S(1)}, u32[]{:S(2)}, u32[]{:S(2)}) %collective-permute-start.18) | collective-permute-done | bytes 163872 | tf_op jit(solution)/shard_map/ppermute | solution.py:333
  47.0 1.8 %collective-permute-done.20.rest_4_ = bf16[640,128]{1,0:T(8,128)(2,1)S(1)} collective-permute-done((bf16[640,128]{1,0:T(8,128)(2,1)S(1)}, bf16[640,128]{1,0:T(8,128)(2,1)S(1)}, u32[]{:S(2)}, u32[]{:S(2)}) %collective-permute-start.20) | collective-permute-done | bytes 163872 | tf_op jit(solution)/shard_map/ppermute | solution.py:333
  48.8 2.0 %collective-permute-done.22.rest_6_ = bf16[640,128]{1,0:T(8,128)(2,1)S(1)} collective-permute-done((bf16[640,128]{1,0:T(8,128)(2,1)S(1)}, bf16[640,128]{1,0:T(8,128)(2,1)S(1)}, u32[]{:S(2)}, u32[]{:S(2)}) %collective-permute-start.22) | collective-permute-done | bytes 163872 | tf_op jit(solution)/shard_map/ppermute | solution.py:333
  50.9 1.2 %merge_tail.1.rest_9_ = bf16[640,1024]{1,0:T(8,128)(2,1)S(1)} custom-call(bf16[640,5120]{1,0:T(8,128)(2,1)S(1)} %copy-done, bf16[640,128]{1,0:T(8,128)(2,1)S(1)} %project.1.token_ref.rest_0_), custom_call_target="tpu_custom_call" | custom-call | bytes 4194304 | tf_op jit(solution)/shard_map/merge_tail/pallas_call | solution.py:412
  52.2 3.3 %merge.1 = bf16[1,640,128]{2,1,0:T(8,128)(2,1)} custom-call(bf16[640,128]{1,0:T(8,128)(2,1)S(1)} %project.1.token_ref.rest_0_, bf16[640,128]{1,0:T(8,128)(2,1)S(1)} %collective-permute-done.17.rest_1_, bf16[640,128]{1,0:T(8,128)(2,1)S(1)} %collective-permute-done.18.rest_2_, bf16[640,128]{1,0:T(8,128)(2,1)S(1)} %collective-permute-done.19.rest_3_, ...), custom_call_target="tpu_custom_call" | custom-call | flops 838860800 | bytes 8388608 | tf_op jit(solution)/shard_map/merge/pallas_call | solution.py:413
  (44 shorter events, 5.4 us)
Async XLA Ops:
  2.4 4.9 %collective-permute-start = (bf16[64,640]{1,0:T(8,128)(2,1)S(1)}, bf16[64,640]{1,0:T(8,128)(2,1)S(1)}, u32[]{:S(2)}, u32[]{:S(2)}) collective-permute-start(bf16[64,640]{1,0:T(8,128)(2,1)S(1)} %get-tuple-element.24), channel_id=1, source_target_pairs={{0,1},{1,0},{2,3},{3,2},{4,5},{5,4},{6,7},{7,6},{8,9},{9,8},{10,11... | collective-permute-start | bytes 245768 | tf_op jit(solution)/shard_map/ppermute | solution.py:333
  2.9 7.0 %collective-permute-start.1 = (bf16[64,640]{1,0:T(8,128)(2,1)S(1)}, bf16[64,640]{1,0:T(8,128)(2,1)S(1)}, u32[]{:S(2)}, u32[]{:S(2)}) collective-permute-start(bf16[64,640]{1,0:T(8,128)(2,1)S(1)} %get-tuple-element.25), channel_id=1, source_target_pairs={{0,2},{1,3},{2,0},{3,1},{4,6},{5,7},{6,4},{7,5},{8,10},{9,11},{10,... | collective-permute-start | bytes 245768 | tf_op jit(solution)/shard_map/ppermute | solution.py:333
  5.4 7.9 %collective-permute-start.2 = (bf16[64,640]{1,0:T(8,128)(2,1)S(1)}, bf16[64,640]{1,0:T(8,128)(2,1)S(1)}, u32[]{:S(2)}, u32[]{:S(2)}) collective-permute-start(bf16[64,640]{1,0:T(8,128)(2,1)S(1)} %get-tuple-element.26), channel_id=1, source_target_pairs={{0,3},{1,2},{2,1},{3,0},{4,7},{5,6},{6,5},{7,4},{8,11},{9,10},{10,... | collective-permute-start | bytes 245768 | tf_op jit(solution)/shard_map/ppermute | solution.py:333
  5.5 7.9 %collective-permute-start.3 = (bf16[64,640]{1,0:T(8,128)(2,1)S(1)}, bf16[64,640]{1,0:T(8,128)(2,1)S(1)}, u32[]{:S(2)}, u32[]{:S(2)}) collective-permute-start(bf16[64,640]{1,0:T(8,128)(2,1)S(1)} %get-tuple-element.27), channel_id=1, source_target_pairs={{0,4},{1,5},{2,6},{3,7},{4,0},{5,1},{6,2},{7,3},{8,12},{9,13},{10,... | collective-permute-start | bytes 245768 | tf_op jit(solution)/shard_map/ppermute | solution.py:333
  7.3 7.5 %collective-permute-start.4 = (bf16[64,640]{1,0:T(8,128)(2,1)S(1)}, bf16[64,640]{1,0:T(8,128)(2,1)S(1)}, u32[]{:S(2)}, u32[]{:S(2)}) collective-permute-start(bf16[64,640]{1,0:T(8,128)(2,1)S(1)} %get-tuple-element.28), channel_id=1, source_target_pairs={{0,5},{1,4},{2,7},{3,6},{4,1},{5,0},{6,3},{7,2},{8,13},{9,12},{10,... | collective-permute-start | bytes 245768 | tf_op jit(solution)/shard_map/ppermute | solution.py:333
  7.3 7.5 %collective-permute-start.5 = (bf16[64,640]{1,0:T(8,128)(2,1)S(1)}, bf16[64,640]{1,0:T(8,128)(2,1)S(1)}, u32[]{:S(2)}, u32[]{:S(2)}) collective-permute-start(bf16[64,640]{1,0:T(8,128)(2,1)S(1)} %get-tuple-element.29), channel_id=1, source_target_pairs={{0,6},{1,7},{2,4},{3,5},{4,2},{5,3},{6,0},{7,1},{8,14},{9,15},{10,... | collective-permute-start | bytes 245768 | tf_op jit(solution)/shard_map/ppermute | solution.py:333
  9.9 5.3 %collective-permute-start.6 = (bf16[64,640]{1,0:T(8,128)(2,1)S(1)}, bf16[64,640]{1,0:T(8,128)(2,1)S(1)}, u32[]{:S(2)}, u32[]{:S(2)}) collective-permute-start(bf16[64,640]{1,0:T(8,128)(2,1)S(1)} %get-tuple-element.30), channel_id=1, source_target_pairs={{0,7},{1,6},{2,5},{3,4},{4,3},{5,2},{6,1},{7,0},{8,15},{9,14},{10,... | collective-permute-start | bytes 245768 | tf_op jit(solution)/shard_map/ppermute | solution.py:333
  16.6 10.4 %collective-permute-start.10 = (bf16[640,128]{1,0:T(8,128)(2,1)S(1)}, bf16[640,128]{1,0:T(8,128)(2,1)S(1)}, u32[]{:S(2)}, u32[]{:S(2)}) collective-permute-start(bf16[640,128]{1,0:T(8,128)(2,1)S(1)} %attend.1.token_ref.rest_0_), channel_id=1, source_target_pairs={{0,4},{1,5},{2,6},{3,7},{4,0},{5,1},{6,2},{7,3},{8,12},{9,13},{10,... | collective-permute-start | bytes 491528 | tf_op jit(solution)/shard_map/ppermute | solution.py:333
  18.1 9.4 %collective-permute-start.12 = (bf16[640,128]{1,0:T(8,128)(2,1)S(1)}, bf16[640,128]{1,0:T(8,128)(2,1)S(1)}, u32[]{:S(2)}, u32[]{:S(2)}) collective-permute-start(bf16[640,128]{1,0:T(8,128)(2,1)S(1)} %attend.1.token_ref.rest_0_), channel_id=1, source_target_pairs={{0,6},{1,7},{2,4},{3,5},{4,2},{5,3},{6,0},{7,1},{8,14},{9,15},{10,... | collective-permute-start | bytes 491528 | tf_op jit(solution)/shard_map/ppermute | solution.py:333
  19.9 7.8 %collective-permute-start.8 = (bf16[640,128]{1,0:T(8,128)(2,1)S(1)}, bf16[640,128]{1,0:T(8,128)(2,1)S(1)}, u32[]{:S(2)}, u32[]{:S(2)}) collective-permute-start(bf16[640,128]{1,0:T(8,128)(2,1)S(1)} %attend.1.token_ref.rest_0_), channel_id=1, source_target_pairs={{0,2},{1,3},{2,0},{3,1},{4,6},{5,7},{6,4},{7,5},{8,10},{9,11},{10,... | collective-permute-start | bytes 491528 | tf_op jit(solution)/shard_map/ppermute | solution.py:333
  20.4 6.5 %collective-permute-start.14 = (bf16[400,128]{1,0:T(8,128)(2,1)S(1)}, bf16[400,128]{1,0:T(8,128)(2,1)S(1)}, u32[]{:S(2)}, u32[]{:S(2)}) collective-permute-start(bf16[400,128]{1,0:T(8,128)(2,1)S(1)} %weight_slice.1.rest_8_), channel_id=1, source_target_pairs={{0,8},{8,16},{16,24},{24,0},{1,9},{9,17},{17,25},{25,1},{2,10},{10... | collective-permute-start | bytes 307208 | tf_op jit(solution)/shard_map/ppermute | solution.py:368
  26.9 6.5 %collective-permute-start.15 = (bf16[400,128]{1,0:T(8,128)(2,1)S(1)}, bf16[400,128]{1,0:T(8,128)(2,1)S(1)}, u32[]{:S(2)}, u32[]{:S(2)}) collective-permute-start(bf16[400,128]{1,0:T(8,128)(2,1)S(1)} %collective-permute-done.14.rest_9_), channel_id=1, source_target_pairs={{0,8},{8,16},{16,24},{24,0},{1,9},{9,17},{17,25},{25,1},{2,10},{10... | collective-permute-start | bytes 307208 | tf_op jit(solution)/shard_map/ppermute | solution.py:368
  26.9 13.5 %collective-permute-start.7 = (bf16[640,128]{1,0:T(8,128)(2,1)S(1)}, bf16[640,128]{1,0:T(8,128)(2,1)S(1)}, u32[]{:S(2)}, u32[]{:S(2)}) collective-permute-start(bf16[640,128]{1,0:T(8,128)(2,1)S(1)} %attend.1.token_ref.rest_0_), channel_id=1, source_target_pairs={{0,1},{1,0},{2,3},{3,2},{4,5},{5,4},{6,7},{7,6},{8,9},{9,8},{10,11... | collective-permute-start | bytes 491528 | tf_op jit(solution)/shard_map/ppermute | solution.py:333
  26.9 13.5 %collective-permute-start.11 = (bf16[640,128]{1,0:T(8,128)(2,1)S(1)}, bf16[640,128]{1,0:T(8,128)(2,1)S(1)}, u32[]{:S(2)}, u32[]{:S(2)}) collective-permute-start(bf16[640,128]{1,0:T(8,128)(2,1)S(1)} %collective-permute-done.10.rest_4_), channel_id=1, source_target_pairs={{0,1},{1,0},{2,3},{3,2},{4,5},{5,4},{6,7},{7,6},{8,9},{9,8},{10,11... | collective-permute-start | bytes 491528 | tf_op jit(solution)/shard_map/ppermute | solution.py:333
  27.5 13.0 %collective-permute-start.13 = (bf16[640,128]{1,0:T(8,128)(2,1)S(1)}, bf16[640,128]{1,0:T(8,128)(2,1)S(1)}, u32[]{:S(2)}, u32[]{:S(2)}) collective-permute-start(bf16[640,128]{1,0:T(8,128)(2,1)S(1)} %collective-permute-done.12.rest_6_), channel_id=1, source_target_pairs={{0,1},{1,0},{2,3},{3,2},{4,5},{5,4},{6,7},{7,6},{8,9},{9,8},{10,11... | collective-permute-start | bytes 491528 | tf_op jit(solution)/shard_map/ppermute | solution.py:333
  27.7 12.8 %collective-permute-start.9 = (bf16[640,128]{1,0:T(8,128)(2,1)S(1)}, bf16[640,128]{1,0:T(8,128)(2,1)S(1)}, u32[]{:S(2)}, u32[]{:S(2)}) collective-permute-start(bf16[640,128]{1,0:T(8,128)(2,1)S(1)} %collective-permute-done.8.rest_2_), channel_id=1, source_target_pairs={{0,1},{1,0},{2,3},{3,2},{4,5},{5,4},{6,7},{7,6},{8,9},{9,8},{10,11... | collective-permute-start | bytes 491528 | tf_op jit(solution)/shard_map/ppermute | solution.py:333
  33.4 6.5 %collective-permute-start.16 = (bf16[400,128]{1,0:T(8,128)(2,1)S(1)}, bf16[400,128]{1,0:T(8,128)(2,1)S(1)}, u32[]{:S(2)}, u32[]{:S(2)}) collective-permute-start(bf16[400,128]{1,0:T(8,128)(2,1)S(1)} %collective-permute-done.15.rest_10_), channel_id=1, source_target_pairs={{0,8},{8,16},{16,24},{24,0},{1,9},{9,17},{17,25},{25,1},{2,10},{10... | collective-permute-start | bytes 307208 | tf_op jit(solution)/shard_map/ppermute | solution.py:368
  41.6 5.4 %collective-permute-start.18 = (bf16[640,128]{1,0:T(8,128)(2,1)S(1)}, bf16[640,128]{1,0:T(8,128)(2,1)S(1)}, u32[]{:S(2)}, u32[]{:S(2)}) collective-permute-start(bf16[640,128]{1,0:T(8,128)(2,1)S(1)} %project.1.token_ref.rest_0_), channel_id=1, source_target_pairs={{0,2},{1,3},{2,0},{3,1},{4,6},{5,7},{6,4},{7,5},{8,10},{9,11},{10,... | collective-permute-start | bytes 491528 | tf_op jit(solution)/shard_map/ppermute | solution.py:333
  43.5 5.3 %collective-permute-start.20 = (bf16[640,128]{1,0:T(8,128)(2,1)S(1)}, bf16[640,128]{1,0:T(8,128)(2,1)S(1)}, u32[]{:S(2)}, u32[]{:S(2)}) collective-permute-start(bf16[640,128]{1,0:T(8,128)(2,1)S(1)} %project.1.token_ref.rest_0_), channel_id=1, source_target_pairs={{0,4},{1,5},{2,6},{3,7},{4,0},{5,1},{6,2},{7,3},{8,12},{9,13},{10,... | collective-permute-start | bytes 491528 | tf_op jit(solution)/shard_map/ppermute | solution.py:333
  44.6 6.2 %collective-permute-start.22 = (bf16[640,128]{1,0:T(8,128)(2,1)S(1)}, bf16[640,128]{1,0:T(8,128)(2,1)S(1)}, u32[]{:S(2)}, u32[]{:S(2)}) collective-permute-start(bf16[640,128]{1,0:T(8,128)(2,1)S(1)} %project.1.token_ref.rest_0_), channel_id=1, source_target_pairs={{0,6},{1,7},{2,4},{3,5},{4,2},{5,3},{6,0},{7,1},{8,14},{9,15},{10,... | collective-permute-start | bytes 491528 | tf_op jit(solution)/shard_map/ppermute | solution.py:333
  45.2 6.9 %collective-permute-start.17 = (bf16[640,128]{1,0:T(8,128)(2,1)S(1)}, bf16[640,128]{1,0:T(8,128)(2,1)S(1)}, u32[]{:S(2)}, u32[]{:S(2)}) collective-permute-start(bf16[640,128]{1,0:T(8,128)(2,1)S(1)} %project.1.token_ref.rest_0_), channel_id=1, source_target_pairs={{0,1},{1,0},{2,3},{3,2},{4,5},{5,4},{6,7},{7,6},{8,9},{9,8},{10,11... | collective-permute-start | bytes 491528 | tf_op jit(solution)/shard_map/ppermute | solution.py:333
  47.0 5.1 %collective-permute-start.19 = (bf16[640,128]{1,0:T(8,128)(2,1)S(1)}, bf16[640,128]{1,0:T(8,128)(2,1)S(1)}, u32[]{:S(2)}, u32[]{:S(2)}) collective-permute-start(bf16[640,128]{1,0:T(8,128)(2,1)S(1)} %collective-permute-done.18.rest_2_), channel_id=1, source_target_pairs={{0,1},{1,0},{2,3},{3,2},{4,5},{5,4},{6,7},{7,6},{8,9},{9,8},{10,11... | collective-permute-start | bytes 491528 | tf_op jit(solution)/shard_map/ppermute | solution.py:333
  48.8 3.3 %collective-permute-start.21 = (bf16[640,128]{1,0:T(8,128)(2,1)S(1)}, bf16[640,128]{1,0:T(8,128)(2,1)S(1)}, u32[]{:S(2)}, u32[]{:S(2)}) collective-permute-start(bf16[640,128]{1,0:T(8,128)(2,1)S(1)} %collective-permute-done.20.rest_4_), channel_id=1, source_target_pairs={{0,1},{1,0},{2,3},{3,2},{4,5},{5,4},{6,7},{7,6},{8,9},{9,8},{10,11... | collective-permute-start | bytes 491528 | tf_op jit(solution)/shard_map/ppermute | solution.py:333
  50.8 1.4 %collective-permute-start.23 = (bf16[640,128]{1,0:T(8,128)(2,1)S(1)}, bf16[640,128]{1,0:T(8,128)(2,1)S(1)}, u32[]{:S(2)}, u32[]{:S(2)}) collective-permute-start(bf16[640,128]{1,0:T(8,128)(2,1)S(1)} %collective-permute-done.22.rest_6_), channel_id=1, source_target_pairs={{0,1},{1,0},{2,3},{3,2},{4,5},{5,4},{6,7},{7,6},{8,9},{9,8},{10,11... | collective-permute-start | bytes 491528 | tf_op jit(solution)/shard_map/ppermute | solution.py:333
  (5 other events, 53.5 us)

commit v3 on v2

--- a/solution.py
+++ b/solution.py
@@ -121,6 +121,7 @@
 WIDE = 128
 REST = HPAIR - WIDE
 MAIN = ROWS * WIDE
+NOTES = 16
 ROOT = math.log2(math.e) / math.sqrt(HDIM)
 BF16 = jnp.bfloat16
 F32 = jnp.float32
@@ -135,38 +136,47 @@
     return jnp.concatenate([wide[at * groups : (at + 1) * groups] for at in range(4)], axis=1)
 
 
-def spread_kernel(qkv_ref, resid_ref, *rest):
-    outs, held = rest[:ROWS], rest[ROWS]
+def spread_kernel(qkv_hbm, resid_hbm, weight_hbm, grid_hbm, *rest):
+    outs = rest[:ROWS]
+    slice_ref, grid_out, qkv, resid, tile, held, grid, sems = rest[ROWS:]
     me = row_index()
+    depth = weight_hbm.shape[0]
+    main = pl.ds(pl.multiple_of(me * WIDE, WIDE), WIDE)
+    ends = pl.ds(pl.multiple_of(MAIN + me // 4 * WIDE, WIDE), WIDE)
+    copies = [
+        pltpu.make_async_copy(qkv_hbm.at[0], qkv, sems.at[0]),
+        pltpu.make_async_copy(resid_hbm.at[0], resid, sems.at[1]),
+        pltpu.make_async_copy(weight_hbm.at[:, main], slice_ref.at[:depth], sems.at[2]),
+        pltpu.make_async_copy(weight_hbm.at[:, ends], tile, sems.at[3]),
+        pltpu.make_async_copy(grid_hbm, grid, sems.at[4]),
+    ]
+    for copy in copies:
+        copy.start()
+    for copy in copies:
+        copy.wait()
     for dest in range(ROWS):
         at = dest * HPAIR
-        resid = [resid_ref[0, :, dest * WIDE : (dest + 1) * WIDE]]
-        resid.append(resid_ref[0, :, MAIN + dest * REST : MAIN + (dest + 1) * REST])
-        parts = [qkv_ref[0, :, part * D + at : part * D + at + HPAIR] for part in range(3)]
-        held[dest] = jnp.concatenate(parts + resid, axis=1)
+        parts = [qkv[:, part * D + at : part * D + at + HPAIR] for part in range(3)]
+        parts.append(resid[:, dest * WIDE : (dest + 1) * WIDE])
+        parts.append(resid[:, MAIN + dest * REST : MAIN + (dest + 1) * REST])
+        held[dest] = jnp.concatenate(parts, axis=1)
     for step in range(ROWS):
         outs[step][...] = held[me ^ step]
-
-
-def slice_kernel(weight_ref, token_ref, out_ref):
-    del token_ref
-    me = row_index()
-    depth = weight_ref.shape[0]
-    out_ref[:depth, :] = weight_ref[:, pl.ds(pl.multiple_of(me * WIDE, WIDE), WIDE)]
-    tile = weight_ref[:, pl.ds(pl.multiple_of(MAIN + me // 4 * WIDE, WIDE), WIDE)]
     tail = tile[:, :REST]
     for at in range(1, 4):
         tail = jnp.where(lax.rem(me, 4) == at, tile[:, at * REST : (at + 1) * REST], tail)
-    out_ref[depth:, :] = pack_tail(tail)
-
-
-def layout_kernel(grid_ref, gain_ref, bias_ref, token_ref, select_ref, keys_ref, live_ref, gain_out, bias_out):
-    del token_ref
-    rows_n, cols_n = grid_ref[0, 0], grid_ref[0, 1]
+    slice_ref[depth:, :] = pack_tail(tail)
+    row = lax.broadcasted_iota(jnp.int32, grid_out.shape, 0)
+    grid_out[...] = jnp.where(row == 0, grid[0, 0], grid[0, 1])
+
+
+def layout_kernel(grid_ref, gain_ref, bias_ref, early_ref, select_ref, keys_ref, live_ref, gain_out, bias_out):
+    del early_ref
+    rows_n, cols_n = grid_ref[:1, :1], grid_ref[1:2, :1]
     patches = select_ref.shape[0]
     groups = patches // 4
-    half = cols_n // 2
-    count = (rows_n // 2) * half
+    half = cols_n >> 1
+    count = (rows_n >> 1) * half
     slots = lax.broadcasted_iota(jnp.int32, (groups, 1), 0)
     line = jnp.floor((slots.astype(F32) + 0.5) / half.astype(F32)).astype(jnp.int32)
     first = 2 * line * cols_n + 2 * (slots - line * half)
@@ -178,8 +188,9 @@
     keys_ref[...] = jnp.where(key < rows_n * cols_n, 0.0, -1e30)
     slot = lax.broadcasted_iota(jnp.int32, live_ref.shape, 1)
     live_ref[...] = jnp.where(slot < count, 1.0, 0.0)
-    gain_out[...] = gain_ref[...]
-    bias_out[...] = bias_ref[...]
+    gain_out[...] = gain_ref[...].reshape(gain_out.shape)
+    bias = jnp.broadcast_to(bias_ref[...].reshape(1, bias_out.shape[0]), (8, bias_out.shape[0]))
+    bias_out[...] = bias.T[:, :1]
 
 
 def attend_kernel(select_ref, dead_ref, *rest):
@@ -209,10 +220,10 @@
     out_ref[patches:, :] = pack_tail(attn[:, WIDE:]).astype(BF16)
 
 
-def ready_kernel(select_ref, token_ref, *rest):
+def ready_kernel(select_ref, gain_ref, token_ref, *rest):
     del token_ref
     blocks, slices = rest[:ROWS], rest[ROWS : ROWS + PAGES]
-    resid_ref, main_ref, tail_ref, held = rest[ROWS + PAGES :]
+    resid_ref, gain_out, main_ref, tail_ref, held = rest[ROWS + PAGES :]
     me = row_index()
     page = lax.axis_index("page")
     band = blocks[0].shape[0]
@@ -220,6 +231,12 @@
         at = pl.ds(pl.multiple_of((me ^ step) * band, band), band)
         held[at, :] = blocks[step][:, 3 * HPAIR :]
     resid_ref[...] = jnp.dot(select_ref[...], held[...], preferred_element_type=F32)
+    gain = jnp.zeros(gain_out.shape, F32)
+    for pair in range(ROWS):
+        parts = [gain_ref[:, pair * WIDE : (pair + 1) * WIDE]]
+        parts.append(gain_ref[:, MAIN + pair * REST : MAIN + (pair + 1) * REST])
+        gain = jnp.where(me == pair, jnp.concatenate(parts, axis=1), gain)
+    gain_out[...] = gain
     tail_ref[...] = jnp.zeros_like(tail_ref)
     depth = 2 * HPAIR
     for step in range(PAGES):
@@ -244,18 +261,31 @@
 
 def project_kernel(*rest):
     pieces = rest[:ROWS]
-    main_ref, tail_ref, resid_ref, out_ref, full = rest[ROWS:]
+    main_ref, tail_ref, resid_ref, gain_ref, out_ref, full = rest[ROWS:]
     collect(pieces, full)
     patches = resid_ref.shape[0]
     groups = patches // 4
-    hidden = jnp.dot(full[:patches], main_ref[...], preferred_element_type=F32) + resid_ref[...]
+    base = jnp.dot(full[:patches], main_ref[...], preferred_element_type=F32) + resid_ref[...]
+    ones = jnp.ones((NOTES, HPAIR), BF16)
+    contract = (((1,), (1,)), ((), ()))
+    row = lax.broadcasted_iota(jnp.int32, (NOTES, groups), 0)
+    notes = jnp.zeros((NOTES, groups), F32)
     ends = []
     for corner in range(4):
         span = slice(corner * groups, (corner + 1) * groups)
-        part = hidden[span] + jnp.dot(full[patches:], tail_ref[corner], preferred_element_type=F32)
-        out_ref[span, :] = part[:, :WIDE].astype(BF16)
-        ends.append(part[:, WIDE:])
-    out_ref[patches:, :] = jnp.concatenate(ends, axis=1).astype(BF16)
+        hidden = base[span] + jnp.dot(full[patches:], tail_ref[corner], preferred_element_type=F32)
+        square = hidden * hidden
+        high = square.astype(BF16)
+        low = (square - high.astype(F32)).astype(BF16)
+        total = lax.dot_general(ones, high, contract, preferred_element_type=F32)
+        total = total + lax.dot_general(ones, low, contract, preferred_element_type=F32)
+        coarse = total.astype(BF16).astype(F32)
+        notes = jnp.where(row == corner, coarse, jnp.where(row == 4 + corner, total - coarse, notes))
+        sent = hidden * gain_ref[...]
+        out_ref[span, :] = sent[:, :WIDE].astype(BF16)
+        ends.append(sent[:, WIDE:])
+    out_ref[patches : patches + groups, :] = jnp.concatenate(ends, axis=1).astype(BF16)
+    out_ref[patches + groups :, :] = notes.astype(BF16)
 
 
 def tail_kernel(weight_ref, token_ref, out_ref):
@@ -269,49 +299,34 @@
 
 def merge_kernel(*rest):
     pieces = rest[:ROWS]
-    weight_ref, tail_ref, gain_ref, bias_ref, live_ref, out_ref, full = rest[ROWS:]
+    weight_ref, tail_ref, bias_ref, live_ref, out_ref, full = rest[ROWS:]
     collect(pieces, full)
     groups = live_ref.shape[1]
     patches = 4 * groups
-    gain = gain_ref[...]
-    ends = full[patches:].astype(F32)
-    squares = ends * ends
-    folded = squares[:, :WIDE]
-    for pair in range(1, ROWS):
-        folded = folded + squares[:, pair * WIDE : (pair + 1) * WIDE]
-    lane = lax.broadcasted_iota(jnp.int32, (1, WIDE), 1)
+    notes = jnp.zeros((NOTES, groups), F32)
+    for step in range(ROWS):
+        notes = notes + pieces[step][patches + groups :].astype(F32)
+    scale = lax.rsqrt((notes[:4] + notes[4:8]) * (1.0 / D) + 1e-06)
     contract = (((1,), (1,)), ((), ()))
     total = jnp.zeros((weight_ref.shape[0], groups), F32)
-    spread = jnp.zeros((groups, WIDE), F32)
     for corner in range(4):
-        mine = (lane >= corner * REST) & (lane < (corner + 1) * REST)
-        rows = full[corner * groups : (corner + 1) * groups].astype(F32)
-        square = jnp.sum(rows * rows, axis=1, keepdims=True)
-        square = square + jnp.sum(jnp.where(mine, folded, 0.0), axis=1, keepdims=True)
-        scale = lax.rsqrt(square * (1.0 / D) + 1e-06)
-        spread = jnp.where(mine, scale, spread)
-        normed = (rows * scale * gain[:, :MAIN]).astype(BF16)
-        total = total + lax.dot_general(
-            weight_ref[:, corner * D : corner * D + MAIN], normed, contract, preferred_element_type=F32
+        total = total + scale[corner : corner + 1] * lax.dot_general(
+            weight_ref[:, corner * D : corner * D + MAIN],
+            full[corner * groups : (corner + 1) * groups],
+            contract,
+            preferred_element_type=F32,
         )
-    normed = []
-    for pair in range(ROWS):
-        piece = gain[:, MAIN + pair * REST : MAIN + (pair + 1) * REST]
-        piece = jnp.concatenate([piece] * 4, axis=1)
-        normed.append((ends[:, pair * WIDE : (pair + 1) * WIDE] * spread * piece).astype(BF16))
-    total = total + lax.dot_general(
-        tail_ref[...], jnp.concatenate(normed, axis=1), contract, preferred_element_type=F32
-    )
+    spread = jnp.concatenate([jnp.broadcast_to(scale[at : at + 1], (REST, groups)) for at in range(4)], axis=0).T
+    ends = full[patches : patches + groups].astype(F32) * jnp.concatenate([spread] * ROWS, axis=1)
+    total = total + lax.dot_general(tail_ref[...], ends.astype(BF16), contract, preferred_element_type=F32)
     total = total + bias_ref[...]
     merged = 0.5 * total * (1.0 + lax.erf(total * math.sqrt(0.5)))
     out_ref[0] = jnp.where(live_ref[...] > 0.0, merged, 0.0).astype(BF16)
 
 
-def kernel(body, name, out_shape, scratch=(), first="vmem", tokens=(), count=0, limit=24, flops=0, moved=0):
-    spaces = {"vmem": pltpu.VMEM, "smem": pltpu.SMEM, "any": pl.ANY}
+def kernel(body, name, out_shape, scratch=(), fetched=(), count=0, limit=24, flops=0, moved=0):
     specs = [pl.BlockSpec(memory_space=pltpu.VMEM) for _ in range(count)]
-    specs[0] = pl.BlockSpec(memory_space=spaces[first])
-    for at in tokens:
+    for at in fetched:
         specs[at] = pl.BlockSpec(memory_space=pl.ANY)
     return pl.pallas_call(
         body,
@@ -333,6 +348,10 @@
     return lax.ppermute(value, "row", [(row, row ^ step) for row in range(ROWS)])
 
 
+def turn(value, step):
+    return lax.ppermute(value, "page", [(page, (page + step) % PAGES) for page in range(PAGES)])
+
+
 def gather_rows(value):
     far = [swap(value, step) for step in (6, 2, 4)]
     near = [swap(piece, 1) for piece in [value] + far]
@@ -345,27 +364,27 @@
     groups = patches // 4
     units = merge_weight.shape[0]
     depth = out_weight.shape[0]
-    piece = shape(patches + groups, WIDE)
-    assembled = pltpu.VMEM((patches + groups, MAIN), BF16)
-
-    sends = kernel(
+    piece = patches + groups
+
+    *sends, own, grid = kernel(
         spread_kernel,
         "spread",
-        [shape(band, 4 * HPAIR)] * ROWS,
-        [pltpu.VMEM((ROWS, band, 4 * HPAIR), BF16)],
-        count=2,
+        [shape(band, 4 * HPAIR)] * ROWS + [shape(depth + depth // 4, WIDE), shape(8, WIDE, dtype=jnp.int32)],
+        [
+            pltpu.VMEM((band, 3 * D), BF16),
+            pltpu.VMEM((band, D), BF16),
+            pltpu.VMEM((depth, WIDE), BF16),
+            pltpu.VMEM((ROWS, band, 4 * HPAIR), BF16),
+            pltpu.SMEM(page_grid.shape, jnp.int32),
+            pltpu.SemaphoreType.DMA((5,)),
+        ],
+        fetched=range(4),
+        count=4,
+        limit=24,
         moved=1 << 20,
-    )(qkv_rows, residual)
-    blocks = [None] * ROWS
-    blocks[0] = sends[0]
-    for step in (6, 7, 2, 4, 3, 5, 1):
-        blocks[step] = swap(sends[step], step)
-    own = kernel(slice_kernel, "weight_slice", shape(depth + depth // 4, WIDE), tokens=(1,), count=2, moved=1 << 20)(
-        out_weight, sends[0]
-    )
-    slices = [own]
-    for _ in range(PAGES - 1):
-        slices.append(lax.ppermute(slices[-1], "page", [(page, (page + 1) % PAGES) for page in range(PAGES)]))
+    )(*[pltpu.with_memory_space_constraint(value, pltpu.HBM) for value in (qkv_rows, residual, out_weight, page_grid)])
+    blocks = [sends[0]] + [swap(sends[step], step) for step in range(1, ROWS)]
+    slices = [own] + [turn(own, step) for step in range(1, PAGES)]
     select, dead, live, gain, bias = kernel(
         layout_kernel,
         "layout",
@@ -376,49 +395,50 @@
             shape(1, D, dtype=F32),
             shape(units, 1, dtype=F32),
         ],
-        first="smem",
-        tokens=(3,),
+        fetched=(3,),
         count=4,
         moved=1 << 20,
-    )(page_grid, norm_gain.reshape(1, D), merge_bias.reshape(units, 1), sends[0])
+    )(grid, norm_gain, merge_bias, blocks[4])
     attn = kernel(
         attend_kernel,
         "attend",
-        piece,
+        shape(piece, WIDE),
         [pltpu.VMEM((patches, HPAIR), BF16)] * 3,
         count=2 + ROWS,
-        flops=6 * patches * patches * 256,
+        flops=20 * patches * patches * 4096,
         moved=1 << 20,
     )(select, dead, *blocks)
-    resid, main, tail = kernel(
+    resid, own_gain, main, tail = kernel(
         ready_kernel,
         "ready",
-        [shape(patches, HPAIR, dtype=F32), shape(MAIN, HPAIR), shape(4, MAIN, HPAIR)],
+        [shape(patches, HPAIR, dtype=F32), shape(1, HPAIR, dtype=F32), shape(MAIN, HPAIR), shape(4, MAIN, HPAIR)],
         [pltpu.VMEM((patches, HPAIR), BF16)],
-        tokens=(1,),
-        count=2 + ROWS + PAGES,
-        flops=2 * patches * patches * 256,
+        fetched=(2,),
+        count=3 + ROWS + PAGES,
+        flops=10 * patches * patches * 4096,
         moved=4 << 20,
-    )(select, attn, *blocks, *slices)
+    )(select, gain, attn, *blocks, *slices)
     hidden = kernel(
         project_kernel,
         "project",
-        piece,
-        [assembled],
-        count=ROWS + 3,
+        shape(piece + NOTES, WIDE),
+        [pltpu.VMEM((piece, MAIN), BF16)],
+        count=ROWS + 4,
         flops=4 * patches * MAIN * 256,
         moved=4 << 20,
-    )(*gather_rows(attn), main, tail, resid)
-    ends = kernel(tail_kernel, "merge_tail", shape(units, MAIN), tokens=(1,), count=2, moved=4 << 20)(merge_weight, hidden)
+    )(*gather_rows(attn), main, tail, resid, own_gain)
+    ends = kernel(tail_kernel, "merge_tail", shape(units, MAIN), fetched=(1,), count=2, moved=4 << 20)(
+        merge_weight, hidden
+    )
     return kernel(
         merge_kernel,
         "merge",
         shape(1, units, groups),
-        [assembled],
-        count=ROWS + 5,
+        [pltpu.VMEM((piece + NOTES, MAIN), BF16)],
+        count=ROWS + 4,
         flops=10 * units * groups * MAIN,
         moved=8 << 20,
-    )(*gather_rows(hidden), merge_weight, ends, gain, bias, live)
+    )(*gather_rows(hidden), merge_weight, ends, bias, live)
 
 
 def solution(mesh):

time: 55.8 us -> 47.7 us (0.85)
  waiting for transfers between devices: 24.4 us -> 14.4 us
  starting transfers between devices: 17.8 us -> 22 us
  local copies, waits for them, and re-layouts: 4.21 us -> 1.39 us
  Pallas kernels: 8.92 us -> 9.55 us
    ppermute x3, waiting for transfers between devices: 16.7 us -> 3.61 us  [turn(): lax.ppermute(value, 'page', [(page, (page + step) % PAGES) for page in ra...]
    ppermute x3, starting transfers between devices: 1.74 us -> 5.57 us  [turn(): lax.ppermute(value, 'page', [(page, (page + step) % PAGES) for page in ra...]
    ppermute x21, waiting for transfers between devices: 7.77 us -> 10.7 us  [swap(): lax.ppermute(value, 'row', [(row, row ^ step) for row in range(ROWS)])]
    reshape x2 -> x0, local copies, waits for them, and re-layouts: 1.53 us -> none  [the longest x1 0.82 us: local_eight(): merge_bias.reshape(units, 1)]
    unnamed x10 -> x8, local copies, waits for them, and re-layouts: 2.68 us -> 1.39 us
    pallas_call x7 -> x6, Pallas kernels: 8.2 us -> 9.27 us  [the longest x1 3.01 us: local_eight(): kernel(merge_kernel, 'merge', shape(1, units, groups), [pltpu.VMEM((piece...]
  transfers between devices with their start and end apart: 24 -> 24, of which waited for: 10 -> 7; matrix products, arithmetic and copies ran while one was open for 3% -> 0% of each run, Pallas kernels for 5% -> 7%
where the time goes in v3:
time: 47.7 us; the launch traced here: 47.4 us
  starting transfers between devices  22 us (46%)
  waiting for transfers between devices  14.4 us (30%)
  Pallas kernels  9.55 us (20%)
  local copies, waits for them, and re-layouts  1.39 us (3%)
    ppermute x21, starting transfers between devices, swap(): lax.ppermute(value, 'row', [(row, row ^ step) for row in range(ROWS)])  16.4 us
    ppermute x21, waiting for transfers between devices, swap(): lax.ppermute(value, 'row', [(row, row ^ step) for row in range(ROWS)])  10.7 us
    ppermute x3, starting transfers between devices, turn(): lax.ppermute(value, 'page', [(page, (page + step) % PAGES) for page in ra...  5.57 us
    ppermute x3, waiting for transfers between devices, turn(): lax.ppermute(value, 'page', [(page, (page + step) % PAGES) for page in ra...  3.61 us
    pallas_call x1, Pallas kernels, local_eight(): kernel(merge_kernel, 'merge', shape(1, units, groups), [pltpu.VMEM((piece...  3.01 us
    pallas_call x1, Pallas kernels, local_eight(): kernel(spread_kernel, 'spread', [shape(band, 4 * HPAIR)] * ROWS + [shape(...  1.74 us
    pallas_call x1, Pallas kernels, local_eight(): kernel(project_kernel, 'project', shape(piece + NOTES, WIDE), [pltpu.VMEM...  1.42 us
    unnamed x8, local copies, waits for them, and re-layouts  1.39 us
  transfers between devices with their start and end apart: 24, of which 7 were waited for; matrix products, arithmetic and copies ran while one was open for 0% of the time, Pallas kernels for 7%

profile of v3, /device:TPU:0, one launch (start us, length us, event | category | flops | bytes accessed | tf_op | source)
XLA Modules:
  0.0 47.4 jit_solution(17895477031484041173)
XLA Ops:
  0.0 1.7 %spread.1 = (bf16[64,640]{1,0:T(8,128)(2,1)S(1)}, bf16[64,640]{1,0:T(8,128)(2,1)S(1)}, bf16[64,640]{1,0:T(8,128)(2,1)S(1)}, bf16[64,640]{1,0:T(8,128)(2,1)S(1)},...) custom-call(bf16[1,64,3840]{2,1,0:T(8,128)(2,1)} %qkv_hbm.1, ...), custom_call_target="tpu_custom_call" | custom-call | bytes 1048576 | tf_op jit(solution)/shard_map/spread/pallas_call | solution.py:369
  1.7 3.0 %collective-permute-start = (bf16[64,640]{1,0:T(8,128)(2,1)S(1)}, bf16[64,640]{1,0:T(8,128)(2,1)S(1)}, u32[]{:S(2)}, u32[]{:S(2)}) collective-permute-start(bf16[64,640]{1,0:T(8,128)(2,1)S(1)} %get-tuple-element.25), channel_id=1, source_target_pairs={{0,4},{1,5},{2,6},{3,7},{4,0},{5,1},{6,2},{7,3},{8,12},{9,13},{10,... | collective-permute-start | bytes 245768 | tf_op jit(solution)/shard_map/ppermute | solution.py:348
  4.8 1.5 %collective-permute-start.2 = (bf16[64,640]{1,0:T(8,128)(2,1)S(1)}, bf16[64,640]{1,0:T(8,128)(2,1)S(1)}, u32[]{:S(2)}, u32[]{:S(2)}) collective-permute-start(bf16[64,640]{1,0:T(8,128)(2,1)S(1)} %get-tuple-element.30), channel_id=1, source_target_pairs={{0,2},{1,3},{2,0},{3,1},{4,6},{5,7},{6,4},{7,5},{8,10},{9,11},{10,... | collective-permute-start | bytes 245768 | tf_op jit(solution)/shard_map/ppermute | solution.py:348
  7.2 2.9 %collective-permute-start.5 = (bf16[64,640]{1,0:T(8,128)(2,1)S(1)}, bf16[64,640]{1,0:T(8,128)(2,1)S(1)}, u32[]{:S(2)}, u32[]{:S(2)}) collective-permute-start(bf16[64,640]{1,0:T(8,128)(2,1)S(1)} %get-tuple-element.33), channel_id=1, source_target_pairs={{0,6},{1,7},{2,4},{3,5},{4,2},{5,3},{6,0},{7,1},{8,14},{9,15},{10,... | collective-permute-start | bytes 245768 | tf_op jit(solution)/shard_map/ppermute | solution.py:348
  10.2 0.7 %copy-done = f32[1280]{0:T(1024)S(1)} copy-done((f32[1280]{0:T(1024)S(1)}, f32[1280]{0:T(1024)}, u32[]{:S(2)}) %copy-start) | copy-done | bytes 5144
  10.9 0.7 %copy-done.1 = f32[640]{0:T(1024)S(1)} copy-done((f32[640]{0:T(1024)S(1)}, f32[640]{0:T(1024)}, u32[]{:S(2)}) %copy-start.1) | copy-done | bytes 2584
  11.8 1.6 %collective-permute-start.14 = (bf16[400,128]{1,0:T(8,128)(2,1)S(1)}, bf16[400,128]{1,0:T(8,128)(2,1)S(1)}, u32[]{:S(2)}, u32[]{:S(2)}) collective-permute-start(bf16[400,128]{1,0:T(8,128)(2,1)S(1)} %get-tuple-element.36.rest_8_), channel_id=1, source_target_pairs={{0,8},{8,16},{16,24},{24,0},{1,9},{9,17},{17,25},{25,1},{2,10},{10... | collective-permute-start | bytes 307208 | tf_op jit(solution)/shard_map/ppermute | solution.py:352
  13.5 1.8 %collective-permute-done.6.rest_7_ = bf16[64,640]{1,0:T(8,128)(2,1)S(1)} collective-permute-done((bf16[64,640]{1,0:T(8,128)(2,1)S(1)}, bf16[64,640]{1,0:T(8,128)(2,1)S(1)}, u32[]{:S(2)}, u32[]{:S(2)}) %collective-permute-start.6) | collective-permute-done | bytes 81952 | tf_op jit(solution)/shard_map/ppermute | solution.py:348
  15.3 1.3 %attend.1.token_ref.rest_0_ = bf16[640,128]{1,0:T(8,128)(2,1)S(1)} custom-call(bf16[512,512]{1,0:T(8,128)(2,1)S(1)} %get-tuple-element.26.select_ref, f32[1,512]{1,0:T(1,128)S(1)} %get-tuple-element.27.dead_ref, bf16[64,640]{1,0:T(8,128)(2,1)S(1)} %get-tuple-element.28.rest_0_, bf16[64,640]{1,0:T(8,128)(2,1)S(1)} %collective-permute-done.1.rest_1_, ...), custom_call_target="tpu_custom_call" | custom-call | flops 21474836480 | bytes 1048576 | tf_op jit(solution)/shard_map/attend/pallas_call | solution.py:402
  16.6 1.1 %collective-permute-start.10 = (bf16[640,128]{1,0:T(8,128)(2,1)S(1)}, bf16[640,128]{1,0:T(8,128)(2,1)S(1)}, u32[]{:S(2)}, u32[]{:S(2)}) collective-permute-start(bf16[640,128]{1,0:T(8,128)(2,1)S(1)} %attend.1.token_ref.rest_0_), channel_id=1, source_target_pairs={{0,4},{1,5},{2,6},{3,7},{4,0},{5,1},{6,2},{7,3},{8,12},{9,13},{10,... | collective-permute-start | bytes 491528 | tf_op jit(solution)/shard_map/ppermute | solution.py:348
  17.7 1.6 %collective-permute-start.12 = (bf16[640,128]{1,0:T(8,128)(2,1)S(1)}, bf16[640,128]{1,0:T(8,128)(2,1)S(1)}, u32[]{:S(2)}, u32[]{:S(2)}) collective-permute-start(bf16[640,128]{1,0:T(8,128)(2,1)S(1)} %attend.1.token_ref.rest_0_), channel_id=1, source_target_pairs={{0,6},{1,7},{2,4},{3,5},{4,2},{5,3},{6,0},{7,1},{8,14},{9,15},{10,... | collective-permute-start | bytes 491528 | tf_op jit(solution)/shard_map/ppermute | solution.py:348
  19.2 0.9 %collective-permute-start.8 = (bf16[640,128]{1,0:T(8,128)(2,1)S(1)}, bf16[640,128]{1,0:T(8,128)(2,1)S(1)}, u32[]{:S(2)}, u32[]{:S(2)}) collective-permute-start(bf16[640,128]{1,0:T(8,128)(2,1)S(1)} %attend.1.token_ref.rest_0_), channel_id=1, source_target_pairs={{0,2},{1,3},{2,0},{3,1},{4,6},{5,7},{6,4},{7,5},{8,10},{9,11},{10,... | collective-permute-start | bytes 491528 | tf_op jit(solution)/shard_map/ppermute | solution.py:348
  20.2 2.6 %collective-permute-start.15 = (bf16[400,128]{1,0:T(8,128)(2,1)S(1)}, bf16[400,128]{1,0:T(8,128)(2,1)S(1)}, u32[]{:S(2)}, u32[]{:S(2)}) collective-permute-start(bf16[400,128]{1,0:T(8,128)(2,1)S(1)} %get-tuple-element.36.rest_8_), channel_id=1, source_target_pairs={{0,16},{8,24},{16,0},{24,8},{1,17},{9,25},{17,1},{25,9},{2,18},{10... | collective-permute-start | bytes 307208 | tf_op jit(solution)/shard_map/ppermute | solution.py:352
  22.8 1.3 %collective-permute-start.16 = (bf16[400,128]{1,0:T(8,128)(2,1)S(1)}, bf16[400,128]{1,0:T(8,128)(2,1)S(1)}, u32[]{:S(2)}, u32[]{:S(2)}) collective-permute-start(bf16[400,128]{1,0:T(8,128)(2,1)S(1)} %get-tuple-element.36.rest_8_), channel_id=1, source_target_pairs={{0,24},{8,0},{16,8},{24,16},{1,25},{9,1},{17,9},{25,17},{2,26},{10... | collective-permute-start | bytes 307208 | tf_op jit(solution)/shard_map/ppermute | solution.py:352
  24.1 3.6 %collective-permute-done.15.rest_10_ = bf16[400,128]{1,0:T(8,128)(2,1)S(1)} collective-permute-done((bf16[400,128]{1,0:T(8,128)(2,1)S(1)}, bf16[400,128]{1,0:T(8,128)(2,1)S(1)}, u32[]{:S(2)}, u32[]{:S(2)}) %collective-permute-start.15) | collective-permute-done | bytes 102432 | tf_op jit(solution)/shard_map/ppermute | solution.py:352
  28.8 0.5 %ready.1 = (f32[512,160]{1,0:T(8,128)S(1)}, f32[1,160]{1,0:T(1,128)S(1)}, bf16[1024,160]{1,0:T(8,128)(2,1)S(1)}, bf16[4,1024,160]{2,1,0:T(8,128)(2,1)S(1)}) custom-call(bf16[512,512]{1,0:T(8,128)(2,1)S(1)} %get-tuple-element.26.select_ref, f32[1,1280]{1,0:T(1,128)S(1)} %get-tuple-element.35.gain_ref, bf16[640,128]{1,0:T(8,128)(2,1)S(1)} %attend.1.token_ref.rest_0_, ...), custom_call_target="tpu_custom_call" | custom-call | flops 10737418240 | bytes 4194304 | tf_op jit(solution)/shard_map/ready/pallas_call | solution.py:411
  29.9 1.4 %project.1.token_ref.rest_0_ = bf16[656,128]{1,0:T(8,128)(2,1)S(1)} custom-call(bf16[640,128]{1,0:T(8,128)(2,1)S(1)} %attend.1.token_ref.rest_0_, bf16[640,128]{1,0:T(8,128)(2,1)S(1)} %collective-permute-done.7.rest_1_, bf16[640,128]{1,0:T(8,128)(2,1)S(1)} %collective-permute-done.8.rest_2_, bf16[640,128]{1,0:T(8,128)(2,1)S(1)} %collective-permute-done.9.rest_3_, ...), custom_call_target="tpu_custom_call" | custom-call | flops 536870912 | bytes 4194304 | tf_op jit(solution)/shard_map/project/pallas_call | solution.py:421
  31.3 1.5 %collective-permute-start.18 = (bf16[656,128]{1,0:T(8,128)(2,1)S(1)}, bf16[656,128]{1,0:T(8,128)(2,1)S(1)}, u32[]{:S(2)}, u32[]{:S(2)}) collective-permute-start(bf16[656,128]{1,0:T(8,128)(2,1)S(1)} %project.1.token_ref.rest_0_), channel_id=1, source_target_pairs={{0,2},{1,3},{2,0},{3,1},{4,6},{5,7},{6,4},{7,5},{8,10},{9,11},{10,... | collective-permute-start | bytes 503816 | tf_op jit(solution)/shard_map/ppermute | solution.py:348
  32.8 1.4 %collective-permute-start.20 = (bf16[656,128]{1,0:T(8,128)(2,1)S(1)}, bf16[656,128]{1,0:T(8,128)(2,1)S(1)}, u32[]{:S(2)}, u32[]{:S(2)}) collective-permute-start(bf16[656,128]{1,0:T(8,128)(2,1)S(1)} %project.1.token_ref.rest_0_), channel_id=1, source_target_pairs={{0,4},{1,5},{2,6},{3,7},{4,0},{5,1},{6,2},{7,3},{8,12},{9,13},{10,... | collective-permute-start | bytes 503816 | tf_op jit(solution)/shard_map/ppermute | solution.py:348
  34.2 0.5 %collective-permute-start.22 = (bf16[656,128]{1,0:T(8,128)(2,1)S(1)}, bf16[656,128]{1,0:T(8,128)(2,1)S(1)}, u32[]{:S(2)}, u32[]{:S(2)}) collective-permute-start(bf16[656,128]{1,0:T(8,128)(2,1)S(1)} %project.1.token_ref.rest_0_), channel_id=1, source_target_pairs={{0,6},{1,7},{2,4},{3,5},{4,2},{5,3},{6,0},{7,1},{8,14},{9,15},{10,... | collective-permute-start | bytes 503816 | tf_op jit(solution)/shard_map/ppermute | solution.py:348
  34.8 3.6 %collective-permute-done.18.rest_2_ = bf16[656,128]{1,0:T(8,128)(2,1)S(1)} collective-permute-done((bf16[656,128]{1,0:T(8,128)(2,1)S(1)}, bf16[656,128]{1,0:T(8,128)(2,1)S(1)}, u32[]{:S(2)}, u32[]{:S(2)}) %collective-permute-start.18) | collective-permute-done | bytes 167968 | tf_op jit(solution)/shard_map/ppermute | solution.py:348
  38.4 4.2 %collective-permute-done.20.rest_4_ = bf16[656,128]{1,0:T(8,128)(2,1)S(1)} collective-permute-done((bf16[656,128]{1,0:T(8,128)(2,1)S(1)}, bf16[656,128]{1,0:T(8,128)(2,1)S(1)}, u32[]{:S(2)}, u32[]{:S(2)}) %collective-permute-start.20) | collective-permute-done | bytes 167968 | tf_op jit(solution)/shard_map/ppermute | solution.py:348
  43.1 1.2 %merge_tail.1.rest_9_ = bf16[640,1024]{1,0:T(8,128)(2,1)S(1)} custom-call(bf16[640,5120]{1,0:T(8,128)(2,1)S(1)} %bitcast.1, bf16[656,128]{1,0:T(8,128)(2,1)S(1)} %project.1.token_ref.rest_0_), custom_call_target="tpu_custom_call" | custom-call | bytes 4194304 | tf_op jit(solution)/shard_map/merge_tail/pallas_call | solution.py:430
  44.4 3.0 %merge.1 = bf16[1,640,128]{2,1,0:T(8,128)(2,1)} custom-call(bf16[656,128]{1,0:T(8,128)(2,1)S(1)} %project.1.token_ref.rest_0_, bf16[656,128]{1,0:T(8,128)(2,1)S(1)} %collective-permute-done.17.rest_1_, bf16[656,128]{1,0:T(8,128)(2,1)S(1)} %collective-permute-done.18.rest_2_, bf16[656,128]{1,0:T(8,128)(2,1)S(1)} %collective-permute-done.19.rest_3_, ...), custom_call_target="tpu_custom_call" | custom-call | flops 838860800 | bytes 8388608 | tf_op jit(solution)/shard_map/merge/pallas_call | solution.py:433
  (40 shorter events, 3.4 us)
Async XLA Ops:
  1.7 5.5 %collective-permute-start = (bf16[64,640]{1,0:T(8,128)(2,1)S(1)}, bf16[64,640]{1,0:T(8,128)(2,1)S(1)}, u32[]{:S(2)}, u32[]{:S(2)}) collective-permute-start(bf16[64,640]{1,0:T(8,128)(2,1)S(1)} %get-tuple-element.25), channel_id=1, source_target_pairs={{0,4},{1,5},{2,6},{3,7},{4,0},{5,1},{6,2},{7,3},{8,12},{9,13},{10,... | collective-permute-start | bytes 245768 | tf_op jit(solution)/shard_map/ppermute | solution.py:348
  4.8 5.4 %collective-permute-start.1 = (bf16[64,640]{1,0:T(8,128)(2,1)S(1)}, bf16[64,640]{1,0:T(8,128)(2,1)S(1)}, u32[]{:S(2)}, u32[]{:S(2)}) collective-permute-start(bf16[64,640]{1,0:T(8,128)(2,1)S(1)} %get-tuple-element.29), channel_id=1, source_target_pairs={{0,1},{1,0},{2,3},{3,2},{4,5},{5,4},{6,7},{7,6},{8,9},{9,8},{10,11... | collective-permute-start | bytes 245768 | tf_op jit(solution)/shard_map/ppermute | solution.py:348
  4.8 7.0 %collective-permute-start.2 = (bf16[64,640]{1,0:T(8,128)(2,1)S(1)}, bf16[64,640]{1,0:T(8,128)(2,1)S(1)}, u32[]{:S(2)}, u32[]{:S(2)}) collective-permute-start(bf16[64,640]{1,0:T(8,128)(2,1)S(1)} %get-tuple-element.30), channel_id=1, source_target_pairs={{0,2},{1,3},{2,0},{3,1},{4,6},{5,7},{6,4},{7,5},{8,10},{9,11},{10,... | collective-permute-start | bytes 245768 | tf_op jit(solution)/shard_map/ppermute | solution.py:348
  6.3 7.2 %collective-permute-start.3 = (bf16[64,640]{1,0:T(8,128)(2,1)S(1)}, bf16[64,640]{1,0:T(8,128)(2,1)S(1)}, u32[]{:S(2)}, u32[]{:S(2)}) collective-permute-start(bf16[64,640]{1,0:T(8,128)(2,1)S(1)} %get-tuple-element.31), channel_id=1, source_target_pairs={{0,3},{1,2},{2,1},{3,0},{4,7},{5,6},{6,5},{7,4},{8,11},{9,10},{10,... | collective-permute-start | bytes 245768 | tf_op jit(solution)/shard_map/ppermute | solution.py:348
  6.6 6.8 %collective-permute-start.4 = (bf16[64,640]{1,0:T(8,128)(2,1)S(1)}, bf16[64,640]{1,0:T(8,128)(2,1)S(1)}, u32[]{:S(2)}, u32[]{:S(2)}) collective-permute-start(bf16[64,640]{1,0:T(8,128)(2,1)S(1)} %get-tuple-element.32), channel_id=1, source_target_pairs={{0,5},{1,4},{2,7},{3,6},{4,1},{5,0},{6,3},{7,2},{8,13},{9,12},{10,... | collective-permute-start | bytes 245768 | tf_op jit(solution)/shard_map/ppermute | solution.py:348
  7.2 6.2 %collective-permute-start.5 = (bf16[64,640]{1,0:T(8,128)(2,1)S(1)}, bf16[64,640]{1,0:T(8,128)(2,1)S(1)}, u32[]{:S(2)}, u32[]{:S(2)}) collective-permute-start(bf16[64,640]{1,0:T(8,128)(2,1)S(1)} %get-tuple-element.33), channel_id=1, source_target_pairs={{0,6},{1,7},{2,4},{3,5},{4,2},{5,3},{6,0},{7,1},{8,14},{9,15},{10,... | collective-permute-start | bytes 245768 | tf_op jit(solution)/shard_map/ppermute | solution.py:348
  10.1 5.1 %collective-permute-start.6 = (bf16[64,640]{1,0:T(8,128)(2,1)S(1)}, bf16[64,640]{1,0:T(8,128)(2,1)S(1)}, u32[]{:S(2)}, u32[]{:S(2)}) collective-permute-start(bf16[64,640]{1,0:T(8,128)(2,1)S(1)} %get-tuple-element.34), channel_id=1, source_target_pairs={{0,7},{1,6},{2,5},{3,4},{4,3},{5,2},{6,1},{7,0},{8,15},{9,14},{10,... | collective-permute-start | bytes 245768 | tf_op jit(solution)/shard_map/ppermute | solution.py:348
  11.8 10.9 %collective-permute-start.14 = (bf16[400,128]{1,0:T(8,128)(2,1)S(1)}, bf16[400,128]{1,0:T(8,128)(2,1)S(1)}, u32[]{:S(2)}, u32[]{:S(2)}) collective-permute-start(bf16[400,128]{1,0:T(8,128)(2,1)S(1)} %get-tuple-element.36.rest_8_), channel_id=1, source_target_pairs={{0,8},{8,16},{16,24},{24,0},{1,9},{9,17},{17,25},{25,1},{2,10},{10... | collective-permute-start | bytes 307208 | tf_op jit(solution)/shard_map/ppermute | solution.py:352
  16.6 11.1 %collective-permute-start.10 = (bf16[640,128]{1,0:T(8,128)(2,1)S(1)}, bf16[640,128]{1,0:T(8,128)(2,1)S(1)}, u32[]{:S(2)}, u32[]{:S(2)}) collective-permute-start(bf16[640,128]{1,0:T(8,128)(2,1)S(1)} %attend.1.token_ref.rest_0_), channel_id=1, source_target_pairs={{0,4},{1,5},{2,6},{3,7},{4,0},{5,1},{6,2},{7,3},{8,12},{9,13},{10,... | collective-permute-start | bytes 491528 | tf_op jit(solution)/shard_map/ppermute | solution.py:348
  17.7 10.5 %collective-permute-start.12 = (bf16[640,128]{1,0:T(8,128)(2,1)S(1)}, bf16[640,128]{1,0:T(8,128)(2,1)S(1)}, u32[]{:S(2)}, u32[]{:S(2)}) collective-permute-start(bf16[640,128]{1,0:T(8,128)(2,1)S(1)} %attend.1.token_ref.rest_0_), channel_id=1, source_target_pairs={{0,6},{1,7},{2,4},{3,5},{4,2},{5,3},{6,0},{7,1},{8,14},{9,15},{10,... | collective-permute-start | bytes 491528 | tf_op jit(solution)/shard_map/ppermute | solution.py:348
  19.2 9.1 %collective-permute-start.8 = (bf16[640,128]{1,0:T(8,128)(2,1)S(1)}, bf16[640,128]{1,0:T(8,128)(2,1)S(1)}, u32[]{:S(2)}, u32[]{:S(2)}) collective-permute-start(bf16[640,128]{1,0:T(8,128)(2,1)S(1)} %attend.1.token_ref.rest_0_), channel_id=1, source_target_pairs={{0,2},{1,3},{2,0},{3,1},{4,6},{5,7},{6,4},{7,5},{8,10},{9,11},{10,... | collective-permute-start | bytes 491528 | tf_op jit(solution)/shard_map/ppermute | solution.py:348
  20.2 7.5 %collective-permute-start.15 = (bf16[400,128]{1,0:T(8,128)(2,1)S(1)}, bf16[400,128]{1,0:T(8,128)(2,1)S(1)}, u32[]{:S(2)}, u32[]{:S(2)}) collective-permute-start(bf16[400,128]{1,0:T(8,128)(2,1)S(1)} %get-tuple-element.36.rest_8_), channel_id=1, source_target_pairs={{0,16},{8,24},{16,0},{24,8},{1,17},{9,25},{17,1},{25,9},{2,18},{10... | collective-permute-start | bytes 307208 | tf_op jit(solution)/shard_map/ppermute | solution.py:352
  22.8 6.0 %collective-permute-start.16 = (bf16[400,128]{1,0:T(8,128)(2,1)S(1)}, bf16[400,128]{1,0:T(8,128)(2,1)S(1)}, u32[]{:S(2)}, u32[]{:S(2)}) collective-permute-start(bf16[400,128]{1,0:T(8,128)(2,1)S(1)} %get-tuple-element.36.rest_8_), channel_id=1, source_target_pairs={{0,24},{8,0},{16,8},{24,16},{1,25},{9,1},{17,9},{25,17},{2,26},{10... | collective-permute-start | bytes 307208 | tf_op jit(solution)/shard_map/ppermute | solution.py:352
  27.7 1.6 %collective-permute-start.7 = (bf16[640,128]{1,0:T(8,128)(2,1)S(1)}, bf16[640,128]{1,0:T(8,128)(2,1)S(1)}, u32[]{:S(2)}, u32[]{:S(2)}) collective-permute-start(bf16[640,128]{1,0:T(8,128)(2,1)S(1)} %attend.1.token_ref.rest_0_), channel_id=1, source_target_pairs={{0,1},{1,0},{2,3},{3,2},{4,5},{5,4},{6,7},{7,6},{8,9},{9,8},{10,11... | collective-permute-start | bytes 491528 | tf_op jit(solution)/shard_map/ppermute | solution.py:348
  27.7 1.6 %collective-permute-start.11 = (bf16[640,128]{1,0:T(8,128)(2,1)S(1)}, bf16[640,128]{1,0:T(8,128)(2,1)S(1)}, u32[]{:S(2)}, u32[]{:S(2)}) collective-permute-start(bf16[640,128]{1,0:T(8,128)(2,1)S(1)} %collective-permute-done.10.rest_4_), channel_id=1, source_target_pairs={{0,1},{1,0},{2,3},{3,2},{4,5},{5,4},{6,7},{7,6},{8,9},{9,8},{10,11... | collective-permute-start | bytes 491528 | tf_op jit(solution)/shard_map/ppermute | solution.py:348
  28.2 1.4 %collective-permute-start.13 = (bf16[640,128]{1,0:T(8,128)(2,1)S(1)}, bf16[640,128]{1,0:T(8,128)(2,1)S(1)}, u32[]{:S(2)}, u32[]{:S(2)}) collective-permute-start(bf16[640,128]{1,0:T(8,128)(2,1)S(1)} %collective-permute-done.12.rest_6_), channel_id=1, source_target_pairs={{0,1},{1,0},{2,3},{3,2},{4,5},{5,4},{6,7},{7,6},{8,9},{9,8},{10,11... | collective-permute-start | bytes 491528 | tf_op jit(solution)/shard_map/ppermute | solution.py:348
  28.3 1.6 %collective-permute-start.9 = (bf16[640,128]{1,0:T(8,128)(2,1)S(1)}, bf16[640,128]{1,0:T(8,128)(2,1)S(1)}, u32[]{:S(2)}, u32[]{:S(2)}) collective-permute-start(bf16[640,128]{1,0:T(8,128)(2,1)S(1)} %collective-permute-done.8.rest_2_), channel_id=1, source_target_pairs={{0,1},{1,0},{2,3},{3,2},{4,5},{5,4},{6,7},{7,6},{8,9},{9,8},{10,11... | collective-permute-start | bytes 491528 | tf_op jit(solution)/shard_map/ppermute | solution.py:348
  31.3 7.1 %collective-permute-start.18 = (bf16[656,128]{1,0:T(8,128)(2,1)S(1)}, bf16[656,128]{1,0:T(8,128)(2,1)S(1)}, u32[]{:S(2)}, u32[]{:S(2)}) collective-permute-start(bf16[656,128]{1,0:T(8,128)(2,1)S(1)} %project.1.token_ref.rest_0_), channel_id=1, source_target_pairs={{0,2},{1,3},{2,0},{3,1},{4,6},{5,7},{6,4},{7,5},{8,10},{9,11},{10,... | collective-permute-start | bytes 503816 | tf_op jit(solution)/shard_map/ppermute | solution.py:348
  32.8 9.8 %collective-permute-start.20 = (bf16[656,128]{1,0:T(8,128)(2,1)S(1)}, bf16[656,128]{1,0:T(8,128)(2,1)S(1)}, u32[]{:S(2)}, u32[]{:S(2)}) collective-permute-start(bf16[656,128]{1,0:T(8,128)(2,1)S(1)} %project.1.token_ref.rest_0_), channel_id=1, source_target_pairs={{0,4},{1,5},{2,6},{3,7},{4,0},{5,1},{6,2},{7,3},{8,12},{9,13},{10,... | collective-permute-start | bytes 503816 | tf_op jit(solution)/shard_map/ppermute | solution.py:348
  34.2 8.4 %collective-permute-start.22 = (bf16[656,128]{1,0:T(8,128)(2,1)S(1)}, bf16[656,128]{1,0:T(8,128)(2,1)S(1)}, u32[]{:S(2)}, u32[]{:S(2)}) collective-permute-start(bf16[656,128]{1,0:T(8,128)(2,1)S(1)} %project.1.token_ref.rest_0_), channel_id=1, source_target_pairs={{0,6},{1,7},{2,4},{3,5},{4,2},{5,3},{6,0},{7,1},{8,14},{9,15},{10,... | collective-permute-start | bytes 503816 | tf_op jit(solution)/shard_map/ppermute | solution.py:348
  34.8 9.6 %collective-permute-start.17 = (bf16[656,128]{1,0:T(8,128)(2,1)S(1)}, bf16[656,128]{1,0:T(8,128)(2,1)S(1)}, u32[]{:S(2)}, u32[]{:S(2)}) collective-permute-start(bf16[656,128]{1,0:T(8,128)(2,1)S(1)} %project.1.token_ref.rest_0_), channel_id=1, source_target_pairs={{0,1},{1,0},{2,3},{3,2},{4,5},{5,4},{6,7},{7,6},{8,9},{9,8},{10,11... | collective-permute-start | bytes 503816 | tf_op jit(solution)/shard_map/ppermute | solution.py:348
  38.4 6.0 %collective-permute-start.19 = (bf16[656,128]{1,0:T(8,128)(2,1)S(1)}, bf16[656,128]{1,0:T(8,128)(2,1)S(1)}, u32[]{:S(2)}, u32[]{:S(2)}) collective-permute-start(bf16[656,128]{1,0:T(8,128)(2,1)S(1)} %collective-permute-done.18.rest_2_), channel_id=1, source_target_pairs={{0,1},{1,0},{2,3},{3,2},{4,5},{5,4},{6,7},{7,6},{8,9},{9,8},{10,11... | collective-permute-start | bytes 503816 | tf_op jit(solution)/shard_map/ppermute | solution.py:348
  42.6 1.8 %collective-permute-start.21 = (bf16[656,128]{1,0:T(8,128)(2,1)S(1)}, bf16[656,128]{1,0:T(8,128)(2,1)S(1)}, u32[]{:S(2)}, u32[]{:S(2)}) collective-permute-start(bf16[656,128]{1,0:T(8,128)(2,1)S(1)} %collective-permute-done.20.rest_4_), channel_id=1, source_target_pairs={{0,1},{1,0},{2,3},{3,2},{4,5},{5,4},{6,7},{7,6},{8,9},{9,8},{10,11... | collective-permute-start | bytes 503816 | tf_op jit(solution)/shard_map/ppermute | solution.py:348
  42.6 1.8 %collective-permute-start.23 = (bf16[656,128]{1,0:T(8,128)(2,1)S(1)}, bf16[656,128]{1,0:T(8,128)(2,1)S(1)}, u32[]{:S(2)}, u32[]{:S(2)}) collective-permute-start(bf16[656,128]{1,0:T(8,128)(2,1)S(1)} %collective-permute-done.22.rest_6_), channel_id=1, source_target_pairs={{0,1},{1,0},{2,3},{3,2},{4,5},{5,4},{6,7},{7,6},{8,9},{9,8},{10,11... | collective-permute-start | bytes 503816 | tf_op jit(solution)/shard_map/ppermute | solution.py:348
  (4 other events, 30.2 us)

commit v4 on v3

--- a/solution.py
+++ b/solution.py
@@ -170,8 +170,12 @@
     grid_out[...] = jnp.where(row == 0, grid[0, 0], grid[0, 1])
 
 
-def layout_kernel(grid_ref, gain_ref, bias_ref, early_ref, select_ref, keys_ref, live_ref, gain_out, bias_out):
-    del early_ref
+def layout_kernel(grid_ref, gain_hbm, bias_hbm, *rest):
+    select_ref, keys_ref, live_ref, gain_out, bias_out, gain_ref, bias_ref, sems = rest[-8:]
+    fetch_gain = pltpu.make_async_copy(gain_hbm, gain_ref, sems.at[0])
+    fetch_bias = pltpu.make_async_copy(bias_hbm, bias_ref, sems.at[1])
+    fetch_gain.start()
+    fetch_bias.start()
     rows_n, cols_n = grid_ref[:1, :1], grid_ref[1:2, :1]
     patches = select_ref.shape[0]
     groups = patches // 4
@@ -188,6 +192,8 @@
     keys_ref[...] = jnp.where(key < rows_n * cols_n, 0.0, -1e30)
     slot = lax.broadcasted_iota(jnp.int32, live_ref.shape, 1)
     live_ref[...] = jnp.where(slot < count, 1.0, 0.0)
+    fetch_gain.wait()
+    fetch_bias.wait()
     gain_out[...] = gain_ref[...].reshape(gain_out.shape)
     bias = jnp.broadcast_to(bias_ref[...].reshape(1, bias_out.shape[0]), (8, bias_out.shape[0]))
     bias_out[...] = bias.T[:, :1]
@@ -195,7 +201,7 @@
 
 def attend_kernel(select_ref, dead_ref, *rest):
     blocks = rest[:ROWS]
-    out_ref, q_all, k_all, v_all = rest[ROWS:]
+    out_ref, q_all, k_all, v_all = rest[-4:]
     me = row_index()
     band = blocks[0].shape[0]
     patches = band * ROWS
@@ -340,6 +346,10 @@
     )
 
 
+def in_hbm(value):
+    return pltpu.with_memory_space_constraint(value, pltpu.HBM)
+
+
 def shape(*dims, dtype=BF16):
     return jax.ShapeDtypeStruct(dims, dtype)
 
@@ -382,7 +392,7 @@
         count=4,
         limit=24,
         moved=1 << 20,
-    )(*[pltpu.with_memory_space_constraint(value, pltpu.HBM) for value in (qkv_rows, residual, out_weight, page_grid)])
+    )(in_hbm(qkv_rows), in_hbm(residual), in_hbm(out_weight), in_hbm(page_grid))
     blocks = [sends[0]] + [swap(sends[step], step) for step in range(1, ROWS)]
     slices = [own] + [turn(own, step) for step in range(1, PAGES)]
     select, dead, live, gain, bias = kernel(
@@ -395,19 +405,22 @@
             shape(1, D, dtype=F32),
             shape(units, 1, dtype=F32),
         ],
-        fetched=(3,),
-        count=4,
+        [pltpu.VMEM((D,), F32), pltpu.VMEM((units,), F32), pltpu.SemaphoreType.DMA((2,))],
+        fetched=range(1, 3 + 5),
+        count=3 + 5,
         moved=1 << 20,
-    )(grid, norm_gain, merge_bias, blocks[4])
+    )(grid, in_hbm(norm_gain), in_hbm(merge_bias), *blocks[1:6])
+    early = [slices[1], slices[2]]
     attn = kernel(
         attend_kernel,
         "attend",
         shape(piece, WIDE),
         [pltpu.VMEM((patches, HPAIR), BF16)] * 3,
-        count=2 + ROWS,
+        fetched=range(2 + ROWS, 2 + ROWS + len(early)),
+        count=2 + ROWS + len(early),
         flops=20 * patches * patches * 4096,
         moved=1 << 20,
-    )(select, dead, *blocks)
+    )(select, dead, *blocks, *early)
     resid, own_gain, main, tail = kernel(
         ready_kernel,
         "ready",

time: 47.7 us -> 49.5 us (1.038)
  waiting for transfers between devices: 14.4 us -> 17.9 us
  local copies, waits for them, and re-layouts: 1.39 us -> 0.01 us
  starting transfers between devices: 22 us -> 21.1 us
  Pallas kernels: 9.55 us -> 10.2 us
    ppermute x21, waiting for transfers between devices: 10.7 us -> 17.9 us  [swap(): lax.ppermute(value, 'row', [(row, row ^ step) for row in range(ROWS)])]
    ppermute x3, waiting for transfers between devices: 3.61 us -> 0.01 us  [turn(): lax.ppermute(value, 'page', [(page, (page + step) % PAGES) for page in ra...]
    unnamed x8 -> x4, local copies, waits for them, and re-layouts: 1.39 us -> 0.01 us
    pallas_call x1, Pallas kernels: 0.27 us -> 0.89 us  [local_eight(): kernel(layout_kernel, 'layout', [shape(patches, patches), shape(1, patche...]
    ppermute x21, starting transfers between devices: 16.4 us -> 15.9 us  [swap(): lax.ppermute(value, 'row', [(row, row ^ step) for row in range(ROWS)])]
  transfers between devices with their start and end apart: 24 -> 24, of which waited for: 7 -> 8; matrix products, arithmetic and copies ran while one was open for 0% -> 0% of each run, Pallas kernels for 7% -> 5%
where the time goes in v4:
time: 49.5 us; the launch traced here: 49.2 us
  starting transfers between devices  21.1 us (43%)
  waiting for transfers between devices  17.9 us (36%)
  Pallas kernels  10.2 us (21%)
    ppermute x21, waiting for transfers between devices, swap(): lax.ppermute(value, 'row', [(row, row ^ step) for row in range(ROWS)])  17.9 us
    ppermute x21, starting transfers between devices, swap(): lax.ppermute(value, 'row', [(row, row ^ step) for row in range(ROWS)])  15.9 us
    ppermute x3, starting transfers between devices, turn(): lax.ppermute(value, 'page', [(page, (page + step) % PAGES) for page in ra...  5.2 us
    pallas_call x1, Pallas kernels, local_eight(): kernel(merge_kernel, 'merge', shape(1, units, groups), [pltpu.VMEM((piece...  3.01 us
    pallas_call x1, Pallas kernels, local_eight(): kernel(spread_kernel, 'spread', [shape(band, 4 * HPAIR)] * ROWS + [shape(...  1.74 us
    pallas_call x1, Pallas kernels, local_eight(): kernel(project_kernel, 'project', shape(piece + NOTES, WIDE), [pltpu.VMEM...  1.42 us
    pallas_call x1, Pallas kernels, local_eight(): kernel(attend_kernel, 'attend', shape(piece, WIDE), [pltpu.VMEM((patches,...  1.35 us
    pallas_call x1, Pallas kernels, local_eight(): kernel(tail_kernel, 'merge_tail', shape(units, MAIN), fetched=(1,), count...  1.22 us
  transfers between devices with their start and end apart: 24, of which 8 were waited for; matrix products, arithmetic and copies ran while one was open for 0% of the time, Pallas kernels for 5%

profile of v4, /device:TPU:0, one launch (start us, length us, event | category | flops | bytes accessed | tf_op | source)
XLA Modules:
  0.0 49.2 jit_solution(16722271125723351899)
XLA Ops:
  0.0 1.7 %spread.1 = (bf16[64,640]{1,0:T(8,128)(2,1)S(1)}, bf16[64,640]{1,0:T(8,128)(2,1)S(1)}, bf16[64,640]{1,0:T(8,128)(2,1)S(1)}, bf16[64,640]{1,0:T(8,128)(2,1)S(1)},...) custom-call(bf16[1,64,3840]{2,1,0:T(8,128)(2,1)} %qkv_hbm.1, ...), custom_call_target="tpu_custom_call" | custom-call | bytes 1048576 | tf_op jit(solution)/shard_map/spread/pallas_call | solution.py:379
  1.7 0.5 %collective-permute-start = (bf16[64,640]{1,0:T(8,128)(2,1)S(1)}, bf16[64,640]{1,0:T(8,128)(2,1)S(1)}, u32[]{:S(2)}, u32[]{:S(2)}) collective-permute-start(bf16[64,640]{1,0:T(8,128)(2,1)S(1)} %get-tuple-element.25), channel_id=1, source_target_pairs={{0,1},{1,0},{2,3},{3,2},{4,5},{5,4},{6,7},{7,6},{8,9},{9,8},{10,11... | collective-permute-start | bytes 245768 | tf_op jit(solution)/shard_map/ppermute | solution.py:358
  2.3 2.6 %collective-permute-start.1 = (bf16[64,640]{1,0:T(8,128)(2,1)S(1)}, bf16[64,640]{1,0:T(8,128)(2,1)S(1)}, u32[]{:S(2)}, u32[]{:S(2)}) collective-permute-start(bf16[64,640]{1,0:T(8,128)(2,1)S(1)} %get-tuple-element.26), channel_id=1, source_target_pairs={{0,2},{1,3},{2,0},{3,1},{4,6},{5,7},{6,4},{7,5},{8,10},{9,11},{10,... | collective-permute-start | bytes 245768 | tf_op jit(solution)/shard_map/ppermute | solution.py:358
  4.9 1.8 %collective-permute-start.3 = (bf16[64,640]{1,0:T(8,128)(2,1)S(1)}, bf16[64,640]{1,0:T(8,128)(2,1)S(1)}, u32[]{:S(2)}, u32[]{:S(2)}) collective-permute-start(bf16[64,640]{1,0:T(8,128)(2,1)S(1)} %get-tuple-element.28), channel_id=1, source_target_pairs={{0,4},{1,5},{2,6},{3,7},{4,0},{5,1},{6,2},{7,3},{8,12},{9,13},{10,... | collective-permute-start | bytes 245768 | tf_op jit(solution)/shard_map/ppermute | solution.py:358
  6.7 1.6 %collective-permute-start.7 = (bf16[400,128]{1,0:T(8,128)(2,1)S(1)}, bf16[400,128]{1,0:T(8,128)(2,1)S(1)}, u32[]{:S(2)}, u32[]{:S(2)}) collective-permute-start(bf16[400,128]{1,0:T(8,128)(2,1)S(1)} %get-tuple-element.35.rest_8_), channel_id=1, source_target_pairs={{0,8},{8,16},{16,24},{24,0},{1,9},{9,17},{17,25},{25,1},{2,10},{10... | collective-permute-start | bytes 307208 | tf_op jit(solution)/shard_map/ppermute | solution.py:362
  8.2 2.6 %collective-permute-start.8 = (bf16[400,128]{1,0:T(8,128)(2,1)S(1)}, bf16[400,128]{1,0:T(8,128)(2,1)S(1)}, u32[]{:S(2)}, u32[]{:S(2)}) collective-permute-start(bf16[400,128]{1,0:T(8,128)(2,1)S(1)} %get-tuple-element.35.rest_8_), channel_id=1, source_target_pairs={{0,16},{8,24},{16,0},{24,8},{1,17},{9,25},{17,1},{25,9},{2,18},{10... | collective-permute-start | bytes 307208 | tf_op jit(solution)/shard_map/ppermute | solution.py:362
  10.8 2.1 %collective-permute-start.5 = (bf16[64,640]{1,0:T(8,128)(2,1)S(1)}, bf16[64,640]{1,0:T(8,128)(2,1)S(1)}, u32[]{:S(2)}, u32[]{:S(2)}) collective-permute-start(bf16[64,640]{1,0:T(8,128)(2,1)S(1)} %get-tuple-element.33), channel_id=1, source_target_pairs={{0,6},{1,7},{2,4},{3,5},{4,2},{5,3},{6,0},{7,1},{8,14},{9,15},{10,... | collective-permute-start | bytes 245768 | tf_op jit(solution)/shard_map/ppermute | solution.py:358
  12.9 0.8 %collective-permute-start.6 = (bf16[64,640]{1,0:T(8,128)(2,1)S(1)}, bf16[64,640]{1,0:T(8,128)(2,1)S(1)}, u32[]{:S(2)}, u32[]{:S(2)}) collective-permute-start(bf16[64,640]{1,0:T(8,128)(2,1)S(1)} %get-tuple-element.34), channel_id=1, source_target_pairs={{0,7},{1,6},{2,5},{3,4},{4,3},{5,2},{6,1},{7,0},{8,15},{9,14},{10,... | collective-permute-start | bytes 245768 | tf_op jit(solution)/shard_map/ppermute | solution.py:358
  13.7 5.1 %collective-permute-done.4.rest_4_.rest_5_ = bf16[64,640]{1,0:T(8,128)(2,1)S(1)} collective-permute-done((bf16[64,640]{1,0:T(8,128)(2,1)S(1)}, bf16[64,640]{1,0:T(8,128)(2,1)S(1)}, u32[]{:S(2)}, u32[]{:S(2)}) %collective-permute-start.4) | collective-permute-done | bytes 81952 | tf_op jit(solution)/shard_map/ppermute | solution.py:358
  18.8 0.9 %layout.1 = (bf16[512,512]{1,0:T(8,128)(2,1)S(1)}, f32[1,512]{1,0:T(1,128)S(1)}, f32[1,128]{1,0:T(1,128)S(1)}, f32[1,1280]{1,0:T(1,128)S(1)}, f32[640,1]{1,0:T(8,128)S(1)}) custom-call(s32[8,128]{1,0:T(8,128)S(1)} %get-tuple-element.24.grid_ref, f32[1280]{0:T(1024)} %gain_hbm.1, f32[640]{0:T(1024)} %bias_hbm.1, ...), custom_call_target="tpu_custom_call" | custom-call | bytes 1048576 | tf_op jit(solution)/shard_map/layout/pallas_call | solution.py:398
  19.7 1.4 %attend.1.token_ref.rest_0_ = bf16[640,128]{1,0:T(8,128)(2,1)S(1)} custom-call(bf16[512,512]{1,0:T(8,128)(2,1)S(1)} %get-tuple-element.30.select_ref, f32[1,512]{1,0:T(1,128)S(1)} %get-tuple-element.31.dead_ref, bf16[64,640]{1,0:T(8,128)(2,1)S(1)} %get-tuple-element.32.rest_0_, bf16[64,640]{1,0:T(8,128)(2,1)S(1)} %collective-permute-done.rest_0_.rest_1_, ...), custom_call_target="tpu_custom_call" | custom-call | flops 21474836480 | bytes 1048576 | tf_op jit(solution)/shard_map/attend/pallas_call | solution.py:414
  21.1 1.6 %collective-permute-start.10 = (bf16[640,128]{1,0:T(8,128)(2,1)S(1)}, bf16[640,128]{1,0:T(8,128)(2,1)S(1)}, u32[]{:S(2)}, u32[]{:S(2)}) collective-permute-start(bf16[640,128]{1,0:T(8,128)(2,1)S(1)} %attend.1.token_ref.rest_0_), channel_id=1, source_target_pairs={{0,2},{1,3},{2,0},{3,1},{4,6},{5,7},{6,4},{7,5},{8,10},{9,11},{10,... | collective-permute-start | bytes 491528 | tf_op jit(solution)/shard_map/ppermute | solution.py:358
  22.9 1.8 %collective-permute-start.14 = (bf16[640,128]{1,0:T(8,128)(2,1)S(1)}, bf16[640,128]{1,0:T(8,128)(2,1)S(1)}, u32[]{:S(2)}, u32[]{:S(2)}) collective-permute-start(bf16[640,128]{1,0:T(8,128)(2,1)S(1)} %attend.1.token_ref.rest_0_), channel_id=1, source_target_pairs={{0,6},{1,7},{2,4},{3,5},{4,2},{5,3},{6,0},{7,1},{8,14},{9,15},{10,... | collective-permute-start | bytes 491528 | tf_op jit(solution)/shard_map/ppermute | solution.py:358
  24.6 1.0 %collective-permute-start.16 = (bf16[400,128]{1,0:T(8,128)(2,1)S(1)}, bf16[400,128]{1,0:T(8,128)(2,1)S(1)}, u32[]{:S(2)}, u32[]{:S(2)}) collective-permute-start(bf16[400,128]{1,0:T(8,128)(2,1)S(1)} %get-tuple-element.35.rest_8_), channel_id=1, source_target_pairs={{0,24},{8,0},{16,8},{24,16},{1,25},{9,1},{17,9},{25,17},{2,26},{10... | collective-permute-start | bytes 307208 | tf_op jit(solution)/shard_map/ppermute | solution.py:362
  25.6 2.4 %collective-permute-done.10.rest_2_ = bf16[640,128]{1,0:T(8,128)(2,1)S(1)} collective-permute-done((bf16[640,128]{1,0:T(8,128)(2,1)S(1)}, bf16[640,128]{1,0:T(8,128)(2,1)S(1)}, u32[]{:S(2)}, u32[]{:S(2)}) %collective-permute-start.10) | collective-permute-done | bytes 163872 | tf_op jit(solution)/shard_map/ppermute | solution.py:358
  28.1 3.3 %collective-permute-done.12.rest_4_ = bf16[640,128]{1,0:T(8,128)(2,1)S(1)} collective-permute-done((bf16[640,128]{1,0:T(8,128)(2,1)S(1)}, bf16[640,128]{1,0:T(8,128)(2,1)S(1)}, u32[]{:S(2)}, u32[]{:S(2)}) %collective-permute-start.12) | collective-permute-done | bytes 163872 | tf_op jit(solution)/shard_map/ppermute | solution.py:358
  31.9 0.5 %ready.1 = (f32[512,160]{1,0:T(8,128)S(1)}, f32[1,160]{1,0:T(1,128)S(1)}, bf16[1024,160]{1,0:T(8,128)(2,1)S(1)}, bf16[4,1024,160]{2,1,0:T(8,128)(2,1)S(1)}) custom-call(bf16[512,512]{1,0:T(8,128)(2,1)S(1)} %get-tuple-element.30.select_ref, f32[1,1280]{1,0:T(1,128)S(1)} %get-tuple-element.36.gain_ref, bf16[640,128]{1,0:T(8,128)(2,1)S(1)} %attend.1.token_ref.rest_0_, ...), custom_call_target="tpu_custom_call" | custom-call | flops 10737418240 | bytes 4194304 | tf_op jit(solution)/shard_map/ready/pallas_call | solution.py:424
  33.0 1.4 %project.1.token_ref.rest_0_ = bf16[656,128]{1,0:T(8,128)(2,1)S(1)} custom-call(bf16[640,128]{1,0:T(8,128)(2,1)S(1)} %attend.1.token_ref.rest_0_, bf16[640,128]{1,0:T(8,128)(2,1)S(1)} %collective-permute-done.9.rest_1_, bf16[640,128]{1,0:T(8,128)(2,1)S(1)} %collective-permute-done.10.rest_2_, bf16[640,128]{1,0:T(8,128)(2,1)S(1)} %collective-permute-done.11.rest_3_, ...), custom_call_target="tpu_custom_call" | custom-call | flops 536870912 | bytes 4194304 | tf_op jit(solution)/shard_map/project/pallas_call | solution.py:434
  34.8 1.0 %collective-permute-start.20 = (bf16[656,128]{1,0:T(8,128)(2,1)S(1)}, bf16[656,128]{1,0:T(8,128)(2,1)S(1)}, u32[]{:S(2)}, u32[]{:S(2)}) collective-permute-start(bf16[656,128]{1,0:T(8,128)(2,1)S(1)} %project.1.token_ref.rest_0_), channel_id=1, source_target_pairs={{0,4},{1,5},{2,6},{3,7},{4,0},{5,1},{6,2},{7,3},{8,12},{9,13},{10,... | collective-permute-start | bytes 503816 | tf_op jit(solution)/shard_map/ppermute | solution.py:358
  35.8 2.1 %collective-permute-start.22 = (bf16[656,128]{1,0:T(8,128)(2,1)S(1)}, bf16[656,128]{1,0:T(8,128)(2,1)S(1)}, u32[]{:S(2)}, u32[]{:S(2)}) collective-permute-start(bf16[656,128]{1,0:T(8,128)(2,1)S(1)} %project.1.token_ref.rest_0_), channel_id=1, source_target_pairs={{0,6},{1,7},{2,4},{3,5},{4,2},{5,3},{6,0},{7,1},{8,14},{9,15},{10,... | collective-permute-start | bytes 503816 | tf_op jit(solution)/shard_map/ppermute | solution.py:358
  38.0 3.6 %collective-permute-done.18.rest_2_ = bf16[656,128]{1,0:T(8,128)(2,1)S(1)} collective-permute-done((bf16[656,128]{1,0:T(8,128)(2,1)S(1)}, bf16[656,128]{1,0:T(8,128)(2,1)S(1)}, u32[]{:S(2)}, u32[]{:S(2)}) %collective-permute-start.18) | collective-permute-done | bytes 167968 | tf_op jit(solution)/shard_map/ppermute | solution.py:358
  42.1 2.7 %collective-permute-done.22.rest_6_ = bf16[656,128]{1,0:T(8,128)(2,1)S(1)} collective-permute-done((bf16[656,128]{1,0:T(8,128)(2,1)S(1)}, bf16[656,128]{1,0:T(8,128)(2,1)S(1)}, u32[]{:S(2)}, u32[]{:S(2)}) %collective-permute-start.22) | collective-permute-done | bytes 167968 | tf_op jit(solution)/shard_map/ppermute | solution.py:358
  44.9 1.2 %merge_tail.1.rest_9_ = bf16[640,1024]{1,0:T(8,128)(2,1)S(1)} custom-call(bf16[640,5120]{1,0:T(8,128)(2,1)S(1)} %bitcast.1, bf16[656,128]{1,0:T(8,128)(2,1)S(1)} %project.1.token_ref.rest_0_), custom_call_target="tpu_custom_call" | custom-call | bytes 4194304 | tf_op jit(solution)/shard_map/merge_tail/pallas_call | solution.py:443
  46.2 3.0 %merge.1 = bf16[1,640,128]{2,1,0:T(8,128)(2,1)} custom-call(bf16[656,128]{1,0:T(8,128)(2,1)S(1)} %project.1.token_ref.rest_0_, bf16[656,128]{1,0:T(8,128)(2,1)S(1)} %collective-permute-done.17.rest_1_, bf16[656,128]{1,0:T(8,128)(2,1)S(1)} %collective-permute-done.18.rest_2_, bf16[656,128]{1,0:T(8,128)(2,1)S(1)} %collective-permute-done.19.rest_3_, ...), custom_call_target="tpu_custom_call" | custom-call | flops 838860800 | bytes 8388608 | tf_op jit(solution)/shard_map/merge/pallas_call | solution.py:446
  (36 shorter events, 2.4 us)
Async XLA Ops:
  1.7 6.5 %collective-permute-start = (bf16[64,640]{1,0:T(8,128)(2,1)S(1)}, bf16[64,640]{1,0:T(8,128)(2,1)S(1)}, u32[]{:S(2)}, u32[]{:S(2)}) collective-permute-start(bf16[64,640]{1,0:T(8,128)(2,1)S(1)} %get-tuple-element.25), channel_id=1, source_target_pairs={{0,1},{1,0},{2,3},{3,2},{4,5},{5,4},{6,7},{7,6},{8,9},{9,8},{10,11... | collective-permute-start | bytes 245768 | tf_op jit(solution)/shard_map/ppermute | solution.py:358
  2.3 8.6 %collective-permute-start.1 = (bf16[64,640]{1,0:T(8,128)(2,1)S(1)}, bf16[64,640]{1,0:T(8,128)(2,1)S(1)}, u32[]{:S(2)}, u32[]{:S(2)}) collective-permute-start(bf16[64,640]{1,0:T(8,128)(2,1)S(1)} %get-tuple-element.26), channel_id=1, source_target_pairs={{0,2},{1,3},{2,0},{3,1},{4,6},{5,7},{6,4},{7,5},{8,10},{9,11},{10,... | collective-permute-start | bytes 245768 | tf_op jit(solution)/shard_map/ppermute | solution.py:358
  4.8 6.0 %collective-permute-start.2 = (bf16[64,640]{1,0:T(8,128)(2,1)S(1)}, bf16[64,640]{1,0:T(8,128)(2,1)S(1)}, u32[]{:S(2)}, u32[]{:S(2)}) collective-permute-start(bf16[64,640]{1,0:T(8,128)(2,1)S(1)} %get-tuple-element.27), channel_id=1, source_target_pairs={{0,3},{1,2},{2,1},{3,0},{4,7},{5,6},{6,5},{7,4},{8,11},{9,10},{10,... | collective-permute-start | bytes 245768 | tf_op jit(solution)/shard_map/ppermute | solution.py:358
  4.9 8.0 %collective-permute-start.3 = (bf16[64,640]{1,0:T(8,128)(2,1)S(1)}, bf16[64,640]{1,0:T(8,128)(2,1)S(1)}, u32[]{:S(2)}, u32[]{:S(2)}) collective-permute-start(bf16[64,640]{1,0:T(8,128)(2,1)S(1)} %get-tuple-element.28), channel_id=1, source_target_pairs={{0,4},{1,5},{2,6},{3,7},{4,0},{5,1},{6,2},{7,3},{8,12},{9,13},{10,... | collective-permute-start | bytes 245768 | tf_op jit(solution)/shard_map/ppermute | solution.py:358
  6.7 13.0 %collective-permute-start.7 = (bf16[400,128]{1,0:T(8,128)(2,1)S(1)}, bf16[400,128]{1,0:T(8,128)(2,1)S(1)}, u32[]{:S(2)}, u32[]{:S(2)}) collective-permute-start(bf16[400,128]{1,0:T(8,128)(2,1)S(1)} %get-tuple-element.35.rest_8_), channel_id=1, source_target_pairs={{0,8},{8,16},{16,24},{24,0},{1,9},{9,17},{17,25},{25,1},{2,10},{10... | collective-permute-start | bytes 307208 | tf_op jit(solution)/shard_map/ppermute | solution.py:362
  8.2 11.5 %collective-permute-start.8 = (bf16[400,128]{1,0:T(8,128)(2,1)S(1)}, bf16[400,128]{1,0:T(8,128)(2,1)S(1)}, u32[]{:S(2)}, u32[]{:S(2)}) collective-permute-start(bf16[400,128]{1,0:T(8,128)(2,1)S(1)} %get-tuple-element.35.rest_8_), channel_id=1, source_target_pairs={{0,16},{8,24},{16,0},{24,8},{1,17},{9,25},{17,1},{25,9},{2,18},{10... | collective-permute-start | bytes 307208 | tf_op jit(solution)/shard_map/ppermute | solution.py:362
  10.8 7.9 %collective-permute-start.4 = (bf16[64,640]{1,0:T(8,128)(2,1)S(1)}, bf16[64,640]{1,0:T(8,128)(2,1)S(1)}, u32[]{:S(2)}, u32[]{:S(2)}) collective-permute-start(bf16[64,640]{1,0:T(8,128)(2,1)S(1)} %get-tuple-element.29), channel_id=1, source_target_pairs={{0,5},{1,4},{2,7},{3,6},{4,1},{5,0},{6,3},{7,2},{8,13},{9,12},{10,... | collective-permute-start | bytes 245768 | tf_op jit(solution)/shard_map/ppermute | solution.py:358
  10.8 8.8 %collective-permute-start.5 = (bf16[64,640]{1,0:T(8,128)(2,1)S(1)}, bf16[64,640]{1,0:T(8,128)(2,1)S(1)}, u32[]{:S(2)}, u32[]{:S(2)}) collective-permute-start(bf16[64,640]{1,0:T(8,128)(2,1)S(1)} %get-tuple-element.33), channel_id=1, source_target_pairs={{0,6},{1,7},{2,4},{3,5},{4,2},{5,3},{6,0},{7,1},{8,14},{9,15},{10,... | collective-permute-start | bytes 245768 | tf_op jit(solution)/shard_map/ppermute | solution.py:358
  12.9 6.8 %collective-permute-start.6 = (bf16[64,640]{1,0:T(8,128)(2,1)S(1)}, bf16[64,640]{1,0:T(8,128)(2,1)S(1)}, u32[]{:S(2)}, u32[]{:S(2)}) collective-permute-start(bf16[64,640]{1,0:T(8,128)(2,1)S(1)} %get-tuple-element.34), channel_id=1, source_target_pairs={{0,7},{1,6},{2,5},{3,4},{4,3},{5,2},{6,1},{7,0},{8,15},{9,14},{10,... | collective-permute-start | bytes 245768 | tf_op jit(solution)/shard_map/ppermute | solution.py:358
  21.1 7.0 %collective-permute-start.10 = (bf16[640,128]{1,0:T(8,128)(2,1)S(1)}, bf16[640,128]{1,0:T(8,128)(2,1)S(1)}, u32[]{:S(2)}, u32[]{:S(2)}) collective-permute-start(bf16[640,128]{1,0:T(8,128)(2,1)S(1)} %attend.1.token_ref.rest_0_), channel_id=1, source_target_pairs={{0,2},{1,3},{2,0},{3,1},{4,6},{5,7},{6,4},{7,5},{8,10},{9,11},{10,... | collective-permute-start | bytes 491528 | tf_op jit(solution)/shard_map/ppermute | solution.py:358
  22.6 8.8 %collective-permute-start.12 = (bf16[640,128]{1,0:T(8,128)(2,1)S(1)}, bf16[640,128]{1,0:T(8,128)(2,1)S(1)}, u32[]{:S(2)}, u32[]{:S(2)}) collective-permute-start(bf16[640,128]{1,0:T(8,128)(2,1)S(1)} %attend.1.token_ref.rest_0_), channel_id=1, source_target_pairs={{0,4},{1,5},{2,6},{3,7},{4,0},{5,1},{6,2},{7,3},{8,12},{9,13},{10,... | collective-permute-start | bytes 491528 | tf_op jit(solution)/shard_map/ppermute | solution.py:358
  22.9 8.6 %collective-permute-start.14 = (bf16[640,128]{1,0:T(8,128)(2,1)S(1)}, bf16[640,128]{1,0:T(8,128)(2,1)S(1)}, u32[]{:S(2)}, u32[]{:S(2)}) collective-permute-start(bf16[640,128]{1,0:T(8,128)(2,1)S(1)} %attend.1.token_ref.rest_0_), channel_id=1, source_target_pairs={{0,6},{1,7},{2,4},{3,5},{4,2},{5,3},{6,0},{7,1},{8,14},{9,15},{10,... | collective-permute-start | bytes 491528 | tf_op jit(solution)/shard_map/ppermute | solution.py:358
  24.6 7.3 %collective-permute-start.16 = (bf16[400,128]{1,0:T(8,128)(2,1)S(1)}, bf16[400,128]{1,0:T(8,128)(2,1)S(1)}, u32[]{:S(2)}, u32[]{:S(2)}) collective-permute-start(bf16[400,128]{1,0:T(8,128)(2,1)S(1)} %get-tuple-element.35.rest_8_), channel_id=1, source_target_pairs={{0,24},{8,0},{16,8},{24,16},{1,25},{9,1},{17,9},{25,17},{2,26},{10... | collective-permute-start | bytes 307208 | tf_op jit(solution)/shard_map/ppermute | solution.py:362
  25.6 6.8 %collective-permute-start.9 = (bf16[640,128]{1,0:T(8,128)(2,1)S(1)}, bf16[640,128]{1,0:T(8,128)(2,1)S(1)}, u32[]{:S(2)}, u32[]{:S(2)}) collective-permute-start(bf16[640,128]{1,0:T(8,128)(2,1)S(1)} %attend.1.token_ref.rest_0_), channel_id=1, source_target_pairs={{0,1},{1,0},{2,3},{3,2},{4,5},{5,4},{6,7},{7,6},{8,9},{9,8},{10,11... | collective-permute-start | bytes 491528 | tf_op jit(solution)/shard_map/ppermute | solution.py:358
  28.1 4.4 %collective-permute-start.11 = (bf16[640,128]{1,0:T(8,128)(2,1)S(1)}, bf16[640,128]{1,0:T(8,128)(2,1)S(1)}, u32[]{:S(2)}, u32[]{:S(2)}) collective-permute-start(bf16[640,128]{1,0:T(8,128)(2,1)S(1)} %collective-permute-done.10.rest_2_), channel_id=1, source_target_pairs={{0,1},{1,0},{2,3},{3,2},{4,5},{5,4},{6,7},{7,6},{8,9},{9,8},{10,11... | collective-permute-start | bytes 491528 | tf_op jit(solution)/shard_map/ppermute | solution.py:358
  31.4 1.4 %collective-permute-start.13 = (bf16[640,128]{1,0:T(8,128)(2,1)S(1)}, bf16[640,128]{1,0:T(8,128)(2,1)S(1)}, u32[]{:S(2)}, u32[]{:S(2)}) collective-permute-start(bf16[640,128]{1,0:T(8,128)(2,1)S(1)} %collective-permute-done.12.rest_4_), channel_id=1, source_target_pairs={{0,1},{1,0},{2,3},{3,2},{4,5},{5,4},{6,7},{7,6},{8,9},{9,8},{10,11... | collective-permute-start | bytes 491528 | tf_op jit(solution)/shard_map/ppermute | solution.py:358
  31.4 1.6 %collective-permute-start.15 = (bf16[640,128]{1,0:T(8,128)(2,1)S(1)}, bf16[640,128]{1,0:T(8,128)(2,1)S(1)}, u32[]{:S(2)}, u32[]{:S(2)}) collective-permute-start(bf16[640,128]{1,0:T(8,128)(2,1)S(1)} %collective-permute-done.14.rest_6_), channel_id=1, source_target_pairs={{0,1},{1,0},{2,3},{3,2},{4,5},{5,4},{6,7},{7,6},{8,9},{9,8},{10,11... | collective-permute-start | bytes 491528 | tf_op jit(solution)/shard_map/ppermute | solution.py:358
  34.5 7.1 %collective-permute-start.18 = (bf16[656,128]{1,0:T(8,128)(2,1)S(1)}, bf16[656,128]{1,0:T(8,128)(2,1)S(1)}, u32[]{:S(2)}, u32[]{:S(2)}) collective-permute-start(bf16[656,128]{1,0:T(8,128)(2,1)S(1)} %project.1.token_ref.rest_0_), channel_id=1, source_target_pairs={{0,2},{1,3},{2,0},{3,1},{4,6},{5,7},{6,4},{7,5},{8,10},{9,11},{10,... | collective-permute-start | bytes 503816 | tf_op jit(solution)/shard_map/ppermute | solution.py:358
  34.8 6.8 %collective-permute-start.20 = (bf16[656,128]{1,0:T(8,128)(2,1)S(1)}, bf16[656,128]{1,0:T(8,128)(2,1)S(1)}, u32[]{:S(2)}, u32[]{:S(2)}) collective-permute-start(bf16[656,128]{1,0:T(8,128)(2,1)S(1)} %project.1.token_ref.rest_0_), channel_id=1, source_target_pairs={{0,4},{1,5},{2,6},{3,7},{4,0},{5,1},{6,2},{7,3},{8,12},{9,13},{10,... | collective-permute-start | bytes 503816 | tf_op jit(solution)/shard_map/ppermute | solution.py:358
  35.8 9.0 %collective-permute-start.22 = (bf16[656,128]{1,0:T(8,128)(2,1)S(1)}, bf16[656,128]{1,0:T(8,128)(2,1)S(1)}, u32[]{:S(2)}, u32[]{:S(2)}) collective-permute-start(bf16[656,128]{1,0:T(8,128)(2,1)S(1)} %project.1.token_ref.rest_0_), channel_id=1, source_target_pairs={{0,6},{1,7},{2,4},{3,5},{4,2},{5,3},{6,0},{7,1},{8,14},{9,15},{10,... | collective-permute-start | bytes 503816 | tf_op jit(solution)/shard_map/ppermute | solution.py:358
  38.0 8.1 %collective-permute-start.17 = (bf16[656,128]{1,0:T(8,128)(2,1)S(1)}, bf16[656,128]{1,0:T(8,128)(2,1)S(1)}, u32[]{:S(2)}, u32[]{:S(2)}) collective-permute-start(bf16[656,128]{1,0:T(8,128)(2,1)S(1)} %project.1.token_ref.rest_0_), channel_id=1, source_target_pairs={{0,1},{1,0},{2,3},{3,2},{4,5},{5,4},{6,7},{7,6},{8,9},{9,8},{10,11... | collective-permute-start | bytes 503816 | tf_op jit(solution)/shard_map/ppermute | solution.py:358
  41.6 4.5 %collective-permute-start.19 = (bf16[656,128]{1,0:T(8,128)(2,1)S(1)}, bf16[656,128]{1,0:T(8,128)(2,1)S(1)}, u32[]{:S(2)}, u32[]{:S(2)}) collective-permute-start(bf16[656,128]{1,0:T(8,128)(2,1)S(1)} %collective-permute-done.18.rest_2_), channel_id=1, source_target_pairs={{0,1},{1,0},{2,3},{3,2},{4,5},{5,4},{6,7},{7,6},{8,9},{9,8},{10,11... | collective-permute-start | bytes 503816 | tf_op jit(solution)/shard_map/ppermute | solution.py:358
  41.6 4.5 %collective-permute-start.21 = (bf16[656,128]{1,0:T(8,128)(2,1)S(1)}, bf16[656,128]{1,0:T(8,128)(2,1)S(1)}, u32[]{:S(2)}, u32[]{:S(2)}) collective-permute-start(bf16[656,128]{1,0:T(8,128)(2,1)S(1)} %collective-permute-done.20.rest_4_), channel_id=1, source_target_pairs={{0,1},{1,0},{2,3},{3,2},{4,5},{5,4},{6,7},{7,6},{8,9},{9,8},{10,11... | collective-permute-start | bytes 503816 | tf_op jit(solution)/shard_map/ppermute | solution.py:358
  44.8 1.4 %collective-permute-start.23 = (bf16[656,128]{1,0:T(8,128)(2,1)S(1)}, bf16[656,128]{1,0:T(8,128)(2,1)S(1)}, u32[]{:S(2)}, u32[]{:S(2)}) collective-permute-start(bf16[656,128]{1,0:T(8,128)(2,1)S(1)} %collective-permute-done.22.rest_6_), channel_id=1, source_target_pairs={{0,1},{1,0},{2,3},{3,2},{4,5},{5,4},{6,7},{7,6},{8,9},{9,8},{10,11... | collective-permute-start | bytes 503816 | tf_op jit(solution)/shard_map/ppermute | solution.py:358
  (2 other events, 25.8 us)

commit v5 on v4

--- a/solution.py
+++ b/solution.py
@@ -122,6 +122,8 @@
 REST = HPAIR - WIDE
 MAIN = ROWS * WIDE
 NOTES = 16
+BLOCK_ORDER = (0, 6, 7, 2, 4, 3, 5, 1)
+PIECE_ORDER = (0, 6, 2, 4, 1, 7, 3, 5)
 ROOT = math.log2(math.e) / math.sqrt(HDIM)
 BF16 = jnp.bfloat16
 F32 = jnp.float32
@@ -205,11 +207,11 @@
     me = row_index()
     band = blocks[0].shape[0]
     patches = band * ROWS
-    for step in range(ROWS):
+    for step, block in zip(BLOCK_ORDER, blocks):
         at = pl.ds(pl.multiple_of((me ^ step) * band, band), band)
-        q_all[at, :] = blocks[step][:, :HPAIR]
-        k_all[at, :] = blocks[step][:, HPAIR : 2 * HPAIR]
-        v_all[at, :] = blocks[step][:, 2 * HPAIR : 3 * HPAIR]
+        q_all[at, :] = block[:, :HPAIR]
+        k_all[at, :] = block[:, HPAIR : 2 * HPAIR]
+        v_all[at, :] = block[:, 2 * HPAIR : 3 * HPAIR]
     queries = jnp.dot(select_ref[...], q_all[...], preferred_element_type=F32).astype(BF16)
     lane = lax.broadcasted_iota(jnp.int32, (1, HPAIR), 1)
     keys, values, dead = k_all[...], v_all[...], dead_ref[...]
@@ -233,9 +235,9 @@
     me = row_index()
     page = lax.axis_index("page")
     band = blocks[0].shape[0]
-    for step in range(ROWS):
+    for step, block in zip(BLOCK_ORDER, blocks):
         at = pl.ds(pl.multiple_of((me ^ step) * band, band), band)
-        held[at, :] = blocks[step][:, 3 * HPAIR :]
+        held[at, :] = block[:, 3 * HPAIR :]
     resid_ref[...] = jnp.dot(select_ref[...], held[...], preferred_element_type=F32)
     gain = jnp.zeros(gain_out.shape, F32)
     for pair in range(ROWS):
@@ -261,8 +263,8 @@
 
 def collect(pieces, full):
     me = row_index()
-    for step in range(ROWS):
-        full[:, pl.ds(pl.multiple_of((me ^ step) * WIDE, WIDE), WIDE)] = pieces[step][...]
+    for step, piece in zip(PIECE_ORDER, pieces):
+        full[:, pl.ds(pl.multiple_of((me ^ step) * WIDE, WIDE), WIDE)] = piece[...]
 
 
 def project_kernel(*rest):
@@ -364,8 +366,7 @@
 
 def gather_rows(value):
     far = [swap(value, step) for step in (6, 2, 4)]
-    near = [swap(piece, 1) for piece in [value] + far]
-    return [value, near[0], far[1], near[2], far[2], near[3], far[0], near[1]]
+    return [value] + far + [swap(piece, 1) for piece in [value] + far]
 
 
 def local_eight(qkv_rows, residual, out_weight, norm_gain, merge_weight, merge_bias, page_grid):
@@ -393,7 +394,7 @@
         limit=24,
         moved=1 << 20,
     )(in_hbm(qkv_rows), in_hbm(residual), in_hbm(out_weight), in_hbm(page_grid))
-    blocks = [sends[0]] + [swap(sends[step], step) for step in range(1, ROWS)]
+    blocks = [sends[0]] + [swap(sends[step], step) for step in BLOCK_ORDER[1:]]
     slices = [own] + [turn(own, step) for step in range(1, PAGES)]
     select, dead, live, gain, bias = kernel(
         layout_kernel,

time: 49.5 us -> 50.1 us (1.012)
  starting transfers between devices: 21.1 us -> 21.9 us
    ppermute x21, waiting for transfers between devices: 17.9 us -> 16 us  [swap(): lax.ppermute(value, 'row', [(row, row ^ step) for row in range(ROWS)])]
    ppermute x3, waiting for transfers between devices: 0.01 us -> 1.64 us  [turn(): lax.ppermute(value, 'page', [(page, (page + step) % PAGES) for page in ra...]
    ppermute x3, starting transfers between devices: 5.2 us -> 5.83 us  [turn(): lax.ppermute(value, 'page', [(page, (page + step) % PAGES) for page in ra...]
  transfers between devices with their start and end apart: 24 -> 24, of which waited for: 8 -> 10; matrix products, arithmetic and copies ran while one was open for 0% -> 0% of each run, Pallas kernels for 5% -> 5%
where the time goes in v5:
time: 50.1 us; the launch traced here: 49.8 us
  starting transfers between devices  21.9 us (44%)
  waiting for transfers between devices  17.7 us (35%)
  Pallas kernels  10.2 us (20%)
    ppermute x21, waiting for transfers between devices, swap(): lax.ppermute(value, 'row', [(row, row ^ step) for row in range(ROWS)])  16 us
    ppermute x21, starting transfers between devices, swap(): lax.ppermute(value, 'row', [(row, row ^ step) for row in range(ROWS)])  16 us
    ppermute x3, starting transfers between devices, turn(): lax.ppermute(value, 'page', [(page, (page + step) % PAGES) for page in ra...  5.83 us
    pallas_call x1, Pallas kernels, local_eight(): kernel(merge_kernel, 'merge', shape(1, units, groups), [pltpu.VMEM((piece...  3.01 us
    pallas_call x1, Pallas kernels, local_eight(): kernel(spread_kernel, 'spread', [shape(band, 4 * HPAIR)] * ROWS + [shape(...  1.74 us
    ppermute x3, waiting for transfers between devices, turn(): lax.ppermute(value, 'page', [(page, (page + step) % PAGES) for page in ra...  1.64 us
    pallas_call x1, Pallas kernels, local_eight(): kernel(project_kernel, 'project', shape(piece + NOTES, WIDE), [pltpu.VMEM...  1.42 us
    pallas_call x1, Pallas kernels, local_eight(): kernel(attend_kernel, 'attend', shape(piece, WIDE), [pltpu.VMEM((patches,...  1.34 us
  transfers between devices with their start and end apart: 24, of which 10 were waited for; matrix products, arithmetic and copies ran while one was open for 0% of the time, Pallas kernels for 5%

profile of v5, /device:TPU:0, one launch (start us, length us, event | category | flops | bytes accessed | tf_op | source)
XLA Modules:
  0.0 49.8 jit_solution(9522818001003123041)
XLA Ops:
  0.0 1.7 %spread.1 = (bf16[64,640]{1,0:T(8,128)(2,1)S(1)}, bf16[64,640]{1,0:T(8,128)(2,1)S(1)}, bf16[64,640]{1,0:T(8,128)(2,1)S(1)}, bf16[64,640]{1,0:T(8,128)(2,1)S(1)},...) custom-call(bf16[1,64,3840]{2,1,0:T(8,128)(2,1)} %qkv_hbm.1, ...), custom_call_target="tpu_custom_call" | custom-call | bytes 1048576 | tf_op jit(solution)/shard_map/spread/pallas_call | solution.py:380
  1.7 4.0 %collective-permute-start = (bf16[64,640]{1,0:T(8,128)(2,1)S(1)}, bf16[64,640]{1,0:T(8,128)(2,1)S(1)}, u32[]{:S(2)}, u32[]{:S(2)}) collective-permute-start(bf16[64,640]{1,0:T(8,128)(2,1)S(1)} %get-tuple-element.25), channel_id=1, source_target_pairs={{0,6},{1,7},{2,4},{3,5},{4,2},{5,3},{6,0},{7,1},{8,14},{9,15},{10,... | collective-permute-start | bytes 245768 | tf_op jit(solution)/shard_map/ppermute | solution.py:360
  5.7 1.1 %collective-permute-start.2 = (bf16[64,640]{1,0:T(8,128)(2,1)S(1)}, bf16[64,640]{1,0:T(8,128)(2,1)S(1)}, u32[]{:S(2)}, u32[]{:S(2)}) collective-permute-start(bf16[64,640]{1,0:T(8,128)(2,1)S(1)} %get-tuple-element.27), channel_id=1, source_target_pairs={{0,2},{1,3},{2,0},{3,1},{4,6},{5,7},{6,4},{7,5},{8,10},{9,11},{10,... | collective-permute-start | bytes 245768 | tf_op jit(solution)/shard_map/ppermute | solution.py:360
  6.8 1.5 %collective-permute-start.3 = (bf16[64,640]{1,0:T(8,128)(2,1)S(1)}, bf16[64,640]{1,0:T(8,128)(2,1)S(1)}, u32[]{:S(2)}, u32[]{:S(2)}) collective-permute-start(bf16[64,640]{1,0:T(8,128)(2,1)S(1)} %get-tuple-element.28), channel_id=1, source_target_pairs={{0,4},{1,5},{2,6},{3,7},{4,0},{5,1},{6,2},{7,3},{8,12},{9,13},{10,... | collective-permute-start | bytes 245768 | tf_op jit(solution)/shard_map/ppermute | solution.py:360
  8.4 1.6 %collective-permute-start.7 = (bf16[400,128]{1,0:T(8,128)(2,1)S(1)}, bf16[400,128]{1,0:T(8,128)(2,1)S(1)}, u32[]{:S(2)}, u32[]{:S(2)}) collective-permute-start(bf16[400,128]{1,0:T(8,128)(2,1)S(1)} %get-tuple-element.35.rest_8_), channel_id=1, source_target_pairs={{0,8},{8,16},{16,24},{24,0},{1,9},{9,17},{17,25},{25,1},{2,10},{10... | collective-permute-start | bytes 307208 | tf_op jit(solution)/shard_map/ppermute | solution.py:364
  9.9 2.6 %collective-permute-start.8 = (bf16[400,128]{1,0:T(8,128)(2,1)S(1)}, bf16[400,128]{1,0:T(8,128)(2,1)S(1)}, u32[]{:S(2)}, u32[]{:S(2)}) collective-permute-start(bf16[400,128]{1,0:T(8,128)(2,1)S(1)} %get-tuple-element.35.rest_8_), channel_id=1, source_target_pairs={{0,16},{8,24},{16,0},{24,8},{1,17},{9,25},{17,1},{25,9},{2,18},{10... | collective-permute-start | bytes 307208 | tf_op jit(solution)/shard_map/ppermute | solution.py:364
  12.5 2.3 %collective-permute-start.5 = (bf16[64,640]{1,0:T(8,128)(2,1)S(1)}, bf16[64,640]{1,0:T(8,128)(2,1)S(1)}, u32[]{:S(2)}, u32[]{:S(2)}) collective-permute-start(bf16[64,640]{1,0:T(8,128)(2,1)S(1)} %get-tuple-element.33), channel_id=1, source_target_pairs={{0,5},{1,4},{2,7},{3,6},{4,1},{5,0},{6,3},{7,2},{8,13},{9,12},{10,... | collective-permute-start | bytes 245768 | tf_op jit(solution)/shard_map/ppermute | solution.py:360
  14.8 2.4 %collective-permute-done.4.rest_4_.rest_5_ = bf16[64,640]{1,0:T(8,128)(2,1)S(1)} collective-permute-done((bf16[64,640]{1,0:T(8,128)(2,1)S(1)}, bf16[64,640]{1,0:T(8,128)(2,1)S(1)}, u32[]{:S(2)}, u32[]{:S(2)}) %collective-permute-start.4) | collective-permute-done | bytes 81952 | tf_op jit(solution)/shard_map/ppermute | solution.py:360
  17.2 0.9 %layout.1 = (bf16[512,512]{1,0:T(8,128)(2,1)S(1)}, f32[1,512]{1,0:T(1,128)S(1)}, f32[1,128]{1,0:T(1,128)S(1)}, f32[1,1280]{1,0:T(1,128)S(1)}, f32[640,1]{1,0:T(8,128)S(1)}) custom-call(s32[8,128]{1,0:T(8,128)S(1)} %get-tuple-element.24.grid_ref, f32[1280]{0:T(1024)} %gain_hbm.1, f32[640]{0:T(1024)} %bias_hbm.1, ...), custom_call_target="tpu_custom_call" | custom-call | bytes 1048576 | tf_op jit(solution)/shard_map/layout/pallas_call | solution.py:399
  18.1 1.6 %collective-permute-done.8.rest_9_.rest_10_ = bf16[400,128]{1,0:T(8,128)(2,1)S(1)} collective-permute-done((bf16[400,128]{1,0:T(8,128)(2,1)S(1)}, bf16[400,128]{1,0:T(8,128)(2,1)S(1)}, u32[]{:S(2)}, u32[]{:S(2)}) %collective-permute-start.8) | collective-permute-done | bytes 102432 | tf_op jit(solution)/shard_map/ppermute | solution.py:364
  19.8 1.3 %attend.1.token_ref.rest_0_ = bf16[640,128]{1,0:T(8,128)(2,1)S(1)} custom-call(bf16[512,512]{1,0:T(8,128)(2,1)S(1)} %get-tuple-element.30.select_ref, f32[1,512]{1,0:T(1,128)S(1)} %get-tuple-element.31.dead_ref, bf16[64,640]{1,0:T(8,128)(2,1)S(1)} %get-tuple-element.32.rest_0_, bf16[64,640]{1,0:T(8,128)(2,1)S(1)} %collective-permute-done.rest_0_.rest_1_, ...), custom_call_target="tpu_custom_call" | custom-call | flops 21474836480 | bytes 1048576 | tf_op jit(solution)/shard_map/attend/pallas_call | solution.py:415
  21.7 1.5 %collective-permute-start.10 = (bf16[640,128]{1,0:T(8,128)(2,1)S(1)}, bf16[640,128]{1,0:T(8,128)(2,1)S(1)}, u32[]{:S(2)}, u32[]{:S(2)}) collective-permute-start(bf16[640,128]{1,0:T(8,128)(2,1)S(1)} %attend.1.token_ref.rest_0_), channel_id=1, source_target_pairs={{0,2},{1,3},{2,0},{3,1},{4,6},{5,7},{6,4},{7,5},{8,10},{9,11},{10,... | collective-permute-start | bytes 491528 | tf_op jit(solution)/shard_map/ppermute | solution.py:360
  23.2 1.5 %collective-permute-start.11 = (bf16[640,128]{1,0:T(8,128)(2,1)S(1)}, bf16[640,128]{1,0:T(8,128)(2,1)S(1)}, u32[]{:S(2)}, u32[]{:S(2)}) collective-permute-start(bf16[640,128]{1,0:T(8,128)(2,1)S(1)} %attend.1.token_ref.rest_0_), channel_id=1, source_target_pairs={{0,4},{1,5},{2,6},{3,7},{4,0},{5,1},{6,2},{7,3},{8,12},{9,13},{10,... | collective-permute-start | bytes 491528 | tf_op jit(solution)/shard_map/ppermute | solution.py:360
  24.7 1.7 %collective-permute-start.16 = (bf16[400,128]{1,0:T(8,128)(2,1)S(1)}, bf16[400,128]{1,0:T(8,128)(2,1)S(1)}, u32[]{:S(2)}, u32[]{:S(2)}) collective-permute-start(bf16[400,128]{1,0:T(8,128)(2,1)S(1)} %get-tuple-element.35.rest_8_), channel_id=1, source_target_pairs={{0,24},{8,0},{16,8},{24,16},{1,25},{9,1},{17,9},{25,17},{2,26},{10... | collective-permute-start | bytes 307208 | tf_op jit(solution)/shard_map/ppermute | solution.py:364
  26.4 2.8 %collective-permute-done.9.rest_1_ = bf16[640,128]{1,0:T(8,128)(2,1)S(1)} collective-permute-done((bf16[640,128]{1,0:T(8,128)(2,1)S(1)}, bf16[640,128]{1,0:T(8,128)(2,1)S(1)}, u32[]{:S(2)}, u32[]{:S(2)}) %collective-permute-start.9) | collective-permute-done | bytes 163872 | tf_op jit(solution)/shard_map/ppermute | solution.py:360
  29.2 1.6 %collective-permute-done.10.rest_2_ = bf16[640,128]{1,0:T(8,128)(2,1)S(1)} collective-permute-done((bf16[640,128]{1,0:T(8,128)(2,1)S(1)}, bf16[640,128]{1,0:T(8,128)(2,1)S(1)}, u32[]{:S(2)}, u32[]{:S(2)}) %collective-permute-start.10) | collective-permute-done | bytes 163872 | tf_op jit(solution)/shard_map/ppermute | solution.py:360
  30.8 1.0 %collective-permute-done.11.rest_3_ = bf16[640,128]{1,0:T(8,128)(2,1)S(1)} collective-permute-done((bf16[640,128]{1,0:T(8,128)(2,1)S(1)}, bf16[640,128]{1,0:T(8,128)(2,1)S(1)}, u32[]{:S(2)}, u32[]{:S(2)}) %collective-permute-start.11) | collective-permute-done | bytes 163872 | tf_op jit(solution)/shard_map/ppermute | solution.py:360
  33.2 1.4 %project.1.token_ref.rest_0_ = bf16[656,128]{1,0:T(8,128)(2,1)S(1)} custom-call(bf16[640,128]{1,0:T(8,128)(2,1)S(1)} %attend.1.token_ref.rest_0_, bf16[640,128]{1,0:T(8,128)(2,1)S(1)} %collective-permute-done.9.rest_1_, bf16[640,128]{1,0:T(8,128)(2,1)S(1)} %collective-permute-done.10.rest_2_, bf16[640,128]{1,0:T(8,128)(2,1)S(1)} %collective-permute-done.11.rest_3_, ...), custom_call_target="tpu_custom_call" | custom-call | flops 536870912 | bytes 4194304 | tf_op jit(solution)/shard_map/project/pallas_call | solution.py:435
  35.4 1.5 %collective-permute-start.18 = (bf16[656,128]{1,0:T(8,128)(2,1)S(1)}, bf16[656,128]{1,0:T(8,128)(2,1)S(1)}, u32[]{:S(2)}, u32[]{:S(2)}) collective-permute-start(bf16[656,128]{1,0:T(8,128)(2,1)S(1)} %project.1.token_ref.rest_0_), channel_id=1, source_target_pairs={{0,2},{1,3},{2,0},{3,1},{4,6},{5,7},{6,4},{7,5},{8,10},{9,11},{10,... | collective-permute-start | bytes 503816 | tf_op jit(solution)/shard_map/ppermute | solution.py:360
  36.9 1.2 %collective-permute-start.19 = (bf16[656,128]{1,0:T(8,128)(2,1)S(1)}, bf16[656,128]{1,0:T(8,128)(2,1)S(1)}, u32[]{:S(2)}, u32[]{:S(2)}) collective-permute-start(bf16[656,128]{1,0:T(8,128)(2,1)S(1)} %project.1.token_ref.rest_0_), channel_id=1, source_target_pairs={{0,4},{1,5},{2,6},{3,7},{4,0},{5,1},{6,2},{7,3},{8,12},{9,13},{10,... | collective-permute-start | bytes 503816 | tf_op jit(solution)/shard_map/ppermute | solution.py:360
  38.1 4.6 %collective-permute-done.17.rest_1_ = bf16[656,128]{1,0:T(8,128)(2,1)S(1)} collective-permute-done((bf16[656,128]{1,0:T(8,128)(2,1)S(1)}, bf16[656,128]{1,0:T(8,128)(2,1)S(1)}, u32[]{:S(2)}, u32[]{:S(2)}) %collective-permute-start.17) | collective-permute-done | bytes 167968 | tf_op jit(solution)/shard_map/ppermute | solution.py:360
  42.7 2.3 %collective-permute-done.18.rest_2_ = bf16[656,128]{1,0:T(8,128)(2,1)S(1)} collective-permute-done((bf16[656,128]{1,0:T(8,128)(2,1)S(1)}, bf16[656,128]{1,0:T(8,128)(2,1)S(1)}, u32[]{:S(2)}, u32[]{:S(2)}) %collective-permute-start.18) | collective-permute-done | bytes 167968 | tf_op jit(solution)/shard_map/ppermute | solution.py:360
  45.5 1.2 %merge_tail.1.rest_9_ = bf16[640,1024]{1,0:T(8,128)(2,1)S(1)} custom-call(bf16[640,5120]{1,0:T(8,128)(2,1)S(1)} %bitcast.1, bf16[656,128]{1,0:T(8,128)(2,1)S(1)} %project.1.token_ref.rest_0_), custom_call_target="tpu_custom_call" | custom-call | bytes 4194304 | tf_op jit(solution)/shard_map/merge_tail/pallas_call | solution.py:444
  46.8 3.0 %merge.1 = bf16[1,640,128]{2,1,0:T(8,128)(2,1)} custom-call(bf16[656,128]{1,0:T(8,128)(2,1)S(1)} %project.1.token_ref.rest_0_, bf16[656,128]{1,0:T(8,128)(2,1)S(1)} %collective-permute-done.17.rest_1_, bf16[656,128]{1,0:T(8,128)(2,1)S(1)} %collective-permute-done.18.rest_2_, bf16[656,128]{1,0:T(8,128)(2,1)S(1)} %collective-permute-done.19.rest_3_, ...), custom_call_target="tpu_custom_call" | custom-call | flops 838860800 | bytes 8388608 | tf_op jit(solution)/shard_map/merge/pallas_call | solution.py:447
  (36 shorter events, 3.4 us)
Async XLA Ops:
  1.7 8.2 %collective-permute-start = (bf16[64,640]{1,0:T(8,128)(2,1)S(1)}, bf16[64,640]{1,0:T(8,128)(2,1)S(1)}, u32[]{:S(2)}, u32[]{:S(2)}) collective-permute-start(bf16[64,640]{1,0:T(8,128)(2,1)S(1)} %get-tuple-element.25), channel_id=1, source_target_pairs={{0,6},{1,7},{2,4},{3,5},{4,2},{5,3},{6,0},{7,1},{8,14},{9,15},{10,... | collective-permute-start | bytes 245768 | tf_op jit(solution)/shard_map/ppermute | solution.py:360
  5.7 6.8 %collective-permute-start.1 = (bf16[64,640]{1,0:T(8,128)(2,1)S(1)}, bf16[64,640]{1,0:T(8,128)(2,1)S(1)}, u32[]{:S(2)}, u32[]{:S(2)}) collective-permute-start(bf16[64,640]{1,0:T(8,128)(2,1)S(1)} %get-tuple-element.26), channel_id=1, source_target_pairs={{0,7},{1,6},{2,5},{3,4},{4,3},{5,2},{6,1},{7,0},{8,15},{9,14},{10,... | collective-permute-start | bytes 245768 | tf_op jit(solution)/shard_map/ppermute | solution.py:360
  5.7 6.8 %collective-permute-start.2 = (bf16[64,640]{1,0:T(8,128)(2,1)S(1)}, bf16[64,640]{1,0:T(8,128)(2,1)S(1)}, u32[]{:S(2)}, u32[]{:S(2)}) collective-permute-start(bf16[64,640]{1,0:T(8,128)(2,1)S(1)} %get-tuple-element.27), channel_id=1, source_target_pairs={{0,2},{1,3},{2,0},{3,1},{4,6},{5,7},{6,4},{7,5},{8,10},{9,11},{10,... | collective-permute-start | bytes 245768 | tf_op jit(solution)/shard_map/ppermute | solution.py:360
  6.8 8.0 %collective-permute-start.3 = (bf16[64,640]{1,0:T(8,128)(2,1)S(1)}, bf16[64,640]{1,0:T(8,128)(2,1)S(1)}, u32[]{:S(2)}, u32[]{:S(2)}) collective-permute-start(bf16[64,640]{1,0:T(8,128)(2,1)S(1)} %get-tuple-element.28), channel_id=1, source_target_pairs={{0,4},{1,5},{2,6},{3,7},{4,0},{5,1},{6,2},{7,3},{8,12},{9,13},{10,... | collective-permute-start | bytes 245768 | tf_op jit(solution)/shard_map/ppermute | solution.py:360
  8.4 9.8 %collective-permute-start.7 = (bf16[400,128]{1,0:T(8,128)(2,1)S(1)}, bf16[400,128]{1,0:T(8,128)(2,1)S(1)}, u32[]{:S(2)}, u32[]{:S(2)}) collective-permute-start(bf16[400,128]{1,0:T(8,128)(2,1)S(1)} %get-tuple-element.35.rest_8_), channel_id=1, source_target_pairs={{0,8},{8,16},{16,24},{24,0},{1,9},{9,17},{17,25},{25,1},{2,10},{10... | collective-permute-start | bytes 307208 | tf_op jit(solution)/shard_map/ppermute | solution.py:364
  9.9 9.9 %collective-permute-start.8 = (bf16[400,128]{1,0:T(8,128)(2,1)S(1)}, bf16[400,128]{1,0:T(8,128)(2,1)S(1)}, u32[]{:S(2)}, u32[]{:S(2)}) collective-permute-start(bf16[400,128]{1,0:T(8,128)(2,1)S(1)} %get-tuple-element.35.rest_8_), channel_id=1, source_target_pairs={{0,16},{8,24},{16,0},{24,8},{1,17},{9,25},{17,1},{25,9},{2,18},{10... | collective-permute-start | bytes 307208 | tf_op jit(solution)/shard_map/ppermute | solution.py:364
  12.5 4.7 %collective-permute-start.4 = (bf16[64,640]{1,0:T(8,128)(2,1)S(1)}, bf16[64,640]{1,0:T(8,128)(2,1)S(1)}, u32[]{:S(2)}, u32[]{:S(2)}) collective-permute-start(bf16[64,640]{1,0:T(8,128)(2,1)S(1)} %get-tuple-element.29), channel_id=1, source_target_pairs={{0,3},{1,2},{2,1},{3,0},{4,7},{5,6},{6,5},{7,4},{8,11},{9,10},{10,... | collective-permute-start | bytes 245768 | tf_op jit(solution)/shard_map/ppermute | solution.py:360
  12.5 5.6 %collective-permute-start.5 = (bf16[64,640]{1,0:T(8,128)(2,1)S(1)}, bf16[64,640]{1,0:T(8,128)(2,1)S(1)}, u32[]{:S(2)}, u32[]{:S(2)}) collective-permute-start(bf16[64,640]{1,0:T(8,128)(2,1)S(1)} %get-tuple-element.33), channel_id=1, source_target_pairs={{0,5},{1,4},{2,7},{3,6},{4,1},{5,0},{6,3},{7,2},{8,13},{9,12},{10,... | collective-permute-start | bytes 245768 | tf_op jit(solution)/shard_map/ppermute | solution.py:360
  14.8 3.3 %collective-permute-start.6 = (bf16[64,640]{1,0:T(8,128)(2,1)S(1)}, bf16[64,640]{1,0:T(8,128)(2,1)S(1)}, u32[]{:S(2)}, u32[]{:S(2)}) collective-permute-start(bf16[64,640]{1,0:T(8,128)(2,1)S(1)} %get-tuple-element.34), channel_id=1, source_target_pairs={{0,1},{1,0},{2,3},{3,2},{4,5},{5,4},{6,7},{7,6},{8,9},{9,8},{10,11... | collective-permute-start | bytes 245768 | tf_op jit(solution)/shard_map/ppermute | solution.py:360
  21.1 8.1 %collective-permute-start.9 = (bf16[640,128]{1,0:T(8,128)(2,1)S(1)}, bf16[640,128]{1,0:T(8,128)(2,1)S(1)}, u32[]{:S(2)}, u32[]{:S(2)}) collective-permute-start(bf16[640,128]{1,0:T(8,128)(2,1)S(1)} %attend.1.token_ref.rest_0_), channel_id=1, source_target_pairs={{0,6},{1,7},{2,4},{3,5},{4,2},{5,3},{6,0},{7,1},{8,14},{9,15},{10,... | collective-permute-start | bytes 491528 | tf_op jit(solution)/shard_map/ppermute | solution.py:360
  21.7 9.1 %collective-permute-start.10 = (bf16[640,128]{1,0:T(8,128)(2,1)S(1)}, bf16[640,128]{1,0:T(8,128)(2,1)S(1)}, u32[]{:S(2)}, u32[]{:S(2)}) collective-permute-start(bf16[640,128]{1,0:T(8,128)(2,1)S(1)} %attend.1.token_ref.rest_0_), channel_id=1, source_target_pairs={{0,2},{1,3},{2,0},{3,1},{4,6},{5,7},{6,4},{7,5},{8,10},{9,11},{10,... | collective-permute-start | bytes 491528 | tf_op jit(solution)/shard_map/ppermute | solution.py:360
  23.2 8.6 %collective-permute-start.11 = (bf16[640,128]{1,0:T(8,128)(2,1)S(1)}, bf16[640,128]{1,0:T(8,128)(2,1)S(1)}, u32[]{:S(2)}, u32[]{:S(2)}) collective-permute-start(bf16[640,128]{1,0:T(8,128)(2,1)S(1)} %attend.1.token_ref.rest_0_), channel_id=1, source_target_pairs={{0,4},{1,5},{2,6},{3,7},{4,0},{5,1},{6,2},{7,3},{8,12},{9,13},{10,... | collective-permute-start | bytes 491528 | tf_op jit(solution)/shard_map/ppermute | solution.py:360
  24.7 7.1 %collective-permute-start.16 = (bf16[400,128]{1,0:T(8,128)(2,1)S(1)}, bf16[400,128]{1,0:T(8,128)(2,1)S(1)}, u32[]{:S(2)}, u32[]{:S(2)}) collective-permute-start(bf16[400,128]{1,0:T(8,128)(2,1)S(1)} %get-tuple-element.35.rest_8_), channel_id=1, source_target_pairs={{0,24},{8,0},{16,8},{24,16},{1,25},{9,1},{17,9},{25,17},{2,26},{10... | collective-permute-start | bytes 307208 | tf_op jit(solution)/shard_map/ppermute | solution.py:364
  26.4 6.0 %collective-permute-start.12 = (bf16[640,128]{1,0:T(8,128)(2,1)S(1)}, bf16[640,128]{1,0:T(8,128)(2,1)S(1)}, u32[]{:S(2)}, u32[]{:S(2)}) collective-permute-start(bf16[640,128]{1,0:T(8,128)(2,1)S(1)} %attend.1.token_ref.rest_0_), channel_id=1, source_target_pairs={{0,1},{1,0},{2,3},{3,2},{4,5},{5,4},{6,7},{7,6},{8,9},{9,8},{10,11... | collective-permute-start | bytes 491528 | tf_op jit(solution)/shard_map/ppermute | solution.py:360
  29.2 3.1 %collective-permute-start.13 = (bf16[640,128]{1,0:T(8,128)(2,1)S(1)}, bf16[640,128]{1,0:T(8,128)(2,1)S(1)}, u32[]{:S(2)}, u32[]{:S(2)}) collective-permute-start(bf16[640,128]{1,0:T(8,128)(2,1)S(1)} %collective-permute-done.9.rest_1_), channel_id=1, source_target_pairs={{0,1},{1,0},{2,3},{3,2},{4,5},{5,4},{6,7},{7,6},{8,9},{9,8},{10,11... | collective-permute-start | bytes 491528 | tf_op jit(solution)/shard_map/ppermute | solution.py:360
  30.8 1.6 %collective-permute-start.14 = (bf16[640,128]{1,0:T(8,128)(2,1)S(1)}, bf16[640,128]{1,0:T(8,128)(2,1)S(1)}, u32[]{:S(2)}, u32[]{:S(2)}) collective-permute-start(bf16[640,128]{1,0:T(8,128)(2,1)S(1)} %collective-permute-done.10.rest_2_), channel_id=1, source_target_pairs={{0,1},{1,0},{2,3},{3,2},{4,5},{5,4},{6,7},{7,6},{8,9},{9,8},{10,11... | collective-permute-start | bytes 491528 | tf_op jit(solution)/shard_map/ppermute | solution.py:360
  31.8 1.4 %collective-permute-start.15 = (bf16[640,128]{1,0:T(8,128)(2,1)S(1)}, bf16[640,128]{1,0:T(8,128)(2,1)S(1)}, u32[]{:S(2)}, u32[]{:S(2)}) collective-permute-start(bf16[640,128]{1,0:T(8,128)(2,1)S(1)} %collective-permute-done.11.rest_3_), channel_id=1, source_target_pairs={{0,1},{1,0},{2,3},{3,2},{4,5},{5,4},{6,7},{7,6},{8,9},{9,8},{10,11... | collective-permute-start | bytes 491528 | tf_op jit(solution)/shard_map/ppermute | solution.py:360
  34.6 8.1 %collective-permute-start.17 = (bf16[656,128]{1,0:T(8,128)(2,1)S(1)}, bf16[656,128]{1,0:T(8,128)(2,1)S(1)}, u32[]{:S(2)}, u32[]{:S(2)}) collective-permute-start(bf16[656,128]{1,0:T(8,128)(2,1)S(1)} %project.1.token_ref.rest_0_), channel_id=1, source_target_pairs={{0,6},{1,7},{2,4},{3,5},{4,2},{5,3},{6,0},{7,1},{8,14},{9,15},{10,... | collective-permute-start | bytes 503816 | tf_op jit(solution)/shard_map/ppermute | solution.py:360
  35.4 9.6 %collective-permute-start.18 = (bf16[656,128]{1,0:T(8,128)(2,1)S(1)}, bf16[656,128]{1,0:T(8,128)(2,1)S(1)}, u32[]{:S(2)}, u32[]{:S(2)}) collective-permute-start(bf16[656,128]{1,0:T(8,128)(2,1)S(1)} %project.1.token_ref.rest_0_), channel_id=1, source_target_pairs={{0,2},{1,3},{2,0},{3,1},{4,6},{5,7},{6,4},{7,5},{8,10},{9,11},{10,... | collective-permute-start | bytes 503816 | tf_op jit(solution)/shard_map/ppermute | solution.py:360
  36.9 8.5 %collective-permute-start.19 = (bf16[656,128]{1,0:T(8,128)(2,1)S(1)}, bf16[656,128]{1,0:T(8,128)(2,1)S(1)}, u32[]{:S(2)}, u32[]{:S(2)}) collective-permute-start(bf16[656,128]{1,0:T(8,128)(2,1)S(1)} %project.1.token_ref.rest_0_), channel_id=1, source_target_pairs={{0,4},{1,5},{2,6},{3,7},{4,0},{5,1},{6,2},{7,3},{8,12},{9,13},{10,... | collective-permute-start | bytes 503816 | tf_op jit(solution)/shard_map/ppermute | solution.py:360
  38.1 8.6 %collective-permute-start.20 = (bf16[656,128]{1,0:T(8,128)(2,1)S(1)}, bf16[656,128]{1,0:T(8,128)(2,1)S(1)}, u32[]{:S(2)}, u32[]{:S(2)}) collective-permute-start(bf16[656,128]{1,0:T(8,128)(2,1)S(1)} %project.1.token_ref.rest_0_), channel_id=1, source_target_pairs={{0,1},{1,0},{2,3},{3,2},{4,5},{5,4},{6,7},{7,6},{8,9},{9,8},{10,11... | collective-permute-start | bytes 503816 | tf_op jit(solution)/shard_map/ppermute | solution.py:360
  42.7 4.1 %collective-permute-start.21 = (bf16[656,128]{1,0:T(8,128)(2,1)S(1)}, bf16[656,128]{1,0:T(8,128)(2,1)S(1)}, u32[]{:S(2)}, u32[]{:S(2)}) collective-permute-start(bf16[656,128]{1,0:T(8,128)(2,1)S(1)} %collective-permute-done.17.rest_1_), channel_id=1, source_target_pairs={{0,1},{1,0},{2,3},{3,2},{4,5},{5,4},{6,7},{7,6},{8,9},{9,8},{10,11... | collective-permute-start | bytes 503816 | tf_op jit(solution)/shard_map/ppermute | solution.py:360
  45.0 1.8 %collective-permute-start.22 = (bf16[656,128]{1,0:T(8,128)(2,1)S(1)}, bf16[656,128]{1,0:T(8,128)(2,1)S(1)}, u32[]{:S(2)}, u32[]{:S(2)}) collective-permute-start(bf16[656,128]{1,0:T(8,128)(2,1)S(1)} %collective-permute-done.18.rest_2_), channel_id=1, source_target_pairs={{0,1},{1,0},{2,3},{3,2},{4,5},{5,4},{6,7},{7,6},{8,9},{9,8},{10,11... | collective-permute-start | bytes 503816 | tf_op jit(solution)/shard_map/ppermute | solution.py:360
  45.4 1.4 %collective-permute-start.23 = (bf16[656,128]{1,0:T(8,128)(2,1)S(1)}, bf16[656,128]{1,0:T(8,128)(2,1)S(1)}, u32[]{:S(2)}, u32[]{:S(2)}) collective-permute-start(bf16[656,128]{1,0:T(8,128)(2,1)S(1)} %collective-permute-done.19.rest_3_), channel_id=1, source_target_pairs={{0,1},{1,0},{2,3},{3,2},{4,5},{5,4},{6,7},{7,6},{8,9},{9,8},{10,11... | collective-permute-start | bytes 503816 | tf_op jit(solution)/shard_map/ppermute | solution.py:360
  (2 other events, 27.4 us)

commit v6 on v5

--- a/solution.py
+++ b/solution.py
@@ -123,7 +123,7 @@
 MAIN = ROWS * WIDE
 NOTES = 16
 BLOCK_ORDER = (0, 6, 7, 2, 4, 3, 5, 1)
-PIECE_ORDER = (0, 6, 2, 4, 1, 7, 3, 5)
+SHIFTS = (0, 2, 1, 3)
 ROOT = math.log2(math.e) / math.sqrt(HDIM)
 BF16 = jnp.bfloat16
 F32 = jnp.float32
@@ -228,10 +228,27 @@
     out_ref[patches:, :] = pack_tail(attn[:, WIDE:]).astype(BF16)
 
 
+def weight_rows(cut):
+    depth = 2 * HPAIR
+    packed = cut[depth:]
+    tail = jnp.concatenate([packed[:, at * REST : (at + 1) * REST] for at in range(4)], axis=0)
+    whole = jnp.concatenate([cut[:depth], tail], axis=1)
+    return [whole[core * HPAIR : (core + 1) * HPAIR] for core in range(2)]
+
+
+def place_rows(rows, base, main_ref, tail_ref):
+    for core in range(2):
+        pair = base + core
+        main_ref[pl.ds(pl.multiple_of(pair * WIDE, WIDE), WIDE), :] = rows[core][:WIDE]
+        for corner in range(4):
+            spot = pl.multiple_of(pair * WIDE + corner * REST, REST)
+            tail_ref[corner, pl.ds(spot, REST), :] = rows[core][WIDE:]
+
+
 def ready_kernel(select_ref, gain_ref, token_ref, *rest):
     del token_ref
-    blocks, slices = rest[:ROWS], rest[ROWS : ROWS + PAGES]
-    resid_ref, gain_out, main_ref, tail_ref, held = rest[ROWS + PAGES :]
+    blocks, slices = rest[:ROWS], rest[ROWS : ROWS + PAGES - 1]
+    resid_ref, gain_out, main_ref, tail_ref, held = rest[-5:]
     me = row_index()
     page = lax.axis_index("page")
     band = blocks[0].shape[0]
@@ -245,35 +262,39 @@
         parts.append(gain_ref[:, MAIN + pair * REST : MAIN + (pair + 1) * REST])
         gain = jnp.where(me == pair, jnp.concatenate(parts, axis=1), gain)
     gain_out[...] = gain
+    main_ref[...] = jnp.zeros_like(main_ref)
     tail_ref[...] = jnp.zeros_like(tail_ref)
-    depth = 2 * HPAIR
-    for step in range(PAGES):
+    for step, cut in zip(SHIFTS, slices):
         source = lax.rem(page + PAGES - step, PAGES)
-        packed = slices[step][depth:]
-        tail = jnp.concatenate([packed[:, at * REST : (at + 1) * REST] for at in range(4)], axis=0)
-        whole = jnp.concatenate([slices[step][:depth], tail], axis=1)
-        for core in range(2):
-            pair = 2 * source + core
-            rows = whole[core * HPAIR : (core + 1) * HPAIR]
-            main_ref[pl.ds(pl.multiple_of(pair * WIDE, WIDE), WIDE), :] = rows[:WIDE]
-            for corner in range(4):
-                spot = pl.multiple_of(pair * WIDE + corner * REST, REST)
-                tail_ref[corner, pl.ds(spot, REST), :] = rows[WIDE:]
+        place_rows(weight_rows(cut), 2 * source, main_ref, tail_ref)
+
+
+def last_kernel(cut_ref, token_ref, main_ref, tail_ref):
+    del token_ref
+    tail_ref[...] = jnp.zeros_like(tail_ref)
+    place_rows(weight_rows(cut_ref), 0, main_ref, tail_ref)
 
 
 def collect(pieces, full):
     me = row_index()
-    for step, piece in zip(PIECE_ORDER, pieces):
+    core = me % 2
+    first, second = 2 + 2 * core, 4 - 2 * core
+    near = [0, first, second, 6]
+    far = [1, 1 ^ second, 1 ^ first, 7]
+    for step, piece in zip(near + far, pieces):
         full[:, pl.ds(pl.multiple_of((me ^ step) * WIDE, WIDE), WIDE)] = piece[...]
 
 
 def project_kernel(*rest):
     pieces = rest[:ROWS]
-    main_ref, tail_ref, resid_ref, gain_ref, out_ref, full = rest[ROWS:]
+    main_ref, tail_ref, last_main_ref, last_tail_ref, resid_ref, gain_ref, out_ref, full = rest[ROWS:]
     collect(pieces, full)
     patches = resid_ref.shape[0]
     groups = patches // 4
+    source = lax.rem(lax.axis_index("page") + PAGES - SHIFTS[-1], PAGES)
+    late = pl.ds(pl.multiple_of(source * 2 * WIDE, 2 * WIDE), 2 * WIDE)
     base = jnp.dot(full[:patches], main_ref[...], preferred_element_type=F32) + resid_ref[...]
+    base = base + jnp.dot(full[:patches, late], last_main_ref[...], preferred_element_type=F32)
     ones = jnp.ones((NOTES, HPAIR), BF16)
     contract = (((1,), (1,)), ((), ()))
     row = lax.broadcasted_iota(jnp.int32, (NOTES, groups), 0)
@@ -282,6 +303,7 @@
     for corner in range(4):
         span = slice(corner * groups, (corner + 1) * groups)
         hidden = base[span] + jnp.dot(full[patches:], tail_ref[corner], preferred_element_type=F32)
+        hidden = hidden + jnp.dot(full[patches:, late], last_tail_ref[corner], preferred_element_type=F32)
         square = hidden * hidden
         high = square.astype(BF16)
         low = (square - high.astype(F32)).astype(BF16)
@@ -364,9 +386,18 @@
     return lax.ppermute(value, "page", [(page, (page + step) % PAGES) for page in range(PAGES)])
 
 
-def gather_rows(value):
-    far = [swap(value, step) for step in (6, 2, 4)]
-    return [value] + far + [swap(piece, 1) for piece in [value] + far]
+def gather_rows(value, early=None, late=None):
+    first = [(row, row ^ (2 + 2 * (row % 2))) for row in range(ROWS)]
+    second = [(row, row ^ (4 - 2 * (row % 2))) for row in range(ROWS)]
+    head = lax.ppermute(value, "row", first)
+    side = lax.ppermute(value, "row", second)
+    if early is not None:
+        head = lax.optimization_barrier((head, early))[0]
+    diagonal = lax.ppermute(head, "row", second)
+    if late is not None:
+        head = lax.optimization_barrier((head, late))[0]
+    mine = [value, head, side, diagonal]
+    return mine + [swap(piece, 1) for piece in mine]
 
 
 def local_eight(qkv_rows, residual, out_weight, norm_gain, merge_weight, merge_bias, page_grid):
@@ -395,7 +426,7 @@
         moved=1 << 20,
     )(in_hbm(qkv_rows), in_hbm(residual), in_hbm(out_weight), in_hbm(page_grid))
     blocks = [sends[0]] + [swap(sends[step], step) for step in BLOCK_ORDER[1:]]
-    slices = [own] + [turn(own, step) for step in range(1, PAGES)]
+    slices = [own] + [turn(own, step) for step in SHIFTS[1:]]
     select, dead, live, gain, bias = kernel(
         layout_kernel,
         "layout",
@@ -407,40 +438,47 @@
             shape(units, 1, dtype=F32),
         ],
         [pltpu.VMEM((D,), F32), pltpu.VMEM((units,), F32), pltpu.SemaphoreType.DMA((2,))],
-        fetched=range(1, 3 + 5),
-        count=3 + 5,
+        fetched=range(1, 3 + 3),
+        count=3 + 3,
         moved=1 << 20,
-    )(grid, in_hbm(norm_gain), in_hbm(merge_bias), *blocks[1:6])
-    early = [slices[1], slices[2]]
+    )(grid, in_hbm(norm_gain), in_hbm(merge_bias), *blocks[1:4])
     attn = kernel(
         attend_kernel,
         "attend",
         shape(piece, WIDE),
         [pltpu.VMEM((patches, HPAIR), BF16)] * 3,
-        fetched=range(2 + ROWS, 2 + ROWS + len(early)),
-        count=2 + ROWS + len(early),
+        count=2 + ROWS,
         flops=20 * patches * patches * 4096,
         moved=1 << 20,
-    )(select, dead, *blocks, *early)
+    )(select, dead, *blocks)
     resid, own_gain, main, tail = kernel(
         ready_kernel,
         "ready",
         [shape(patches, HPAIR, dtype=F32), shape(1, HPAIR, dtype=F32), shape(MAIN, HPAIR), shape(4, MAIN, HPAIR)],
         [pltpu.VMEM((patches, HPAIR), BF16)],
         fetched=(2,),
-        count=3 + ROWS + PAGES,
+        count=2 + ROWS + PAGES,
         flops=10 * patches * patches * 4096,
         moved=4 << 20,
-    )(select, gain, attn, *blocks, *slices)
+    )(select, gain, attn, *blocks, *slices[:-1])
+    last = kernel(
+        last_kernel,
+        "ready_last",
+        [shape(2 * WIDE, HPAIR), shape(4, 2 * WIDE, HPAIR)],
+        fetched=(1,),
+        count=2,
+        moved=4 << 20,
+    )(slices[-1], main)
+    pieces = gather_rows(attn, main, last[0])
     hidden = kernel(
         project_kernel,
         "project",
         shape(piece + NOTES, WIDE),
         [pltpu.VMEM((piece, MAIN), BF16)],
-        count=ROWS + 4,
+        count=ROWS + 6,
         flops=4 * patches * MAIN * 256,
         moved=4 << 20,
-    )(*gather_rows(attn), main, tail, resid, own_gain)
+    )(*pieces, main, tail, *last, resid, own_gain)
     ends = kernel(tail_kernel, "merge_tail", shape(units, MAIN), fetched=(1,), count=2, moved=4 << 20)(
         merge_weight, hidden
     )

time: 50.1 us -> 51 us (1.018)
  starting transfers between devices: 21.9 us -> 22.7 us
    ppermute x21 -> x15, waiting for transfers between devices: 16 us -> 4.17 us  [swap(): lax.ppermute(value, 'row', [(row, row ^ step) for row in range(ROWS)])]
    ppermute x0 -> x6, waiting for transfers between devices: none -> 9.5 us  [the longest x2 6.49 us: gather_rows(): head = lax.ppermute(value, 'row', first)]
    ppermute x0 -> x6, starting transfers between devices: none -> 7.35 us  [the longest x2 3.24 us: gather_rows(): head = lax.ppermute(value, 'row', first)]
    ppermute x21 -> x15, starting transfers between devices: 16 us -> 8.9 us  [swap(): lax.ppermute(value, 'row', [(row, row ^ step) for row in range(ROWS)])]
    ppermute x3, waiting for transfers between devices: 1.64 us -> 3.73 us  [turn(): lax.ppermute(value, 'page', [(page, (page + step) % PAGES) for page in ra...]
    ppermute x3, starting transfers between devices: 5.83 us -> 6.47 us  [turn(): lax.ppermute(value, 'page', [(page, (page + step) % PAGES) for page in ra...]
  transfers between devices with their start and end apart: 24 -> 24, of which waited for: 10 -> 11; matrix products, arithmetic and copies ran while one was open for 0% -> 0% of each run, Pallas kernels for 5% -> 8%
where the time goes in v6:
time: 51 us; the launch traced here: 50.8 us
  starting transfers between devices  22.7 us (45%)
  waiting for transfers between devices  17.4 us (34%)
  Pallas kernels  10.5 us (21%)
    ppermute x15, starting transfers between devices, swap(): lax.ppermute(value, 'row', [(row, row ^ step) for row in range(ROWS)])  8.9 us
    ppermute x2, waiting for transfers between devices, gather_rows(): head = lax.ppermute(value, 'row', first)  6.49 us
    ppermute x3, starting transfers between devices, turn(): lax.ppermute(value, 'page', [(page, (page + step) % PAGES) for page in ra...  6.47 us
    ppermute x15, waiting for transfers between devices, swap(): lax.ppermute(value, 'row', [(row, row ^ step) for row in range(ROWS)])  4.17 us
    ppermute x3, waiting for transfers between devices, turn(): lax.ppermute(value, 'page', [(page, (page + step) % PAGES) for page in ra...  3.73 us
    ppermute x2, starting transfers between devices, gather_rows(): head = lax.ppermute(value, 'row', first)  3.24 us
    ppermute x2, waiting for transfers between devices, gather_rows(): diagonal = lax.ppermute(head, 'row', second)  3.01 us
    pallas_call x1, Pallas kernels, local_eight(): kernel(merge_kernel, 'merge', shape(1, units, groups), [pltpu.VMEM((piece...  3 us
  transfers between devices with their start and end apart: 24, of which 11 were waited for; matrix products, arithmetic and copies ran while one was open for 0% of the time, Pallas kernels for 8%

profile of v6, /device:TPU:0, one launch (start us, length us, event | category | flops | bytes accessed | tf_op | source)
XLA Modules:
  0.0 50.8 jit_solution(17104772462541329097)
XLA Ops:
  0.0 1.9 %spread.1 = (bf16[64,640]{1,0:T(8,128)(2,1)S(1)}, bf16[64,640]{1,0:T(8,128)(2,1)S(1)}, bf16[64,640]{1,0:T(8,128)(2,1)S(1)}, bf16[64,640]{1,0:T(8,128)(2,1)S(1)},...) custom-call(bf16[1,64,3840]{2,1,0:T(8,128)(2,1)} %qkv_hbm.1, ...), custom_call_target="tpu_custom_call" | custom-call | bytes 1048576 | tf_op jit(solution)/shard_map/spread/pallas_call | solution.py:411
  1.9 4.0 %collective-permute-start = (bf16[64,640]{1,0:T(8,128)(2,1)S(1)}, bf16[64,640]{1,0:T(8,128)(2,1)S(1)}, u32[]{:S(2)}, u32[]{:S(2)}) collective-permute-start(bf16[64,640]{1,0:T(8,128)(2,1)S(1)} %get-tuple-element.29), channel_id=1, source_target_pairs={{0,6},{1,7},{2,4},{3,5},{4,2},{5,3},{6,0},{7,1},{8,14},{9,15},{10,... | collective-permute-start | bytes 245768 | tf_op jit(solution)/shard_map/ppermute | solution.py:382
  5.9 1.1 %collective-permute-start.2 = (bf16[64,640]{1,0:T(8,128)(2,1)S(1)}, bf16[64,640]{1,0:T(8,128)(2,1)S(1)}, u32[]{:S(2)}, u32[]{:S(2)}) collective-permute-start(bf16[64,640]{1,0:T(8,128)(2,1)S(1)} %get-tuple-element.31), channel_id=1, source_target_pairs={{0,2},{1,3},{2,0},{3,1},{4,6},{5,7},{6,4},{7,5},{8,10},{9,11},{10,... | collective-permute-start | bytes 245768 | tf_op jit(solution)/shard_map/ppermute | solution.py:382
  7.0 1.5 %collective-permute-start.3 = (bf16[64,640]{1,0:T(8,128)(2,1)S(1)}, bf16[64,640]{1,0:T(8,128)(2,1)S(1)}, u32[]{:S(2)}, u32[]{:S(2)}) collective-permute-start(bf16[64,640]{1,0:T(8,128)(2,1)S(1)} %get-tuple-element.35), channel_id=1, source_target_pairs={{0,4},{1,5},{2,6},{3,7},{4,0},{5,1},{6,2},{7,3},{8,12},{9,13},{10,... | collective-permute-start | bytes 245768 | tf_op jit(solution)/shard_map/ppermute | solution.py:382
  9.6 1.9 %collective-permute-done.1.rest_1_.rest_2_ = bf16[64,640]{1,0:T(8,128)(2,1)S(1)} collective-permute-done((bf16[64,640]{1,0:T(8,128)(2,1)S(1)}, bf16[64,640]{1,0:T(8,128)(2,1)S(1)}, u32[]{:S(2)}, u32[]{:S(2)}) %collective-permute-start.1) | collective-permute-done | bytes 81952 | tf_op jit(solution)/shard_map/ppermute | solution.py:382
  11.5 0.9 %collective-permute-done.2.rest_2_.rest_3_ = bf16[64,640]{1,0:T(8,128)(2,1)S(1)} collective-permute-done((bf16[64,640]{1,0:T(8,128)(2,1)S(1)}, bf16[64,640]{1,0:T(8,128)(2,1)S(1)}, u32[]{:S(2)}, u32[]{:S(2)}) %collective-permute-start.2) | collective-permute-done | bytes 81952 | tf_op jit(solution)/shard_map/ppermute | solution.py:382
  12.4 2.6 %collective-permute-start.8 = (bf16[400,128]{1,0:T(8,128)(2,1)S(1)}, bf16[400,128]{1,0:T(8,128)(2,1)S(1)}, u32[]{:S(2)}, u32[]{:S(2)}) collective-permute-start(bf16[400,128]{1,0:T(8,128)(2,1)S(1)} %get-tuple-element.40.rest_8_), channel_id=1, source_target_pairs={{0,16},{8,24},{16,0},{24,8},{1,17},{9,25},{17,1},{25,9},{2,18},{10... | collective-permute-start | bytes 307208 | tf_op jit(solution)/shard_map/ppermute | solution.py:386
  14.9 0.9 %layout.1 = (bf16[512,512]{1,0:T(8,128)(2,1)S(1)}, f32[1,512]{1,0:T(1,128)S(1)}, f32[1,128]{1,0:T(1,128)S(1)}, f32[1,1280]{1,0:T(1,128)S(1)}, f32[640,1]{1,0:T(8,128)S(1)}) custom-call(s32[8,128]{1,0:T(8,128)S(1)} %get-tuple-element.28.grid_ref, f32[1280]{0:T(1024)} %gain_hbm.1, f32[640]{0:T(1024)} %bias_hbm.1, ...), custom_call_target="tpu_custom_call" | custom-call | bytes 1048576 | tf_op jit(solution)/shard_map/layout/pallas_call | solution.py:430
  15.8 1.6 %collective-permute-start.9 = (bf16[400,128]{1,0:T(8,128)(2,1)S(1)}, bf16[400,128]{1,0:T(8,128)(2,1)S(1)}, u32[]{:S(2)}, u32[]{:S(2)}) collective-permute-start(bf16[400,128]{1,0:T(8,128)(2,1)S(1)} %get-tuple-element.40.rest_8_), channel_id=1, source_target_pairs={{0,8},{8,16},{16,24},{24,0},{1,9},{9,17},{17,25},{25,1},{2,10},{10... | collective-permute-start | bytes 307208 | tf_op jit(solution)/shard_map/ppermute | solution.py:386
  17.5 1.4 %attend.1.token_ref.rest_0_ = bf16[640,128]{1,0:T(8,128)(2,1)S(1)} custom-call(bf16[512,512]{1,0:T(8,128)(2,1)S(1)} %get-tuple-element.32.select_ref, f32[1,512]{1,0:T(1,128)S(1)} %get-tuple-element.33.dead_ref, bf16[64,640]{1,0:T(8,128)(2,1)S(1)} %get-tuple-element.34.rest_0_, bf16[64,640]{1,0:T(8,128)(2,1)S(1)} %collective-permute-done.rest_0_.rest_1_, ...), custom_call_target="tpu_custom_call" | custom-call | flops 21474836480 | bytes 1048576 | tf_op jit(solution)/shard_map/attend/pallas_call | solution.py:445
  18.9 2.3 %collective-permute-start.7 = (bf16[640,128]{1,0:T(8,128)(2,1)S(1)}, bf16[640,128]{1,0:T(8,128)(2,1)S(1)}, u32[]{:S(2)}, u32[]{:S(2)}) collective-permute-start(bf16[640,128]{1,0:T(8,128)(2,1)S(1)} %attend.1.token_ref.rest_0_), channel_id=1, source_target_pairs={{0,2},{1,5},{2,0},{3,7},{4,6},{5,1},{6,4},{7,3},{8,10},{9,13},{10,... | collective-permute-start | bytes 491528 | tf_op jit(solution)/shard_map/ppermute | solution.py:392
  21.2 1.3 %collective-permute-done.8.rest_9_ = bf16[400,128]{1,0:T(8,128)(2,1)S(1)} collective-permute-done((bf16[400,128]{1,0:T(8,128)(2,1)S(1)}, bf16[400,128]{1,0:T(8,128)(2,1)S(1)}, u32[]{:S(2)}, u32[]{:S(2)}) %collective-permute-start.8) | collective-permute-done | bytes 102432 | tf_op jit(solution)/shard_map/ppermute | solution.py:386
  23.0 3.0 %collective-permute-done.7.rest_1_ = bf16[640,128]{1,0:T(8,128)(2,1)S(1)} collective-permute-done((bf16[640,128]{1,0:T(8,128)(2,1)S(1)}, bf16[640,128]{1,0:T(8,128)(2,1)S(1)}, u32[]{:S(2)}, u32[]{:S(2)}) %collective-permute-start.7) | collective-permute-done | bytes 163872 | tf_op jit(solution)/shard_map/ppermute | solution.py:392
  26.2 2.2 %collective-permute-start.10 = (bf16[400,128]{1,0:T(8,128)(2,1)S(1)}, bf16[400,128]{1,0:T(8,128)(2,1)S(1)}, u32[]{:S(2)}, u32[]{:S(2)}) collective-permute-start(bf16[400,128]{1,0:T(8,128)(2,1)S(1)} %get-tuple-element.40.rest_8_), channel_id=1, source_target_pairs={{0,24},{8,0},{16,8},{24,16},{1,25},{9,1},{17,9},{25,17},{2,26},{10... | collective-permute-start | bytes 307208 | tf_op jit(solution)/shard_map/ppermute | solution.py:386
  28.5 2.4 %collective-permute-done.10.cut_ref = bf16[400,128]{1,0:T(8,128)(2,1)S(1)} collective-permute-done((bf16[400,128]{1,0:T(8,128)(2,1)S(1)}, bf16[400,128]{1,0:T(8,128)(2,1)S(1)}, u32[]{:S(2)}, u32[]{:S(2)}) %collective-permute-start.10) | collective-permute-done | bytes 102432 | tf_op jit(solution)/shard_map/ppermute | solution.py:386
  31.7 0.8 %collective-permute-done.14.rest_5_ = bf16[640,128]{1,0:T(8,128)(2,1)S(1)} collective-permute-done((bf16[640,128]{1,0:T(8,128)(2,1)S(1)}, bf16[640,128]{1,0:T(8,128)(2,1)S(1)}, u32[]{:S(2)}, u32[]{:S(2)}) %collective-permute-start.14) | collective-permute-done | bytes 163872 | tf_op jit(solution)/shard_map/ppermute | solution.py:382
  33.0 1.6 %project.1.token_ref.rest_0_ = bf16[656,128]{1,0:T(8,128)(2,1)S(1)} custom-call(bf16[640,128]{1,0:T(8,128)(2,1)S(1)} %attend.1.token_ref.rest_0_, bf16[640,128]{1,0:T(8,128)(2,1)S(1)} %collective-permute-done.7.rest_1_, bf16[640,128]{1,0:T(8,128)(2,1)S(1)} %collective-permute-done.11.rest_2_, bf16[640,128]{1,0:T(8,128)(2,1)S(1)} %collective-permute-done.12.rest_3_, ...), custom_call_target="tpu_custom_call" | custom-call | flops 536870912 | bytes 4194304 | tf_op jit(solution)/shard_map/project/pallas_call | solution.py:473
  34.6 1.0 %collective-permute-start.17 = (bf16[656,128]{1,0:T(8,128)(2,1)S(1)}, bf16[656,128]{1,0:T(8,128)(2,1)S(1)}, u32[]{:S(2)}, u32[]{:S(2)}) collective-permute-start(bf16[656,128]{1,0:T(8,128)(2,1)S(1)} %project.1.token_ref.rest_0_), channel_id=1, source_target_pairs={{0,2},{1,5},{2,0},{3,7},{4,6},{5,1},{6,4},{7,3},{8,10},{9,13},{10,... | collective-permute-start | bytes 503816 | tf_op jit(solution)/shard_map/ppermute | solution.py:392
  35.5 2.0 %collective-permute-start.18 = (bf16[656,128]{1,0:T(8,128)(2,1)S(1)}, bf16[656,128]{1,0:T(8,128)(2,1)S(1)}, u32[]{:S(2)}, u32[]{:S(2)}) collective-permute-start(bf16[656,128]{1,0:T(8,128)(2,1)S(1)} %project.1.token_ref.rest_0_), channel_id=1, source_target_pairs={{0,4},{1,3},{2,6},{3,1},{4,0},{5,7},{6,2},{7,5},{8,12},{9,11},{10,... | collective-permute-start | bytes 503816 | tf_op jit(solution)/shard_map/ppermute | solution.py:393
  37.5 3.5 %collective-permute-done.17.rest_1_ = bf16[656,128]{1,0:T(8,128)(2,1)S(1)} collective-permute-done((bf16[656,128]{1,0:T(8,128)(2,1)S(1)}, bf16[656,128]{1,0:T(8,128)(2,1)S(1)}, u32[]{:S(2)}, u32[]{:S(2)}) %collective-permute-start.17) | collective-permute-done | bytes 167968 | tf_op jit(solution)/shard_map/ppermute | solution.py:392
  41.0 1.8 %collective-permute-start.19 = (bf16[656,128]{1,0:T(8,128)(2,1)S(1)}, bf16[656,128]{1,0:T(8,128)(2,1)S(1)}, u32[]{:S(2)}, u32[]{:S(2)}) collective-permute-start(bf16[656,128]{1,0:T(8,128)(2,1)S(1)} %collective-permute-done.17.rest_1_), channel_id=1, source_target_pairs={{0,4},{1,3},{2,6},{3,1},{4,0},{5,7},{6,2},{7,5},{8,12},{9,11},{10,... | collective-permute-start | bytes 503816 | tf_op jit(solution)/shard_map/ppermute | solution.py:396
  43.3 3.0 %collective-permute-done.19.rest_3_ = bf16[656,128]{1,0:T(8,128)(2,1)S(1)} collective-permute-done((bf16[656,128]{1,0:T(8,128)(2,1)S(1)}, bf16[656,128]{1,0:T(8,128)(2,1)S(1)}, u32[]{:S(2)}, u32[]{:S(2)}) %collective-permute-start.19) | collective-permute-done | bytes 167968 | tf_op jit(solution)/shard_map/ppermute | solution.py:396
  46.4 1.2 %merge_tail.1.rest_9_ = bf16[640,1024]{1,0:T(8,128)(2,1)S(1)} custom-call(bf16[640,5120]{1,0:T(8,128)(2,1)S(1)} %bitcast.1, bf16[656,128]{1,0:T(8,128)(2,1)S(1)} %project.1.token_ref.rest_0_), custom_call_target="tpu_custom_call" | custom-call | bytes 4194304 | tf_op jit(solution)/shard_map/merge_tail/pallas_call | solution.py:482
  47.8 3.0 %merge.1 = bf16[1,640,128]{2,1,0:T(8,128)(2,1)} custom-call(bf16[656,128]{1,0:T(8,128)(2,1)S(1)} %project.1.token_ref.rest_0_, bf16[656,128]{1,0:T(8,128)(2,1)S(1)} %collective-permute-done.17.rest_1_, bf16[656,128]{1,0:T(8,128)(2,1)S(1)} %collective-permute-done.18.rest_2_, bf16[656,128]{1,0:T(8,128)(2,1)S(1)} %collective-permute-done.19.rest_3_, ...), custom_call_target="tpu_custom_call" | custom-call | flops 838860800 | bytes 8388608 | tf_op jit(solution)/shard_map/merge/pallas_call | solution.py:485
  (37 shorter events, 3.8 us)
Async XLA Ops:
  1.9 7.2 %collective-permute-start = (bf16[64,640]{1,0:T(8,128)(2,1)S(1)}, bf16[64,640]{1,0:T(8,128)(2,1)S(1)}, u32[]{:S(2)}, u32[]{:S(2)}) collective-permute-start(bf16[64,640]{1,0:T(8,128)(2,1)S(1)} %get-tuple-element.29), channel_id=1, source_target_pairs={{0,6},{1,7},{2,4},{3,5},{4,2},{5,3},{6,0},{7,1},{8,14},{9,15},{10,... | collective-permute-start | bytes 245768 | tf_op jit(solution)/shard_map/ppermute | solution.py:382
  5.9 5.6 %collective-permute-start.1 = (bf16[64,640]{1,0:T(8,128)(2,1)S(1)}, bf16[64,640]{1,0:T(8,128)(2,1)S(1)}, u32[]{:S(2)}, u32[]{:S(2)}) collective-permute-start(bf16[64,640]{1,0:T(8,128)(2,1)S(1)} %get-tuple-element.30), channel_id=1, source_target_pairs={{0,7},{1,6},{2,5},{3,4},{4,3},{5,2},{6,1},{7,0},{8,15},{9,14},{10,... | collective-permute-start | bytes 245768 | tf_op jit(solution)/shard_map/ppermute | solution.py:382
  5.9 6.5 %collective-permute-start.2 = (bf16[64,640]{1,0:T(8,128)(2,1)S(1)}, bf16[64,640]{1,0:T(8,128)(2,1)S(1)}, u32[]{:S(2)}, u32[]{:S(2)}) collective-permute-start(bf16[64,640]{1,0:T(8,128)(2,1)S(1)} %get-tuple-element.31), channel_id=1, source_target_pairs={{0,2},{1,3},{2,0},{3,1},{4,6},{5,7},{6,4},{7,5},{8,10},{9,11},{10,... | collective-permute-start | bytes 245768 | tf_op jit(solution)/shard_map/ppermute | solution.py:382
  7.0 8.9 %collective-permute-start.3 = (bf16[64,640]{1,0:T(8,128)(2,1)S(1)}, bf16[64,640]{1,0:T(8,128)(2,1)S(1)}, u32[]{:S(2)}, u32[]{:S(2)}) collective-permute-start(bf16[64,640]{1,0:T(8,128)(2,1)S(1)} %get-tuple-element.35), channel_id=1, source_target_pairs={{0,4},{1,5},{2,6},{3,7},{4,0},{5,1},{6,2},{7,3},{8,12},{9,13},{10,... | collective-permute-start | bytes 245768 | tf_op jit(solution)/shard_map/ppermute | solution.py:382
  8.5 9.0 %collective-permute-start.4 = (bf16[64,640]{1,0:T(8,128)(2,1)S(1)}, bf16[64,640]{1,0:T(8,128)(2,1)S(1)}, u32[]{:S(2)}, u32[]{:S(2)}) collective-permute-start(bf16[64,640]{1,0:T(8,128)(2,1)S(1)} %get-tuple-element.36), channel_id=1, source_target_pairs={{0,3},{1,2},{2,1},{3,0},{4,7},{5,6},{6,5},{7,4},{8,11},{9,10},{10,... | collective-permute-start | bytes 245768 | tf_op jit(solution)/shard_map/ppermute | solution.py:382
  9.1 8.4 %collective-permute-start.5 = (bf16[64,640]{1,0:T(8,128)(2,1)S(1)}, bf16[64,640]{1,0:T(8,128)(2,1)S(1)}, u32[]{:S(2)}, u32[]{:S(2)}) collective-permute-start(bf16[64,640]{1,0:T(8,128)(2,1)S(1)} %get-tuple-element.37), channel_id=1, source_target_pairs={{0,5},{1,4},{2,7},{3,6},{4,1},{5,0},{6,3},{7,2},{8,13},{9,12},{10,... | collective-permute-start | bytes 245768 | tf_op jit(solution)/shard_map/ppermute | solution.py:382
  11.5 6.0 %collective-permute-start.6 = (bf16[64,640]{1,0:T(8,128)(2,1)S(1)}, bf16[64,640]{1,0:T(8,128)(2,1)S(1)}, u32[]{:S(2)}, u32[]{:S(2)}) collective-permute-start(bf16[64,640]{1,0:T(8,128)(2,1)S(1)} %get-tuple-element.38), channel_id=1, source_target_pairs={{0,1},{1,0},{2,3},{3,2},{4,5},{5,4},{6,7},{7,6},{8,9},{9,8},{10,11... | collective-permute-start | bytes 245768 | tf_op jit(solution)/shard_map/ppermute | solution.py:382
  12.4 10.1 %collective-permute-start.8 = (bf16[400,128]{1,0:T(8,128)(2,1)S(1)}, bf16[400,128]{1,0:T(8,128)(2,1)S(1)}, u32[]{:S(2)}, u32[]{:S(2)}) collective-permute-start(bf16[400,128]{1,0:T(8,128)(2,1)S(1)} %get-tuple-element.40.rest_8_), channel_id=1, source_target_pairs={{0,16},{8,24},{16,0},{24,8},{1,17},{9,25},{17,1},{25,9},{2,18},{10... | collective-permute-start | bytes 307208 | tf_op jit(solution)/shard_map/ppermute | solution.py:386
  15.8 6.6 %collective-permute-start.9 = (bf16[400,128]{1,0:T(8,128)(2,1)S(1)}, bf16[400,128]{1,0:T(8,128)(2,1)S(1)}, u32[]{:S(2)}, u32[]{:S(2)}) collective-permute-start(bf16[400,128]{1,0:T(8,128)(2,1)S(1)} %get-tuple-element.40.rest_8_), channel_id=1, source_target_pairs={{0,8},{8,16},{16,24},{24,0},{1,9},{9,17},{17,25},{25,1},{2,10},{10... | collective-permute-start | bytes 307208 | tf_op jit(solution)/shard_map/ppermute | solution.py:386
  18.9 7.1 %collective-permute-start.7 = (bf16[640,128]{1,0:T(8,128)(2,1)S(1)}, bf16[640,128]{1,0:T(8,128)(2,1)S(1)}, u32[]{:S(2)}, u32[]{:S(2)}) collective-permute-start(bf16[640,128]{1,0:T(8,128)(2,1)S(1)} %attend.1.token_ref.rest_0_), channel_id=1, source_target_pairs={{0,2},{1,5},{2,0},{3,7},{4,6},{5,1},{6,4},{7,3},{8,10},{9,13},{10,... | collective-permute-start | bytes 491528 | tf_op jit(solution)/shard_map/ppermute | solution.py:392
  21.1 9.9 %collective-permute-start.11 = (bf16[640,128]{1,0:T(8,128)(2,1)S(1)}, bf16[640,128]{1,0:T(8,128)(2,1)S(1)}, u32[]{:S(2)}, u32[]{:S(2)}) collective-permute-start(bf16[640,128]{1,0:T(8,128)(2,1)S(1)} %attend.1.token_ref.rest_0_), channel_id=1, source_target_pairs={{0,4},{1,3},{2,6},{3,1},{4,0},{5,7},{6,2},{7,5},{8,12},{9,11},{10,... | collective-permute-start | bytes 491528 | tf_op jit(solution)/shard_map/ppermute | solution.py:393
  26.0 5.6 %collective-permute-start.12 = (bf16[640,128]{1,0:T(8,128)(2,1)S(1)}, bf16[640,128]{1,0:T(8,128)(2,1)S(1)}, u32[]{:S(2)}, u32[]{:S(2)}) collective-permute-start(bf16[640,128]{1,0:T(8,128)(2,1)S(1)} %collective-permute-done.7.rest_1_), channel_id=1, source_target_pairs={{0,4},{1,3},{2,6},{3,1},{4,0},{5,7},{6,2},{7,5},{8,12},{9,11},{10,... | collective-permute-start | bytes 491528 | tf_op jit(solution)/shard_map/ppermute | solution.py:396
  26.2 4.7 %collective-permute-start.10 = (bf16[400,128]{1,0:T(8,128)(2,1)S(1)}, bf16[400,128]{1,0:T(8,128)(2,1)S(1)}, u32[]{:S(2)}, u32[]{:S(2)}) collective-permute-start(bf16[400,128]{1,0:T(8,128)(2,1)S(1)} %get-tuple-element.40.rest_8_), channel_id=1, source_target_pairs={{0,24},{8,0},{16,8},{24,16},{1,25},{9,1},{17,9},{25,17},{2,26},{10... | collective-permute-start | bytes 307208 | tf_op jit(solution)/shard_map/ppermute | solution.py:386
  28.5 3.2 %collective-permute-start.13 = (bf16[640,128]{1,0:T(8,128)(2,1)S(1)}, bf16[640,128]{1,0:T(8,128)(2,1)S(1)}, u32[]{:S(2)}, u32[]{:S(2)}) collective-permute-start(bf16[640,128]{1,0:T(8,128)(2,1)S(1)} %attend.1.token_ref.rest_0_), channel_id=1, source_target_pairs={{0,1},{1,0},{2,3},{3,2},{4,5},{5,4},{6,7},{7,6},{8,9},{9,8},{10,11... | collective-permute-start | bytes 491528 | tf_op jit(solution)/shard_map/ppermute | solution.py:382
  31.0 1.5 %collective-permute-start.14 = (bf16[640,128]{1,0:T(8,128)(2,1)S(1)}, bf16[640,128]{1,0:T(8,128)(2,1)S(1)}, u32[]{:S(2)}, u32[]{:S(2)}) collective-permute-start(bf16[640,128]{1,0:T(8,128)(2,1)S(1)} %collective-permute-done.7.rest_1_), channel_id=1, source_target_pairs={{0,1},{1,0},{2,3},{3,2},{4,5},{5,4},{6,7},{7,6},{8,9},{9,8},{10,11... | collective-permute-start | bytes 491528 | tf_op jit(solution)/shard_map/ppermute | solution.py:382
  31.1 1.6 %collective-permute-start.15 = (bf16[640,128]{1,0:T(8,128)(2,1)S(1)}, bf16[640,128]{1,0:T(8,128)(2,1)S(1)}, u32[]{:S(2)}, u32[]{:S(2)}) collective-permute-start(bf16[640,128]{1,0:T(8,128)(2,1)S(1)} %collective-permute-done.11.rest_2_), channel_id=1, source_target_pairs={{0,1},{1,0},{2,3},{3,2},{4,5},{5,4},{6,7},{7,6},{8,9},{9,8},{10,11... | collective-permute-start | bytes 491528 | tf_op jit(solution)/shard_map/ppermute | solution.py:382
  31.6 1.4 %collective-permute-start.16 = (bf16[640,128]{1,0:T(8,128)(2,1)S(1)}, bf16[640,128]{1,0:T(8,128)(2,1)S(1)}, u32[]{:S(2)}, u32[]{:S(2)}) collective-permute-start(bf16[640,128]{1,0:T(8,128)(2,1)S(1)} %collective-permute-done.12.rest_3_), channel_id=1, source_target_pairs={{0,1},{1,0},{2,3},{3,2},{4,5},{5,4},{6,7},{7,6},{8,9},{9,8},{10,11... | collective-permute-start | bytes 491528 | tf_op jit(solution)/shard_map/ppermute | solution.py:382
  34.6 6.4 %collective-permute-start.17 = (bf16[656,128]{1,0:T(8,128)(2,1)S(1)}, bf16[656,128]{1,0:T(8,128)(2,1)S(1)}, u32[]{:S(2)}, u32[]{:S(2)}) collective-permute-start(bf16[656,128]{1,0:T(8,128)(2,1)S(1)} %project.1.token_ref.rest_0_), channel_id=1, source_target_pairs={{0,2},{1,5},{2,0},{3,7},{4,6},{5,1},{6,4},{7,3},{8,10},{9,13},{10,... | collective-permute-start | bytes 503816 | tf_op jit(solution)/shard_map/ppermute | solution.py:392
  35.5 7.8 %collective-permute-start.18 = (bf16[656,128]{1,0:T(8,128)(2,1)S(1)}, bf16[656,128]{1,0:T(8,128)(2,1)S(1)}, u32[]{:S(2)}, u32[]{:S(2)}) collective-permute-start(bf16[656,128]{1,0:T(8,128)(2,1)S(1)} %project.1.token_ref.rest_0_), channel_id=1, source_target_pairs={{0,4},{1,3},{2,6},{3,1},{4,0},{5,7},{6,2},{7,5},{8,12},{9,11},{10,... | collective-permute-start | bytes 503816 | tf_op jit(solution)/shard_map/ppermute | solution.py:393
  41.0 5.4 %collective-permute-start.19 = (bf16[656,128]{1,0:T(8,128)(2,1)S(1)}, bf16[656,128]{1,0:T(8,128)(2,1)S(1)}, u32[]{:S(2)}, u32[]{:S(2)}) collective-permute-start(bf16[656,128]{1,0:T(8,128)(2,1)S(1)} %collective-permute-done.17.rest_1_), channel_id=1, source_target_pairs={{0,4},{1,3},{2,6},{3,1},{4,0},{5,7},{6,2},{7,5},{8,12},{9,11},{10,... | collective-permute-start | bytes 503816 | tf_op jit(solution)/shard_map/ppermute | solution.py:396
  42.8 4.8 %collective-permute-start.20 = (bf16[656,128]{1,0:T(8,128)(2,1)S(1)}, bf16[656,128]{1,0:T(8,128)(2,1)S(1)}, u32[]{:S(2)}, u32[]{:S(2)}) collective-permute-start(bf16[656,128]{1,0:T(8,128)(2,1)S(1)} %project.1.token_ref.rest_0_), channel_id=1, source_target_pairs={{0,1},{1,0},{2,3},{3,2},{4,5},{5,4},{6,7},{7,6},{8,9},{9,8},{10,11... | collective-permute-start | bytes 503816 | tf_op jit(solution)/shard_map/ppermute | solution.py:382
  42.8 4.8 %collective-permute-start.21 = (bf16[656,128]{1,0:T(8,128)(2,1)S(1)}, bf16[656,128]{1,0:T(8,128)(2,1)S(1)}, u32[]{:S(2)}, u32[]{:S(2)}) collective-permute-start(bf16[656,128]{1,0:T(8,128)(2,1)S(1)} %collective-permute-done.17.rest_1_), channel_id=1, source_target_pairs={{0,1},{1,0},{2,3},{3,2},{4,5},{5,4},{6,7},{7,6},{8,9},{9,8},{10,11... | collective-permute-start | bytes 503816 | tf_op jit(solution)/shard_map/ppermute | solution.py:382
  43.3 4.3 %collective-permute-start.22 = (bf16[656,128]{1,0:T(8,128)(2,1)S(1)}, bf16[656,128]{1,0:T(8,128)(2,1)S(1)}, u32[]{:S(2)}, u32[]{:S(2)}) collective-permute-start(bf16[656,128]{1,0:T(8,128)(2,1)S(1)} %collective-permute-done.18.rest_2_), channel_id=1, source_target_pairs={{0,1},{1,0},{2,3},{3,2},{4,5},{5,4},{6,7},{7,6},{8,9},{9,8},{10,11... | collective-permute-start | bytes 503816 | tf_op jit(solution)/shard_map/ppermute | solution.py:382
  46.4 1.4 %collective-permute-start.23 = (bf16[656,128]{1,0:T(8,128)(2,1)S(1)}, bf16[656,128]{1,0:T(8,128)(2,1)S(1)}, u32[]{:S(2)}, u32[]{:S(2)}) collective-permute-start(bf16[656,128]{1,0:T(8,128)(2,1)S(1)} %collective-permute-done.19.rest_3_), channel_id=1, source_target_pairs={{0,1},{1,0},{2,3},{3,2},{4,5},{5,4},{6,7},{7,6},{8,9},{9,8},{10,11... | collective-permute-start | bytes 503816 | tf_op jit(solution)/shard_map/ppermute | solution.py:382
  (2 other events, 75.2 us)

commit v7 on v6

--- a/solution.py
+++ b/solution.py
@@ -122,7 +122,9 @@
 REST = HPAIR - WIDE
 MAIN = ROWS * WIDE
 NOTES = 16
-BLOCK_ORDER = (0, 6, 7, 2, 4, 3, 5, 1)
+BLOCK_ORDER = (0, 2, 4, 6, 7, 3, 5, 1)
+PIECE_ORDER = (0, 2, 4, 1, 3, 5, 6, 7)
+EARLY = 6
 SHIFTS = (0, 2, 1, 3)
 ROOT = math.log2(math.e) / math.sqrt(HDIM)
 BF16 = jnp.bfloat16
@@ -172,12 +174,8 @@
     grid_out[...] = jnp.where(row == 0, grid[0, 0], grid[0, 1])
 
 
-def layout_kernel(grid_ref, gain_hbm, bias_hbm, *rest):
-    select_ref, keys_ref, live_ref, gain_out, bias_out, gain_ref, bias_ref, sems = rest[-8:]
-    fetch_gain = pltpu.make_async_copy(gain_hbm, gain_ref, sems.at[0])
-    fetch_bias = pltpu.make_async_copy(bias_hbm, bias_ref, sems.at[1])
-    fetch_gain.start()
-    fetch_bias.start()
+def layout_kernel(grid_ref, *rest):
+    select_ref, keys_ref, live_ref = rest[-3:]
     rows_n, cols_n = grid_ref[:1, :1], grid_ref[1:2, :1]
     patches = select_ref.shape[0]
     groups = patches // 4
@@ -194,11 +192,6 @@
     keys_ref[...] = jnp.where(key < rows_n * cols_n, 0.0, -1e30)
     slot = lax.broadcasted_iota(jnp.int32, live_ref.shape, 1)
     live_ref[...] = jnp.where(slot < count, 1.0, 0.0)
-    fetch_gain.wait()
-    fetch_bias.wait()
-    gain_out[...] = gain_ref[...].reshape(gain_out.shape)
-    bias = jnp.broadcast_to(bias_ref[...].reshape(1, bias_out.shape[0]), (8, bias_out.shape[0]))
-    bias_out[...] = bias.T[:, :1]
 
 
 def attend_kernel(select_ref, dead_ref, *rest):
@@ -245,10 +238,12 @@
             tail_ref[corner, pl.ds(spot, REST), :] = rows[core][WIDE:]
 
 
-def ready_kernel(select_ref, gain_ref, token_ref, *rest):
+def ready_kernel(select_ref, gain_hbm, token_ref, *rest):
     del token_ref
     blocks, slices = rest[:ROWS], rest[ROWS : ROWS + PAGES - 1]
-    resid_ref, gain_out, main_ref, tail_ref, held = rest[-5:]
+    resid_ref, gain_out, main_ref, tail_ref, held, line, sem = rest[-7:]
+    fetch = pltpu.make_async_copy(gain_hbm, line, sem)
+    fetch.start()
     me = row_index()
     page = lax.axis_index("page")
     band = blocks[0].shape[0]
@@ -256,17 +251,19 @@
         at = pl.ds(pl.multiple_of((me ^ step) * band, band), band)
         held[at, :] = block[:, 3 * HPAIR :]
     resid_ref[...] = jnp.dot(select_ref[...], held[...], preferred_element_type=F32)
-    gain = jnp.zeros(gain_out.shape, F32)
-    for pair in range(ROWS):
-        parts = [gain_ref[:, pair * WIDE : (pair + 1) * WIDE]]
-        parts.append(gain_ref[:, MAIN + pair * REST : MAIN + (pair + 1) * REST])
-        gain = jnp.where(me == pair, jnp.concatenate(parts, axis=1), gain)
-    gain_out[...] = gain
     main_ref[...] = jnp.zeros_like(main_ref)
     tail_ref[...] = jnp.zeros_like(tail_ref)
     for step, cut in zip(SHIFTS, slices):
         source = lax.rem(page + PAGES - step, PAGES)
         place_rows(weight_rows(cut), 2 * source, main_ref, tail_ref)
+    fetch.wait()
+    whole = line[...].reshape(1, D)
+    gain = jnp.zeros(gain_out.shape, F32)
+    for pair in range(ROWS):
+        parts = [whole[:, pair * WIDE : (pair + 1) * WIDE]]
+        parts.append(whole[:, MAIN + pair * REST : MAIN + (pair + 1) * REST])
+        gain = jnp.where(me == pair, jnp.concatenate(parts, axis=1), gain)
+    gain_out[...] = gain
 
 
 def last_kernel(cut_ref, token_ref, main_ref, tail_ref):
@@ -275,26 +272,54 @@
     place_rows(weight_rows(cut_ref), 0, main_ref, tail_ref)
 
 
-def collect(pieces, full):
+def far_block():
     me = row_index()
-    core = me % 2
-    first, second = 2 + 2 * core, 4 - 2 * core
-    near = [0, first, second, 6]
-    far = [1, 1 ^ second, 1 ^ first, 7]
-    for step, piece in zip(near + far, pieces):
+    return pl.ds(pl.multiple_of((me // 2 ^ 3) * 2 * WIDE, 2 * WIDE), 2 * WIDE)
+
+
+def collect_early(pieces, full):
+    me = row_index()
+    full[:, far_block()] = jnp.zeros((full.shape[0], 2 * WIDE), BF16)
+    for step, piece in zip(PIECE_ORDER[:EARLY], pieces):
         full[:, pl.ds(pl.multiple_of((me ^ step) * WIDE, WIDE), WIDE)] = piece[...]
 
 
-def project_kernel(*rest):
-    pieces = rest[:ROWS]
-    main_ref, tail_ref, last_main_ref, last_tail_ref, resid_ref, gain_ref, out_ref, full = rest[ROWS:]
-    collect(pieces, full)
+def collect_late(same, other):
+    core = row_index() % 2
+    left = jnp.where(core == 0, same[...], other[...])
+    right = jnp.where(core == 0, other[...], same[...])
+    return jnp.concatenate([left, right], axis=1)
+
+
+def late_source():
+    return lax.rem(lax.axis_index("page") + PAGES - SHIFTS[-1], PAGES)
+
+
+def project_early_kernel(*rest):
+    pieces = rest[:EARLY]
+    main_ref, tail_ref, last_main_ref, last_tail_ref, resid_ref, out_ref, full = rest[EARLY:]
+    collect_early(pieces, full)
     patches = resid_ref.shape[0]
     groups = patches // 4
-    source = lax.rem(lax.axis_index("page") + PAGES - SHIFTS[-1], PAGES)
-    late = pl.ds(pl.multiple_of(source * 2 * WIDE, 2 * WIDE), 2 * WIDE)
+    late = pl.ds(pl.multiple_of(late_source() * 2 * WIDE, 2 * WIDE), 2 * WIDE)
     base = jnp.dot(full[:patches], main_ref[...], preferred_element_type=F32) + resid_ref[...]
     base = base + jnp.dot(full[:patches, late], last_main_ref[...], preferred_element_type=F32)
+    for corner in range(4):
+        span = slice(corner * groups, (corner + 1) * groups)
+        part = jnp.dot(full[patches:], tail_ref[corner], preferred_element_type=F32)
+        part = part + jnp.dot(full[patches:, late], last_tail_ref[corner], preferred_element_type=F32)
+        out_ref[span, :] = base[span] + part
+
+
+def project_kernel(*rest):
+    same, other, base_ref, main_ref, tail_ref, last_main_ref, last_tail_ref, gain_ref, out_ref = rest
+    patches = base_ref.shape[0]
+    groups = patches // 4
+    block = far_block()
+    is_last = late_source() == (row_index() // 2 ^ 3)
+    full = collect_late(same, other)
+    main = jnp.where(is_last, last_main_ref[...], main_ref[block, :])
+    base = base_ref[...] + jnp.dot(full[:patches], main, preferred_element_type=F32)
     ones = jnp.ones((NOTES, HPAIR), BF16)
     contract = (((1,), (1,)), ((), ()))
     row = lax.broadcasted_iota(jnp.int32, (NOTES, groups), 0)
@@ -302,8 +327,8 @@
     ends = []
     for corner in range(4):
         span = slice(corner * groups, (corner + 1) * groups)
-        hidden = base[span] + jnp.dot(full[patches:], tail_ref[corner], preferred_element_type=F32)
-        hidden = hidden + jnp.dot(full[patches:, late], last_tail_ref[corner], preferred_element_type=F32)
+        tail = jnp.where(is_last, last_tail_ref[corner], tail_ref[corner, block, :])
+        hidden = base[span] + jnp.dot(full[patches:], tail, preferred_element_type=F32)
         square = hidden * hidden
         high = square.astype(BF16)
         low = (square - high.astype(F32)).astype(BF16)
@@ -318,36 +343,59 @@
     out_ref[patches + groups :, :] = notes.astype(BF16)
 
 
-def tail_kernel(weight_ref, token_ref, out_ref):
+def tail_kernel(weight_ref, bias_hbm, token_ref, out_ref, bias_out, line, sem):
     del token_ref
+    fetch = pltpu.make_async_copy(bias_hbm, line, sem)
+    fetch.start()
     for pair in range(ROWS):
         cut = [corner * D + MAIN + pair * REST for corner in range(4)]
         out_ref[:, pair * WIDE : (pair + 1) * WIDE] = jnp.concatenate(
             [weight_ref[:, at : at + REST] for at in cut], axis=1
         )
+    fetch.wait()
+    units = bias_out.shape[0]
+    bias_out[...] = jnp.broadcast_to(line[...].reshape(1, units), (8, units)).T[:, :1]
+
+
+def merge_early_kernel(*rest):
+    pieces = rest[:EARLY]
+    weight_ref, out_ref, full = rest[EARLY:]
+    collect_early(pieces, full)
+    groups = out_ref.shape[2]
+    for corner in range(4):
+        out_ref[corner] = lax.dot_general(
+            weight_ref[:, corner * D : corner * D + MAIN],
+            full[corner * groups : (corner + 1) * groups],
+            (((1,), (1,)), ((), ())),
+            preferred_element_type=F32,
+        )
 
 
 def merge_kernel(*rest):
     pieces = rest[:ROWS]
-    weight_ref, tail_ref, bias_ref, live_ref, out_ref, full = rest[ROWS:]
-    collect(pieces, full)
+    early_ref, weight_ref, tail_ref, bias_ref, live_ref, out_ref, ends_ref = rest[ROWS:]
+    me = row_index()
     groups = live_ref.shape[1]
     patches = 4 * groups
     notes = jnp.zeros((NOTES, groups), F32)
-    for step in range(ROWS):
-        notes = notes + pieces[step][patches + groups :].astype(F32)
+    for step, piece in zip(PIECE_ORDER, pieces):
+        ends_ref[:, pl.ds(pl.multiple_of((me ^ step) * WIDE, WIDE), WIDE)] = piece[patches : patches + groups]
+        notes = notes + piece[patches + groups :].astype(F32)
     scale = lax.rsqrt((notes[:4] + notes[4:8]) * (1.0 / D) + 1e-06)
     contract = (((1,), (1,)), ((), ()))
-    total = jnp.zeros((weight_ref.shape[0], groups), F32)
+    full = collect_late(pieces[EARLY], pieces[EARLY + 1])
+    total = jnp.zeros(bias_ref.shape[:1] + (groups,), F32)
     for corner in range(4):
-        total = total + scale[corner : corner + 1] * lax.dot_general(
-            weight_ref[:, corner * D : corner * D + MAIN],
+        at = pl.multiple_of(corner * D + (me // 2 ^ 3) * 2 * WIDE, 2 * WIDE)
+        part = lax.dot_general(
+            weight_ref[:, pl.ds(at, 2 * WIDE)],
             full[corner * groups : (corner + 1) * groups],
             contract,
             preferred_element_type=F32,
         )
+        total = total + scale[corner : corner + 1] * (early_ref[corner] + part)
     spread = jnp.concatenate([jnp.broadcast_to(scale[at : at + 1], (REST, groups)) for at in range(4)], axis=0).T
-    ends = full[patches : patches + groups].astype(F32) * jnp.concatenate([spread] * ROWS, axis=1)
+    ends = ends_ref[...].astype(F32) * jnp.concatenate([spread] * ROWS, axis=1)
     total = total + lax.dot_general(tail_ref[...], ends.astype(BF16), contract, preferred_element_type=F32)
     total = total + bias_ref[...]
     merged = 0.5 * total * (1.0 + lax.erf(total * math.sqrt(0.5)))
@@ -386,18 +434,14 @@
     return lax.ppermute(value, "page", [(page, (page + step) % PAGES) for page in range(PAGES)])
 
 
-def gather_rows(value, early=None, late=None):
-    first = [(row, row ^ (2 + 2 * (row % 2))) for row in range(ROWS)]
-    second = [(row, row ^ (4 - 2 * (row % 2))) for row in range(ROWS)]
-    head = lax.ppermute(value, "row", first)
-    side = lax.ppermute(value, "row", second)
-    if early is not None:
-        head = lax.optimization_barrier((head, early))[0]
-    diagonal = lax.ppermute(head, "row", second)
-    if late is not None:
-        head = lax.optimization_barrier((head, late))[0]
-    mine = [value, head, side, diagonal]
-    return mine + [swap(piece, 1) for piece in mine]
+def gather_rows(value, *early):
+    far = [swap(value, step) for step in (2, 4, 6)]
+    passed = [value] + far
+    for at, array in enumerate(early):
+        if array is not None:
+            passed[at] = lax.optimization_barrier((passed[at], array))[0]
+    near = [swap(piece, 1) for piece in passed]
+    return [value, far[0], far[1], near[0], near[1], near[2], far[2], near[3]]
 
 
 def local_eight(qkv_rows, residual, out_weight, norm_gain, merge_weight, merge_bias, page_grid):
@@ -427,21 +471,14 @@
     )(in_hbm(qkv_rows), in_hbm(residual), in_hbm(out_weight), in_hbm(page_grid))
     blocks = [sends[0]] + [swap(sends[step], step) for step in BLOCK_ORDER[1:]]
     slices = [own] + [turn(own, step) for step in SHIFTS[1:]]
-    select, dead, live, gain, bias = kernel(
+    select, dead, live = kernel(
         layout_kernel,
         "layout",
-        [
-            shape(patches, patches),
-            shape(1, patches, dtype=F32),
-            shape(1, groups, dtype=F32),
-            shape(1, D, dtype=F32),
-            shape(units, 1, dtype=F32),
-        ],
-        [pltpu.VMEM((D,), F32), pltpu.VMEM((units,), F32), pltpu.SemaphoreType.DMA((2,))],
-        fetched=range(1, 3 + 3),
-        count=3 + 3,
+        [shape(patches, patches), shape(1, patches, dtype=F32), shape(1, groups, dtype=F32)],
+        fetched=range(1, 1 + 3),
+        count=1 + 3,
         moved=1 << 20,
-    )(grid, in_hbm(norm_gain), in_hbm(merge_bias), *blocks[1:4])
+    )(grid, *blocks[1:4])
     attn = kernel(
         attend_kernel,
         "attend",
@@ -455,12 +492,12 @@
         ready_kernel,
         "ready",
         [shape(patches, HPAIR, dtype=F32), shape(1, HPAIR, dtype=F32), shape(MAIN, HPAIR), shape(4, MAIN, HPAIR)],
-        [pltpu.VMEM((patches, HPAIR), BF16)],
-        fetched=(2,),
+        [pltpu.VMEM((patches, HPAIR), BF16), pltpu.VMEM((D,), F32), pltpu.SemaphoreType.DMA],
+        fetched=(1, 2),
         count=2 + ROWS + PAGES,
         flops=10 * patches * patches * 4096,
         moved=4 << 20,
-    )(select, gain, attn, *blocks, *slices[:-1])
+    )(select, in_hbm(norm_gain), attn, *blocks, *slices[:-1])
     last = kernel(
         last_kernel,
         "ready_last",
@@ -469,28 +506,52 @@
         count=2,
         moved=4 << 20,
     )(slices[-1], main)
-    pieces = gather_rows(attn, main, last[0])
+    pieces = gather_rows(attn, main, None, last[0])
+    base = kernel(
+        project_early_kernel,
+        "project_early",
+        shape(patches, HPAIR, dtype=F32),
+        [pltpu.VMEM((piece, MAIN), BF16)],
+        count=EARLY + 5,
+        flops=4 * patches * MAIN * 4096,
+        moved=4 << 20,
+    )(*pieces[:EARLY], main, tail, *last, resid)
     hidden = kernel(
         project_kernel,
         "project",
         shape(piece + NOTES, WIDE),
-        [pltpu.VMEM((piece, MAIN), BF16)],
-        count=ROWS + 6,
-        flops=4 * patches * MAIN * 256,
+        count=2 + 6,
+        flops=patches * MAIN * 256,
         moved=4 << 20,
-    )(*pieces, main, tail, *last, resid, own_gain)
-    ends = kernel(tail_kernel, "merge_tail", shape(units, MAIN), fetched=(1,), count=2, moved=4 << 20)(
-        merge_weight, hidden
-    )
+    )(*pieces[EARLY:], base, main, tail, *last, own_gain)
+    ends, bias = kernel(
+        tail_kernel,
+        "merge_tail",
+        [shape(units, MAIN), shape(units, 1, dtype=F32)],
+        [pltpu.VMEM((units,), F32), pltpu.SemaphoreType.DMA],
+        fetched=(1, 2),
+        count=3,
+        moved=4 << 20,
+    )(merge_weight, in_hbm(merge_bias), hidden)
+    pieces = gather_rows(hidden)
+    early = kernel(
+        merge_early_kernel,
+        "merge_early",
+        shape(4, units, groups, dtype=F32),
+        [pltpu.VMEM((piece + NOTES, MAIN), BF16)],
+        count=EARLY + 1,
+        flops=8 * units * groups * MAIN * 16,
+        moved=8 << 20,
+    )(*pieces[:EARLY], merge_weight)
     return kernel(
         merge_kernel,
         "merge",
         shape(1, units, groups),
-        [pltpu.VMEM((piece + NOTES, MAIN), BF16)],
-        count=ROWS + 4,
-        flops=10 * units * groups * MAIN,
+        [pltpu.VMEM((groups, MAIN), BF16)],
+        count=ROWS + 5,
+        flops=4 * units * groups * MAIN,
         moved=8 << 20,
-    )(*gather_rows(hidden), merge_weight, ends, bias, live)
+    )(*pieces, early, merge_weight, ends, bias, live)
 
 
 def solution(mesh):

time: 51 us -> 46.9 us (0.920)
  waiting for transfers between devices: 17.4 us -> 12.9 us
  Pallas kernels: 10.5 us -> 11.3 us
  starting transfers between devices: 22.7 us -> 22.1 us
    ppermute x6 -> x0, waiting for transfers between devices: 9.5 us -> none  [the longest x2 6.49 us: gather_rows(): head = lax.ppermute(value, 'row', first)]
    ppermute x15 -> x21, waiting for transfers between devices: 4.17 us -> 12.9 us  [swap(): lax.ppermute(value, 'row', [(row, row ^ step) for row in range(ROWS)])]
    ppermute x6 -> x0, starting transfers between devices: 7.35 us -> none  [the longest x2 3.24 us: gather_rows(): head = lax.ppermute(value, 'row', first)]
    ppermute x15 -> x21, starting transfers between devices: 8.9 us -> 15.6 us  [swap(): lax.ppermute(value, 'row', [(row, row ^ step) for row in range(ROWS)])]
    ppermute x3, waiting for transfers between devices: 3.73 us -> 0.01 us  [turn(): lax.ppermute(value, 'page', [(page, (page + step) % PAGES) for page in ra...]
    pallas_call x3 -> x5, Pallas kernels: 5.79 us -> 6.76 us  [the longest x1 1.9 us: local_eight(): kernel(merge_early_kernel, 'merge_early', shape(4, units, groups, dtype=F...]
    pallas_call x1, Pallas kernels: 0.5 us -> 1.22 us  [local_eight(): kernel(ready_kernel, 'ready', [shape(patches, HPAIR, dtype=F32), shape(1,...]
    pallas_call x1, Pallas kernels: 0.88 us -> 0.17 us  [local_eight(): kernel(layout_kernel, 'layout', [shape(patches, patches), shape(1, patche...]
  transfers between devices with their start and end apart: 24 -> 24, of which waited for: 11 -> 9; matrix products, arithmetic and copies ran while one was open for 0% -> 0% of each run, Pallas kernels for 8% -> 16%
where the time goes in v7:
time: 46.9 us; the launch traced here: 46.5 us
  starting transfers between devices  22.1 us (47%)
  waiting for transfers between devices  12.9 us (28%)
  Pallas kernels  11.3 us (24%)
    ppermute x21, starting transfers between devices, swap(): lax.ppermute(value, 'row', [(row, row ^ step) for row in range(ROWS)])  15.6 us
    ppermute x21, waiting for transfers between devices, swap(): lax.ppermute(value, 'row', [(row, row ^ step) for row in range(ROWS)])  12.9 us
    ppermute x3, starting transfers between devices, turn(): lax.ppermute(value, 'page', [(page, (page + step) % PAGES) for page in ra...  6.53 us
    pallas_call x1, Pallas kernels, local_eight(): kernel(merge_early_kernel, 'merge_early', shape(4, units, groups, dtype=F...  1.9 us
    pallas_call x1, Pallas kernels, local_eight(): kernel(spread_kernel, 'spread', [shape(band, 4 * HPAIR)] * ROWS + [shape(...  1.74 us
    pallas_call x1, Pallas kernels, local_eight(): kernel(merge_kernel, 'merge', shape(1, units, groups), [pltpu.VMEM((group...  1.61 us
    pallas_call x1, Pallas kernels, local_eight(): kernel(tail_kernel, 'merge_tail', [shape(units, MAIN), shape(units, 1, dt...  1.4 us
    pallas_call x1, Pallas kernels, local_eight(): kernel(attend_kernel, 'attend', shape(piece, WIDE), [pltpu.VMEM((patches,...  1.35 us
  transfers between devices with their start and end apart: 24, of which 9 were waited for; matrix products, arithmetic and copies ran while one was open for 0% of the time, Pallas kernels for 16%

profile of v7, /device:TPU:0, one launch (start us, length us, event | category | flops | bytes accessed | tf_op | source)
XLA Modules:
  0.0 46.5 jit_solution(4709909198312068658)
XLA Ops:
  0.0 1.7 %spread.1 = (bf16[64,640]{1,0:T(8,128)(2,1)S(1)}, bf16[64,640]{1,0:T(8,128)(2,1)S(1)}, bf16[64,640]{1,0:T(8,128)(2,1)S(1)}, bf16[64,640]{1,0:T(8,128)(2,1)S(1)},...) custom-call(bf16[1,64,3840]{2,1,0:T(8,128)(2,1)} %qkv_hbm.1, ...), custom_call_target="tpu_custom_call" | custom-call | bytes 1048576 | tf_op jit(solution)/shard_map/spread/pallas_call | solution.py:455
  1.7 3.0 %collective-permute-start = (bf16[64,640]{1,0:T(8,128)(2,1)S(1)}, bf16[64,640]{1,0:T(8,128)(2,1)S(1)}, u32[]{:S(2)}, u32[]{:S(2)}) collective-permute-start(bf16[64,640]{1,0:T(8,128)(2,1)S(1)} %get-tuple-element.29), channel_id=1, source_target_pairs={{0,2},{1,3},{2,0},{3,1},{4,6},{5,7},{6,4},{7,5},{8,10},{9,11},{10,... | collective-permute-start | bytes 245768 | tf_op jit(solution)/shard_map/ppermute | solution.py:430
  4.7 1.5 %collective-permute-start.1 = (bf16[64,640]{1,0:T(8,128)(2,1)S(1)}, bf16[64,640]{1,0:T(8,128)(2,1)S(1)}, u32[]{:S(2)}, u32[]{:S(2)}) collective-permute-start(bf16[64,640]{1,0:T(8,128)(2,1)S(1)} %get-tuple-element.30), channel_id=1, source_target_pairs={{0,4},{1,5},{2,6},{3,7},{4,0},{5,1},{6,2},{7,3},{8,12},{9,13},{10,... | collective-permute-start | bytes 245768 | tf_op jit(solution)/shard_map/ppermute | solution.py:430
  6.3 1.5 %collective-permute-start.3 = (bf16[64,640]{1,0:T(8,128)(2,1)S(1)}, bf16[64,640]{1,0:T(8,128)(2,1)S(1)}, u32[]{:S(2)}, u32[]{:S(2)}) collective-permute-start(bf16[64,640]{1,0:T(8,128)(2,1)S(1)} %get-tuple-element.35), channel_id=1, source_target_pairs={{0,7},{1,6},{2,5},{3,4},{4,3},{5,2},{6,1},{7,0},{8,15},{9,14},{10,... | collective-permute-start | bytes 245768 | tf_op jit(solution)/shard_map/ppermute | solution.py:430
  7.8 1.7 %collective-permute-start.4 = (bf16[64,640]{1,0:T(8,128)(2,1)S(1)}, bf16[64,640]{1,0:T(8,128)(2,1)S(1)}, u32[]{:S(2)}, u32[]{:S(2)}) collective-permute-start(bf16[64,640]{1,0:T(8,128)(2,1)S(1)} %get-tuple-element.36), channel_id=1, source_target_pairs={{0,3},{1,2},{2,1},{3,0},{4,7},{5,6},{6,5},{7,4},{8,11},{9,10},{10,... | collective-permute-start | bytes 245768 | tf_op jit(solution)/shard_map/ppermute | solution.py:430
  10.1 2.3 %collective-permute-done.2.rest_2_.rest_3_ = bf16[64,640]{1,0:T(8,128)(2,1)S(1)} collective-permute-done((bf16[64,640]{1,0:T(8,128)(2,1)S(1)}, bf16[64,640]{1,0:T(8,128)(2,1)S(1)}, u32[]{:S(2)}, u32[]{:S(2)}) %collective-permute-start.2) | collective-permute-done | bytes 81952 | tf_op jit(solution)/shard_map/ppermute | solution.py:430
  12.4 2.7 %collective-permute-start.11 = (bf16[400,128]{1,0:T(8,128)(2,1)S(1)}, bf16[400,128]{1,0:T(8,128)(2,1)S(1)}, u32[]{:S(2)}, u32[]{:S(2)}) collective-permute-start(bf16[400,128]{1,0:T(8,128)(2,1)S(1)} %get-tuple-element.39.rest_8_), channel_id=1, source_target_pairs={{0,16},{8,24},{16,0},{24,8},{1,17},{9,25},{17,1},{25,9},{2,18},{10... | collective-permute-start | bytes 307208 | tf_op jit(solution)/shard_map/ppermute | solution.py:434
  15.3 1.6 %collective-permute-start.12 = (bf16[400,128]{1,0:T(8,128)(2,1)S(1)}, bf16[400,128]{1,0:T(8,128)(2,1)S(1)}, u32[]{:S(2)}, u32[]{:S(2)}) collective-permute-start(bf16[400,128]{1,0:T(8,128)(2,1)S(1)} %get-tuple-element.39.rest_8_), channel_id=1, source_target_pairs={{0,8},{8,16},{16,24},{24,0},{1,9},{9,17},{17,25},{25,1},{2,10},{10... | collective-permute-start | bytes 307208 | tf_op jit(solution)/shard_map/ppermute | solution.py:434
  16.9 2.2 %collective-permute-start.15 = (bf16[400,128]{1,0:T(8,128)(2,1)S(1)}, bf16[400,128]{1,0:T(8,128)(2,1)S(1)}, u32[]{:S(2)}, u32[]{:S(2)}) collective-permute-start(bf16[400,128]{1,0:T(8,128)(2,1)S(1)} %get-tuple-element.39.rest_8_), channel_id=1, source_target_pairs={{0,24},{8,0},{16,8},{24,16},{1,25},{9,1},{17,9},{25,17},{2,26},{10... | collective-permute-start | bytes 307208 | tf_op jit(solution)/shard_map/ppermute | solution.py:434
  19.2 1.4 %attend.1.token_ref.rest_0_ = bf16[640,128]{1,0:T(8,128)(2,1)S(1)} custom-call(bf16[512,512]{1,0:T(8,128)(2,1)S(1)} %get-tuple-element.32.select_ref, f32[1,512]{1,0:T(1,128)S(1)} %get-tuple-element.33.dead_ref, bf16[64,640]{1,0:T(8,128)(2,1)S(1)} %get-tuple-element.34.rest_0_, bf16[64,640]{1,0:T(8,128)(2,1)S(1)} %collective-permute-done.rest_0_.rest_1_, ...), custom_call_target="tpu_custom_call" | custom-call | flops 21474836480 | bytes 1048576 | tf_op jit(solution)/shard_map/attend/pallas_call | solution.py:482
  21.2 2.8 %collective-permute-start.7 = (bf16[640,128]{1,0:T(8,128)(2,1)S(1)}, bf16[640,128]{1,0:T(8,128)(2,1)S(1)}, u32[]{:S(2)}, u32[]{:S(2)}) collective-permute-start(bf16[640,128]{1,0:T(8,128)(2,1)S(1)} %attend.1.token_ref.rest_0_), channel_id=1, source_target_pairs={{0,6},{1,7},{2,4},{3,5},{4,2},{5,3},{6,0},{7,1},{8,14},{9,15},{10,... | collective-permute-start | bytes 491528 | tf_op jit(solution)/shard_map/ppermute | solution.py:430
  24.1 1.2 %ready.1 = (f32[512,160]{1,0:T(8,128)S(1)}, f32[1,160]{1,0:T(1,128)S(1)}, bf16[1024,160]{1,0:T(8,128)(2,1)S(1)}, bf16[4,1024,160]{2,1,0:T(8,128)(2,1)S(1)}) custom-call(bf16[512,512]{1,0:T(8,128)(2,1)S(1)} %get-tuple-element.32.select_ref, f32[1280]{0:T(1024)} %gain_hbm.1, bf16[640,128]{1,0:T(8,128)(2,1)S(1)} %attend.1.token_ref.rest_0_, ...), custom_call_target="tpu_custom_call" | custom-call | flops 10737418240 | bytes 4194304 | tf_op jit(solution)/shard_map/ready/pallas_call | solution.py:491
  25.5 2.2 %collective-permute-done.10.rest_2_ = bf16[640,128]{1,0:T(8,128)(2,1)S(1)} collective-permute-done((bf16[640,128]{1,0:T(8,128)(2,1)S(1)}, bf16[640,128]{1,0:T(8,128)(2,1)S(1)}, u32[]{:S(2)}, u32[]{:S(2)}) %collective-permute-start.10) | collective-permute-done | bytes 163872 | tf_op jit(solution)/shard_map/ppermute | solution.py:430
  28.2 1.7 %collective-permute-done.7.rest_0_ = bf16[640,128]{1,0:T(8,128)(2,1)S(1)} collective-permute-done((bf16[640,128]{1,0:T(8,128)(2,1)S(1)}, bf16[640,128]{1,0:T(8,128)(2,1)S(1)}, u32[]{:S(2)}, u32[]{:S(2)}) %collective-permute-start.7) | collective-permute-done | bytes 163872 | tf_op jit(solution)/shard_map/ppermute | solution.py:430
  29.9 1.2 %project_early.1.rest_2_ = f32[512,160]{1,0:T(8,128)S(1)} custom-call(bf16[640,128]{1,0:T(8,128)(2,1)S(1)} %attend.1.token_ref.rest_0_, bf16[640,128]{1,0:T(8,128)(2,1)S(1)} %collective-permute-done.9.rest_1_, bf16[640,128]{1,0:T(8,128)(2,1)S(1)} %collective-permute-done.10.rest_2_, bf16[640,128]{1,0:T(8,128)(2,1)S(1)} %collective-permute-done.13.rest_3_, ...), custom_call_target="tpu_custom_call" | custom-call | flops 8589934592 | bytes 4194304 | tf_op jit(solution)/shard_map/project_early/pallas_call | solution.py:510
  31.3 0.7 %project.1.rest_0_.token_ref = bf16[656,128]{1,0:T(8,128)(2,1)S(1)} custom-call(bf16[640,128]{1,0:T(8,128)(2,1)S(1)} %collective-permute-done.7.rest_0_, bf16[640,128]{1,0:T(8,128)(2,1)S(1)} %collective-permute-done.8.rest_1_, f32[512,160]{1,0:T(8,128)S(1)} %project_early.1.rest_2_, bf16[1024,160]{1,0:T(8,128)(2,1)S(1)} %get-tuple-element.40.token_ref.rest_6_.rest_3_, ...), custom_call_target="tpu_custom_call" | custom-call | flops 134217728 | bytes 4194304 | tf_op jit(solution)/shard_map/project/pallas_call | solution.py:519
  32.0 0.8 %collective-permute-start.17 = (bf16[656,128]{1,0:T(8,128)(2,1)S(1)}, bf16[656,128]{1,0:T(8,128)(2,1)S(1)}, u32[]{:S(2)}, u32[]{:S(2)}) collective-permute-start(bf16[656,128]{1,0:T(8,128)(2,1)S(1)} %project.1.rest_0_.token_ref), channel_id=1, source_target_pairs={{0,2},{1,3},{2,0},{3,1},{4,6},{5,7},{6,4},{7,5},{8,10},{9,11},{10,... | collective-permute-start | bytes 503816 | tf_op jit(solution)/shard_map/ppermute | solution.py:430
  32.8 1.2 %collective-permute-start.18 = (bf16[656,128]{1,0:T(8,128)(2,1)S(1)}, bf16[656,128]{1,0:T(8,128)(2,1)S(1)}, u32[]{:S(2)}, u32[]{:S(2)}) collective-permute-start(bf16[656,128]{1,0:T(8,128)(2,1)S(1)} %project.1.rest_0_.token_ref), channel_id=1, source_target_pairs={{0,4},{1,5},{2,6},{3,7},{4,0},{5,1},{6,2},{7,3},{8,12},{9,13},{10,... | collective-permute-start | bytes 503816 | tf_op jit(solution)/shard_map/ppermute | solution.py:430
  34.0 1.5 %collective-permute-start.22 = (bf16[656,128]{1,0:T(8,128)(2,1)S(1)}, bf16[656,128]{1,0:T(8,128)(2,1)S(1)}, u32[]{:S(2)}, u32[]{:S(2)}) collective-permute-start(bf16[656,128]{1,0:T(8,128)(2,1)S(1)} %project.1.rest_0_.token_ref), channel_id=1, source_target_pairs={{0,6},{1,7},{2,4},{3,5},{4,2},{5,3},{6,0},{7,1},{8,14},{9,15},{10,... | collective-permute-start | bytes 503816 | tf_op jit(solution)/shard_map/ppermute | solution.py:430
  35.5 3.6 %collective-permute-done.17.rest_1_ = bf16[656,128]{1,0:T(8,128)(2,1)S(1)} collective-permute-done((bf16[656,128]{1,0:T(8,128)(2,1)S(1)}, bf16[656,128]{1,0:T(8,128)(2,1)S(1)}, u32[]{:S(2)}, u32[]{:S(2)}) %collective-permute-start.17) | collective-permute-done | bytes 167968 | tf_op jit(solution)/shard_map/ppermute | solution.py:430
  39.6 1.4 %merge_tail.1 = (bf16[640,1024]{1,0:T(8,128)(2,1)S(1)}, f32[640,1]{1,0:T(8,128)S(1)}) custom-call(bf16[640,5120]{1,0:T(8,128)(2,1)S(1)} %bitcast.1, f32[640]{0:T(1024)} %bias_hbm.1, bf16[656,128]{1,0:T(8,128)(2,1)S(1)} %project.1.rest_0_.token_ref), custom_call_target="tpu_custom_call" | custom-call | bytes 4194304 | tf_op jit(solution)/shard_map/merge_tail/pallas_call | solution.py:527
  41.0 1.9 %collective-permute-done.22.rest_6_ = bf16[656,128]{1,0:T(8,128)(2,1)S(1)} collective-permute-done((bf16[656,128]{1,0:T(8,128)(2,1)S(1)}, bf16[656,128]{1,0:T(8,128)(2,1)S(1)}, u32[]{:S(2)}, u32[]{:S(2)}) %collective-permute-start.22) | collective-permute-done | bytes 167968 | tf_op jit(solution)/shard_map/ppermute | solution.py:430
  43.0 1.9 %merge_early.1.rest_8_ = f32[4,640,128]{2,1,0:T(8,128)S(1)} custom-call(bf16[656,128]{1,0:T(8,128)(2,1)S(1)} %project.1.rest_0_.token_ref, bf16[656,128]{1,0:T(8,128)(2,1)S(1)} %collective-permute-done.17.rest_1_, bf16[656,128]{1,0:T(8,128)(2,1)S(1)} %collective-permute-done.18.rest_2_, bf16[656,128]{1,0:T(8,128)(2,1)S(1)} %collective-permute-done.19.rest_3_, ...), custom_call_target="tpu_custom_call" | custom-call | flops 10737418240 | bytes 8388608 | tf_op jit(solution)/shard_map/merge_early/pallas_call | solution.py:537
  44.9 1.6 %merge.1 = bf16[1,640,128]{2,1,0:T(8,128)(2,1)} custom-call(bf16[656,128]{1,0:T(8,128)(2,1)S(1)} %project.1.rest_0_.token_ref, bf16[656,128]{1,0:T(8,128)(2,1)S(1)} %collective-permute-done.17.rest_1_, bf16[656,128]{1,0:T(8,128)(2,1)S(1)} %collective-permute-done.18.rest_2_, bf16[656,128]{1,0:T(8,128)(2,1)S(1)} %collective-permute-done.19.rest_3_, ...), custom_call_target="tpu_custom_call" | custom-call | flops 335544320 | bytes 8388608 | tf_op jit(solution)/shard_map/merge/pallas_call | solution.py:546
  (39 shorter events, 2.9 us)
Async XLA Ops:
  1.7 7.7 %collective-permute-start = (bf16[64,640]{1,0:T(8,128)(2,1)S(1)}, bf16[64,640]{1,0:T(8,128)(2,1)S(1)}, u32[]{:S(2)}, u32[]{:S(2)}) collective-permute-start(bf16[64,640]{1,0:T(8,128)(2,1)S(1)} %get-tuple-element.29), channel_id=1, source_target_pairs={{0,2},{1,3},{2,0},{3,1},{4,6},{5,7},{6,4},{7,5},{8,10},{9,11},{10,... | collective-permute-start | bytes 245768 | tf_op jit(solution)/shard_map/ppermute | solution.py:430
  4.7 5.3 %collective-permute-start.1 = (bf16[64,640]{1,0:T(8,128)(2,1)S(1)}, bf16[64,640]{1,0:T(8,128)(2,1)S(1)}, u32[]{:S(2)}, u32[]{:S(2)}) collective-permute-start(bf16[64,640]{1,0:T(8,128)(2,1)S(1)} %get-tuple-element.30), channel_id=1, source_target_pairs={{0,4},{1,5},{2,6},{3,7},{4,0},{5,1},{6,2},{7,3},{8,12},{9,13},{10,... | collective-permute-start | bytes 245768 | tf_op jit(solution)/shard_map/ppermute | solution.py:430
  6.3 6.2 %collective-permute-start.2 = (bf16[64,640]{1,0:T(8,128)(2,1)S(1)}, bf16[64,640]{1,0:T(8,128)(2,1)S(1)}, u32[]{:S(2)}, u32[]{:S(2)}) collective-permute-start(bf16[64,640]{1,0:T(8,128)(2,1)S(1)} %get-tuple-element.31), channel_id=1, source_target_pairs={{0,6},{1,7},{2,4},{3,5},{4,2},{5,3},{6,0},{7,1},{8,14},{9,15},{10,... | collective-permute-start | bytes 245768 | tf_op jit(solution)/shard_map/ppermute | solution.py:430
  6.3 9.0 %collective-permute-start.3 = (bf16[64,640]{1,0:T(8,128)(2,1)S(1)}, bf16[64,640]{1,0:T(8,128)(2,1)S(1)}, u32[]{:S(2)}, u32[]{:S(2)}) collective-permute-start(bf16[64,640]{1,0:T(8,128)(2,1)S(1)} %get-tuple-element.35), channel_id=1, source_target_pairs={{0,7},{1,6},{2,5},{3,4},{4,3},{5,2},{6,1},{7,0},{8,15},{9,14},{10,... | collective-permute-start | bytes 245768 | tf_op jit(solution)/shard_map/ppermute | solution.py:430
  7.8 9.1 %collective-permute-start.4 = (bf16[64,640]{1,0:T(8,128)(2,1)S(1)}, bf16[64,640]{1,0:T(8,128)(2,1)S(1)}, u32[]{:S(2)}, u32[]{:S(2)}) collective-permute-start(bf16[64,640]{1,0:T(8,128)(2,1)S(1)} %get-tuple-element.36), channel_id=1, source_target_pairs={{0,3},{1,2},{2,1},{3,0},{4,7},{5,6},{6,5},{7,4},{8,11},{9,10},{10,... | collective-permute-start | bytes 245768 | tf_op jit(solution)/shard_map/ppermute | solution.py:430
  9.5 9.7 %collective-permute-start.5 = (bf16[64,640]{1,0:T(8,128)(2,1)S(1)}, bf16[64,640]{1,0:T(8,128)(2,1)S(1)}, u32[]{:S(2)}, u32[]{:S(2)}) collective-permute-start(bf16[64,640]{1,0:T(8,128)(2,1)S(1)} %get-tuple-element.37), channel_id=1, source_target_pairs={{0,5},{1,4},{2,7},{3,6},{4,1},{5,0},{6,3},{7,2},{8,13},{9,12},{10,... | collective-permute-start | bytes 245768 | tf_op jit(solution)/shard_map/ppermute | solution.py:430
  10.1 9.1 %collective-permute-start.6 = (bf16[64,640]{1,0:T(8,128)(2,1)S(1)}, bf16[64,640]{1,0:T(8,128)(2,1)S(1)}, u32[]{:S(2)}, u32[]{:S(2)}) collective-permute-start(bf16[64,640]{1,0:T(8,128)(2,1)S(1)} %get-tuple-element.38), channel_id=1, source_target_pairs={{0,1},{1,0},{2,3},{3,2},{4,5},{5,4},{6,7},{7,6},{8,9},{9,8},{10,11... | collective-permute-start | bytes 245768 | tf_op jit(solution)/shard_map/ppermute | solution.py:430
  12.4 8.8 %collective-permute-start.11 = (bf16[400,128]{1,0:T(8,128)(2,1)S(1)}, bf16[400,128]{1,0:T(8,128)(2,1)S(1)}, u32[]{:S(2)}, u32[]{:S(2)}) collective-permute-start(bf16[400,128]{1,0:T(8,128)(2,1)S(1)} %get-tuple-element.39.rest_8_), channel_id=1, source_target_pairs={{0,16},{8,24},{16,0},{24,8},{1,17},{9,25},{17,1},{25,9},{2,18},{10... | collective-permute-start | bytes 307208 | tf_op jit(solution)/shard_map/ppermute | solution.py:434
  15.3 8.8 %collective-permute-start.12 = (bf16[400,128]{1,0:T(8,128)(2,1)S(1)}, bf16[400,128]{1,0:T(8,128)(2,1)S(1)}, u32[]{:S(2)}, u32[]{:S(2)}) collective-permute-start(bf16[400,128]{1,0:T(8,128)(2,1)S(1)} %get-tuple-element.39.rest_8_), channel_id=1, source_target_pairs={{0,8},{8,16},{16,24},{24,0},{1,9},{9,17},{17,25},{25,1},{2,10},{10... | collective-permute-start | bytes 307208 | tf_op jit(solution)/shard_map/ppermute | solution.py:434
  16.9 8.5 %collective-permute-start.15 = (bf16[400,128]{1,0:T(8,128)(2,1)S(1)}, bf16[400,128]{1,0:T(8,128)(2,1)S(1)}, u32[]{:S(2)}, u32[]{:S(2)}) collective-permute-start(bf16[400,128]{1,0:T(8,128)(2,1)S(1)} %get-tuple-element.39.rest_8_), channel_id=1, source_target_pairs={{0,24},{8,0},{16,8},{24,16},{1,25},{9,1},{17,9},{25,17},{2,26},{10... | collective-permute-start | bytes 307208 | tf_op jit(solution)/shard_map/ppermute | solution.py:434
  20.5 7.1 %collective-permute-start.10 = (bf16[640,128]{1,0:T(8,128)(2,1)S(1)}, bf16[640,128]{1,0:T(8,128)(2,1)S(1)}, u32[]{:S(2)}, u32[]{:S(2)}) collective-permute-start(bf16[640,128]{1,0:T(8,128)(2,1)S(1)} %attend.1.token_ref.rest_0_), channel_id=1, source_target_pairs={{0,4},{1,5},{2,6},{3,7},{4,0},{5,1},{6,2},{7,3},{8,12},{9,13},{10,... | collective-permute-start | bytes 491528 | tf_op jit(solution)/shard_map/ppermute | solution.py:430
  20.6 7.2 %collective-permute-start.9 = (bf16[640,128]{1,0:T(8,128)(2,1)S(1)}, bf16[640,128]{1,0:T(8,128)(2,1)S(1)}, u32[]{:S(2)}, u32[]{:S(2)}) collective-permute-start(bf16[640,128]{1,0:T(8,128)(2,1)S(1)} %attend.1.token_ref.rest_0_), channel_id=1, source_target_pairs={{0,2},{1,3},{2,0},{3,1},{4,6},{5,7},{6,4},{7,5},{8,10},{9,11},{10,... | collective-permute-start | bytes 491528 | tf_op jit(solution)/shard_map/ppermute | solution.py:430
  21.2 8.6 %collective-permute-start.7 = (bf16[640,128]{1,0:T(8,128)(2,1)S(1)}, bf16[640,128]{1,0:T(8,128)(2,1)S(1)}, u32[]{:S(2)}, u32[]{:S(2)}) collective-permute-start(bf16[640,128]{1,0:T(8,128)(2,1)S(1)} %attend.1.token_ref.rest_0_), channel_id=1, source_target_pairs={{0,6},{1,7},{2,4},{3,5},{4,2},{5,3},{6,0},{7,1},{8,14},{9,15},{10,... | collective-permute-start | bytes 491528 | tf_op jit(solution)/shard_map/ppermute | solution.py:430
  25.3 4.6 %collective-permute-start.13 = (bf16[640,128]{1,0:T(8,128)(2,1)S(1)}, bf16[640,128]{1,0:T(8,128)(2,1)S(1)}, u32[]{:S(2)}, u32[]{:S(2)}) collective-permute-start(bf16[640,128]{1,0:T(8,128)(2,1)S(1)} %attend.1.token_ref.rest_0_), channel_id=1, source_target_pairs={{0,1},{1,0},{2,3},{3,2},{4,5},{5,4},{6,7},{7,6},{8,9},{9,8},{10,11... | collective-permute-start | bytes 491528 | tf_op jit(solution)/shard_map/ppermute | solution.py:430
  27.6 2.2 %collective-permute-start.16 = (bf16[640,128]{1,0:T(8,128)(2,1)S(1)}, bf16[640,128]{1,0:T(8,128)(2,1)S(1)}, u32[]{:S(2)}, u32[]{:S(2)}) collective-permute-start(bf16[640,128]{1,0:T(8,128)(2,1)S(1)} %collective-permute-done.10.rest_2_), channel_id=1, source_target_pairs={{0,1},{1,0},{2,3},{3,2},{4,5},{5,4},{6,7},{7,6},{8,9},{9,8},{10,11... | collective-permute-start | bytes 491528 | tf_op jit(solution)/shard_map/ppermute | solution.py:430
  27.8 2.1 %collective-permute-start.14 = (bf16[640,128]{1,0:T(8,128)(2,1)S(1)}, bf16[640,128]{1,0:T(8,128)(2,1)S(1)}, u32[]{:S(2)}, u32[]{:S(2)}) collective-permute-start(bf16[640,128]{1,0:T(8,128)(2,1)S(1)} %collective-permute-done.9.rest_1_), channel_id=1, source_target_pairs={{0,1},{1,0},{2,3},{3,2},{4,5},{5,4},{6,7},{7,6},{8,9},{9,8},{10,11... | collective-permute-start | bytes 491528 | tf_op jit(solution)/shard_map/ppermute | solution.py:430
  29.9 1.4 %collective-permute-start.8 = (bf16[640,128]{1,0:T(8,128)(2,1)S(1)}, bf16[640,128]{1,0:T(8,128)(2,1)S(1)}, u32[]{:S(2)}, u32[]{:S(2)}) collective-permute-start(bf16[640,128]{1,0:T(8,128)(2,1)S(1)} %collective-permute-done.7.rest_0_), channel_id=1, source_target_pairs={{0,1},{1,0},{2,3},{3,2},{4,5},{5,4},{6,7},{7,6},{8,9},{9,8},{10,11... | collective-permute-start | bytes 491528 | tf_op jit(solution)/shard_map/ppermute | solution.py:430
  32.0 7.1 %collective-permute-start.17 = (bf16[656,128]{1,0:T(8,128)(2,1)S(1)}, bf16[656,128]{1,0:T(8,128)(2,1)S(1)}, u32[]{:S(2)}, u32[]{:S(2)}) collective-permute-start(bf16[656,128]{1,0:T(8,128)(2,1)S(1)} %project.1.rest_0_.token_ref), channel_id=1, source_target_pairs={{0,2},{1,3},{2,0},{3,1},{4,6},{5,7},{6,4},{7,5},{8,10},{9,11},{10,... | collective-permute-start | bytes 503816 | tf_op jit(solution)/shard_map/ppermute | solution.py:430
  32.8 6.5 %collective-permute-start.18 = (bf16[656,128]{1,0:T(8,128)(2,1)S(1)}, bf16[656,128]{1,0:T(8,128)(2,1)S(1)}, u32[]{:S(2)}, u32[]{:S(2)}) collective-permute-start(bf16[656,128]{1,0:T(8,128)(2,1)S(1)} %project.1.rest_0_.token_ref), channel_id=1, source_target_pairs={{0,4},{1,5},{2,6},{3,7},{4,0},{5,1},{6,2},{7,3},{8,12},{9,13},{10,... | collective-permute-start | bytes 503816 | tf_op jit(solution)/shard_map/ppermute | solution.py:430
  34.0 8.9 %collective-permute-start.19 = (bf16[656,128]{1,0:T(8,128)(2,1)S(1)}, bf16[656,128]{1,0:T(8,128)(2,1)S(1)}, u32[]{:S(2)}, u32[]{:S(2)}) collective-permute-start(bf16[656,128]{1,0:T(8,128)(2,1)S(1)} %project.1.rest_0_.token_ref), channel_id=1, source_target_pairs={{0,1},{1,0},{2,3},{3,2},{4,5},{5,4},{6,7},{7,6},{8,9},{9,8},{10,11... | collective-permute-start | bytes 503816 | tf_op jit(solution)/shard_map/ppermute | solution.py:430
  34.0 8.9 %collective-permute-start.22 = (bf16[656,128]{1,0:T(8,128)(2,1)S(1)}, bf16[656,128]{1,0:T(8,128)(2,1)S(1)}, u32[]{:S(2)}, u32[]{:S(2)}) collective-permute-start(bf16[656,128]{1,0:T(8,128)(2,1)S(1)} %project.1.rest_0_.token_ref), channel_id=1, source_target_pairs={{0,6},{1,7},{2,4},{3,5},{4,2},{5,3},{6,0},{7,1},{8,14},{9,15},{10,... | collective-permute-start | bytes 503816 | tf_op jit(solution)/shard_map/ppermute | solution.py:430
  39.1 3.8 %collective-permute-start.20 = (bf16[656,128]{1,0:T(8,128)(2,1)S(1)}, bf16[656,128]{1,0:T(8,128)(2,1)S(1)}, u32[]{:S(2)}, u32[]{:S(2)}) collective-permute-start(bf16[656,128]{1,0:T(8,128)(2,1)S(1)} %collective-permute-done.17.rest_1_), channel_id=1, source_target_pairs={{0,1},{1,0},{2,3},{3,2},{4,5},{5,4},{6,7},{7,6},{8,9},{9,8},{10,11... | collective-permute-start | bytes 503816 | tf_op jit(solution)/shard_map/ppermute | solution.py:430
  39.3 3.6 %collective-permute-start.21 = (bf16[656,128]{1,0:T(8,128)(2,1)S(1)}, bf16[656,128]{1,0:T(8,128)(2,1)S(1)}, u32[]{:S(2)}, u32[]{:S(2)}) collective-permute-start(bf16[656,128]{1,0:T(8,128)(2,1)S(1)} %collective-permute-done.18.rest_2_), channel_id=1, source_target_pairs={{0,1},{1,0},{2,3},{3,2},{4,5},{5,4},{6,7},{7,6},{8,9},{9,8},{10,11... | collective-permute-start | bytes 503816 | tf_op jit(solution)/shard_map/ppermute | solution.py:430
  42.9 1.9 %collective-permute-start.23 = (bf16[656,128]{1,0:T(8,128)(2,1)S(1)}, bf16[656,128]{1,0:T(8,128)(2,1)S(1)}, u32[]{:S(2)}, u32[]{:S(2)}) collective-permute-start(bf16[656,128]{1,0:T(8,128)(2,1)S(1)} %collective-permute-done.22.rest_6_), channel_id=1, source_target_pairs={{0,1},{1,0},{2,3},{3,2},{4,5},{5,4},{6,7},{7,6},{8,9},{9,8},{10,11... | collective-permute-start | bytes 503816 | tf_op jit(solution)/shard_map/ppermute | solution.py:430
  (2 other events, 19.4 us)

commit v8 on v7

--- a/solution.py
+++ b/solution.py
@@ -357,17 +357,34 @@
     bias_out[...] = jnp.broadcast_to(line[...].reshape(1, units), (8, units)).T[:, :1]
 
 
+def piece_steps():
+    core = row_index() % 2
+    first, second = 2 + 2 * core, 4 - 2 * core
+    return [0, first, second, 6, 1, 1 ^ second, 1 ^ first, 7]
+
+
+def merge_product(weight_ref, corner, pieces):
+    me = row_index()
+    groups = pieces[0][1].shape[0] // 4
+    at = [pl.multiple_of(corner * D + (me ^ step) * WIDE, WIDE) for step, _ in pieces]
+    return lax.dot_general(
+        jnp.concatenate([weight_ref[:, pl.ds(spot, WIDE)] for spot in at], axis=1),
+        jnp.concatenate([piece[corner * groups : (corner + 1) * groups] for _, piece in pieces], axis=1),
+        (((1,), (1,)), ((), ())),
+        preferred_element_type=F32,
+    )
+
+
 def merge_early_kernel(*rest):
-    pieces = rest[:EARLY]
-    weight_ref, out_ref, full = rest[EARLY:]
-    collect_early(pieces, full)
-    groups = out_ref.shape[2]
+    pieces, (weight_ref, out_ref) = rest[:4], rest[4:]
+    steps = piece_steps()
+    patches = 4 * out_ref.shape[2]
+    own, one, near_own, near_one = [
+        (steps[at], piece[:patches]) for at, piece in zip((0, 1, 4, 5), pieces)
+    ]
     for corner in range(4):
-        out_ref[corner] = lax.dot_general(
-            weight_ref[:, corner * D : corner * D + MAIN],
-            full[corner * groups : (corner + 1) * groups],
-            (((1,), (1,)), ((), ())),
-            preferred_element_type=F32,
+        out_ref[corner] = merge_product(weight_ref, corner, (own, near_own)) + merge_product(
+            weight_ref, corner, (one, near_one)
         )
 
 
@@ -378,25 +395,23 @@
     groups = live_ref.shape[1]
     patches = 4 * groups
     notes = jnp.zeros((NOTES, groups), F32)
-    for step, piece in zip(PIECE_ORDER, pieces):
+    steps = piece_steps()
+    for step, piece in zip(steps, pieces):
         ends_ref[:, pl.ds(pl.multiple_of((me ^ step) * WIDE, WIDE), WIDE)] = piece[patches : patches + groups]
         notes = notes + piece[patches + groups :].astype(F32)
+    late = [[(steps[at], pieces[at][:patches]) for at in couple] for couple in ((2, 6), (3, 7))]
     scale = lax.rsqrt((notes[:4] + notes[4:8]) * (1.0 / D) + 1e-06)
-    contract = (((1,), (1,)), ((), ()))
-    full = collect_late(pieces[EARLY], pieces[EARLY + 1])
     total = jnp.zeros(bias_ref.shape[:1] + (groups,), F32)
     for corner in range(4):
-        at = pl.multiple_of(corner * D + (me // 2 ^ 3) * 2 * WIDE, 2 * WIDE)
-        part = lax.dot_general(
-            weight_ref[:, pl.ds(at, 2 * WIDE)],
-            full[corner * groups : (corner + 1) * groups],
-            contract,
-            preferred_element_type=F32,
-        )
-        total = total + scale[corner : corner + 1] * (early_ref[corner] + part)
+        part = early_ref[corner]
+        for couple in late:
+            part = part + merge_product(weight_ref, corner, couple)
+        total = total + scale[corner : corner + 1] * part
     spread = jnp.concatenate([jnp.broadcast_to(scale[at : at + 1], (REST, groups)) for at in range(4)], axis=0).T
     ends = ends_ref[...].astype(F32) * jnp.concatenate([spread] * ROWS, axis=1)
-    total = total + lax.dot_general(tail_ref[...], ends.astype(BF16), contract, preferred_element_type=F32)
+    total = total + lax.dot_general(
+        tail_ref[...], ends.astype(BF16), (((1,), (1,)), ((), ())), preferred_element_type=F32
+    )
     total = total + bias_ref[...]
     merged = 0.5 * total * (1.0 + lax.erf(total * math.sqrt(0.5)))
     out_ref[0] = jnp.where(live_ref[...] > 0.0, merged, 0.0).astype(BF16)
@@ -442,6 +457,10 @@
             passed[at] = lax.optimization_barrier((passed[at], array))[0]
     near = [swap(piece, 1) for piece in passed]
     return [value, far[0], far[1], near[0], near[1], near[2], far[2], near[3]]
+
+
+def after(value, array):
+    return lax.optimization_barrier((value, array))[0]
 
 
 def local_eight(qkv_rows, residual, out_weight, norm_gain, merge_weight, merge_bias, page_grid):
@@ -533,16 +552,21 @@
         count=3,
         moved=4 << 20,
     )(merge_weight, in_hbm(merge_bias), hidden)
-    pieces = gather_rows(hidden)
+    first = [(row, row ^ (2 + 2 * (row % 2))) for row in range(ROWS)]
+    second = [(row, row ^ (4 - 2 * (row % 2))) for row in range(ROWS)]
+    one = lax.ppermute(hidden, "row", first)
+    two = lax.ppermute(after(hidden, ends), "row", second)
+    three = lax.ppermute(one, "row", second)
+    near = [swap(hidden, 1), swap(one, 1), swap(two, 1)]
     early = kernel(
         merge_early_kernel,
         "merge_early",
         shape(4, units, groups, dtype=F32),
-        [pltpu.VMEM((piece + NOTES, MAIN), BF16)],
-        count=EARLY + 1,
-        flops=8 * units * groups * MAIN * 16,
+        count=5,
+        flops=4 * units * groups * MAIN * 16,
         moved=8 << 20,
-    )(*pieces[:EARLY], merge_weight)
+    )(hidden, one, near[0], near[1], merge_weight)
+    near.append(swap(after(three, early), 1))
     return kernel(
         merge_kernel,
         "merge",
@@ -551,7 +575,7 @@
         count=ROWS + 5,
         flops=4 * units * groups * MAIN,
         moved=8 << 20,
-    )(*pieces, early, merge_weight, ends, bias, live)
+    )(hidden, one, two, three, *near, early, merge_weight, ends, bias, live)
 
 
 def solution(mesh):

time: 46.9 us -> 46.5 us (level)
    ppermute x0 -> x3, waiting for transfers between devices: none -> 4.46 us  [the longest x1 2.22 us: local_eight(): three = lax.ppermute(one, 'row', second)]
    ppermute x21 -> x18, waiting for transfers between devices: 12.9 us -> 8.55 us  [swap(): lax.ppermute(value, 'row', [(row, row ^ step) for row in range(ROWS)])]
    ppermute x0 -> x3, starting transfers between devices: none -> 4 us  [the longest x1 1.91 us: local_eight(): three = lax.ppermute(one, 'row', second)]
    ppermute x21 -> x18, starting transfers between devices: 15.6 us -> 11.7 us  [swap(): lax.ppermute(value, 'row', [(row, row ^ step) for row in range(ROWS)])]
    pallas_call x1, Pallas kernels: 1.9 us -> 0.86 us  [local_eight(): kernel(merge_early_kernel, 'merge_early', shape(4, units, groups, dtype=F...]
  transfers between devices with their start and end apart: 24 -> 24, of which waited for: 9 -> 10; matrix products, arithmetic and copies ran while one was open for 0% -> 0% of each run, Pallas kernels for 16% -> 14%
where the time goes in v8:
time: 46.5 us; the launch traced here: 46.3 us
  starting transfers between devices  22.3 us (48%)
  waiting for transfers between devices  13 us (28%)
  Pallas kernels  10.9 us (23%)
    ppermute x18, starting transfers between devices, swap(): lax.ppermute(value, 'row', [(row, row ^ step) for row in range(ROWS)])  11.7 us
    ppermute x18, waiting for transfers between devices, swap(): lax.ppermute(value, 'row', [(row, row ^ step) for row in range(ROWS)])  8.55 us
    ppermute x3, starting transfers between devices, turn(): lax.ppermute(value, 'page', [(page, (page + step) % PAGES) for page in ra...  6.53 us
    ppermute x1, waiting for transfers between devices, local_eight(): three = lax.ppermute(one, 'row', second)  2.22 us
    pallas_call x1, Pallas kernels, local_eight(): kernel(merge_kernel, 'merge', shape(1, units, groups), [pltpu.VMEM((group...  2.02 us
    ppermute x1, starting transfers between devices, local_eight(): three = lax.ppermute(one, 'row', second)  1.91 us
    pallas_call x1, Pallas kernels, local_eight(): kernel(spread_kernel, 'spread', [shape(band, 4 * HPAIR)] * ROWS + [shape(...  1.89 us
    ppermute x1, waiting for transfers between devices, local_eight(): one = lax.ppermute(hidden, 'row', first)  1.88 us
  transfers between devices with their start and end apart: 24, of which 10 were waited for; matrix products, arithmetic and copies ran while one was open for 0% of the time, Pallas kernels for 14%

profile of v8, /device:TPU:0, one launch (start us, length us, event | category | flops | bytes accessed | tf_op | source)
XLA Modules:
  0.0 46.3 jit_solution(303808621361303289)
XLA Ops:
  0.0 1.9 %spread.1 = (bf16[64,640]{1,0:T(8,128)(2,1)S(1)}, bf16[64,640]{1,0:T(8,128)(2,1)S(1)}, bf16[64,640]{1,0:T(8,128)(2,1)S(1)}, bf16[64,640]{1,0:T(8,128)(2,1)S(1)},...) custom-call(bf16[1,64,3840]{2,1,0:T(8,128)(2,1)} %qkv_hbm.1, ...), custom_call_target="tpu_custom_call" | custom-call | bytes 1048576 | tf_op jit(solution)/shard_map/spread/pallas_call | solution.py:474
  1.9 3.0 %collective-permute-start = (bf16[64,640]{1,0:T(8,128)(2,1)S(1)}, bf16[64,640]{1,0:T(8,128)(2,1)S(1)}, u32[]{:S(2)}, u32[]{:S(2)}) collective-permute-start(bf16[64,640]{1,0:T(8,128)(2,1)S(1)} %get-tuple-element.31), channel_id=1, source_target_pairs={{0,2},{1,3},{2,0},{3,1},{4,6},{5,7},{6,4},{7,5},{8,10},{9,11},{10,... | collective-permute-start | bytes 245768 | tf_op jit(solution)/shard_map/ppermute | solution.py:445
  4.9 1.5 %collective-permute-start.1 = (bf16[64,640]{1,0:T(8,128)(2,1)S(1)}, bf16[64,640]{1,0:T(8,128)(2,1)S(1)}, u32[]{:S(2)}, u32[]{:S(2)}) collective-permute-start(bf16[64,640]{1,0:T(8,128)(2,1)S(1)} %get-tuple-element.32), channel_id=1, source_target_pairs={{0,4},{1,5},{2,6},{3,7},{4,0},{5,1},{6,2},{7,3},{8,12},{9,13},{10,... | collective-permute-start | bytes 245768 | tf_op jit(solution)/shard_map/ppermute | solution.py:445
  6.4 1.5 %collective-permute-start.3 = (bf16[64,640]{1,0:T(8,128)(2,1)S(1)}, bf16[64,640]{1,0:T(8,128)(2,1)S(1)}, u32[]{:S(2)}, u32[]{:S(2)}) collective-permute-start(bf16[64,640]{1,0:T(8,128)(2,1)S(1)} %get-tuple-element.37), channel_id=1, source_target_pairs={{0,7},{1,6},{2,5},{3,4},{4,3},{5,2},{6,1},{7,0},{8,15},{9,14},{10,... | collective-permute-start | bytes 245768 | tf_op jit(solution)/shard_map/ppermute | solution.py:445
  7.9 1.7 %collective-permute-start.4 = (bf16[64,640]{1,0:T(8,128)(2,1)S(1)}, bf16[64,640]{1,0:T(8,128)(2,1)S(1)}, u32[]{:S(2)}, u32[]{:S(2)}) collective-permute-start(bf16[64,640]{1,0:T(8,128)(2,1)S(1)} %get-tuple-element.38), channel_id=1, source_target_pairs={{0,3},{1,2},{2,1},{3,0},{4,7},{5,6},{6,5},{7,4},{8,11},{9,10},{10,... | collective-permute-start | bytes 245768 | tf_op jit(solution)/shard_map/ppermute | solution.py:445
  10.2 2.3 %collective-permute-done.2.rest_2_.rest_3_ = bf16[64,640]{1,0:T(8,128)(2,1)S(1)} collective-permute-done((bf16[64,640]{1,0:T(8,128)(2,1)S(1)}, bf16[64,640]{1,0:T(8,128)(2,1)S(1)}, u32[]{:S(2)}, u32[]{:S(2)}) %collective-permute-start.2) | collective-permute-done | bytes 81952 | tf_op jit(solution)/shard_map/ppermute | solution.py:445
  12.6 2.7 %collective-permute-start.11 = (bf16[400,128]{1,0:T(8,128)(2,1)S(1)}, bf16[400,128]{1,0:T(8,128)(2,1)S(1)}, u32[]{:S(2)}, u32[]{:S(2)}) collective-permute-start(bf16[400,128]{1,0:T(8,128)(2,1)S(1)} %get-tuple-element.41.rest_8_), channel_id=1, source_target_pairs={{0,16},{8,24},{16,0},{24,8},{1,17},{9,25},{17,1},{25,9},{2,18},{10... | collective-permute-start | bytes 307208 | tf_op jit(solution)/shard_map/ppermute | solution.py:449
  15.4 1.6 %collective-permute-start.12 = (bf16[400,128]{1,0:T(8,128)(2,1)S(1)}, bf16[400,128]{1,0:T(8,128)(2,1)S(1)}, u32[]{:S(2)}, u32[]{:S(2)}) collective-permute-start(bf16[400,128]{1,0:T(8,128)(2,1)S(1)} %get-tuple-element.41.rest_8_), channel_id=1, source_target_pairs={{0,8},{8,16},{16,24},{24,0},{1,9},{9,17},{17,25},{25,1},{2,10},{10... | collective-permute-start | bytes 307208 | tf_op jit(solution)/shard_map/ppermute | solution.py:449
  17.1 2.2 %collective-permute-start.15 = (bf16[400,128]{1,0:T(8,128)(2,1)S(1)}, bf16[400,128]{1,0:T(8,128)(2,1)S(1)}, u32[]{:S(2)}, u32[]{:S(2)}) collective-permute-start(bf16[400,128]{1,0:T(8,128)(2,1)S(1)} %get-tuple-element.41.rest_8_), channel_id=1, source_target_pairs={{0,24},{8,0},{16,8},{24,16},{1,25},{9,1},{17,9},{25,17},{2,26},{10... | collective-permute-start | bytes 307208 | tf_op jit(solution)/shard_map/ppermute | solution.py:449
  19.3 1.4 %attend.1.token_ref.rest_0_ = bf16[640,128]{1,0:T(8,128)(2,1)S(1)} custom-call(bf16[512,512]{1,0:T(8,128)(2,1)S(1)} %get-tuple-element.34.select_ref, f32[1,512]{1,0:T(1,128)S(1)} %get-tuple-element.35.dead_ref, bf16[64,640]{1,0:T(8,128)(2,1)S(1)} %get-tuple-element.36.rest_0_, bf16[64,640]{1,0:T(8,128)(2,1)S(1)} %collective-permute-done.rest_0_.rest_1_, ...), custom_call_target="tpu_custom_call" | custom-call | flops 21474836480 | bytes 1048576 | tf_op jit(solution)/shard_map/attend/pallas_call | solution.py:501
  21.4 2.8 %collective-permute-start.7 = (bf16[640,128]{1,0:T(8,128)(2,1)S(1)}, bf16[640,128]{1,0:T(8,128)(2,1)S(1)}, u32[]{:S(2)}, u32[]{:S(2)}) collective-permute-start(bf16[640,128]{1,0:T(8,128)(2,1)S(1)} %attend.1.token_ref.rest_0_), channel_id=1, source_target_pairs={{0,6},{1,7},{2,4},{3,5},{4,2},{5,3},{6,0},{7,1},{8,14},{9,15},{10,... | collective-permute-start | bytes 491528 | tf_op jit(solution)/shard_map/ppermute | solution.py:445
  24.2 1.2 %ready.1 = (f32[512,160]{1,0:T(8,128)S(1)}, f32[1,160]{1,0:T(1,128)S(1)}, bf16[1024,160]{1,0:T(8,128)(2,1)S(1)}, bf16[4,1024,160]{2,1,0:T(8,128)(2,1)S(1)}) custom-call(bf16[512,512]{1,0:T(8,128)(2,1)S(1)} %get-tuple-element.34.select_ref, f32[1280]{0:T(1024)} %gain_hbm.1, bf16[640,128]{1,0:T(8,128)(2,1)S(1)} %attend.1.token_ref.rest_0_, ...), custom_call_target="tpu_custom_call" | custom-call | flops 10737418240 | bytes 4194304 | tf_op jit(solution)/shard_map/ready/pallas_call | solution.py:510
  25.6 2.2 %collective-permute-done.10.rest_2_ = bf16[640,128]{1,0:T(8,128)(2,1)S(1)} collective-permute-done((bf16[640,128]{1,0:T(8,128)(2,1)S(1)}, bf16[640,128]{1,0:T(8,128)(2,1)S(1)}, u32[]{:S(2)}, u32[]{:S(2)}) %collective-permute-start.10) | collective-permute-done | bytes 163872 | tf_op jit(solution)/shard_map/ppermute | solution.py:445
  28.3 1.7 %collective-permute-done.7.rest_0_ = bf16[640,128]{1,0:T(8,128)(2,1)S(1)} collective-permute-done((bf16[640,128]{1,0:T(8,128)(2,1)S(1)}, bf16[640,128]{1,0:T(8,128)(2,1)S(1)}, u32[]{:S(2)}, u32[]{:S(2)}) %collective-permute-start.7) | collective-permute-done | bytes 163872 | tf_op jit(solution)/shard_map/ppermute | solution.py:445
  30.1 1.2 %project_early.1.rest_2_ = f32[512,160]{1,0:T(8,128)S(1)} custom-call(bf16[640,128]{1,0:T(8,128)(2,1)S(1)} %attend.1.token_ref.rest_0_, bf16[640,128]{1,0:T(8,128)(2,1)S(1)} %collective-permute-done.9.rest_1_, bf16[640,128]{1,0:T(8,128)(2,1)S(1)} %collective-permute-done.10.rest_2_, bf16[640,128]{1,0:T(8,128)(2,1)S(1)} %collective-permute-done.13.rest_3_, ...), custom_call_target="tpu_custom_call" | custom-call | flops 8589934592 | bytes 4194304 | tf_op jit(solution)/shard_map/project_early/pallas_call | solution.py:529
  32.1 0.8 %collective-permute-start.17 = (bf16[656,128]{1,0:T(8,128)(2,1)S(1)}, bf16[656,128]{1,0:T(8,128)(2,1)S(1)}, u32[]{:S(2)}, u32[]{:S(2)}) collective-permute-start(bf16[656,128]{1,0:T(8,128)(2,1)S(1)} %project.1.token_ref.rest_0_), channel_id=1, source_target_pairs={{0,2},{1,5},{2,0},{3,7},{4,6},{5,1},{6,4},{7,3},{8,10},{9,13},{10,... | collective-permute-start | bytes 503816 | tf_op jit(solution)/shard_map/ppermute | solution.py:557
  32.9 1.4 %merge_tail.1 = (bf16[640,1024]{1,0:T(8,128)(2,1)S(1)}, f32[640,1]{1,0:T(8,128)S(1)}) custom-call(bf16[640,5120]{1,0:T(8,128)(2,1)S(1)} %bitcast.1, f32[640]{0:T(1024)} %bias_hbm.1, bf16[656,128]{1,0:T(8,128)(2,1)S(1)} %project.1.token_ref.rest_0_), custom_call_target="tpu_custom_call" | custom-call | bytes 4194304 | tf_op jit(solution)/shard_map/merge_tail/pallas_call | solution.py:546
  34.3 1.3 %collective-permute-start.18 = (bf16[656,128]{1,0:T(8,128)(2,1)S(1)}, bf16[656,128]{1,0:T(8,128)(2,1)S(1)}, u32[]{:S(2)}, u32[]{:S(2)}) collective-permute-start(bf16[656,128]{1,0:T(8,128)(2,1)S(1)} %project.1.token_ref.rest_0_), channel_id=1, source_target_pairs={{0,4},{1,3},{2,6},{3,1},{4,0},{5,7},{6,2},{7,5},{8,12},{9,11},{10,... | collective-permute-start | bytes 503816 | tf_op jit(solution)/shard_map/ppermute | solution.py:558
  35.6 1.9 %collective-permute-done.17.rest_1_ = bf16[656,128]{1,0:T(8,128)(2,1)S(1)} collective-permute-done((bf16[656,128]{1,0:T(8,128)(2,1)S(1)}, bf16[656,128]{1,0:T(8,128)(2,1)S(1)}, u32[]{:S(2)}, u32[]{:S(2)}) %collective-permute-start.17) | collective-permute-done | bytes 167968 | tf_op jit(solution)/shard_map/ppermute | solution.py:557
  37.5 1.9 %collective-permute-start.19 = (bf16[656,128]{1,0:T(8,128)(2,1)S(1)}, bf16[656,128]{1,0:T(8,128)(2,1)S(1)}, u32[]{:S(2)}, u32[]{:S(2)}) collective-permute-start(bf16[656,128]{1,0:T(8,128)(2,1)S(1)} %collective-permute-done.17.rest_1_), channel_id=1, source_target_pairs={{0,4},{1,3},{2,6},{3,1},{4,0},{5,7},{6,2},{7,5},{8,12},{9,11},{10,... | collective-permute-start | bytes 503816 | tf_op jit(solution)/shard_map/ppermute | solution.py:559
  39.8 0.9 %merge_early.1.rest_8_ = f32[4,640,128]{2,1,0:T(8,128)S(1)} custom-call(bf16[656,128]{1,0:T(8,128)(2,1)S(1)} %project.1.token_ref.rest_0_, bf16[656,128]{1,0:T(8,128)(2,1)S(1)} %collective-permute-done.17.rest_1_, bf16[656,128]{1,0:T(8,128)(2,1)S(1)} %collective-permute-done.20.rest_2_.rest_4_, bf16[656,128]{1,0:T(8,128)(2,1)S(1)} %collective-permute-done.21.rest_3_.rest_5_, ...), custom_call_target="tpu_custom_call" | custom-call | flops 5368709120 | bytes 8388608 | tf_op jit(solution)/shard_map/merge_early/pallas_call | solution.py:561
  40.6 2.2 %collective-permute-done.19.rest_3_ = bf16[656,128]{1,0:T(8,128)(2,1)S(1)} collective-permute-done((bf16[656,128]{1,0:T(8,128)(2,1)S(1)}, bf16[656,128]{1,0:T(8,128)(2,1)S(1)}, u32[]{:S(2)}, u32[]{:S(2)}) %collective-permute-start.19) | collective-permute-done | bytes 167968 | tf_op jit(solution)/shard_map/ppermute | solution.py:559
  42.9 1.4 %collective-permute-done.23.rest_7_ = bf16[656,128]{1,0:T(8,128)(2,1)S(1)} collective-permute-done((bf16[656,128]{1,0:T(8,128)(2,1)S(1)}, bf16[656,128]{1,0:T(8,128)(2,1)S(1)}, u32[]{:S(2)}, u32[]{:S(2)}) %collective-permute-start.23) | collective-permute-done | bytes 167968 | tf_op jit(solution)/shard_map/ppermute | solution.py:445
  44.3 2.0 %merge.1 = bf16[1,640,128]{2,1,0:T(8,128)(2,1)} custom-call(bf16[656,128]{1,0:T(8,128)(2,1)S(1)} %project.1.token_ref.rest_0_, bf16[656,128]{1,0:T(8,128)(2,1)S(1)} %collective-permute-done.17.rest_1_, bf16[656,128]{1,0:T(8,128)(2,1)S(1)} %collective-permute-done.18.rest_2_, bf16[656,128]{1,0:T(8,128)(2,1)S(1)} %collective-permute-done.19.rest_3_, ...), custom_call_target="tpu_custom_call" | custom-call | flops 335544320 | bytes 8388608 | tf_op jit(solution)/shard_map/merge/pallas_call | solution.py:570
  (39 shorter events, 3.5 us)
Async XLA Ops:
  1.9 7.7 %collective-permute-start = (bf16[64,640]{1,0:T(8,128)(2,1)S(1)}, bf16[64,640]{1,0:T(8,128)(2,1)S(1)}, u32[]{:S(2)}, u32[]{:S(2)}) collective-permute-start(bf16[64,640]{1,0:T(8,128)(2,1)S(1)} %get-tuple-element.31), channel_id=1, source_target_pairs={{0,2},{1,3},{2,0},{3,1},{4,6},{5,7},{6,4},{7,5},{8,10},{9,11},{10,... | collective-permute-start | bytes 245768 | tf_op jit(solution)/shard_map/ppermute | solution.py:445
  4.9 5.3 %collective-permute-start.1 = (bf16[64,640]{1,0:T(8,128)(2,1)S(1)}, bf16[64,640]{1,0:T(8,128)(2,1)S(1)}, u32[]{:S(2)}, u32[]{:S(2)}) collective-permute-start(bf16[64,640]{1,0:T(8,128)(2,1)S(1)} %get-tuple-element.32), channel_id=1, source_target_pairs={{0,4},{1,5},{2,6},{3,7},{4,0},{5,1},{6,2},{7,3},{8,12},{9,13},{10,... | collective-permute-start | bytes 245768 | tf_op jit(solution)/shard_map/ppermute | solution.py:445
  6.4 6.2 %collective-permute-start.2 = (bf16[64,640]{1,0:T(8,128)(2,1)S(1)}, bf16[64,640]{1,0:T(8,128)(2,1)S(1)}, u32[]{:S(2)}, u32[]{:S(2)}) collective-permute-start(bf16[64,640]{1,0:T(8,128)(2,1)S(1)} %get-tuple-element.33), channel_id=1, source_target_pairs={{0,6},{1,7},{2,4},{3,5},{4,2},{5,3},{6,0},{7,1},{8,14},{9,15},{10,... | collective-permute-start | bytes 245768 | tf_op jit(solution)/shard_map/ppermute | solution.py:445
  6.4 9.0 %collective-permute-start.3 = (bf16[64,640]{1,0:T(8,128)(2,1)S(1)}, bf16[64,640]{1,0:T(8,128)(2,1)S(1)}, u32[]{:S(2)}, u32[]{:S(2)}) collective-permute-start(bf16[64,640]{1,0:T(8,128)(2,1)S(1)} %get-tuple-element.37), channel_id=1, source_target_pairs={{0,7},{1,6},{2,5},{3,4},{4,3},{5,2},{6,1},{7,0},{8,15},{9,14},{10,... | collective-permute-start | bytes 245768 | tf_op jit(solution)/shard_map/ppermute | solution.py:445
  7.9 9.1 %collective-permute-start.4 = (bf16[64,640]{1,0:T(8,128)(2,1)S(1)}, bf16[64,640]{1,0:T(8,128)(2,1)S(1)}, u32[]{:S(2)}, u32[]{:S(2)}) collective-permute-start(bf16[64,640]{1,0:T(8,128)(2,1)S(1)} %get-tuple-element.38), channel_id=1, source_target_pairs={{0,3},{1,2},{2,1},{3,0},{4,7},{5,6},{6,5},{7,4},{8,11},{9,10},{10,... | collective-permute-start | bytes 245768 | tf_op jit(solution)/shard_map/ppermute | solution.py:445
  9.6 9.7 %collective-permute-start.5 = (bf16[64,640]{1,0:T(8,128)(2,1)S(1)}, bf16[64,640]{1,0:T(8,128)(2,1)S(1)}, u32[]{:S(2)}, u32[]{:S(2)}) collective-permute-start(bf16[64,640]{1,0:T(8,128)(2,1)S(1)} %get-tuple-element.39), channel_id=1, source_target_pairs={{0,5},{1,4},{2,7},{3,6},{4,1},{5,0},{6,3},{7,2},{8,13},{9,12},{10,... | collective-permute-start | bytes 245768 | tf_op jit(solution)/shard_map/ppermute | solution.py:445
  10.2 9.1 %collective-permute-start.6 = (bf16[64,640]{1,0:T(8,128)(2,1)S(1)}, bf16[64,640]{1,0:T(8,128)(2,1)S(1)}, u32[]{:S(2)}, u32[]{:S(2)}) collective-permute-start(bf16[64,640]{1,0:T(8,128)(2,1)S(1)} %get-tuple-element.40), channel_id=1, source_target_pairs={{0,1},{1,0},{2,3},{3,2},{4,5},{5,4},{6,7},{7,6},{8,9},{9,8},{10,11... | collective-permute-start | bytes 245768 | tf_op jit(solution)/shard_map/ppermute | solution.py:445
  12.6 8.8 %collective-permute-start.11 = (bf16[400,128]{1,0:T(8,128)(2,1)S(1)}, bf16[400,128]{1,0:T(8,128)(2,1)S(1)}, u32[]{:S(2)}, u32[]{:S(2)}) collective-permute-start(bf16[400,128]{1,0:T(8,128)(2,1)S(1)} %get-tuple-element.41.rest_8_), channel_id=1, source_target_pairs={{0,16},{8,24},{16,0},{24,8},{1,17},{9,25},{17,1},{25,9},{2,18},{10... | collective-permute-start | bytes 307208 | tf_op jit(solution)/shard_map/ppermute | solution.py:449
  15.4 8.8 %collective-permute-start.12 = (bf16[400,128]{1,0:T(8,128)(2,1)S(1)}, bf16[400,128]{1,0:T(8,128)(2,1)S(1)}, u32[]{:S(2)}, u32[]{:S(2)}) collective-permute-start(bf16[400,128]{1,0:T(8,128)(2,1)S(1)} %get-tuple-element.41.rest_8_), channel_id=1, source_target_pairs={{0,8},{8,16},{16,24},{24,0},{1,9},{9,17},{17,25},{25,1},{2,10},{10... | collective-permute-start | bytes 307208 | tf_op jit(solution)/shard_map/ppermute | solution.py:449
  17.1 8.5 %collective-permute-start.15 = (bf16[400,128]{1,0:T(8,128)(2,1)S(1)}, bf16[400,128]{1,0:T(8,128)(2,1)S(1)}, u32[]{:S(2)}, u32[]{:S(2)}) collective-permute-start(bf16[400,128]{1,0:T(8,128)(2,1)S(1)} %get-tuple-element.41.rest_8_), channel_id=1, source_target_pairs={{0,24},{8,0},{16,8},{24,16},{1,25},{9,1},{17,9},{25,17},{2,26},{10... | collective-permute-start | bytes 307208 | tf_op jit(solution)/shard_map/ppermute | solution.py:449
  20.7 7.1 %collective-permute-start.10 = (bf16[640,128]{1,0:T(8,128)(2,1)S(1)}, bf16[640,128]{1,0:T(8,128)(2,1)S(1)}, u32[]{:S(2)}, u32[]{:S(2)}) collective-permute-start(bf16[640,128]{1,0:T(8,128)(2,1)S(1)} %attend.1.token_ref.rest_0_), channel_id=1, source_target_pairs={{0,4},{1,5},{2,6},{3,7},{4,0},{5,1},{6,2},{7,3},{8,12},{9,13},{10,... | collective-permute-start | bytes 491528 | tf_op jit(solution)/shard_map/ppermute | solution.py:445
  20.7 7.2 %collective-permute-start.9 = (bf16[640,128]{1,0:T(8,128)(2,1)S(1)}, bf16[640,128]{1,0:T(8,128)(2,1)S(1)}, u32[]{:S(2)}, u32[]{:S(2)}) collective-permute-start(bf16[640,128]{1,0:T(8,128)(2,1)S(1)} %attend.1.token_ref.rest_0_), channel_id=1, source_target_pairs={{0,2},{1,3},{2,0},{3,1},{4,6},{5,7},{6,4},{7,5},{8,10},{9,11},{10,... | collective-permute-start | bytes 491528 | tf_op jit(solution)/shard_map/ppermute | solution.py:445
  21.4 8.6 %collective-permute-start.7 = (bf16[640,128]{1,0:T(8,128)(2,1)S(1)}, bf16[640,128]{1,0:T(8,128)(2,1)S(1)}, u32[]{:S(2)}, u32[]{:S(2)}) collective-permute-start(bf16[640,128]{1,0:T(8,128)(2,1)S(1)} %attend.1.token_ref.rest_0_), channel_id=1, source_target_pairs={{0,6},{1,7},{2,4},{3,5},{4,2},{5,3},{6,0},{7,1},{8,14},{9,15},{10,... | collective-permute-start | bytes 491528 | tf_op jit(solution)/shard_map/ppermute | solution.py:445
  25.5 4.6 %collective-permute-start.13 = (bf16[640,128]{1,0:T(8,128)(2,1)S(1)}, bf16[640,128]{1,0:T(8,128)(2,1)S(1)}, u32[]{:S(2)}, u32[]{:S(2)}) collective-permute-start(bf16[640,128]{1,0:T(8,128)(2,1)S(1)} %attend.1.token_ref.rest_0_), channel_id=1, source_target_pairs={{0,1},{1,0},{2,3},{3,2},{4,5},{5,4},{6,7},{7,6},{8,9},{9,8},{10,11... | collective-permute-start | bytes 491528 | tf_op jit(solution)/shard_map/ppermute | solution.py:445
  27.8 2.2 %collective-permute-start.16 = (bf16[640,128]{1,0:T(8,128)(2,1)S(1)}, bf16[640,128]{1,0:T(8,128)(2,1)S(1)}, u32[]{:S(2)}, u32[]{:S(2)}) collective-permute-start(bf16[640,128]{1,0:T(8,128)(2,1)S(1)} %collective-permute-done.10.rest_2_), channel_id=1, source_target_pairs={{0,1},{1,0},{2,3},{3,2},{4,5},{5,4},{6,7},{7,6},{8,9},{9,8},{10,11... | collective-permute-start | bytes 491528 | tf_op jit(solution)/shard_map/ppermute | solution.py:445
  27.9 2.1 %collective-permute-start.14 = (bf16[640,128]{1,0:T(8,128)(2,1)S(1)}, bf16[640,128]{1,0:T(8,128)(2,1)S(1)}, u32[]{:S(2)}, u32[]{:S(2)}) collective-permute-start(bf16[640,128]{1,0:T(8,128)(2,1)S(1)} %collective-permute-done.9.rest_1_), channel_id=1, source_target_pairs={{0,1},{1,0},{2,3},{3,2},{4,5},{5,4},{6,7},{7,6},{8,9},{9,8},{10,11... | collective-permute-start | bytes 491528 | tf_op jit(solution)/shard_map/ppermute | solution.py:445
  30.0 1.4 %collective-permute-start.8 = (bf16[640,128]{1,0:T(8,128)(2,1)S(1)}, bf16[640,128]{1,0:T(8,128)(2,1)S(1)}, u32[]{:S(2)}, u32[]{:S(2)}) collective-permute-start(bf16[640,128]{1,0:T(8,128)(2,1)S(1)} %collective-permute-done.7.rest_0_), channel_id=1, source_target_pairs={{0,1},{1,0},{2,3},{3,2},{4,5},{5,4},{6,7},{7,6},{8,9},{9,8},{10,11... | collective-permute-start | bytes 491528 | tf_op jit(solution)/shard_map/ppermute | solution.py:445
  32.1 5.4 %collective-permute-start.17 = (bf16[656,128]{1,0:T(8,128)(2,1)S(1)}, bf16[656,128]{1,0:T(8,128)(2,1)S(1)}, u32[]{:S(2)}, u32[]{:S(2)}) collective-permute-start(bf16[656,128]{1,0:T(8,128)(2,1)S(1)} %project.1.token_ref.rest_0_), channel_id=1, source_target_pairs={{0,2},{1,5},{2,0},{3,7},{4,6},{5,1},{6,4},{7,3},{8,10},{9,13},{10,... | collective-permute-start | bytes 503816 | tf_op jit(solution)/shard_map/ppermute | solution.py:557
  34.3 5.4 %collective-permute-start.18 = (bf16[656,128]{1,0:T(8,128)(2,1)S(1)}, bf16[656,128]{1,0:T(8,128)(2,1)S(1)}, u32[]{:S(2)}, u32[]{:S(2)}) collective-permute-start(bf16[656,128]{1,0:T(8,128)(2,1)S(1)} %project.1.token_ref.rest_0_), channel_id=1, source_target_pairs={{0,4},{1,3},{2,6},{3,1},{4,0},{5,7},{6,2},{7,5},{8,12},{9,11},{10,... | collective-permute-start | bytes 503816 | tf_op jit(solution)/shard_map/ppermute | solution.py:558
  35.6 4.2 %collective-permute-start.20 = (bf16[656,128]{1,0:T(8,128)(2,1)S(1)}, bf16[656,128]{1,0:T(8,128)(2,1)S(1)}, u32[]{:S(2)}, u32[]{:S(2)}) collective-permute-start(bf16[656,128]{1,0:T(8,128)(2,1)S(1)} %project.1.token_ref.rest_0_), channel_id=1, source_target_pairs={{0,1},{1,0},{2,3},{3,2},{4,5},{5,4},{6,7},{7,6},{8,9},{9,8},{10,11... | collective-permute-start | bytes 503816 | tf_op jit(solution)/shard_map/ppermute | solution.py:445
  37.5 2.3 %collective-permute-start.21 = (bf16[656,128]{1,0:T(8,128)(2,1)S(1)}, bf16[656,128]{1,0:T(8,128)(2,1)S(1)}, u32[]{:S(2)}, u32[]{:S(2)}) collective-permute-start(bf16[656,128]{1,0:T(8,128)(2,1)S(1)} %collective-permute-done.17.rest_1_), channel_id=1, source_target_pairs={{0,1},{1,0},{2,3},{3,2},{4,5},{5,4},{6,7},{7,6},{8,9},{9,8},{10,11... | collective-permute-start | bytes 503816 | tf_op jit(solution)/shard_map/ppermute | solution.py:445
  37.5 5.4 %collective-permute-start.19 = (bf16[656,128]{1,0:T(8,128)(2,1)S(1)}, bf16[656,128]{1,0:T(8,128)(2,1)S(1)}, u32[]{:S(2)}, u32[]{:S(2)}) collective-permute-start(bf16[656,128]{1,0:T(8,128)(2,1)S(1)} %collective-permute-done.17.rest_1_), channel_id=1, source_target_pairs={{0,4},{1,3},{2,6},{3,1},{4,0},{5,7},{6,2},{7,5},{8,12},{9,11},{10,... | collective-permute-start | bytes 503816 | tf_op jit(solution)/shard_map/ppermute | solution.py:559
  39.8 3.1 %collective-permute-start.22 = (bf16[656,128]{1,0:T(8,128)(2,1)S(1)}, bf16[656,128]{1,0:T(8,128)(2,1)S(1)}, u32[]{:S(2)}, u32[]{:S(2)}) collective-permute-start(bf16[656,128]{1,0:T(8,128)(2,1)S(1)} %collective-permute-done.18.rest_2_), channel_id=1, source_target_pairs={{0,1},{1,0},{2,3},{3,2},{4,5},{5,4},{6,7},{7,6},{8,9},{9,8},{10,11... | collective-permute-start | bytes 503816 | tf_op jit(solution)/shard_map/ppermute | solution.py:445
  42.9 1.4 %collective-permute-start.23 = (bf16[656,128]{1,0:T(8,128)(2,1)S(1)}, bf16[656,128]{1,0:T(8,128)(2,1)S(1)}, u32[]{:S(2)}, u32[]{:S(2)}) collective-permute-start(bf16[656,128]{1,0:T(8,128)(2,1)S(1)} %collective-permute-done.19.rest_3_), channel_id=1, source_target_pairs={{0,1},{1,0},{2,3},{3,2},{4,5},{5,4},{6,7},{7,6},{8,9},{9,8},{10,11... | collective-permute-start | bytes 503816 | tf_op jit(solution)/shard_map/ppermute | solution.py:445
  (2 other events, 46.6 us)

commit v9 on v8

--- a/solution.py
+++ b/solution.py
@@ -311,10 +311,30 @@
         out_ref[span, :] = base[span] + part
 
 
+def piece_rows(refs, what, groups):
+    order = (0, 1, "ends", 2, 3, "notes")
+    at = order.index(what) * groups
+    size = NOTES if what == "notes" else groups
+    if len(refs) == 2 and at >= 3 * groups:
+        return refs[1], slice(at - 3 * groups, at - 3 * groups + size)
+    return refs[0], slice(at, at + size)
+
+
+def piece_part(refs, what, groups):
+    ref, span = piece_rows(refs, what, groups)
+    return ref[span, :]
+
+
 def project_kernel(*rest):
-    same, other, base_ref, main_ref, tail_ref, last_main_ref, last_tail_ref, gain_ref, out_ref = rest
+    same, other, base_ref, main_ref, tail_ref, last_main_ref, last_tail_ref, gain_ref, out_ref, *halves = rest
     patches = base_ref.shape[0]
     groups = patches // 4
+
+    def put(what, rows):
+        for refs in ([out_ref], halves):
+            ref, span = piece_rows(refs, what, groups)
+            ref[span, :] = rows.astype(BF16)
+
     block = far_block()
     is_last = late_source() == (row_index() // 2 ^ 3)
     full = collect_late(same, other)
@@ -337,10 +357,10 @@
         coarse = total.astype(BF16).astype(F32)
         notes = jnp.where(row == corner, coarse, jnp.where(row == 4 + corner, total - coarse, notes))
         sent = hidden * gain_ref[...]
-        out_ref[span, :] = sent[:, :WIDE].astype(BF16)
+        put(corner, sent[:, :WIDE])
         ends.append(sent[:, WIDE:])
-    out_ref[patches : patches + groups, :] = jnp.concatenate(ends, axis=1).astype(BF16)
-    out_ref[patches + groups :, :] = notes.astype(BF16)
+    put("ends", jnp.concatenate(ends, axis=1))
+    put("notes", notes)
 
 
 def tail_kernel(weight_ref, bias_hbm, token_ref, out_ref, bias_out, line, sem):
@@ -363,49 +383,48 @@
     return [0, first, second, 6, 1, 1 ^ second, 1 ^ first, 7]
 
 
-def merge_product(weight_ref, corner, pieces):
+def merge_product(weight_ref, corner, groups, pieces):
     me = row_index()
-    groups = pieces[0][1].shape[0] // 4
     at = [pl.multiple_of(corner * D + (me ^ step) * WIDE, WIDE) for step, _ in pieces]
     return lax.dot_general(
         jnp.concatenate([weight_ref[:, pl.ds(spot, WIDE)] for spot in at], axis=1),
-        jnp.concatenate([piece[corner * groups : (corner + 1) * groups] for _, piece in pieces], axis=1),
+        jnp.concatenate([piece_part(refs, corner, groups) for _, refs in pieces], axis=1),
         (((1,), (1,)), ((), ())),
         preferred_element_type=F32,
     )
 
 
 def merge_early_kernel(*rest):
-    pieces, (weight_ref, out_ref) = rest[:4], rest[4:]
+    own, near_own, one, near_one = rest[:1], rest[1:2], rest[2:4], rest[4:6]
+    weight_ref, out_ref = rest[6:]
     steps = piece_steps()
-    patches = 4 * out_ref.shape[2]
-    own, one, near_own, near_one = [
-        (steps[at], piece[:patches]) for at, piece in zip((0, 1, 4, 5), pieces)
-    ]
+    groups = out_ref.shape[2]
     for corner in range(4):
-        out_ref[corner] = merge_product(weight_ref, corner, (own, near_own)) + merge_product(
-            weight_ref, corner, (one, near_one)
-        )
+        out_ref[corner] = merge_product(
+            weight_ref, corner, groups, [(steps[0], own), (steps[4], near_own)]
+        ) + merge_product(weight_ref, corner, groups, [(steps[1], one), (steps[5], near_one)])
 
 
 def merge_kernel(*rest):
-    pieces = rest[:ROWS]
-    early_ref, weight_ref, tail_ref, bias_ref, live_ref, out_ref, ends_ref = rest[ROWS:]
+    pieces, rest = [], list(rest)
+    for count in (1, 2, 1, 2, 1, 2, 1, 2):
+        pieces.append(rest[:count])
+        del rest[:count]
+    early_ref, weight_ref, tail_ref, bias_ref, live_ref, out_ref, ends_ref = rest
     me = row_index()
     groups = live_ref.shape[1]
-    patches = 4 * groups
     notes = jnp.zeros((NOTES, groups), F32)
     steps = piece_steps()
-    for step, piece in zip(steps, pieces):
-        ends_ref[:, pl.ds(pl.multiple_of((me ^ step) * WIDE, WIDE), WIDE)] = piece[patches : patches + groups]
-        notes = notes + piece[patches + groups :].astype(F32)
-    late = [[(steps[at], pieces[at][:patches]) for at in couple] for couple in ((2, 6), (3, 7))]
+    for step, refs in zip(steps, pieces):
+        ends_ref[:, pl.ds(pl.multiple_of((me ^ step) * WIDE, WIDE), WIDE)] = piece_part(refs, "ends", groups)
+        notes = notes + piece_part(refs, "notes", groups).astype(F32)
+    late = [[(steps[at], pieces[at]) for at in couple] for couple in ((2, 6), (3, 7))]
     scale = lax.rsqrt((notes[:4] + notes[4:8]) * (1.0 / D) + 1e-06)
     total = jnp.zeros(bias_ref.shape[:1] + (groups,), F32)
     for corner in range(4):
         part = early_ref[corner]
         for couple in late:
-            part = part + merge_product(weight_ref, corner, couple)
+            part = part + merge_product(weight_ref, corner, groups, couple)
         total = total + scale[corner : corner + 1] * part
     spread = jnp.concatenate([jnp.broadcast_to(scale[at : at + 1], (REST, groups)) for at in range(4)], axis=0).T
     ends = ends_ref[...].astype(F32) * jnp.concatenate([spread] * ROWS, axis=1)
@@ -459,8 +478,8 @@
     return [value, far[0], far[1], near[0], near[1], near[2], far[2], near[3]]
 
 
-def after(value, array):
-    return lax.optimization_barrier((value, array))[0]
+def after(value, *arrays):
+    return lax.optimization_barrier((value, *arrays))[0]
 
 
 def local_eight(qkv_rows, residual, out_weight, norm_gain, merge_weight, merge_bias, page_grid):
@@ -535,10 +554,10 @@
         flops=4 * patches * MAIN * 4096,
         moved=4 << 20,
     )(*pieces[:EARLY], main, tail, *last, resid)
-    hidden = kernel(
+    hidden, *halves = kernel(
         project_kernel,
         "project",
-        shape(piece + NOTES, WIDE),
+        [shape(piece + NOTES, WIDE), shape(3 * groups, WIDE), shape(2 * groups + NOTES, WIDE)],
         count=2 + 6,
         flops=patches * MAIN * 256,
         moved=4 << 20,
@@ -554,28 +573,28 @@
     )(merge_weight, in_hbm(merge_bias), hidden)
     first = [(row, row ^ (2 + 2 * (row % 2))) for row in range(ROWS)]
     second = [(row, row ^ (4 - 2 * (row % 2))) for row in range(ROWS)]
-    one = lax.ppermute(hidden, "row", first)
-    two = lax.ppermute(after(hidden, ends), "row", second)
-    three = lax.ppermute(one, "row", second)
-    near = [swap(hidden, 1), swap(one, 1), swap(two, 1)]
+    one = [lax.ppermute(half, "row", first) for half in halves]
+    two = lax.ppermute(hidden, "row", second)
+    three = [lax.ppermute(half, "row", second) for half in one]
+    near = [[swap(after(hidden, one[1], ends), 1)], [swap(after(half, three[1]), 1) for half in one], [swap(after(two, three[1]), 1)]]
     early = kernel(
         merge_early_kernel,
         "merge_early",
         shape(4, units, groups, dtype=F32),
-        count=5,
-        flops=4 * units * groups * MAIN * 16,
+        count=7,
+        flops=1000,
         moved=8 << 20,
-    )(hidden, one, near[0], near[1], merge_weight)
-    near.append(swap(after(three, early), 1))
+    )(hidden, *near[0], *one, *near[1], merge_weight)
+    near.append([swap(half, 1) for half in three])
     return kernel(
         merge_kernel,
         "merge",
         shape(1, units, groups),
         [pltpu.VMEM((groups, MAIN), BF16)],
-        count=ROWS + 5,
+        count=12 + 5,
         flops=4 * units * groups * MAIN,
         moved=8 << 20,
-    )(hidden, one, two, three, *near, early, merge_weight, ends, bias, live)
+    )(hidden, *one, two, *three, *sum(near, []), early, merge_weight, ends, bias, live)
 
 
 def solution(mesh):

time: 46.5 us -> 47.1 us (1.013)
  starting transfers between devices: 22.3 us -> 25 us
  waiting for transfers between devices: 13 us -> 11 us
    ppermute x3 -> x5, starting transfers between devices: 4 us -> 5.66 us  [the longest x2 2.24 us: local_eight(): three = [lax.ppermute(half, 'row', second) for half in one]]
    ppermute x18 -> x20, waiting for transfers between devices: 8.55 us -> 7.18 us  [swap(): lax.ppermute(value, 'row', [(row, row ^ step) for row in range(ROWS)])]
    ppermute x18 -> x20, starting transfers between devices: 11.7 us -> 12.8 us  [swap(): lax.ppermute(value, 'row', [(row, row ^ step) for row in range(ROWS)])]
    ppermute x3 -> x5, waiting for transfers between devices: 4.46 us -> 3.85 us  [the longest x2 2.29 us: local_eight(): one = [lax.ppermute(half, 'row', first) for half in halves]]
  transfers between devices with their start and end apart: 24 -> 28, of which waited for: 10 -> 9; matrix products, arithmetic and copies ran while one was open for 0% -> 0% of each run, Pallas kernels for 14% -> 13%
where the time goes in v9:
time: 47.1 us; the launch traced here: 46.9 us
  starting transfers between devices  25 us (53%)
  waiting for transfers between devices  11 us (23%)
  Pallas kernels  10.7 us (23%)
    ppermute x20, starting transfers between devices, swap(): lax.ppermute(value, 'row', [(row, row ^ step) for row in range(ROWS)])  12.8 us
    ppermute x20, waiting for transfers between devices, swap(): lax.ppermute(value, 'row', [(row, row ^ step) for row in range(ROWS)])  7.18 us
    ppermute x3, starting transfers between devices, turn(): lax.ppermute(value, 'page', [(page, (page + step) % PAGES) for page in ra...  6.53 us
    ppermute x2, waiting for transfers between devices, local_eight(): one = [lax.ppermute(half, 'row', first) for half in halves]  2.29 us
    ppermute x2, starting transfers between devices, local_eight(): three = [lax.ppermute(half, 'row', second) for half in one]  2.24 us
    ppermute x2, starting transfers between devices, local_eight(): one = [lax.ppermute(half, 'row', first) for half in halves]  2.03 us
    pallas_call x1, Pallas kernels, local_eight(): kernel(merge_kernel, 'merge', shape(1, units, groups), [pltpu.VMEM((group...  2.02 us
    pallas_call x1, Pallas kernels, local_eight(): kernel(spread_kernel, 'spread', [shape(band, 4 * HPAIR)] * ROWS + [shape(...  1.74 us
  transfers between devices with their start and end apart: 28, of which 9 were waited for; matrix products, arithmetic and copies ran while one was open for 0% of the time, Pallas kernels for 13%

profile of v9, /device:TPU:0, one launch (start us, length us, event | category | flops | bytes accessed | tf_op | source)
XLA Modules:
  0.0 46.9 jit_solution(8059175544593863167)
XLA Ops:
  0.0 1.7 %spread.1 = (bf16[64,640]{1,0:T(8,128)(2,1)S(1)}, bf16[64,640]{1,0:T(8,128)(2,1)S(1)}, bf16[64,640]{1,0:T(8,128)(2,1)S(1)}, bf16[64,640]{1,0:T(8,128)(2,1)S(1)},...) custom-call(bf16[1,64,3840]{2,1,0:T(8,128)(2,1)} %qkv_hbm.1, ...), custom_call_target="tpu_custom_call" | custom-call | bytes 1048576 | tf_op jit(solution)/shard_map/spread/pallas_call | solution.py:493
  1.7 3.0 %collective-permute-start = (bf16[64,640]{1,0:T(8,128)(2,1)S(1)}, bf16[64,640]{1,0:T(8,128)(2,1)S(1)}, u32[]{:S(2)}, u32[]{:S(2)}) collective-permute-start(bf16[64,640]{1,0:T(8,128)(2,1)S(1)} %get-tuple-element.36), channel_id=1, source_target_pairs={{0,2},{1,3},{2,0},{3,1},{4,6},{5,7},{6,4},{7,5},{8,10},{9,11},{10,... | collective-permute-start | bytes 245768 | tf_op jit(solution)/shard_map/ppermute | solution.py:464
  4.7 1.5 %collective-permute-start.1 = (bf16[64,640]{1,0:T(8,128)(2,1)S(1)}, bf16[64,640]{1,0:T(8,128)(2,1)S(1)}, u32[]{:S(2)}, u32[]{:S(2)}) collective-permute-start(bf16[64,640]{1,0:T(8,128)(2,1)S(1)} %get-tuple-element.37), channel_id=1, source_target_pairs={{0,4},{1,5},{2,6},{3,7},{4,0},{5,1},{6,2},{7,3},{8,12},{9,13},{10,... | collective-permute-start | bytes 245768 | tf_op jit(solution)/shard_map/ppermute | solution.py:464
  6.3 1.5 %collective-permute-start.3 = (bf16[64,640]{1,0:T(8,128)(2,1)S(1)}, bf16[64,640]{1,0:T(8,128)(2,1)S(1)}, u32[]{:S(2)}, u32[]{:S(2)}) collective-permute-start(bf16[64,640]{1,0:T(8,128)(2,1)S(1)} %get-tuple-element.42), channel_id=1, source_target_pairs={{0,7},{1,6},{2,5},{3,4},{4,3},{5,2},{6,1},{7,0},{8,15},{9,14},{10,... | collective-permute-start | bytes 245768 | tf_op jit(solution)/shard_map/ppermute | solution.py:464
  7.8 1.7 %collective-permute-start.4 = (bf16[64,640]{1,0:T(8,128)(2,1)S(1)}, bf16[64,640]{1,0:T(8,128)(2,1)S(1)}, u32[]{:S(2)}, u32[]{:S(2)}) collective-permute-start(bf16[64,640]{1,0:T(8,128)(2,1)S(1)} %get-tuple-element.43), channel_id=1, source_target_pairs={{0,3},{1,2},{2,1},{3,0},{4,7},{5,6},{6,5},{7,4},{8,11},{9,10},{10,... | collective-permute-start | bytes 245768 | tf_op jit(solution)/shard_map/ppermute | solution.py:464
  10.1 2.3 %collective-permute-done.2.rest_2_.rest_3_ = bf16[64,640]{1,0:T(8,128)(2,1)S(1)} collective-permute-done((bf16[64,640]{1,0:T(8,128)(2,1)S(1)}, bf16[64,640]{1,0:T(8,128)(2,1)S(1)}, u32[]{:S(2)}, u32[]{:S(2)}) %collective-permute-start.2) | collective-permute-done | bytes 81952 | tf_op jit(solution)/shard_map/ppermute | solution.py:464
  12.4 2.7 %collective-permute-start.11 = (bf16[400,128]{1,0:T(8,128)(2,1)S(1)}, bf16[400,128]{1,0:T(8,128)(2,1)S(1)}, u32[]{:S(2)}, u32[]{:S(2)}) collective-permute-start(bf16[400,128]{1,0:T(8,128)(2,1)S(1)} %get-tuple-element.46.rest_8_), channel_id=1, source_target_pairs={{0,16},{8,24},{16,0},{24,8},{1,17},{9,25},{17,1},{25,9},{2,18},{10... | collective-permute-start | bytes 307208 | tf_op jit(solution)/shard_map/ppermute | solution.py:468
  15.3 1.6 %collective-permute-start.12 = (bf16[400,128]{1,0:T(8,128)(2,1)S(1)}, bf16[400,128]{1,0:T(8,128)(2,1)S(1)}, u32[]{:S(2)}, u32[]{:S(2)}) collective-permute-start(bf16[400,128]{1,0:T(8,128)(2,1)S(1)} %get-tuple-element.46.rest_8_), channel_id=1, source_target_pairs={{0,8},{8,16},{16,24},{24,0},{1,9},{9,17},{17,25},{25,1},{2,10},{10... | collective-permute-start | bytes 307208 | tf_op jit(solution)/shard_map/ppermute | solution.py:468
  16.9 2.2 %collective-permute-start.15 = (bf16[400,128]{1,0:T(8,128)(2,1)S(1)}, bf16[400,128]{1,0:T(8,128)(2,1)S(1)}, u32[]{:S(2)}, u32[]{:S(2)}) collective-permute-start(bf16[400,128]{1,0:T(8,128)(2,1)S(1)} %get-tuple-element.46.rest_8_), channel_id=1, source_target_pairs={{0,24},{8,0},{16,8},{24,16},{1,25},{9,1},{17,9},{25,17},{2,26},{10... | collective-permute-start | bytes 307208 | tf_op jit(solution)/shard_map/ppermute | solution.py:468
  19.2 1.4 %attend.1.token_ref.rest_0_ = bf16[640,128]{1,0:T(8,128)(2,1)S(1)} custom-call(bf16[512,512]{1,0:T(8,128)(2,1)S(1)} %get-tuple-element.39.select_ref, f32[1,512]{1,0:T(1,128)S(1)} %get-tuple-element.40.dead_ref, bf16[64,640]{1,0:T(8,128)(2,1)S(1)} %get-tuple-element.41.rest_0_, bf16[64,640]{1,0:T(8,128)(2,1)S(1)} %collective-permute-done.rest_0_.rest_1_, ...), custom_call_target="tpu_custom_call" | custom-call | flops 21474836480 | bytes 1048576 | tf_op jit(solution)/shard_map/attend/pallas_call | solution.py:520
  21.2 2.8 %collective-permute-start.7 = (bf16[640,128]{1,0:T(8,128)(2,1)S(1)}, bf16[640,128]{1,0:T(8,128)(2,1)S(1)}, u32[]{:S(2)}, u32[]{:S(2)}) collective-permute-start(bf16[640,128]{1,0:T(8,128)(2,1)S(1)} %attend.1.token_ref.rest_0_), channel_id=1, source_target_pairs={{0,6},{1,7},{2,4},{3,5},{4,2},{5,3},{6,0},{7,1},{8,14},{9,15},{10,... | collective-permute-start | bytes 491528 | tf_op jit(solution)/shard_map/ppermute | solution.py:464
  24.1 1.2 %ready.1 = (f32[512,160]{1,0:T(8,128)S(1)}, f32[1,160]{1,0:T(1,128)S(1)}, bf16[1024,160]{1,0:T(8,128)(2,1)S(1)}, bf16[4,1024,160]{2,1,0:T(8,128)(2,1)S(1)}) custom-call(bf16[512,512]{1,0:T(8,128)(2,1)S(1)} %get-tuple-element.39.select_ref, f32[1280]{0:T(1024)} %gain_hbm.1, bf16[640,128]{1,0:T(8,128)(2,1)S(1)} %attend.1.token_ref.rest_0_, ...), custom_call_target="tpu_custom_call" | custom-call | flops 10737418240 | bytes 4194304 | tf_op jit(solution)/shard_map/ready/pallas_call | solution.py:529
  25.5 2.2 %collective-permute-done.10.rest_2_ = bf16[640,128]{1,0:T(8,128)(2,1)S(1)} collective-permute-done((bf16[640,128]{1,0:T(8,128)(2,1)S(1)}, bf16[640,128]{1,0:T(8,128)(2,1)S(1)}, u32[]{:S(2)}, u32[]{:S(2)}) %collective-permute-start.10) | collective-permute-done | bytes 163872 | tf_op jit(solution)/shard_map/ppermute | solution.py:464
  28.2 1.7 %collective-permute-done.7.rest_0_ = bf16[640,128]{1,0:T(8,128)(2,1)S(1)} collective-permute-done((bf16[640,128]{1,0:T(8,128)(2,1)S(1)}, bf16[640,128]{1,0:T(8,128)(2,1)S(1)}, u32[]{:S(2)}, u32[]{:S(2)}) %collective-permute-start.7) | collective-permute-done | bytes 163872 | tf_op jit(solution)/shard_map/ppermute | solution.py:464
  29.9 1.2 %project_early.1.rest_2_ = f32[512,160]{1,0:T(8,128)S(1)} custom-call(bf16[640,128]{1,0:T(8,128)(2,1)S(1)} %attend.1.token_ref.rest_0_, bf16[640,128]{1,0:T(8,128)(2,1)S(1)} %collective-permute-done.9.rest_1_, bf16[640,128]{1,0:T(8,128)(2,1)S(1)} %collective-permute-done.10.rest_2_, bf16[640,128]{1,0:T(8,128)(2,1)S(1)} %collective-permute-done.13.rest_3_, ...), custom_call_target="tpu_custom_call" | custom-call | flops 8589934592 | bytes 4194304 | tf_op jit(solution)/shard_map/project_early/pallas_call | solution.py:548
  32.0 1.4 %collective-permute-start.19 = (bf16[656,128]{1,0:T(8,128)(2,1)S(1)}, bf16[656,128]{1,0:T(8,128)(2,1)S(1)}, u32[]{:S(2)}, u32[]{:S(2)}) collective-permute-start(bf16[656,128]{1,0:T(8,128)(2,1)S(1)} %get-tuple-element.59.token_ref.rest_0_), channel_id=1, source_target_pairs={{0,4},{1,3},{2,6},{3,1},{4,0},{5,7},{6,2},{7,5},{8,12},{9,11},{10,... | collective-permute-start | bytes 503816 | tf_op jit(solution)/shard_map/ppermute | solution.py:577
  34.0 1.4 %collective-permute-start.17 = (bf16[384,128]{1,0:T(8,128)(2,1)S(1)}, bf16[384,128]{1,0:T(8,128)(2,1)S(1)}, u32[]{:S(2)}, u32[]{:S(2)}) collective-permute-start(bf16[384,128]{1,0:T(8,128)(2,1)S(1)} %get-tuple-element.56), channel_id=1, source_target_pairs={{0,2},{1,5},{2,0},{3,7},{4,6},{5,1},{6,4},{7,3},{8,10},{9,13},{10,... | collective-permute-start | bytes 294920 | tf_op jit(solution)/shard_map/ppermute | solution.py:576
  35.4 2.3 %collective-permute-done.18.rest_3_.rest_2_ = bf16[272,128]{1,0:T(8,128)(2,1)S(1)} collective-permute-done((bf16[272,128]{1,0:T(8,128)(2,1)S(1)}, bf16[272,128]{1,0:T(8,128)(2,1)S(1)}, u32[]{:S(2)}, u32[]{:S(2)}) %collective-permute-start.18) | collective-permute-done | bytes 69664 | tf_op jit(solution)/shard_map/ppermute | solution.py:576
  37.7 1.2 %collective-permute-start.21 = (bf16[272,128]{1,0:T(8,128)(2,1)S(1)}, bf16[272,128]{1,0:T(8,128)(2,1)S(1)}, u32[]{:S(2)}, u32[]{:S(2)}) collective-permute-start(bf16[272,128]{1,0:T(8,128)(2,1)S(1)} %collective-permute-done.18.rest_3_.rest_2_), channel_id=1, source_target_pairs={{0,4},{1,3},{2,6},{3,1},{4,0},{5,7},{6,2},{7,5},{8,12},{9,11},{10,... | collective-permute-start | bytes 208904 | tf_op jit(solution)/shard_map/ppermute | solution.py:578
  38.8 1.0 %collective-permute-start.20 = (bf16[384,128]{1,0:T(8,128)(2,1)S(1)}, bf16[384,128]{1,0:T(8,128)(2,1)S(1)}, u32[]{:S(2)}, u32[]{:S(2)}) collective-permute-start(bf16[384,128]{1,0:T(8,128)(2,1)S(1)} %collective-permute-done.17.rest_2_.rest_1_), channel_id=1, source_target_pairs={{0,4},{1,3},{2,6},{3,1},{4,0},{5,7},{6,2},{7,5},{8,12},{9,11},{10,... | collective-permute-start | bytes 294920 | tf_op jit(solution)/shard_map/ppermute | solution.py:578
  39.9 1.4 %merge_tail.1 = (bf16[640,1024]{1,0:T(8,128)(2,1)S(1)}, f32[640,1]{1,0:T(8,128)S(1)}) custom-call(bf16[640,5120]{1,0:T(8,128)(2,1)S(1)} %bitcast.1, f32[640]{0:T(1024)} %bias_hbm.1, bf16[656,128]{1,0:T(8,128)(2,1)S(1)} %get-tuple-element.59.token_ref.rest_0_), custom_call_target="tpu_custom_call" | custom-call | bytes 4194304 | tf_op jit(solution)/shard_map/merge_tail/pallas_call | solution.py:565
  42.5 1.0 %collective-permute-done.20.rest_4_ = bf16[384,128]{1,0:T(8,128)(2,1)S(1)} collective-permute-done((bf16[384,128]{1,0:T(8,128)(2,1)S(1)}, bf16[384,128]{1,0:T(8,128)(2,1)S(1)}, u32[]{:S(2)}, u32[]{:S(2)}) %collective-permute-start.20) | collective-permute-done | bytes 98336 | tf_op jit(solution)/shard_map/ppermute | solution.py:578
  44.0 0.9 %merge_early.1.rest_12_ = f32[4,640,128]{2,1,0:T(8,128)S(1)} custom-call(bf16[656,128]{1,0:T(8,128)(2,1)S(1)} %get-tuple-element.59.token_ref.rest_0_, bf16[656,128]{1,0:T(8,128)(2,1)S(1)} %collective-permute-done.22.rest_1_.rest_6_, bf16[384,128]{1,0:T(8,128)(2,1)S(1)} %collective-permute-done.17.rest_2_.rest_1_, ...), custom_call_target="tpu_custom_call" | custom-call | flops 1000 | bytes 8388608 | tf_op jit(solution)/shard_map/merge_early/pallas_call | solution.py:580
  44.9 2.0 %merge.1 = bf16[1,640,128]{2,1,0:T(8,128)(2,1)} custom-call(bf16[656,128]{1,0:T(8,128)(2,1)S(1)} %get-tuple-element.59.token_ref.rest_0_, bf16[384,128]{1,0:T(8,128)(2,1)S(1)} %collective-permute-done.17.rest_2_.rest_1_, bf16[272,128]{1,0:T(8,128)(2,1)S(1)} %collective-permute-done.18.rest_3_.rest_2_, bf16[656,128]{1,0:T(8,128)(2,1)S(1)} %collective-permute-done.19.rest_3_, ...), custom_call_target="tpu_custom_call" | custom-call | flops 335544320 | bytes 8388608 | tf_op jit(solution)/shard_map/merge/pallas_call | solution.py:589
  (47 shorter events, 5.4 us)
Async XLA Ops:
  1.7 7.7 %collective-permute-start = (bf16[64,640]{1,0:T(8,128)(2,1)S(1)}, bf16[64,640]{1,0:T(8,128)(2,1)S(1)}, u32[]{:S(2)}, u32[]{:S(2)}) collective-permute-start(bf16[64,640]{1,0:T(8,128)(2,1)S(1)} %get-tuple-element.36), channel_id=1, source_target_pairs={{0,2},{1,3},{2,0},{3,1},{4,6},{5,7},{6,4},{7,5},{8,10},{9,11},{10,... | collective-permute-start | bytes 245768 | tf_op jit(solution)/shard_map/ppermute | solution.py:464
  4.7 5.3 %collective-permute-start.1 = (bf16[64,640]{1,0:T(8,128)(2,1)S(1)}, bf16[64,640]{1,0:T(8,128)(2,1)S(1)}, u32[]{:S(2)}, u32[]{:S(2)}) collective-permute-start(bf16[64,640]{1,0:T(8,128)(2,1)S(1)} %get-tuple-element.37), channel_id=1, source_target_pairs={{0,4},{1,5},{2,6},{3,7},{4,0},{5,1},{6,2},{7,3},{8,12},{9,13},{10,... | collective-permute-start | bytes 245768 | tf_op jit(solution)/shard_map/ppermute | solution.py:464
  6.3 6.2 %collective-permute-start.2 = (bf16[64,640]{1,0:T(8,128)(2,1)S(1)}, bf16[64,640]{1,0:T(8,128)(2,1)S(1)}, u32[]{:S(2)}, u32[]{:S(2)}) collective-permute-start(bf16[64,640]{1,0:T(8,128)(2,1)S(1)} %get-tuple-element.38), channel_id=1, source_target_pairs={{0,6},{1,7},{2,4},{3,5},{4,2},{5,3},{6,0},{7,1},{8,14},{9,15},{10,... | collective-permute-start | bytes 245768 | tf_op jit(solution)/shard_map/ppermute | solution.py:464
  6.3 9.0 %collective-permute-start.3 = (bf16[64,640]{1,0:T(8,128)(2,1)S(1)}, bf16[64,640]{1,0:T(8,128)(2,1)S(1)}, u32[]{:S(2)}, u32[]{:S(2)}) collective-permute-start(bf16[64,640]{1,0:T(8,128)(2,1)S(1)} %get-tuple-element.42), channel_id=1, source_target_pairs={{0,7},{1,6},{2,5},{3,4},{4,3},{5,2},{6,1},{7,0},{8,15},{9,14},{10,... | collective-permute-start | bytes 245768 | tf_op jit(solution)/shard_map/ppermute | solution.py:464
  7.8 9.1 %collective-permute-start.4 = (bf16[64,640]{1,0:T(8,128)(2,1)S(1)}, bf16[64,640]{1,0:T(8,128)(2,1)S(1)}, u32[]{:S(2)}, u32[]{:S(2)}) collective-permute-start(bf16[64,640]{1,0:T(8,128)(2,1)S(1)} %get-tuple-element.43), channel_id=1, source_target_pairs={{0,3},{1,2},{2,1},{3,0},{4,7},{5,6},{6,5},{7,4},{8,11},{9,10},{10,... | collective-permute-start | bytes 245768 | tf_op jit(solution)/shard_map/ppermute | solution.py:464
  9.5 9.7 %collective-permute-start.5 = (bf16[64,640]{1,0:T(8,128)(2,1)S(1)}, bf16[64,640]{1,0:T(8,128)(2,1)S(1)}, u32[]{:S(2)}, u32[]{:S(2)}) collective-permute-start(bf16[64,640]{1,0:T(8,128)(2,1)S(1)} %get-tuple-element.44), channel_id=1, source_target_pairs={{0,5},{1,4},{2,7},{3,6},{4,1},{5,0},{6,3},{7,2},{8,13},{9,12},{10,... | collective-permute-start | bytes 245768 | tf_op jit(solution)/shard_map/ppermute | solution.py:464
  10.1 9.1 %collective-permute-start.6 = (bf16[64,640]{1,0:T(8,128)(2,1)S(1)}, bf16[64,640]{1,0:T(8,128)(2,1)S(1)}, u32[]{:S(2)}, u32[]{:S(2)}) collective-permute-start(bf16[64,640]{1,0:T(8,128)(2,1)S(1)} %get-tuple-element.45), channel_id=1, source_target_pairs={{0,1},{1,0},{2,3},{3,2},{4,5},{5,4},{6,7},{7,6},{8,9},{9,8},{10,11... | collective-permute-start | bytes 245768 | tf_op jit(solution)/shard_map/ppermute | solution.py:464
  12.4 8.8 %collective-permute-start.11 = (bf16[400,128]{1,0:T(8,128)(2,1)S(1)}, bf16[400,128]{1,0:T(8,128)(2,1)S(1)}, u32[]{:S(2)}, u32[]{:S(2)}) collective-permute-start(bf16[400,128]{1,0:T(8,128)(2,1)S(1)} %get-tuple-element.46.rest_8_), channel_id=1, source_target_pairs={{0,16},{8,24},{16,0},{24,8},{1,17},{9,25},{17,1},{25,9},{2,18},{10... | collective-permute-start | bytes 307208 | tf_op jit(solution)/shard_map/ppermute | solution.py:468
  15.3 8.8 %collective-permute-start.12 = (bf16[400,128]{1,0:T(8,128)(2,1)S(1)}, bf16[400,128]{1,0:T(8,128)(2,1)S(1)}, u32[]{:S(2)}, u32[]{:S(2)}) collective-permute-start(bf16[400,128]{1,0:T(8,128)(2,1)S(1)} %get-tuple-element.46.rest_8_), channel_id=1, source_target_pairs={{0,8},{8,16},{16,24},{24,0},{1,9},{9,17},{17,25},{25,1},{2,10},{10... | collective-permute-start | bytes 307208 | tf_op jit(solution)/shard_map/ppermute | solution.py:468
  16.9 8.5 %collective-permute-start.15 = (bf16[400,128]{1,0:T(8,128)(2,1)S(1)}, bf16[400,128]{1,0:T(8,128)(2,1)S(1)}, u32[]{:S(2)}, u32[]{:S(2)}) collective-permute-start(bf16[400,128]{1,0:T(8,128)(2,1)S(1)} %get-tuple-element.46.rest_8_), channel_id=1, source_target_pairs={{0,24},{8,0},{16,8},{24,16},{1,25},{9,1},{17,9},{25,17},{2,26},{10... | collective-permute-start | bytes 307208 | tf_op jit(solution)/shard_map/ppermute | solution.py:468
  20.5 7.1 %collective-permute-start.10 = (bf16[640,128]{1,0:T(8,128)(2,1)S(1)}, bf16[640,128]{1,0:T(8,128)(2,1)S(1)}, u32[]{:S(2)}, u32[]{:S(2)}) collective-permute-start(bf16[640,128]{1,0:T(8,128)(2,1)S(1)} %attend.1.token_ref.rest_0_), channel_id=1, source_target_pairs={{0,4},{1,5},{2,6},{3,7},{4,0},{5,1},{6,2},{7,3},{8,12},{9,13},{10,... | collective-permute-start | bytes 491528 | tf_op jit(solution)/shard_map/ppermute | solution.py:464
  20.6 7.2 %collective-permute-start.9 = (bf16[640,128]{1,0:T(8,128)(2,1)S(1)}, bf16[640,128]{1,0:T(8,128)(2,1)S(1)}, u32[]{:S(2)}, u32[]{:S(2)}) collective-permute-start(bf16[640,128]{1,0:T(8,128)(2,1)S(1)} %attend.1.token_ref.rest_0_), channel_id=1, source_target_pairs={{0,2},{1,3},{2,0},{3,1},{4,6},{5,7},{6,4},{7,5},{8,10},{9,11},{10,... | collective-permute-start | bytes 491528 | tf_op jit(solution)/shard_map/ppermute | solution.py:464
  21.2 8.6 %collective-permute-start.7 = (bf16[640,128]{1,0:T(8,128)(2,1)S(1)}, bf16[640,128]{1,0:T(8,128)(2,1)S(1)}, u32[]{:S(2)}, u32[]{:S(2)}) collective-permute-start(bf16[640,128]{1,0:T(8,128)(2,1)S(1)} %attend.1.token_ref.rest_0_), channel_id=1, source_target_pairs={{0,6},{1,7},{2,4},{3,5},{4,2},{5,3},{6,0},{7,1},{8,14},{9,15},{10,... | collective-permute-start | bytes 491528 | tf_op jit(solution)/shard_map/ppermute | solution.py:464
  25.3 4.6 %collective-permute-start.13 = (bf16[640,128]{1,0:T(8,128)(2,1)S(1)}, bf16[640,128]{1,0:T(8,128)(2,1)S(1)}, u32[]{:S(2)}, u32[]{:S(2)}) collective-permute-start(bf16[640,128]{1,0:T(8,128)(2,1)S(1)} %attend.1.token_ref.rest_0_), channel_id=1, source_target_pairs={{0,1},{1,0},{2,3},{3,2},{4,5},{5,4},{6,7},{7,6},{8,9},{9,8},{10,11... | collective-permute-start | bytes 491528 | tf_op jit(solution)/shard_map/ppermute | solution.py:464
  27.6 2.2 %collective-permute-start.16 = (bf16[640,128]{1,0:T(8,128)(2,1)S(1)}, bf16[640,128]{1,0:T(8,128)(2,1)S(1)}, u32[]{:S(2)}, u32[]{:S(2)}) collective-permute-start(bf16[640,128]{1,0:T(8,128)(2,1)S(1)} %collective-permute-done.10.rest_2_), channel_id=1, source_target_pairs={{0,1},{1,0},{2,3},{3,2},{4,5},{5,4},{6,7},{7,6},{8,9},{9,8},{10,11... | collective-permute-start | bytes 491528 | tf_op jit(solution)/shard_map/ppermute | solution.py:464
  27.8 2.1 %collective-permute-start.14 = (bf16[640,128]{1,0:T(8,128)(2,1)S(1)}, bf16[640,128]{1,0:T(8,128)(2,1)S(1)}, u32[]{:S(2)}, u32[]{:S(2)}) collective-permute-start(bf16[640,128]{1,0:T(8,128)(2,1)S(1)} %collective-permute-done.9.rest_1_), channel_id=1, source_target_pairs={{0,1},{1,0},{2,3},{3,2},{4,5},{5,4},{6,7},{7,6},{8,9},{9,8},{10,11... | collective-permute-start | bytes 491528 | tf_op jit(solution)/shard_map/ppermute | solution.py:464
  32.0 10.0 %collective-permute-start.19 = (bf16[656,128]{1,0:T(8,128)(2,1)S(1)}, bf16[656,128]{1,0:T(8,128)(2,1)S(1)}, u32[]{:S(2)}, u32[]{:S(2)}) collective-permute-start(bf16[656,128]{1,0:T(8,128)(2,1)S(1)} %get-tuple-element.59.token_ref.rest_0_), channel_id=1, source_target_pairs={{0,4},{1,3},{2,6},{3,1},{4,0},{5,7},{6,2},{7,5},{8,12},{9,11},{10,... | collective-permute-start | bytes 503816 | tf_op jit(solution)/shard_map/ppermute | solution.py:577
  33.3 4.3 %collective-permute-start.18 = (bf16[272,128]{1,0:T(8,128)(2,1)S(1)}, bf16[272,128]{1,0:T(8,128)(2,1)S(1)}, u32[]{:S(2)}, u32[]{:S(2)}) collective-permute-start(bf16[272,128]{1,0:T(8,128)(2,1)S(1)} %get-tuple-element.57), channel_id=1, source_target_pairs={{0,2},{1,5},{2,0},{3,7},{4,6},{5,1},{6,4},{7,3},{8,10},{9,13},{10,... | collective-permute-start | bytes 208904 | tf_op jit(solution)/shard_map/ppermute | solution.py:576
  34.0 4.9 %collective-permute-start.17 = (bf16[384,128]{1,0:T(8,128)(2,1)S(1)}, bf16[384,128]{1,0:T(8,128)(2,1)S(1)}, u32[]{:S(2)}, u32[]{:S(2)}) collective-permute-start(bf16[384,128]{1,0:T(8,128)(2,1)S(1)} %get-tuple-element.56), channel_id=1, source_target_pairs={{0,2},{1,5},{2,0},{3,7},{4,6},{5,1},{6,4},{7,3},{8,10},{9,13},{10,... | collective-permute-start | bytes 294920 | tf_op jit(solution)/shard_map/ppermute | solution.py:576
  37.7 4.3 %collective-permute-start.21 = (bf16[272,128]{1,0:T(8,128)(2,1)S(1)}, bf16[272,128]{1,0:T(8,128)(2,1)S(1)}, u32[]{:S(2)}, u32[]{:S(2)}) collective-permute-start(bf16[272,128]{1,0:T(8,128)(2,1)S(1)} %collective-permute-done.18.rest_3_.rest_2_), channel_id=1, source_target_pairs={{0,4},{1,3},{2,6},{3,1},{4,0},{5,7},{6,2},{7,5},{8,12},{9,11},{10,... | collective-permute-start | bytes 208904 | tf_op jit(solution)/shard_map/ppermute | solution.py:578
  38.8 4.6 %collective-permute-start.20 = (bf16[384,128]{1,0:T(8,128)(2,1)S(1)}, bf16[384,128]{1,0:T(8,128)(2,1)S(1)}, u32[]{:S(2)}, u32[]{:S(2)}) collective-permute-start(bf16[384,128]{1,0:T(8,128)(2,1)S(1)} %collective-permute-done.17.rest_2_.rest_1_), channel_id=1, source_target_pairs={{0,4},{1,3},{2,6},{3,1},{4,0},{5,7},{6,2},{7,5},{8,12},{9,11},{10,... | collective-permute-start | bytes 294920 | tf_op jit(solution)/shard_map/ppermute | solution.py:578
  41.3 2.7 %collective-permute-start.22 = (bf16[656,128]{1,0:T(8,128)(2,1)S(1)}, bf16[656,128]{1,0:T(8,128)(2,1)S(1)}, u32[]{:S(2)}, u32[]{:S(2)}) collective-permute-start(bf16[656,128]{1,0:T(8,128)(2,1)S(1)} %get-tuple-element.59.token_ref.rest_0_), channel_id=1, source_target_pairs={{0,1},{1,0},{2,3},{3,2},{4,5},{5,4},{6,7},{7,6},{8,9},{9,8},{10,11... | collective-permute-start | bytes 503816 | tf_op jit(solution)/shard_map/ppermute | solution.py:464
  42.0 2.9 %collective-permute-start.25 = (bf16[656,128]{1,0:T(8,128)(2,1)S(1)}, bf16[656,128]{1,0:T(8,128)(2,1)S(1)}, u32[]{:S(2)}, u32[]{:S(2)}) collective-permute-start(bf16[656,128]{1,0:T(8,128)(2,1)S(1)} %collective-permute-done.19.rest_3_), channel_id=1, source_target_pairs={{0,1},{1,0},{2,3},{3,2},{4,5},{5,4},{6,7},{7,6},{8,9},{9,8},{10,11... | collective-permute-start | bytes 503816 | tf_op jit(solution)/shard_map/ppermute | solution.py:464
  42.5 1.5 %collective-permute-start.23 = (bf16[384,128]{1,0:T(8,128)(2,1)S(1)}, bf16[384,128]{1,0:T(8,128)(2,1)S(1)}, u32[]{:S(2)}, u32[]{:S(2)}) collective-permute-start(bf16[384,128]{1,0:T(8,128)(2,1)S(1)} %collective-permute-done.17.rest_2_.rest_1_), channel_id=1, source_target_pairs={{0,1},{1,0},{2,3},{3,2},{4,5},{5,4},{6,7},{7,6},{8,9},{9,8},{10,11... | collective-permute-start | bytes 294920 | tf_op jit(solution)/shard_map/ppermute | solution.py:464
  (6 other events, 25.7 us)

commit v10 on v7

--- a/solution.py
+++ b/solution.py
@@ -125,7 +125,6 @@
 BLOCK_ORDER = (0, 2, 4, 6, 7, 3, 5, 1)
 PIECE_ORDER = (0, 2, 4, 1, 3, 5, 6, 7)
 EARLY = 6
-SHIFTS = (0, 2, 1, 3)
 ROOT = math.log2(math.e) / math.sqrt(HDIM)
 BF16 = jnp.bfloat16
 F32 = jnp.float32
@@ -142,15 +141,15 @@
 
 def spread_kernel(qkv_hbm, resid_hbm, weight_hbm, grid_hbm, *rest):
     outs = rest[:ROWS]
-    slice_ref, grid_out, qkv, resid, tile, held, grid, sems = rest[ROWS:]
+    chip_ref, slice_ref, grid_out, qkv, resid, main, tile, held, grid, sems = rest[ROWS:]
     me = row_index()
     depth = weight_hbm.shape[0]
-    main = pl.ds(pl.multiple_of(me * WIDE, WIDE), WIDE)
+    chip = pl.ds(pl.multiple_of(me // 2 * 2 * WIDE, 2 * WIDE), 2 * WIDE)
     ends = pl.ds(pl.multiple_of(MAIN + me // 4 * WIDE, WIDE), WIDE)
     copies = [
         pltpu.make_async_copy(qkv_hbm.at[0], qkv, sems.at[0]),
         pltpu.make_async_copy(resid_hbm.at[0], resid, sems.at[1]),
-        pltpu.make_async_copy(weight_hbm.at[:, main], slice_ref.at[:depth], sems.at[2]),
+        pltpu.make_async_copy(weight_hbm.at[:, chip], main, sems.at[2]),
         pltpu.make_async_copy(weight_hbm.at[:, ends], tile, sems.at[3]),
         pltpu.make_async_copy(grid_hbm, grid, sems.at[4]),
     ]
@@ -166,10 +165,13 @@
         held[dest] = jnp.concatenate(parts, axis=1)
     for step in range(ROWS):
         outs[step][...] = held[me ^ step]
-    tail = tile[:, :REST]
-    for at in range(1, 4):
-        tail = jnp.where(lax.rem(me, 4) == at, tile[:, at * REST : (at + 1) * REST], tail)
-    slice_ref[depth:, :] = pack_tail(tail)
+    low = me // 2 % 2 == 0
+    size = depth + depth // 4
+    for core in range(2):
+        tail = jnp.where(low, tile[:, core * REST : (core + 1) * REST], tile[:, (core + 2) * REST : (core + 3) * REST])
+        chip_ref[core * size : core * size + depth, :] = main[:, core * WIDE : (core + 1) * WIDE]
+        chip_ref[core * size + depth : (core + 1) * size, :] = pack_tail(tail)
+    slice_ref[...] = chip_ref[pl.ds(pl.multiple_of(me % 2 * size, 16), size), :]
     row = lax.broadcasted_iota(jnp.int32, grid_out.shape, 0)
     grid_out[...] = jnp.where(row == 0, grid[0, 0], grid[0, 1])
 
@@ -240,7 +242,8 @@
 
 def ready_kernel(select_ref, gain_hbm, token_ref, *rest):
     del token_ref
-    blocks, slices = rest[:ROWS], rest[ROWS : ROWS + PAGES - 1]
+    blocks = rest[:ROWS]
+    own_ref, across_ref, near_ref = rest[ROWS : ROWS + 3]
     resid_ref, gain_out, main_ref, tail_ref, held, line, sem = rest[-7:]
     fetch = pltpu.make_async_copy(gain_hbm, line, sem)
     fetch.start()
@@ -253,9 +256,12 @@
     resid_ref[...] = jnp.dot(select_ref[...], held[...], preferred_element_type=F32)
     main_ref[...] = jnp.zeros_like(main_ref)
     tail_ref[...] = jnp.zeros_like(tail_ref)
-    for step, cut in zip(SHIFTS, slices):
-        source = lax.rem(page + PAGES - step, PAGES)
-        place_rows(weight_rows(cut), 2 * source, main_ref, tail_ref)
+    core = me % 2
+    size = own_ref.shape[0]
+    half = pl.ds(pl.multiple_of(core * size, 16), size)
+    cuts = ((0, own_ref[...]), (2, across_ref[...]), (3 - 2 * core, near_ref[half, :]))
+    for step, cut in cuts:
+        place_rows(weight_rows(cut), 2 * lax.rem(page + step, PAGES), main_ref, tail_ref)
     fetch.wait()
     whole = line[...].reshape(1, D)
     gain = jnp.zeros(gain_out.shape, F32)
@@ -266,10 +272,12 @@
     gain_out[...] = gain
 
 
-def last_kernel(cut_ref, token_ref, main_ref, tail_ref):
+def last_kernel(swapped_ref, token_ref, main_ref, tail_ref):
     del token_ref
+    size = swapped_ref.shape[0] // 2
+    cut = swapped_ref[pl.ds(pl.multiple_of(row_index() % 2 * size, 16), size), :]
     tail_ref[...] = jnp.zeros_like(tail_ref)
-    place_rows(weight_rows(cut_ref), 0, main_ref, tail_ref)
+    place_rows(weight_rows(cut), 0, main_ref, tail_ref)
 
 
 def far_block():
@@ -292,7 +300,7 @@
 
 
 def late_source():
-    return lax.rem(lax.axis_index("page") + PAGES - SHIFTS[-1], PAGES)
+    return lax.rem(lax.axis_index("page") + 1 + 2 * (row_index() % 2), PAGES)
 
 
 def project_early_kernel(*rest):
@@ -357,18 +365,30 @@
     bias_out[...] = jnp.broadcast_to(line[...].reshape(1, units), (8, units)).T[:, :1]
 
 
-def merge_early_kernel(*rest):
-    pieces = rest[:EARLY]
-    weight_ref, out_ref, full = rest[EARLY:]
-    collect_early(pieces, full)
+def chip_product(weight_ref, corner, groups, other, rows):
+    at = pl.multiple_of(corner * D + (row_index() // 2 ^ other) * 2 * WIDE, 2 * WIDE)
+    return lax.dot_general(
+        weight_ref[:, pl.ds(at, 2 * WIDE)],
+        rows[corner * groups : (corner + 1) * groups],
+        (((1,), (1,)), ((), ())),
+        preferred_element_type=F32,
+    )
+
+
+def merge_first_kernel(own, near_own, one, near_one, weight_ref, out_ref):
     groups = out_ref.shape[2]
-    for corner in range(4):
-        out_ref[corner] = lax.dot_general(
-            weight_ref[:, corner * D : corner * D + MAIN],
-            full[corner * groups : (corner + 1) * groups],
-            (((1,), (1,)), ((), ())),
-            preferred_element_type=F32,
+    rows = [collect_late(own, near_own), collect_late(one, near_one)]
+    for corner in range(4):
+        out_ref[corner] = chip_product(weight_ref, corner, groups, 0, rows[0]) + chip_product(
+            weight_ref, corner, groups, 1, rows[1]
         )
+
+
+def merge_second_kernel(two, near_two, sum_ref, weight_ref, out_ref):
+    groups = out_ref.shape[2]
+    rows = collect_late(two, near_two)
+    for corner in range(4):
+        out_ref[corner] = sum_ref[corner] + chip_product(weight_ref, corner, groups, 2, rows)
 
 
 def merge_kernel(*rest):
@@ -383,17 +403,11 @@
         notes = notes + piece[patches + groups :].astype(F32)
     scale = lax.rsqrt((notes[:4] + notes[4:8]) * (1.0 / D) + 1e-06)
     contract = (((1,), (1,)), ((), ()))
-    full = collect_late(pieces[EARLY], pieces[EARLY + 1])
+    rows = collect_late(pieces[EARLY], pieces[EARLY + 1])
     total = jnp.zeros(bias_ref.shape[:1] + (groups,), F32)
     for corner in range(4):
-        at = pl.multiple_of(corner * D + (me // 2 ^ 3) * 2 * WIDE, 2 * WIDE)
-        part = lax.dot_general(
-            weight_ref[:, pl.ds(at, 2 * WIDE)],
-            full[corner * groups : (corner + 1) * groups],
-            contract,
-            preferred_element_type=F32,
-        )
-        total = total + scale[corner : corner + 1] * (early_ref[corner] + part)
+        part = early_ref[corner] + chip_product(weight_ref, corner, groups, 3, rows)
+        total = total + scale[corner : corner + 1] * part
     spread = jnp.concatenate([jnp.broadcast_to(scale[at : at + 1], (REST, groups)) for at in range(4)], axis=0).T
     ends = ends_ref[...].astype(F32) * jnp.concatenate([spread] * ROWS, axis=1)
     total = total + lax.dot_general(tail_ref[...], ends.astype(BF16), contract, preferred_element_type=F32)
@@ -430,18 +444,17 @@
     return lax.ppermute(value, "row", [(row, row ^ step) for row in range(ROWS)])
 
 
-def turn(value, step):
-    return lax.ppermute(value, "page", [(page, (page + step) % PAGES) for page in range(PAGES)])
-
-
-def gather_rows(value, *early):
-    far = [swap(value, step) for step in (2, 4, 6)]
-    passed = [value] + far
-    for at, array in enumerate(early):
-        if array is not None:
-            passed[at] = lax.optimization_barrier((passed[at], array))[0]
-    near = [swap(piece, 1) for piece in passed]
-    return [value, far[0], far[1], near[0], near[1], near[2], far[2], near[3]]
+def turn(value, low, high):
+    pairs = [
+        (page * ROWS + row, (page + (high if row % 2 else low)) % PAGES * ROWS + row)
+        for page in range(PAGES)
+        for row in range(ROWS)
+    ]
+    return lax.ppermute(value, ("page", "row"), pairs)
+
+
+def after(value, *arrays):
+    return lax.optimization_barrier((value, *arrays))[0]
 
 
 def local_eight(qkv_rows, residual, out_weight, norm_gain, merge_weight, merge_bias, page_grid):
@@ -451,14 +464,17 @@
     units = merge_weight.shape[0]
     depth = out_weight.shape[0]
     piece = patches + groups
-
-    *sends, own, grid = kernel(
+    size = depth + depth // 4
+
+    *sends, chip, own, grid = kernel(
         spread_kernel,
         "spread",
-        [shape(band, 4 * HPAIR)] * ROWS + [shape(depth + depth // 4, WIDE), shape(8, WIDE, dtype=jnp.int32)],
+        [shape(band, 4 * HPAIR)] * ROWS
+        + [shape(2 * size, WIDE), shape(size, WIDE), shape(8, WIDE, dtype=jnp.int32)],
         [
             pltpu.VMEM((band, 3 * D), BF16),
             pltpu.VMEM((band, D), BF16),
+            pltpu.VMEM((depth, 2 * WIDE), BF16),
             pltpu.VMEM((depth, WIDE), BF16),
             pltpu.VMEM((ROWS, band, 4 * HPAIR), BF16),
             pltpu.SMEM(page_grid.shape, jnp.int32),
@@ -470,7 +486,6 @@
         moved=1 << 20,
     )(in_hbm(qkv_rows), in_hbm(residual), in_hbm(out_weight), in_hbm(page_grid))
     blocks = [sends[0]] + [swap(sends[step], step) for step in BLOCK_ORDER[1:]]
-    slices = [own] + [turn(own, step) for step in SHIFTS[1:]]
     select, dead, live = kernel(
         layout_kernel,
         "layout",
@@ -479,6 +494,9 @@
         count=1 + 3,
         moved=1 << 20,
     )(grid, *blocks[1:4])
+    across = turn(after(own, *()), 2, 2)
+    near = turn(after(chip, *()), 1, PAGES - 1)
+    swapped = swap(near, 1)
     attn = kernel(
         attend_kernel,
         "attend",
@@ -494,10 +512,10 @@
         [shape(patches, HPAIR, dtype=F32), shape(1, HPAIR, dtype=F32), shape(MAIN, HPAIR), shape(4, MAIN, HPAIR)],
         [pltpu.VMEM((patches, HPAIR), BF16), pltpu.VMEM((D,), F32), pltpu.SemaphoreType.DMA],
         fetched=(1, 2),
-        count=2 + ROWS + PAGES,
+        count=3 + ROWS + 3,
         flops=10 * patches * patches * 4096,
         moved=4 << 20,
-    )(select, in_hbm(norm_gain), attn, *blocks, *slices[:-1])
+    )(select, in_hbm(norm_gain), attn, *blocks, own, across, near)
     last = kernel(
         last_kernel,
         "ready_last",
@@ -505,8 +523,9 @@
         fetched=(1,),
         count=2,
         moved=4 << 20,
-    )(slices[-1], main)
-    pieces = gather_rows(attn, main, None, last[0])
+    )(swapped, main)
+    x, y, far = [swap(attn, step) for step in (2, 4, 6)]
+    pieces = [attn, x, y, swap(after(attn, main), 1), swap(x, 1), swap(after(y, last[0]), 1), far, swap(far, 1)]
     base = kernel(
         project_early_kernel,
         "project_early",
@@ -533,16 +552,17 @@
         count=3,
         moved=4 << 20,
     )(merge_weight, in_hbm(merge_bias), hidden)
-    pieces = gather_rows(hidden)
-    early = kernel(
-        merge_early_kernel,
-        "merge_early",
-        shape(4, units, groups, dtype=F32),
-        [pltpu.VMEM((piece + NOTES, MAIN), BF16)],
-        count=EARLY + 1,
-        flops=8 * units * groups * MAIN * 16,
-        moved=8 << 20,
-    )(*pieces[:EARLY], merge_weight)
+    sums = shape(4, units, groups, dtype=F32)
+    x, y, far = [swap(hidden, step) for step in (2, 4, 6)]
+    near_own, near_x = swap(after(hidden, ends), 1), swap(x, 1)
+    first = kernel(
+        merge_first_kernel, "merge_first", sums, count=5, flops=4 * units * groups * MAIN * 1, moved=4 << 20
+    )(hidden, near_own, x, near_x, merge_weight)
+    near_y = swap(y, 1)
+    second = kernel(
+        merge_second_kernel, "merge_second", sums, count=4, flops=2 * units * groups * MAIN * 1, moved=4 << 20
+    )(y, near_y, first, merge_weight)
+    pieces = [hidden, x, y, near_own, near_x, near_y, far, swap(far, 1)]
     return kernel(
         merge_kernel,
         "merge",
@@ -551,7 +571,7 @@
         count=ROWS + 5,
         flops=4 * units * groups * MAIN,
         moved=8 << 20,
-    )(*pieces, early, merge_weight, ends, bias, live)
+    )(*pieces, second, merge_weight, ends, bias, live)
 
 
 def solution(mesh):

time: 46.9 us -> 44.6 us (0.951)
  starting transfers between devices: 22.1 us -> 20.4 us
  Pallas kernels: 11.3 us -> 10.8 us
    ppermute x3 -> x2, waiting for transfers between devices: 0.01 us -> 2.4 us  [turn(): return lax.ppermute(value, ('page', 'row'), pairs)]
    ppermute x3 -> x2, starting transfers between devices: 6.53 us -> 4.3 us  [turn(): return lax.ppermute(value, ('page', 'row'), pairs)]
    ppermute x21 -> x22, waiting for transfers between devices: 12.9 us -> 10.7 us  [swap(): lax.ppermute(value, 'row', [(row, row ^ step) for row in range(ROWS)])]
    ppermute x21 -> x22, starting transfers between devices: 15.6 us -> 16.1 us  [swap(): lax.ppermute(value, 'row', [(row, row ^ step) for row in range(ROWS)])]
    pallas_call x1 -> x2, Pallas kernels: 1.9 us -> 1.39 us  [the longest x1 0.86 us: local_eight(): kernel(merge_first_kernel, 'merge_first', sums, count=5, flops=4 * units...]
  transfers between devices with their start and end apart: 24 -> 24, of which waited for: 9 -> 7; matrix products, arithmetic and copies ran while one was open for 0% -> 0% of each run, Pallas kernels for 16% -> 15%
where the time goes in v10:
time: 44.6 us; the launch traced here: 44.5 us
  starting transfers between devices  20.4 us (46%)
  waiting for transfers between devices  13.1 us (29%)
  Pallas kernels  10.8 us (24%)
    ppermute x22, starting transfers between devices, swap(): lax.ppermute(value, 'row', [(row, row ^ step) for row in range(ROWS)])  16.1 us
    ppermute x22, waiting for transfers between devices, swap(): lax.ppermute(value, 'row', [(row, row ^ step) for row in range(ROWS)])  10.7 us
    ppermute x2, starting transfers between devices, turn(): return lax.ppermute(value, ('page', 'row'), pairs)  4.3 us
    ppermute x2, waiting for transfers between devices, turn(): return lax.ppermute(value, ('page', 'row'), pairs)  2.4 us
    pallas_call x1, Pallas kernels, local_eight(): kernel(spread_kernel, 'spread', [shape(band, 4 * HPAIR)] * ROWS + [shape(...  1.65 us
    pallas_call x1, Pallas kernels, local_eight(): kernel(merge_kernel, 'merge', shape(1, units, groups), [pltpu.VMEM((group...  1.64 us
    pallas_call x1, Pallas kernels, local_eight(): kernel(tail_kernel, 'merge_tail', [shape(units, MAIN), shape(units, 1, dt...  1.4 us
    pallas_call x1, Pallas kernels, local_eight(): kernel(attend_kernel, 'attend', shape(piece, WIDE), [pltpu.VMEM((patches,...  1.35 us
  transfers between devices with their start and end apart: 24, of which 7 were waited for; matrix products, arithmetic and copies ran while one was open for 0% of the time, Pallas kernels for 15%

profile of v10, /device:TPU:0, one launch (start us, length us, event | category | flops | bytes accessed | tf_op | source)
XLA Modules:
  0.0 44.5 jit_solution(2143238705301354388)
XLA Ops:
  0.0 1.7 %spread.1 = (bf16[64,640]{1,0:T(8,128)(2,1)S(1)}, bf16[64,640]{1,0:T(8,128)(2,1)S(1)}, bf16[64,640]{1,0:T(8,128)(2,1)S(1)}, bf16[64,640]{1,0:T(8,128)(2,1)S(1)},...) custom-call(bf16[1,64,3840]{2,1,0:T(8,128)(2,1)} %qkv_hbm.1, ...), custom_call_target="tpu_custom_call" | custom-call | bytes 1048576 | tf_op jit(solution)/shard_map/spread/pallas_call | solution.py:469
  1.7 3.0 %collective-permute-start = (bf16[64,640]{1,0:T(8,128)(2,1)S(1)}, bf16[64,640]{1,0:T(8,128)(2,1)S(1)}, u32[]{:S(2)}, u32[]{:S(2)}) collective-permute-start(bf16[64,640]{1,0:T(8,128)(2,1)S(1)} %get-tuple-element.31), channel_id=1, source_target_pairs={{0,2},{1,3},{2,0},{3,1},{4,6},{5,7},{6,4},{7,5},{8,10},{9,11},{10,... | collective-permute-start | bytes 245768 | tf_op jit(solution)/shard_map/ppermute | solution.py:444
  4.7 1.5 %collective-permute-start.1 = (bf16[64,640]{1,0:T(8,128)(2,1)S(1)}, bf16[64,640]{1,0:T(8,128)(2,1)S(1)}, u32[]{:S(2)}, u32[]{:S(2)}) collective-permute-start(bf16[64,640]{1,0:T(8,128)(2,1)S(1)} %get-tuple-element.32), channel_id=1, source_target_pairs={{0,4},{1,5},{2,6},{3,7},{4,0},{5,1},{6,2},{7,3},{8,12},{9,13},{10,... | collective-permute-start | bytes 245768 | tf_op jit(solution)/shard_map/ppermute | solution.py:444
  6.2 1.5 %collective-permute-start.3 = (bf16[64,640]{1,0:T(8,128)(2,1)S(1)}, bf16[64,640]{1,0:T(8,128)(2,1)S(1)}, u32[]{:S(2)}, u32[]{:S(2)}) collective-permute-start(bf16[64,640]{1,0:T(8,128)(2,1)S(1)} %get-tuple-element.37), channel_id=1, source_target_pairs={{0,7},{1,6},{2,5},{3,4},{4,3},{5,2},{6,1},{7,0},{8,15},{9,14},{10,... | collective-permute-start | bytes 245768 | tf_op jit(solution)/shard_map/ppermute | solution.py:444
  7.7 1.6 %collective-permute-start.4 = (bf16[64,640]{1,0:T(8,128)(2,1)S(1)}, bf16[64,640]{1,0:T(8,128)(2,1)S(1)}, u32[]{:S(2)}, u32[]{:S(2)}) collective-permute-start(bf16[64,640]{1,0:T(8,128)(2,1)S(1)} %get-tuple-element.38), channel_id=1, source_target_pairs={{0,3},{1,2},{2,1},{3,0},{4,7},{5,6},{6,5},{7,4},{8,11},{9,10},{10,... | collective-permute-start | bytes 245768 | tf_op jit(solution)/shard_map/ppermute | solution.py:444
  9.4 0.6 %collective-permute-done.1.rest_1_.rest_2_ = bf16[64,640]{1,0:T(8,128)(2,1)S(1)} collective-permute-done((bf16[64,640]{1,0:T(8,128)(2,1)S(1)}, bf16[64,640]{1,0:T(8,128)(2,1)S(1)}, u32[]{:S(2)}, u32[]{:S(2)}) %collective-permute-start.1) | collective-permute-done | bytes 81952 | tf_op jit(solution)/shard_map/ppermute | solution.py:444
  10.0 2.3 %collective-permute-done.2.rest_2_.rest_3_ = bf16[64,640]{1,0:T(8,128)(2,1)S(1)} collective-permute-done((bf16[64,640]{1,0:T(8,128)(2,1)S(1)}, bf16[64,640]{1,0:T(8,128)(2,1)S(1)}, u32[]{:S(2)}, u32[]{:S(2)}) %collective-permute-start.2) | collective-permute-done | bytes 81952 | tf_op jit(solution)/shard_map/ppermute | solution.py:444
  12.3 1.6 %collective-permute-start.12 = (bf16[800,128]{1,0:T(8,128)(2,1)S(1)}, bf16[800,128]{1,0:T(8,128)(2,1)S(1)}, u32[]{:S(2)}, u32[]{:S(2)}) collective-permute-start(bf16[800,128]{1,0:T(8,128)(2,1)S(1)} %get-tuple-element.42), channel_id=1, source_target_pairs={{0,8},{1,25},{2,10},{3,27},{4,12},{5,29},{6,14},{7,31},{8,16},{9,1... | collective-permute-start | bytes 614408 | tf_op jit(solution)/shard_map/ppermute | solution.py:453
  14.2 2.7 %collective-permute-start.11 = (bf16[400,128]{1,0:T(8,128)(2,1)S(1)}, bf16[400,128]{1,0:T(8,128)(2,1)S(1)}, u32[]{:S(2)}, u32[]{:S(2)}) collective-permute-start(bf16[400,128]{1,0:T(8,128)(2,1)S(1)} %get-tuple-element.41.rest_8_), channel_id=1, source_target_pairs={{0,16},{1,17},{2,18},{3,19},{4,20},{5,21},{6,22},{7,23},{8,24},{9,... | collective-permute-start | bytes 307208 | tf_op jit(solution)/shard_map/ppermute | solution.py:453
  16.8 1.4 %attend.1.token_ref.rest_0_ = bf16[640,128]{1,0:T(8,128)(2,1)S(1)} custom-call(bf16[512,512]{1,0:T(8,128)(2,1)S(1)} %get-tuple-element.34.select_ref, f32[1,512]{1,0:T(1,128)S(1)} %get-tuple-element.35.dead_ref, bf16[64,640]{1,0:T(8,128)(2,1)S(1)} %get-tuple-element.36.rest_0_, bf16[64,640]{1,0:T(8,128)(2,1)S(1)} %collective-permute-done.rest_0_.rest_1_, ...), custom_call_target="tpu_custom_call" | custom-call | flops 21474836480 | bytes 1048576 | tf_op jit(solution)/shard_map/attend/pallas_call | solution.py:500
  18.3 0.6 %collective-permute-start.9 = (bf16[640,128]{1,0:T(8,128)(2,1)S(1)}, bf16[640,128]{1,0:T(8,128)(2,1)S(1)}, u32[]{:S(2)}, u32[]{:S(2)}) collective-permute-start(bf16[640,128]{1,0:T(8,128)(2,1)S(1)} %attend.1.token_ref.rest_0_), channel_id=1, source_target_pairs={{0,2},{1,3},{2,0},{3,1},{4,6},{5,7},{6,4},{7,5},{8,10},{9,11},{10,... | collective-permute-start | bytes 491528 | tf_op jit(solution)/shard_map/ppermute | solution.py:444
  18.9 2.9 %collective-permute-start.7 = (bf16[640,128]{1,0:T(8,128)(2,1)S(1)}, bf16[640,128]{1,0:T(8,128)(2,1)S(1)}, u32[]{:S(2)}, u32[]{:S(2)}) collective-permute-start(bf16[640,128]{1,0:T(8,128)(2,1)S(1)} %attend.1.token_ref.rest_0_), channel_id=1, source_target_pairs={{0,6},{1,7},{2,4},{3,5},{4,2},{5,3},{6,0},{7,1},{8,14},{9,15},{10,... | collective-permute-start | bytes 491528 | tf_op jit(solution)/shard_map/ppermute | solution.py:444
  21.8 2.4 %collective-permute-done.11.rest_9_ = bf16[400,128]{1,0:T(8,128)(2,1)S(1)} collective-permute-done((bf16[400,128]{1,0:T(8,128)(2,1)S(1)}, bf16[400,128]{1,0:T(8,128)(2,1)S(1)}, u32[]{:S(2)}, u32[]{:S(2)}) %collective-permute-start.11) | collective-permute-done | bytes 102432 | tf_op jit(solution)/shard_map/ppermute | solution.py:453
  24.2 1.2 %ready.1 = (f32[512,160]{1,0:T(8,128)S(1)}, f32[1,160]{1,0:T(1,128)S(1)}, bf16[1024,160]{1,0:T(8,128)(2,1)S(1)}, bf16[4,1024,160]{2,1,0:T(8,128)(2,1)S(1)}) custom-call(bf16[512,512]{1,0:T(8,128)(2,1)S(1)} %get-tuple-element.34.select_ref, f32[1280]{0:T(1024)} %gain_hbm.1, bf16[640,128]{1,0:T(8,128)(2,1)S(1)} %attend.1.token_ref.rest_0_, ...), custom_call_target="tpu_custom_call" | custom-call | flops 10737418240 | bytes 4194304 | tf_op jit(solution)/shard_map/ready/pallas_call | solution.py:509
  26.2 2.3 %collective-permute-done.7.rest_0_ = bf16[640,128]{1,0:T(8,128)(2,1)S(1)} collective-permute-done((bf16[640,128]{1,0:T(8,128)(2,1)S(1)}, bf16[640,128]{1,0:T(8,128)(2,1)S(1)}, u32[]{:S(2)}, u32[]{:S(2)}) %collective-permute-start.7) | collective-permute-done | bytes 163872 | tf_op jit(solution)/shard_map/ppermute | solution.py:444
  28.6 1.2 %project_early.1.rest_2_ = f32[512,160]{1,0:T(8,128)S(1)} custom-call(bf16[640,128]{1,0:T(8,128)(2,1)S(1)} %attend.1.token_ref.rest_0_, bf16[640,128]{1,0:T(8,128)(2,1)S(1)} %collective-permute-done.9.rest_1_, bf16[640,128]{1,0:T(8,128)(2,1)S(1)} %collective-permute-done.10.rest_2_, bf16[640,128]{1,0:T(8,128)(2,1)S(1)} %collective-permute-done.13.rest_3_, ...), custom_call_target="tpu_custom_call" | custom-call | flops 8589934592 | bytes 4194304 | tf_op jit(solution)/shard_map/project_early/pallas_call | solution.py:529
  29.9 0.7 %project.1.token_ref.own.rest_0_ = bf16[656,128]{1,0:T(8,128)(2,1)S(1)} custom-call(bf16[640,128]{1,0:T(8,128)(2,1)S(1)} %collective-permute-done.7.rest_0_, bf16[640,128]{1,0:T(8,128)(2,1)S(1)} %collective-permute-done.8.rest_1_, f32[512,160]{1,0:T(8,128)S(1)} %project_early.1.rest_2_, bf16[1024,160]{1,0:T(8,128)(2,1)S(1)} %get-tuple-element.43.token_ref.rest_6_.rest_3_, ...), custom_call_target="tpu_custom_call" | custom-call | flops 134217728 | bytes 4194304 | tf_op jit(solution)/shard_map/project/pallas_call | solution.py:538
  30.9 0.6 %collective-permute-start.18 = (bf16[656,128]{1,0:T(8,128)(2,1)S(1)}, bf16[656,128]{1,0:T(8,128)(2,1)S(1)}, u32[]{:S(2)}, u32[]{:S(2)}) collective-permute-start(bf16[656,128]{1,0:T(8,128)(2,1)S(1)} %project.1.token_ref.own.rest_0_), channel_id=1, source_target_pairs={{0,4},{1,5},{2,6},{3,7},{4,0},{5,1},{6,2},{7,3},{8,12},{9,13},{10,... | collective-permute-start | bytes 503816 | tf_op jit(solution)/shard_map/ppermute | solution.py:444
  31.5 2.6 %collective-permute-start.22 = (bf16[656,128]{1,0:T(8,128)(2,1)S(1)}, bf16[656,128]{1,0:T(8,128)(2,1)S(1)}, u32[]{:S(2)}, u32[]{:S(2)}) collective-permute-start(bf16[656,128]{1,0:T(8,128)(2,1)S(1)} %project.1.token_ref.own.rest_0_), channel_id=1, source_target_pairs={{0,6},{1,7},{2,4},{3,5},{4,2},{5,3},{6,0},{7,1},{8,14},{9,15},{10,... | collective-permute-start | bytes 503816 | tf_op jit(solution)/shard_map/ppermute | solution.py:444
  34.2 1.4 %merge_tail.1 = (bf16[640,1024]{1,0:T(8,128)(2,1)S(1)}, f32[640,1]{1,0:T(8,128)S(1)}) custom-call(bf16[640,5120]{1,0:T(8,128)(2,1)S(1)} %bitcast.1, f32[640]{0:T(1024)} %bias_hbm.1, bf16[656,128]{1,0:T(8,128)(2,1)S(1)} %project.1.token_ref.own.rest_0_), custom_call_target="tpu_custom_call" | custom-call | bytes 4194304 | tf_op jit(solution)/shard_map/merge_tail/pallas_call | solution.py:546
  35.6 2.1 %collective-permute-done.17.one.rest_1_ = bf16[656,128]{1,0:T(8,128)(2,1)S(1)} collective-permute-done((bf16[656,128]{1,0:T(8,128)(2,1)S(1)}, bf16[656,128]{1,0:T(8,128)(2,1)S(1)}, u32[]{:S(2)}, u32[]{:S(2)}) %collective-permute-start.17) | collective-permute-done | bytes 167968 | tf_op jit(solution)/shard_map/ppermute | solution.py:444
  37.8 3.1 %collective-permute-done.18.two.rest_2_ = bf16[656,128]{1,0:T(8,128)(2,1)S(1)} collective-permute-done((bf16[656,128]{1,0:T(8,128)(2,1)S(1)}, bf16[656,128]{1,0:T(8,128)(2,1)S(1)}, u32[]{:S(2)}, u32[]{:S(2)}) %collective-permute-start.18) | collective-permute-done | bytes 167968 | tf_op jit(solution)/shard_map/ppermute | solution.py:444
  41.4 0.9 %merge_first.1.sum_ref = f32[4,640,128]{2,1,0:T(8,128)S(1)} custom-call(bf16[656,128]{1,0:T(8,128)(2,1)S(1)} %project.1.token_ref.own.rest_0_, bf16[656,128]{1,0:T(8,128)(2,1)S(1)} %collective-permute-done.19.near_own.rest_3_, bf16[656,128]{1,0:T(8,128)(2,1)S(1)} %collective-permute-done.17.one.rest_1_, ...), custom_call_target="tpu_custom_call" | custom-call | flops 335544320 | bytes 4194304 | tf_op jit(solution)/shard_map/merge_first/pallas_call | solution.py:558
  42.8 1.6 %merge.1 = bf16[1,640,128]{2,1,0:T(8,128)(2,1)} custom-call(bf16[656,128]{1,0:T(8,128)(2,1)S(1)} %project.1.token_ref.own.rest_0_, bf16[656,128]{1,0:T(8,128)(2,1)S(1)} %collective-permute-done.17.one.rest_1_, bf16[656,128]{1,0:T(8,128)(2,1)S(1)} %collective-permute-done.18.two.rest_2_, bf16[656,128]{1,0:T(8,128)(2,1)S(1)} %collective-permute-done.19.near_own.rest_3_, ...), custom_call_target="tpu_custom_call" | custom-call | flops 335544320 | bytes 8388608 | tf_op jit(solution)/shard_map/merge/pallas_call | solution.py:566
  (40 shorter events, 2.8 us)
Async XLA Ops:
  1.7 7.7 %collective-permute-start = (bf16[64,640]{1,0:T(8,128)(2,1)S(1)}, bf16[64,640]{1,0:T(8,128)(2,1)S(1)}, u32[]{:S(2)}, u32[]{:S(2)}) collective-permute-start(bf16[64,640]{1,0:T(8,128)(2,1)S(1)} %get-tuple-element.31), channel_id=1, source_target_pairs={{0,2},{1,3},{2,0},{3,1},{4,6},{5,7},{6,4},{7,5},{8,10},{9,11},{10,... | collective-permute-start | bytes 245768 | tf_op jit(solution)/shard_map/ppermute | solution.py:444
  4.7 5.3 %collective-permute-start.1 = (bf16[64,640]{1,0:T(8,128)(2,1)S(1)}, bf16[64,640]{1,0:T(8,128)(2,1)S(1)}, u32[]{:S(2)}, u32[]{:S(2)}) collective-permute-start(bf16[64,640]{1,0:T(8,128)(2,1)S(1)} %get-tuple-element.32), channel_id=1, source_target_pairs={{0,4},{1,5},{2,6},{3,7},{4,0},{5,1},{6,2},{7,3},{8,12},{9,13},{10,... | collective-permute-start | bytes 245768 | tf_op jit(solution)/shard_map/ppermute | solution.py:444
  6.2 6.2 %collective-permute-start.2 = (bf16[64,640]{1,0:T(8,128)(2,1)S(1)}, bf16[64,640]{1,0:T(8,128)(2,1)S(1)}, u32[]{:S(2)}, u32[]{:S(2)}) collective-permute-start(bf16[64,640]{1,0:T(8,128)(2,1)S(1)} %get-tuple-element.33), channel_id=1, source_target_pairs={{0,6},{1,7},{2,4},{3,5},{4,2},{5,3},{6,0},{7,1},{8,14},{9,15},{10,... | collective-permute-start | bytes 245768 | tf_op jit(solution)/shard_map/ppermute | solution.py:444
  6.2 8.0 %collective-permute-start.3 = (bf16[64,640]{1,0:T(8,128)(2,1)S(1)}, bf16[64,640]{1,0:T(8,128)(2,1)S(1)}, u32[]{:S(2)}, u32[]{:S(2)}) collective-permute-start(bf16[64,640]{1,0:T(8,128)(2,1)S(1)} %get-tuple-element.37), channel_id=1, source_target_pairs={{0,7},{1,6},{2,5},{3,4},{4,3},{5,2},{6,1},{7,0},{8,15},{9,14},{10,... | collective-permute-start | bytes 245768 | tf_op jit(solution)/shard_map/ppermute | solution.py:444
  7.7 9.1 %collective-permute-start.4 = (bf16[64,640]{1,0:T(8,128)(2,1)S(1)}, bf16[64,640]{1,0:T(8,128)(2,1)S(1)}, u32[]{:S(2)}, u32[]{:S(2)}) collective-permute-start(bf16[64,640]{1,0:T(8,128)(2,1)S(1)} %get-tuple-element.38), channel_id=1, source_target_pairs={{0,3},{1,2},{2,1},{3,0},{4,7},{5,6},{6,5},{7,4},{8,11},{9,10},{10,... | collective-permute-start | bytes 245768 | tf_op jit(solution)/shard_map/ppermute | solution.py:444
  9.4 7.5 %collective-permute-start.5 = (bf16[64,640]{1,0:T(8,128)(2,1)S(1)}, bf16[64,640]{1,0:T(8,128)(2,1)S(1)}, u32[]{:S(2)}, u32[]{:S(2)}) collective-permute-start(bf16[64,640]{1,0:T(8,128)(2,1)S(1)} %get-tuple-element.39), channel_id=1, source_target_pairs={{0,5},{1,4},{2,7},{3,6},{4,1},{5,0},{6,3},{7,2},{8,13},{9,12},{10,... | collective-permute-start | bytes 245768 | tf_op jit(solution)/shard_map/ppermute | solution.py:444
  10.0 6.8 %collective-permute-start.6 = (bf16[64,640]{1,0:T(8,128)(2,1)S(1)}, bf16[64,640]{1,0:T(8,128)(2,1)S(1)}, u32[]{:S(2)}, u32[]{:S(2)}) collective-permute-start(bf16[64,640]{1,0:T(8,128)(2,1)S(1)} %get-tuple-element.40), channel_id=1, source_target_pairs={{0,1},{1,0},{2,3},{3,2},{4,5},{5,4},{6,7},{7,6},{8,9},{9,8},{10,11... | collective-permute-start | bytes 245768 | tf_op jit(solution)/shard_map/ppermute | solution.py:444
  12.3 9.4 %collective-permute-start.12 = (bf16[800,128]{1,0:T(8,128)(2,1)S(1)}, bf16[800,128]{1,0:T(8,128)(2,1)S(1)}, u32[]{:S(2)}, u32[]{:S(2)}) collective-permute-start(bf16[800,128]{1,0:T(8,128)(2,1)S(1)} %get-tuple-element.42), channel_id=1, source_target_pairs={{0,8},{1,25},{2,10},{3,27},{4,12},{5,29},{6,14},{7,31},{8,16},{9,1... | collective-permute-start | bytes 614408 | tf_op jit(solution)/shard_map/ppermute | solution.py:453
  14.2 10.0 %collective-permute-start.11 = (bf16[400,128]{1,0:T(8,128)(2,1)S(1)}, bf16[400,128]{1,0:T(8,128)(2,1)S(1)}, u32[]{:S(2)}, u32[]{:S(2)}) collective-permute-start(bf16[400,128]{1,0:T(8,128)(2,1)S(1)} %get-tuple-element.41.rest_8_), channel_id=1, source_target_pairs={{0,16},{1,17},{2,18},{3,19},{4,20},{5,21},{6,22},{7,23},{8,24},{9,... | collective-permute-start | bytes 307208 | tf_op jit(solution)/shard_map/ppermute | solution.py:453
  18.2 7.9 %collective-permute-start.10 = (bf16[640,128]{1,0:T(8,128)(2,1)S(1)}, bf16[640,128]{1,0:T(8,128)(2,1)S(1)}, u32[]{:S(2)}, u32[]{:S(2)}) collective-permute-start(bf16[640,128]{1,0:T(8,128)(2,1)S(1)} %attend.1.token_ref.rest_0_), channel_id=1, source_target_pairs={{0,4},{1,5},{2,6},{3,7},{4,0},{5,1},{6,2},{7,3},{8,12},{9,13},{10,... | collective-permute-start | bytes 491528 | tf_op jit(solution)/shard_map/ppermute | solution.py:444
  18.3 7.2 %collective-permute-start.9 = (bf16[640,128]{1,0:T(8,128)(2,1)S(1)}, bf16[640,128]{1,0:T(8,128)(2,1)S(1)}, u32[]{:S(2)}, u32[]{:S(2)}) collective-permute-start(bf16[640,128]{1,0:T(8,128)(2,1)S(1)} %attend.1.token_ref.rest_0_), channel_id=1, source_target_pairs={{0,2},{1,3},{2,0},{3,1},{4,6},{5,7},{6,4},{7,5},{8,10},{9,11},{10,... | collective-permute-start | bytes 491528 | tf_op jit(solution)/shard_map/ppermute | solution.py:444
  18.9 9.6 %collective-permute-start.7 = (bf16[640,128]{1,0:T(8,128)(2,1)S(1)}, bf16[640,128]{1,0:T(8,128)(2,1)S(1)}, u32[]{:S(2)}, u32[]{:S(2)}) collective-permute-start(bf16[640,128]{1,0:T(8,128)(2,1)S(1)} %attend.1.token_ref.rest_0_), channel_id=1, source_target_pairs={{0,6},{1,7},{2,4},{3,5},{4,2},{5,3},{6,0},{7,1},{8,14},{9,15},{10,... | collective-permute-start | bytes 491528 | tf_op jit(solution)/shard_map/ppermute | solution.py:444
  21.7 4.2 %collective-permute-start.15 = (bf16[800,128]{1,0:T(8,128)(2,1)S(1)}, bf16[800,128]{1,0:T(8,128)(2,1)S(1)}, u32[]{:S(2)}, u32[]{:S(2)}) collective-permute-start(bf16[800,128]{1,0:T(8,128)(2,1)S(1)} %collective-permute-done.12.rest_10_), channel_id=1, source_target_pairs={{0,1},{1,0},{2,3},{3,2},{4,5},{5,4},{6,7},{7,6},{8,9},{9,8},{10,11... | collective-permute-start | bytes 614408 | tf_op jit(solution)/shard_map/ppermute | solution.py:444
  25.4 3.2 %collective-permute-start.13 = (bf16[640,128]{1,0:T(8,128)(2,1)S(1)}, bf16[640,128]{1,0:T(8,128)(2,1)S(1)}, u32[]{:S(2)}, u32[]{:S(2)}) collective-permute-start(bf16[640,128]{1,0:T(8,128)(2,1)S(1)} %attend.1.token_ref.rest_0_), channel_id=1, source_target_pairs={{0,1},{1,0},{2,3},{3,2},{4,5},{5,4},{6,7},{7,6},{8,9},{9,8},{10,11... | collective-permute-start | bytes 491528 | tf_op jit(solution)/shard_map/ppermute | solution.py:444
  25.5 3.1 %collective-permute-start.14 = (bf16[640,128]{1,0:T(8,128)(2,1)S(1)}, bf16[640,128]{1,0:T(8,128)(2,1)S(1)}, u32[]{:S(2)}, u32[]{:S(2)}) collective-permute-start(bf16[640,128]{1,0:T(8,128)(2,1)S(1)} %collective-permute-done.9.rest_1_), channel_id=1, source_target_pairs={{0,1},{1,0},{2,3},{3,2},{4,5},{5,4},{6,7},{7,6},{8,9},{9,8},{10,11... | collective-permute-start | bytes 491528 | tf_op jit(solution)/shard_map/ppermute | solution.py:444
  26.1 2.5 %collective-permute-start.16 = (bf16[640,128]{1,0:T(8,128)(2,1)S(1)}, bf16[640,128]{1,0:T(8,128)(2,1)S(1)}, u32[]{:S(2)}, u32[]{:S(2)}) collective-permute-start(bf16[640,128]{1,0:T(8,128)(2,1)S(1)} %collective-permute-done.10.rest_2_), channel_id=1, source_target_pairs={{0,1},{1,0},{2,3},{3,2},{4,5},{5,4},{6,7},{7,6},{8,9},{9,8},{10,11... | collective-permute-start | bytes 491528 | tf_op jit(solution)/shard_map/ppermute | solution.py:444
  28.5 1.4 %collective-permute-start.8 = (bf16[640,128]{1,0:T(8,128)(2,1)S(1)}, bf16[640,128]{1,0:T(8,128)(2,1)S(1)}, u32[]{:S(2)}, u32[]{:S(2)}) collective-permute-start(bf16[640,128]{1,0:T(8,128)(2,1)S(1)} %collective-permute-done.7.rest_0_), channel_id=1, source_target_pairs={{0,1},{1,0},{2,3},{3,2},{4,5},{5,4},{6,7},{7,6},{8,9},{9,8},{10,11... | collective-permute-start | bytes 491528 | tf_op jit(solution)/shard_map/ppermute | solution.py:444
  30.6 7.2 %collective-permute-start.17 = (bf16[656,128]{1,0:T(8,128)(2,1)S(1)}, bf16[656,128]{1,0:T(8,128)(2,1)S(1)}, u32[]{:S(2)}, u32[]{:S(2)}) collective-permute-start(bf16[656,128]{1,0:T(8,128)(2,1)S(1)} %project.1.token_ref.own.rest_0_), channel_id=1, source_target_pairs={{0,2},{1,3},{2,0},{3,1},{4,6},{5,7},{6,4},{7,5},{8,10},{9,11},{10,... | collective-permute-start | bytes 503816 | tf_op jit(solution)/shard_map/ppermute | solution.py:444
  30.9 9.9 %collective-permute-start.18 = (bf16[656,128]{1,0:T(8,128)(2,1)S(1)}, bf16[656,128]{1,0:T(8,128)(2,1)S(1)}, u32[]{:S(2)}, u32[]{:S(2)}) collective-permute-start(bf16[656,128]{1,0:T(8,128)(2,1)S(1)} %project.1.token_ref.own.rest_0_), channel_id=1, source_target_pairs={{0,4},{1,5},{2,6},{3,7},{4,0},{5,1},{6,2},{7,3},{8,12},{9,13},{10,... | collective-permute-start | bytes 503816 | tf_op jit(solution)/shard_map/ppermute | solution.py:444
  31.5 9.4 %collective-permute-start.22 = (bf16[656,128]{1,0:T(8,128)(2,1)S(1)}, bf16[656,128]{1,0:T(8,128)(2,1)S(1)}, u32[]{:S(2)}, u32[]{:S(2)}) collective-permute-start(bf16[656,128]{1,0:T(8,128)(2,1)S(1)} %project.1.token_ref.own.rest_0_), channel_id=1, source_target_pairs={{0,6},{1,7},{2,4},{3,5},{4,2},{5,3},{6,0},{7,1},{8,14},{9,15},{10,... | collective-permute-start | bytes 503816 | tf_op jit(solution)/shard_map/ppermute | solution.py:444
  35.6 5.8 %collective-permute-start.19 = (bf16[656,128]{1,0:T(8,128)(2,1)S(1)}, bf16[656,128]{1,0:T(8,128)(2,1)S(1)}, u32[]{:S(2)}, u32[]{:S(2)}) collective-permute-start(bf16[656,128]{1,0:T(8,128)(2,1)S(1)} %project.1.token_ref.own.rest_0_), channel_id=1, source_target_pairs={{0,1},{1,0},{2,3},{3,2},{4,5},{5,4},{6,7},{7,6},{8,9},{9,8},{10,11... | collective-permute-start | bytes 503816 | tf_op jit(solution)/shard_map/ppermute | solution.py:444
  37.8 3.6 %collective-permute-start.20 = (bf16[656,128]{1,0:T(8,128)(2,1)S(1)}, bf16[656,128]{1,0:T(8,128)(2,1)S(1)}, u32[]{:S(2)}, u32[]{:S(2)}) collective-permute-start(bf16[656,128]{1,0:T(8,128)(2,1)S(1)} %collective-permute-done.17.one.rest_1_), channel_id=1, source_target_pairs={{0,1},{1,0},{2,3},{3,2},{4,5},{5,4},{6,7},{7,6},{8,9},{9,8},{10,11... | collective-permute-start | bytes 503816 | tf_op jit(solution)/shard_map/ppermute | solution.py:444
  40.9 1.4 %collective-permute-start.21 = (bf16[656,128]{1,0:T(8,128)(2,1)S(1)}, bf16[656,128]{1,0:T(8,128)(2,1)S(1)}, u32[]{:S(2)}, u32[]{:S(2)}) collective-permute-start(bf16[656,128]{1,0:T(8,128)(2,1)S(1)} %collective-permute-done.18.two.rest_2_), channel_id=1, source_target_pairs={{0,1},{1,0},{2,3},{3,2},{4,5},{5,4},{6,7},{7,6},{8,9},{9,8},{10,11... | collective-permute-start | bytes 503816 | tf_op jit(solution)/shard_map/ppermute | solution.py:444
  40.9 1.9 %collective-permute-start.23 = (bf16[656,128]{1,0:T(8,128)(2,1)S(1)}, bf16[656,128]{1,0:T(8,128)(2,1)S(1)}, u32[]{:S(2)}, u32[]{:S(2)}) collective-permute-start(bf16[656,128]{1,0:T(8,128)(2,1)S(1)} %collective-permute-done.22.rest_6_), channel_id=1, source_target_pairs={{0,1},{1,0},{2,3},{3,2},{4,5},{5,4},{6,7},{7,6},{8,9},{9,8},{10,11... | collective-permute-start | bytes 503816 | tf_op jit(solution)/shard_map/ppermute | solution.py:444
  (2 other events, 11.2 us)

commit v11 on v10

--- a/solution.py
+++ b/solution.py
@@ -122,7 +122,7 @@
 REST = HPAIR - WIDE
 MAIN = ROWS * WIDE
 NOTES = 16
-BLOCK_ORDER = (0, 2, 4, 6, 7, 3, 5, 1)
+BLOCK_ORDER = (0, 4, 2, 6, 7, 3, 5, 1)
 PIECE_ORDER = (0, 2, 4, 1, 3, 5, 6, 7)
 EARLY = 6
 ROOT = math.log2(math.e) / math.sqrt(HDIM)
@@ -365,53 +365,45 @@
     bias_out[...] = jnp.broadcast_to(line[...].reshape(1, units), (8, units)).T[:, :1]
 
 
-def chip_product(weight_ref, corner, groups, other, rows):
-    at = pl.multiple_of(corner * D + (row_index() // 2 ^ other) * 2 * WIDE, 2 * WIDE)
-    return lax.dot_general(
-        weight_ref[:, pl.ds(at, 2 * WIDE)],
-        rows[corner * groups : (corner + 1) * groups],
-        (((1,), (1,)), ((), ())),
-        preferred_element_type=F32,
-    )
-
-
-def merge_first_kernel(own, near_own, one, near_one, weight_ref, out_ref):
-    groups = out_ref.shape[2]
-    rows = [collect_late(own, near_own), collect_late(one, near_one)]
+def add_pieces(sum_ref, before, weight_ref, tail_ref, pieces):
+    groups = sum_ref.shape[2]
+    patches = 4 * groups
+    me = row_index()
+    rows = jnp.concatenate([piece[: patches + groups] for _, piece in pieces], axis=1)
+    spots = [pl.multiple_of((me ^ step) * WIDE, WIDE) for step, _ in pieces]
+    ends = rows[patches:]
+    tails = jnp.concatenate([tail_ref[:, pl.ds(spot, WIDE)] for spot in spots], axis=1)
+    lane = lax.rem(lax.broadcasted_iota(jnp.int32, (1, rows.shape[1]), 1), WIDE)
+    contract = (((1,), (1,)), ((), ()))
     for corner in range(4):
-        out_ref[corner] = chip_product(weight_ref, corner, groups, 0, rows[0]) + chip_product(
-            weight_ref, corner, groups, 1, rows[1]
+        columns = [weight_ref[:, pl.ds(pl.multiple_of(corner * D + spot, WIDE), WIDE)] for spot in spots]
+        part = lax.dot_general(
+            jnp.concatenate(columns, axis=1),
+            rows[corner * groups : (corner + 1) * groups],
+            contract,
+            preferred_element_type=F32,
         )
-
-
-def merge_second_kernel(two, near_two, sum_ref, weight_ref, out_ref):
-    groups = out_ref.shape[2]
-    rows = collect_late(two, near_two)
+        mine = jnp.where(lane // REST == corner, ends, jnp.zeros_like(ends))
+        part = part + lax.dot_general(tails, mine, contract, preferred_element_type=F32)
+        sum_ref[corner] = part if before is None else before[corner] + part
+    return sum(piece[patches + groups :].astype(F32) for _, piece in pieces)
+
+
+def merge_first_kernel(own, y, x, weight_ref, tail_ref, sum_ref, notes_ref):
+    notes_ref[...] = add_pieces(sum_ref, None, weight_ref, tail_ref, [(0, own), (4, y), (2, x)])
+
+
+def merge_second_kernel(own, y, x, before_ref, notes_before_ref, weight_ref, tail_ref, sum_ref, notes_ref):
+    pieces = [(1, own), (5, y), (3, x)]
+    notes_ref[...] = notes_before_ref[...] + add_pieces(sum_ref, before_ref, weight_ref, tail_ref, pieces)
+
+
+def merge_kernel(far, near_far, before_ref, notes_ref, weight_ref, tail_ref, bias_ref, live_ref, out_ref, sum_ref):
+    notes = notes_ref[...] + add_pieces(sum_ref, before_ref, weight_ref, tail_ref, [(6, far), (7, near_far)])
+    scale = lax.rsqrt((notes[:4] + notes[4:8]) * (1.0 / D) + 1e-06)
+    total = bias_ref[...]
     for corner in range(4):
-        out_ref[corner] = sum_ref[corner] + chip_product(weight_ref, corner, groups, 2, rows)
-
-
-def merge_kernel(*rest):
-    pieces = rest[:ROWS]
-    early_ref, weight_ref, tail_ref, bias_ref, live_ref, out_ref, ends_ref = rest[ROWS:]
-    me = row_index()
-    groups = live_ref.shape[1]
-    patches = 4 * groups
-    notes = jnp.zeros((NOTES, groups), F32)
-    for step, piece in zip(PIECE_ORDER, pieces):
-        ends_ref[:, pl.ds(pl.multiple_of((me ^ step) * WIDE, WIDE), WIDE)] = piece[patches : patches + groups]
-        notes = notes + piece[patches + groups :].astype(F32)
-    scale = lax.rsqrt((notes[:4] + notes[4:8]) * (1.0 / D) + 1e-06)
-    contract = (((1,), (1,)), ((), ()))
-    rows = collect_late(pieces[EARLY], pieces[EARLY + 1])
-    total = jnp.zeros(bias_ref.shape[:1] + (groups,), F32)
-    for corner in range(4):
-        part = early_ref[corner] + chip_product(weight_ref, corner, groups, 3, rows)
-        total = total + scale[corner : corner + 1] * part
-    spread = jnp.concatenate([jnp.broadcast_to(scale[at : at + 1], (REST, groups)) for at in range(4)], axis=0).T
-    ends = ends_ref[...].astype(F32) * jnp.concatenate([spread] * ROWS, axis=1)
-    total = total + lax.dot_general(tail_ref[...], ends.astype(BF16), contract, preferred_element_type=F32)
-    total = total + bias_ref[...]
+        total = total + scale[corner : corner + 1] * sum_ref[corner]
     merged = 0.5 * total * (1.0 + lax.erf(total * math.sqrt(0.5)))
     out_ref[0] = jnp.where(live_ref[...] > 0.0, merged, 0.0).astype(BF16)
 
@@ -552,26 +544,24 @@
         count=3,
         moved=4 << 20,
     )(merge_weight, in_hbm(merge_bias), hidden)
-    sums = shape(4, units, groups, dtype=F32)
-    x, y, far = [swap(hidden, step) for step in (2, 4, 6)]
-    near_own, near_x = swap(after(hidden, ends), 1), swap(x, 1)
-    first = kernel(
-        merge_first_kernel, "merge_first", sums, count=5, flops=4 * units * groups * MAIN * 1, moved=4 << 20
-    )(hidden, near_own, x, near_x, merge_weight)
-    near_y = swap(y, 1)
-    second = kernel(
-        merge_second_kernel, "merge_second", sums, count=4, flops=2 * units * groups * MAIN * 1, moved=4 << 20
-    )(y, near_y, first, merge_weight)
-    pieces = [hidden, x, y, near_own, near_x, near_y, far, swap(far, 1)]
+    sums = [shape(4, units, groups, dtype=F32), shape(NOTES, groups, dtype=F32)]
+    y, x, far = [swap(hidden, step) for step in (4, 2, 6)]
+    first = kernel(merge_first_kernel, "merge_first", sums, count=5, flops=1, moved=1)(
+        hidden, y, x, merge_weight, ends
+    )
+    near = [swap(after(hidden, ends), 1), swap(y, 1), swap(x, 1)]
+    second = kernel(merge_second_kernel, "merge_second", sums, count=7, flops=1, moved=1)(
+        *near, *first, merge_weight, ends
+    )
     return kernel(
         merge_kernel,
         "merge",
         shape(1, units, groups),
-        [pltpu.VMEM((groups, MAIN), BF16)],
-        count=ROWS + 5,
+        [pltpu.VMEM((4, units, groups), F32)],
+        count=8,
         flops=4 * units * groups * MAIN,
         moved=8 << 20,
-    )(*pieces, second, merge_weight, ends, bias, live)
+    )(far, swap(after(far, first[0]), 1), *second, merge_weight, ends, bias, live)
 
 
 def solution(mesh):

time: 44.6 us -> 45.2 us (1.013)
  Pallas kernels: 10.8 us -> 11.8 us
  starting transfers between devices: 20.4 us -> 19.9 us
    pallas_call x3, Pallas kernels: 3.02 us -> 4.07 us  [the longest x1 1.59 us: local_eight(): kernel(merge_kernel, 'merge', shape(1, units, groups), [pltpu.VMEM((4, un...]
    ppermute x22, starting transfers between devices: 16.1 us -> 15.6 us  [swap(): lax.ppermute(value, 'row', [(row, row ^ step) for row in range(ROWS)])]
  transfers between devices with their start and end apart: 24 -> 24, of which waited for: 7 -> 10; matrix products, arithmetic and copies ran while one was open for 0% -> 0% of each run, Pallas kernels for 15% -> 18%
where the time goes in v11:
time: 45.2 us; the launch traced here: 45 us
  starting transfers between devices  19.9 us (44%)
  waiting for transfers between devices  13 us (29%)
  Pallas kernels  11.8 us (26%)
    ppermute x22, starting transfers between devices, swap(): lax.ppermute(value, 'row', [(row, row ^ step) for row in range(ROWS)])  15.6 us
    ppermute x22, waiting for transfers between devices, swap(): lax.ppermute(value, 'row', [(row, row ^ step) for row in range(ROWS)])  10.8 us
    ppermute x2, starting transfers between devices, turn(): return lax.ppermute(value, ('page', 'row'), pairs)  4.3 us
    ppermute x2, waiting for transfers between devices, turn(): return lax.ppermute(value, ('page', 'row'), pairs)  2.26 us
    pallas_call x1, Pallas kernels, local_eight(): kernel(spread_kernel, 'spread', [shape(band, 4 * HPAIR)] * ROWS + [shape(...  1.65 us
    pallas_call x1, Pallas kernels, local_eight(): kernel(merge_kernel, 'merge', shape(1, units, groups), [pltpu.VMEM((4, un...  1.59 us
    pallas_call x1, Pallas kernels, local_eight(): kernel(tail_kernel, 'merge_tail', [shape(units, MAIN), shape(units, 1, dt...  1.39 us
    pallas_call x1, Pallas kernels, local_eight(): kernel(attend_kernel, 'attend', shape(piece, WIDE), [pltpu.VMEM((patches,...  1.35 us
  transfers between devices with their start and end apart: 24, of which 10 were waited for; matrix products, arithmetic and copies ran while one was open for 0% of the time, Pallas kernels for 18%

profile of v11, /device:TPU:0, one launch (start us, length us, event | category | flops | bytes accessed | tf_op | source)
XLA Modules:
  0.0 45.0 jit_solution(12949505514541947295)
XLA Ops:
  0.0 1.7 %spread.1 = (bf16[64,640]{1,0:T(8,128)(2,1)S(1)}, bf16[64,640]{1,0:T(8,128)(2,1)S(1)}, bf16[64,640]{1,0:T(8,128)(2,1)S(1)}, bf16[64,640]{1,0:T(8,128)(2,1)S(1)},...) custom-call(bf16[1,64,3840]{2,1,0:T(8,128)(2,1)} %qkv_hbm.1, ...), custom_call_target="tpu_custom_call" | custom-call | bytes 1048576 | tf_op jit(solution)/shard_map/spread/pallas_call | solution.py:461
  1.7 3.0 %collective-permute-start = (bf16[64,640]{1,0:T(8,128)(2,1)S(1)}, bf16[64,640]{1,0:T(8,128)(2,1)S(1)}, u32[]{:S(2)}, u32[]{:S(2)}) collective-permute-start(bf16[64,640]{1,0:T(8,128)(2,1)S(1)} %get-tuple-element.36), channel_id=1, source_target_pairs={{0,4},{1,5},{2,6},{3,7},{4,0},{5,1},{6,2},{7,3},{8,12},{9,13},{10,... | collective-permute-start | bytes 245768 | tf_op jit(solution)/shard_map/ppermute | solution.py:436
  4.7 1.5 %collective-permute-start.1 = (bf16[64,640]{1,0:T(8,128)(2,1)S(1)}, bf16[64,640]{1,0:T(8,128)(2,1)S(1)}, u32[]{:S(2)}, u32[]{:S(2)}) collective-permute-start(bf16[64,640]{1,0:T(8,128)(2,1)S(1)} %get-tuple-element.37), channel_id=1, source_target_pairs={{0,2},{1,3},{2,0},{3,1},{4,6},{5,7},{6,4},{7,5},{8,10},{9,11},{10,... | collective-permute-start | bytes 245768 | tf_op jit(solution)/shard_map/ppermute | solution.py:436
  6.2 1.5 %collective-permute-start.3 = (bf16[64,640]{1,0:T(8,128)(2,1)S(1)}, bf16[64,640]{1,0:T(8,128)(2,1)S(1)}, u32[]{:S(2)}, u32[]{:S(2)}) collective-permute-start(bf16[64,640]{1,0:T(8,128)(2,1)S(1)} %get-tuple-element.42), channel_id=1, source_target_pairs={{0,7},{1,6},{2,5},{3,4},{4,3},{5,2},{6,1},{7,0},{8,15},{9,14},{10,... | collective-permute-start | bytes 245768 | tf_op jit(solution)/shard_map/ppermute | solution.py:436
  7.7 1.6 %collective-permute-start.4 = (bf16[64,640]{1,0:T(8,128)(2,1)S(1)}, bf16[64,640]{1,0:T(8,128)(2,1)S(1)}, u32[]{:S(2)}, u32[]{:S(2)}) collective-permute-start(bf16[64,640]{1,0:T(8,128)(2,1)S(1)} %get-tuple-element.43), channel_id=1, source_target_pairs={{0,3},{1,2},{2,1},{3,0},{4,7},{5,6},{6,5},{7,4},{8,11},{9,10},{10,... | collective-permute-start | bytes 245768 | tf_op jit(solution)/shard_map/ppermute | solution.py:436
  9.8 2.6 %collective-permute-done.2.rest_2_.rest_3_ = bf16[64,640]{1,0:T(8,128)(2,1)S(1)} collective-permute-done((bf16[64,640]{1,0:T(8,128)(2,1)S(1)}, bf16[64,640]{1,0:T(8,128)(2,1)S(1)}, u32[]{:S(2)}, u32[]{:S(2)}) %collective-permute-start.2) | collective-permute-done | bytes 81952 | tf_op jit(solution)/shard_map/ppermute | solution.py:436
  12.3 1.7 %collective-permute-start.12 = (bf16[800,128]{1,0:T(8,128)(2,1)S(1)}, bf16[800,128]{1,0:T(8,128)(2,1)S(1)}, u32[]{:S(2)}, u32[]{:S(2)}) collective-permute-start(bf16[800,128]{1,0:T(8,128)(2,1)S(1)} %get-tuple-element.47), channel_id=1, source_target_pairs={{0,8},{1,25},{2,10},{3,27},{4,12},{5,29},{6,14},{7,31},{8,16},{9,1... | collective-permute-start | bytes 614408 | tf_op jit(solution)/shard_map/ppermute | solution.py:445
  14.2 2.7 %collective-permute-start.11 = (bf16[400,128]{1,0:T(8,128)(2,1)S(1)}, bf16[400,128]{1,0:T(8,128)(2,1)S(1)}, u32[]{:S(2)}, u32[]{:S(2)}) collective-permute-start(bf16[400,128]{1,0:T(8,128)(2,1)S(1)} %get-tuple-element.46.rest_8_), channel_id=1, source_target_pairs={{0,16},{1,17},{2,18},{3,19},{4,20},{5,21},{6,22},{7,23},{8,24},{9,... | collective-permute-start | bytes 307208 | tf_op jit(solution)/shard_map/ppermute | solution.py:445
  16.8 1.4 %attend.1.token_ref.rest_0_ = bf16[640,128]{1,0:T(8,128)(2,1)S(1)} custom-call(bf16[512,512]{1,0:T(8,128)(2,1)S(1)} %get-tuple-element.39.select_ref, f32[1,512]{1,0:T(1,128)S(1)} %get-tuple-element.40.dead_ref, bf16[64,640]{1,0:T(8,128)(2,1)S(1)} %get-tuple-element.41.rest_0_, bf16[64,640]{1,0:T(8,128)(2,1)S(1)} %collective-permute-done.rest_0_.rest_1_, ...), custom_call_target="tpu_custom_call" | custom-call | flops 21474836480 | bytes 1048576 | tf_op jit(solution)/shard_map/attend/pallas_call | solution.py:492
  18.3 1.1 %collective-permute-start.9 = (bf16[640,128]{1,0:T(8,128)(2,1)S(1)}, bf16[640,128]{1,0:T(8,128)(2,1)S(1)}, u32[]{:S(2)}, u32[]{:S(2)}) collective-permute-start(bf16[640,128]{1,0:T(8,128)(2,1)S(1)} %attend.1.token_ref.rest_0_), channel_id=1, source_target_pairs={{0,2},{1,3},{2,0},{3,1},{4,6},{5,7},{6,4},{7,5},{8,10},{9,11},{10,... | collective-permute-start | bytes 491528 | tf_op jit(solution)/shard_map/ppermute | solution.py:436
  19.4 2.3 %collective-permute-start.7 = (bf16[640,128]{1,0:T(8,128)(2,1)S(1)}, bf16[640,128]{1,0:T(8,128)(2,1)S(1)}, u32[]{:S(2)}, u32[]{:S(2)}) collective-permute-start(bf16[640,128]{1,0:T(8,128)(2,1)S(1)} %attend.1.token_ref.rest_0_), channel_id=1, source_target_pairs={{0,6},{1,7},{2,4},{3,5},{4,2},{5,3},{6,0},{7,1},{8,14},{9,15},{10,... | collective-permute-start | bytes 491528 | tf_op jit(solution)/shard_map/ppermute | solution.py:436
  21.8 2.3 %collective-permute-done.11.rest_9_ = bf16[400,128]{1,0:T(8,128)(2,1)S(1)} collective-permute-done((bf16[400,128]{1,0:T(8,128)(2,1)S(1)}, bf16[400,128]{1,0:T(8,128)(2,1)S(1)}, u32[]{:S(2)}, u32[]{:S(2)}) %collective-permute-start.11) | collective-permute-done | bytes 102432 | tf_op jit(solution)/shard_map/ppermute | solution.py:445
  24.0 1.2 %ready.1 = (f32[512,160]{1,0:T(8,128)S(1)}, f32[1,160]{1,0:T(1,128)S(1)}, bf16[1024,160]{1,0:T(8,128)(2,1)S(1)}, bf16[4,1024,160]{2,1,0:T(8,128)(2,1)S(1)}) custom-call(bf16[512,512]{1,0:T(8,128)(2,1)S(1)} %get-tuple-element.39.select_ref, f32[1280]{0:T(1024)} %gain_hbm.1, bf16[640,128]{1,0:T(8,128)(2,1)S(1)} %attend.1.token_ref.rest_0_, ...), custom_call_target="tpu_custom_call" | custom-call | flops 10737418240 | bytes 4194304 | tf_op jit(solution)/shard_map/ready/pallas_call | solution.py:501
  26.2 2.4 %collective-permute-done.7.rest_0_ = bf16[640,128]{1,0:T(8,128)(2,1)S(1)} collective-permute-done((bf16[640,128]{1,0:T(8,128)(2,1)S(1)}, bf16[640,128]{1,0:T(8,128)(2,1)S(1)}, u32[]{:S(2)}, u32[]{:S(2)}) %collective-permute-start.7) | collective-permute-done | bytes 163872 | tf_op jit(solution)/shard_map/ppermute | solution.py:436
  28.6 1.2 %project_early.1.rest_2_ = f32[512,160]{1,0:T(8,128)S(1)} custom-call(bf16[640,128]{1,0:T(8,128)(2,1)S(1)} %attend.1.token_ref.rest_0_, bf16[640,128]{1,0:T(8,128)(2,1)S(1)} %collective-permute-done.9.rest_1_, bf16[640,128]{1,0:T(8,128)(2,1)S(1)} %collective-permute-done.10.rest_2_, bf16[640,128]{1,0:T(8,128)(2,1)S(1)} %collective-permute-done.13.rest_3_, ...), custom_call_target="tpu_custom_call" | custom-call | flops 8589934592 | bytes 4194304 | tf_op jit(solution)/shard_map/project_early/pallas_call | solution.py:521
  31.0 0.8 %collective-permute-start.19 = (bf16[656,128]{1,0:T(8,128)(2,1)S(1)}, bf16[656,128]{1,0:T(8,128)(2,1)S(1)}, u32[]{:S(2)}, u32[]{:S(2)}) collective-permute-start(bf16[656,128]{1,0:T(8,128)(2,1)S(1)} %project.1.token_ref.own), channel_id=1, source_target_pairs={{0,2},{1,3},{2,0},{3,1},{4,6},{5,7},{6,4},{7,5},{8,10},{9,11},{10,... | collective-permute-start | bytes 503816 | tf_op jit(solution)/shard_map/ppermute | solution.py:436
  31.8 2.3 %collective-permute-start.17 = (bf16[656,128]{1,0:T(8,128)(2,1)S(1)}, bf16[656,128]{1,0:T(8,128)(2,1)S(1)}, u32[]{:S(2)}, u32[]{:S(2)}) collective-permute-start(bf16[656,128]{1,0:T(8,128)(2,1)S(1)} %project.1.token_ref.own), channel_id=1, source_target_pairs={{0,6},{1,7},{2,4},{3,5},{4,2},{5,3},{6,0},{7,1},{8,14},{9,15},{10,... | collective-permute-start | bytes 503816 | tf_op jit(solution)/shard_map/ppermute | solution.py:436
  34.1 1.4 %merge_tail.1 = (bf16[640,1024]{1,0:T(8,128)(2,1)S(1)}, f32[640,1]{1,0:T(8,128)S(1)}) custom-call(bf16[640,5120]{1,0:T(8,128)(2,1)S(1)} %bitcast.1, f32[640]{0:T(1024)} %bias_hbm.1, bf16[656,128]{1,0:T(8,128)(2,1)S(1)} %project.1.token_ref.own), custom_call_target="tpu_custom_call" | custom-call | bytes 4194304 | tf_op jit(solution)/shard_map/merge_tail/pallas_call | solution.py:538
  35.6 1.6 %collective-permute-done.18.y = bf16[656,128]{1,0:T(8,128)(2,1)S(1)} collective-permute-done((bf16[656,128]{1,0:T(8,128)(2,1)S(1)}, bf16[656,128]{1,0:T(8,128)(2,1)S(1)}, u32[]{:S(2)}, u32[]{:S(2)}) %collective-permute-start.18) | collective-permute-done | bytes 167968 | tf_op jit(solution)/shard_map/ppermute | solution.py:436
  37.2 0.9 %collective-permute-done.19.x = bf16[656,128]{1,0:T(8,128)(2,1)S(1)} collective-permute-done((bf16[656,128]{1,0:T(8,128)(2,1)S(1)}, bf16[656,128]{1,0:T(8,128)(2,1)S(1)}, u32[]{:S(2)}, u32[]{:S(2)}) %collective-permute-start.19) | collective-permute-done | bytes 167968 | tf_op jit(solution)/shard_map/ppermute | solution.py:436
  38.2 1.2 %merge_first.1 = (f32[4,640,128]{2,1,0:T(8,128)S(1)}, f32[16,128]{1,0:T(8,128)S(1)}) custom-call(bf16[656,128]{1,0:T(8,128)(2,1)S(1)} %project.1.token_ref.own, bf16[656,128]{1,0:T(8,128)(2,1)S(1)} %collective-permute-done.18.y, bf16[656,128]{1,0:T(8,128)(2,1)S(1)} %collective-permute-done.19.x, bf16[640,5120]{1,0:T(8,128)(2,1)S(1)} %bitcast.1, ...), custom_call_target="tpu_custom_call" | custom-call | flops 1 | bytes 1 | tf_op jit(solution)/shard_map/merge_first/pallas_call | solution.py:549
  39.5 2.5 %collective-permute-done.17.far = bf16[656,128]{1,0:T(8,128)(2,1)S(1)} collective-permute-done((bf16[656,128]{1,0:T(8,128)(2,1)S(1)}, bf16[656,128]{1,0:T(8,128)(2,1)S(1)}, u32[]{:S(2)}, u32[]{:S(2)}) %collective-permute-start.17) | collective-permute-done | bytes 167968 | tf_op jit(solution)/shard_map/ppermute | solution.py:436
  42.0 1.3 %merge_second.1 = (f32[4,640,128]{2,1,0:T(8,128)S(1)}, f32[16,128]{1,0:T(8,128)S(1)}) custom-call(bf16[656,128]{1,0:T(8,128)(2,1)S(1)} %collective-permute-done.21.own, bf16[656,128]{1,0:T(8,128)(2,1)S(1)} %collective-permute-done.22.y, bf16[656,128]{1,0:T(8,128)(2,1)S(1)} %collective-permute-done.23.x, f32[4,640,128]{2,1,0:T(8,128)S(1)} %get-tuple-element.57.before_ref, ...), custom_call_target="tpu_custom_call" | custom-call | flops 1 | bytes 1 | tf_op jit(solution)/shard_map/merge_second/pallas_call | solution.py:553
  43.4 1.6 %merge.1 = bf16[1,640,128]{2,1,0:T(8,128)(2,1)} custom-call(bf16[656,128]{1,0:T(8,128)(2,1)S(1)} %collective-permute-done.17.far, bf16[656,128]{1,0:T(8,128)(2,1)S(1)} %collective-permute-done.20.near_far, f32[4,640,128]{2,1,0:T(8,128)S(1)} %get-tuple-element.61.before_ref, f32[16,128]{1,0:T(8,128)S(1)} %get-tuple-element.62.notes_ref, ...), custom_call_target="tpu_custom_call" | custom-call | flops 335544320 | bytes 8388608 | tf_op jit(solution)/shard_map/merge/pallas_call | solution.py:556
  (40 shorter events, 3.1 us)
Async XLA Ops:
  1.7 7.7 %collective-permute-start = (bf16[64,640]{1,0:T(8,128)(2,1)S(1)}, bf16[64,640]{1,0:T(8,128)(2,1)S(1)}, u32[]{:S(2)}, u32[]{:S(2)}) collective-permute-start(bf16[64,640]{1,0:T(8,128)(2,1)S(1)} %get-tuple-element.36), channel_id=1, source_target_pairs={{0,4},{1,5},{2,6},{3,7},{4,0},{5,1},{6,2},{7,3},{8,12},{9,13},{10,... | collective-permute-start | bytes 245768 | tf_op jit(solution)/shard_map/ppermute | solution.py:436
  4.7 5.1 %collective-permute-start.1 = (bf16[64,640]{1,0:T(8,128)(2,1)S(1)}, bf16[64,640]{1,0:T(8,128)(2,1)S(1)}, u32[]{:S(2)}, u32[]{:S(2)}) collective-permute-start(bf16[64,640]{1,0:T(8,128)(2,1)S(1)} %get-tuple-element.37), channel_id=1, source_target_pairs={{0,2},{1,3},{2,0},{3,1},{4,6},{5,7},{6,4},{7,5},{8,10},{9,11},{10,... | collective-permute-start | bytes 245768 | tf_op jit(solution)/shard_map/ppermute | solution.py:436
  6.2 6.1 %collective-permute-start.2 = (bf16[64,640]{1,0:T(8,128)(2,1)S(1)}, bf16[64,640]{1,0:T(8,128)(2,1)S(1)}, u32[]{:S(2)}, u32[]{:S(2)}) collective-permute-start(bf16[64,640]{1,0:T(8,128)(2,1)S(1)} %get-tuple-element.38), channel_id=1, source_target_pairs={{0,6},{1,7},{2,4},{3,5},{4,2},{5,3},{6,0},{7,1},{8,14},{9,15},{10,... | collective-permute-start | bytes 245768 | tf_op jit(solution)/shard_map/ppermute | solution.py:436
  6.2 7.9 %collective-permute-start.3 = (bf16[64,640]{1,0:T(8,128)(2,1)S(1)}, bf16[64,640]{1,0:T(8,128)(2,1)S(1)}, u32[]{:S(2)}, u32[]{:S(2)}) collective-permute-start(bf16[64,640]{1,0:T(8,128)(2,1)S(1)} %get-tuple-element.42), channel_id=1, source_target_pairs={{0,7},{1,6},{2,5},{3,4},{4,3},{5,2},{6,1},{7,0},{8,15},{9,14},{10,... | collective-permute-start | bytes 245768 | tf_op jit(solution)/shard_map/ppermute | solution.py:436
  7.7 9.1 %collective-permute-start.4 = (bf16[64,640]{1,0:T(8,128)(2,1)S(1)}, bf16[64,640]{1,0:T(8,128)(2,1)S(1)}, u32[]{:S(2)}, u32[]{:S(2)}) collective-permute-start(bf16[64,640]{1,0:T(8,128)(2,1)S(1)} %get-tuple-element.43), channel_id=1, source_target_pairs={{0,3},{1,2},{2,1},{3,0},{4,7},{5,6},{6,5},{7,4},{8,11},{9,10},{10,... | collective-permute-start | bytes 245768 | tf_op jit(solution)/shard_map/ppermute | solution.py:436
  9.4 7.5 %collective-permute-start.5 = (bf16[64,640]{1,0:T(8,128)(2,1)S(1)}, bf16[64,640]{1,0:T(8,128)(2,1)S(1)}, u32[]{:S(2)}, u32[]{:S(2)}) collective-permute-start(bf16[64,640]{1,0:T(8,128)(2,1)S(1)} %get-tuple-element.44), channel_id=1, source_target_pairs={{0,5},{1,4},{2,7},{3,6},{4,1},{5,0},{6,3},{7,2},{8,13},{9,12},{10,... | collective-permute-start | bytes 245768 | tf_op jit(solution)/shard_map/ppermute | solution.py:436
  9.8 7.1 %collective-permute-start.6 = (bf16[64,640]{1,0:T(8,128)(2,1)S(1)}, bf16[64,640]{1,0:T(8,128)(2,1)S(1)}, u32[]{:S(2)}, u32[]{:S(2)}) collective-permute-start(bf16[64,640]{1,0:T(8,128)(2,1)S(1)} %get-tuple-element.45), channel_id=1, source_target_pairs={{0,1},{1,0},{2,3},{3,2},{4,5},{5,4},{6,7},{7,6},{8,9},{9,8},{10,11... | collective-permute-start | bytes 245768 | tf_op jit(solution)/shard_map/ppermute | solution.py:436
  12.3 9.4 %collective-permute-start.12 = (bf16[800,128]{1,0:T(8,128)(2,1)S(1)}, bf16[800,128]{1,0:T(8,128)(2,1)S(1)}, u32[]{:S(2)}, u32[]{:S(2)}) collective-permute-start(bf16[800,128]{1,0:T(8,128)(2,1)S(1)} %get-tuple-element.47), channel_id=1, source_target_pairs={{0,8},{1,25},{2,10},{3,27},{4,12},{5,29},{6,14},{7,31},{8,16},{9,1... | collective-permute-start | bytes 614408 | tf_op jit(solution)/shard_map/ppermute | solution.py:445
  14.2 9.8 %collective-permute-start.11 = (bf16[400,128]{1,0:T(8,128)(2,1)S(1)}, bf16[400,128]{1,0:T(8,128)(2,1)S(1)}, u32[]{:S(2)}, u32[]{:S(2)}) collective-permute-start(bf16[400,128]{1,0:T(8,128)(2,1)S(1)} %get-tuple-element.46.rest_8_), channel_id=1, source_target_pairs={{0,16},{1,17},{2,18},{3,19},{4,20},{5,21},{6,22},{7,23},{8,24},{9,... | collective-permute-start | bytes 307208 | tf_op jit(solution)/shard_map/ppermute | solution.py:445
  18.2 7.7 %collective-permute-start.10 = (bf16[640,128]{1,0:T(8,128)(2,1)S(1)}, bf16[640,128]{1,0:T(8,128)(2,1)S(1)}, u32[]{:S(2)}, u32[]{:S(2)}) collective-permute-start(bf16[640,128]{1,0:T(8,128)(2,1)S(1)} %attend.1.token_ref.rest_0_), channel_id=1, source_target_pairs={{0,4},{1,5},{2,6},{3,7},{4,0},{5,1},{6,2},{7,3},{8,12},{9,13},{10,... | collective-permute-start | bytes 491528 | tf_op jit(solution)/shard_map/ppermute | solution.py:436
  18.3 7.2 %collective-permute-start.9 = (bf16[640,128]{1,0:T(8,128)(2,1)S(1)}, bf16[640,128]{1,0:T(8,128)(2,1)S(1)}, u32[]{:S(2)}, u32[]{:S(2)}) collective-permute-start(bf16[640,128]{1,0:T(8,128)(2,1)S(1)} %attend.1.token_ref.rest_0_), channel_id=1, source_target_pairs={{0,2},{1,3},{2,0},{3,1},{4,6},{5,7},{6,4},{7,5},{8,10},{9,11},{10,... | collective-permute-start | bytes 491528 | tf_op jit(solution)/shard_map/ppermute | solution.py:436
  19.4 9.1 %collective-permute-start.7 = (bf16[640,128]{1,0:T(8,128)(2,1)S(1)}, bf16[640,128]{1,0:T(8,128)(2,1)S(1)}, u32[]{:S(2)}, u32[]{:S(2)}) collective-permute-start(bf16[640,128]{1,0:T(8,128)(2,1)S(1)} %attend.1.token_ref.rest_0_), channel_id=1, source_target_pairs={{0,6},{1,7},{2,4},{3,5},{4,2},{5,3},{6,0},{7,1},{8,14},{9,15},{10,... | collective-permute-start | bytes 491528 | tf_op jit(solution)/shard_map/ppermute | solution.py:436
  21.7 4.1 %collective-permute-start.15 = (bf16[800,128]{1,0:T(8,128)(2,1)S(1)}, bf16[800,128]{1,0:T(8,128)(2,1)S(1)}, u32[]{:S(2)}, u32[]{:S(2)}) collective-permute-start(bf16[800,128]{1,0:T(8,128)(2,1)S(1)} %collective-permute-done.12.rest_10_), channel_id=1, source_target_pairs={{0,1},{1,0},{2,3},{3,2},{4,5},{5,4},{6,7},{7,6},{8,9},{9,8},{10,11... | collective-permute-start | bytes 614408 | tf_op jit(solution)/shard_map/ppermute | solution.py:436
  25.2 3.3 %collective-permute-start.13 = (bf16[640,128]{1,0:T(8,128)(2,1)S(1)}, bf16[640,128]{1,0:T(8,128)(2,1)S(1)}, u32[]{:S(2)}, u32[]{:S(2)}) collective-permute-start(bf16[640,128]{1,0:T(8,128)(2,1)S(1)} %attend.1.token_ref.rest_0_), channel_id=1, source_target_pairs={{0,1},{1,0},{2,3},{3,2},{4,5},{5,4},{6,7},{7,6},{8,9},{9,8},{10,11... | collective-permute-start | bytes 491528 | tf_op jit(solution)/shard_map/ppermute | solution.py:436
  25.5 3.1 %collective-permute-start.14 = (bf16[640,128]{1,0:T(8,128)(2,1)S(1)}, bf16[640,128]{1,0:T(8,128)(2,1)S(1)}, u32[]{:S(2)}, u32[]{:S(2)}) collective-permute-start(bf16[640,128]{1,0:T(8,128)(2,1)S(1)} %collective-permute-done.9.rest_1_), channel_id=1, source_target_pairs={{0,1},{1,0},{2,3},{3,2},{4,5},{5,4},{6,7},{7,6},{8,9},{9,8},{10,11... | collective-permute-start | bytes 491528 | tf_op jit(solution)/shard_map/ppermute | solution.py:436
  25.9 2.6 %collective-permute-start.16 = (bf16[640,128]{1,0:T(8,128)(2,1)S(1)}, bf16[640,128]{1,0:T(8,128)(2,1)S(1)}, u32[]{:S(2)}, u32[]{:S(2)}) collective-permute-start(bf16[640,128]{1,0:T(8,128)(2,1)S(1)} %collective-permute-done.10.rest_2_), channel_id=1, source_target_pairs={{0,1},{1,0},{2,3},{3,2},{4,5},{5,4},{6,7},{7,6},{8,9},{9,8},{10,11... | collective-permute-start | bytes 491528 | tf_op jit(solution)/shard_map/ppermute | solution.py:436
  28.5 1.4 %collective-permute-start.8 = (bf16[640,128]{1,0:T(8,128)(2,1)S(1)}, bf16[640,128]{1,0:T(8,128)(2,1)S(1)}, u32[]{:S(2)}, u32[]{:S(2)}) collective-permute-start(bf16[640,128]{1,0:T(8,128)(2,1)S(1)} %collective-permute-done.7.rest_0_), channel_id=1, source_target_pairs={{0,1},{1,0},{2,3},{3,2},{4,5},{5,4},{6,7},{7,6},{8,9},{9,8},{10,11... | collective-permute-start | bytes 491528 | tf_op jit(solution)/shard_map/ppermute | solution.py:436
  30.6 6.6 %collective-permute-start.18 = (bf16[656,128]{1,0:T(8,128)(2,1)S(1)}, bf16[656,128]{1,0:T(8,128)(2,1)S(1)}, u32[]{:S(2)}, u32[]{:S(2)}) collective-permute-start(bf16[656,128]{1,0:T(8,128)(2,1)S(1)} %project.1.token_ref.own), channel_id=1, source_target_pairs={{0,4},{1,5},{2,6},{3,7},{4,0},{5,1},{6,2},{7,3},{8,12},{9,13},{10,... | collective-permute-start | bytes 503816 | tf_op jit(solution)/shard_map/ppermute | solution.py:436
  31.0 7.1 %collective-permute-start.19 = (bf16[656,128]{1,0:T(8,128)(2,1)S(1)}, bf16[656,128]{1,0:T(8,128)(2,1)S(1)}, u32[]{:S(2)}, u32[]{:S(2)}) collective-permute-start(bf16[656,128]{1,0:T(8,128)(2,1)S(1)} %project.1.token_ref.own), channel_id=1, source_target_pairs={{0,2},{1,3},{2,0},{3,1},{4,6},{5,7},{6,4},{7,5},{8,10},{9,11},{10,... | collective-permute-start | bytes 503816 | tf_op jit(solution)/shard_map/ppermute | solution.py:436
  31.8 10.2 %collective-permute-start.17 = (bf16[656,128]{1,0:T(8,128)(2,1)S(1)}, bf16[656,128]{1,0:T(8,128)(2,1)S(1)}, u32[]{:S(2)}, u32[]{:S(2)}) collective-permute-start(bf16[656,128]{1,0:T(8,128)(2,1)S(1)} %project.1.token_ref.own), channel_id=1, source_target_pairs={{0,6},{1,7},{2,4},{3,5},{4,2},{5,3},{6,0},{7,1},{8,14},{9,15},{10,... | collective-permute-start | bytes 503816 | tf_op jit(solution)/shard_map/ppermute | solution.py:436
  35.6 6.4 %collective-permute-start.21 = (bf16[656,128]{1,0:T(8,128)(2,1)S(1)}, bf16[656,128]{1,0:T(8,128)(2,1)S(1)}, u32[]{:S(2)}, u32[]{:S(2)}) collective-permute-start(bf16[656,128]{1,0:T(8,128)(2,1)S(1)} %project.1.token_ref.own), channel_id=1, source_target_pairs={{0,1},{1,0},{2,3},{3,2},{4,5},{5,4},{6,7},{7,6},{8,9},{9,8},{10,11... | collective-permute-start | bytes 503816 | tf_op jit(solution)/shard_map/ppermute | solution.py:436
  37.2 4.8 %collective-permute-start.22 = (bf16[656,128]{1,0:T(8,128)(2,1)S(1)}, bf16[656,128]{1,0:T(8,128)(2,1)S(1)}, u32[]{:S(2)}, u32[]{:S(2)}) collective-permute-start(bf16[656,128]{1,0:T(8,128)(2,1)S(1)} %collective-permute-done.18.y), channel_id=1, source_target_pairs={{0,1},{1,0},{2,3},{3,2},{4,5},{5,4},{6,7},{7,6},{8,9},{9,8},{10,11... | collective-permute-start | bytes 503816 | tf_op jit(solution)/shard_map/ppermute | solution.py:436
  39.4 2.6 %collective-permute-start.23 = (bf16[656,128]{1,0:T(8,128)(2,1)S(1)}, bf16[656,128]{1,0:T(8,128)(2,1)S(1)}, u32[]{:S(2)}, u32[]{:S(2)}) collective-permute-start(bf16[656,128]{1,0:T(8,128)(2,1)S(1)} %collective-permute-done.19.x), channel_id=1, source_target_pairs={{0,1},{1,0},{2,3},{3,2},{4,5},{5,4},{6,7},{7,6},{8,9},{9,8},{10,11... | collective-permute-start | bytes 503816 | tf_op jit(solution)/shard_map/ppermute | solution.py:436
  42.0 1.4 %collective-permute-start.20 = (bf16[656,128]{1,0:T(8,128)(2,1)S(1)}, bf16[656,128]{1,0:T(8,128)(2,1)S(1)}, u32[]{:S(2)}, u32[]{:S(2)}) collective-permute-start(bf16[656,128]{1,0:T(8,128)(2,1)S(1)} %collective-permute-done.17.far), channel_id=1, source_target_pairs={{0,1},{1,0},{2,3},{3,2},{4,5},{5,4},{6,7},{7,6},{8,9},{9,8},{10,11... | collective-permute-start | bytes 503816 | tf_op jit(solution)/shard_map/ppermute | solution.py:436
  (2 other events, 11.2 us)

commit v12 on v10

--- a/solution.py
+++ b/solution.py
@@ -122,9 +122,8 @@
 REST = HPAIR - WIDE
 MAIN = ROWS * WIDE
 NOTES = 16
-BLOCK_ORDER = (0, 2, 4, 6, 7, 3, 5, 1)
-PIECE_ORDER = (0, 2, 4, 1, 3, 5, 6, 7)
-EARLY = 6
+BLOCK_ORDER = (0, 4, 2, 6, 7, 3, 5, 1)
+PIECE_ORDER = (0, 4, 2, 1, 5, 3, 6, 7)
 ROOT = math.log2(math.e) / math.sqrt(HDIM)
 BF16 = jnp.bfloat16
 F32 = jnp.float32
@@ -155,7 +154,18 @@
     ]
     for copy in copies:
         copy.start()
-    for copy in copies:
+    for copy in copies[2:]:
+        copy.wait()
+    low = me // 2 % 2 == 0
+    size = depth + depth // 4
+    for core in range(2):
+        tail = jnp.where(low, tile[:, core * REST : (core + 1) * REST], tile[:, (core + 2) * REST : (core + 3) * REST])
+        chip_ref[core * size : core * size + depth, :] = main[:, core * WIDE : (core + 1) * WIDE]
+        chip_ref[core * size + depth : (core + 1) * size, :] = pack_tail(tail)
+    slice_ref[...] = chip_ref[pl.ds(pl.multiple_of(me % 2 * size, 16), size), :]
+    row = lax.broadcasted_iota(jnp.int32, grid_out.shape, 0)
+    grid_out[...] = jnp.where(row == 0, grid[0, 0], grid[0, 1])
+    for copy in copies[:2]:
         copy.wait()
     for dest in range(ROWS):
         at = dest * HPAIR
@@ -165,15 +175,6 @@
         held[dest] = jnp.concatenate(parts, axis=1)
     for step in range(ROWS):
         outs[step][...] = held[me ^ step]
-    low = me // 2 % 2 == 0
-    size = depth + depth // 4
-    for core in range(2):
-        tail = jnp.where(low, tile[:, core * REST : (core + 1) * REST], tile[:, (core + 2) * REST : (core + 3) * REST])
-        chip_ref[core * size : core * size + depth, :] = main[:, core * WIDE : (core + 1) * WIDE]
-        chip_ref[core * size + depth : (core + 1) * size, :] = pack_tail(tail)
-    slice_ref[...] = chip_ref[pl.ds(pl.multiple_of(me % 2 * size, 16), size), :]
-    row = lax.broadcasted_iota(jnp.int32, grid_out.shape, 0)
-    grid_out[...] = jnp.where(row == 0, grid[0, 0], grid[0, 1])
 
 
 def layout_kernel(grid_ref, *rest):
@@ -285,13 +286,6 @@
     return pl.ds(pl.multiple_of((me // 2 ^ 3) * 2 * WIDE, 2 * WIDE), 2 * WIDE)
 
 
-def collect_early(pieces, full):
-    me = row_index()
-    full[:, far_block()] = jnp.zeros((full.shape[0], 2 * WIDE), BF16)
-    for step, piece in zip(PIECE_ORDER[:EARLY], pieces):
-        full[:, pl.ds(pl.multiple_of((me ^ step) * WIDE, WIDE), WIDE)] = piece[...]
-
-
 def collect_late(same, other):
     core = row_index() % 2
     left = jnp.where(core == 0, same[...], other[...])
@@ -303,20 +297,33 @@
     return lax.rem(lax.axis_index("page") + 1 + 2 * (row_index() % 2), PAGES)
 
 
-def project_early_kernel(*rest):
-    pieces = rest[:EARLY]
-    main_ref, tail_ref, last_main_ref, last_tail_ref, resid_ref, out_ref, full = rest[EARLY:]
-    collect_early(pieces, full)
-    patches = resid_ref.shape[0]
+def add_features(steps, pieces, weights, before_ref, out_ref):
+    main_ref, tail_ref, last_main_ref, last_tail_ref = weights
+    me = row_index()
+    patches = out_ref.shape[0]
     groups = patches // 4
-    late = pl.ds(pl.multiple_of(late_source() * 2 * WIDE, 2 * WIDE), 2 * WIDE)
-    base = jnp.dot(full[:patches], main_ref[...], preferred_element_type=F32) + resid_ref[...]
-    base = base + jnp.dot(full[:patches, late], last_main_ref[...], preferred_element_type=F32)
+    mains, tails = [], []
+    for step in steps:
+        pair = me ^ step
+        columns = pl.ds(pl.multiple_of(pair * WIDE, WIDE), WIDE)
+        late = pl.ds(pl.multiple_of(pair % 2 * WIDE, WIDE), WIDE)
+        is_late = pair // 2 == late_source()
+        mains.append(jnp.where(is_late, last_main_ref[late, :], main_ref[columns, :]))
+        tails.append([jnp.where(is_late, last_tail_ref[at, late, :], tail_ref[at, columns, :]) for at in range(4)])
+    rows = jnp.concatenate([piece[...] for piece in pieces], axis=1)
+    base = before_ref[...] + jnp.dot(rows[:patches], jnp.concatenate(mains, axis=0), preferred_element_type=F32)
     for corner in range(4):
         span = slice(corner * groups, (corner + 1) * groups)
-        part = jnp.dot(full[patches:], tail_ref[corner], preferred_element_type=F32)
-        part = part + jnp.dot(full[patches:, late], last_tail_ref[corner], preferred_element_type=F32)
-        out_ref[span, :] = base[span] + part
+        tail = jnp.concatenate([tail[corner] for tail in tails], axis=0)
+        out_ref[span, :] = base[span] + jnp.dot(rows[patches:], tail, preferred_element_type=F32)
+
+
+def project_first_kernel(own, y, x, *rest):
+    add_features((0, 4, 2), (own, y, x), rest[:4], *rest[4:])
+
+
+def project_second_kernel(own, y, x, *rest):
+    add_features((1, 5, 3), (own, y, x), rest[:4], *rest[4:])
 
 
 def project_kernel(*rest):
@@ -365,53 +372,60 @@
     bias_out[...] = jnp.broadcast_to(line[...].reshape(1, units), (8, units)).T[:, :1]
 
 
-def chip_product(weight_ref, corner, groups, other, rows):
-    at = pl.multiple_of(corner * D + (row_index() // 2 ^ other) * 2 * WIDE, 2 * WIDE)
+def merge_product(weight_ref, corner, groups, pieces):
+    me = row_index()
+    spots = [pl.multiple_of(corner * D + (me ^ step) * WIDE, WIDE) for step, _ in pieces]
+    span = slice(corner * groups, (corner + 1) * groups)
     return lax.dot_general(
-        weight_ref[:, pl.ds(at, 2 * WIDE)],
-        rows[corner * groups : (corner + 1) * groups],
+        jnp.concatenate([weight_ref[:, pl.ds(spot, WIDE)] for spot in spots], axis=1),
+        jnp.concatenate([piece[span, :] for _, piece in pieces], axis=1),
         (((1,), (1,)), ((), ())),
         preferred_element_type=F32,
     )
 
 
-def merge_first_kernel(own, near_own, one, near_one, weight_ref, out_ref):
-    groups = out_ref.shape[2]
-    rows = [collect_late(own, near_own), collect_late(one, near_one)]
-    for corner in range(4):
-        out_ref[corner] = chip_product(weight_ref, corner, groups, 0, rows[0]) + chip_product(
-            weight_ref, corner, groups, 1, rows[1]
-        )
-
-
-def merge_second_kernel(two, near_two, sum_ref, weight_ref, out_ref):
-    groups = out_ref.shape[2]
-    rows = collect_late(two, near_two)
-    for corner in range(4):
-        out_ref[corner] = sum_ref[corner] + chip_product(weight_ref, corner, groups, 2, rows)
+def merge_first_kernel(own, y, x, weight_ref, sum_ref):
+    for corner in range(4):
+        sum_ref[corner] = merge_product(weight_ref, corner, sum_ref.shape[2], [(0, own), (4, y), (2, x)])
+
+
+def merge_second_kernel(own, y, x, before_ref, weight_ref, sum_ref):
+    for corner in range(4):
+        part = merge_product(weight_ref, corner, sum_ref.shape[2], [(1, own), (5, y), (3, x)])
+        sum_ref[corner] = before_ref[corner] + part
 
 
 def merge_kernel(*rest):
     pieces = rest[:ROWS]
-    early_ref, weight_ref, tail_ref, bias_ref, live_ref, out_ref, ends_ref = rest[ROWS:]
+    before_ref, weight_ref, tail_ref, bias_ref, live_ref, out_ref, ends_ref = rest[ROWS:]
     me = row_index()
     groups = live_ref.shape[1]
     patches = 4 * groups
+    contract = (((1,), (1,)), ((), ()))
+    block = pl.multiple_of((me // 2 ^ 3) * 2 * WIDE, 2 * WIDE)
+    rows = collect_late(pieces[6], pieces[7])
+    parts = []
+    for corner in range(4):
+        parts.append(
+            before_ref[corner]
+            + lax.dot_general(
+                weight_ref[:, pl.ds(pl.multiple_of(corner * D + block, 2 * WIDE), 2 * WIDE)],
+                rows[corner * groups : (corner + 1) * groups],
+                contract,
+                preferred_element_type=F32,
+            )
+        )
     notes = jnp.zeros((NOTES, groups), F32)
     for step, piece in zip(PIECE_ORDER, pieces):
-        ends_ref[:, pl.ds(pl.multiple_of((me ^ step) * WIDE, WIDE), WIDE)] = piece[patches : patches + groups]
-        notes = notes + piece[patches + groups :].astype(F32)
+        notes = notes + piece[patches + groups :, :].astype(F32)
     scale = lax.rsqrt((notes[:4] + notes[4:8]) * (1.0 / D) + 1e-06)
-    contract = (((1,), (1,)), ((), ()))
-    rows = collect_late(pieces[EARLY], pieces[EARLY + 1])
-    total = jnp.zeros(bias_ref.shape[:1] + (groups,), F32)
-    for corner in range(4):
-        part = early_ref[corner] + chip_product(weight_ref, corner, groups, 3, rows)
-        total = total + scale[corner : corner + 1] * part
     spread = jnp.concatenate([jnp.broadcast_to(scale[at : at + 1], (REST, groups)) for at in range(4)], axis=0).T
-    ends = ends_ref[...].astype(F32) * jnp.concatenate([spread] * ROWS, axis=1)
-    total = total + lax.dot_general(tail_ref[...], ends.astype(BF16), contract, preferred_element_type=F32)
-    total = total + bias_ref[...]
+    for step, piece in zip(PIECE_ORDER, pieces):
+        at = pl.ds(pl.multiple_of((me ^ step) * WIDE, WIDE), WIDE)
+        ends_ref[:, at] = (piece[patches : patches + groups, :].astype(F32) * spread).astype(BF16)
+    total = bias_ref[...] + lax.dot_general(tail_ref[...], ends_ref[...], contract, preferred_element_type=F32)
+    for corner in range(4):
+        total = total + scale[corner : corner + 1] * parts[corner]
     merged = 0.5 * total * (1.0 + lax.erf(total * math.sqrt(0.5)))
     out_ref[0] = jnp.where(live_ref[...] > 0.0, merged, 0.0).astype(BF16)
 
@@ -524,17 +538,12 @@
         count=2,
         moved=4 << 20,
     )(swapped, main)
-    x, y, far = [swap(attn, step) for step in (2, 4, 6)]
-    pieces = [attn, x, y, swap(after(attn, main), 1), swap(x, 1), swap(after(y, last[0]), 1), far, swap(far, 1)]
-    base = kernel(
-        project_early_kernel,
-        "project_early",
-        shape(patches, HPAIR, dtype=F32),
-        [pltpu.VMEM((piece, MAIN), BF16)],
-        count=EARLY + 5,
-        flops=4 * patches * MAIN * 4096,
-        moved=4 << 20,
-    )(*pieces[:EARLY], main, tail, *last, resid)
+    y, x, far = [swap(attn, step) for step in (4, 2, 6)]
+    weights = (main, tail, *last)
+    rows = shape(patches, HPAIR, dtype=F32)
+    first = kernel(project_first_kernel, "project_first", rows, count=8, flops=1, moved=1)(attn, y, x, *weights, resid)
+    near = [swap(after(attn, main), 1), swap(after(y, last[0]), 1), swap(x, 1)]
+    second = kernel(project_second_kernel, "project_second", rows, count=8, flops=1, moved=1)(*near, *weights, first)
     hidden = kernel(
         project_kernel,
         "project",
@@ -542,7 +551,7 @@
         count=2 + 6,
         flops=patches * MAIN * 256,
         moved=4 << 20,
-    )(*pieces[EARLY:], base, main, tail, *last, own_gain)
+    )(far, swap(after(far, first), 1), second, *weights, own_gain)
     ends, bias = kernel(
         tail_kernel,
         "merge_tail",
@@ -553,16 +562,10 @@
         moved=4 << 20,
     )(merge_weight, in_hbm(merge_bias), hidden)
     sums = shape(4, units, groups, dtype=F32)
-    x, y, far = [swap(hidden, step) for step in (2, 4, 6)]
-    near_own, near_x = swap(after(hidden, ends), 1), swap(x, 1)
-    first = kernel(
-        merge_first_kernel, "merge_first", sums, count=5, flops=4 * units * groups * MAIN * 1, moved=4 << 20
-    )(hidden, near_own, x, near_x, merge_weight)
-    near_y = swap(y, 1)
-    second = kernel(
-        merge_second_kernel, "merge_second", sums, count=4, flops=2 * units * groups * MAIN * 1, moved=4 << 20
-    )(y, near_y, first, merge_weight)
-    pieces = [hidden, x, y, near_own, near_x, near_y, far, swap(far, 1)]
+    y, x, far = [swap(hidden, step) for step in (4, 2, 6)]
+    first = kernel(merge_first_kernel, "merge_first", sums, count=4, flops=1, moved=1)(hidden, y, x, merge_weight)
+    near = [swap(after(hidden, ends), 1), swap(y, 1), swap(x, 1)]
+    second = kernel(merge_second_kernel, "merge_second", sums, count=5, flops=1, moved=1)(*near, first, merge_weight)
     return kernel(
         merge_kernel,
         "merge",
@@ -571,7 +574,7 @@
         count=ROWS + 5,
         flops=4 * units * groups * MAIN,
         moved=8 << 20,
-    )(*pieces, second, merge_weight, ends, bias, live)
+    )(hidden, y, x, *near, far, swap(after(far, first, *near), 1), second, merge_weight, ends, bias, live)
 
 
 def solution(mesh):

time: 44.6 us -> 45.1 us (1.011)
  waiting for transfers between devices: 13.1 us -> 14.2 us
  starting transfers between devices: 20.4 us -> 19.8 us
    ppermute x22, waiting for transfers between devices: 10.7 us -> 11.9 us  [swap(): lax.ppermute(value, 'row', [(row, row ^ step) for row in range(ROWS)])]
    ppermute x22, starting transfers between devices: 16.1 us -> 15.5 us  [swap(): lax.ppermute(value, 'row', [(row, row ^ step) for row in range(ROWS)])]
    pallas_call x3 -> x4, Pallas kernels: 2.58 us -> 2.39 us  [the longest x1 0.74 us: local_eight(): kernel(merge_second_kernel, 'merge_second', sums, count=5, flops=1, moved=1)]
  transfers between devices with their start and end apart: 24 -> 24, of which waited for: 7 -> 10; matrix products, arithmetic and copies ran while one was open for 0% -> 0% of each run, Pallas kernels for 15% -> 15%
where the time goes in v12:
time: 45.1 us; the launch traced here: 45 us
  starting transfers between devices  19.8 us (44%)
  waiting for transfers between devices  14.2 us (31%)
  Pallas kernels  10.8 us (24%)
    ppermute x22, starting transfers between devices, swap(): lax.ppermute(value, 'row', [(row, row ^ step) for row in range(ROWS)])  15.5 us
    ppermute x22, waiting for transfers between devices, swap(): lax.ppermute(value, 'row', [(row, row ^ step) for row in range(ROWS)])  11.9 us
    ppermute x2, starting transfers between devices, turn(): return lax.ppermute(value, ('page', 'row'), pairs)  4.3 us
    ppermute x2, waiting for transfers between devices, turn(): return lax.ppermute(value, ('page', 'row'), pairs)  2.27 us
    pallas_call x1, Pallas kernels, local_eight(): kernel(spread_kernel, 'spread', [shape(band, 4 * HPAIR)] * ROWS + [shape(...  1.76 us
    pallas_call x1, Pallas kernels, local_eight(): kernel(merge_kernel, 'merge', shape(1, units, groups), [pltpu.VMEM((group...  1.68 us
    pallas_call x1, Pallas kernels, local_eight(): kernel(tail_kernel, 'merge_tail', [shape(units, MAIN), shape(units, 1, dt...  1.39 us
    pallas_call x1, Pallas kernels, local_eight(): kernel(attend_kernel, 'attend', shape(piece, WIDE), [pltpu.VMEM((patches,...  1.35 us
  transfers between devices with their start and end apart: 24, of which 10 were waited for; matrix products, arithmetic and copies ran while one was open for 0% of the time, Pallas kernels for 15%

profile of v12, /device:TPU:0, one launch (start us, length us, event | category | flops | bytes accessed | tf_op | source)
XLA Modules:
  0.0 45.0 jit_solution(17158238797160899956)
XLA Ops:
  0.0 1.8 %spread.1 = (bf16[64,640]{1,0:T(8,128)(2,1)S(1)}, bf16[64,640]{1,0:T(8,128)(2,1)S(1)}, bf16[64,640]{1,0:T(8,128)(2,1)S(1)}, bf16[64,640]{1,0:T(8,128)(2,1)S(1)},...) custom-call(bf16[1,64,3840]{2,1,0:T(8,128)(2,1)} %qkv_hbm.1, ...), custom_call_target="tpu_custom_call" | custom-call | bytes 1048576 | tf_op jit(solution)/shard_map/spread/pallas_call | solution.py:483
  1.8 3.0 %collective-permute-start = (bf16[64,640]{1,0:T(8,128)(2,1)S(1)}, bf16[64,640]{1,0:T(8,128)(2,1)S(1)}, u32[]{:S(2)}, u32[]{:S(2)}) collective-permute-start(bf16[64,640]{1,0:T(8,128)(2,1)S(1)} %get-tuple-element.33), channel_id=1, source_target_pairs={{0,4},{1,5},{2,6},{3,7},{4,0},{5,1},{6,2},{7,3},{8,12},{9,13},{10,... | collective-permute-start | bytes 245768 | tf_op jit(solution)/shard_map/ppermute | solution.py:458
  4.8 1.5 %collective-permute-start.1 = (bf16[64,640]{1,0:T(8,128)(2,1)S(1)}, bf16[64,640]{1,0:T(8,128)(2,1)S(1)}, u32[]{:S(2)}, u32[]{:S(2)}) collective-permute-start(bf16[64,640]{1,0:T(8,128)(2,1)S(1)} %get-tuple-element.34), channel_id=1, source_target_pairs={{0,2},{1,3},{2,0},{3,1},{4,6},{5,7},{6,4},{7,5},{8,10},{9,11},{10,... | collective-permute-start | bytes 245768 | tf_op jit(solution)/shard_map/ppermute | solution.py:458
  6.3 1.5 %collective-permute-start.3 = (bf16[64,640]{1,0:T(8,128)(2,1)S(1)}, bf16[64,640]{1,0:T(8,128)(2,1)S(1)}, u32[]{:S(2)}, u32[]{:S(2)}) collective-permute-start(bf16[64,640]{1,0:T(8,128)(2,1)S(1)} %get-tuple-element.39), channel_id=1, source_target_pairs={{0,7},{1,6},{2,5},{3,4},{4,3},{5,2},{6,1},{7,0},{8,15},{9,14},{10,... | collective-permute-start | bytes 245768 | tf_op jit(solution)/shard_map/ppermute | solution.py:458
  7.8 1.6 %collective-permute-start.4 = (bf16[64,640]{1,0:T(8,128)(2,1)S(1)}, bf16[64,640]{1,0:T(8,128)(2,1)S(1)}, u32[]{:S(2)}, u32[]{:S(2)}) collective-permute-start(bf16[64,640]{1,0:T(8,128)(2,1)S(1)} %get-tuple-element.40), channel_id=1, source_target_pairs={{0,3},{1,2},{2,1},{3,0},{4,7},{5,6},{6,5},{7,4},{8,11},{9,10},{10,... | collective-permute-start | bytes 245768 | tf_op jit(solution)/shard_map/ppermute | solution.py:458
  9.9 2.6 %collective-permute-done.2.rest_2_.rest_3_ = bf16[64,640]{1,0:T(8,128)(2,1)S(1)} collective-permute-done((bf16[64,640]{1,0:T(8,128)(2,1)S(1)}, bf16[64,640]{1,0:T(8,128)(2,1)S(1)}, u32[]{:S(2)}, u32[]{:S(2)}) %collective-permute-start.2) | collective-permute-done | bytes 81952 | tf_op jit(solution)/shard_map/ppermute | solution.py:458
  12.4 1.7 %collective-permute-start.11 = (bf16[800,128]{1,0:T(8,128)(2,1)S(1)}, bf16[800,128]{1,0:T(8,128)(2,1)S(1)}, u32[]{:S(2)}, u32[]{:S(2)}) collective-permute-start(bf16[800,128]{1,0:T(8,128)(2,1)S(1)} %get-tuple-element.44), channel_id=1, source_target_pairs={{0,8},{1,25},{2,10},{3,27},{4,12},{5,29},{6,14},{7,31},{8,16},{9,1... | collective-permute-start | bytes 614408 | tf_op jit(solution)/shard_map/ppermute | solution.py:467
  14.3 2.7 %collective-permute-start.10 = (bf16[400,128]{1,0:T(8,128)(2,1)S(1)}, bf16[400,128]{1,0:T(8,128)(2,1)S(1)}, u32[]{:S(2)}, u32[]{:S(2)}) collective-permute-start(bf16[400,128]{1,0:T(8,128)(2,1)S(1)} %get-tuple-element.43.rest_8_), channel_id=1, source_target_pairs={{0,16},{1,17},{2,18},{3,19},{4,20},{5,21},{6,22},{7,23},{8,24},{9,... | collective-permute-start | bytes 307208 | tf_op jit(solution)/shard_map/ppermute | solution.py:467
  16.9 1.4 %attend.1.token_ref.own = bf16[640,128]{1,0:T(8,128)(2,1)S(1)} custom-call(bf16[512,512]{1,0:T(8,128)(2,1)S(1)} %get-tuple-element.36.select_ref, f32[1,512]{1,0:T(1,128)S(1)} %get-tuple-element.37.dead_ref, bf16[64,640]{1,0:T(8,128)(2,1)S(1)} %get-tuple-element.38.rest_0_, bf16[64,640]{1,0:T(8,128)(2,1)S(1)} %collective-permute-done.rest_0_.rest_1_, ...), custom_call_target="tpu_custom_call" | custom-call | flops 21474836480 | bytes 1048576 | tf_op jit(solution)/shard_map/attend/pallas_call | solution.py:514
  18.4 1.1 %collective-permute-start.9 = (bf16[640,128]{1,0:T(8,128)(2,1)S(1)}, bf16[640,128]{1,0:T(8,128)(2,1)S(1)}, u32[]{:S(2)}, u32[]{:S(2)}) collective-permute-start(bf16[640,128]{1,0:T(8,128)(2,1)S(1)} %attend.1.token_ref.own), channel_id=1, source_target_pairs={{0,2},{1,3},{2,0},{3,1},{4,6},{5,7},{6,4},{7,5},{8,10},{9,11},{10,... | collective-permute-start | bytes 491528 | tf_op jit(solution)/shard_map/ppermute | solution.py:458
  19.5 2.3 %collective-permute-start.7 = (bf16[640,128]{1,0:T(8,128)(2,1)S(1)}, bf16[640,128]{1,0:T(8,128)(2,1)S(1)}, u32[]{:S(2)}, u32[]{:S(2)}) collective-permute-start(bf16[640,128]{1,0:T(8,128)(2,1)S(1)} %attend.1.token_ref.own), channel_id=1, source_target_pairs={{0,6},{1,7},{2,4},{3,5},{4,2},{5,3},{6,0},{7,1},{8,14},{9,15},{10,... | collective-permute-start | bytes 491528 | tf_op jit(solution)/shard_map/ppermute | solution.py:458
  21.9 2.3 %collective-permute-done.10.rest_9_ = bf16[400,128]{1,0:T(8,128)(2,1)S(1)} collective-permute-done((bf16[400,128]{1,0:T(8,128)(2,1)S(1)}, bf16[400,128]{1,0:T(8,128)(2,1)S(1)}, u32[]{:S(2)}, u32[]{:S(2)}) %collective-permute-start.10) | collective-permute-done | bytes 102432 | tf_op jit(solution)/shard_map/ppermute | solution.py:467
  24.1 1.2 %ready.1 = (f32[512,160]{1,0:T(8,128)S(1)}, f32[1,160]{1,0:T(1,128)S(1)}, bf16[1024,160]{1,0:T(8,128)(2,1)S(1)}, bf16[4,1024,160]{2,1,0:T(8,128)(2,1)S(1)}) custom-call(bf16[512,512]{1,0:T(8,128)(2,1)S(1)} %get-tuple-element.36.select_ref, f32[1280]{0:T(1024)} %gain_hbm.1, bf16[640,128]{1,0:T(8,128)(2,1)S(1)} %attend.1.token_ref.own, ...), custom_call_target="tpu_custom_call" | custom-call | flops 10737418240 | bytes 4194304 | tf_op jit(solution)/shard_map/ready/pallas_call | solution.py:523
  26.8 1.9 %collective-permute-done.7.rest_0_ = bf16[640,128]{1,0:T(8,128)(2,1)S(1)} collective-permute-done((bf16[640,128]{1,0:T(8,128)(2,1)S(1)}, bf16[640,128]{1,0:T(8,128)(2,1)S(1)}, u32[]{:S(2)}, u32[]{:S(2)}) %collective-permute-start.7) | collective-permute-done | bytes 163872 | tf_op jit(solution)/shard_map/ppermute | solution.py:458
  29.2 0.9 %collective-permute-done.13.rest_1_ = bf16[640,128]{1,0:T(8,128)(2,1)S(1)} collective-permute-done((bf16[640,128]{1,0:T(8,128)(2,1)S(1)}, bf16[640,128]{1,0:T(8,128)(2,1)S(1)}, u32[]{:S(2)}, u32[]{:S(2)}) %collective-permute-start.13) | collective-permute-done | bytes 163872 | tf_op jit(solution)/shard_map/ppermute | solution.py:458
  31.1 0.8 %collective-permute-start.18 = (bf16[656,128]{1,0:T(8,128)(2,1)S(1)}, bf16[656,128]{1,0:T(8,128)(2,1)S(1)}, u32[]{:S(2)}, u32[]{:S(2)}) collective-permute-start(bf16[656,128]{1,0:T(8,128)(2,1)S(1)} %project.1.token_ref.own.rest_0_), channel_id=1, source_target_pairs={{0,2},{1,3},{2,0},{3,1},{4,6},{5,7},{6,4},{7,5},{8,10},{9,11},{10,... | collective-permute-start | bytes 503816 | tf_op jit(solution)/shard_map/ppermute | solution.py:458
  31.9 2.3 %collective-permute-start.22 = (bf16[656,128]{1,0:T(8,128)(2,1)S(1)}, bf16[656,128]{1,0:T(8,128)(2,1)S(1)}, u32[]{:S(2)}, u32[]{:S(2)}) collective-permute-start(bf16[656,128]{1,0:T(8,128)(2,1)S(1)} %project.1.token_ref.own.rest_0_), channel_id=1, source_target_pairs={{0,6},{1,7},{2,4},{3,5},{4,2},{5,3},{6,0},{7,1},{8,14},{9,15},{10,... | collective-permute-start | bytes 503816 | tf_op jit(solution)/shard_map/ppermute | solution.py:458
  34.2 1.4 %merge_tail.1 = (bf16[640,1024]{1,0:T(8,128)(2,1)S(1)}, f32[640,1]{1,0:T(8,128)S(1)}) custom-call(bf16[640,5120]{1,0:T(8,128)(2,1)S(1)} %bitcast.1, f32[640]{0:T(1024)} %bias_hbm.1, bf16[656,128]{1,0:T(8,128)(2,1)S(1)} %project.1.token_ref.own.rest_0_), custom_call_target="tpu_custom_call" | custom-call | bytes 4194304 | tf_op jit(solution)/shard_map/merge_tail/pallas_call | solution.py:555
  35.7 1.4 %collective-permute-done.17.y.rest_1_ = bf16[656,128]{1,0:T(8,128)(2,1)S(1)} collective-permute-done((bf16[656,128]{1,0:T(8,128)(2,1)S(1)}, bf16[656,128]{1,0:T(8,128)(2,1)S(1)}, u32[]{:S(2)}, u32[]{:S(2)}) %collective-permute-start.17) | collective-permute-done | bytes 167968 | tf_op jit(solution)/shard_map/ppermute | solution.py:458
  37.1 1.2 %collective-permute-done.18.x.rest_2_ = bf16[656,128]{1,0:T(8,128)(2,1)S(1)} collective-permute-done((bf16[656,128]{1,0:T(8,128)(2,1)S(1)}, bf16[656,128]{1,0:T(8,128)(2,1)S(1)}, u32[]{:S(2)}, u32[]{:S(2)}) %collective-permute-start.18) | collective-permute-done | bytes 167968 | tf_op jit(solution)/shard_map/ppermute | solution.py:458
  38.3 0.7 %merge_first.1.before_ref = f32[4,640,128]{2,1,0:T(8,128)S(1)} custom-call(bf16[656,128]{1,0:T(8,128)(2,1)S(1)} %project.1.token_ref.own.rest_0_, bf16[656,128]{1,0:T(8,128)(2,1)S(1)} %collective-permute-done.17.y.rest_1_, bf16[656,128]{1,0:T(8,128)(2,1)S(1)} %collective-permute-done.18.x.rest_2_, bf16[640,5120]{1,0:T(8,128)(2,1)S(1)} %bitcast.1), custom_call_target="tpu_custom_call" | custom-call | flops 1 | bytes 1 | tf_op jit(solution)/shard_map/merge_first/pallas_call | solution.py:566
  39.0 2.9 %collective-permute-done.22.rest_6_ = bf16[656,128]{1,0:T(8,128)(2,1)S(1)} collective-permute-done((bf16[656,128]{1,0:T(8,128)(2,1)S(1)}, bf16[656,128]{1,0:T(8,128)(2,1)S(1)}, u32[]{:S(2)}, u32[]{:S(2)}) %collective-permute-start.22) | collective-permute-done | bytes 167968 | tf_op jit(solution)/shard_map/ppermute | solution.py:458
  41.9 0.7 %merge_second.1.rest_8_ = f32[4,640,128]{2,1,0:T(8,128)S(1)} custom-call(bf16[656,128]{1,0:T(8,128)(2,1)S(1)} %collective-permute-done.19.own.rest_3_, bf16[656,128]{1,0:T(8,128)(2,1)S(1)} %collective-permute-done.20.y.rest_4_, bf16[656,128]{1,0:T(8,128)(2,1)S(1)} %collective-permute-done.21.x.rest_5_, f32[4,640,128]{2,1,0:T(8,128)S(1)} %merge_first.1.before_ref, ...), custom_call_target="tpu_custom_call" | custom-call | flops 1 | bytes 1 | tf_op jit(solution)/shard_map/merge_second/pallas_call | solution.py:568
  43.3 1.7 %merge.1 = bf16[1,640,128]{2,1,0:T(8,128)(2,1)} custom-call(bf16[656,128]{1,0:T(8,128)(2,1)S(1)} %project.1.token_ref.own.rest_0_, bf16[656,128]{1,0:T(8,128)(2,1)S(1)} %collective-permute-done.17.y.rest_1_, bf16[656,128]{1,0:T(8,128)(2,1)S(1)} %collective-permute-done.18.x.rest_2_, bf16[656,128]{1,0:T(8,128)(2,1)S(1)} %collective-permute-done.19.own.rest_3_, ...), custom_call_target="tpu_custom_call" | custom-call | flops 335544320 | bytes 8388608 | tf_op jit(solution)/shard_map/merge/pallas_call | solution.py:569
  (41 shorter events, 4.4 us)
Async XLA Ops:
  1.8 7.7 %collective-permute-start = (bf16[64,640]{1,0:T(8,128)(2,1)S(1)}, bf16[64,640]{1,0:T(8,128)(2,1)S(1)}, u32[]{:S(2)}, u32[]{:S(2)}) collective-permute-start(bf16[64,640]{1,0:T(8,128)(2,1)S(1)} %get-tuple-element.33), channel_id=1, source_target_pairs={{0,4},{1,5},{2,6},{3,7},{4,0},{5,1},{6,2},{7,3},{8,12},{9,13},{10,... | collective-permute-start | bytes 245768 | tf_op jit(solution)/shard_map/ppermute | solution.py:458
  4.8 5.1 %collective-permute-start.1 = (bf16[64,640]{1,0:T(8,128)(2,1)S(1)}, bf16[64,640]{1,0:T(8,128)(2,1)S(1)}, u32[]{:S(2)}, u32[]{:S(2)}) collective-permute-start(bf16[64,640]{1,0:T(8,128)(2,1)S(1)} %get-tuple-element.34), channel_id=1, source_target_pairs={{0,2},{1,3},{2,0},{3,1},{4,6},{5,7},{6,4},{7,5},{8,10},{9,11},{10,... | collective-permute-start | bytes 245768 | tf_op jit(solution)/shard_map/ppermute | solution.py:458
  6.3 6.1 %collective-permute-start.2 = (bf16[64,640]{1,0:T(8,128)(2,1)S(1)}, bf16[64,640]{1,0:T(8,128)(2,1)S(1)}, u32[]{:S(2)}, u32[]{:S(2)}) collective-permute-start(bf16[64,640]{1,0:T(8,128)(2,1)S(1)} %get-tuple-element.35), channel_id=1, source_target_pairs={{0,6},{1,7},{2,4},{3,5},{4,2},{5,3},{6,0},{7,1},{8,14},{9,15},{10,... | collective-permute-start | bytes 245768 | tf_op jit(solution)/shard_map/ppermute | solution.py:458
  6.3 7.9 %collective-permute-start.3 = (bf16[64,640]{1,0:T(8,128)(2,1)S(1)}, bf16[64,640]{1,0:T(8,128)(2,1)S(1)}, u32[]{:S(2)}, u32[]{:S(2)}) collective-permute-start(bf16[64,640]{1,0:T(8,128)(2,1)S(1)} %get-tuple-element.39), channel_id=1, source_target_pairs={{0,7},{1,6},{2,5},{3,4},{4,3},{5,2},{6,1},{7,0},{8,15},{9,14},{10,... | collective-permute-start | bytes 245768 | tf_op jit(solution)/shard_map/ppermute | solution.py:458
  7.8 9.1 %collective-permute-start.4 = (bf16[64,640]{1,0:T(8,128)(2,1)S(1)}, bf16[64,640]{1,0:T(8,128)(2,1)S(1)}, u32[]{:S(2)}, u32[]{:S(2)}) collective-permute-start(bf16[64,640]{1,0:T(8,128)(2,1)S(1)} %get-tuple-element.40), channel_id=1, source_target_pairs={{0,3},{1,2},{2,1},{3,0},{4,7},{5,6},{6,5},{7,4},{8,11},{9,10},{10,... | collective-permute-start | bytes 245768 | tf_op jit(solution)/shard_map/ppermute | solution.py:458
  9.5 7.5 %collective-permute-start.5 = (bf16[64,640]{1,0:T(8,128)(2,1)S(1)}, bf16[64,640]{1,0:T(8,128)(2,1)S(1)}, u32[]{:S(2)}, u32[]{:S(2)}) collective-permute-start(bf16[64,640]{1,0:T(8,128)(2,1)S(1)} %get-tuple-element.41), channel_id=1, source_target_pairs={{0,5},{1,4},{2,7},{3,6},{4,1},{5,0},{6,3},{7,2},{8,13},{9,12},{10,... | collective-permute-start | bytes 245768 | tf_op jit(solution)/shard_map/ppermute | solution.py:458
  9.9 7.1 %collective-permute-start.6 = (bf16[64,640]{1,0:T(8,128)(2,1)S(1)}, bf16[64,640]{1,0:T(8,128)(2,1)S(1)}, u32[]{:S(2)}, u32[]{:S(2)}) collective-permute-start(bf16[64,640]{1,0:T(8,128)(2,1)S(1)} %get-tuple-element.42), channel_id=1, source_target_pairs={{0,1},{1,0},{2,3},{3,2},{4,5},{5,4},{6,7},{7,6},{8,9},{9,8},{10,11... | collective-permute-start | bytes 245768 | tf_op jit(solution)/shard_map/ppermute | solution.py:458
  12.4 9.4 %collective-permute-start.11 = (bf16[800,128]{1,0:T(8,128)(2,1)S(1)}, bf16[800,128]{1,0:T(8,128)(2,1)S(1)}, u32[]{:S(2)}, u32[]{:S(2)}) collective-permute-start(bf16[800,128]{1,0:T(8,128)(2,1)S(1)} %get-tuple-element.44), channel_id=1, source_target_pairs={{0,8},{1,25},{2,10},{3,27},{4,12},{5,29},{6,14},{7,31},{8,16},{9,1... | collective-permute-start | bytes 614408 | tf_op jit(solution)/shard_map/ppermute | solution.py:467
  14.3 9.8 %collective-permute-start.10 = (bf16[400,128]{1,0:T(8,128)(2,1)S(1)}, bf16[400,128]{1,0:T(8,128)(2,1)S(1)}, u32[]{:S(2)}, u32[]{:S(2)}) collective-permute-start(bf16[400,128]{1,0:T(8,128)(2,1)S(1)} %get-tuple-element.43.rest_8_), channel_id=1, source_target_pairs={{0,16},{1,17},{2,18},{3,19},{4,20},{5,21},{6,22},{7,23},{8,24},{9,... | collective-permute-start | bytes 307208 | tf_op jit(solution)/shard_map/ppermute | solution.py:467
  18.3 7.8 %collective-permute-start.8 = (bf16[640,128]{1,0:T(8,128)(2,1)S(1)}, bf16[640,128]{1,0:T(8,128)(2,1)S(1)}, u32[]{:S(2)}, u32[]{:S(2)}) collective-permute-start(bf16[640,128]{1,0:T(8,128)(2,1)S(1)} %attend.1.token_ref.own), channel_id=1, source_target_pairs={{0,4},{1,5},{2,6},{3,7},{4,0},{5,1},{6,2},{7,3},{8,12},{9,13},{10,... | collective-permute-start | bytes 491528 | tf_op jit(solution)/shard_map/ppermute | solution.py:458
  18.4 7.2 %collective-permute-start.9 = (bf16[640,128]{1,0:T(8,128)(2,1)S(1)}, bf16[640,128]{1,0:T(8,128)(2,1)S(1)}, u32[]{:S(2)}, u32[]{:S(2)}) collective-permute-start(bf16[640,128]{1,0:T(8,128)(2,1)S(1)} %attend.1.token_ref.own), channel_id=1, source_target_pairs={{0,2},{1,3},{2,0},{3,1},{4,6},{5,7},{6,4},{7,5},{8,10},{9,11},{10,... | collective-permute-start | bytes 491528 | tf_op jit(solution)/shard_map/ppermute | solution.py:458
  19.5 9.1 %collective-permute-start.7 = (bf16[640,128]{1,0:T(8,128)(2,1)S(1)}, bf16[640,128]{1,0:T(8,128)(2,1)S(1)}, u32[]{:S(2)}, u32[]{:S(2)}) collective-permute-start(bf16[640,128]{1,0:T(8,128)(2,1)S(1)} %attend.1.token_ref.own), channel_id=1, source_target_pairs={{0,6},{1,7},{2,4},{3,5},{4,2},{5,3},{6,0},{7,1},{8,14},{9,15},{10,... | collective-permute-start | bytes 491528 | tf_op jit(solution)/shard_map/ppermute | solution.py:458
  21.9 4.1 %collective-permute-start.12 = (bf16[800,128]{1,0:T(8,128)(2,1)S(1)}, bf16[800,128]{1,0:T(8,128)(2,1)S(1)}, u32[]{:S(2)}, u32[]{:S(2)}) collective-permute-start(bf16[800,128]{1,0:T(8,128)(2,1)S(1)} %collective-permute-done.11.rest_10_), channel_id=1, source_target_pairs={{0,1},{1,0},{2,3},{3,2},{4,5},{5,4},{6,7},{7,6},{8,9},{9,8},{10,11... | collective-permute-start | bytes 614408 | tf_op jit(solution)/shard_map/ppermute | solution.py:458
  25.4 3.3 %collective-permute-start.14 = (bf16[640,128]{1,0:T(8,128)(2,1)S(1)}, bf16[640,128]{1,0:T(8,128)(2,1)S(1)}, u32[]{:S(2)}, u32[]{:S(2)}) collective-permute-start(bf16[640,128]{1,0:T(8,128)(2,1)S(1)} %attend.1.token_ref.own), channel_id=1, source_target_pairs={{0,1},{1,0},{2,3},{3,2},{4,5},{5,4},{6,7},{7,6},{8,9},{9,8},{10,11... | collective-permute-start | bytes 491528 | tf_op jit(solution)/shard_map/ppermute | solution.py:458
  25.6 3.1 %collective-permute-start.16 = (bf16[640,128]{1,0:T(8,128)(2,1)S(1)}, bf16[640,128]{1,0:T(8,128)(2,1)S(1)}, u32[]{:S(2)}, u32[]{:S(2)}) collective-permute-start(bf16[640,128]{1,0:T(8,128)(2,1)S(1)} %collective-permute-done.9.x), channel_id=1, source_target_pairs={{0,1},{1,0},{2,3},{3,2},{4,5},{5,4},{6,7},{7,6},{8,9},{9,8},{10,11... | collective-permute-start | bytes 491528 | tf_op jit(solution)/shard_map/ppermute | solution.py:458
  26.1 2.6 %collective-permute-start.15 = (bf16[640,128]{1,0:T(8,128)(2,1)S(1)}, bf16[640,128]{1,0:T(8,128)(2,1)S(1)}, u32[]{:S(2)}, u32[]{:S(2)}) collective-permute-start(bf16[640,128]{1,0:T(8,128)(2,1)S(1)} %collective-permute-done.8.y), channel_id=1, source_target_pairs={{0,1},{1,0},{2,3},{3,2},{4,5},{5,4},{6,7},{7,6},{8,9},{9,8},{10,11... | collective-permute-start | bytes 491528 | tf_op jit(solution)/shard_map/ppermute | solution.py:458
  28.6 1.4 %collective-permute-start.13 = (bf16[640,128]{1,0:T(8,128)(2,1)S(1)}, bf16[640,128]{1,0:T(8,128)(2,1)S(1)}, u32[]{:S(2)}, u32[]{:S(2)}) collective-permute-start(bf16[640,128]{1,0:T(8,128)(2,1)S(1)} %collective-permute-done.7.rest_0_), channel_id=1, source_target_pairs={{0,1},{1,0},{2,3},{3,2},{4,5},{5,4},{6,7},{7,6},{8,9},{9,8},{10,11... | collective-permute-start | bytes 491528 | tf_op jit(solution)/shard_map/ppermute | solution.py:458
  30.7 6.4 %collective-permute-start.17 = (bf16[656,128]{1,0:T(8,128)(2,1)S(1)}, bf16[656,128]{1,0:T(8,128)(2,1)S(1)}, u32[]{:S(2)}, u32[]{:S(2)}) collective-permute-start(bf16[656,128]{1,0:T(8,128)(2,1)S(1)} %project.1.token_ref.own.rest_0_), channel_id=1, source_target_pairs={{0,4},{1,5},{2,6},{3,7},{4,0},{5,1},{6,2},{7,3},{8,12},{9,13},{10,... | collective-permute-start | bytes 503816 | tf_op jit(solution)/shard_map/ppermute | solution.py:458
  31.1 7.2 %collective-permute-start.18 = (bf16[656,128]{1,0:T(8,128)(2,1)S(1)}, bf16[656,128]{1,0:T(8,128)(2,1)S(1)}, u32[]{:S(2)}, u32[]{:S(2)}) collective-permute-start(bf16[656,128]{1,0:T(8,128)(2,1)S(1)} %project.1.token_ref.own.rest_0_), channel_id=1, source_target_pairs={{0,2},{1,3},{2,0},{3,1},{4,6},{5,7},{6,4},{7,5},{8,10},{9,11},{10,... | collective-permute-start | bytes 503816 | tf_op jit(solution)/shard_map/ppermute | solution.py:458
  31.9 10.0 %collective-permute-start.22 = (bf16[656,128]{1,0:T(8,128)(2,1)S(1)}, bf16[656,128]{1,0:T(8,128)(2,1)S(1)}, u32[]{:S(2)}, u32[]{:S(2)}) collective-permute-start(bf16[656,128]{1,0:T(8,128)(2,1)S(1)} %project.1.token_ref.own.rest_0_), channel_id=1, source_target_pairs={{0,6},{1,7},{2,4},{3,5},{4,2},{5,3},{6,0},{7,1},{8,14},{9,15},{10,... | collective-permute-start | bytes 503816 | tf_op jit(solution)/shard_map/ppermute | solution.py:458
  35.6 3.3 %collective-permute-start.19 = (bf16[656,128]{1,0:T(8,128)(2,1)S(1)}, bf16[656,128]{1,0:T(8,128)(2,1)S(1)}, u32[]{:S(2)}, u32[]{:S(2)}) collective-permute-start(bf16[656,128]{1,0:T(8,128)(2,1)S(1)} %project.1.token_ref.own.rest_0_), channel_id=1, source_target_pairs={{0,1},{1,0},{2,3},{3,2},{4,5},{5,4},{6,7},{7,6},{8,9},{9,8},{10,11... | collective-permute-start | bytes 503816 | tf_op jit(solution)/shard_map/ppermute | solution.py:458
  37.1 4.8 %collective-permute-start.20 = (bf16[656,128]{1,0:T(8,128)(2,1)S(1)}, bf16[656,128]{1,0:T(8,128)(2,1)S(1)}, u32[]{:S(2)}, u32[]{:S(2)}) collective-permute-start(bf16[656,128]{1,0:T(8,128)(2,1)S(1)} %collective-permute-done.17.y.rest_1_), channel_id=1, source_target_pairs={{0,1},{1,0},{2,3},{3,2},{4,5},{5,4},{6,7},{7,6},{8,9},{9,8},{10,11... | collective-permute-start | bytes 503816 | tf_op jit(solution)/shard_map/ppermute | solution.py:458
  38.3 3.6 %collective-permute-start.21 = (bf16[656,128]{1,0:T(8,128)(2,1)S(1)}, bf16[656,128]{1,0:T(8,128)(2,1)S(1)}, u32[]{:S(2)}, u32[]{:S(2)}) collective-permute-start(bf16[656,128]{1,0:T(8,128)(2,1)S(1)} %collective-permute-done.18.x.rest_2_), channel_id=1, source_target_pairs={{0,1},{1,0},{2,3},{3,2},{4,5},{5,4},{6,7},{7,6},{8,9},{9,8},{10,11... | collective-permute-start | bytes 503816 | tf_op jit(solution)/shard_map/ppermute | solution.py:458
  41.9 1.4 %collective-permute-start.23 = (bf16[656,128]{1,0:T(8,128)(2,1)S(1)}, bf16[656,128]{1,0:T(8,128)(2,1)S(1)}, u32[]{:S(2)}, u32[]{:S(2)}) collective-permute-start(bf16[656,128]{1,0:T(8,128)(2,1)S(1)} %collective-permute-done.22.rest_6_), channel_id=1, source_target_pairs={{0,1},{1,0},{2,3},{3,2},{4,5},{5,4},{6,7},{7,6},{8,9},{9,8},{10,11... | collective-permute-start | bytes 503816 | tf_op jit(solution)/shard_map/ppermute | solution.py:458
  (2 other events, 15.4 us)

commit v13 on v12

--- a/solution.py
+++ b/solution.py
@@ -244,25 +244,20 @@
 def ready_kernel(select_ref, gain_hbm, token_ref, *rest):
     del token_ref
     blocks = rest[:ROWS]
-    own_ref, across_ref, near_ref = rest[ROWS : ROWS + 3]
+    own_ref, near_ref = rest[ROWS : ROWS + 2]
     resid_ref, gain_out, main_ref, tail_ref, held, line, sem = rest[-7:]
     fetch = pltpu.make_async_copy(gain_hbm, line, sem)
     fetch.start()
     me = row_index()
-    page = lax.axis_index("page")
     band = blocks[0].shape[0]
     for step, block in zip(BLOCK_ORDER, blocks):
         at = pl.ds(pl.multiple_of((me ^ step) * band, band), band)
         held[at, :] = block[:, 3 * HPAIR :]
     resid_ref[...] = jnp.dot(select_ref[...], held[...], preferred_element_type=F32)
-    main_ref[...] = jnp.zeros_like(main_ref)
-    tail_ref[...] = jnp.zeros_like(tail_ref)
     core = me % 2
     size = own_ref.shape[0]
     half = pl.ds(pl.multiple_of(core * size, 16), size)
-    cuts = ((0, own_ref[...]), (2, across_ref[...]), (3 - 2 * core, near_ref[half, :]))
-    for step, cut in cuts:
-        place_rows(weight_rows(cut), 2 * lax.rem(page + step, PAGES), main_ref, tail_ref)
+    place_slices([(0, own_ref[...]), (3 - 2 * core, near_ref[half, :])], main_ref, tail_ref)
     fetch.wait()
     whole = line[...].reshape(1, D)
     gain = jnp.zeros(gain_out.shape, F32)
@@ -273,12 +268,18 @@
     gain_out[...] = gain
 
 
-def last_kernel(swapped_ref, token_ref, main_ref, tail_ref):
+def place_slices(cuts, main_ref, tail_ref):
+    tail_ref[...] = jnp.zeros_like(tail_ref)
+    for step, cut in cuts:
+        place_rows(weight_rows(cut), 2 * lax.rem(lax.axis_index("page") + step, PAGES), main_ref, tail_ref)
+
+
+def last_kernel(across_ref, swapped_ref, token_ref, main_ref, tail_ref):
     del token_ref
-    size = swapped_ref.shape[0] // 2
-    cut = swapped_ref[pl.ds(pl.multiple_of(row_index() % 2 * size, 16), size), :]
-    tail_ref[...] = jnp.zeros_like(tail_ref)
-    place_rows(weight_rows(cut), 0, main_ref, tail_ref)
+    core = row_index() % 2
+    size = across_ref.shape[0]
+    half = pl.ds(pl.multiple_of(core * size, 16), size)
+    place_slices([(2, across_ref[...]), (1 + 2 * core, swapped_ref[half, :])], main_ref, tail_ref)
 
 
 def far_block():
@@ -293,8 +294,9 @@
     return jnp.concatenate([left, right], axis=1)
 
 
-def late_source():
-    return lax.rem(lax.axis_index("page") + 1 + 2 * (row_index() % 2), PAGES)
+def came_last(block):
+    page, core = lax.axis_index("page"), row_index() % 2
+    return (block == lax.rem(page + 2, PAGES)) | (block == lax.rem(page + 1 + 2 * core, PAGES))
 
 
 def add_features(steps, pieces, weights, before_ref, out_ref):
@@ -306,10 +308,9 @@
     for step in steps:
         pair = me ^ step
         columns = pl.ds(pl.multiple_of(pair * WIDE, WIDE), WIDE)
-        late = pl.ds(pl.multiple_of(pair % 2 * WIDE, WIDE), WIDE)
-        is_late = pair // 2 == late_source()
-        mains.append(jnp.where(is_late, last_main_ref[late, :], main_ref[columns, :]))
-        tails.append([jnp.where(is_late, last_tail_ref[at, late, :], tail_ref[at, columns, :]) for at in range(4)])
+        is_last = came_last(pair // 2)
+        mains.append(jnp.where(is_last, last_main_ref[columns, :], main_ref[columns, :]))
+        tails.append([jnp.where(is_last, last_tail_ref[at, columns, :], tail_ref[at, columns, :]) for at in range(4)])
     rows = jnp.concatenate([piece[...] for piece in pieces], axis=1)
     base = before_ref[...] + jnp.dot(rows[:patches], jnp.concatenate(mains, axis=0), preferred_element_type=F32)
     for corner in range(4):
@@ -331,9 +332,9 @@
     patches = base_ref.shape[0]
     groups = patches // 4
     block = far_block()
-    is_last = late_source() == (row_index() // 2 ^ 3)
+    is_last = came_last(row_index() // 2 ^ 3)
     full = collect_late(same, other)
-    main = jnp.where(is_last, last_main_ref[...], main_ref[block, :])
+    main = jnp.where(is_last, last_main_ref[block, :], main_ref[block, :])
     base = base_ref[...] + jnp.dot(full[:patches], main, preferred_element_type=F32)
     ones = jnp.ones((NOTES, HPAIR), BF16)
     contract = (((1,), (1,)), ((), ()))
@@ -342,7 +343,7 @@
     ends = []
     for corner in range(4):
         span = slice(corner * groups, (corner + 1) * groups)
-        tail = jnp.where(is_last, last_tail_ref[corner], tail_ref[corner, block, :])
+        tail = jnp.where(is_last, last_tail_ref[corner, block, :], tail_ref[corner, block, :])
         hidden = base[span] + jnp.dot(full[patches:], tail, preferred_element_type=F32)
         square = hidden * hidden
         high = square.astype(BF16)
@@ -508,7 +509,6 @@
         count=1 + 3,
         moved=1 << 20,
     )(grid, *blocks[1:4])
-    across = turn(after(own, *()), 2, 2)
     near = turn(after(chip, *()), 1, PAGES - 1)
     swapped = swap(near, 1)
     attn = kernel(
@@ -520,29 +520,31 @@
         flops=20 * patches * patches * 4096,
         moved=1 << 20,
     )(select, dead, *blocks)
+    across = turn(after(own, attn), 2, 2)
     resid, own_gain, main, tail = kernel(
         ready_kernel,
         "ready",
         [shape(patches, HPAIR, dtype=F32), shape(1, HPAIR, dtype=F32), shape(MAIN, HPAIR), shape(4, MAIN, HPAIR)],
         [pltpu.VMEM((patches, HPAIR), BF16), pltpu.VMEM((D,), F32), pltpu.SemaphoreType.DMA],
         fetched=(1, 2),
-        count=3 + ROWS + 3,
+        count=3 + ROWS + 2,
         flops=10 * patches * patches * 4096,
         moved=4 << 20,
-    )(select, in_hbm(norm_gain), attn, *blocks, own, across, near)
+    )(select, in_hbm(norm_gain), attn, *blocks, own, near)
     last = kernel(
         last_kernel,
         "ready_last",
-        [shape(2 * WIDE, HPAIR), shape(4, 2 * WIDE, HPAIR)],
-        fetched=(1,),
-        count=2,
-        moved=4 << 20,
-    )(swapped, main)
+        [shape(MAIN, HPAIR), shape(4, MAIN, HPAIR)],
+        fetched=(2,),
+        count=3,
+        flops=1,
+        moved=1,
+    )(across, swapped, main)
     y, x, far = [swap(attn, step) for step in (4, 2, 6)]
     weights = (main, tail, *last)
     rows = shape(patches, HPAIR, dtype=F32)
     first = kernel(project_first_kernel, "project_first", rows, count=8, flops=1, moved=1)(attn, y, x, *weights, resid)
-    near = [swap(after(attn, main), 1), swap(after(y, last[0]), 1), swap(x, 1)]
+    near = [swap(after(attn, last[0]), 1), swap(y, 1), swap(x, 1)]
     second = kernel(project_second_kernel, "project_second", rows, count=8, flops=1, moved=1)(*near, *weights, first)
     hidden = kernel(
         project_kernel,
@@ -551,7 +553,7 @@
         count=2 + 6,
         flops=patches * MAIN * 256,
         moved=4 << 20,
-    )(far, swap(after(far, first), 1), second, *weights, own_gain)
+    )(far, swap(far, 1), second, *weights, own_gain)
     ends, bias = kernel(
         tail_kernel,
         "merge_tail",

time: 45.1 us -> 44.4 us (0.984)
  waiting for transfers between devices: 14.2 us -> 12.7 us
  starting transfers between devices: 19.8 us -> 20.4 us
    ppermute x22, waiting for transfers between devices: 11.9 us -> 10.2 us  [swap(): lax.ppermute(value, 'row', [(row, row ^ step) for row in range(ROWS)])]
    ppermute x22, starting transfers between devices: 15.5 us -> 16.1 us  [swap(): lax.ppermute(value, 'row', [(row, row ^ step) for row in range(ROWS)])]
  transfers between devices with their start and end apart: 24 -> 24, of which waited for: 10 -> 9; matrix products, arithmetic and copies ran while one was open for 0% -> 0% of each run, Pallas kernels for 15% -> 15%
where the time goes in v13:
time: 44.4 us; the launch traced here: 44.3 us
  starting transfers between devices  20.4 us (46%)
  waiting for transfers between devices  12.7 us (29%)
  Pallas kernels  10.9 us (25%)
    ppermute x22, starting transfers between devices, swap(): lax.ppermute(value, 'row', [(row, row ^ step) for row in range(ROWS)])  16.1 us
    ppermute x22, waiting for transfers between devices, swap(): lax.ppermute(value, 'row', [(row, row ^ step) for row in range(ROWS)])  10.2 us
    ppermute x2, starting transfers between devices, turn(): return lax.ppermute(value, ('page', 'row'), pairs)  4.28 us
    ppermute x2, waiting for transfers between devices, turn(): return lax.ppermute(value, ('page', 'row'), pairs)  2.58 us
    pallas_call x1, Pallas kernels, local_eight(): kernel(spread_kernel, 'spread', [shape(band, 4 * HPAIR)] * ROWS + [shape(...  1.76 us
    pallas_call x1, Pallas kernels, local_eight(): kernel(merge_kernel, 'merge', shape(1, units, groups), [pltpu.VMEM((group...  1.7 us
    pallas_call x1, Pallas kernels, local_eight(): kernel(tail_kernel, 'merge_tail', [shape(units, MAIN), shape(units, 1, dt...  1.39 us
    pallas_call x1, Pallas kernels, local_eight(): kernel(attend_kernel, 'attend', shape(piece, WIDE), [pltpu.VMEM((patches,...  1.34 us
  transfers between devices with their start and end apart: 24, of which 9 were waited for; matrix products, arithmetic and copies ran while one was open for 0% of the time, Pallas kernels for 15%

profile of v13, /device:TPU:0, one launch (start us, length us, event | category | flops | bytes accessed | tf_op | source)
XLA Modules:
  0.0 44.3 jit_solution(1885292322140353837)
XLA Ops:
  0.0 1.8 %spread.1 = (bf16[64,640]{1,0:T(8,128)(2,1)S(1)}, bf16[64,640]{1,0:T(8,128)(2,1)S(1)}, bf16[64,640]{1,0:T(8,128)(2,1)S(1)}, bf16[64,640]{1,0:T(8,128)(2,1)S(1)},...) custom-call(bf16[1,64,3840]{2,1,0:T(8,128)(2,1)} %qkv_hbm.1, ...), custom_call_target="tpu_custom_call" | custom-call | bytes 1048576 | tf_op jit(solution)/shard_map/spread/pallas_call | solution.py:484
  1.8 3.0 %collective-permute-start = (bf16[64,640]{1,0:T(8,128)(2,1)S(1)}, bf16[64,640]{1,0:T(8,128)(2,1)S(1)}, u32[]{:S(2)}, u32[]{:S(2)}) collective-permute-start(bf16[64,640]{1,0:T(8,128)(2,1)S(1)} %get-tuple-element.32), channel_id=1, source_target_pairs={{0,4},{1,5},{2,6},{3,7},{4,0},{5,1},{6,2},{7,3},{8,12},{9,13},{10,... | collective-permute-start | bytes 245768 | tf_op jit(solution)/shard_map/ppermute | solution.py:459
  4.8 1.5 %collective-permute-start.1 = (bf16[64,640]{1,0:T(8,128)(2,1)S(1)}, bf16[64,640]{1,0:T(8,128)(2,1)S(1)}, u32[]{:S(2)}, u32[]{:S(2)}) collective-permute-start(bf16[64,640]{1,0:T(8,128)(2,1)S(1)} %get-tuple-element.33), channel_id=1, source_target_pairs={{0,2},{1,3},{2,0},{3,1},{4,6},{5,7},{6,4},{7,5},{8,10},{9,11},{10,... | collective-permute-start | bytes 245768 | tf_op jit(solution)/shard_map/ppermute | solution.py:459
  6.3 1.5 %collective-permute-start.3 = (bf16[64,640]{1,0:T(8,128)(2,1)S(1)}, bf16[64,640]{1,0:T(8,128)(2,1)S(1)}, u32[]{:S(2)}, u32[]{:S(2)}) collective-permute-start(bf16[64,640]{1,0:T(8,128)(2,1)S(1)} %get-tuple-element.38), channel_id=1, source_target_pairs={{0,7},{1,6},{2,5},{3,4},{4,3},{5,2},{6,1},{7,0},{8,15},{9,14},{10,... | collective-permute-start | bytes 245768 | tf_op jit(solution)/shard_map/ppermute | solution.py:459
  7.8 1.6 %collective-permute-start.4 = (bf16[64,640]{1,0:T(8,128)(2,1)S(1)}, bf16[64,640]{1,0:T(8,128)(2,1)S(1)}, u32[]{:S(2)}, u32[]{:S(2)}) collective-permute-start(bf16[64,640]{1,0:T(8,128)(2,1)S(1)} %get-tuple-element.39), channel_id=1, source_target_pairs={{0,3},{1,2},{2,1},{3,0},{4,7},{5,6},{6,5},{7,4},{8,11},{9,10},{10,... | collective-permute-start | bytes 245768 | tf_op jit(solution)/shard_map/ppermute | solution.py:459
  9.9 2.6 %collective-permute-done.2.rest_2_.rest_3_ = bf16[64,640]{1,0:T(8,128)(2,1)S(1)} collective-permute-done((bf16[64,640]{1,0:T(8,128)(2,1)S(1)}, bf16[64,640]{1,0:T(8,128)(2,1)S(1)}, u32[]{:S(2)}, u32[]{:S(2)}) %collective-permute-start.2) | collective-permute-done | bytes 81952 | tf_op jit(solution)/shard_map/ppermute | solution.py:459
  12.4 1.7 %collective-permute-start.10 = (bf16[800,128]{1,0:T(8,128)(2,1)S(1)}, bf16[800,128]{1,0:T(8,128)(2,1)S(1)}, u32[]{:S(2)}, u32[]{:S(2)}) collective-permute-start(bf16[800,128]{1,0:T(8,128)(2,1)S(1)} %get-tuple-element.44), channel_id=1, source_target_pairs={{0,8},{1,25},{2,10},{3,27},{4,12},{5,29},{6,14},{7,31},{8,16},{9,1... | collective-permute-start | bytes 614408 | tf_op jit(solution)/shard_map/ppermute | solution.py:468
  14.3 0.8 %collective-permute-done.5.rest_6_ = bf16[64,640]{1,0:T(8,128)(2,1)S(1)} collective-permute-done((bf16[64,640]{1,0:T(8,128)(2,1)S(1)}, bf16[64,640]{1,0:T(8,128)(2,1)S(1)}, u32[]{:S(2)}, u32[]{:S(2)}) %collective-permute-start.5) | collective-permute-done | bytes 81952 | tf_op jit(solution)/shard_map/ppermute | solution.py:459
  15.1 1.3 %attend.1.token_ref.own = bf16[640,128]{1,0:T(8,128)(2,1)S(1)} custom-call(bf16[512,512]{1,0:T(8,128)(2,1)S(1)} %get-tuple-element.35.select_ref, f32[1,512]{1,0:T(1,128)S(1)} %get-tuple-element.36.dead_ref, bf16[64,640]{1,0:T(8,128)(2,1)S(1)} %get-tuple-element.37.rest_0_, bf16[64,640]{1,0:T(8,128)(2,1)S(1)} %collective-permute-done.rest_0_.rest_1_, ...), custom_call_target="tpu_custom_call" | custom-call | flops 21474836480 | bytes 1048576 | tf_op jit(solution)/shard_map/attend/pallas_call | solution.py:514
  17.1 1.3 %collective-permute-start.15 = (bf16[640,128]{1,0:T(8,128)(2,1)S(1)}, bf16[640,128]{1,0:T(8,128)(2,1)S(1)}, u32[]{:S(2)}, u32[]{:S(2)}) collective-permute-start(bf16[640,128]{1,0:T(8,128)(2,1)S(1)} %attend.1.token_ref.own), channel_id=1, source_target_pairs={{0,2},{1,3},{2,0},{3,1},{4,6},{5,7},{6,4},{7,5},{8,10},{9,11},{10,... | collective-permute-start | bytes 491528 | tf_op jit(solution)/shard_map/ppermute | solution.py:459
  18.3 1.6 %collective-permute-start.7 = (bf16[640,128]{1,0:T(8,128)(2,1)S(1)}, bf16[640,128]{1,0:T(8,128)(2,1)S(1)}, u32[]{:S(2)}, u32[]{:S(2)}) collective-permute-start(bf16[640,128]{1,0:T(8,128)(2,1)S(1)} %attend.1.token_ref.own), channel_id=1, source_target_pairs={{0,6},{1,7},{2,4},{3,5},{4,2},{5,3},{6,0},{7,1},{8,14},{9,15},{10,... | collective-permute-start | bytes 491528 | tf_op jit(solution)/shard_map/ppermute | solution.py:459
  20.0 2.6 %collective-permute-start.9 = (bf16[400,128]{1,0:T(8,128)(2,1)S(1)}, bf16[400,128]{1,0:T(8,128)(2,1)S(1)}, u32[]{:S(2)}, u32[]{:S(2)}) collective-permute-start(bf16[400,128]{1,0:T(8,128)(2,1)S(1)} %get-tuple-element.43.rest_8_), channel_id=1, source_target_pairs={{0,16},{1,17},{2,18},{3,19},{4,20},{5,21},{6,22},{7,23},{8,24},{9,... | collective-permute-start | bytes 307208 | tf_op jit(solution)/shard_map/ppermute | solution.py:468
  22.6 1.3 %ready.1 = (f32[512,160]{1,0:T(8,128)S(1)}, f32[1,160]{1,0:T(1,128)S(1)}, bf16[1024,160]{1,0:T(8,128)(2,1)S(1)}, bf16[4,1024,160]{2,1,0:T(8,128)(2,1)S(1)}) custom-call(bf16[512,512]{1,0:T(8,128)(2,1)S(1)} %get-tuple-element.35.select_ref, f32[1280]{0:T(1024)} %gain_hbm.1, bf16[640,128]{1,0:T(8,128)(2,1)S(1)} %attend.1.token_ref.own, ...), custom_call_target="tpu_custom_call" | custom-call | flops 10737418240 | bytes 4194304 | tf_op jit(solution)/shard_map/ready/pallas_call | solution.py:524
  24.6 2.6 %collective-permute-done.9.across_ref = bf16[400,128]{1,0:T(8,128)(2,1)S(1)} collective-permute-done((bf16[400,128]{1,0:T(8,128)(2,1)S(1)}, bf16[400,128]{1,0:T(8,128)(2,1)S(1)}, u32[]{:S(2)}, u32[]{:S(2)}) %collective-permute-start.9) | collective-permute-done | bytes 102432 | tf_op jit(solution)/shard_map/ppermute | solution.py:468
  29.3 0.7 %project.1.token_ref.own.rest_0_ = bf16[656,128]{1,0:T(8,128)(2,1)S(1)} custom-call(bf16[640,128]{1,0:T(8,128)(2,1)S(1)} %collective-permute-done.7.rest_0_, bf16[640,128]{1,0:T(8,128)(2,1)S(1)} %collective-permute-done.8.rest_1_, f32[512,160]{1,0:T(8,128)S(1)} %project_second.1.rest_2_, bf16[1024,160]{1,0:T(8,128)(2,1)S(1)} %get-tuple-element.45.token_ref.rest_0_.rest_3_, ...), custom_call_target="tpu_custom_call" | custom-call | flops 134217728 | bytes 4194304 | tf_op jit(solution)/shard_map/project/pallas_call | solution.py:549
  30.6 1.3 %collective-permute-start.18 = (bf16[656,128]{1,0:T(8,128)(2,1)S(1)}, bf16[656,128]{1,0:T(8,128)(2,1)S(1)}, u32[]{:S(2)}, u32[]{:S(2)}) collective-permute-start(bf16[656,128]{1,0:T(8,128)(2,1)S(1)} %project.1.token_ref.own.rest_0_), channel_id=1, source_target_pairs={{0,2},{1,3},{2,0},{3,1},{4,6},{5,7},{6,4},{7,5},{8,10},{9,11},{10,... | collective-permute-start | bytes 503816 | tf_op jit(solution)/shard_map/ppermute | solution.py:459
  31.9 1.6 %collective-permute-start.22 = (bf16[656,128]{1,0:T(8,128)(2,1)S(1)}, bf16[656,128]{1,0:T(8,128)(2,1)S(1)}, u32[]{:S(2)}, u32[]{:S(2)}) collective-permute-start(bf16[656,128]{1,0:T(8,128)(2,1)S(1)} %project.1.token_ref.own.rest_0_), channel_id=1, source_target_pairs={{0,6},{1,7},{2,4},{3,5},{4,2},{5,3},{6,0},{7,1},{8,14},{9,15},{10,... | collective-permute-start | bytes 503816 | tf_op jit(solution)/shard_map/ppermute | solution.py:459
  33.5 1.4 %merge_tail.1 = (bf16[640,1024]{1,0:T(8,128)(2,1)S(1)}, f32[640,1]{1,0:T(8,128)S(1)}) custom-call(bf16[640,5120]{1,0:T(8,128)(2,1)S(1)} %bitcast.1, f32[640]{0:T(1024)} %bias_hbm.1, bf16[656,128]{1,0:T(8,128)(2,1)S(1)} %project.1.token_ref.own.rest_0_), custom_call_target="tpu_custom_call" | custom-call | bytes 4194304 | tf_op jit(solution)/shard_map/merge_tail/pallas_call | solution.py:557
  35.0 1.4 %collective-permute-done.17.y.rest_1_ = bf16[656,128]{1,0:T(8,128)(2,1)S(1)} collective-permute-done((bf16[656,128]{1,0:T(8,128)(2,1)S(1)}, bf16[656,128]{1,0:T(8,128)(2,1)S(1)}, u32[]{:S(2)}, u32[]{:S(2)}) %collective-permute-start.17) | collective-permute-done | bytes 167968 | tf_op jit(solution)/shard_map/ppermute | solution.py:459
  36.4 1.4 %collective-permute-done.18.x.rest_2_ = bf16[656,128]{1,0:T(8,128)(2,1)S(1)} collective-permute-done((bf16[656,128]{1,0:T(8,128)(2,1)S(1)}, bf16[656,128]{1,0:T(8,128)(2,1)S(1)}, u32[]{:S(2)}, u32[]{:S(2)}) %collective-permute-start.18) | collective-permute-done | bytes 167968 | tf_op jit(solution)/shard_map/ppermute | solution.py:459
  37.8 0.7 %merge_first.1.before_ref = f32[4,640,128]{2,1,0:T(8,128)S(1)} custom-call(bf16[656,128]{1,0:T(8,128)(2,1)S(1)} %project.1.token_ref.own.rest_0_, bf16[656,128]{1,0:T(8,128)(2,1)S(1)} %collective-permute-done.17.y.rest_1_, bf16[656,128]{1,0:T(8,128)(2,1)S(1)} %collective-permute-done.18.x.rest_2_, bf16[640,5120]{1,0:T(8,128)(2,1)S(1)} %bitcast.1), custom_call_target="tpu_custom_call" | custom-call | flops 1 | bytes 1 | tf_op jit(solution)/shard_map/merge_first/pallas_call | solution.py:568
  38.5 2.6 %collective-permute-done.22.rest_6_ = bf16[656,128]{1,0:T(8,128)(2,1)S(1)} collective-permute-done((bf16[656,128]{1,0:T(8,128)(2,1)S(1)}, bf16[656,128]{1,0:T(8,128)(2,1)S(1)}, u32[]{:S(2)}, u32[]{:S(2)}) %collective-permute-start.22) | collective-permute-done | bytes 167968 | tf_op jit(solution)/shard_map/ppermute | solution.py:459
  41.2 0.7 %merge_second.1.rest_8_ = f32[4,640,128]{2,1,0:T(8,128)S(1)} custom-call(bf16[656,128]{1,0:T(8,128)(2,1)S(1)} %collective-permute-done.19.own.rest_3_, bf16[656,128]{1,0:T(8,128)(2,1)S(1)} %collective-permute-done.20.y.rest_4_, bf16[656,128]{1,0:T(8,128)(2,1)S(1)} %collective-permute-done.21.x.rest_5_, f32[4,640,128]{2,1,0:T(8,128)S(1)} %merge_first.1.before_ref, ...), custom_call_target="tpu_custom_call" | custom-call | flops 1 | bytes 1 | tf_op jit(solution)/shard_map/merge_second/pallas_call | solution.py:570
  42.6 1.7 %merge.1 = bf16[1,640,128]{2,1,0:T(8,128)(2,1)} custom-call(bf16[656,128]{1,0:T(8,128)(2,1)S(1)} %project.1.token_ref.own.rest_0_, bf16[656,128]{1,0:T(8,128)(2,1)S(1)} %collective-permute-done.17.y.rest_1_, bf16[656,128]{1,0:T(8,128)(2,1)S(1)} %collective-permute-done.18.x.rest_2_, bf16[656,128]{1,0:T(8,128)(2,1)S(1)} %collective-permute-done.19.own.rest_3_, ...), custom_call_target="tpu_custom_call" | custom-call | flops 335544320 | bytes 8388608 | tf_op jit(solution)/shard_map/merge/pallas_call | solution.py:571
  (41 shorter events, 5.4 us)
Async XLA Ops:
  1.8 7.7 %collective-permute-start = (bf16[64,640]{1,0:T(8,128)(2,1)S(1)}, bf16[64,640]{1,0:T(8,128)(2,1)S(1)}, u32[]{:S(2)}, u32[]{:S(2)}) collective-permute-start(bf16[64,640]{1,0:T(8,128)(2,1)S(1)} %get-tuple-element.32), channel_id=1, source_target_pairs={{0,4},{1,5},{2,6},{3,7},{4,0},{5,1},{6,2},{7,3},{8,12},{9,13},{10,... | collective-permute-start | bytes 245768 | tf_op jit(solution)/shard_map/ppermute | solution.py:459
  4.8 5.1 %collective-permute-start.1 = (bf16[64,640]{1,0:T(8,128)(2,1)S(1)}, bf16[64,640]{1,0:T(8,128)(2,1)S(1)}, u32[]{:S(2)}, u32[]{:S(2)}) collective-permute-start(bf16[64,640]{1,0:T(8,128)(2,1)S(1)} %get-tuple-element.33), channel_id=1, source_target_pairs={{0,2},{1,3},{2,0},{3,1},{4,6},{5,7},{6,4},{7,5},{8,10},{9,11},{10,... | collective-permute-start | bytes 245768 | tf_op jit(solution)/shard_map/ppermute | solution.py:459
  6.3 6.1 %collective-permute-start.2 = (bf16[64,640]{1,0:T(8,128)(2,1)S(1)}, bf16[64,640]{1,0:T(8,128)(2,1)S(1)}, u32[]{:S(2)}, u32[]{:S(2)}) collective-permute-start(bf16[64,640]{1,0:T(8,128)(2,1)S(1)} %get-tuple-element.34), channel_id=1, source_target_pairs={{0,6},{1,7},{2,4},{3,5},{4,2},{5,3},{6,0},{7,1},{8,14},{9,15},{10,... | collective-permute-start | bytes 245768 | tf_op jit(solution)/shard_map/ppermute | solution.py:459
  6.3 7.9 %collective-permute-start.3 = (bf16[64,640]{1,0:T(8,128)(2,1)S(1)}, bf16[64,640]{1,0:T(8,128)(2,1)S(1)}, u32[]{:S(2)}, u32[]{:S(2)}) collective-permute-start(bf16[64,640]{1,0:T(8,128)(2,1)S(1)} %get-tuple-element.38), channel_id=1, source_target_pairs={{0,7},{1,6},{2,5},{3,4},{4,3},{5,2},{6,1},{7,0},{8,15},{9,14},{10,... | collective-permute-start | bytes 245768 | tf_op jit(solution)/shard_map/ppermute | solution.py:459
  7.8 6.5 %collective-permute-start.4 = (bf16[64,640]{1,0:T(8,128)(2,1)S(1)}, bf16[64,640]{1,0:T(8,128)(2,1)S(1)}, u32[]{:S(2)}, u32[]{:S(2)}) collective-permute-start(bf16[64,640]{1,0:T(8,128)(2,1)S(1)} %get-tuple-element.39), channel_id=1, source_target_pairs={{0,3},{1,2},{2,1},{3,0},{4,7},{5,6},{6,5},{7,4},{8,11},{9,10},{10,... | collective-permute-start | bytes 245768 | tf_op jit(solution)/shard_map/ppermute | solution.py:459
  9.5 5.6 %collective-permute-start.5 = (bf16[64,640]{1,0:T(8,128)(2,1)S(1)}, bf16[64,640]{1,0:T(8,128)(2,1)S(1)}, u32[]{:S(2)}, u32[]{:S(2)}) collective-permute-start(bf16[64,640]{1,0:T(8,128)(2,1)S(1)} %get-tuple-element.40), channel_id=1, source_target_pairs={{0,5},{1,4},{2,7},{3,6},{4,1},{5,0},{6,3},{7,2},{8,13},{9,12},{10,... | collective-permute-start | bytes 245768 | tf_op jit(solution)/shard_map/ppermute | solution.py:459
  9.9 5.2 %collective-permute-start.6 = (bf16[64,640]{1,0:T(8,128)(2,1)S(1)}, bf16[64,640]{1,0:T(8,128)(2,1)S(1)}, u32[]{:S(2)}, u32[]{:S(2)}) collective-permute-start(bf16[64,640]{1,0:T(8,128)(2,1)S(1)} %get-tuple-element.41), channel_id=1, source_target_pairs={{0,1},{1,0},{2,3},{3,2},{4,5},{5,4},{6,7},{7,6},{8,9},{9,8},{10,11... | collective-permute-start | bytes 245768 | tf_op jit(solution)/shard_map/ppermute | solution.py:459
  12.4 10.2 %collective-permute-start.10 = (bf16[800,128]{1,0:T(8,128)(2,1)S(1)}, bf16[800,128]{1,0:T(8,128)(2,1)S(1)}, u32[]{:S(2)}, u32[]{:S(2)}) collective-permute-start(bf16[800,128]{1,0:T(8,128)(2,1)S(1)} %get-tuple-element.44), channel_id=1, source_target_pairs={{0,8},{1,25},{2,10},{3,27},{4,12},{5,29},{6,14},{7,31},{8,16},{9,1... | collective-permute-start | bytes 614408 | tf_op jit(solution)/shard_map/ppermute | solution.py:468
  16.4 7.5 %collective-permute-start.13 = (bf16[640,128]{1,0:T(8,128)(2,1)S(1)}, bf16[640,128]{1,0:T(8,128)(2,1)S(1)}, u32[]{:S(2)}, u32[]{:S(2)}) collective-permute-start(bf16[640,128]{1,0:T(8,128)(2,1)S(1)} %attend.1.token_ref.own), channel_id=1, source_target_pairs={{0,4},{1,5},{2,6},{3,7},{4,0},{5,1},{6,2},{7,3},{8,12},{9,13},{10,... | collective-permute-start | bytes 491528 | tf_op jit(solution)/shard_map/ppermute | solution.py:459
  17.1 7.4 %collective-permute-start.15 = (bf16[640,128]{1,0:T(8,128)(2,1)S(1)}, bf16[640,128]{1,0:T(8,128)(2,1)S(1)}, u32[]{:S(2)}, u32[]{:S(2)}) collective-permute-start(bf16[640,128]{1,0:T(8,128)(2,1)S(1)} %attend.1.token_ref.own), channel_id=1, source_target_pairs={{0,2},{1,3},{2,0},{3,1},{4,6},{5,7},{6,4},{7,5},{8,10},{9,11},{10,... | collective-permute-start | bytes 491528 | tf_op jit(solution)/shard_map/ppermute | solution.py:459
  18.3 9.1 %collective-permute-start.7 = (bf16[640,128]{1,0:T(8,128)(2,1)S(1)}, bf16[640,128]{1,0:T(8,128)(2,1)S(1)}, u32[]{:S(2)}, u32[]{:S(2)}) collective-permute-start(bf16[640,128]{1,0:T(8,128)(2,1)S(1)} %attend.1.token_ref.own), channel_id=1, source_target_pairs={{0,6},{1,7},{2,4},{3,5},{4,2},{5,3},{6,0},{7,1},{8,14},{9,15},{10,... | collective-permute-start | bytes 491528 | tf_op jit(solution)/shard_map/ppermute | solution.py:459
  20.0 7.2 %collective-permute-start.9 = (bf16[400,128]{1,0:T(8,128)(2,1)S(1)}, bf16[400,128]{1,0:T(8,128)(2,1)S(1)}, u32[]{:S(2)}, u32[]{:S(2)}) collective-permute-start(bf16[400,128]{1,0:T(8,128)(2,1)S(1)} %get-tuple-element.43.rest_8_), channel_id=1, source_target_pairs={{0,16},{1,17},{2,18},{3,19},{4,20},{5,21},{6,22},{7,23},{8,24},{9,... | collective-permute-start | bytes 307208 | tf_op jit(solution)/shard_map/ppermute | solution.py:468
  22.6 4.5 %collective-permute-start.11 = (bf16[800,128]{1,0:T(8,128)(2,1)S(1)}, bf16[800,128]{1,0:T(8,128)(2,1)S(1)}, u32[]{:S(2)}, u32[]{:S(2)}) collective-permute-start(bf16[800,128]{1,0:T(8,128)(2,1)S(1)} %collective-permute-done.10.rest_9_), channel_id=1, source_target_pairs={{0,1},{1,0},{2,3},{3,2},{4,5},{5,4},{6,7},{7,6},{8,9},{9,8},{10,11... | collective-permute-start | bytes 614408 | tf_op jit(solution)/shard_map/ppermute | solution.py:459
  23.9 4.5 %collective-permute-start.14 = (bf16[640,128]{1,0:T(8,128)(2,1)S(1)}, bf16[640,128]{1,0:T(8,128)(2,1)S(1)}, u32[]{:S(2)}, u32[]{:S(2)}) collective-permute-start(bf16[640,128]{1,0:T(8,128)(2,1)S(1)} %collective-permute-done.13.y), channel_id=1, source_target_pairs={{0,1},{1,0},{2,3},{3,2},{4,5},{5,4},{6,7},{7,6},{8,9},{9,8},{10,11... | collective-permute-start | bytes 491528 | tf_op jit(solution)/shard_map/ppermute | solution.py:459
  24.5 4.0 %collective-permute-start.16 = (bf16[640,128]{1,0:T(8,128)(2,1)S(1)}, bf16[640,128]{1,0:T(8,128)(2,1)S(1)}, u32[]{:S(2)}, u32[]{:S(2)}) collective-permute-start(bf16[640,128]{1,0:T(8,128)(2,1)S(1)} %collective-permute-done.15.x), channel_id=1, source_target_pairs={{0,1},{1,0},{2,3},{3,2},{4,5},{5,4},{6,7},{7,6},{8,9},{9,8},{10,11... | collective-permute-start | bytes 491528 | tf_op jit(solution)/shard_map/ppermute | solution.py:459
  27.4 1.5 %collective-permute-start.12 = (bf16[640,128]{1,0:T(8,128)(2,1)S(1)}, bf16[640,128]{1,0:T(8,128)(2,1)S(1)}, u32[]{:S(2)}, u32[]{:S(2)}) collective-permute-start(bf16[640,128]{1,0:T(8,128)(2,1)S(1)} %attend.1.token_ref.own), channel_id=1, source_target_pairs={{0,1},{1,0},{2,3},{3,2},{4,5},{5,4},{6,7},{7,6},{8,9},{9,8},{10,11... | collective-permute-start | bytes 491528 | tf_op jit(solution)/shard_map/ppermute | solution.py:459
  27.4 1.9 %collective-permute-start.8 = (bf16[640,128]{1,0:T(8,128)(2,1)S(1)}, bf16[640,128]{1,0:T(8,128)(2,1)S(1)}, u32[]{:S(2)}, u32[]{:S(2)}) collective-permute-start(bf16[640,128]{1,0:T(8,128)(2,1)S(1)} %collective-permute-done.7.rest_0_), channel_id=1, source_target_pairs={{0,1},{1,0},{2,3},{3,2},{4,5},{5,4},{6,7},{7,6},{8,9},{9,8},{10,11... | collective-permute-start | bytes 491528 | tf_op jit(solution)/shard_map/ppermute | solution.py:459
  30.0 6.4 %collective-permute-start.17 = (bf16[656,128]{1,0:T(8,128)(2,1)S(1)}, bf16[656,128]{1,0:T(8,128)(2,1)S(1)}, u32[]{:S(2)}, u32[]{:S(2)}) collective-permute-start(bf16[656,128]{1,0:T(8,128)(2,1)S(1)} %project.1.token_ref.own.rest_0_), channel_id=1, source_target_pairs={{0,4},{1,5},{2,6},{3,7},{4,0},{5,1},{6,2},{7,3},{8,12},{9,13},{10,... | collective-permute-start | bytes 503816 | tf_op jit(solution)/shard_map/ppermute | solution.py:459
  30.6 7.2 %collective-permute-start.18 = (bf16[656,128]{1,0:T(8,128)(2,1)S(1)}, bf16[656,128]{1,0:T(8,128)(2,1)S(1)}, u32[]{:S(2)}, u32[]{:S(2)}) collective-permute-start(bf16[656,128]{1,0:T(8,128)(2,1)S(1)} %project.1.token_ref.own.rest_0_), channel_id=1, source_target_pairs={{0,2},{1,3},{2,0},{3,1},{4,6},{5,7},{6,4},{7,5},{8,10},{9,11},{10,... | collective-permute-start | bytes 503816 | tf_op jit(solution)/shard_map/ppermute | solution.py:459
  31.9 9.3 %collective-permute-start.22 = (bf16[656,128]{1,0:T(8,128)(2,1)S(1)}, bf16[656,128]{1,0:T(8,128)(2,1)S(1)}, u32[]{:S(2)}, u32[]{:S(2)}) collective-permute-start(bf16[656,128]{1,0:T(8,128)(2,1)S(1)} %project.1.token_ref.own.rest_0_), channel_id=1, source_target_pairs={{0,6},{1,7},{2,4},{3,5},{4,2},{5,3},{6,0},{7,1},{8,14},{9,15},{10,... | collective-permute-start | bytes 503816 | tf_op jit(solution)/shard_map/ppermute | solution.py:459
  34.9 3.6 %collective-permute-start.19 = (bf16[656,128]{1,0:T(8,128)(2,1)S(1)}, bf16[656,128]{1,0:T(8,128)(2,1)S(1)}, u32[]{:S(2)}, u32[]{:S(2)}) collective-permute-start(bf16[656,128]{1,0:T(8,128)(2,1)S(1)} %project.1.token_ref.own.rest_0_), channel_id=1, source_target_pairs={{0,1},{1,0},{2,3},{3,2},{4,5},{5,4},{6,7},{7,6},{8,9},{9,8},{10,11... | collective-permute-start | bytes 503816 | tf_op jit(solution)/shard_map/ppermute | solution.py:459
  36.4 4.8 %collective-permute-start.20 = (bf16[656,128]{1,0:T(8,128)(2,1)S(1)}, bf16[656,128]{1,0:T(8,128)(2,1)S(1)}, u32[]{:S(2)}, u32[]{:S(2)}) collective-permute-start(bf16[656,128]{1,0:T(8,128)(2,1)S(1)} %collective-permute-done.17.y.rest_1_), channel_id=1, source_target_pairs={{0,1},{1,0},{2,3},{3,2},{4,5},{5,4},{6,7},{7,6},{8,9},{9,8},{10,11... | collective-permute-start | bytes 503816 | tf_op jit(solution)/shard_map/ppermute | solution.py:459
  37.8 3.4 %collective-permute-start.21 = (bf16[656,128]{1,0:T(8,128)(2,1)S(1)}, bf16[656,128]{1,0:T(8,128)(2,1)S(1)}, u32[]{:S(2)}, u32[]{:S(2)}) collective-permute-start(bf16[656,128]{1,0:T(8,128)(2,1)S(1)} %collective-permute-done.18.x.rest_2_), channel_id=1, source_target_pairs={{0,1},{1,0},{2,3},{3,2},{4,5},{5,4},{6,7},{7,6},{8,9},{9,8},{10,11... | collective-permute-start | bytes 503816 | tf_op jit(solution)/shard_map/ppermute | solution.py:459
  41.2 1.4 %collective-permute-start.23 = (bf16[656,128]{1,0:T(8,128)(2,1)S(1)}, bf16[656,128]{1,0:T(8,128)(2,1)S(1)}, u32[]{:S(2)}, u32[]{:S(2)}) collective-permute-start(bf16[656,128]{1,0:T(8,128)(2,1)S(1)} %collective-permute-done.22.rest_6_), channel_id=1, source_target_pairs={{0,1},{1,0},{2,3},{3,2},{4,5},{5,4},{6,7},{7,6},{8,9},{9,8},{10,11... | collective-permute-start | bytes 503816 | tf_op jit(solution)/shard_map/ppermute | solution.py:459
  (2 other events, 10.7 us)

commit v14 on v13

--- a/solution.py
+++ b/solution.py
@@ -122,8 +122,9 @@
 REST = HPAIR - WIDE
 MAIN = ROWS * WIDE
 NOTES = 16
-BLOCK_ORDER = (0, 4, 2, 6, 7, 3, 5, 1)
-PIECE_ORDER = (0, 4, 2, 1, 5, 3, 6, 7)
+RECEIVERS = ((0, 0), (4, 2), (2, 4), (6, 6), (7, 7), (3, 5), (5, 3), (1, 1))
+SENDERS = ((0, 0), (4, 2), (2, 4), (6, 6), (7, 7), (5, 3), (3, 5), (1, 1))
+OWNERS = ((0, 0), (4, 2), (2, 4), (1, 1), (3, 5), (5, 3), (6, 6), (7, 7))
 ROOT = math.log2(math.e) / math.sqrt(HDIM)
 BF16 = jnp.bfloat16
 F32 = jnp.float32
@@ -131,6 +132,11 @@
 
 def row_index():
     return lax.axis_index("row")
+
+
+def steps(pairs):
+    core = row_index() % 2
+    return [even + (odd - even) * core for even, odd in pairs]
 
 
 def pack_tail(wide):
@@ -173,8 +179,8 @@
         parts.append(resid[:, dest * WIDE : (dest + 1) * WIDE])
         parts.append(resid[:, MAIN + dest * REST : MAIN + (dest + 1) * REST])
         held[dest] = jnp.concatenate(parts, axis=1)
-    for step in range(ROWS):
-        outs[step][...] = held[me ^ step]
+    for step, out in zip(steps(RECEIVERS), outs):
+        out[...] = held[me ^ step]
 
 
 def layout_kernel(grid_ref, *rest):
@@ -203,7 +209,7 @@
     me = row_index()
     band = blocks[0].shape[0]
     patches = band * ROWS
-    for step, block in zip(BLOCK_ORDER, blocks):
+    for step, block in zip(steps(SENDERS), blocks):
         at = pl.ds(pl.multiple_of((me ^ step) * band, band), band)
         q_all[at, :] = block[:, :HPAIR]
         k_all[at, :] = block[:, HPAIR : 2 * HPAIR]
@@ -250,7 +256,7 @@
     fetch.start()
     me = row_index()
     band = blocks[0].shape[0]
-    for step, block in zip(BLOCK_ORDER, blocks):
+    for step, block in zip(steps(SENDERS), blocks):
         at = pl.ds(pl.multiple_of((me ^ step) * band, band), band)
         held[at, :] = block[:, 3 * HPAIR :]
     resid_ref[...] = jnp.dot(select_ref[...], held[...], preferred_element_type=F32)
@@ -299,13 +305,13 @@
     return (block == lax.rem(page + 2, PAGES)) | (block == lax.rem(page + 1 + 2 * core, PAGES))
 
 
-def add_features(steps, pieces, weights, before_ref, out_ref):
+def add_features(owners, pieces, weights, before_ref, out_ref):
     main_ref, tail_ref, last_main_ref, last_tail_ref = weights
     me = row_index()
     patches = out_ref.shape[0]
     groups = patches // 4
     mains, tails = [], []
-    for step in steps:
+    for step in steps(owners):
         pair = me ^ step
         columns = pl.ds(pl.multiple_of(pair * WIDE, WIDE), WIDE)
         is_last = came_last(pair // 2)
@@ -319,12 +325,12 @@
         out_ref[span, :] = base[span] + jnp.dot(rows[patches:], tail, preferred_element_type=F32)
 
 
-def project_first_kernel(own, y, x, *rest):
-    add_features((0, 4, 2), (own, y, x), rest[:4], *rest[4:])
-
-
-def project_second_kernel(own, y, x, *rest):
-    add_features((1, 5, 3), (own, y, x), rest[:4], *rest[4:])
+def project_first_kernel(*rest):
+    add_features(OWNERS[:3], rest[:3], rest[3:7], *rest[7:])
+
+
+def project_second_kernel(*rest):
+    add_features(OWNERS[3:6], rest[:3], rest[3:7], *rest[7:])
 
 
 def project_kernel(*rest):
@@ -385,15 +391,16 @@
     )
 
 
-def merge_first_kernel(own, y, x, weight_ref, sum_ref):
-    for corner in range(4):
-        sum_ref[corner] = merge_product(weight_ref, corner, sum_ref.shape[2], [(0, own), (4, y), (2, x)])
-
-
-def merge_second_kernel(own, y, x, before_ref, weight_ref, sum_ref):
-    for corner in range(4):
-        part = merge_product(weight_ref, corner, sum_ref.shape[2], [(1, own), (5, y), (3, x)])
-        sum_ref[corner] = before_ref[corner] + part
+def merge_first_kernel(*rest):
+    pieces, (weight_ref, sum_ref) = list(zip(steps(OWNERS[:3]), rest[:3])), rest[3:]
+    for corner in range(4):
+        sum_ref[corner] = merge_product(weight_ref, corner, sum_ref.shape[2], pieces)
+
+
+def merge_second_kernel(*rest):
+    pieces, (before_ref, weight_ref, sum_ref) = list(zip(steps(OWNERS[3:6]), rest[:3])), rest[3:]
+    for corner in range(4):
+        sum_ref[corner] = before_ref[corner] + merge_product(weight_ref, corner, sum_ref.shape[2], pieces)
 
 
 def merge_kernel(*rest):
@@ -417,11 +424,11 @@
             )
         )
     notes = jnp.zeros((NOTES, groups), F32)
-    for step, piece in zip(PIECE_ORDER, pieces):
+    for step, piece in zip(steps(OWNERS), pieces):
         notes = notes + piece[patches + groups :, :].astype(F32)
     scale = lax.rsqrt((notes[:4] + notes[4:8]) * (1.0 / D) + 1e-06)
     spread = jnp.concatenate([jnp.broadcast_to(scale[at : at + 1], (REST, groups)) for at in range(4)], axis=0).T
-    for step, piece in zip(PIECE_ORDER, pieces):
+    for step, piece in zip(steps(OWNERS), pieces):
         at = pl.ds(pl.multiple_of((me ^ step) * WIDE, WIDE), WIDE)
         ends_ref[:, at] = (piece[patches : patches + groups, :].astype(F32) * spread).astype(BF16)
     total = bias_ref[...] + lax.dot_general(tail_ref[...], ends_ref[...], contract, preferred_element_type=F32)
@@ -455,8 +462,9 @@
     return jax.ShapeDtypeStruct(dims, dtype)
 
 
-def swap(value, step):
-    return lax.ppermute(value, "row", [(row, row ^ step) for row in range(ROWS)])
+def swap(value, even, odd=None):
+    odd = even if odd is None else odd
+    return lax.ppermute(value, "row", [(row, row ^ (odd if row % 2 else even)) for row in range(ROWS)])
 
 
 def turn(value, low, high):
@@ -500,7 +508,7 @@
         limit=24,
         moved=1 << 20,
     )(in_hbm(qkv_rows), in_hbm(residual), in_hbm(out_weight), in_hbm(page_grid))
-    blocks = [sends[0]] + [swap(sends[step], step) for step in BLOCK_ORDER[1:]]
+    blocks = [sends[0]] + [swap(send, *pair) for send, pair in zip(sends[1:], RECEIVERS[1:])]
     select, dead, live = kernel(
         layout_kernel,
         "layout",
@@ -540,11 +548,11 @@
         flops=1,
         moved=1,
     )(across, swapped, main)
-    y, x, far = [swap(attn, step) for step in (4, 2, 6)]
+    one, two, far = swap(attn, 4, 2), swap(attn, 2, 4), swap(attn, 6)
     weights = (main, tail, *last)
     rows = shape(patches, HPAIR, dtype=F32)
-    first = kernel(project_first_kernel, "project_first", rows, count=8, flops=1, moved=1)(attn, y, x, *weights, resid)
-    near = [swap(after(attn, last[0]), 1), swap(y, 1), swap(x, 1)]
+    first = kernel(project_first_kernel, "project_first", rows, count=8, flops=1, moved=1)(attn, one, two, *weights, resid)
+    near = [swap(after(attn, last[0]), 1), swap(one, 1), swap(two, 1)]
     second = kernel(project_second_kernel, "project_second", rows, count=8, flops=1, moved=1)(*near, *weights, first)
     hidden = kernel(
         project_kernel,
@@ -564,9 +572,9 @@
         moved=4 << 20,
     )(merge_weight, in_hbm(merge_bias), hidden)
     sums = shape(4, units, groups, dtype=F32)
-    y, x, far = [swap(hidden, step) for step in (4, 2, 6)]
-    first = kernel(merge_first_kernel, "merge_first", sums, count=4, flops=1, moved=1)(hidden, y, x, merge_weight)
-    near = [swap(after(hidden, ends), 1), swap(y, 1), swap(x, 1)]
+    one, two, far = swap(hidden, 4, 2), swap(hidden, 2, 4), swap(hidden, 6)
+    first = kernel(merge_first_kernel, "merge_first", sums, count=4, flops=1, moved=1)(hidden, one, two, merge_weight)
+    near = [swap(after(hidden, ends), 1), swap(one, 1), swap(two, 1)]
     second = kernel(merge_second_kernel, "merge_second", sums, count=5, flops=1, moved=1)(*near, first, merge_weight)
     return kernel(
         merge_kernel,
@@ -576,7 +584,7 @@
         count=ROWS + 5,
         flops=4 * units * groups * MAIN,
         moved=8 << 20,
-    )(hidden, y, x, *near, far, swap(after(far, first, *near), 1), second, merge_weight, ends, bias, live)
+    )(hidden, one, two, *near, far, swap(after(far, first, *near), 1), second, merge_weight, ends, bias, live)
 
 
 def solution(mesh):

time: 44.4 us -> 45.5 us (1.025)
  starting transfers between devices: 20.4 us -> 23 us
  waiting for transfers between devices: 12.7 us -> 11.1 us
    ppermute x2, waiting for transfers between devices: 2.58 us -> 0.01 us  [turn(): return lax.ppermute(value, ('page', 'row'), pairs)]
    ppermute x22, starting transfers between devices: 16.1 us -> 18 us  [swap(): lax.ppermute(value, 'row', [(row, row ^ (odd if row % 2 else even)) for r...]
    ppermute x22, waiting for transfers between devices: 10.2 us -> 11.1 us  [swap(): lax.ppermute(value, 'row', [(row, row ^ (odd if row % 2 else even)) for r...]
    ppermute x2, starting transfers between devices: 4.28 us -> 5.02 us  [turn(): return lax.ppermute(value, ('page', 'row'), pairs)]
where the time goes in v14:
time: 45.5 us; the launch traced here: 45.3 us
  starting transfers between devices  23 us (51%)
  waiting for transfers between devices  11.1 us (24%)
  Pallas kernels  10.9 us (24%)
    ppermute x22, starting transfers between devices, swap(): lax.ppermute(value, 'row', [(row, row ^ (odd if row % 2 else even)) for r...  18 us
    ppermute x22, waiting for transfers between devices, swap(): lax.ppermute(value, 'row', [(row, row ^ (odd if row % 2 else even)) for r...  11.1 us
    ppermute x2, starting transfers between devices, turn(): return lax.ppermute(value, ('page', 'row'), pairs)  5.02 us
    pallas_call x1, Pallas kernels, local_eight(): kernel(spread_kernel, 'spread', [shape(band, 4 * HPAIR)] * ROWS + [shape(...  1.76 us
    pallas_call x1, Pallas kernels, local_eight(): kernel(merge_kernel, 'merge', shape(1, units, groups), [pltpu.VMEM((group...  1.7 us
    pallas_call x1, Pallas kernels, local_eight(): kernel(tail_kernel, 'merge_tail', [shape(units, MAIN), shape(units, 1, dt...  1.39 us
    pallas_call x1, Pallas kernels, local_eight(): kernel(attend_kernel, 'attend', shape(piece, WIDE), [pltpu.VMEM((patches,...  1.33 us
    pallas_call x1, Pallas kernels, local_eight(): kernel(ready_kernel, 'ready', [shape(patches, HPAIR, dtype=F32), shape(1,...  1.28 us
  transfers between devices with their start and end apart: 24, of which 9 were waited for; matrix products, arithmetic and copies ran while one was open for 0% of the time, Pallas kernels for 15%

profile of v14, /device:TPU:0, one launch (start us, length us, event | category | flops | bytes accessed | tf_op | source)
XLA Modules:
  0.0 45.3 jit_solution(9326180854460874855)
XLA Ops:
  0.0 1.8 %spread.1 = (bf16[64,640]{1,0:T(8,128)(2,1)S(1)}, bf16[64,640]{1,0:T(8,128)(2,1)S(1)}, bf16[64,640]{1,0:T(8,128)(2,1)S(1)}, bf16[64,640]{1,0:T(8,128)(2,1)S(1)},...) custom-call(bf16[1,64,3840]{2,1,0:T(8,128)(2,1)} %qkv_hbm.1, ...), custom_call_target="tpu_custom_call" | custom-call | bytes 1048576 | tf_op jit(solution)/shard_map/spread/pallas_call | solution.py:492
  1.8 3.0 %collective-permute-start = (bf16[64,640]{1,0:T(8,128)(2,1)S(1)}, bf16[64,640]{1,0:T(8,128)(2,1)S(1)}, u32[]{:S(2)}, u32[]{:S(2)}) collective-permute-start(bf16[64,640]{1,0:T(8,128)(2,1)S(1)} %get-tuple-element.32), channel_id=1, source_target_pairs={{0,4},{1,3},{2,6},{3,1},{4,0},{5,7},{6,2},{7,5},{8,12},{9,11},{10,... | collective-permute-start | bytes 245768 | tf_op jit(solution)/shard_map/ppermute | solution.py:467
  4.8 1.5 %collective-permute-start.1 = (bf16[64,640]{1,0:T(8,128)(2,1)S(1)}, bf16[64,640]{1,0:T(8,128)(2,1)S(1)}, u32[]{:S(2)}, u32[]{:S(2)}) collective-permute-start(bf16[64,640]{1,0:T(8,128)(2,1)S(1)} %get-tuple-element.33), channel_id=1, source_target_pairs={{0,2},{1,5},{2,0},{3,7},{4,6},{5,1},{6,4},{7,3},{8,10},{9,13},{10,... | collective-permute-start | bytes 245768 | tf_op jit(solution)/shard_map/ppermute | solution.py:467
  6.3 1.5 %collective-permute-start.3 = (bf16[64,640]{1,0:T(8,128)(2,1)S(1)}, bf16[64,640]{1,0:T(8,128)(2,1)S(1)}, u32[]{:S(2)}, u32[]{:S(2)}) collective-permute-start(bf16[64,640]{1,0:T(8,128)(2,1)S(1)} %get-tuple-element.38), channel_id=1, source_target_pairs={{0,7},{1,6},{2,5},{3,4},{4,3},{5,2},{6,1},{7,0},{8,15},{9,14},{10,... | collective-permute-start | bytes 245768 | tf_op jit(solution)/shard_map/ppermute | solution.py:467
  7.8 1.6 %collective-permute-start.4 = (bf16[64,640]{1,0:T(8,128)(2,1)S(1)}, bf16[64,640]{1,0:T(8,128)(2,1)S(1)}, u32[]{:S(2)}, u32[]{:S(2)}) collective-permute-start(bf16[64,640]{1,0:T(8,128)(2,1)S(1)} %get-tuple-element.39), channel_id=1, source_target_pairs={{0,3},{1,4},{2,1},{3,6},{4,7},{5,0},{6,5},{7,2},{8,11},{9,12},{10,... | collective-permute-start | bytes 245768 | tf_op jit(solution)/shard_map/ppermute | solution.py:467
  9.9 1.2 %collective-permute-start.6 = (bf16[64,640]{1,0:T(8,128)(2,1)S(1)}, bf16[64,640]{1,0:T(8,128)(2,1)S(1)}, u32[]{:S(2)}, u32[]{:S(2)}) collective-permute-start(bf16[64,640]{1,0:T(8,128)(2,1)S(1)} %get-tuple-element.41), channel_id=1, source_target_pairs={{0,1},{1,0},{2,3},{3,2},{4,5},{5,4},{6,7},{7,6},{8,9},{9,8},{10,11... | collective-permute-start | bytes 245768 | tf_op jit(solution)/shard_map/ppermute | solution.py:467
  11.1 1.0 %collective-permute-done.2.rest_2_.rest_3_ = bf16[64,640]{1,0:T(8,128)(2,1)S(1)} collective-permute-done((bf16[64,640]{1,0:T(8,128)(2,1)S(1)}, bf16[64,640]{1,0:T(8,128)(2,1)S(1)}, u32[]{:S(2)}, u32[]{:S(2)}) %collective-permute-start.2) | collective-permute-done | bytes 81952 | tf_op jit(solution)/shard_map/ppermute | solution.py:467
  12.1 2.0 %collective-permute-start.10 = (bf16[800,128]{1,0:T(8,128)(2,1)S(1)}, bf16[800,128]{1,0:T(8,128)(2,1)S(1)}, u32[]{:S(2)}, u32[]{:S(2)}) collective-permute-start(bf16[800,128]{1,0:T(8,128)(2,1)S(1)} %get-tuple-element.44), channel_id=1, source_target_pairs={{0,8},{1,25},{2,10},{3,27},{4,12},{5,29},{6,14},{7,31},{8,16},{9,1... | collective-permute-start | bytes 614408 | tf_op jit(solution)/shard_map/ppermute | solution.py:476
  14.5 1.3 %attend.1.token_ref.rest_0_ = bf16[640,128]{1,0:T(8,128)(2,1)S(1)} custom-call(bf16[512,512]{1,0:T(8,128)(2,1)S(1)} %get-tuple-element.35.select_ref, f32[1,512]{1,0:T(1,128)S(1)} %get-tuple-element.36.dead_ref, bf16[64,640]{1,0:T(8,128)(2,1)S(1)} %get-tuple-element.37.rest_0_, bf16[64,640]{1,0:T(8,128)(2,1)S(1)} %collective-permute-done.rest_0_.rest_1_, ...), custom_call_target="tpu_custom_call" | custom-call | flops 21474836480 | bytes 1048576 | tf_op jit(solution)/shard_map/attend/pallas_call | solution.py:522
  15.9 1.2 %collective-permute-start.13 = (bf16[640,128]{1,0:T(8,128)(2,1)S(1)}, bf16[640,128]{1,0:T(8,128)(2,1)S(1)}, u32[]{:S(2)}, u32[]{:S(2)}) collective-permute-start(bf16[640,128]{1,0:T(8,128)(2,1)S(1)} %attend.1.token_ref.rest_0_), channel_id=1, source_target_pairs={{0,4},{1,3},{2,6},{3,1},{4,0},{5,7},{6,2},{7,5},{8,12},{9,11},{10,... | collective-permute-start | bytes 491528 | tf_op jit(solution)/shard_map/ppermute | solution.py:467
  17.1 0.8 %collective-permute-start.15 = (bf16[640,128]{1,0:T(8,128)(2,1)S(1)}, bf16[640,128]{1,0:T(8,128)(2,1)S(1)}, u32[]{:S(2)}, u32[]{:S(2)}) collective-permute-start(bf16[640,128]{1,0:T(8,128)(2,1)S(1)} %attend.1.token_ref.rest_0_), channel_id=1, source_target_pairs={{0,2},{1,5},{2,0},{3,7},{4,6},{5,1},{6,4},{7,3},{8,10},{9,13},{10,... | collective-permute-start | bytes 491528 | tf_op jit(solution)/shard_map/ppermute | solution.py:467
  17.9 1.5 %collective-permute-start.7 = (bf16[640,128]{1,0:T(8,128)(2,1)S(1)}, bf16[640,128]{1,0:T(8,128)(2,1)S(1)}, u32[]{:S(2)}, u32[]{:S(2)}) collective-permute-start(bf16[640,128]{1,0:T(8,128)(2,1)S(1)} %attend.1.token_ref.rest_0_), channel_id=1, source_target_pairs={{0,6},{1,7},{2,4},{3,5},{4,2},{5,3},{6,0},{7,1},{8,14},{9,15},{10,... | collective-permute-start | bytes 491528 | tf_op jit(solution)/shard_map/ppermute | solution.py:467
  19.4 3.0 %collective-permute-start.9 = (bf16[400,128]{1,0:T(8,128)(2,1)S(1)}, bf16[400,128]{1,0:T(8,128)(2,1)S(1)}, u32[]{:S(2)}, u32[]{:S(2)}) collective-permute-start(bf16[400,128]{1,0:T(8,128)(2,1)S(1)} %get-tuple-element.43.rest_8_), channel_id=1, source_target_pairs={{0,16},{1,17},{2,18},{3,19},{4,20},{5,21},{6,22},{7,23},{8,24},{9,... | collective-permute-start | bytes 307208 | tf_op jit(solution)/shard_map/ppermute | solution.py:476
  22.4 1.3 %ready.1 = (f32[512,160]{1,0:T(8,128)S(1)}, f32[1,160]{1,0:T(1,128)S(1)}, bf16[1024,160]{1,0:T(8,128)(2,1)S(1)}, bf16[4,1024,160]{2,1,0:T(8,128)(2,1)S(1)}) custom-call(bf16[512,512]{1,0:T(8,128)(2,1)S(1)} %get-tuple-element.35.select_ref, f32[1280]{0:T(1024)} %gain_hbm.1, bf16[640,128]{1,0:T(8,128)(2,1)S(1)} %attend.1.token_ref.rest_0_, ...), custom_call_target="tpu_custom_call" | custom-call | flops 10737418240 | bytes 4194304 | tf_op jit(solution)/shard_map/ready/pallas_call | solution.py:532
  23.7 2.8 %collective-permute-done.13.rest_1_ = bf16[640,128]{1,0:T(8,128)(2,1)S(1)} collective-permute-done((bf16[640,128]{1,0:T(8,128)(2,1)S(1)}, bf16[640,128]{1,0:T(8,128)(2,1)S(1)}, u32[]{:S(2)}, u32[]{:S(2)}) %collective-permute-start.13) | collective-permute-done | bytes 163872 | tf_op jit(solution)/shard_map/ppermute | solution.py:467
  29.2 0.7 %project.1.token_ref.rest_0_ = bf16[656,128]{1,0:T(8,128)(2,1)S(1)} custom-call(bf16[640,128]{1,0:T(8,128)(2,1)S(1)} %collective-permute-done.7.rest_0_, bf16[640,128]{1,0:T(8,128)(2,1)S(1)} %collective-permute-done.8.rest_1_, f32[512,160]{1,0:T(8,128)S(1)} %project_second.1.rest_2_, bf16[1024,160]{1,0:T(8,128)(2,1)S(1)} %get-tuple-element.45.token_ref.rest_3_, ...), custom_call_target="tpu_custom_call" | custom-call | flops 134217728 | bytes 4194304 | tf_op jit(solution)/shard_map/project/pallas_call | solution.py:557
  29.9 0.7 %collective-permute-start.17 = (bf16[656,128]{1,0:T(8,128)(2,1)S(1)}, bf16[656,128]{1,0:T(8,128)(2,1)S(1)}, u32[]{:S(2)}, u32[]{:S(2)}) collective-permute-start(bf16[656,128]{1,0:T(8,128)(2,1)S(1)} %project.1.token_ref.rest_0_), channel_id=1, source_target_pairs={{0,4},{1,3},{2,6},{3,1},{4,0},{5,7},{6,2},{7,5},{8,12},{9,11},{10,... | collective-permute-start | bytes 503816 | tf_op jit(solution)/shard_map/ppermute | solution.py:467
  30.6 1.2 %collective-permute-start.18 = (bf16[656,128]{1,0:T(8,128)(2,1)S(1)}, bf16[656,128]{1,0:T(8,128)(2,1)S(1)}, u32[]{:S(2)}, u32[]{:S(2)}) collective-permute-start(bf16[656,128]{1,0:T(8,128)(2,1)S(1)} %project.1.token_ref.rest_0_), channel_id=1, source_target_pairs={{0,2},{1,5},{2,0},{3,7},{4,6},{5,1},{6,4},{7,3},{8,10},{9,13},{10,... | collective-permute-start | bytes 503816 | tf_op jit(solution)/shard_map/ppermute | solution.py:467
  31.8 1.5 %collective-permute-start.22 = (bf16[656,128]{1,0:T(8,128)(2,1)S(1)}, bf16[656,128]{1,0:T(8,128)(2,1)S(1)}, u32[]{:S(2)}, u32[]{:S(2)}) collective-permute-start(bf16[656,128]{1,0:T(8,128)(2,1)S(1)} %project.1.token_ref.rest_0_), channel_id=1, source_target_pairs={{0,6},{1,7},{2,4},{3,5},{4,2},{5,3},{6,0},{7,1},{8,14},{9,15},{10,... | collective-permute-start | bytes 503816 | tf_op jit(solution)/shard_map/ppermute | solution.py:467
  33.4 1.4 %merge_tail.1 = (bf16[640,1024]{1,0:T(8,128)(2,1)S(1)}, f32[640,1]{1,0:T(8,128)S(1)}) custom-call(bf16[640,5120]{1,0:T(8,128)(2,1)S(1)} %bitcast.1, f32[640]{0:T(1024)} %bias_hbm.1, bf16[656,128]{1,0:T(8,128)(2,1)S(1)} %project.1.token_ref.rest_0_), custom_call_target="tpu_custom_call" | custom-call | bytes 4194304 | tf_op jit(solution)/shard_map/merge_tail/pallas_call | solution.py:565
  34.9 5.7 %collective-permute-done.17.rest_1_ = bf16[656,128]{1,0:T(8,128)(2,1)S(1)} collective-permute-done((bf16[656,128]{1,0:T(8,128)(2,1)S(1)}, bf16[656,128]{1,0:T(8,128)(2,1)S(1)}, u32[]{:S(2)}, u32[]{:S(2)}) %collective-permute-start.17) | collective-permute-done | bytes 167968 | tf_op jit(solution)/shard_map/ppermute | solution.py:467
  41.1 0.7 %merge_first.1.rest_3_ = f32[4,640,128]{2,1,0:T(8,128)S(1)} custom-call(bf16[656,128]{1,0:T(8,128)(2,1)S(1)} %project.1.token_ref.rest_0_, bf16[656,128]{1,0:T(8,128)(2,1)S(1)} %collective-permute-done.17.rest_1_, bf16[656,128]{1,0:T(8,128)(2,1)S(1)} %collective-permute-done.18.rest_2_, bf16[640,5120]{1,0:T(8,128)(2,1)S(1)} %bitcast.1), custom_call_target="tpu_custom_call" | custom-call | flops 1 | bytes 1 | tf_op jit(solution)/shard_map/merge_first/pallas_call | solution.py:576
  42.5 0.7 %merge_second.1.rest_8_ = f32[4,640,128]{2,1,0:T(8,128)S(1)} custom-call(bf16[656,128]{1,0:T(8,128)(2,1)S(1)} %collective-permute-done.19.rest_0_.rest_3_, bf16[656,128]{1,0:T(8,128)(2,1)S(1)} %collective-permute-done.20.rest_1_.rest_4_, bf16[656,128]{1,0:T(8,128)(2,1)S(1)} %collective-permute-done.21.rest_2_.rest_5_, ...), custom_call_target="tpu_custom_call" | custom-call | flops 1 | bytes 1 | tf_op jit(solution)/shard_map/merge_second/pallas_call | solution.py:578
  43.6 1.7 %merge.1 = bf16[1,640,128]{2,1,0:T(8,128)(2,1)} custom-call(bf16[656,128]{1,0:T(8,128)(2,1)S(1)} %project.1.token_ref.rest_0_, bf16[656,128]{1,0:T(8,128)(2,1)S(1)} %collective-permute-done.17.rest_1_, bf16[656,128]{1,0:T(8,128)(2,1)S(1)} %collective-permute-done.18.rest_2_, bf16[656,128]{1,0:T(8,128)(2,1)S(1)} %collective-permute-done.19.rest_0_.rest_3_, ...), custom_call_target="tpu_custom_call" | custom-call | flops 335544320 | bytes 8388608 | tf_op jit(solution)/shard_map/merge/pallas_call | solution.py:579
  (41 shorter events, 5.1 us)
Async XLA Ops:
  1.8 7.7 %collective-permute-start = (bf16[64,640]{1,0:T(8,128)(2,1)S(1)}, bf16[64,640]{1,0:T(8,128)(2,1)S(1)}, u32[]{:S(2)}, u32[]{:S(2)}) collective-permute-start(bf16[64,640]{1,0:T(8,128)(2,1)S(1)} %get-tuple-element.32), channel_id=1, source_target_pairs={{0,4},{1,3},{2,6},{3,1},{4,0},{5,7},{6,2},{7,5},{8,12},{9,11},{10,... | collective-permute-start | bytes 245768 | tf_op jit(solution)/shard_map/ppermute | solution.py:467
  4.8 5.1 %collective-permute-start.1 = (bf16[64,640]{1,0:T(8,128)(2,1)S(1)}, bf16[64,640]{1,0:T(8,128)(2,1)S(1)}, u32[]{:S(2)}, u32[]{:S(2)}) collective-permute-start(bf16[64,640]{1,0:T(8,128)(2,1)S(1)} %get-tuple-element.33), channel_id=1, source_target_pairs={{0,2},{1,5},{2,0},{3,7},{4,6},{5,1},{6,4},{7,3},{8,10},{9,13},{10,... | collective-permute-start | bytes 245768 | tf_op jit(solution)/shard_map/ppermute | solution.py:467
  6.3 5.8 %collective-permute-start.2 = (bf16[64,640]{1,0:T(8,128)(2,1)S(1)}, bf16[64,640]{1,0:T(8,128)(2,1)S(1)}, u32[]{:S(2)}, u32[]{:S(2)}) collective-permute-start(bf16[64,640]{1,0:T(8,128)(2,1)S(1)} %get-tuple-element.34), channel_id=1, source_target_pairs={{0,6},{1,7},{2,4},{3,5},{4,2},{5,3},{6,0},{7,1},{8,14},{9,15},{10,... | collective-permute-start | bytes 245768 | tf_op jit(solution)/shard_map/ppermute | solution.py:467
  6.3 7.9 %collective-permute-start.3 = (bf16[64,640]{1,0:T(8,128)(2,1)S(1)}, bf16[64,640]{1,0:T(8,128)(2,1)S(1)}, u32[]{:S(2)}, u32[]{:S(2)}) collective-permute-start(bf16[64,640]{1,0:T(8,128)(2,1)S(1)} %get-tuple-element.38), channel_id=1, source_target_pairs={{0,7},{1,6},{2,5},{3,4},{4,3},{5,2},{6,1},{7,0},{8,15},{9,14},{10,... | collective-permute-start | bytes 245768 | tf_op jit(solution)/shard_map/ppermute | solution.py:467
  7.8 6.7 %collective-permute-start.4 = (bf16[64,640]{1,0:T(8,128)(2,1)S(1)}, bf16[64,640]{1,0:T(8,128)(2,1)S(1)}, u32[]{:S(2)}, u32[]{:S(2)}) collective-permute-start(bf16[64,640]{1,0:T(8,128)(2,1)S(1)} %get-tuple-element.39), channel_id=1, source_target_pairs={{0,3},{1,4},{2,1},{3,6},{4,7},{5,0},{6,5},{7,2},{8,11},{9,12},{10,... | collective-permute-start | bytes 245768 | tf_op jit(solution)/shard_map/ppermute | solution.py:467
  9.5 5.0 %collective-permute-start.5 = (bf16[64,640]{1,0:T(8,128)(2,1)S(1)}, bf16[64,640]{1,0:T(8,128)(2,1)S(1)}, u32[]{:S(2)}, u32[]{:S(2)}) collective-permute-start(bf16[64,640]{1,0:T(8,128)(2,1)S(1)} %get-tuple-element.40), channel_id=1, source_target_pairs={{0,5},{1,2},{2,7},{3,0},{4,1},{5,6},{6,3},{7,4},{8,13},{9,10},{10,... | collective-permute-start | bytes 245768 | tf_op jit(solution)/shard_map/ppermute | solution.py:467
  9.9 4.7 %collective-permute-start.6 = (bf16[64,640]{1,0:T(8,128)(2,1)S(1)}, bf16[64,640]{1,0:T(8,128)(2,1)S(1)}, u32[]{:S(2)}, u32[]{:S(2)}) collective-permute-start(bf16[64,640]{1,0:T(8,128)(2,1)S(1)} %get-tuple-element.41), channel_id=1, source_target_pairs={{0,1},{1,0},{2,3},{3,2},{4,5},{5,4},{6,7},{7,6},{8,9},{9,8},{10,11... | collective-permute-start | bytes 245768 | tf_op jit(solution)/shard_map/ppermute | solution.py:467
  12.1 10.4 %collective-permute-start.10 = (bf16[800,128]{1,0:T(8,128)(2,1)S(1)}, bf16[800,128]{1,0:T(8,128)(2,1)S(1)}, u32[]{:S(2)}, u32[]{:S(2)}) collective-permute-start(bf16[800,128]{1,0:T(8,128)(2,1)S(1)} %get-tuple-element.44), channel_id=1, source_target_pairs={{0,8},{1,25},{2,10},{3,27},{4,12},{5,29},{6,14},{7,31},{8,16},{9,1... | collective-permute-start | bytes 614408 | tf_op jit(solution)/shard_map/ppermute | solution.py:476
  15.9 10.6 %collective-permute-start.13 = (bf16[640,128]{1,0:T(8,128)(2,1)S(1)}, bf16[640,128]{1,0:T(8,128)(2,1)S(1)}, u32[]{:S(2)}, u32[]{:S(2)}) collective-permute-start(bf16[640,128]{1,0:T(8,128)(2,1)S(1)} %attend.1.token_ref.rest_0_), channel_id=1, source_target_pairs={{0,4},{1,3},{2,6},{3,1},{4,0},{5,7},{6,2},{7,5},{8,12},{9,11},{10,... | collective-permute-start | bytes 491528 | tf_op jit(solution)/shard_map/ppermute | solution.py:467
  17.1 9.4 %collective-permute-start.15 = (bf16[640,128]{1,0:T(8,128)(2,1)S(1)}, bf16[640,128]{1,0:T(8,128)(2,1)S(1)}, u32[]{:S(2)}, u32[]{:S(2)}) collective-permute-start(bf16[640,128]{1,0:T(8,128)(2,1)S(1)} %attend.1.token_ref.rest_0_), channel_id=1, source_target_pairs={{0,2},{1,5},{2,0},{3,7},{4,6},{5,1},{6,4},{7,3},{8,10},{9,13},{10,... | collective-permute-start | bytes 491528 | tf_op jit(solution)/shard_map/ppermute | solution.py:467
  17.9 9.4 %collective-permute-start.7 = (bf16[640,128]{1,0:T(8,128)(2,1)S(1)}, bf16[640,128]{1,0:T(8,128)(2,1)S(1)}, u32[]{:S(2)}, u32[]{:S(2)}) collective-permute-start(bf16[640,128]{1,0:T(8,128)(2,1)S(1)} %attend.1.token_ref.rest_0_), channel_id=1, source_target_pairs={{0,6},{1,7},{2,4},{3,5},{4,2},{5,3},{6,0},{7,1},{8,14},{9,15},{10,... | collective-permute-start | bytes 491528 | tf_op jit(solution)/shard_map/ppermute | solution.py:467
  19.4 7.6 %collective-permute-start.9 = (bf16[400,128]{1,0:T(8,128)(2,1)S(1)}, bf16[400,128]{1,0:T(8,128)(2,1)S(1)}, u32[]{:S(2)}, u32[]{:S(2)}) collective-permute-start(bf16[400,128]{1,0:T(8,128)(2,1)S(1)} %get-tuple-element.43.rest_8_), channel_id=1, source_target_pairs={{0,16},{1,17},{2,18},{3,19},{4,20},{5,21},{6,22},{7,23},{8,24},{9,... | collective-permute-start | bytes 307208 | tf_op jit(solution)/shard_map/ppermute | solution.py:476
  22.4 4.6 %collective-permute-start.11 = (bf16[800,128]{1,0:T(8,128)(2,1)S(1)}, bf16[800,128]{1,0:T(8,128)(2,1)S(1)}, u32[]{:S(2)}, u32[]{:S(2)}) collective-permute-start(bf16[800,128]{1,0:T(8,128)(2,1)S(1)} %collective-permute-done.10.rest_9_), channel_id=1, source_target_pairs={{0,1},{1,0},{2,3},{3,2},{4,5},{5,4},{6,7},{7,6},{8,9},{9,8},{10,11... | collective-permute-start | bytes 614408 | tf_op jit(solution)/shard_map/ppermute | solution.py:467
  26.5 1.8 %collective-permute-start.14 = (bf16[640,128]{1,0:T(8,128)(2,1)S(1)}, bf16[640,128]{1,0:T(8,128)(2,1)S(1)}, u32[]{:S(2)}, u32[]{:S(2)}) collective-permute-start(bf16[640,128]{1,0:T(8,128)(2,1)S(1)} %collective-permute-done.13.rest_1_), channel_id=1, source_target_pairs={{0,1},{1,0},{2,3},{3,2},{4,5},{5,4},{6,7},{7,6},{8,9},{9,8},{10,11... | collective-permute-start | bytes 491528 | tf_op jit(solution)/shard_map/ppermute | solution.py:467
  26.5 1.8 %collective-permute-start.16 = (bf16[640,128]{1,0:T(8,128)(2,1)S(1)}, bf16[640,128]{1,0:T(8,128)(2,1)S(1)}, u32[]{:S(2)}, u32[]{:S(2)}) collective-permute-start(bf16[640,128]{1,0:T(8,128)(2,1)S(1)} %collective-permute-done.15.rest_2_), channel_id=1, source_target_pairs={{0,1},{1,0},{2,3},{3,2},{4,5},{5,4},{6,7},{7,6},{8,9},{9,8},{10,11... | collective-permute-start | bytes 491528 | tf_op jit(solution)/shard_map/ppermute | solution.py:467
  27.2 1.5 %collective-permute-start.12 = (bf16[640,128]{1,0:T(8,128)(2,1)S(1)}, bf16[640,128]{1,0:T(8,128)(2,1)S(1)}, u32[]{:S(2)}, u32[]{:S(2)}) collective-permute-start(bf16[640,128]{1,0:T(8,128)(2,1)S(1)} %attend.1.token_ref.rest_0_), channel_id=1, source_target_pairs={{0,1},{1,0},{2,3},{3,2},{4,5},{5,4},{6,7},{7,6},{8,9},{9,8},{10,11... | collective-permute-start | bytes 491528 | tf_op jit(solution)/shard_map/ppermute | solution.py:467
  27.3 1.9 %collective-permute-start.8 = (bf16[640,128]{1,0:T(8,128)(2,1)S(1)}, bf16[640,128]{1,0:T(8,128)(2,1)S(1)}, u32[]{:S(2)}, u32[]{:S(2)}) collective-permute-start(bf16[640,128]{1,0:T(8,128)(2,1)S(1)} %collective-permute-done.7.rest_0_), channel_id=1, source_target_pairs={{0,1},{1,0},{2,3},{3,2},{4,5},{5,4},{6,7},{7,6},{8,9},{9,8},{10,11... | collective-permute-start | bytes 491528 | tf_op jit(solution)/shard_map/ppermute | solution.py:467
  29.9 10.7 %collective-permute-start.17 = (bf16[656,128]{1,0:T(8,128)(2,1)S(1)}, bf16[656,128]{1,0:T(8,128)(2,1)S(1)}, u32[]{:S(2)}, u32[]{:S(2)}) collective-permute-start(bf16[656,128]{1,0:T(8,128)(2,1)S(1)} %project.1.token_ref.rest_0_), channel_id=1, source_target_pairs={{0,4},{1,3},{2,6},{3,1},{4,0},{5,7},{6,2},{7,5},{8,12},{9,11},{10,... | collective-permute-start | bytes 503816 | tf_op jit(solution)/shard_map/ppermute | solution.py:467
  30.6 9.9 %collective-permute-start.18 = (bf16[656,128]{1,0:T(8,128)(2,1)S(1)}, bf16[656,128]{1,0:T(8,128)(2,1)S(1)}, u32[]{:S(2)}, u32[]{:S(2)}) collective-permute-start(bf16[656,128]{1,0:T(8,128)(2,1)S(1)} %project.1.token_ref.rest_0_), channel_id=1, source_target_pairs={{0,2},{1,5},{2,0},{3,7},{4,6},{5,1},{6,4},{7,3},{8,10},{9,13},{10,... | collective-permute-start | bytes 503816 | tf_op jit(solution)/shard_map/ppermute | solution.py:467
  31.8 9.9 %collective-permute-start.22 = (bf16[656,128]{1,0:T(8,128)(2,1)S(1)}, bf16[656,128]{1,0:T(8,128)(2,1)S(1)}, u32[]{:S(2)}, u32[]{:S(2)}) collective-permute-start(bf16[656,128]{1,0:T(8,128)(2,1)S(1)} %project.1.token_ref.rest_0_), channel_id=1, source_target_pairs={{0,6},{1,7},{2,4},{3,5},{4,2},{5,3},{6,0},{7,1},{8,14},{9,15},{10,... | collective-permute-start | bytes 503816 | tf_op jit(solution)/shard_map/ppermute | solution.py:467
  34.8 7.0 %collective-permute-start.19 = (bf16[656,128]{1,0:T(8,128)(2,1)S(1)}, bf16[656,128]{1,0:T(8,128)(2,1)S(1)}, u32[]{:S(2)}, u32[]{:S(2)}) collective-permute-start(bf16[656,128]{1,0:T(8,128)(2,1)S(1)} %project.1.token_ref.rest_0_), channel_id=1, source_target_pairs={{0,1},{1,0},{2,3},{3,2},{4,5},{5,4},{6,7},{7,6},{8,9},{9,8},{10,11... | collective-permute-start | bytes 503816 | tf_op jit(solution)/shard_map/ppermute | solution.py:467
  40.5 1.4 %collective-permute-start.20 = (bf16[656,128]{1,0:T(8,128)(2,1)S(1)}, bf16[656,128]{1,0:T(8,128)(2,1)S(1)}, u32[]{:S(2)}, u32[]{:S(2)}) collective-permute-start(bf16[656,128]{1,0:T(8,128)(2,1)S(1)} %collective-permute-done.17.rest_1_), channel_id=1, source_target_pairs={{0,1},{1,0},{2,3},{3,2},{4,5},{5,4},{6,7},{7,6},{8,9},{9,8},{10,11... | collective-permute-start | bytes 503816 | tf_op jit(solution)/shard_map/ppermute | solution.py:467
  40.5 1.6 %collective-permute-start.21 = (bf16[656,128]{1,0:T(8,128)(2,1)S(1)}, bf16[656,128]{1,0:T(8,128)(2,1)S(1)}, u32[]{:S(2)}, u32[]{:S(2)}) collective-permute-start(bf16[656,128]{1,0:T(8,128)(2,1)S(1)} %collective-permute-done.18.rest_2_), channel_id=1, source_target_pairs={{0,1},{1,0},{2,3},{3,2},{4,5},{5,4},{6,7},{7,6},{8,9},{9,8},{10,11... | collective-permute-start | bytes 503816 | tf_op jit(solution)/shard_map/ppermute | solution.py:467
  42.2 1.4 %collective-permute-start.23 = (bf16[656,128]{1,0:T(8,128)(2,1)S(1)}, bf16[656,128]{1,0:T(8,128)(2,1)S(1)}, u32[]{:S(2)}, u32[]{:S(2)}) collective-permute-start(bf16[656,128]{1,0:T(8,128)(2,1)S(1)} %collective-permute-done.22.rest_6_), channel_id=1, source_target_pairs={{0,1},{1,0},{2,3},{3,2},{4,5},{5,4},{6,7},{7,6},{8,9},{9,8},{10,11... | collective-permute-start | bytes 503816 | tf_op jit(solution)/shard_map/ppermute | solution.py:467
  (2 other events, 10.7 us)

commit v15 on v12

--- a/solution.py
+++ b/solution.py
@@ -122,8 +122,9 @@
 REST = HPAIR - WIDE
 MAIN = ROWS * WIDE
 NOTES = 16
-BLOCK_ORDER = (0, 4, 2, 6, 7, 3, 5, 1)
-PIECE_ORDER = (0, 4, 2, 1, 5, 3, 6, 7)
+RECEIVERS = ((0, 0), (6, 6), (7, 7), (4, 2), (2, 4), (3, 5), (5, 3), (1, 1))
+SENDERS = ((0, 0), (6, 6), (7, 7), (4, 2), (2, 4), (5, 3), (3, 5), (1, 1))
+OWNERS = (0, 4, 2, 1, 5, 3, 6, 7)
 ROOT = math.log2(math.e) / math.sqrt(HDIM)
 BF16 = jnp.bfloat16
 F32 = jnp.float32
@@ -131,6 +132,11 @@
 
 def row_index():
     return lax.axis_index("row")
+
+
+def steps(pairs):
+    core = row_index() % 2
+    return [even + (odd - even) * core for even, odd in pairs]
 
 
 def pack_tail(wide):
@@ -173,8 +179,8 @@
         parts.append(resid[:, dest * WIDE : (dest + 1) * WIDE])
         parts.append(resid[:, MAIN + dest * REST : MAIN + (dest + 1) * REST])
         held[dest] = jnp.concatenate(parts, axis=1)
-    for step in range(ROWS):
-        outs[step][...] = held[me ^ step]
+    for step, out in zip(steps(RECEIVERS), outs):
+        out[...] = held[me ^ step]
 
 
 def layout_kernel(grid_ref, *rest):
@@ -203,7 +209,7 @@
     me = row_index()
     band = blocks[0].shape[0]
     patches = band * ROWS
-    for step, block in zip(BLOCK_ORDER, blocks):
+    for step, block in zip(steps(SENDERS), blocks):
         at = pl.ds(pl.multiple_of((me ^ step) * band, band), band)
         q_all[at, :] = block[:, :HPAIR]
         k_all[at, :] = block[:, HPAIR : 2 * HPAIR]
@@ -251,7 +257,7 @@
     me = row_index()
     page = lax.axis_index("page")
     band = blocks[0].shape[0]
-    for step, block in zip(BLOCK_ORDER, blocks):
+    for step, block in zip(steps(SENDERS), blocks):
         at = pl.ds(pl.multiple_of((me ^ step) * band, band), band)
         held[at, :] = block[:, 3 * HPAIR :]
     resid_ref[...] = jnp.dot(select_ref[...], held[...], preferred_element_type=F32)
@@ -297,13 +303,13 @@
     return lax.rem(lax.axis_index("page") + 1 + 2 * (row_index() % 2), PAGES)
 
 
-def add_features(steps, pieces, weights, before_ref, out_ref):
+def add_features(owners, pieces, weights, before_ref, out_ref):
     main_ref, tail_ref, last_main_ref, last_tail_ref = weights
     me = row_index()
     patches = out_ref.shape[0]
     groups = patches // 4
     mains, tails = [], []
-    for step in steps:
+    for step in owners:
         pair = me ^ step
         columns = pl.ds(pl.multiple_of(pair * WIDE, WIDE), WIDE)
         late = pl.ds(pl.multiple_of(pair % 2 * WIDE, WIDE), WIDE)
@@ -318,12 +324,12 @@
         out_ref[span, :] = base[span] + jnp.dot(rows[patches:], tail, preferred_element_type=F32)
 
 
-def project_first_kernel(own, y, x, *rest):
-    add_features((0, 4, 2), (own, y, x), rest[:4], *rest[4:])
-
-
-def project_second_kernel(own, y, x, *rest):
-    add_features((1, 5, 3), (own, y, x), rest[:4], *rest[4:])
+def project_first_kernel(*rest):
+    add_features(OWNERS[:3], rest[:3], rest[3:7], *rest[7:])
+
+
+def project_second_kernel(*rest):
+    add_features(OWNERS[3:6], rest[:3], rest[3:7], *rest[7:])
 
 
 def project_kernel(*rest):
@@ -384,15 +390,16 @@
     )
 
 
-def merge_first_kernel(own, y, x, weight_ref, sum_ref):
-    for corner in range(4):
-        sum_ref[corner] = merge_product(weight_ref, corner, sum_ref.shape[2], [(0, own), (4, y), (2, x)])
-
-
-def merge_second_kernel(own, y, x, before_ref, weight_ref, sum_ref):
-    for corner in range(4):
-        part = merge_product(weight_ref, corner, sum_ref.shape[2], [(1, own), (5, y), (3, x)])
-        sum_ref[corner] = before_ref[corner] + part
+def merge_first_kernel(*rest):
+    pieces, (weight_ref, sum_ref) = list(zip(OWNERS[:3], rest[:3])), rest[3:]
+    for corner in range(4):
+        sum_ref[corner] = merge_product(weight_ref, corner, sum_ref.shape[2], pieces)
+
+
+def merge_second_kernel(*rest):
+    pieces, (before_ref, weight_ref, sum_ref) = list(zip(OWNERS[3:6], rest[:3])), rest[3:]
+    for corner in range(4):
+        sum_ref[corner] = before_ref[corner] + merge_product(weight_ref, corner, sum_ref.shape[2], pieces)
 
 
 def merge_kernel(*rest):
@@ -416,11 +423,11 @@
             )
         )
     notes = jnp.zeros((NOTES, groups), F32)
-    for step, piece in zip(PIECE_ORDER, pieces):
+    for step, piece in zip(OWNERS, pieces):
         notes = notes + piece[patches + groups :, :].astype(F32)
     scale = lax.rsqrt((notes[:4] + notes[4:8]) * (1.0 / D) + 1e-06)
     spread = jnp.concatenate([jnp.broadcast_to(scale[at : at + 1], (REST, groups)) for at in range(4)], axis=0).T
-    for step, piece in zip(PIECE_ORDER, pieces):
+    for step, piece in zip(OWNERS, pieces):
         at = pl.ds(pl.multiple_of((me ^ step) * WIDE, WIDE), WIDE)
         ends_ref[:, at] = (piece[patches : patches + groups, :].astype(F32) * spread).astype(BF16)
     total = bias_ref[...] + lax.dot_general(tail_ref[...], ends_ref[...], contract, preferred_element_type=F32)
@@ -454,8 +461,9 @@
     return jax.ShapeDtypeStruct(dims, dtype)
 
 
-def swap(value, step):
-    return lax.ppermute(value, "row", [(row, row ^ step) for row in range(ROWS)])
+def swap(value, even, odd=None):
+    odd = even if odd is None else odd
+    return lax.ppermute(value, "row", [(row, row ^ (odd if row % 2 else even)) for row in range(ROWS)])
 
 
 def turn(value, low, high):
@@ -499,15 +507,15 @@
         limit=24,
         moved=1 << 20,
     )(in_hbm(qkv_rows), in_hbm(residual), in_hbm(out_weight), in_hbm(page_grid))
-    blocks = [sends[0]] + [swap(sends[step], step) for step in BLOCK_ORDER[1:]]
+    blocks = [sends[0]] + [swap(send, *pair) for send, pair in zip(sends[1:], RECEIVERS[1:])]
     select, dead, live = kernel(
         layout_kernel,
         "layout",
         [shape(patches, patches), shape(1, patches, dtype=F32), shape(1, groups, dtype=F32)],
-        fetched=range(1, 1 + 3),
-        count=1 + 3,
+        fetched=range(1, 1 + 2),
+        count=1 + 2,
         moved=1 << 20,
-    )(grid, *blocks[1:4])
+    )(grid, *blocks[1:3])
     across = turn(after(own, *()), 2, 2)
     near = turn(after(chip, *()), 1, PAGES - 1)
     swapped = swap(near, 1)
@@ -538,11 +546,11 @@
         count=2,
         moved=4 << 20,
     )(swapped, main)
-    y, x, far = [swap(attn, step) for step in (4, 2, 6)]
+    one, two, far = swap(attn, 4), swap(attn, 2), swap(attn, 6)
     weights = (main, tail, *last)
     rows = shape(patches, HPAIR, dtype=F32)
-    first = kernel(project_first_kernel, "project_first", rows, count=8, flops=1, moved=1)(attn, y, x, *weights, resid)
-    near = [swap(after(attn, main), 1), swap(after(y, last[0]), 1), swap(x, 1)]
+    first = kernel(project_first_kernel, "project_first", rows, count=8, flops=1, moved=1)(attn, one, two, *weights, resid)
+    near = [swap(after(attn, main), 1), swap(after(one, last[0]), 1), swap(two, 1)]
     second = kernel(project_second_kernel, "project_second", rows, count=8, flops=1, moved=1)(*near, *weights, first)
     hidden = kernel(
         project_kernel,
@@ -562,9 +570,9 @@
         moved=4 << 20,
     )(merge_weight, in_hbm(merge_bias), hidden)
     sums = shape(4, units, groups, dtype=F32)
-    y, x, far = [swap(hidden, step) for step in (4, 2, 6)]
-    first = kernel(merge_first_kernel, "merge_first", sums, count=4, flops=1, moved=1)(hidden, y, x, merge_weight)
-    near = [swap(after(hidden, ends), 1), swap(y, 1), swap(x, 1)]
+    one, two, far = swap(hidden, 4), swap(hidden, 2), swap(hidden, 6)
+    first = kernel(merge_first_kernel, "merge_first", sums, count=4, flops=1, moved=1)(hidden, one, two, merge_weight)
+    near = [swap(after(hidden, ends), 1), swap(one, 1), swap(two, 1)]
     second = kernel(merge_second_kernel, "merge_second", sums, count=5, flops=1, moved=1)(*near, first, merge_weight)
     return kernel(
         merge_kernel,
@@ -574,7 +582,7 @@
         count=ROWS + 5,
         flops=4 * units * groups * MAIN,
         moved=8 << 20,
-    )(hidden, y, x, *near, far, swap(after(far, first, *near), 1), second, merge_weight, ends, bias, live)
+    )(hidden, one, two, *near, far, swap(after(far, first, *near), 1), second, merge_weight, ends, bias, live)
 
 
 def solution(mesh):

time: 45.1 us -> 44.3 us (0.982)
  waiting for transfers between devices: 14.2 us -> 12.8 us
  starting transfers between devices: 19.8 us -> 20.4 us
    ppermute x22, waiting for transfers between devices: 11.9 us -> 9.84 us  [swap(): lax.ppermute(value, 'row', [(row, row ^ (odd if row % 2 else even)) for r...]
    ppermute x22, starting transfers between devices: 15.5 us -> 16.3 us  [swap(): lax.ppermute(value, 'row', [(row, row ^ (odd if row % 2 else even)) for r...]
    ppermute x2, waiting for transfers between devices: 2.27 us -> 3 us  [turn(): return lax.ppermute(value, ('page', 'row'), pairs)]
  transfers between devices with their start and end apart: 24 -> 24, of which waited for: 10 -> 12; matrix products, arithmetic and copies ran while one was open for 0% -> 0% of each run, Pallas kernels for 15% -> 15%
where the time goes in v15:
time: 44.3 us; the launch traced here: 44.2 us
  starting transfers between devices  20.4 us (46%)
  waiting for transfers between devices  12.8 us (29%)
  Pallas kernels  10.7 us (24%)
    ppermute x22, starting transfers between devices, swap(): lax.ppermute(value, 'row', [(row, row ^ (odd if row % 2 else even)) for r...  16.3 us
    ppermute x22, waiting for transfers between devices, swap(): lax.ppermute(value, 'row', [(row, row ^ (odd if row % 2 else even)) for r...  9.84 us
    ppermute x2, starting transfers between devices, turn(): return lax.ppermute(value, ('page', 'row'), pairs)  4.17 us
    ppermute x2, waiting for transfers between devices, turn(): return lax.ppermute(value, ('page', 'row'), pairs)  3 us
    pallas_call x1, Pallas kernels, local_eight(): kernel(spread_kernel, 'spread', [shape(band, 4 * HPAIR)] * ROWS + [shape(...  1.76 us
    pallas_call x1, Pallas kernels, local_eight(): kernel(merge_kernel, 'merge', shape(1, units, groups), [pltpu.VMEM((group...  1.68 us
    pallas_call x1, Pallas kernels, local_eight(): kernel(tail_kernel, 'merge_tail', [shape(units, MAIN), shape(units, 1, dt...  1.39 us
    pallas_call x1, Pallas kernels, local_eight(): kernel(attend_kernel, 'attend', shape(piece, WIDE), [pltpu.VMEM((patches,...  1.36 us
  transfers between devices with their start and end apart: 24, of which 12 were waited for; matrix products, arithmetic and copies ran while one was open for 0% of the time, Pallas kernels for 15%

profile of v15, /device:TPU:0, one launch (start us, length us, event | category | flops | bytes accessed | tf_op | source)
XLA Modules:
  0.0 44.2 jit_solution(8351184142249952416)
XLA Ops:
  0.0 1.8 %spread.1 = (bf16[64,640]{1,0:T(8,128)(2,1)S(1)}, bf16[64,640]{1,0:T(8,128)(2,1)S(1)}, bf16[64,640]{1,0:T(8,128)(2,1)S(1)}, bf16[64,640]{1,0:T(8,128)(2,1)S(1)},...) custom-call(bf16[1,64,3840]{2,1,0:T(8,128)(2,1)} %qkv_hbm.1, ...), custom_call_target="tpu_custom_call" | custom-call | bytes 1048576 | tf_op jit(solution)/shard_map/spread/pallas_call | solution.py:491
  1.8 4.0 %collective-permute-start = (bf16[64,640]{1,0:T(8,128)(2,1)S(1)}, bf16[64,640]{1,0:T(8,128)(2,1)S(1)}, u32[]{:S(2)}, u32[]{:S(2)}) collective-permute-start(bf16[64,640]{1,0:T(8,128)(2,1)S(1)} %get-tuple-element.33), channel_id=1, source_target_pairs={{0,6},{1,7},{2,4},{3,5},{4,2},{5,3},{6,0},{7,1},{8,14},{9,15},{10,... | collective-permute-start | bytes 245768 | tf_op jit(solution)/shard_map/ppermute | solution.py:466
  5.7 1.2 %collective-permute-start.2 = (bf16[64,640]{1,0:T(8,128)(2,1)S(1)}, bf16[64,640]{1,0:T(8,128)(2,1)S(1)}, u32[]{:S(2)}, u32[]{:S(2)}) collective-permute-start(bf16[64,640]{1,0:T(8,128)(2,1)S(1)} %get-tuple-element.38), channel_id=1, source_target_pairs={{0,4},{1,3},{2,6},{3,1},{4,0},{5,7},{6,2},{7,5},{8,12},{9,11},{10,... | collective-permute-start | bytes 245768 | tf_op jit(solution)/shard_map/ppermute | solution.py:466
  6.9 1.5 %collective-permute-start.3 = (bf16[64,640]{1,0:T(8,128)(2,1)S(1)}, bf16[64,640]{1,0:T(8,128)(2,1)S(1)}, u32[]{:S(2)}, u32[]{:S(2)}) collective-permute-start(bf16[64,640]{1,0:T(8,128)(2,1)S(1)} %get-tuple-element.39), channel_id=1, source_target_pairs={{0,2},{1,5},{2,0},{3,7},{4,6},{5,1},{6,4},{7,3},{8,10},{9,13},{10,... | collective-permute-start | bytes 245768 | tf_op jit(solution)/shard_map/ppermute | solution.py:466
  8.9 1.2 %collective-permute-start.5 = (bf16[64,640]{1,0:T(8,128)(2,1)S(1)}, bf16[64,640]{1,0:T(8,128)(2,1)S(1)}, u32[]{:S(2)}, u32[]{:S(2)}) collective-permute-start(bf16[64,640]{1,0:T(8,128)(2,1)S(1)} %get-tuple-element.41), channel_id=1, source_target_pairs={{0,5},{1,2},{2,7},{3,0},{4,1},{5,6},{6,3},{7,4},{8,13},{9,10},{10,... | collective-permute-start | bytes 245768 | tf_op jit(solution)/shard_map/ppermute | solution.py:466
  10.1 1.3 %collective-permute-done.1.rest_1_.rest_2_ = bf16[64,640]{1,0:T(8,128)(2,1)S(1)} collective-permute-done((bf16[64,640]{1,0:T(8,128)(2,1)S(1)}, bf16[64,640]{1,0:T(8,128)(2,1)S(1)}, u32[]{:S(2)}, u32[]{:S(2)}) %collective-permute-start.1) | collective-permute-done | bytes 81952 | tf_op jit(solution)/shard_map/ppermute | solution.py:466
  11.6 1.0 %collective-permute-done.2.rest_3_ = bf16[64,640]{1,0:T(8,128)(2,1)S(1)} collective-permute-done((bf16[64,640]{1,0:T(8,128)(2,1)S(1)}, bf16[64,640]{1,0:T(8,128)(2,1)S(1)}, u32[]{:S(2)}, u32[]{:S(2)}) %collective-permute-start.2) | collective-permute-done | bytes 81952 | tf_op jit(solution)/shard_map/ppermute | solution.py:466
  12.6 1.6 %collective-permute-start.11 = (bf16[800,128]{1,0:T(8,128)(2,1)S(1)}, bf16[800,128]{1,0:T(8,128)(2,1)S(1)}, u32[]{:S(2)}, u32[]{:S(2)}) collective-permute-start(bf16[800,128]{1,0:T(8,128)(2,1)S(1)} %get-tuple-element.44), channel_id=1, source_target_pairs={{0,8},{1,25},{2,10},{3,27},{4,12},{5,29},{6,14},{7,31},{8,16},{9,1... | collective-permute-start | bytes 614408 | tf_op jit(solution)/shard_map/ppermute | solution.py:475
  14.2 2.6 %collective-permute-start.10 = (bf16[400,128]{1,0:T(8,128)(2,1)S(1)}, bf16[400,128]{1,0:T(8,128)(2,1)S(1)}, u32[]{:S(2)}, u32[]{:S(2)}) collective-permute-start(bf16[400,128]{1,0:T(8,128)(2,1)S(1)} %get-tuple-element.43.rest_8_), channel_id=1, source_target_pairs={{0,16},{1,17},{2,18},{3,19},{4,20},{5,21},{6,22},{7,23},{8,24},{9,... | collective-permute-start | bytes 307208 | tf_op jit(solution)/shard_map/ppermute | solution.py:475
  16.8 1.4 %attend.1.token_ref.rest_0_ = bf16[640,128]{1,0:T(8,128)(2,1)S(1)} custom-call(bf16[512,512]{1,0:T(8,128)(2,1)S(1)} %get-tuple-element.35.select_ref, f32[1,512]{1,0:T(1,128)S(1)} %get-tuple-element.36.dead_ref, bf16[64,640]{1,0:T(8,128)(2,1)S(1)} %get-tuple-element.37.rest_0_, bf16[64,640]{1,0:T(8,128)(2,1)S(1)} %collective-permute-done.rest_0_.rest_1_, ...), custom_call_target="tpu_custom_call" | custom-call | flops 21474836480 | bytes 1048576 | tf_op jit(solution)/shard_map/attend/pallas_call | solution.py:522
  18.2 1.0 %collective-permute-start.8 = (bf16[640,128]{1,0:T(8,128)(2,1)S(1)}, bf16[640,128]{1,0:T(8,128)(2,1)S(1)}, u32[]{:S(2)}, u32[]{:S(2)}) collective-permute-start(bf16[640,128]{1,0:T(8,128)(2,1)S(1)} %attend.1.token_ref.rest_0_), channel_id=1, source_target_pairs={{0,4},{1,5},{2,6},{3,7},{4,0},{5,1},{6,2},{7,3},{8,12},{9,13},{10,... | collective-permute-start | bytes 491528 | tf_op jit(solution)/shard_map/ppermute | solution.py:466
  19.2 1.5 %collective-permute-start.9 = (bf16[640,128]{1,0:T(8,128)(2,1)S(1)}, bf16[640,128]{1,0:T(8,128)(2,1)S(1)}, u32[]{:S(2)}, u32[]{:S(2)}) collective-permute-start(bf16[640,128]{1,0:T(8,128)(2,1)S(1)} %attend.1.token_ref.rest_0_), channel_id=1, source_target_pairs={{0,2},{1,3},{2,0},{3,1},{4,6},{5,7},{6,4},{7,5},{8,10},{9,11},{10,... | collective-permute-start | bytes 491528 | tf_op jit(solution)/shard_map/ppermute | solution.py:466
  20.6 1.1 %collective-permute-start.7 = (bf16[640,128]{1,0:T(8,128)(2,1)S(1)}, bf16[640,128]{1,0:T(8,128)(2,1)S(1)}, u32[]{:S(2)}, u32[]{:S(2)}) collective-permute-start(bf16[640,128]{1,0:T(8,128)(2,1)S(1)} %attend.1.token_ref.rest_0_), channel_id=1, source_target_pairs={{0,6},{1,7},{2,4},{3,5},{4,2},{5,3},{6,0},{7,1},{8,14},{9,15},{10,... | collective-permute-start | bytes 491528 | tf_op jit(solution)/shard_map/ppermute | solution.py:466
  21.7 0.7 %collective-permute-done.11.rest_10_ = bf16[800,128]{1,0:T(8,128)(2,1)S(1)} collective-permute-done((bf16[800,128]{1,0:T(8,128)(2,1)S(1)}, bf16[800,128]{1,0:T(8,128)(2,1)S(1)}, u32[]{:S(2)}, u32[]{:S(2)}) %collective-permute-start.11) | collective-permute-done | bytes 204832 | tf_op jit(solution)/shard_map/ppermute | solution.py:475
  22.5 2.3 %collective-permute-done.10.rest_9_ = bf16[400,128]{1,0:T(8,128)(2,1)S(1)} collective-permute-done((bf16[400,128]{1,0:T(8,128)(2,1)S(1)}, bf16[400,128]{1,0:T(8,128)(2,1)S(1)}, u32[]{:S(2)}, u32[]{:S(2)}) %collective-permute-start.10) | collective-permute-done | bytes 102432 | tf_op jit(solution)/shard_map/ppermute | solution.py:475
  24.7 1.2 %ready.1 = (f32[512,160]{1,0:T(8,128)S(1)}, f32[1,160]{1,0:T(1,128)S(1)}, bf16[1024,160]{1,0:T(8,128)(2,1)S(1)}, bf16[4,1024,160]{2,1,0:T(8,128)(2,1)S(1)}) custom-call(bf16[512,512]{1,0:T(8,128)(2,1)S(1)} %get-tuple-element.35.select_ref, f32[1280]{0:T(1024)} %gain_hbm.1, bf16[640,128]{1,0:T(8,128)(2,1)S(1)} %attend.1.token_ref.rest_0_, ...), custom_call_target="tpu_custom_call" | custom-call | flops 10737418240 | bytes 4194304 | tf_op jit(solution)/shard_map/ready/pallas_call | solution.py:531
  29.9 1.6 %collective-permute-start.17 = (bf16[656,128]{1,0:T(8,128)(2,1)S(1)}, bf16[656,128]{1,0:T(8,128)(2,1)S(1)}, u32[]{:S(2)}, u32[]{:S(2)}) collective-permute-start(bf16[656,128]{1,0:T(8,128)(2,1)S(1)} %project.1.token_ref.rest_0_), channel_id=1, source_target_pairs={{0,4},{1,5},{2,6},{3,7},{4,0},{5,1},{6,2},{7,3},{8,12},{9,13},{10,... | collective-permute-start | bytes 503816 | tf_op jit(solution)/shard_map/ppermute | solution.py:466
  32.0 1.4 %collective-permute-start.22 = (bf16[656,128]{1,0:T(8,128)(2,1)S(1)}, bf16[656,128]{1,0:T(8,128)(2,1)S(1)}, u32[]{:S(2)}, u32[]{:S(2)}) collective-permute-start(bf16[656,128]{1,0:T(8,128)(2,1)S(1)} %project.1.token_ref.rest_0_), channel_id=1, source_target_pairs={{0,6},{1,7},{2,4},{3,5},{4,2},{5,3},{6,0},{7,1},{8,14},{9,15},{10,... | collective-permute-start | bytes 503816 | tf_op jit(solution)/shard_map/ppermute | solution.py:466
  33.4 1.4 %merge_tail.1 = (bf16[640,1024]{1,0:T(8,128)(2,1)S(1)}, f32[640,1]{1,0:T(8,128)S(1)}) custom-call(bf16[640,5120]{1,0:T(8,128)(2,1)S(1)} %bitcast.1, f32[640]{0:T(1024)} %bias_hbm.1, bf16[656,128]{1,0:T(8,128)(2,1)S(1)} %project.1.token_ref.rest_0_), custom_call_target="tpu_custom_call" | custom-call | bytes 4194304 | tf_op jit(solution)/shard_map/merge_tail/pallas_call | solution.py:563
  34.9 1.4 %collective-permute-done.17.rest_1_ = bf16[656,128]{1,0:T(8,128)(2,1)S(1)} collective-permute-done((bf16[656,128]{1,0:T(8,128)(2,1)S(1)}, bf16[656,128]{1,0:T(8,128)(2,1)S(1)}, u32[]{:S(2)}, u32[]{:S(2)}) %collective-permute-start.17) | collective-permute-done | bytes 167968 | tf_op jit(solution)/shard_map/ppermute | solution.py:466
  36.3 2.4 %collective-permute-done.18.rest_2_ = bf16[656,128]{1,0:T(8,128)(2,1)S(1)} collective-permute-done((bf16[656,128]{1,0:T(8,128)(2,1)S(1)}, bf16[656,128]{1,0:T(8,128)(2,1)S(1)}, u32[]{:S(2)}, u32[]{:S(2)}) %collective-permute-start.18) | collective-permute-done | bytes 167968 | tf_op jit(solution)/shard_map/ppermute | solution.py:466
  39.4 1.7 %collective-permute-done.22.rest_6_ = bf16[656,128]{1,0:T(8,128)(2,1)S(1)} collective-permute-done((bf16[656,128]{1,0:T(8,128)(2,1)S(1)}, bf16[656,128]{1,0:T(8,128)(2,1)S(1)}, u32[]{:S(2)}, u32[]{:S(2)}) %collective-permute-start.22) | collective-permute-done | bytes 167968 | tf_op jit(solution)/shard_map/ppermute | solution.py:466
  41.1 0.7 %merge_second.1.rest_8_ = f32[4,640,128]{2,1,0:T(8,128)S(1)} custom-call(bf16[656,128]{1,0:T(8,128)(2,1)S(1)} %collective-permute-done.19.rest_0_.rest_3_, bf16[656,128]{1,0:T(8,128)(2,1)S(1)} %collective-permute-done.20.rest_1_.rest_4_, bf16[656,128]{1,0:T(8,128)(2,1)S(1)} %collective-permute-done.21.rest_2_.rest_5_, ...), custom_call_target="tpu_custom_call" | custom-call | flops 1 | bytes 1 | tf_op jit(solution)/shard_map/merge_second/pallas_call | solution.py:576
  42.5 1.7 %merge.1 = bf16[1,640,128]{2,1,0:T(8,128)(2,1)} custom-call(bf16[656,128]{1,0:T(8,128)(2,1)S(1)} %project.1.token_ref.rest_0_, bf16[656,128]{1,0:T(8,128)(2,1)S(1)} %collective-permute-done.17.rest_1_, bf16[656,128]{1,0:T(8,128)(2,1)S(1)} %collective-permute-done.18.rest_2_, bf16[656,128]{1,0:T(8,128)(2,1)S(1)} %collective-permute-done.19.rest_0_.rest_3_, ...), custom_call_target="tpu_custom_call" | custom-call | flops 335544320 | bytes 8388608 | tf_op jit(solution)/shard_map/merge/pallas_call | solution.py:577
  (41 shorter events, 6.6 us)
Async XLA Ops:
  1.8 7.1 %collective-permute-start = (bf16[64,640]{1,0:T(8,128)(2,1)S(1)}, bf16[64,640]{1,0:T(8,128)(2,1)S(1)}, u32[]{:S(2)}, u32[]{:S(2)}) collective-permute-start(bf16[64,640]{1,0:T(8,128)(2,1)S(1)} %get-tuple-element.33), channel_id=1, source_target_pairs={{0,6},{1,7},{2,4},{3,5},{4,2},{5,3},{6,0},{7,1},{8,14},{9,15},{10,... | collective-permute-start | bytes 245768 | tf_op jit(solution)/shard_map/ppermute | solution.py:466
  5.7 5.7 %collective-permute-start.1 = (bf16[64,640]{1,0:T(8,128)(2,1)S(1)}, bf16[64,640]{1,0:T(8,128)(2,1)S(1)}, u32[]{:S(2)}, u32[]{:S(2)}) collective-permute-start(bf16[64,640]{1,0:T(8,128)(2,1)S(1)} %get-tuple-element.34), channel_id=1, source_target_pairs={{0,7},{1,6},{2,5},{3,4},{4,3},{5,2},{6,1},{7,0},{8,15},{9,14},{10,... | collective-permute-start | bytes 245768 | tf_op jit(solution)/shard_map/ppermute | solution.py:466
  5.7 6.9 %collective-permute-start.2 = (bf16[64,640]{1,0:T(8,128)(2,1)S(1)}, bf16[64,640]{1,0:T(8,128)(2,1)S(1)}, u32[]{:S(2)}, u32[]{:S(2)}) collective-permute-start(bf16[64,640]{1,0:T(8,128)(2,1)S(1)} %get-tuple-element.38), channel_id=1, source_target_pairs={{0,4},{1,3},{2,6},{3,1},{4,0},{5,7},{6,2},{7,5},{8,12},{9,11},{10,... | collective-permute-start | bytes 245768 | tf_op jit(solution)/shard_map/ppermute | solution.py:466
  6.9 7.3 %collective-permute-start.3 = (bf16[64,640]{1,0:T(8,128)(2,1)S(1)}, bf16[64,640]{1,0:T(8,128)(2,1)S(1)}, u32[]{:S(2)}, u32[]{:S(2)}) collective-permute-start(bf16[64,640]{1,0:T(8,128)(2,1)S(1)} %get-tuple-element.39), channel_id=1, source_target_pairs={{0,2},{1,5},{2,0},{3,7},{4,6},{5,1},{6,4},{7,3},{8,10},{9,13},{10,... | collective-permute-start | bytes 245768 | tf_op jit(solution)/shard_map/ppermute | solution.py:466
  8.4 8.4 %collective-permute-start.4 = (bf16[64,640]{1,0:T(8,128)(2,1)S(1)}, bf16[64,640]{1,0:T(8,128)(2,1)S(1)}, u32[]{:S(2)}, u32[]{:S(2)}) collective-permute-start(bf16[64,640]{1,0:T(8,128)(2,1)S(1)} %get-tuple-element.40), channel_id=1, source_target_pairs={{0,3},{1,4},{2,1},{3,6},{4,7},{5,0},{6,5},{7,2},{8,11},{9,12},{10,... | collective-permute-start | bytes 245768 | tf_op jit(solution)/shard_map/ppermute | solution.py:466
  8.9 7.9 %collective-permute-start.5 = (bf16[64,640]{1,0:T(8,128)(2,1)S(1)}, bf16[64,640]{1,0:T(8,128)(2,1)S(1)}, u32[]{:S(2)}, u32[]{:S(2)}) collective-permute-start(bf16[64,640]{1,0:T(8,128)(2,1)S(1)} %get-tuple-element.41), channel_id=1, source_target_pairs={{0,5},{1,2},{2,7},{3,0},{4,1},{5,6},{6,3},{7,4},{8,13},{9,10},{10,... | collective-permute-start | bytes 245768 | tf_op jit(solution)/shard_map/ppermute | solution.py:466
  11.4 5.4 %collective-permute-start.6 = (bf16[64,640]{1,0:T(8,128)(2,1)S(1)}, bf16[64,640]{1,0:T(8,128)(2,1)S(1)}, u32[]{:S(2)}, u32[]{:S(2)}) collective-permute-start(bf16[64,640]{1,0:T(8,128)(2,1)S(1)} %get-tuple-element.42), channel_id=1, source_target_pairs={{0,1},{1,0},{2,3},{3,2},{4,5},{5,4},{6,7},{7,6},{8,9},{9,8},{10,11... | collective-permute-start | bytes 245768 | tf_op jit(solution)/shard_map/ppermute | solution.py:466
  12.6 9.8 %collective-permute-start.11 = (bf16[800,128]{1,0:T(8,128)(2,1)S(1)}, bf16[800,128]{1,0:T(8,128)(2,1)S(1)}, u32[]{:S(2)}, u32[]{:S(2)}) collective-permute-start(bf16[800,128]{1,0:T(8,128)(2,1)S(1)} %get-tuple-element.44), channel_id=1, source_target_pairs={{0,8},{1,25},{2,10},{3,27},{4,12},{5,29},{6,14},{7,31},{8,16},{9,1... | collective-permute-start | bytes 614408 | tf_op jit(solution)/shard_map/ppermute | solution.py:475
  14.2 10.5 %collective-permute-start.10 = (bf16[400,128]{1,0:T(8,128)(2,1)S(1)}, bf16[400,128]{1,0:T(8,128)(2,1)S(1)}, u32[]{:S(2)}, u32[]{:S(2)}) collective-permute-start(bf16[400,128]{1,0:T(8,128)(2,1)S(1)} %get-tuple-element.43.rest_8_), channel_id=1, source_target_pairs={{0,16},{1,17},{2,18},{3,19},{4,20},{5,21},{6,22},{7,23},{8,24},{9,... | collective-permute-start | bytes 307208 | tf_op jit(solution)/shard_map/ppermute | solution.py:475
  18.2 8.5 %collective-permute-start.8 = (bf16[640,128]{1,0:T(8,128)(2,1)S(1)}, bf16[640,128]{1,0:T(8,128)(2,1)S(1)}, u32[]{:S(2)}, u32[]{:S(2)}) collective-permute-start(bf16[640,128]{1,0:T(8,128)(2,1)S(1)} %attend.1.token_ref.rest_0_), channel_id=1, source_target_pairs={{0,4},{1,5},{2,6},{3,7},{4,0},{5,1},{6,2},{7,3},{8,12},{9,13},{10,... | collective-permute-start | bytes 491528 | tf_op jit(solution)/shard_map/ppermute | solution.py:466
  19.2 7.0 %collective-permute-start.9 = (bf16[640,128]{1,0:T(8,128)(2,1)S(1)}, bf16[640,128]{1,0:T(8,128)(2,1)S(1)}, u32[]{:S(2)}, u32[]{:S(2)}) collective-permute-start(bf16[640,128]{1,0:T(8,128)(2,1)S(1)} %attend.1.token_ref.rest_0_), channel_id=1, source_target_pairs={{0,2},{1,3},{2,0},{3,1},{4,6},{5,7},{6,4},{7,5},{8,10},{9,11},{10,... | collective-permute-start | bytes 491528 | tf_op jit(solution)/shard_map/ppermute | solution.py:466
  20.6 7.2 %collective-permute-start.7 = (bf16[640,128]{1,0:T(8,128)(2,1)S(1)}, bf16[640,128]{1,0:T(8,128)(2,1)S(1)}, u32[]{:S(2)}, u32[]{:S(2)}) collective-permute-start(bf16[640,128]{1,0:T(8,128)(2,1)S(1)} %attend.1.token_ref.rest_0_), channel_id=1, source_target_pairs={{0,6},{1,7},{2,4},{3,5},{4,2},{5,3},{6,0},{7,1},{8,14},{9,15},{10,... | collective-permute-start | bytes 491528 | tf_op jit(solution)/shard_map/ppermute | solution.py:466
  22.5 4.1 %collective-permute-start.12 = (bf16[800,128]{1,0:T(8,128)(2,1)S(1)}, bf16[800,128]{1,0:T(8,128)(2,1)S(1)}, u32[]{:S(2)}, u32[]{:S(2)}) collective-permute-start(bf16[800,128]{1,0:T(8,128)(2,1)S(1)} %collective-permute-done.11.rest_10_), channel_id=1, source_target_pairs={{0,1},{1,0},{2,3},{3,2},{4,5},{5,4},{6,7},{7,6},{8,9},{9,8},{10,11... | collective-permute-start | bytes 614408 | tf_op jit(solution)/shard_map/ppermute | solution.py:466
  26.0 1.9 %collective-permute-start.14 = (bf16[640,128]{1,0:T(8,128)(2,1)S(1)}, bf16[640,128]{1,0:T(8,128)(2,1)S(1)}, u32[]{:S(2)}, u32[]{:S(2)}) collective-permute-start(bf16[640,128]{1,0:T(8,128)(2,1)S(1)} %attend.1.token_ref.rest_0_), channel_id=1, source_target_pairs={{0,1},{1,0},{2,3},{3,2},{4,5},{5,4},{6,7},{7,6},{8,9},{9,8},{10,11... | collective-permute-start | bytes 491528 | tf_op jit(solution)/shard_map/ppermute | solution.py:466
  26.2 1.6 %collective-permute-start.16 = (bf16[640,128]{1,0:T(8,128)(2,1)S(1)}, bf16[640,128]{1,0:T(8,128)(2,1)S(1)}, u32[]{:S(2)}, u32[]{:S(2)}) collective-permute-start(bf16[640,128]{1,0:T(8,128)(2,1)S(1)} %collective-permute-done.9.rest_2_), channel_id=1, source_target_pairs={{0,1},{1,0},{2,3},{3,2},{4,5},{5,4},{6,7},{7,6},{8,9},{9,8},{10,11... | collective-permute-start | bytes 491528 | tf_op jit(solution)/shard_map/ppermute | solution.py:466
  26.7 1.5 %collective-permute-start.15 = (bf16[640,128]{1,0:T(8,128)(2,1)S(1)}, bf16[640,128]{1,0:T(8,128)(2,1)S(1)}, u32[]{:S(2)}, u32[]{:S(2)}) collective-permute-start(bf16[640,128]{1,0:T(8,128)(2,1)S(1)} %collective-permute-done.8.rest_1_), channel_id=1, source_target_pairs={{0,1},{1,0},{2,3},{3,2},{4,5},{5,4},{6,7},{7,6},{8,9},{9,8},{10,11... | collective-permute-start | bytes 491528 | tf_op jit(solution)/shard_map/ppermute | solution.py:466
  27.8 1.4 %collective-permute-start.13 = (bf16[640,128]{1,0:T(8,128)(2,1)S(1)}, bf16[640,128]{1,0:T(8,128)(2,1)S(1)}, u32[]{:S(2)}, u32[]{:S(2)}) collective-permute-start(bf16[640,128]{1,0:T(8,128)(2,1)S(1)} %collective-permute-done.7.rest_0_), channel_id=1, source_target_pairs={{0,1},{1,0},{2,3},{3,2},{4,5},{5,4},{6,7},{7,6},{8,9},{9,8},{10,11... | collective-permute-start | bytes 491528 | tf_op jit(solution)/shard_map/ppermute | solution.py:466
  29.9 6.4 %collective-permute-start.17 = (bf16[656,128]{1,0:T(8,128)(2,1)S(1)}, bf16[656,128]{1,0:T(8,128)(2,1)S(1)}, u32[]{:S(2)}, u32[]{:S(2)}) collective-permute-start(bf16[656,128]{1,0:T(8,128)(2,1)S(1)} %project.1.token_ref.rest_0_), channel_id=1, source_target_pairs={{0,4},{1,5},{2,6},{3,7},{4,0},{5,1},{6,2},{7,3},{8,12},{9,13},{10,... | collective-permute-start | bytes 503816 | tf_op jit(solution)/shard_map/ppermute | solution.py:466
  31.5 7.2 %collective-permute-start.18 = (bf16[656,128]{1,0:T(8,128)(2,1)S(1)}, bf16[656,128]{1,0:T(8,128)(2,1)S(1)}, u32[]{:S(2)}, u32[]{:S(2)}) collective-permute-start(bf16[656,128]{1,0:T(8,128)(2,1)S(1)} %project.1.token_ref.rest_0_), channel_id=1, source_target_pairs={{0,2},{1,3},{2,0},{3,1},{4,6},{5,7},{6,4},{7,5},{8,10},{9,11},{10,... | collective-permute-start | bytes 503816 | tf_op jit(solution)/shard_map/ppermute | solution.py:466
  32.0 9.0 %collective-permute-start.22 = (bf16[656,128]{1,0:T(8,128)(2,1)S(1)}, bf16[656,128]{1,0:T(8,128)(2,1)S(1)}, u32[]{:S(2)}, u32[]{:S(2)}) collective-permute-start(bf16[656,128]{1,0:T(8,128)(2,1)S(1)} %project.1.token_ref.rest_0_), channel_id=1, source_target_pairs={{0,6},{1,7},{2,4},{3,5},{4,2},{5,3},{6,0},{7,1},{8,14},{9,15},{10,... | collective-permute-start | bytes 503816 | tf_op jit(solution)/shard_map/ppermute | solution.py:466
  34.8 4.6 %collective-permute-start.19 = (bf16[656,128]{1,0:T(8,128)(2,1)S(1)}, bf16[656,128]{1,0:T(8,128)(2,1)S(1)}, u32[]{:S(2)}, u32[]{:S(2)}) collective-permute-start(bf16[656,128]{1,0:T(8,128)(2,1)S(1)} %project.1.token_ref.rest_0_), channel_id=1, source_target_pairs={{0,1},{1,0},{2,3},{3,2},{4,5},{5,4},{6,7},{7,6},{8,9},{9,8},{10,11... | collective-permute-start | bytes 503816 | tf_op jit(solution)/shard_map/ppermute | solution.py:466
  36.3 4.8 %collective-permute-start.20 = (bf16[656,128]{1,0:T(8,128)(2,1)S(1)}, bf16[656,128]{1,0:T(8,128)(2,1)S(1)}, u32[]{:S(2)}, u32[]{:S(2)}) collective-permute-start(bf16[656,128]{1,0:T(8,128)(2,1)S(1)} %collective-permute-done.17.rest_1_), channel_id=1, source_target_pairs={{0,1},{1,0},{2,3},{3,2},{4,5},{5,4},{6,7},{7,6},{8,9},{9,8},{10,11... | collective-permute-start | bytes 503816 | tf_op jit(solution)/shard_map/ppermute | solution.py:466
  38.7 2.4 %collective-permute-start.21 = (bf16[656,128]{1,0:T(8,128)(2,1)S(1)}, bf16[656,128]{1,0:T(8,128)(2,1)S(1)}, u32[]{:S(2)}, u32[]{:S(2)}) collective-permute-start(bf16[656,128]{1,0:T(8,128)(2,1)S(1)} %collective-permute-done.18.rest_2_), channel_id=1, source_target_pairs={{0,1},{1,0},{2,3},{3,2},{4,5},{5,4},{6,7},{7,6},{8,9},{9,8},{10,11... | collective-permute-start | bytes 503816 | tf_op jit(solution)/shard_map/ppermute | solution.py:466
  41.1 1.4 %collective-permute-start.23 = (bf16[656,128]{1,0:T(8,128)(2,1)S(1)}, bf16[656,128]{1,0:T(8,128)(2,1)S(1)}, u32[]{:S(2)}, u32[]{:S(2)}) collective-permute-start(bf16[656,128]{1,0:T(8,128)(2,1)S(1)} %collective-permute-done.22.rest_6_), channel_id=1, source_target_pairs={{0,1},{1,0},{2,3},{3,2},{4,5},{5,4},{6,7},{7,6},{8,9},{9,8},{10,11... | collective-permute-start | bytes 503816 | tf_op jit(solution)/shard_map/ppermute | solution.py:466
  (2 other events, 12.6 us)

commit v16 on v14

--- a/solution.py
+++ b/solution.py
@@ -124,7 +124,7 @@
 NOTES = 16
 RECEIVERS = ((0, 0), (4, 2), (2, 4), (6, 6), (7, 7), (3, 5), (5, 3), (1, 1))
 SENDERS = ((0, 0), (4, 2), (2, 4), (6, 6), (7, 7), (5, 3), (3, 5), (1, 1))
-OWNERS = ((0, 0), (4, 2), (2, 4), (1, 1), (3, 5), (5, 3), (6, 6), (7, 7))
+OWNERS = (0, 4, 2, 1, 5, 3, 6, 7)
 ROOT = math.log2(math.e) / math.sqrt(HDIM)
 BF16 = jnp.bfloat16
 F32 = jnp.float32
@@ -144,34 +144,21 @@
     return jnp.concatenate([wide[at * groups : (at + 1) * groups] for at in range(4)], axis=1)
 
 
-def spread_kernel(qkv_hbm, resid_hbm, weight_hbm, grid_hbm, *rest):
+def spread_kernel(qkv_hbm, resid_hbm, grid_hbm, *rest):
     outs = rest[:ROWS]
-    chip_ref, slice_ref, grid_out, qkv, resid, main, tile, held, grid, sems = rest[ROWS:]
-    me = row_index()
-    depth = weight_hbm.shape[0]
-    chip = pl.ds(pl.multiple_of(me // 2 * 2 * WIDE, 2 * WIDE), 2 * WIDE)
-    ends = pl.ds(pl.multiple_of(MAIN + me // 4 * WIDE, WIDE), WIDE)
+    grid_out, qkv, resid, held, grid, sems = rest[ROWS:]
+    me = row_index()
     copies = [
-        pltpu.make_async_copy(qkv_hbm.at[0], qkv, sems.at[0]),
+        pltpu.make_async_copy(grid_hbm, grid, sems.at[0]),
         pltpu.make_async_copy(resid_hbm.at[0], resid, sems.at[1]),
-        pltpu.make_async_copy(weight_hbm.at[:, chip], main, sems.at[2]),
-        pltpu.make_async_copy(weight_hbm.at[:, ends], tile, sems.at[3]),
-        pltpu.make_async_copy(grid_hbm, grid, sems.at[4]),
     ]
+    part = qkv.shape[0] // 4
+    for at in range(4):
+        rows = pl.ds(at * part, part)
+        copies.append(pltpu.make_async_copy(qkv_hbm.at[0, rows], qkv.at[rows], sems.at[2 + at]))
+    for copy in reversed(copies):
+        copy.start()
     for copy in copies:
-        copy.start()
-    for copy in copies[2:]:
-        copy.wait()
-    low = me // 2 % 2 == 0
-    size = depth + depth // 4
-    for core in range(2):
-        tail = jnp.where(low, tile[:, core * REST : (core + 1) * REST], tile[:, (core + 2) * REST : (core + 3) * REST])
-        chip_ref[core * size : core * size + depth, :] = main[:, core * WIDE : (core + 1) * WIDE]
-        chip_ref[core * size + depth : (core + 1) * size, :] = pack_tail(tail)
-    slice_ref[...] = chip_ref[pl.ds(pl.multiple_of(me % 2 * size, 16), size), :]
-    row = lax.broadcasted_iota(jnp.int32, grid_out.shape, 0)
-    grid_out[...] = jnp.where(row == 0, grid[0, 0], grid[0, 1])
-    for copy in copies[:2]:
         copy.wait()
     for dest in range(ROWS):
         at = dest * HPAIR
@@ -181,6 +168,23 @@
         held[dest] = jnp.concatenate(parts, axis=1)
     for step, out in zip(steps(RECEIVERS), outs):
         out[...] = held[me ^ step]
+    row = lax.broadcasted_iota(jnp.int32, grid_out.shape, 0)
+    grid_out[...] = jnp.where(row == 0, grid[0, 0], grid[0, 1])
+
+
+def slice_kernel(weight_ref, *rest):
+    chip_ref, slice_ref = rest[-2:]
+    me = row_index()
+    depth = weight_ref.shape[0]
+    main = weight_ref[:, pl.ds(pl.multiple_of(me // 2 * 2 * WIDE, 2 * WIDE), 2 * WIDE)]
+    tile = weight_ref[:, pl.ds(pl.multiple_of(MAIN + me // 4 * WIDE, WIDE), WIDE)]
+    low = me // 2 % 2 == 0
+    size = depth + depth // 4
+    for core in range(2):
+        tail = jnp.where(low, tile[:, core * REST : (core + 1) * REST], tile[:, (core + 2) * REST : (core + 3) * REST])
+        chip_ref[core * size : core * size + depth, :] = main[:, core * WIDE : (core + 1) * WIDE]
+        chip_ref[core * size + depth : (core + 1) * size, :] = pack_tail(tail)
+    slice_ref[...] = chip_ref[pl.ds(pl.multiple_of(me % 2 * size, 16), size), :]
 
 
 def layout_kernel(grid_ref, *rest):
@@ -311,7 +315,7 @@
     patches = out_ref.shape[0]
     groups = patches // 4
     mains, tails = [], []
-    for step in steps(owners):
+    for step in owners:
         pair = me ^ step
         columns = pl.ds(pl.multiple_of(pair * WIDE, WIDE), WIDE)
         is_last = came_last(pair // 2)
@@ -392,13 +396,13 @@
 
 
 def merge_first_kernel(*rest):
-    pieces, (weight_ref, sum_ref) = list(zip(steps(OWNERS[:3]), rest[:3])), rest[3:]
+    pieces, (weight_ref, sum_ref) = list(zip(OWNERS[:3], rest[:3])), rest[3:]
     for corner in range(4):
         sum_ref[corner] = merge_product(weight_ref, corner, sum_ref.shape[2], pieces)
 
 
 def merge_second_kernel(*rest):
-    pieces, (before_ref, weight_ref, sum_ref) = list(zip(steps(OWNERS[3:6]), rest[:3])), rest[3:]
+    pieces, (before_ref, weight_ref, sum_ref) = list(zip(OWNERS[3:6], rest[:3])), rest[3:]
     for corner in range(4):
         sum_ref[corner] = before_ref[corner] + merge_product(weight_ref, corner, sum_ref.shape[2], pieces)
 
@@ -412,28 +416,23 @@
     contract = (((1,), (1,)), ((), ()))
     block = pl.multiple_of((me // 2 ^ 3) * 2 * WIDE, 2 * WIDE)
     rows = collect_late(pieces[6], pieces[7])
-    parts = []
-    for corner in range(4):
-        parts.append(
-            before_ref[corner]
-            + lax.dot_general(
-                weight_ref[:, pl.ds(pl.multiple_of(corner * D + block, 2 * WIDE), 2 * WIDE)],
-                rows[corner * groups : (corner + 1) * groups],
-                contract,
-                preferred_element_type=F32,
-            )
-        )
     notes = jnp.zeros((NOTES, groups), F32)
-    for step, piece in zip(steps(OWNERS), pieces):
+    for step, piece in zip(OWNERS, pieces):
         notes = notes + piece[patches + groups :, :].astype(F32)
     scale = lax.rsqrt((notes[:4] + notes[4:8]) * (1.0 / D) + 1e-06)
     spread = jnp.concatenate([jnp.broadcast_to(scale[at : at + 1], (REST, groups)) for at in range(4)], axis=0).T
-    for step, piece in zip(steps(OWNERS), pieces):
+    for step, piece in zip(OWNERS, pieces):
         at = pl.ds(pl.multiple_of((me ^ step) * WIDE, WIDE), WIDE)
         ends_ref[:, at] = (piece[patches : patches + groups, :].astype(F32) * spread).astype(BF16)
     total = bias_ref[...] + lax.dot_general(tail_ref[...], ends_ref[...], contract, preferred_element_type=F32)
     for corner in range(4):
-        total = total + scale[corner : corner + 1] * parts[corner]
+        part = before_ref[corner] + lax.dot_general(
+            weight_ref[:, pl.ds(pl.multiple_of(corner * D + block, 2 * WIDE), 2 * WIDE)],
+            rows[corner * groups : (corner + 1) * groups],
+            contract,
+            preferred_element_type=F32,
+        )
+        total = total + scale[corner : corner + 1] * part
     merged = 0.5 * total * (1.0 + lax.erf(total * math.sqrt(0.5)))
     out_ref[0] = jnp.where(live_ref[...] > 0.0, merged, 0.0).astype(BF16)
 
@@ -489,25 +488,21 @@
     piece = patches + groups
     size = depth + depth // 4
 
-    *sends, chip, own, grid = kernel(
+    *sends, grid = kernel(
         spread_kernel,
         "spread",
-        [shape(band, 4 * HPAIR)] * ROWS
-        + [shape(2 * size, WIDE), shape(size, WIDE), shape(8, WIDE, dtype=jnp.int32)],
+        [shape(band, 4 * HPAIR)] * ROWS + [shape(8, WIDE, dtype=jnp.int32)],
         [
             pltpu.VMEM((band, 3 * D), BF16),
             pltpu.VMEM((band, D), BF16),
-            pltpu.VMEM((depth, 2 * WIDE), BF16),
-            pltpu.VMEM((depth, WIDE), BF16),
             pltpu.VMEM((ROWS, band, 4 * HPAIR), BF16),
             pltpu.SMEM(page_grid.shape, jnp.int32),
-            pltpu.SemaphoreType.DMA((5,)),
+            pltpu.SemaphoreType.DMA((6,)),
         ],
-        fetched=range(4),
-        count=4,
-        limit=24,
+        fetched=range(3),
+        count=3,
         moved=1 << 20,
-    )(in_hbm(qkv_rows), in_hbm(residual), in_hbm(out_weight), in_hbm(page_grid))
+    )(in_hbm(qkv_rows), in_hbm(residual), in_hbm(page_grid))
     blocks = [sends[0]] + [swap(send, *pair) for send, pair in zip(sends[1:], RECEIVERS[1:])]
     select, dead, live = kernel(
         layout_kernel,
@@ -517,6 +512,14 @@
         count=1 + 3,
         moved=1 << 20,
     )(grid, *blocks[1:4])
+    chip, own = kernel(
+        slice_kernel,
+        "out_weight_slices",
+        [shape(2 * size, WIDE), shape(size, WIDE)],
+        fetched=(1,),
+        count=2,
+        moved=1 << 20,
+    )(out_weight, sends[0])
     near = turn(after(chip, *()), 1, PAGES - 1)
     swapped = swap(near, 1)
     attn = kernel(
@@ -548,7 +551,7 @@
         flops=1,
         moved=1,
     )(across, swapped, main)
-    one, two, far = swap(attn, 4, 2), swap(attn, 2, 4), swap(attn, 6)
+    one, two, far = swap(attn, 4), swap(attn, 2), swap(attn, 6)
     weights = (main, tail, *last)
     rows = shape(patches, HPAIR, dtype=F32)
     first = kernel(project_first_kernel, "project_first", rows, count=8, flops=1, moved=1)(attn, one, two, *weights, resid)
@@ -572,7 +575,7 @@
         moved=4 << 20,
     )(merge_weight, in_hbm(merge_bias), hidden)
     sums = shape(4, units, groups, dtype=F32)
-    one, two, far = swap(hidden, 4, 2), swap(hidden, 2, 4), swap(hidden, 6)
+    one, two, far = swap(hidden, 4), swap(hidden, 2), swap(hidden, 6)
     first = kernel(merge_first_kernel, "merge_first", sums, count=4, flops=1, moved=1)(hidden, one, two, merge_weight)
     near = [swap(after(hidden, ends), 1), swap(one, 1), swap(two, 1)]
     second = kernel(merge_second_kernel, "merge_second", sums, count=5, flops=1, moved=1)(*near, first, merge_weight)

time: 45.5 us -> 45.1 us (level)
  local copies, waits for them, and re-layouts: 0.01 us -> 1.16 us
  starting transfers between devices: 23 us -> 22 us
  waiting for transfers between devices: 11.1 us -> 10.6 us
    ppermute x22, waiting for transfers between devices: 11.1 us -> 7 us  [swap(): lax.ppermute(value, 'row', [(row, row ^ (odd if row % 2 else even)) for r...]
    ppermute x2, waiting for transfers between devices: 0.01 us -> 3.59 us  [turn(): return lax.ppermute(value, ('page', 'row'), pairs)]
    unnamed x4 -> x6, local copies, waits for them, and re-layouts: 0.01 us -> 1.16 us
    ppermute x22, starting transfers between devices: 18 us -> 17.4 us  [swap(): lax.ppermute(value, 'row', [(row, row ^ (odd if row % 2 else even)) for r...]
  transfers between devices with their start and end apart: 24 -> 24, of which waited for: 9 -> 8; matrix products, arithmetic and copies ran while one was open for 0% -> 0% of each run, Pallas kernels for 15% -> 16%
where the time goes in v16:
time: 45.1 us; the launch traced here: 44.9 us
  starting transfers between devices  22 us (49%)
  Pallas kernels  10.9 us (24%)
  waiting for transfers between devices  10.6 us (24%)
  local copies, waits for them, and re-layouts  1.16 us (3%)
    ppermute x22, starting transfers between devices, swap(): lax.ppermute(value, 'row', [(row, row ^ (odd if row % 2 else even)) for r...  17.4 us
    ppermute x22, waiting for transfers between devices, swap(): lax.ppermute(value, 'row', [(row, row ^ (odd if row % 2 else even)) for r...  7 us
    ppermute x2, starting transfers between devices, turn(): return lax.ppermute(value, ('page', 'row'), pairs)  4.65 us
    ppermute x2, waiting for transfers between devices, turn(): return lax.ppermute(value, ('page', 'row'), pairs)  3.59 us
    pallas_call x1, Pallas kernels, local_eight(): kernel(merge_kernel, 'merge', shape(1, units, groups), [pltpu.VMEM((group...  1.73 us
    pallas_call x1, Pallas kernels, local_eight(): kernel(spread_kernel, 'spread', [shape(band, 4 * HPAIR)] * ROWS + [shape(...  1.54 us
    pallas_call x1, Pallas kernels, local_eight(): kernel(tail_kernel, 'merge_tail', [shape(units, MAIN), shape(units, 1, dt...  1.39 us
    pallas_call x1, Pallas kernels, local_eight(): kernel(attend_kernel, 'attend', shape(piece, WIDE), [pltpu.VMEM((patches,...  1.34 us
  transfers between devices with their start and end apart: 24, of which 8 were waited for; matrix products, arithmetic and copies ran while one was open for 0% of the time, Pallas kernels for 16%

profile of v16, /device:TPU:0, one launch (start us, length us, event | category | flops | bytes accessed | tf_op | source)
XLA Modules:
  0.0 44.9 jit_solution(15217949264599043743)
XLA Ops:
  0.0 1.5 %spread.1 = (bf16[64,640]{1,0:T(8,128)(2,1)S(1)}, bf16[64,640]{1,0:T(8,128)(2,1)S(1)}, bf16[64,640]{1,0:T(8,128)(2,1)S(1)}, bf16[64,640]{1,0:T(8,128)(2,1)S(1)},...) custom-call(bf16[1,64,3840]{2,1,0:T(8,128)(2,1)} %qkv_hbm.1, ...), custom_call_target="tpu_custom_call" | custom-call | bytes 1048576 | tf_op jit(solution)/shard_map/spread/pallas_call | solution.py:491
  1.5 3.0 %collective-permute-start = (bf16[64,640]{1,0:T(8,128)(2,1)S(1)}, bf16[64,640]{1,0:T(8,128)(2,1)S(1)}, u32[]{:S(2)}, u32[]{:S(2)}) collective-permute-start(bf16[64,640]{1,0:T(8,128)(2,1)S(1)} %get-tuple-element.32), channel_id=1, source_target_pairs={{0,4},{1,3},{2,6},{3,1},{4,0},{5,7},{6,2},{7,5},{8,12},{9,11},{10,... | collective-permute-start | bytes 245768 | tf_op jit(solution)/shard_map/ppermute | solution.py:466
  4.6 1.5 %collective-permute-start.1 = (bf16[64,640]{1,0:T(8,128)(2,1)S(1)}, bf16[64,640]{1,0:T(8,128)(2,1)S(1)}, u32[]{:S(2)}, u32[]{:S(2)}) collective-permute-start(bf16[64,640]{1,0:T(8,128)(2,1)S(1)} %get-tuple-element.33), channel_id=1, source_target_pairs={{0,2},{1,5},{2,0},{3,7},{4,6},{5,1},{6,4},{7,3},{8,10},{9,13},{10,... | collective-permute-start | bytes 245768 | tf_op jit(solution)/shard_map/ppermute | solution.py:466
  6.1 1.5 %collective-permute-start.3 = (bf16[64,640]{1,0:T(8,128)(2,1)S(1)}, bf16[64,640]{1,0:T(8,128)(2,1)S(1)}, u32[]{:S(2)}, u32[]{:S(2)}) collective-permute-start(bf16[64,640]{1,0:T(8,128)(2,1)S(1)} %get-tuple-element.38), channel_id=1, source_target_pairs={{0,7},{1,6},{2,5},{3,4},{4,3},{5,2},{6,1},{7,0},{8,15},{9,14},{10,... | collective-permute-start | bytes 245768 | tf_op jit(solution)/shard_map/ppermute | solution.py:466
  7.6 1.7 %collective-permute-start.4 = (bf16[64,640]{1,0:T(8,128)(2,1)S(1)}, bf16[64,640]{1,0:T(8,128)(2,1)S(1)}, u32[]{:S(2)}, u32[]{:S(2)}) collective-permute-start(bf16[64,640]{1,0:T(8,128)(2,1)S(1)} %get-tuple-element.39), channel_id=1, source_target_pairs={{0,3},{1,4},{2,1},{3,6},{4,7},{5,0},{6,5},{7,2},{8,11},{9,12},{10,... | collective-permute-start | bytes 245768 | tf_op jit(solution)/shard_map/ppermute | solution.py:466
  9.6 1.2 %collective-permute-start.6 = (bf16[64,640]{1,0:T(8,128)(2,1)S(1)}, bf16[64,640]{1,0:T(8,128)(2,1)S(1)}, u32[]{:S(2)}, u32[]{:S(2)}) collective-permute-start(bf16[64,640]{1,0:T(8,128)(2,1)S(1)} %get-tuple-element.41), channel_id=1, source_target_pairs={{0,1},{1,0},{2,3},{3,2},{4,5},{5,4},{6,7},{7,6},{8,9},{9,8},{10,11... | collective-permute-start | bytes 245768 | tf_op jit(solution)/shard_map/ppermute | solution.py:466
  10.9 1.1 %copy-done = bf16[320,1280]{1,0:T(8,128)(2,1)S(1)} copy-done((bf16[320,1280]{1,0:T(8,128)(2,1)S(1)}, bf16[320,1280]{1,0:T(8,128)(2,1)}, u32[]{:S(2)}) %copy-start) | copy-done | bytes 819224
  12.2 1.6 %collective-permute-start.10 = (bf16[800,128]{1,0:T(8,128)(2,1)S(1)}, bf16[800,128]{1,0:T(8,128)(2,1)S(1)}, u32[]{:S(2)}, u32[]{:S(2)}) collective-permute-start(bf16[800,128]{1,0:T(8,128)(2,1)S(1)} %get-tuple-element.44), channel_id=1, source_target_pairs={{0,8},{1,25},{2,10},{3,27},{4,12},{5,29},{6,14},{7,31},{8,16},{9,1... | collective-permute-start | bytes 614408 | tf_op jit(solution)/shard_map/ppermute | solution.py:475
  14.3 1.3 %attend.1.token_ref.rest_0_ = bf16[640,128]{1,0:T(8,128)(2,1)S(1)} custom-call(bf16[512,512]{1,0:T(8,128)(2,1)S(1)} %get-tuple-element.35.select_ref, f32[1,512]{1,0:T(1,128)S(1)} %get-tuple-element.36.dead_ref, bf16[64,640]{1,0:T(8,128)(2,1)S(1)} %get-tuple-element.37.rest_0_, bf16[64,640]{1,0:T(8,128)(2,1)S(1)} %collective-permute-done.rest_0_.rest_1_, ...), custom_call_target="tpu_custom_call" | custom-call | flops 21474836480 | bytes 1048576 | tf_op jit(solution)/shard_map/attend/pallas_call | solution.py:525
  15.6 1.2 %collective-permute-start.13 = (bf16[640,128]{1,0:T(8,128)(2,1)S(1)}, bf16[640,128]{1,0:T(8,128)(2,1)S(1)}, u32[]{:S(2)}, u32[]{:S(2)}) collective-permute-start(bf16[640,128]{1,0:T(8,128)(2,1)S(1)} %attend.1.token_ref.rest_0_), channel_id=1, source_target_pairs={{0,4},{1,5},{2,6},{3,7},{4,0},{5,1},{6,2},{7,3},{8,12},{9,13},{10,... | collective-permute-start | bytes 491528 | tf_op jit(solution)/shard_map/ppermute | solution.py:466
  16.8 0.8 %collective-permute-start.15 = (bf16[640,128]{1,0:T(8,128)(2,1)S(1)}, bf16[640,128]{1,0:T(8,128)(2,1)S(1)}, u32[]{:S(2)}, u32[]{:S(2)}) collective-permute-start(bf16[640,128]{1,0:T(8,128)(2,1)S(1)} %attend.1.token_ref.rest_0_), channel_id=1, source_target_pairs={{0,2},{1,3},{2,0},{3,1},{4,6},{5,7},{6,4},{7,5},{8,10},{9,11},{10,... | collective-permute-start | bytes 491528 | tf_op jit(solution)/shard_map/ppermute | solution.py:466
  17.7 1.5 %collective-permute-start.7 = (bf16[640,128]{1,0:T(8,128)(2,1)S(1)}, bf16[640,128]{1,0:T(8,128)(2,1)S(1)}, u32[]{:S(2)}, u32[]{:S(2)}) collective-permute-start(bf16[640,128]{1,0:T(8,128)(2,1)S(1)} %attend.1.token_ref.rest_0_), channel_id=1, source_target_pairs={{0,6},{1,7},{2,4},{3,5},{4,2},{5,3},{6,0},{7,1},{8,14},{9,15},{10,... | collective-permute-start | bytes 491528 | tf_op jit(solution)/shard_map/ppermute | solution.py:466
  19.2 3.0 %collective-permute-start.9 = (bf16[400,128]{1,0:T(8,128)(2,1)S(1)}, bf16[400,128]{1,0:T(8,128)(2,1)S(1)}, u32[]{:S(2)}, u32[]{:S(2)}) collective-permute-start(bf16[400,128]{1,0:T(8,128)(2,1)S(1)} %get-tuple-element.43.rest_8_), channel_id=1, source_target_pairs={{0,16},{1,17},{2,18},{3,19},{4,20},{5,21},{6,22},{7,23},{8,24},{9,... | collective-permute-start | bytes 307208 | tf_op jit(solution)/shard_map/ppermute | solution.py:475
  22.2 1.3 %ready.1 = (f32[512,160]{1,0:T(8,128)S(1)}, f32[1,160]{1,0:T(1,128)S(1)}, bf16[1024,160]{1,0:T(8,128)(2,1)S(1)}, bf16[4,1024,160]{2,1,0:T(8,128)(2,1)S(1)}) custom-call(bf16[512,512]{1,0:T(8,128)(2,1)S(1)} %get-tuple-element.35.select_ref, f32[1280]{0:T(1024)} %gain_hbm.1, bf16[640,128]{1,0:T(8,128)(2,1)S(1)} %attend.1.token_ref.rest_0_, ...), custom_call_target="tpu_custom_call" | custom-call | flops 10737418240 | bytes 4194304 | tf_op jit(solution)/shard_map/ready/pallas_call | solution.py:535
  24.2 3.6 %collective-permute-done.9.across_ref = bf16[400,128]{1,0:T(8,128)(2,1)S(1)} collective-permute-done((bf16[400,128]{1,0:T(8,128)(2,1)S(1)}, bf16[400,128]{1,0:T(8,128)(2,1)S(1)}, u32[]{:S(2)}, u32[]{:S(2)}) %collective-permute-start.9) | collective-permute-done | bytes 102432 | tf_op jit(solution)/shard_map/ppermute | solution.py:475
  31.3 0.9 %collective-permute-start.18 = (bf16[656,128]{1,0:T(8,128)(2,1)S(1)}, bf16[656,128]{1,0:T(8,128)(2,1)S(1)}, u32[]{:S(2)}, u32[]{:S(2)}) collective-permute-start(bf16[656,128]{1,0:T(8,128)(2,1)S(1)} %project.1.token_ref.rest_0_), channel_id=1, source_target_pairs={{0,2},{1,3},{2,0},{3,1},{4,6},{5,7},{6,4},{7,5},{8,10},{9,11},{10,... | collective-permute-start | bytes 503816 | tf_op jit(solution)/shard_map/ppermute | solution.py:466
  32.2 1.9 %collective-permute-start.22 = (bf16[656,128]{1,0:T(8,128)(2,1)S(1)}, bf16[656,128]{1,0:T(8,128)(2,1)S(1)}, u32[]{:S(2)}, u32[]{:S(2)}) collective-permute-start(bf16[656,128]{1,0:T(8,128)(2,1)S(1)} %project.1.token_ref.rest_0_), channel_id=1, source_target_pairs={{0,6},{1,7},{2,4},{3,5},{4,2},{5,3},{6,0},{7,1},{8,14},{9,15},{10,... | collective-permute-start | bytes 503816 | tf_op jit(solution)/shard_map/ppermute | solution.py:466
  34.2 1.4 %merge_tail.1 = (bf16[640,1024]{1,0:T(8,128)(2,1)S(1)}, f32[640,1]{1,0:T(8,128)S(1)}) custom-call(bf16[640,5120]{1,0:T(8,128)(2,1)S(1)} %bitcast.1, f32[640]{0:T(1024)} %bias_hbm.1, bf16[656,128]{1,0:T(8,128)(2,1)S(1)} %project.1.token_ref.rest_0_), custom_call_target="tpu_custom_call" | custom-call | bytes 4194304 | tf_op jit(solution)/shard_map/merge_tail/pallas_call | solution.py:568
  35.6 1.4 %collective-permute-done.17.rest_1_ = bf16[656,128]{1,0:T(8,128)(2,1)S(1)} collective-permute-done((bf16[656,128]{1,0:T(8,128)(2,1)S(1)}, bf16[656,128]{1,0:T(8,128)(2,1)S(1)}, u32[]{:S(2)}, u32[]{:S(2)}) %collective-permute-start.17) | collective-permute-done | bytes 167968 | tf_op jit(solution)/shard_map/ppermute | solution.py:466
  37.0 1.5 %collective-permute-done.18.rest_2_ = bf16[656,128]{1,0:T(8,128)(2,1)S(1)} collective-permute-done((bf16[656,128]{1,0:T(8,128)(2,1)S(1)}, bf16[656,128]{1,0:T(8,128)(2,1)S(1)}, u32[]{:S(2)}, u32[]{:S(2)}) %collective-permute-start.18) | collective-permute-done | bytes 167968 | tf_op jit(solution)/shard_map/ppermute | solution.py:466
  38.5 0.7 %merge_first.1.rest_3_ = f32[4,640,128]{2,1,0:T(8,128)S(1)} custom-call(bf16[656,128]{1,0:T(8,128)(2,1)S(1)} %project.1.token_ref.rest_0_, bf16[656,128]{1,0:T(8,128)(2,1)S(1)} %collective-permute-done.17.rest_1_, bf16[656,128]{1,0:T(8,128)(2,1)S(1)} %collective-permute-done.18.rest_2_, bf16[640,5120]{1,0:T(8,128)(2,1)S(1)} %bitcast.1), custom_call_target="tpu_custom_call" | custom-call | flops 1 | bytes 1 | tf_op jit(solution)/shard_map/merge_first/pallas_call | solution.py:579
  39.2 2.6 %collective-permute-done.22.rest_6_ = bf16[656,128]{1,0:T(8,128)(2,1)S(1)} collective-permute-done((bf16[656,128]{1,0:T(8,128)(2,1)S(1)}, bf16[656,128]{1,0:T(8,128)(2,1)S(1)}, u32[]{:S(2)}, u32[]{:S(2)}) %collective-permute-start.22) | collective-permute-done | bytes 167968 | tf_op jit(solution)/shard_map/ppermute | solution.py:466
  41.8 0.7 %merge_second.1.rest_8_ = f32[4,640,128]{2,1,0:T(8,128)S(1)} custom-call(bf16[656,128]{1,0:T(8,128)(2,1)S(1)} %collective-permute-done.19.rest_0_.rest_3_, bf16[656,128]{1,0:T(8,128)(2,1)S(1)} %collective-permute-done.20.rest_1_.rest_4_, bf16[656,128]{1,0:T(8,128)(2,1)S(1)} %collective-permute-done.21.rest_2_.rest_5_, ...), custom_call_target="tpu_custom_call" | custom-call | flops 1 | bytes 1 | tf_op jit(solution)/shard_map/merge_second/pallas_call | solution.py:581
  43.2 1.7 %merge.1 = bf16[1,640,128]{2,1,0:T(8,128)(2,1)} custom-call(bf16[656,128]{1,0:T(8,128)(2,1)S(1)} %project.1.token_ref.rest_0_, bf16[656,128]{1,0:T(8,128)(2,1)S(1)} %collective-permute-done.17.rest_1_, bf16[656,128]{1,0:T(8,128)(2,1)S(1)} %collective-permute-done.18.rest_2_, bf16[656,128]{1,0:T(8,128)(2,1)S(1)} %collective-permute-done.19.rest_0_.rest_3_, ...), custom_call_target="tpu_custom_call" | custom-call | flops 335544320 | bytes 8388608 | tf_op jit(solution)/shard_map/merge/pallas_call | solution.py:582
  (44 shorter events, 5.9 us)
Async XLA Ops:
  1.5 7.7 %collective-permute-start = (bf16[64,640]{1,0:T(8,128)(2,1)S(1)}, bf16[64,640]{1,0:T(8,128)(2,1)S(1)}, u32[]{:S(2)}, u32[]{:S(2)}) collective-permute-start(bf16[64,640]{1,0:T(8,128)(2,1)S(1)} %get-tuple-element.32), channel_id=1, source_target_pairs={{0,4},{1,3},{2,6},{3,1},{4,0},{5,7},{6,2},{7,5},{8,12},{9,11},{10,... | collective-permute-start | bytes 245768 | tf_op jit(solution)/shard_map/ppermute | solution.py:466
  4.6 5.1 %collective-permute-start.1 = (bf16[64,640]{1,0:T(8,128)(2,1)S(1)}, bf16[64,640]{1,0:T(8,128)(2,1)S(1)}, u32[]{:S(2)}, u32[]{:S(2)}) collective-permute-start(bf16[64,640]{1,0:T(8,128)(2,1)S(1)} %get-tuple-element.33), channel_id=1, source_target_pairs={{0,2},{1,5},{2,0},{3,7},{4,6},{5,1},{6,4},{7,3},{8,10},{9,13},{10,... | collective-permute-start | bytes 245768 | tf_op jit(solution)/shard_map/ppermute | solution.py:466
  6.1 6.2 %collective-permute-start.2 = (bf16[64,640]{1,0:T(8,128)(2,1)S(1)}, bf16[64,640]{1,0:T(8,128)(2,1)S(1)}, u32[]{:S(2)}, u32[]{:S(2)}) collective-permute-start(bf16[64,640]{1,0:T(8,128)(2,1)S(1)} %get-tuple-element.34), channel_id=1, source_target_pairs={{0,6},{1,7},{2,4},{3,5},{4,2},{5,3},{6,0},{7,1},{8,14},{9,15},{10,... | collective-permute-start | bytes 245768 | tf_op jit(solution)/shard_map/ppermute | solution.py:466
  6.1 7.9 %collective-permute-start.3 = (bf16[64,640]{1,0:T(8,128)(2,1)S(1)}, bf16[64,640]{1,0:T(8,128)(2,1)S(1)}, u32[]{:S(2)}, u32[]{:S(2)}) collective-permute-start(bf16[64,640]{1,0:T(8,128)(2,1)S(1)} %get-tuple-element.38), channel_id=1, source_target_pairs={{0,7},{1,6},{2,5},{3,4},{4,3},{5,2},{6,1},{7,0},{8,15},{9,14},{10,... | collective-permute-start | bytes 245768 | tf_op jit(solution)/shard_map/ppermute | solution.py:466
  7.6 6.7 %collective-permute-start.4 = (bf16[64,640]{1,0:T(8,128)(2,1)S(1)}, bf16[64,640]{1,0:T(8,128)(2,1)S(1)}, u32[]{:S(2)}, u32[]{:S(2)}) collective-permute-start(bf16[64,640]{1,0:T(8,128)(2,1)S(1)} %get-tuple-element.39), channel_id=1, source_target_pairs={{0,3},{1,4},{2,1},{3,6},{4,7},{5,0},{6,5},{7,2},{8,11},{9,12},{10,... | collective-permute-start | bytes 245768 | tf_op jit(solution)/shard_map/ppermute | solution.py:466
  9.3 5.0 %collective-permute-start.5 = (bf16[64,640]{1,0:T(8,128)(2,1)S(1)}, bf16[64,640]{1,0:T(8,128)(2,1)S(1)}, u32[]{:S(2)}, u32[]{:S(2)}) collective-permute-start(bf16[64,640]{1,0:T(8,128)(2,1)S(1)} %get-tuple-element.40), channel_id=1, source_target_pairs={{0,5},{1,2},{2,7},{3,0},{4,1},{5,6},{6,3},{7,4},{8,13},{9,10},{10,... | collective-permute-start | bytes 245768 | tf_op jit(solution)/shard_map/ppermute | solution.py:466
  9.6 4.7 %collective-permute-start.6 = (bf16[64,640]{1,0:T(8,128)(2,1)S(1)}, bf16[64,640]{1,0:T(8,128)(2,1)S(1)}, u32[]{:S(2)}, u32[]{:S(2)}) collective-permute-start(bf16[64,640]{1,0:T(8,128)(2,1)S(1)} %get-tuple-element.41), channel_id=1, source_target_pairs={{0,1},{1,0},{2,3},{3,2},{4,5},{5,4},{6,7},{7,6},{8,9},{9,8},{10,11... | collective-permute-start | bytes 245768 | tf_op jit(solution)/shard_map/ppermute | solution.py:466
  12.2 10.0 %collective-permute-start.10 = (bf16[800,128]{1,0:T(8,128)(2,1)S(1)}, bf16[800,128]{1,0:T(8,128)(2,1)S(1)}, u32[]{:S(2)}, u32[]{:S(2)}) collective-permute-start(bf16[800,128]{1,0:T(8,128)(2,1)S(1)} %get-tuple-element.44), channel_id=1, source_target_pairs={{0,8},{1,25},{2,10},{3,27},{4,12},{5,29},{6,14},{7,31},{8,16},{9,1... | collective-permute-start | bytes 614408 | tf_op jit(solution)/shard_map/ppermute | solution.py:475
  15.6 7.9 %collective-permute-start.13 = (bf16[640,128]{1,0:T(8,128)(2,1)S(1)}, bf16[640,128]{1,0:T(8,128)(2,1)S(1)}, u32[]{:S(2)}, u32[]{:S(2)}) collective-permute-start(bf16[640,128]{1,0:T(8,128)(2,1)S(1)} %attend.1.token_ref.rest_0_), channel_id=1, source_target_pairs={{0,4},{1,5},{2,6},{3,7},{4,0},{5,1},{6,2},{7,3},{8,12},{9,13},{10,... | collective-permute-start | bytes 491528 | tf_op jit(solution)/shard_map/ppermute | solution.py:466
  16.8 7.2 %collective-permute-start.15 = (bf16[640,128]{1,0:T(8,128)(2,1)S(1)}, bf16[640,128]{1,0:T(8,128)(2,1)S(1)}, u32[]{:S(2)}, u32[]{:S(2)}) collective-permute-start(bf16[640,128]{1,0:T(8,128)(2,1)S(1)} %attend.1.token_ref.rest_0_), channel_id=1, source_target_pairs={{0,2},{1,3},{2,0},{3,1},{4,6},{5,7},{6,4},{7,5},{8,10},{9,11},{10,... | collective-permute-start | bytes 491528 | tf_op jit(solution)/shard_map/ppermute | solution.py:466
  17.7 10.4 %collective-permute-start.7 = (bf16[640,128]{1,0:T(8,128)(2,1)S(1)}, bf16[640,128]{1,0:T(8,128)(2,1)S(1)}, u32[]{:S(2)}, u32[]{:S(2)}) collective-permute-start(bf16[640,128]{1,0:T(8,128)(2,1)S(1)} %attend.1.token_ref.rest_0_), channel_id=1, source_target_pairs={{0,6},{1,7},{2,4},{3,5},{4,2},{5,3},{6,0},{7,1},{8,14},{9,15},{10,... | collective-permute-start | bytes 491528 | tf_op jit(solution)/shard_map/ppermute | solution.py:466
  19.2 8.6 %collective-permute-start.9 = (bf16[400,128]{1,0:T(8,128)(2,1)S(1)}, bf16[400,128]{1,0:T(8,128)(2,1)S(1)}, u32[]{:S(2)}, u32[]{:S(2)}) collective-permute-start(bf16[400,128]{1,0:T(8,128)(2,1)S(1)} %get-tuple-element.43.rest_8_), channel_id=1, source_target_pairs={{0,16},{1,17},{2,18},{3,19},{4,20},{5,21},{6,22},{7,23},{8,24},{9,... | collective-permute-start | bytes 307208 | tf_op jit(solution)/shard_map/ppermute | solution.py:475
  22.2 5.5 %collective-permute-start.11 = (bf16[800,128]{1,0:T(8,128)(2,1)S(1)}, bf16[800,128]{1,0:T(8,128)(2,1)S(1)}, u32[]{:S(2)}, u32[]{:S(2)}) collective-permute-start(bf16[800,128]{1,0:T(8,128)(2,1)S(1)} %collective-permute-done.10.rest_9_), channel_id=1, source_target_pairs={{0,1},{1,0},{2,3},{3,2},{4,5},{5,4},{6,7},{7,6},{8,9},{9,8},{10,11... | collective-permute-start | bytes 614408 | tf_op jit(solution)/shard_map/ppermute | solution.py:466
  23.5 5.5 %collective-permute-start.14 = (bf16[640,128]{1,0:T(8,128)(2,1)S(1)}, bf16[640,128]{1,0:T(8,128)(2,1)S(1)}, u32[]{:S(2)}, u32[]{:S(2)}) collective-permute-start(bf16[640,128]{1,0:T(8,128)(2,1)S(1)} %collective-permute-done.13.rest_1_), channel_id=1, source_target_pairs={{0,1},{1,0},{2,3},{3,2},{4,5},{5,4},{6,7},{7,6},{8,9},{9,8},{10,11... | collective-permute-start | bytes 491528 | tf_op jit(solution)/shard_map/ppermute | solution.py:466
  24.1 5.0 %collective-permute-start.16 = (bf16[640,128]{1,0:T(8,128)(2,1)S(1)}, bf16[640,128]{1,0:T(8,128)(2,1)S(1)}, u32[]{:S(2)}, u32[]{:S(2)}) collective-permute-start(bf16[640,128]{1,0:T(8,128)(2,1)S(1)} %collective-permute-done.15.rest_2_), channel_id=1, source_target_pairs={{0,1},{1,0},{2,3},{3,2},{4,5},{5,4},{6,7},{7,6},{8,9},{9,8},{10,11... | collective-permute-start | bytes 491528 | tf_op jit(solution)/shard_map/ppermute | solution.py:466
  28.0 1.5 %collective-permute-start.12 = (bf16[640,128]{1,0:T(8,128)(2,1)S(1)}, bf16[640,128]{1,0:T(8,128)(2,1)S(1)}, u32[]{:S(2)}, u32[]{:S(2)}) collective-permute-start(bf16[640,128]{1,0:T(8,128)(2,1)S(1)} %attend.1.token_ref.rest_0_), channel_id=1, source_target_pairs={{0,1},{1,0},{2,3},{3,2},{4,5},{5,4},{6,7},{7,6},{8,9},{9,8},{10,11... | collective-permute-start | bytes 491528 | tf_op jit(solution)/shard_map/ppermute | solution.py:466
  28.1 1.9 %collective-permute-start.8 = (bf16[640,128]{1,0:T(8,128)(2,1)S(1)}, bf16[640,128]{1,0:T(8,128)(2,1)S(1)}, u32[]{:S(2)}, u32[]{:S(2)}) collective-permute-start(bf16[640,128]{1,0:T(8,128)(2,1)S(1)} %collective-permute-done.7.rest_0_), channel_id=1, source_target_pairs={{0,1},{1,0},{2,3},{3,2},{4,5},{5,4},{6,7},{7,6},{8,9},{9,8},{10,11... | collective-permute-start | bytes 491528 | tf_op jit(solution)/shard_map/ppermute | solution.py:466
  30.6 6.4 %collective-permute-start.17 = (bf16[656,128]{1,0:T(8,128)(2,1)S(1)}, bf16[656,128]{1,0:T(8,128)(2,1)S(1)}, u32[]{:S(2)}, u32[]{:S(2)}) collective-permute-start(bf16[656,128]{1,0:T(8,128)(2,1)S(1)} %project.1.token_ref.rest_0_), channel_id=1, source_target_pairs={{0,4},{1,5},{2,6},{3,7},{4,0},{5,1},{6,2},{7,3},{8,12},{9,13},{10,... | collective-permute-start | bytes 503816 | tf_op jit(solution)/shard_map/ppermute | solution.py:466
  31.3 7.2 %collective-permute-start.18 = (bf16[656,128]{1,0:T(8,128)(2,1)S(1)}, bf16[656,128]{1,0:T(8,128)(2,1)S(1)}, u32[]{:S(2)}, u32[]{:S(2)}) collective-permute-start(bf16[656,128]{1,0:T(8,128)(2,1)S(1)} %project.1.token_ref.rest_0_), channel_id=1, source_target_pairs={{0,2},{1,3},{2,0},{3,1},{4,6},{5,7},{6,4},{7,5},{8,10},{9,11},{10,... | collective-permute-start | bytes 503816 | tf_op jit(solution)/shard_map/ppermute | solution.py:466
  32.2 9.5 %collective-permute-start.22 = (bf16[656,128]{1,0:T(8,128)(2,1)S(1)}, bf16[656,128]{1,0:T(8,128)(2,1)S(1)}, u32[]{:S(2)}, u32[]{:S(2)}) collective-permute-start(bf16[656,128]{1,0:T(8,128)(2,1)S(1)} %project.1.token_ref.rest_0_), channel_id=1, source_target_pairs={{0,6},{1,7},{2,4},{3,5},{4,2},{5,3},{6,0},{7,1},{8,14},{9,15},{10,... | collective-permute-start | bytes 503816 | tf_op jit(solution)/shard_map/ppermute | solution.py:466
  35.6 3.6 %collective-permute-start.19 = (bf16[656,128]{1,0:T(8,128)(2,1)S(1)}, bf16[656,128]{1,0:T(8,128)(2,1)S(1)}, u32[]{:S(2)}, u32[]{:S(2)}) collective-permute-start(bf16[656,128]{1,0:T(8,128)(2,1)S(1)} %project.1.token_ref.rest_0_), channel_id=1, source_target_pairs={{0,1},{1,0},{2,3},{3,2},{4,5},{5,4},{6,7},{7,6},{8,9},{9,8},{10,11... | collective-permute-start | bytes 503816 | tf_op jit(solution)/shard_map/ppermute | solution.py:466
  37.0 4.8 %collective-permute-start.20 = (bf16[656,128]{1,0:T(8,128)(2,1)S(1)}, bf16[656,128]{1,0:T(8,128)(2,1)S(1)}, u32[]{:S(2)}, u32[]{:S(2)}) collective-permute-start(bf16[656,128]{1,0:T(8,128)(2,1)S(1)} %collective-permute-done.17.rest_1_), channel_id=1, source_target_pairs={{0,1},{1,0},{2,3},{3,2},{4,5},{5,4},{6,7},{7,6},{8,9},{9,8},{10,11... | collective-permute-start | bytes 503816 | tf_op jit(solution)/shard_map/ppermute | solution.py:466
  38.5 3.3 %collective-permute-start.21 = (bf16[656,128]{1,0:T(8,128)(2,1)S(1)}, bf16[656,128]{1,0:T(8,128)(2,1)S(1)}, u32[]{:S(2)}, u32[]{:S(2)}) collective-permute-start(bf16[656,128]{1,0:T(8,128)(2,1)S(1)} %collective-permute-done.18.rest_2_), channel_id=1, source_target_pairs={{0,1},{1,0},{2,3},{3,2},{4,5},{5,4},{6,7},{7,6},{8,9},{9,8},{10,11... | collective-permute-start | bytes 503816 | tf_op jit(solution)/shard_map/ppermute | solution.py:466
  41.8 1.4 %collective-permute-start.23 = (bf16[656,128]{1,0:T(8,128)(2,1)S(1)}, bf16[656,128]{1,0:T(8,128)(2,1)S(1)}, u32[]{:S(2)}, u32[]{:S(2)}) collective-permute-start(bf16[656,128]{1,0:T(8,128)(2,1)S(1)} %collective-permute-done.22.rest_6_), channel_id=1, source_target_pairs={{0,1},{1,0},{2,3},{3,2},{4,5},{5,4},{6,7},{7,6},{8,9},{9,8},{10,11... | collective-permute-start | bytes 503816 | tf_op jit(solution)/shard_map/ppermute | solution.py:466
  (3 other events, 11.8 us)

commit v17 on v16

--- a/solution.py
+++ b/solution.py
@@ -228,7 +228,7 @@
         scores = lax.dot_general(asked, keys, (((1,), (1,)), ((), ())), preferred_element_type=F32) + dead
         weights = jnp.exp2((scores - jnp.max(scores, axis=1, keepdims=True)) * ROOT)
         total = jnp.sum(weights, axis=1, keepdims=True)
-        mixed.append(jnp.dot(weights.astype(BF16), values, preferred_element_type=F32) / total)
+        mixed.append(jnp.dot(weights.astype(BF16), values, preferred_element_type=F32) * (1.0 / total))
     attn = jnp.where(lane < HDIM, mixed[0], mixed[1])
     out_ref[:patches, :] = attn[:, :WIDE].astype(BF16)
     out_ref[patches:, :] = pack_tail(attn[:, WIDE:]).astype(BF16)
@@ -395,21 +395,40 @@
     )
 
 
+def tail_products(tail_ref, groups, pieces):
+    me = row_index()
+    columns = [tail_ref[:, pl.ds(pl.multiple_of((me ^ step) * WIDE, WIDE), WIDE)] for step, _ in pieces]
+    tails = jnp.concatenate(columns, axis=1)
+    ends = jnp.concatenate([piece[4 * groups : 5 * groups, :] for _, piece in pieces], axis=1)
+    corner_of = lax.rem(lax.broadcasted_iota(jnp.int32, (1, ends.shape[1]), 1), WIDE) // REST
+    return [
+        lax.dot_general(
+            tails,
+            jnp.where(corner_of == corner, ends, jnp.zeros_like(ends)),
+            (((1,), (1,)), ((), ())),
+            preferred_element_type=F32,
+        )
+        for corner in range(4)
+    ]
+
+
 def merge_first_kernel(*rest):
-    pieces, (weight_ref, sum_ref) = list(zip(OWNERS[:3], rest[:3])), rest[3:]
-    for corner in range(4):
-        sum_ref[corner] = merge_product(weight_ref, corner, sum_ref.shape[2], pieces)
+    pieces, (weight_ref, tail_ref, sum_ref) = list(zip(OWNERS[:3], rest[:3])), rest[3:]
+    groups = sum_ref.shape[2]
+    for corner, tail in enumerate(tail_products(tail_ref, groups, pieces)):
+        sum_ref[corner] = tail + merge_product(weight_ref, corner, groups, pieces)
 
 
 def merge_second_kernel(*rest):
-    pieces, (before_ref, weight_ref, sum_ref) = list(zip(OWNERS[3:6], rest[:3])), rest[3:]
-    for corner in range(4):
-        sum_ref[corner] = before_ref[corner] + merge_product(weight_ref, corner, sum_ref.shape[2], pieces)
+    pieces, (before_ref, weight_ref, tail_ref, sum_ref) = list(zip(OWNERS[3:6], rest[:3])), rest[3:]
+    groups = sum_ref.shape[2]
+    for corner, tail in enumerate(tail_products(tail_ref, groups, pieces)):
+        sum_ref[corner] = before_ref[corner] + (tail + merge_product(weight_ref, corner, groups, pieces))
 
 
 def merge_kernel(*rest):
     pieces = rest[:ROWS]
-    before_ref, weight_ref, tail_ref, bias_ref, live_ref, out_ref, ends_ref = rest[ROWS:]
+    before_ref, weight_ref, tail_ref, bias_ref, live_ref, out_ref = rest[ROWS:]
     me = row_index()
     groups = live_ref.shape[1]
     patches = 4 * groups
@@ -417,14 +436,14 @@
     block = pl.multiple_of((me // 2 ^ 3) * 2 * WIDE, 2 * WIDE)
     rows = collect_late(pieces[6], pieces[7])
     notes = jnp.zeros((NOTES, groups), F32)
-    for step, piece in zip(OWNERS, pieces):
+    for piece in pieces:
         notes = notes + piece[patches + groups :, :].astype(F32)
     scale = lax.rsqrt((notes[:4] + notes[4:8]) * (1.0 / D) + 1e-06)
     spread = jnp.concatenate([jnp.broadcast_to(scale[at : at + 1], (REST, groups)) for at in range(4)], axis=0).T
-    for step, piece in zip(OWNERS, pieces):
-        at = pl.ds(pl.multiple_of((me ^ step) * WIDE, WIDE), WIDE)
-        ends_ref[:, at] = (piece[patches : patches + groups, :].astype(F32) * spread).astype(BF16)
-    total = bias_ref[...] + lax.dot_general(tail_ref[...], ends_ref[...], contract, preferred_element_type=F32)
+    ends = rows[patches : patches + groups].astype(F32) * jnp.concatenate([spread] * 2, axis=1)
+    total = bias_ref[...] + lax.dot_general(
+        tail_ref[:, pl.ds(block, 2 * WIDE)], ends.astype(BF16), contract, preferred_element_type=F32
+    )
     for corner in range(4):
         part = before_ref[corner] + lax.dot_general(
             weight_ref[:, pl.ds(pl.multiple_of(corner * D + block, 2 * WIDE), 2 * WIDE)],
@@ -576,14 +595,17 @@
     )(merge_weight, in_hbm(merge_bias), hidden)
     sums = shape(4, units, groups, dtype=F32)
     one, two, far = swap(hidden, 4), swap(hidden, 2), swap(hidden, 6)
-    first = kernel(merge_first_kernel, "merge_first", sums, count=4, flops=1, moved=1)(hidden, one, two, merge_weight)
+    first = kernel(merge_first_kernel, "merge_first", sums, count=5, flops=1, moved=1)(
+        hidden, one, two, merge_weight, ends
+    )
     near = [swap(after(hidden, ends), 1), swap(one, 1), swap(two, 1)]
-    second = kernel(merge_second_kernel, "merge_second", sums, count=5, flops=1, moved=1)(*near, first, merge_weight)
+    second = kernel(merge_second_kernel, "merge_second", sums, count=6, flops=1, moved=1)(
+        *near, first, merge_weight, ends
+    )
     return kernel(
         merge_kernel,
         "merge",
         shape(1, units, groups),
-        [pltpu.VMEM((groups, MAIN), BF16)],
         count=ROWS + 5,
         flops=4 * units * groups * MAIN,
         moved=8 << 20,

time: 45.1 us -> 44.8 us (level)
  waiting for transfers between devices: 10.6 us -> 9.48 us
  Pallas kernels: 10.9 us -> 11.7 us
    ppermute x22, waiting for transfers between devices: 7 us -> 5.89 us  [swap(): lax.ppermute(value, 'row', [(row, row ^ (odd if row % 2 else even)) for r...]
    pallas_call x3, Pallas kernels: 3.17 us -> 3.93 us  [the longest x1 1.39 us: local_eight(): kernel(merge_kernel, 'merge', shape(1, units, groups), count=ROWS + 5, fl...]
  transfers between devices with their start and end apart: 24 -> 24, of which waited for: 8 -> 8; matrix products, arithmetic and copies ran while one was open for 0% -> 0% of each run, Pallas kernels for 16% -> 18%
where the time goes in v17:
time: 44.8 us; the launch traced here: 44.6 us
  starting transfers between devices  22 us (49%)
  Pallas kernels  11.7 us (26%)
  waiting for transfers between devices  9.48 us (21%)
  local copies, waits for them, and re-layouts  1.16 us (3%)
    ppermute x22, starting transfers between devices, swap(): lax.ppermute(value, 'row', [(row, row ^ (odd if row % 2 else even)) for r...  17.4 us
    ppermute x22, waiting for transfers between devices, swap(): lax.ppermute(value, 'row', [(row, row ^ (odd if row % 2 else even)) for r...  5.89 us
    ppermute x2, starting transfers between devices, turn(): return lax.ppermute(value, ('page', 'row'), pairs)  4.65 us
    ppermute x2, waiting for transfers between devices, turn(): return lax.ppermute(value, ('page', 'row'), pairs)  3.59 us
    pallas_call x1, Pallas kernels, local_eight(): kernel(spread_kernel, 'spread', [shape(band, 4 * HPAIR)] * ROWS + [shape(...  1.54 us
    pallas_call x1, Pallas kernels, local_eight(): kernel(tail_kernel, 'merge_tail', [shape(units, MAIN), shape(units, 1, dt...  1.39 us
    pallas_call x1, Pallas kernels, local_eight(): kernel(merge_kernel, 'merge', shape(1, units, groups), count=ROWS + 5, fl...  1.39 us
    pallas_call x1, Pallas kernels, local_eight(): kernel(attend_kernel, 'attend', shape(piece, WIDE), [pltpu.VMEM((patches,...  1.34 us
  transfers between devices with their start and end apart: 24, of which 8 were waited for; matrix products, arithmetic and copies ran while one was open for 0% of the time, Pallas kernels for 18%

profile of v17, /device:TPU:0, one launch (start us, length us, event | category | flops | bytes accessed | tf_op | source)
XLA Modules:
  0.0 44.6 jit_solution(11301217802526243700)
XLA Ops:
  0.0 1.5 %spread.1 = (bf16[64,640]{1,0:T(8,128)(2,1)S(1)}, bf16[64,640]{1,0:T(8,128)(2,1)S(1)}, bf16[64,640]{1,0:T(8,128)(2,1)S(1)}, bf16[64,640]{1,0:T(8,128)(2,1)S(1)},...) custom-call(bf16[1,64,3840]{2,1,0:T(8,128)(2,1)} %qkv_hbm.1, ...), custom_call_target="tpu_custom_call" | custom-call | bytes 1048576 | tf_op jit(solution)/shard_map/spread/pallas_call | solution.py:510
  1.5 3.0 %collective-permute-start = (bf16[64,640]{1,0:T(8,128)(2,1)S(1)}, bf16[64,640]{1,0:T(8,128)(2,1)S(1)}, u32[]{:S(2)}, u32[]{:S(2)}) collective-permute-start(bf16[64,640]{1,0:T(8,128)(2,1)S(1)} %get-tuple-element.32), channel_id=1, source_target_pairs={{0,4},{1,3},{2,6},{3,1},{4,0},{5,7},{6,2},{7,5},{8,12},{9,11},{10,... | collective-permute-start | bytes 245768 | tf_op jit(solution)/shard_map/ppermute | solution.py:485
  4.6 1.5 %collective-permute-start.1 = (bf16[64,640]{1,0:T(8,128)(2,1)S(1)}, bf16[64,640]{1,0:T(8,128)(2,1)S(1)}, u32[]{:S(2)}, u32[]{:S(2)}) collective-permute-start(bf16[64,640]{1,0:T(8,128)(2,1)S(1)} %get-tuple-element.33), channel_id=1, source_target_pairs={{0,2},{1,5},{2,0},{3,7},{4,6},{5,1},{6,4},{7,3},{8,10},{9,13},{10,... | collective-permute-start | bytes 245768 | tf_op jit(solution)/shard_map/ppermute | solution.py:485
  6.1 1.5 %collective-permute-start.3 = (bf16[64,640]{1,0:T(8,128)(2,1)S(1)}, bf16[64,640]{1,0:T(8,128)(2,1)S(1)}, u32[]{:S(2)}, u32[]{:S(2)}) collective-permute-start(bf16[64,640]{1,0:T(8,128)(2,1)S(1)} %get-tuple-element.38), channel_id=1, source_target_pairs={{0,7},{1,6},{2,5},{3,4},{4,3},{5,2},{6,1},{7,0},{8,15},{9,14},{10,... | collective-permute-start | bytes 245768 | tf_op jit(solution)/shard_map/ppermute | solution.py:485
  7.6 1.7 %collective-permute-start.4 = (bf16[64,640]{1,0:T(8,128)(2,1)S(1)}, bf16[64,640]{1,0:T(8,128)(2,1)S(1)}, u32[]{:S(2)}, u32[]{:S(2)}) collective-permute-start(bf16[64,640]{1,0:T(8,128)(2,1)S(1)} %get-tuple-element.39), channel_id=1, source_target_pairs={{0,3},{1,4},{2,1},{3,6},{4,7},{5,0},{6,5},{7,2},{8,11},{9,12},{10,... | collective-permute-start | bytes 245768 | tf_op jit(solution)/shard_map/ppermute | solution.py:485
  9.6 1.2 %collective-permute-start.6 = (bf16[64,640]{1,0:T(8,128)(2,1)S(1)}, bf16[64,640]{1,0:T(8,128)(2,1)S(1)}, u32[]{:S(2)}, u32[]{:S(2)}) collective-permute-start(bf16[64,640]{1,0:T(8,128)(2,1)S(1)} %get-tuple-element.41), channel_id=1, source_target_pairs={{0,1},{1,0},{2,3},{3,2},{4,5},{5,4},{6,7},{7,6},{8,9},{9,8},{10,11... | collective-permute-start | bytes 245768 | tf_op jit(solution)/shard_map/ppermute | solution.py:485
  10.9 1.1 %copy-done = bf16[320,1280]{1,0:T(8,128)(2,1)S(1)} copy-done((bf16[320,1280]{1,0:T(8,128)(2,1)S(1)}, bf16[320,1280]{1,0:T(8,128)(2,1)}, u32[]{:S(2)}) %copy-start) | copy-done | bytes 819224
  12.2 1.6 %collective-permute-start.10 = (bf16[800,128]{1,0:T(8,128)(2,1)S(1)}, bf16[800,128]{1,0:T(8,128)(2,1)S(1)}, u32[]{:S(2)}, u32[]{:S(2)}) collective-permute-start(bf16[800,128]{1,0:T(8,128)(2,1)S(1)} %get-tuple-element.44), channel_id=1, source_target_pairs={{0,8},{1,25},{2,10},{3,27},{4,12},{5,29},{6,14},{7,31},{8,16},{9,1... | collective-permute-start | bytes 614408 | tf_op jit(solution)/shard_map/ppermute | solution.py:494
  14.3 1.3 %attend.1.token_ref.rest_0_ = bf16[640,128]{1,0:T(8,128)(2,1)S(1)} custom-call(bf16[512,512]{1,0:T(8,128)(2,1)S(1)} %get-tuple-element.35.select_ref, f32[1,512]{1,0:T(1,128)S(1)} %get-tuple-element.36.dead_ref, bf16[64,640]{1,0:T(8,128)(2,1)S(1)} %get-tuple-element.37.rest_0_, bf16[64,640]{1,0:T(8,128)(2,1)S(1)} %collective-permute-done.rest_0_.rest_1_, ...), custom_call_target="tpu_custom_call" | custom-call | flops 21474836480 | bytes 1048576 | tf_op jit(solution)/shard_map/attend/pallas_call | solution.py:544
  15.6 1.2 %collective-permute-start.13 = (bf16[640,128]{1,0:T(8,128)(2,1)S(1)}, bf16[640,128]{1,0:T(8,128)(2,1)S(1)}, u32[]{:S(2)}, u32[]{:S(2)}) collective-permute-start(bf16[640,128]{1,0:T(8,128)(2,1)S(1)} %attend.1.token_ref.rest_0_), channel_id=1, source_target_pairs={{0,4},{1,5},{2,6},{3,7},{4,0},{5,1},{6,2},{7,3},{8,12},{9,13},{10,... | collective-permute-start | bytes 491528 | tf_op jit(solution)/shard_map/ppermute | solution.py:485
  16.8 0.8 %collective-permute-start.15 = (bf16[640,128]{1,0:T(8,128)(2,1)S(1)}, bf16[640,128]{1,0:T(8,128)(2,1)S(1)}, u32[]{:S(2)}, u32[]{:S(2)}) collective-permute-start(bf16[640,128]{1,0:T(8,128)(2,1)S(1)} %attend.1.token_ref.rest_0_), channel_id=1, source_target_pairs={{0,2},{1,3},{2,0},{3,1},{4,6},{5,7},{6,4},{7,5},{8,10},{9,11},{10,... | collective-permute-start | bytes 491528 | tf_op jit(solution)/shard_map/ppermute | solution.py:485
  17.7 1.5 %collective-permute-start.7 = (bf16[640,128]{1,0:T(8,128)(2,1)S(1)}, bf16[640,128]{1,0:T(8,128)(2,1)S(1)}, u32[]{:S(2)}, u32[]{:S(2)}) collective-permute-start(bf16[640,128]{1,0:T(8,128)(2,1)S(1)} %attend.1.token_ref.rest_0_), channel_id=1, source_target_pairs={{0,6},{1,7},{2,4},{3,5},{4,2},{5,3},{6,0},{7,1},{8,14},{9,15},{10,... | collective-permute-start | bytes 491528 | tf_op jit(solution)/shard_map/ppermute | solution.py:485
  19.2 3.0 %collective-permute-start.9 = (bf16[400,128]{1,0:T(8,128)(2,1)S(1)}, bf16[400,128]{1,0:T(8,128)(2,1)S(1)}, u32[]{:S(2)}, u32[]{:S(2)}) collective-permute-start(bf16[400,128]{1,0:T(8,128)(2,1)S(1)} %get-tuple-element.43.rest_8_), channel_id=1, source_target_pairs={{0,16},{1,17},{2,18},{3,19},{4,20},{5,21},{6,22},{7,23},{8,24},{9,... | collective-permute-start | bytes 307208 | tf_op jit(solution)/shard_map/ppermute | solution.py:494
  22.2 1.3 %ready.1 = (f32[512,160]{1,0:T(8,128)S(1)}, f32[1,160]{1,0:T(1,128)S(1)}, bf16[1024,160]{1,0:T(8,128)(2,1)S(1)}, bf16[4,1024,160]{2,1,0:T(8,128)(2,1)S(1)}) custom-call(bf16[512,512]{1,0:T(8,128)(2,1)S(1)} %get-tuple-element.35.select_ref, f32[1280]{0:T(1024)} %gain_hbm.1, bf16[640,128]{1,0:T(8,128)(2,1)S(1)} %attend.1.token_ref.rest_0_, ...), custom_call_target="tpu_custom_call" | custom-call | flops 10737418240 | bytes 4194304 | tf_op jit(solution)/shard_map/ready/pallas_call | solution.py:554
  24.2 3.6 %collective-permute-done.9.across_ref = bf16[400,128]{1,0:T(8,128)(2,1)S(1)} collective-permute-done((bf16[400,128]{1,0:T(8,128)(2,1)S(1)}, bf16[400,128]{1,0:T(8,128)(2,1)S(1)}, u32[]{:S(2)}, u32[]{:S(2)}) %collective-permute-start.9) | collective-permute-done | bytes 102432 | tf_op jit(solution)/shard_map/ppermute | solution.py:494
  31.3 0.9 %collective-permute-start.18 = (bf16[656,128]{1,0:T(8,128)(2,1)S(1)}, bf16[656,128]{1,0:T(8,128)(2,1)S(1)}, u32[]{:S(2)}, u32[]{:S(2)}) collective-permute-start(bf16[656,128]{1,0:T(8,128)(2,1)S(1)} %project.1.token_ref.rest_0_), channel_id=1, source_target_pairs={{0,2},{1,3},{2,0},{3,1},{4,6},{5,7},{6,4},{7,5},{8,10},{9,11},{10,... | collective-permute-start | bytes 503816 | tf_op jit(solution)/shard_map/ppermute | solution.py:485
  32.2 1.9 %collective-permute-start.22 = (bf16[656,128]{1,0:T(8,128)(2,1)S(1)}, bf16[656,128]{1,0:T(8,128)(2,1)S(1)}, u32[]{:S(2)}, u32[]{:S(2)}) collective-permute-start(bf16[656,128]{1,0:T(8,128)(2,1)S(1)} %project.1.token_ref.rest_0_), channel_id=1, source_target_pairs={{0,6},{1,7},{2,4},{3,5},{4,2},{5,3},{6,0},{7,1},{8,14},{9,15},{10,... | collective-permute-start | bytes 503816 | tf_op jit(solution)/shard_map/ppermute | solution.py:485
  34.1 1.4 %merge_tail.1 = (bf16[640,1024]{1,0:T(8,128)(2,1)S(1)}, f32[640,1]{1,0:T(8,128)S(1)}) custom-call(bf16[640,5120]{1,0:T(8,128)(2,1)S(1)} %bitcast.1, f32[640]{0:T(1024)} %bias_hbm.1, bf16[656,128]{1,0:T(8,128)(2,1)S(1)} %project.1.token_ref.rest_0_), custom_call_target="tpu_custom_call" | custom-call | bytes 4194304 | tf_op jit(solution)/shard_map/merge_tail/pallas_call | solution.py:587
  35.6 1.4 %collective-permute-done.17.rest_1_ = bf16[656,128]{1,0:T(8,128)(2,1)S(1)} collective-permute-done((bf16[656,128]{1,0:T(8,128)(2,1)S(1)}, bf16[656,128]{1,0:T(8,128)(2,1)S(1)}, u32[]{:S(2)}, u32[]{:S(2)}) %collective-permute-start.17) | collective-permute-done | bytes 167968 | tf_op jit(solution)/shard_map/ppermute | solution.py:485
  37.0 1.5 %collective-permute-done.18.rest_2_ = bf16[656,128]{1,0:T(8,128)(2,1)S(1)} collective-permute-done((bf16[656,128]{1,0:T(8,128)(2,1)S(1)}, bf16[656,128]{1,0:T(8,128)(2,1)S(1)}, u32[]{:S(2)}, u32[]{:S(2)}) %collective-permute-start.18) | collective-permute-done | bytes 167968 | tf_op jit(solution)/shard_map/ppermute | solution.py:485
  38.5 1.2 %merge_first.1.rest_3_ = f32[4,640,128]{2,1,0:T(8,128)S(1)} custom-call(bf16[656,128]{1,0:T(8,128)(2,1)S(1)} %project.1.token_ref.rest_0_, bf16[656,128]{1,0:T(8,128)(2,1)S(1)} %collective-permute-done.17.rest_1_, bf16[656,128]{1,0:T(8,128)(2,1)S(1)} %collective-permute-done.18.rest_2_, bf16[640,5120]{1,0:T(8,128)(2,1)S(1)} %bitcast.1, ...), custom_call_target="tpu_custom_call" | custom-call | flops 1 | bytes 1 | tf_op jit(solution)/shard_map/merge_first/pallas_call | solution.py:598
  39.7 2.0 %collective-permute-done.22.rest_6_ = bf16[656,128]{1,0:T(8,128)(2,1)S(1)} collective-permute-done((bf16[656,128]{1,0:T(8,128)(2,1)S(1)}, bf16[656,128]{1,0:T(8,128)(2,1)S(1)}, u32[]{:S(2)}, u32[]{:S(2)}) %collective-permute-start.22) | collective-permute-done | bytes 167968 | tf_op jit(solution)/shard_map/ppermute | solution.py:485
  41.8 1.3 %merge_second.1.rest_8_ = f32[4,640,128]{2,1,0:T(8,128)S(1)} custom-call(bf16[656,128]{1,0:T(8,128)(2,1)S(1)} %collective-permute-done.19.rest_0_.rest_3_, bf16[656,128]{1,0:T(8,128)(2,1)S(1)} %collective-permute-done.20.rest_1_.rest_4_, bf16[656,128]{1,0:T(8,128)(2,1)S(1)} %collective-permute-done.21.rest_2_.rest_5_, ...), custom_call_target="tpu_custom_call" | custom-call | flops 1 | bytes 1 | tf_op jit(solution)/shard_map/merge_second/pallas_call | solution.py:602
  43.2 1.4 %merge.1 = bf16[1,640,128]{2,1,0:T(8,128)(2,1)} custom-call(bf16[656,128]{1,0:T(8,128)(2,1)S(1)} %project.1.token_ref.rest_0_, bf16[656,128]{1,0:T(8,128)(2,1)S(1)} %collective-permute-done.17.rest_1_, bf16[656,128]{1,0:T(8,128)(2,1)S(1)} %collective-permute-done.18.rest_2_, bf16[656,128]{1,0:T(8,128)(2,1)S(1)} %collective-permute-done.19.rest_0_.rest_3_, ...), custom_call_target="tpu_custom_call" | custom-call | flops 335544320 | bytes 8388608 | tf_op jit(solution)/shard_map/merge/pallas_call | solution.py:605
  (44 shorter events, 5.4 us)
Async XLA Ops:
  1.5 7.7 %collective-permute-start = (bf16[64,640]{1,0:T(8,128)(2,1)S(1)}, bf16[64,640]{1,0:T(8,128)(2,1)S(1)}, u32[]{:S(2)}, u32[]{:S(2)}) collective-permute-start(bf16[64,640]{1,0:T(8,128)(2,1)S(1)} %get-tuple-element.32), channel_id=1, source_target_pairs={{0,4},{1,3},{2,6},{3,1},{4,0},{5,7},{6,2},{7,5},{8,12},{9,11},{10,... | collective-permute-start | bytes 245768 | tf_op jit(solution)/shard_map/ppermute | solution.py:485
  4.6 5.1 %collective-permute-start.1 = (bf16[64,640]{1,0:T(8,128)(2,1)S(1)}, bf16[64,640]{1,0:T(8,128)(2,1)S(1)}, u32[]{:S(2)}, u32[]{:S(2)}) collective-permute-start(bf16[64,640]{1,0:T(8,128)(2,1)S(1)} %get-tuple-element.33), channel_id=1, source_target_pairs={{0,2},{1,5},{2,0},{3,7},{4,6},{5,1},{6,4},{7,3},{8,10},{9,13},{10,... | collective-permute-start | bytes 245768 | tf_op jit(solution)/shard_map/ppermute | solution.py:485
  6.1 6.2 %collective-permute-start.2 = (bf16[64,640]{1,0:T(8,128)(2,1)S(1)}, bf16[64,640]{1,0:T(8,128)(2,1)S(1)}, u32[]{:S(2)}, u32[]{:S(2)}) collective-permute-start(bf16[64,640]{1,0:T(8,128)(2,1)S(1)} %get-tuple-element.34), channel_id=1, source_target_pairs={{0,6},{1,7},{2,4},{3,5},{4,2},{5,3},{6,0},{7,1},{8,14},{9,15},{10,... | collective-permute-start | bytes 245768 | tf_op jit(solution)/shard_map/ppermute | solution.py:485
  6.1 7.9 %collective-permute-start.3 = (bf16[64,640]{1,0:T(8,128)(2,1)S(1)}, bf16[64,640]{1,0:T(8,128)(2,1)S(1)}, u32[]{:S(2)}, u32[]{:S(2)}) collective-permute-start(bf16[64,640]{1,0:T(8,128)(2,1)S(1)} %get-tuple-element.38), channel_id=1, source_target_pairs={{0,7},{1,6},{2,5},{3,4},{4,3},{5,2},{6,1},{7,0},{8,15},{9,14},{10,... | collective-permute-start | bytes 245768 | tf_op jit(solution)/shard_map/ppermute | solution.py:485
  7.6 6.7 %collective-permute-start.4 = (bf16[64,640]{1,0:T(8,128)(2,1)S(1)}, bf16[64,640]{1,0:T(8,128)(2,1)S(1)}, u32[]{:S(2)}, u32[]{:S(2)}) collective-permute-start(bf16[64,640]{1,0:T(8,128)(2,1)S(1)} %get-tuple-element.39), channel_id=1, source_target_pairs={{0,3},{1,4},{2,1},{3,6},{4,7},{5,0},{6,5},{7,2},{8,11},{9,12},{10,... | collective-permute-start | bytes 245768 | tf_op jit(solution)/shard_map/ppermute | solution.py:485
  9.3 5.0 %collective-permute-start.5 = (bf16[64,640]{1,0:T(8,128)(2,1)S(1)}, bf16[64,640]{1,0:T(8,128)(2,1)S(1)}, u32[]{:S(2)}, u32[]{:S(2)}) collective-permute-start(bf16[64,640]{1,0:T(8,128)(2,1)S(1)} %get-tuple-element.40), channel_id=1, source_target_pairs={{0,5},{1,2},{2,7},{3,0},{4,1},{5,6},{6,3},{7,4},{8,13},{9,10},{10,... | collective-permute-start | bytes 245768 | tf_op jit(solution)/shard_map/ppermute | solution.py:485
  9.6 4.7 %collective-permute-start.6 = (bf16[64,640]{1,0:T(8,128)(2,1)S(1)}, bf16[64,640]{1,0:T(8,128)(2,1)S(1)}, u32[]{:S(2)}, u32[]{:S(2)}) collective-permute-start(bf16[64,640]{1,0:T(8,128)(2,1)S(1)} %get-tuple-element.41), channel_id=1, source_target_pairs={{0,1},{1,0},{2,3},{3,2},{4,5},{5,4},{6,7},{7,6},{8,9},{9,8},{10,11... | collective-permute-start | bytes 245768 | tf_op jit(solution)/shard_map/ppermute | solution.py:485
  12.2 10.0 %collective-permute-start.10 = (bf16[800,128]{1,0:T(8,128)(2,1)S(1)}, bf16[800,128]{1,0:T(8,128)(2,1)S(1)}, u32[]{:S(2)}, u32[]{:S(2)}) collective-permute-start(bf16[800,128]{1,0:T(8,128)(2,1)S(1)} %get-tuple-element.44), channel_id=1, source_target_pairs={{0,8},{1,25},{2,10},{3,27},{4,12},{5,29},{6,14},{7,31},{8,16},{9,1... | collective-permute-start | bytes 614408 | tf_op jit(solution)/shard_map/ppermute | solution.py:494
  15.6 7.9 %collective-permute-start.13 = (bf16[640,128]{1,0:T(8,128)(2,1)S(1)}, bf16[640,128]{1,0:T(8,128)(2,1)S(1)}, u32[]{:S(2)}, u32[]{:S(2)}) collective-permute-start(bf16[640,128]{1,0:T(8,128)(2,1)S(1)} %attend.1.token_ref.rest_0_), channel_id=1, source_target_pairs={{0,4},{1,5},{2,6},{3,7},{4,0},{5,1},{6,2},{7,3},{8,12},{9,13},{10,... | collective-permute-start | bytes 491528 | tf_op jit(solution)/shard_map/ppermute | solution.py:485
  16.8 7.2 %collective-permute-start.15 = (bf16[640,128]{1,0:T(8,128)(2,1)S(1)}, bf16[640,128]{1,0:T(8,128)(2,1)S(1)}, u32[]{:S(2)}, u32[]{:S(2)}) collective-permute-start(bf16[640,128]{1,0:T(8,128)(2,1)S(1)} %attend.1.token_ref.rest_0_), channel_id=1, source_target_pairs={{0,2},{1,3},{2,0},{3,1},{4,6},{5,7},{6,4},{7,5},{8,10},{9,11},{10,... | collective-permute-start | bytes 491528 | tf_op jit(solution)/shard_map/ppermute | solution.py:485
  17.7 10.4 %collective-permute-start.7 = (bf16[640,128]{1,0:T(8,128)(2,1)S(1)}, bf16[640,128]{1,0:T(8,128)(2,1)S(1)}, u32[]{:S(2)}, u32[]{:S(2)}) collective-permute-start(bf16[640,128]{1,0:T(8,128)(2,1)S(1)} %attend.1.token_ref.rest_0_), channel_id=1, source_target_pairs={{0,6},{1,7},{2,4},{3,5},{4,2},{5,3},{6,0},{7,1},{8,14},{9,15},{10,... | collective-permute-start | bytes 491528 | tf_op jit(solution)/shard_map/ppermute | solution.py:485
  19.2 8.6 %collective-permute-start.9 = (bf16[400,128]{1,0:T(8,128)(2,1)S(1)}, bf16[400,128]{1,0:T(8,128)(2,1)S(1)}, u32[]{:S(2)}, u32[]{:S(2)}) collective-permute-start(bf16[400,128]{1,0:T(8,128)(2,1)S(1)} %get-tuple-element.43.rest_8_), channel_id=1, source_target_pairs={{0,16},{1,17},{2,18},{3,19},{4,20},{5,21},{6,22},{7,23},{8,24},{9,... | collective-permute-start | bytes 307208 | tf_op jit(solution)/shard_map/ppermute | solution.py:494
  22.2 5.5 %collective-permute-start.11 = (bf16[800,128]{1,0:T(8,128)(2,1)S(1)}, bf16[800,128]{1,0:T(8,128)(2,1)S(1)}, u32[]{:S(2)}, u32[]{:S(2)}) collective-permute-start(bf16[800,128]{1,0:T(8,128)(2,1)S(1)} %collective-permute-done.10.rest_9_), channel_id=1, source_target_pairs={{0,1},{1,0},{2,3},{3,2},{4,5},{5,4},{6,7},{7,6},{8,9},{9,8},{10,11... | collective-permute-start | bytes 614408 | tf_op jit(solution)/shard_map/ppermute | solution.py:485
  23.5 5.6 %collective-permute-start.14 = (bf16[640,128]{1,0:T(8,128)(2,1)S(1)}, bf16[640,128]{1,0:T(8,128)(2,1)S(1)}, u32[]{:S(2)}, u32[]{:S(2)}) collective-permute-start(bf16[640,128]{1,0:T(8,128)(2,1)S(1)} %collective-permute-done.13.rest_1_), channel_id=1, source_target_pairs={{0,1},{1,0},{2,3},{3,2},{4,5},{5,4},{6,7},{7,6},{8,9},{9,8},{10,11... | collective-permute-start | bytes 491528 | tf_op jit(solution)/shard_map/ppermute | solution.py:485
  24.1 5.0 %collective-permute-start.16 = (bf16[640,128]{1,0:T(8,128)(2,1)S(1)}, bf16[640,128]{1,0:T(8,128)(2,1)S(1)}, u32[]{:S(2)}, u32[]{:S(2)}) collective-permute-start(bf16[640,128]{1,0:T(8,128)(2,1)S(1)} %collective-permute-done.15.rest_2_), channel_id=1, source_target_pairs={{0,1},{1,0},{2,3},{3,2},{4,5},{5,4},{6,7},{7,6},{8,9},{9,8},{10,11... | collective-permute-start | bytes 491528 | tf_op jit(solution)/shard_map/ppermute | solution.py:485
  28.0 1.5 %collective-permute-start.12 = (bf16[640,128]{1,0:T(8,128)(2,1)S(1)}, bf16[640,128]{1,0:T(8,128)(2,1)S(1)}, u32[]{:S(2)}, u32[]{:S(2)}) collective-permute-start(bf16[640,128]{1,0:T(8,128)(2,1)S(1)} %attend.1.token_ref.rest_0_), channel_id=1, source_target_pairs={{0,1},{1,0},{2,3},{3,2},{4,5},{5,4},{6,7},{7,6},{8,9},{9,8},{10,11... | collective-permute-start | bytes 491528 | tf_op jit(solution)/shard_map/ppermute | solution.py:485
  28.1 1.8 %collective-permute-start.8 = (bf16[640,128]{1,0:T(8,128)(2,1)S(1)}, bf16[640,128]{1,0:T(8,128)(2,1)S(1)}, u32[]{:S(2)}, u32[]{:S(2)}) collective-permute-start(bf16[640,128]{1,0:T(8,128)(2,1)S(1)} %collective-permute-done.7.rest_0_), channel_id=1, source_target_pairs={{0,1},{1,0},{2,3},{3,2},{4,5},{5,4},{6,7},{7,6},{8,9},{9,8},{10,11... | collective-permute-start | bytes 491528 | tf_op jit(solution)/shard_map/ppermute | solution.py:485
  30.6 6.4 %collective-permute-start.17 = (bf16[656,128]{1,0:T(8,128)(2,1)S(1)}, bf16[656,128]{1,0:T(8,128)(2,1)S(1)}, u32[]{:S(2)}, u32[]{:S(2)}) collective-permute-start(bf16[656,128]{1,0:T(8,128)(2,1)S(1)} %project.1.token_ref.rest_0_), channel_id=1, source_target_pairs={{0,4},{1,5},{2,6},{3,7},{4,0},{5,1},{6,2},{7,3},{8,12},{9,13},{10,... | collective-permute-start | bytes 503816 | tf_op jit(solution)/shard_map/ppermute | solution.py:485
  31.3 7.2 %collective-permute-start.18 = (bf16[656,128]{1,0:T(8,128)(2,1)S(1)}, bf16[656,128]{1,0:T(8,128)(2,1)S(1)}, u32[]{:S(2)}, u32[]{:S(2)}) collective-permute-start(bf16[656,128]{1,0:T(8,128)(2,1)S(1)} %project.1.token_ref.rest_0_), channel_id=1, source_target_pairs={{0,2},{1,3},{2,0},{3,1},{4,6},{5,7},{6,4},{7,5},{8,10},{9,11},{10,... | collective-permute-start | bytes 503816 | tf_op jit(solution)/shard_map/ppermute | solution.py:485
  32.2 9.5 %collective-permute-start.22 = (bf16[656,128]{1,0:T(8,128)(2,1)S(1)}, bf16[656,128]{1,0:T(8,128)(2,1)S(1)}, u32[]{:S(2)}, u32[]{:S(2)}) collective-permute-start(bf16[656,128]{1,0:T(8,128)(2,1)S(1)} %project.1.token_ref.rest_0_), channel_id=1, source_target_pairs={{0,6},{1,7},{2,4},{3,5},{4,2},{5,3},{6,0},{7,1},{8,14},{9,15},{10,... | collective-permute-start | bytes 503816 | tf_op jit(solution)/shard_map/ppermute | solution.py:485
  35.5 4.2 %collective-permute-start.19 = (bf16[656,128]{1,0:T(8,128)(2,1)S(1)}, bf16[656,128]{1,0:T(8,128)(2,1)S(1)}, u32[]{:S(2)}, u32[]{:S(2)}) collective-permute-start(bf16[656,128]{1,0:T(8,128)(2,1)S(1)} %project.1.token_ref.rest_0_), channel_id=1, source_target_pairs={{0,1},{1,0},{2,3},{3,2},{4,5},{5,4},{6,7},{7,6},{8,9},{9,8},{10,11... | collective-permute-start | bytes 503816 | tf_op jit(solution)/shard_map/ppermute | solution.py:485
  37.0 4.8 %collective-permute-start.20 = (bf16[656,128]{1,0:T(8,128)(2,1)S(1)}, bf16[656,128]{1,0:T(8,128)(2,1)S(1)}, u32[]{:S(2)}, u32[]{:S(2)}) collective-permute-start(bf16[656,128]{1,0:T(8,128)(2,1)S(1)} %collective-permute-done.17.rest_1_), channel_id=1, source_target_pairs={{0,1},{1,0},{2,3},{3,2},{4,5},{5,4},{6,7},{7,6},{8,9},{9,8},{10,11... | collective-permute-start | bytes 503816 | tf_op jit(solution)/shard_map/ppermute | solution.py:485
  38.5 3.3 %collective-permute-start.21 = (bf16[656,128]{1,0:T(8,128)(2,1)S(1)}, bf16[656,128]{1,0:T(8,128)(2,1)S(1)}, u32[]{:S(2)}, u32[]{:S(2)}) collective-permute-start(bf16[656,128]{1,0:T(8,128)(2,1)S(1)} %collective-permute-done.18.rest_2_), channel_id=1, source_target_pairs={{0,1},{1,0},{2,3},{3,2},{4,5},{5,4},{6,7},{7,6},{8,9},{9,8},{10,11... | collective-permute-start | bytes 503816 | tf_op jit(solution)/shard_map/ppermute | solution.py:485
  41.8 1.4 %collective-permute-start.23 = (bf16[656,128]{1,0:T(8,128)(2,1)S(1)}, bf16[656,128]{1,0:T(8,128)(2,1)S(1)}, u32[]{:S(2)}, u32[]{:S(2)}) collective-permute-start(bf16[656,128]{1,0:T(8,128)(2,1)S(1)} %collective-permute-done.22.rest_6_), channel_id=1, source_target_pairs={{0,1},{1,0},{2,3},{3,2},{4,5},{5,4},{6,7},{7,6},{8,9},{9,8},{10,11... | collective-permute-start | bytes 503816 | tf_op jit(solution)/shard_map/ppermute | solution.py:485
  (3 other events, 11.8 us)

commit v18 on v17

--- a/solution.py
+++ b/solution.py
@@ -267,6 +267,8 @@
     core = me % 2
     size = own_ref.shape[0]
     half = pl.ds(pl.multiple_of(core * size, 16), size)
+    main_ref[...] = jnp.zeros_like(main_ref)
+    tail_ref[...] = jnp.zeros_like(tail_ref)
     place_slices([(0, own_ref[...]), (3 - 2 * core, near_ref[half, :])], main_ref, tail_ref)
     fetch.wait()
     whole = line[...].reshape(1, D)
@@ -279,13 +281,13 @@
 
 
 def place_slices(cuts, main_ref, tail_ref):
-    tail_ref[...] = jnp.zeros_like(tail_ref)
     for step, cut in cuts:
         place_rows(weight_rows(cut), 2 * lax.rem(lax.axis_index("page") + step, PAGES), main_ref, tail_ref)
 
 
-def last_kernel(across_ref, swapped_ref, token_ref, main_ref, tail_ref):
-    del token_ref
+def last_kernel(across_ref, swapped_ref, main_before_ref, tail_before_ref, main_ref, tail_ref):
+    main_ref[...] = main_before_ref[...]
+    tail_ref[...] = tail_before_ref[...]
     core = row_index() % 2
     size = across_ref.shape[0]
     half = pl.ds(pl.multiple_of(core * size, 16), size)
@@ -304,13 +306,8 @@
     return jnp.concatenate([left, right], axis=1)
 
 
-def came_last(block):
-    page, core = lax.axis_index("page"), row_index() % 2
-    return (block == lax.rem(page + 2, PAGES)) | (block == lax.rem(page + 1 + 2 * core, PAGES))
-
-
 def add_features(owners, pieces, weights, before_ref, out_ref):
-    main_ref, tail_ref, last_main_ref, last_tail_ref = weights
+    main_ref, tail_ref = weights
     me = row_index()
     patches = out_ref.shape[0]
     groups = patches // 4
@@ -318,9 +315,8 @@
     for step in owners:
         pair = me ^ step
         columns = pl.ds(pl.multiple_of(pair * WIDE, WIDE), WIDE)
-        is_last = came_last(pair // 2)
-        mains.append(jnp.where(is_last, last_main_ref[columns, :], main_ref[columns, :]))
-        tails.append([jnp.where(is_last, last_tail_ref[at, columns, :], tail_ref[at, columns, :]) for at in range(4)])
+        mains.append(main_ref[columns, :])
+        tails.append([tail_ref[at, columns, :] for at in range(4)])
     rows = jnp.concatenate([piece[...] for piece in pieces], axis=1)
     base = before_ref[...] + jnp.dot(rows[:patches], jnp.concatenate(mains, axis=0), preferred_element_type=F32)
     for corner in range(4):
@@ -330,40 +326,37 @@
 
 
 def project_first_kernel(*rest):
-    add_features(OWNERS[:3], rest[:3], rest[3:7], *rest[7:])
+    add_features(OWNERS[:3], rest[:3], rest[3:5], *rest[5:])
 
 
 def project_second_kernel(*rest):
-    add_features(OWNERS[3:6], rest[:3], rest[3:7], *rest[7:])
+    add_features(OWNERS[3:6], rest[:3], rest[3:5], *rest[5:])
 
 
 def project_kernel(*rest):
-    same, other, base_ref, main_ref, tail_ref, last_main_ref, last_tail_ref, gain_ref, out_ref = rest
+    same, other, base_ref, main_ref, tail_ref, gain_ref, out_ref = rest
     patches = base_ref.shape[0]
     groups = patches // 4
     block = far_block()
-    is_last = came_last(row_index() // 2 ^ 3)
     full = collect_late(same, other)
-    main = jnp.where(is_last, last_main_ref[block, :], main_ref[block, :])
-    base = base_ref[...] + jnp.dot(full[:patches], main, preferred_element_type=F32)
-    ones = jnp.ones((NOTES, HPAIR), BF16)
-    contract = (((1,), (1,)), ((), ()))
+    base = base_ref[...] + jnp.dot(full[:patches], main_ref[block, :], preferred_element_type=F32)
+    hidden = []
+    for corner in range(4):
+        span = slice(corner * groups, (corner + 1) * groups)
+        hidden.append(base[span] + jnp.dot(full[patches:], tail_ref[corner, block, :], preferred_element_type=F32))
+    squares = jnp.concatenate([(rows * rows).astype(BF16) for rows in hidden], axis=0)
+    sums = lax.dot_general(
+        jnp.ones((NOTES, HPAIR), BF16), squares, (((1,), (1,)), ((), ())), preferred_element_type=F32
+    )
     row = lax.broadcasted_iota(jnp.int32, (NOTES, groups), 0)
     notes = jnp.zeros((NOTES, groups), F32)
     ends = []
     for corner in range(4):
-        span = slice(corner * groups, (corner + 1) * groups)
-        tail = jnp.where(is_last, last_tail_ref[corner, block, :], tail_ref[corner, block, :])
-        hidden = base[span] + jnp.dot(full[patches:], tail, preferred_element_type=F32)
-        square = hidden * hidden
-        high = square.astype(BF16)
-        low = (square - high.astype(F32)).astype(BF16)
-        total = lax.dot_general(ones, high, contract, preferred_element_type=F32)
-        total = total + lax.dot_general(ones, low, contract, preferred_element_type=F32)
+        total = sums[:, corner * groups : (corner + 1) * groups]
         coarse = total.astype(BF16).astype(F32)
         notes = jnp.where(row == corner, coarse, jnp.where(row == 4 + corner, total - coarse, notes))
-        sent = hidden * gain_ref[...]
-        out_ref[span, :] = sent[:, :WIDE].astype(BF16)
+        sent = hidden[corner] * gain_ref[...]
+        out_ref[corner * groups : (corner + 1) * groups, :] = sent[:, :WIDE].astype(BF16)
         ends.append(sent[:, WIDE:])
     out_ref[patches : patches + groups, :] = jnp.concatenate(ends, axis=1).astype(BF16)
     out_ref[patches + groups :, :] = notes.astype(BF16)
@@ -565,22 +558,21 @@
         last_kernel,
         "ready_last",
         [shape(MAIN, HPAIR), shape(4, MAIN, HPAIR)],
-        fetched=(2,),
-        count=3,
+        count=4,
         flops=1,
         moved=1,
-    )(across, swapped, main)
+    )(across, swapped, main, tail)
     one, two, far = swap(attn, 4), swap(attn, 2), swap(attn, 6)
-    weights = (main, tail, *last)
+    weights = tuple(last)
     rows = shape(patches, HPAIR, dtype=F32)
-    first = kernel(project_first_kernel, "project_first", rows, count=8, flops=1, moved=1)(attn, one, two, *weights, resid)
+    first = kernel(project_first_kernel, "project_first", rows, count=6, flops=1, moved=1)(attn, one, two, *weights, resid)
     near = [swap(after(attn, last[0]), 1), swap(one, 1), swap(two, 1)]
-    second = kernel(project_second_kernel, "project_second", rows, count=8, flops=1, moved=1)(*near, *weights, first)
+    second = kernel(project_second_kernel, "project_second", rows, count=6, flops=1, moved=1)(*near, *weights, first)
     hidden = kernel(
         project_kernel,
         "project",
         shape(piece + NOTES, WIDE),
-        count=2 + 6,
+        count=2 + 4,
         flops=patches * MAIN * 256,
         moved=4 << 20,
     )(far, swap(far, 1), second, *weights, own_gain)

time: 44.8 us -> 44.6 us (level)
  no operation moved by 1% of the time
where the time goes in v18:
time: 44.6 us; the launch traced here: 44.4 us
  starting transfers between devices  22.1 us (50%)
  Pallas kernels  11.4 us (26%)
  waiting for transfers between devices  9.55 us (21%)
  local copies, waits for them, and re-layouts  1.16 us (3%)
    ppermute x22, starting transfers between devices, swap(): lax.ppermute(value, 'row', [(row, row ^ (odd if row % 2 else even)) for r...  17.4 us
    ppermute x22, waiting for transfers between devices, swap(): lax.ppermute(value, 'row', [(row, row ^ (odd if row % 2 else even)) for r...  5.92 us
    ppermute x2, starting transfers between devices, turn(): return lax.ppermute(value, ('page', 'row'), pairs)  4.66 us
    ppermute x2, waiting for transfers between devices, turn(): return lax.ppermute(value, ('page', 'row'), pairs)  3.63 us
    pallas_call x1, Pallas kernels, local_eight(): kernel(spread_kernel, 'spread', [shape(band, 4 * HPAIR)] * ROWS + [shape(...  1.54 us
    pallas_call x1, Pallas kernels, local_eight(): kernel(tail_kernel, 'merge_tail', [shape(units, MAIN), shape(units, 1, dt...  1.39 us
    pallas_call x1, Pallas kernels, local_eight(): kernel(merge_kernel, 'merge', shape(1, units, groups), count=ROWS + 5, fl...  1.39 us
    pallas_call x1, Pallas kernels, local_eight(): kernel(attend_kernel, 'attend', shape(piece, WIDE), [pltpu.VMEM((patches,...  1.34 us
  transfers between devices with their start and end apart: 24, of which 8 were waited for; matrix products, arithmetic and copies ran while one was open for 0% of the time, Pallas kernels for 18%

profile of v18, /device:TPU:0, one launch (start us, length us, event | category | flops | bytes accessed | tf_op | source)
XLA Modules:
  0.0 44.4 jit_solution(18143004751267664721)
XLA Ops:
  0.0 1.5 %spread.1 = (bf16[64,640]{1,0:T(8,128)(2,1)S(1)}, bf16[64,640]{1,0:T(8,128)(2,1)S(1)}, bf16[64,640]{1,0:T(8,128)(2,1)S(1)}, bf16[64,640]{1,0:T(8,128)(2,1)S(1)},...) custom-call(bf16[1,64,3840]{2,1,0:T(8,128)(2,1)} %qkv_hbm.1, ...), custom_call_target="tpu_custom_call" | custom-call | bytes 1048576 | tf_op jit(solution)/shard_map/spread/pallas_call | solution.py:503
  1.5 3.0 %collective-permute-start = (bf16[64,640]{1,0:T(8,128)(2,1)S(1)}, bf16[64,640]{1,0:T(8,128)(2,1)S(1)}, u32[]{:S(2)}, u32[]{:S(2)}) collective-permute-start(bf16[64,640]{1,0:T(8,128)(2,1)S(1)} %get-tuple-element.32), channel_id=1, source_target_pairs={{0,4},{1,3},{2,6},{3,1},{4,0},{5,7},{6,2},{7,5},{8,12},{9,11},{10,... | collective-permute-start | bytes 245768 | tf_op jit(solution)/shard_map/ppermute | solution.py:478
  4.6 1.5 %collective-permute-start.1 = (bf16[64,640]{1,0:T(8,128)(2,1)S(1)}, bf16[64,640]{1,0:T(8,128)(2,1)S(1)}, u32[]{:S(2)}, u32[]{:S(2)}) collective-permute-start(bf16[64,640]{1,0:T(8,128)(2,1)S(1)} %get-tuple-element.33), channel_id=1, source_target_pairs={{0,2},{1,5},{2,0},{3,7},{4,6},{5,1},{6,4},{7,3},{8,10},{9,13},{10,... | collective-permute-start | bytes 245768 | tf_op jit(solution)/shard_map/ppermute | solution.py:478
  6.1 1.5 %collective-permute-start.3 = (bf16[64,640]{1,0:T(8,128)(2,1)S(1)}, bf16[64,640]{1,0:T(8,128)(2,1)S(1)}, u32[]{:S(2)}, u32[]{:S(2)}) collective-permute-start(bf16[64,640]{1,0:T(8,128)(2,1)S(1)} %get-tuple-element.38), channel_id=1, source_target_pairs={{0,7},{1,6},{2,5},{3,4},{4,3},{5,2},{6,1},{7,0},{8,15},{9,14},{10,... | collective-permute-start | bytes 245768 | tf_op jit(solution)/shard_map/ppermute | solution.py:478
  7.6 1.7 %collective-permute-start.4 = (bf16[64,640]{1,0:T(8,128)(2,1)S(1)}, bf16[64,640]{1,0:T(8,128)(2,1)S(1)}, u32[]{:S(2)}, u32[]{:S(2)}) collective-permute-start(bf16[64,640]{1,0:T(8,128)(2,1)S(1)} %get-tuple-element.39), channel_id=1, source_target_pairs={{0,3},{1,4},{2,1},{3,6},{4,7},{5,0},{6,5},{7,2},{8,11},{9,12},{10,... | collective-permute-start | bytes 245768 | tf_op jit(solution)/shard_map/ppermute | solution.py:478
  9.6 1.2 %collective-permute-start.6 = (bf16[64,640]{1,0:T(8,128)(2,1)S(1)}, bf16[64,640]{1,0:T(8,128)(2,1)S(1)}, u32[]{:S(2)}, u32[]{:S(2)}) collective-permute-start(bf16[64,640]{1,0:T(8,128)(2,1)S(1)} %get-tuple-element.41), channel_id=1, source_target_pairs={{0,1},{1,0},{2,3},{3,2},{4,5},{5,4},{6,7},{7,6},{8,9},{9,8},{10,11... | collective-permute-start | bytes 245768 | tf_op jit(solution)/shard_map/ppermute | solution.py:478
  10.9 1.1 %copy-done = bf16[320,1280]{1,0:T(8,128)(2,1)S(1)} copy-done((bf16[320,1280]{1,0:T(8,128)(2,1)S(1)}, bf16[320,1280]{1,0:T(8,128)(2,1)}, u32[]{:S(2)}) %copy-start) | copy-done | bytes 819224
  12.2 1.6 %collective-permute-start.10 = (bf16[800,128]{1,0:T(8,128)(2,1)S(1)}, bf16[800,128]{1,0:T(8,128)(2,1)S(1)}, u32[]{:S(2)}, u32[]{:S(2)}) collective-permute-start(bf16[800,128]{1,0:T(8,128)(2,1)S(1)} %get-tuple-element.44), channel_id=1, source_target_pairs={{0,8},{1,25},{2,10},{3,27},{4,12},{5,29},{6,14},{7,31},{8,16},{9,1... | collective-permute-start | bytes 614408 | tf_op jit(solution)/shard_map/ppermute | solution.py:487
  14.3 1.3 %attend.1.token_ref.rest_0_ = bf16[640,128]{1,0:T(8,128)(2,1)S(1)} custom-call(bf16[512,512]{1,0:T(8,128)(2,1)S(1)} %get-tuple-element.35.select_ref, f32[1,512]{1,0:T(1,128)S(1)} %get-tuple-element.36.dead_ref, bf16[64,640]{1,0:T(8,128)(2,1)S(1)} %get-tuple-element.37.rest_0_, bf16[64,640]{1,0:T(8,128)(2,1)S(1)} %collective-permute-done.rest_0_.rest_1_, ...), custom_call_target="tpu_custom_call" | custom-call | flops 21474836480 | bytes 1048576 | tf_op jit(solution)/shard_map/attend/pallas_call | solution.py:537
  15.6 1.2 %collective-permute-start.13 = (bf16[640,128]{1,0:T(8,128)(2,1)S(1)}, bf16[640,128]{1,0:T(8,128)(2,1)S(1)}, u32[]{:S(2)}, u32[]{:S(2)}) collective-permute-start(bf16[640,128]{1,0:T(8,128)(2,1)S(1)} %attend.1.token_ref.rest_0_), channel_id=1, source_target_pairs={{0,4},{1,5},{2,6},{3,7},{4,0},{5,1},{6,2},{7,3},{8,12},{9,13},{10,... | collective-permute-start | bytes 491528 | tf_op jit(solution)/shard_map/ppermute | solution.py:478
  16.9 0.8 %collective-permute-start.15 = (bf16[640,128]{1,0:T(8,128)(2,1)S(1)}, bf16[640,128]{1,0:T(8,128)(2,1)S(1)}, u32[]{:S(2)}, u32[]{:S(2)}) collective-permute-start(bf16[640,128]{1,0:T(8,128)(2,1)S(1)} %attend.1.token_ref.rest_0_), channel_id=1, source_target_pairs={{0,2},{1,3},{2,0},{3,1},{4,6},{5,7},{6,4},{7,5},{8,10},{9,11},{10,... | collective-permute-start | bytes 491528 | tf_op jit(solution)/shard_map/ppermute | solution.py:478
  17.7 1.5 %collective-permute-start.7 = (bf16[640,128]{1,0:T(8,128)(2,1)S(1)}, bf16[640,128]{1,0:T(8,128)(2,1)S(1)}, u32[]{:S(2)}, u32[]{:S(2)}) collective-permute-start(bf16[640,128]{1,0:T(8,128)(2,1)S(1)} %attend.1.token_ref.rest_0_), channel_id=1, source_target_pairs={{0,6},{1,7},{2,4},{3,5},{4,2},{5,3},{6,0},{7,1},{8,14},{9,15},{10,... | collective-permute-start | bytes 491528 | tf_op jit(solution)/shard_map/ppermute | solution.py:478
  19.2 3.0 %collective-permute-start.9 = (bf16[400,128]{1,0:T(8,128)(2,1)S(1)}, bf16[400,128]{1,0:T(8,128)(2,1)S(1)}, u32[]{:S(2)}, u32[]{:S(2)}) collective-permute-start(bf16[400,128]{1,0:T(8,128)(2,1)S(1)} %get-tuple-element.43.rest_8_), channel_id=1, source_target_pairs={{0,16},{1,17},{2,18},{3,19},{4,20},{5,21},{6,22},{7,23},{8,24},{9,... | collective-permute-start | bytes 307208 | tf_op jit(solution)/shard_map/ppermute | solution.py:487
  22.2 1.2 %ready.1 = (f32[512,160]{1,0:T(8,128)S(1)}, f32[1,160]{1,0:T(1,128)S(1)}, bf16[1024,160]{1,0:T(8,128)(2,1)S(1)}, bf16[4,1024,160]{2,1,0:T(8,128)(2,1)S(1)}) custom-call(bf16[512,512]{1,0:T(8,128)(2,1)S(1)} %get-tuple-element.35.select_ref, f32[1280]{0:T(1024)} %gain_hbm.1, bf16[640,128]{1,0:T(8,128)(2,1)S(1)} %attend.1.token_ref.rest_0_, ...), custom_call_target="tpu_custom_call" | custom-call | flops 10737418240 | bytes 4194304 | tf_op jit(solution)/shard_map/ready/pallas_call | solution.py:547
  24.1 3.6 %collective-permute-done.9.across_ref = bf16[400,128]{1,0:T(8,128)(2,1)S(1)} collective-permute-done((bf16[400,128]{1,0:T(8,128)(2,1)S(1)}, bf16[400,128]{1,0:T(8,128)(2,1)S(1)}, u32[]{:S(2)}, u32[]{:S(2)}) %collective-permute-start.9) | collective-permute-done | bytes 102432 | tf_op jit(solution)/shard_map/ppermute | solution.py:487
  31.1 0.9 %collective-permute-start.18 = (bf16[656,128]{1,0:T(8,128)(2,1)S(1)}, bf16[656,128]{1,0:T(8,128)(2,1)S(1)}, u32[]{:S(2)}, u32[]{:S(2)}) collective-permute-start(bf16[656,128]{1,0:T(8,128)(2,1)S(1)} %project.1.token_ref.rest_0_), channel_id=1, source_target_pairs={{0,2},{1,3},{2,0},{3,1},{4,6},{5,7},{6,4},{7,5},{8,10},{9,11},{10,... | collective-permute-start | bytes 503816 | tf_op jit(solution)/shard_map/ppermute | solution.py:478
  32.0 1.9 %collective-permute-start.22 = (bf16[656,128]{1,0:T(8,128)(2,1)S(1)}, bf16[656,128]{1,0:T(8,128)(2,1)S(1)}, u32[]{:S(2)}, u32[]{:S(2)}) collective-permute-start(bf16[656,128]{1,0:T(8,128)(2,1)S(1)} %project.1.token_ref.rest_0_), channel_id=1, source_target_pairs={{0,6},{1,7},{2,4},{3,5},{4,2},{5,3},{6,0},{7,1},{8,14},{9,15},{10,... | collective-permute-start | bytes 503816 | tf_op jit(solution)/shard_map/ppermute | solution.py:478
  34.0 1.4 %merge_tail.1 = (bf16[640,1024]{1,0:T(8,128)(2,1)S(1)}, f32[640,1]{1,0:T(8,128)S(1)}) custom-call(bf16[640,5120]{1,0:T(8,128)(2,1)S(1)} %bitcast.1, f32[640]{0:T(1024)} %bias_hbm.1, bf16[656,128]{1,0:T(8,128)(2,1)S(1)} %project.1.token_ref.rest_0_), custom_call_target="tpu_custom_call" | custom-call | bytes 4194304 | tf_op jit(solution)/shard_map/merge_tail/pallas_call | solution.py:579
  35.4 1.4 %collective-permute-done.17.rest_1_ = bf16[656,128]{1,0:T(8,128)(2,1)S(1)} collective-permute-done((bf16[656,128]{1,0:T(8,128)(2,1)S(1)}, bf16[656,128]{1,0:T(8,128)(2,1)S(1)}, u32[]{:S(2)}, u32[]{:S(2)}) %collective-permute-start.17) | collective-permute-done | bytes 167968 | tf_op jit(solution)/shard_map/ppermute | solution.py:478
  36.8 1.5 %collective-permute-done.18.rest_2_ = bf16[656,128]{1,0:T(8,128)(2,1)S(1)} collective-permute-done((bf16[656,128]{1,0:T(8,128)(2,1)S(1)}, bf16[656,128]{1,0:T(8,128)(2,1)S(1)}, u32[]{:S(2)}, u32[]{:S(2)}) %collective-permute-start.18) | collective-permute-done | bytes 167968 | tf_op jit(solution)/shard_map/ppermute | solution.py:478
  38.3 1.3 %merge_first.1.rest_3_ = f32[4,640,128]{2,1,0:T(8,128)S(1)} custom-call(bf16[656,128]{1,0:T(8,128)(2,1)S(1)} %project.1.token_ref.rest_0_, bf16[656,128]{1,0:T(8,128)(2,1)S(1)} %collective-permute-done.17.rest_1_, bf16[656,128]{1,0:T(8,128)(2,1)S(1)} %collective-permute-done.18.rest_2_, bf16[640,5120]{1,0:T(8,128)(2,1)S(1)} %bitcast.1, ...), custom_call_target="tpu_custom_call" | custom-call | flops 1 | bytes 1 | tf_op jit(solution)/shard_map/merge_first/pallas_call | solution.py:590
  39.6 2.0 %collective-permute-done.22.rest_6_ = bf16[656,128]{1,0:T(8,128)(2,1)S(1)} collective-permute-done((bf16[656,128]{1,0:T(8,128)(2,1)S(1)}, bf16[656,128]{1,0:T(8,128)(2,1)S(1)}, u32[]{:S(2)}, u32[]{:S(2)}) %collective-permute-start.22) | collective-permute-done | bytes 167968 | tf_op jit(solution)/shard_map/ppermute | solution.py:478
  41.6 1.3 %merge_second.1.rest_8_ = f32[4,640,128]{2,1,0:T(8,128)S(1)} custom-call(bf16[656,128]{1,0:T(8,128)(2,1)S(1)} %collective-permute-done.19.rest_0_.rest_3_, bf16[656,128]{1,0:T(8,128)(2,1)S(1)} %collective-permute-done.20.rest_1_.rest_4_, bf16[656,128]{1,0:T(8,128)(2,1)S(1)} %collective-permute-done.21.rest_2_.rest_5_, ...), custom_call_target="tpu_custom_call" | custom-call | flops 1 | bytes 1 | tf_op jit(solution)/shard_map/merge_second/pallas_call | solution.py:594
  43.0 1.4 %merge.1 = bf16[1,640,128]{2,1,0:T(8,128)(2,1)} custom-call(bf16[656,128]{1,0:T(8,128)(2,1)S(1)} %project.1.token_ref.rest_0_, bf16[656,128]{1,0:T(8,128)(2,1)S(1)} %collective-permute-done.17.rest_1_, bf16[656,128]{1,0:T(8,128)(2,1)S(1)} %collective-permute-done.18.rest_2_, bf16[656,128]{1,0:T(8,128)(2,1)S(1)} %collective-permute-done.19.rest_0_.rest_3_, ...), custom_call_target="tpu_custom_call" | custom-call | flops 335544320 | bytes 8388608 | tf_op jit(solution)/shard_map/merge/pallas_call | solution.py:597
  (44 shorter events, 5.2 us)
Async XLA Ops:
  1.5 7.7 %collective-permute-start = (bf16[64,640]{1,0:T(8,128)(2,1)S(1)}, bf16[64,640]{1,0:T(8,128)(2,1)S(1)}, u32[]{:S(2)}, u32[]{:S(2)}) collective-permute-start(bf16[64,640]{1,0:T(8,128)(2,1)S(1)} %get-tuple-element.32), channel_id=1, source_target_pairs={{0,4},{1,3},{2,6},{3,1},{4,0},{5,7},{6,2},{7,5},{8,12},{9,11},{10,... | collective-permute-start | bytes 245768 | tf_op jit(solution)/shard_map/ppermute | solution.py:478
  4.6 5.1 %collective-permute-start.1 = (bf16[64,640]{1,0:T(8,128)(2,1)S(1)}, bf16[64,640]{1,0:T(8,128)(2,1)S(1)}, u32[]{:S(2)}, u32[]{:S(2)}) collective-permute-start(bf16[64,640]{1,0:T(8,128)(2,1)S(1)} %get-tuple-element.33), channel_id=1, source_target_pairs={{0,2},{1,5},{2,0},{3,7},{4,6},{5,1},{6,4},{7,3},{8,10},{9,13},{10,... | collective-permute-start | bytes 245768 | tf_op jit(solution)/shard_map/ppermute | solution.py:478
  6.1 6.2 %collective-permute-start.2 = (bf16[64,640]{1,0:T(8,128)(2,1)S(1)}, bf16[64,640]{1,0:T(8,128)(2,1)S(1)}, u32[]{:S(2)}, u32[]{:S(2)}) collective-permute-start(bf16[64,640]{1,0:T(8,128)(2,1)S(1)} %get-tuple-element.34), channel_id=1, source_target_pairs={{0,6},{1,7},{2,4},{3,5},{4,2},{5,3},{6,0},{7,1},{8,14},{9,15},{10,... | collective-permute-start | bytes 245768 | tf_op jit(solution)/shard_map/ppermute | solution.py:478
  6.1 7.9 %collective-permute-start.3 = (bf16[64,640]{1,0:T(8,128)(2,1)S(1)}, bf16[64,640]{1,0:T(8,128)(2,1)S(1)}, u32[]{:S(2)}, u32[]{:S(2)}) collective-permute-start(bf16[64,640]{1,0:T(8,128)(2,1)S(1)} %get-tuple-element.38), channel_id=1, source_target_pairs={{0,7},{1,6},{2,5},{3,4},{4,3},{5,2},{6,1},{7,0},{8,15},{9,14},{10,... | collective-permute-start | bytes 245768 | tf_op jit(solution)/shard_map/ppermute | solution.py:478
  7.6 6.7 %collective-permute-start.4 = (bf16[64,640]{1,0:T(8,128)(2,1)S(1)}, bf16[64,640]{1,0:T(8,128)(2,1)S(1)}, u32[]{:S(2)}, u32[]{:S(2)}) collective-permute-start(bf16[64,640]{1,0:T(8,128)(2,1)S(1)} %get-tuple-element.39), channel_id=1, source_target_pairs={{0,3},{1,4},{2,1},{3,6},{4,7},{5,0},{6,5},{7,2},{8,11},{9,12},{10,... | collective-permute-start | bytes 245768 | tf_op jit(solution)/shard_map/ppermute | solution.py:478
  9.3 5.0 %collective-permute-start.5 = (bf16[64,640]{1,0:T(8,128)(2,1)S(1)}, bf16[64,640]{1,0:T(8,128)(2,1)S(1)}, u32[]{:S(2)}, u32[]{:S(2)}) collective-permute-start(bf16[64,640]{1,0:T(8,128)(2,1)S(1)} %get-tuple-element.40), channel_id=1, source_target_pairs={{0,5},{1,2},{2,7},{3,0},{4,1},{5,6},{6,3},{7,4},{8,13},{9,10},{10,... | collective-permute-start | bytes 245768 | tf_op jit(solution)/shard_map/ppermute | solution.py:478
  9.6 4.7 %collective-permute-start.6 = (bf16[64,640]{1,0:T(8,128)(2,1)S(1)}, bf16[64,640]{1,0:T(8,128)(2,1)S(1)}, u32[]{:S(2)}, u32[]{:S(2)}) collective-permute-start(bf16[64,640]{1,0:T(8,128)(2,1)S(1)} %get-tuple-element.41), channel_id=1, source_target_pairs={{0,1},{1,0},{2,3},{3,2},{4,5},{5,4},{6,7},{7,6},{8,9},{9,8},{10,11... | collective-permute-start | bytes 245768 | tf_op jit(solution)/shard_map/ppermute | solution.py:478
  12.2 10.0 %collective-permute-start.10 = (bf16[800,128]{1,0:T(8,128)(2,1)S(1)}, bf16[800,128]{1,0:T(8,128)(2,1)S(1)}, u32[]{:S(2)}, u32[]{:S(2)}) collective-permute-start(bf16[800,128]{1,0:T(8,128)(2,1)S(1)} %get-tuple-element.44), channel_id=1, source_target_pairs={{0,8},{1,25},{2,10},{3,27},{4,12},{5,29},{6,14},{7,31},{8,16},{9,1... | collective-permute-start | bytes 614408 | tf_op jit(solution)/shard_map/ppermute | solution.py:487
  15.6 7.8 %collective-permute-start.13 = (bf16[640,128]{1,0:T(8,128)(2,1)S(1)}, bf16[640,128]{1,0:T(8,128)(2,1)S(1)}, u32[]{:S(2)}, u32[]{:S(2)}) collective-permute-start(bf16[640,128]{1,0:T(8,128)(2,1)S(1)} %attend.1.token_ref.rest_0_), channel_id=1, source_target_pairs={{0,4},{1,5},{2,6},{3,7},{4,0},{5,1},{6,2},{7,3},{8,12},{9,13},{10,... | collective-permute-start | bytes 491528 | tf_op jit(solution)/shard_map/ppermute | solution.py:478
  16.9 7.2 %collective-permute-start.15 = (bf16[640,128]{1,0:T(8,128)(2,1)S(1)}, bf16[640,128]{1,0:T(8,128)(2,1)S(1)}, u32[]{:S(2)}, u32[]{:S(2)}) collective-permute-start(bf16[640,128]{1,0:T(8,128)(2,1)S(1)} %attend.1.token_ref.rest_0_), channel_id=1, source_target_pairs={{0,2},{1,3},{2,0},{3,1},{4,6},{5,7},{6,4},{7,5},{8,10},{9,11},{10,... | collective-permute-start | bytes 491528 | tf_op jit(solution)/shard_map/ppermute | solution.py:478
  17.7 10.4 %collective-permute-start.7 = (bf16[640,128]{1,0:T(8,128)(2,1)S(1)}, bf16[640,128]{1,0:T(8,128)(2,1)S(1)}, u32[]{:S(2)}, u32[]{:S(2)}) collective-permute-start(bf16[640,128]{1,0:T(8,128)(2,1)S(1)} %attend.1.token_ref.rest_0_), channel_id=1, source_target_pairs={{0,6},{1,7},{2,4},{3,5},{4,2},{5,3},{6,0},{7,1},{8,14},{9,15},{10,... | collective-permute-start | bytes 491528 | tf_op jit(solution)/shard_map/ppermute | solution.py:478
  19.2 8.6 %collective-permute-start.9 = (bf16[400,128]{1,0:T(8,128)(2,1)S(1)}, bf16[400,128]{1,0:T(8,128)(2,1)S(1)}, u32[]{:S(2)}, u32[]{:S(2)}) collective-permute-start(bf16[400,128]{1,0:T(8,128)(2,1)S(1)} %get-tuple-element.43.rest_8_), channel_id=1, source_target_pairs={{0,16},{1,17},{2,18},{3,19},{4,20},{5,21},{6,22},{7,23},{8,24},{9,... | collective-permute-start | bytes 307208 | tf_op jit(solution)/shard_map/ppermute | solution.py:487
  22.2 5.5 %collective-permute-start.11 = (bf16[800,128]{1,0:T(8,128)(2,1)S(1)}, bf16[800,128]{1,0:T(8,128)(2,1)S(1)}, u32[]{:S(2)}, u32[]{:S(2)}) collective-permute-start(bf16[800,128]{1,0:T(8,128)(2,1)S(1)} %collective-permute-done.10.rest_9_), channel_id=1, source_target_pairs={{0,1},{1,0},{2,3},{3,2},{4,5},{5,4},{6,7},{7,6},{8,9},{9,8},{10,11... | collective-permute-start | bytes 614408 | tf_op jit(solution)/shard_map/ppermute | solution.py:478
  23.5 5.6 %collective-permute-start.14 = (bf16[640,128]{1,0:T(8,128)(2,1)S(1)}, bf16[640,128]{1,0:T(8,128)(2,1)S(1)}, u32[]{:S(2)}, u32[]{:S(2)}) collective-permute-start(bf16[640,128]{1,0:T(8,128)(2,1)S(1)} %collective-permute-done.13.rest_1_), channel_id=1, source_target_pairs={{0,1},{1,0},{2,3},{3,2},{4,5},{5,4},{6,7},{7,6},{8,9},{9,8},{10,11... | collective-permute-start | bytes 491528 | tf_op jit(solution)/shard_map/ppermute | solution.py:478
  24.1 5.0 %collective-permute-start.16 = (bf16[640,128]{1,0:T(8,128)(2,1)S(1)}, bf16[640,128]{1,0:T(8,128)(2,1)S(1)}, u32[]{:S(2)}, u32[]{:S(2)}) collective-permute-start(bf16[640,128]{1,0:T(8,128)(2,1)S(1)} %collective-permute-done.15.rest_2_), channel_id=1, source_target_pairs={{0,1},{1,0},{2,3},{3,2},{4,5},{5,4},{6,7},{7,6},{8,9},{9,8},{10,11... | collective-permute-start | bytes 491528 | tf_op jit(solution)/shard_map/ppermute | solution.py:478
  28.0 1.5 %collective-permute-start.12 = (bf16[640,128]{1,0:T(8,128)(2,1)S(1)}, bf16[640,128]{1,0:T(8,128)(2,1)S(1)}, u32[]{:S(2)}, u32[]{:S(2)}) collective-permute-start(bf16[640,128]{1,0:T(8,128)(2,1)S(1)} %attend.1.token_ref.rest_0_), channel_id=1, source_target_pairs={{0,1},{1,0},{2,3},{3,2},{4,5},{5,4},{6,7},{7,6},{8,9},{9,8},{10,11... | collective-permute-start | bytes 491528 | tf_op jit(solution)/shard_map/ppermute | solution.py:478
  28.1 1.8 %collective-permute-start.8 = (bf16[640,128]{1,0:T(8,128)(2,1)S(1)}, bf16[640,128]{1,0:T(8,128)(2,1)S(1)}, u32[]{:S(2)}, u32[]{:S(2)}) collective-permute-start(bf16[640,128]{1,0:T(8,128)(2,1)S(1)} %collective-permute-done.7.rest_0_), channel_id=1, source_target_pairs={{0,1},{1,0},{2,3},{3,2},{4,5},{5,4},{6,7},{7,6},{8,9},{9,8},{10,11... | collective-permute-start | bytes 491528 | tf_op jit(solution)/shard_map/ppermute | solution.py:478
  30.4 6.4 %collective-permute-start.17 = (bf16[656,128]{1,0:T(8,128)(2,1)S(1)}, bf16[656,128]{1,0:T(8,128)(2,1)S(1)}, u32[]{:S(2)}, u32[]{:S(2)}) collective-permute-start(bf16[656,128]{1,0:T(8,128)(2,1)S(1)} %project.1.token_ref.rest_0_), channel_id=1, source_target_pairs={{0,4},{1,5},{2,6},{3,7},{4,0},{5,1},{6,2},{7,3},{8,12},{9,13},{10,... | collective-permute-start | bytes 503816 | tf_op jit(solution)/shard_map/ppermute | solution.py:478
  31.1 7.2 %collective-permute-start.18 = (bf16[656,128]{1,0:T(8,128)(2,1)S(1)}, bf16[656,128]{1,0:T(8,128)(2,1)S(1)}, u32[]{:S(2)}, u32[]{:S(2)}) collective-permute-start(bf16[656,128]{1,0:T(8,128)(2,1)S(1)} %project.1.token_ref.rest_0_), channel_id=1, source_target_pairs={{0,2},{1,3},{2,0},{3,1},{4,6},{5,7},{6,4},{7,5},{8,10},{9,11},{10,... | collective-permute-start | bytes 503816 | tf_op jit(solution)/shard_map/ppermute | solution.py:478
  32.0 9.6 %collective-permute-start.22 = (bf16[656,128]{1,0:T(8,128)(2,1)S(1)}, bf16[656,128]{1,0:T(8,128)(2,1)S(1)}, u32[]{:S(2)}, u32[]{:S(2)}) collective-permute-start(bf16[656,128]{1,0:T(8,128)(2,1)S(1)} %project.1.token_ref.rest_0_), channel_id=1, source_target_pairs={{0,6},{1,7},{2,4},{3,5},{4,2},{5,3},{6,0},{7,1},{8,14},{9,15},{10,... | collective-permute-start | bytes 503816 | tf_op jit(solution)/shard_map/ppermute | solution.py:478
  35.4 4.2 %collective-permute-start.19 = (bf16[656,128]{1,0:T(8,128)(2,1)S(1)}, bf16[656,128]{1,0:T(8,128)(2,1)S(1)}, u32[]{:S(2)}, u32[]{:S(2)}) collective-permute-start(bf16[656,128]{1,0:T(8,128)(2,1)S(1)} %project.1.token_ref.rest_0_), channel_id=1, source_target_pairs={{0,1},{1,0},{2,3},{3,2},{4,5},{5,4},{6,7},{7,6},{8,9},{9,8},{10,11... | collective-permute-start | bytes 503816 | tf_op jit(solution)/shard_map/ppermute | solution.py:478
  36.8 4.8 %collective-permute-start.20 = (bf16[656,128]{1,0:T(8,128)(2,1)S(1)}, bf16[656,128]{1,0:T(8,128)(2,1)S(1)}, u32[]{:S(2)}, u32[]{:S(2)}) collective-permute-start(bf16[656,128]{1,0:T(8,128)(2,1)S(1)} %collective-permute-done.17.rest_1_), channel_id=1, source_target_pairs={{0,1},{1,0},{2,3},{3,2},{4,5},{5,4},{6,7},{7,6},{8,9},{9,8},{10,11... | collective-permute-start | bytes 503816 | tf_op jit(solution)/shard_map/ppermute | solution.py:478
  38.3 3.3 %collective-permute-start.21 = (bf16[656,128]{1,0:T(8,128)(2,1)S(1)}, bf16[656,128]{1,0:T(8,128)(2,1)S(1)}, u32[]{:S(2)}, u32[]{:S(2)}) collective-permute-start(bf16[656,128]{1,0:T(8,128)(2,1)S(1)} %collective-permute-done.18.rest_2_), channel_id=1, source_target_pairs={{0,1},{1,0},{2,3},{3,2},{4,5},{5,4},{6,7},{7,6},{8,9},{9,8},{10,11... | collective-permute-start | bytes 503816 | tf_op jit(solution)/shard_map/ppermute | solution.py:478
  41.6 1.4 %collective-permute-start.23 = (bf16[656,128]{1,0:T(8,128)(2,1)S(1)}, bf16[656,128]{1,0:T(8,128)(2,1)S(1)}, u32[]{:S(2)}, u32[]{:S(2)}) collective-permute-start(bf16[656,128]{1,0:T(8,128)(2,1)S(1)} %collective-permute-done.22.rest_6_), channel_id=1, source_target_pairs={{0,1},{1,0},{2,3},{3,2},{4,5},{5,4},{6,7},{7,6},{8,9},{9,8},{10,11... | collective-permute-start | bytes 503816 | tf_op jit(solution)/shard_map/ppermute | solution.py:478
  (3 other events, 11.4 us)

commit v19 on v18

--- a/solution.py
+++ b/solution.py
@@ -421,7 +421,7 @@
 
 def merge_kernel(*rest):
     pieces = rest[:ROWS]
-    before_ref, weight_ref, tail_ref, bias_ref, live_ref, out_ref = rest[ROWS:]
+    before_ref, weight_ref, tail_ref, bias_ref, live_ref, out_hbm, held, sems = rest[ROWS:]
     me = row_index()
     groups = live_ref.shape[1]
     patches = 4 * groups
@@ -434,22 +434,31 @@
     scale = lax.rsqrt((notes[:4] + notes[4:8]) * (1.0 / D) + 1e-06)
     spread = jnp.concatenate([jnp.broadcast_to(scale[at : at + 1], (REST, groups)) for at in range(4)], axis=0).T
     ends = rows[patches : patches + groups].astype(F32) * jnp.concatenate([spread] * 2, axis=1)
-    total = bias_ref[...] + lax.dot_general(
-        tail_ref[:, pl.ds(block, 2 * WIDE)], ends.astype(BF16), contract, preferred_element_type=F32
-    )
-    for corner in range(4):
-        part = before_ref[corner] + lax.dot_general(
-            weight_ref[:, pl.ds(pl.multiple_of(corner * D + block, 2 * WIDE), 2 * WIDE)],
-            rows[corner * groups : (corner + 1) * groups],
-            contract,
-            preferred_element_type=F32,
+    ends = ends.astype(BF16)
+    half = held.shape[0] // 2
+    copies = []
+    for at in range(2):
+        units = slice(at * half, (at + 1) * half)
+        total = bias_ref[units, :] + lax.dot_general(
+            tail_ref[units, pl.ds(block, 2 * WIDE)], ends, contract, preferred_element_type=F32
         )
-        total = total + scale[corner : corner + 1] * part
-    merged = 0.5 * total * (1.0 + lax.erf(total * math.sqrt(0.5)))
-    out_ref[0] = jnp.where(live_ref[...] > 0.0, merged, 0.0).astype(BF16)
-
-
-def kernel(body, name, out_shape, scratch=(), fetched=(), count=0, limit=24, flops=0, moved=0):
+        for corner in range(4):
+            part = before_ref[corner, units] + lax.dot_general(
+                weight_ref[units, pl.ds(pl.multiple_of(corner * D + block, 2 * WIDE), 2 * WIDE)],
+                rows[corner * groups : (corner + 1) * groups],
+                contract,
+                preferred_element_type=F32,
+            )
+            total = total + scale[corner : corner + 1] * part
+        merged = 0.5 * total * (1.0 + lax.erf(total * math.sqrt(0.5)))
+        held[units, :] = jnp.where(live_ref[...] > 0.0, merged, 0.0).astype(BF16)
+        copies.append(pltpu.make_async_copy(held.at[units], out_hbm.at[0, units], sems.at[at]))
+        copies[at].start()
+    for copy in copies:
+        copy.wait()
+
+
+def kernel(body, name, out_shape, scratch=(), fetched=(), count=0, limit=24, flops=0, moved=0, out=pltpu.VMEM):
     specs = [pl.BlockSpec(memory_space=pltpu.VMEM) for _ in range(count)]
     for at in fetched:
         specs[at] = pl.BlockSpec(memory_space=pl.ANY)
@@ -457,7 +466,7 @@
         body,
         out_shape=out_shape,
         in_specs=specs,
-        out_specs=jax.tree.map(lambda _: pl.BlockSpec(memory_space=pltpu.VMEM), out_shape),
+        out_specs=jax.tree.map(lambda _: pl.BlockSpec(memory_space=out), out_shape),
         scratch_shapes=list(scratch),
         compiler_params=pltpu.CompilerParams(vmem_limit_bytes=limit * 1024 * 1024),
         cost_estimate=pl.CostEstimate(flops=flops, bytes_accessed=moved, transcendentals=0),
@@ -598,6 +607,8 @@
         merge_kernel,
         "merge",
         shape(1, units, groups),
+        [pltpu.VMEM((units, groups), BF16), pltpu.SemaphoreType.DMA((2,))],
+        out=pl.ANY,
         count=ROWS + 5,
         flops=4 * units * groups * MAIN,
         moved=8 << 20,

time: 44.6 us -> 44.6 us (level)
  no operation moved by 1% of the time
where the time goes in v19:
time: 44.6 us; the launch traced here: 44.4 us
  starting transfers between devices  22.1 us (50%)
  Pallas kernels  11.4 us (26%)
  waiting for transfers between devices  9.55 us (21%)
  local copies, waits for them, and re-layouts  1.16 us (3%)
    ppermute x22, starting transfers between devices, swap(): lax.ppermute(value, 'row', [(row, row ^ (odd if row % 2 else even)) for r...  17.4 us
    ppermute x22, waiting for transfers between devices, swap(): lax.ppermute(value, 'row', [(row, row ^ (odd if row % 2 else even)) for r...  5.92 us
    ppermute x2, starting transfers between devices, turn(): return lax.ppermute(value, ('page', 'row'), pairs)  4.66 us
    ppermute x2, waiting for transfers between devices, turn(): return lax.ppermute(value, ('page', 'row'), pairs)  3.63 us
    pallas_call x1, Pallas kernels, local_eight(): kernel(spread_kernel, 'spread', [shape(band, 4 * HPAIR)] * ROWS + [shape(...  1.54 us
    pallas_call x1, Pallas kernels, local_eight(): kernel(tail_kernel, 'merge_tail', [shape(units, MAIN), shape(units, 1, dt...  1.39 us
    pallas_call x1, Pallas kernels, local_eight(): kernel(merge_kernel, 'merge', shape(1, units, groups), [pltpu.VMEM((units...  1.36 us
    pallas_call x1, Pallas kernels, local_eight(): kernel(attend_kernel, 'attend', shape(piece, WIDE), [pltpu.VMEM((patches,...  1.34 us
  transfers between devices with their start and end apart: 24, of which 8 were waited for; matrix products, arithmetic and copies ran while one was open for 0% of the time, Pallas kernels for 18%

profile of v19, /device:TPU:0, one launch (start us, length us, event | category | flops | bytes accessed | tf_op | source)
XLA Modules:
  0.0 44.4 jit_solution(768833056263293922)
XLA Ops:
  0.0 1.5 %spread.1 = (bf16[64,640]{1,0:T(8,128)(2,1)S(1)}, bf16[64,640]{1,0:T(8,128)(2,1)S(1)}, bf16[64,640]{1,0:T(8,128)(2,1)S(1)}, bf16[64,640]{1,0:T(8,128)(2,1)S(1)},...) custom-call(bf16[1,64,3840]{2,1,0:T(8,128)(2,1)} %qkv_hbm.1, ...), custom_call_target="tpu_custom_call" | custom-call | bytes 1048576 | tf_op jit(solution)/shard_map/spread/pallas_call | solution.py:512
  1.5 3.0 %collective-permute-start = (bf16[64,640]{1,0:T(8,128)(2,1)S(1)}, bf16[64,640]{1,0:T(8,128)(2,1)S(1)}, u32[]{:S(2)}, u32[]{:S(2)}) collective-permute-start(bf16[64,640]{1,0:T(8,128)(2,1)S(1)} %get-tuple-element.32), channel_id=1, source_target_pairs={{0,4},{1,3},{2,6},{3,1},{4,0},{5,7},{6,2},{7,5},{8,12},{9,11},{10,... | collective-permute-start | bytes 245768 | tf_op jit(solution)/shard_map/ppermute | solution.py:487
  4.6 1.5 %collective-permute-start.1 = (bf16[64,640]{1,0:T(8,128)(2,1)S(1)}, bf16[64,640]{1,0:T(8,128)(2,1)S(1)}, u32[]{:S(2)}, u32[]{:S(2)}) collective-permute-start(bf16[64,640]{1,0:T(8,128)(2,1)S(1)} %get-tuple-element.33), channel_id=1, source_target_pairs={{0,2},{1,5},{2,0},{3,7},{4,6},{5,1},{6,4},{7,3},{8,10},{9,13},{10,... | collective-permute-start | bytes 245768 | tf_op jit(solution)/shard_map/ppermute | solution.py:487
  6.1 1.5 %collective-permute-start.3 = (bf16[64,640]{1,0:T(8,128)(2,1)S(1)}, bf16[64,640]{1,0:T(8,128)(2,1)S(1)}, u32[]{:S(2)}, u32[]{:S(2)}) collective-permute-start(bf16[64,640]{1,0:T(8,128)(2,1)S(1)} %get-tuple-element.38), channel_id=1, source_target_pairs={{0,7},{1,6},{2,5},{3,4},{4,3},{5,2},{6,1},{7,0},{8,15},{9,14},{10,... | collective-permute-start | bytes 245768 | tf_op jit(solution)/shard_map/ppermute | solution.py:487
  7.6 1.7 %collective-permute-start.4 = (bf16[64,640]{1,0:T(8,128)(2,1)S(1)}, bf16[64,640]{1,0:T(8,128)(2,1)S(1)}, u32[]{:S(2)}, u32[]{:S(2)}) collective-permute-start(bf16[64,640]{1,0:T(8,128)(2,1)S(1)} %get-tuple-element.39), channel_id=1, source_target_pairs={{0,3},{1,4},{2,1},{3,6},{4,7},{5,0},{6,5},{7,2},{8,11},{9,12},{10,... | collective-permute-start | bytes 245768 | tf_op jit(solution)/shard_map/ppermute | solution.py:487
  9.6 1.2 %collective-permute-start.6 = (bf16[64,640]{1,0:T(8,128)(2,1)S(1)}, bf16[64,640]{1,0:T(8,128)(2,1)S(1)}, u32[]{:S(2)}, u32[]{:S(2)}) collective-permute-start(bf16[64,640]{1,0:T(8,128)(2,1)S(1)} %get-tuple-element.41), channel_id=1, source_target_pairs={{0,1},{1,0},{2,3},{3,2},{4,5},{5,4},{6,7},{7,6},{8,9},{9,8},{10,11... | collective-permute-start | bytes 245768 | tf_op jit(solution)/shard_map/ppermute | solution.py:487
  10.9 1.1 %copy-done = bf16[320,1280]{1,0:T(8,128)(2,1)S(1)} copy-done((bf16[320,1280]{1,0:T(8,128)(2,1)S(1)}, bf16[320,1280]{1,0:T(8,128)(2,1)}, u32[]{:S(2)}) %copy-start) | copy-done | bytes 819224
  12.2 1.6 %collective-permute-start.10 = (bf16[800,128]{1,0:T(8,128)(2,1)S(1)}, bf16[800,128]{1,0:T(8,128)(2,1)S(1)}, u32[]{:S(2)}, u32[]{:S(2)}) collective-permute-start(bf16[800,128]{1,0:T(8,128)(2,1)S(1)} %get-tuple-element.44), channel_id=1, source_target_pairs={{0,8},{1,25},{2,10},{3,27},{4,12},{5,29},{6,14},{7,31},{8,16},{9,1... | collective-permute-start | bytes 614408 | tf_op jit(solution)/shard_map/ppermute | solution.py:496
  14.3 1.3 %attend.1.token_ref.rest_0_ = bf16[640,128]{1,0:T(8,128)(2,1)S(1)} custom-call(bf16[512,512]{1,0:T(8,128)(2,1)S(1)} %get-tuple-element.35.select_ref, f32[1,512]{1,0:T(1,128)S(1)} %get-tuple-element.36.dead_ref, bf16[64,640]{1,0:T(8,128)(2,1)S(1)} %get-tuple-element.37.rest_0_, bf16[64,640]{1,0:T(8,128)(2,1)S(1)} %collective-permute-done.rest_0_.rest_1_, ...), custom_call_target="tpu_custom_call" | custom-call | flops 21474836480 | bytes 1048576 | tf_op jit(solution)/shard_map/attend/pallas_call | solution.py:546
  15.6 1.2 %collective-permute-start.13 = (bf16[640,128]{1,0:T(8,128)(2,1)S(1)}, bf16[640,128]{1,0:T(8,128)(2,1)S(1)}, u32[]{:S(2)}, u32[]{:S(2)}) collective-permute-start(bf16[640,128]{1,0:T(8,128)(2,1)S(1)} %attend.1.token_ref.rest_0_), channel_id=1, source_target_pairs={{0,4},{1,5},{2,6},{3,7},{4,0},{5,1},{6,2},{7,3},{8,12},{9,13},{10,... | collective-permute-start | bytes 491528 | tf_op jit(solution)/shard_map/ppermute | solution.py:487
  16.9 0.8 %collective-permute-start.15 = (bf16[640,128]{1,0:T(8,128)(2,1)S(1)}, bf16[640,128]{1,0:T(8,128)(2,1)S(1)}, u32[]{:S(2)}, u32[]{:S(2)}) collective-permute-start(bf16[640,128]{1,0:T(8,128)(2,1)S(1)} %attend.1.token_ref.rest_0_), channel_id=1, source_target_pairs={{0,2},{1,3},{2,0},{3,1},{4,6},{5,7},{6,4},{7,5},{8,10},{9,11},{10,... | collective-permute-start | bytes 491528 | tf_op jit(solution)/shard_map/ppermute | solution.py:487
  17.7 1.5 %collective-permute-start.7 = (bf16[640,128]{1,0:T(8,128)(2,1)S(1)}, bf16[640,128]{1,0:T(8,128)(2,1)S(1)}, u32[]{:S(2)}, u32[]{:S(2)}) collective-permute-start(bf16[640,128]{1,0:T(8,128)(2,1)S(1)} %attend.1.token_ref.rest_0_), channel_id=1, source_target_pairs={{0,6},{1,7},{2,4},{3,5},{4,2},{5,3},{6,0},{7,1},{8,14},{9,15},{10,... | collective-permute-start | bytes 491528 | tf_op jit(solution)/shard_map/ppermute | solution.py:487
  19.2 3.0 %collective-permute-start.9 = (bf16[400,128]{1,0:T(8,128)(2,1)S(1)}, bf16[400,128]{1,0:T(8,128)(2,1)S(1)}, u32[]{:S(2)}, u32[]{:S(2)}) collective-permute-start(bf16[400,128]{1,0:T(8,128)(2,1)S(1)} %get-tuple-element.43.rest_8_), channel_id=1, source_target_pairs={{0,16},{1,17},{2,18},{3,19},{4,20},{5,21},{6,22},{7,23},{8,24},{9,... | collective-permute-start | bytes 307208 | tf_op jit(solution)/shard_map/ppermute | solution.py:496
  22.2 1.2 %ready.1 = (f32[512,160]{1,0:T(8,128)S(1)}, f32[1,160]{1,0:T(1,128)S(1)}, bf16[1024,160]{1,0:T(8,128)(2,1)S(1)}, bf16[4,1024,160]{2,1,0:T(8,128)(2,1)S(1)}) custom-call(bf16[512,512]{1,0:T(8,128)(2,1)S(1)} %get-tuple-element.35.select_ref, f32[1280]{0:T(1024)} %gain_hbm.1, bf16[640,128]{1,0:T(8,128)(2,1)S(1)} %attend.1.token_ref.rest_0_, ...), custom_call_target="tpu_custom_call" | custom-call | flops 10737418240 | bytes 4194304 | tf_op jit(solution)/shard_map/ready/pallas_call | solution.py:556
  24.1 3.6 %collective-permute-done.9.across_ref = bf16[400,128]{1,0:T(8,128)(2,1)S(1)} collective-permute-done((bf16[400,128]{1,0:T(8,128)(2,1)S(1)}, bf16[400,128]{1,0:T(8,128)(2,1)S(1)}, u32[]{:S(2)}, u32[]{:S(2)}) %collective-permute-start.9) | collective-permute-done | bytes 102432 | tf_op jit(solution)/shard_map/ppermute | solution.py:496
  31.1 0.9 %collective-permute-start.18 = (bf16[656,128]{1,0:T(8,128)(2,1)S(1)}, bf16[656,128]{1,0:T(8,128)(2,1)S(1)}, u32[]{:S(2)}, u32[]{:S(2)}) collective-permute-start(bf16[656,128]{1,0:T(8,128)(2,1)S(1)} %project.1.token_ref.rest_0_), channel_id=1, source_target_pairs={{0,2},{1,3},{2,0},{3,1},{4,6},{5,7},{6,4},{7,5},{8,10},{9,11},{10,... | collective-permute-start | bytes 503816 | tf_op jit(solution)/shard_map/ppermute | solution.py:487
  32.0 1.9 %collective-permute-start.22 = (bf16[656,128]{1,0:T(8,128)(2,1)S(1)}, bf16[656,128]{1,0:T(8,128)(2,1)S(1)}, u32[]{:S(2)}, u32[]{:S(2)}) collective-permute-start(bf16[656,128]{1,0:T(8,128)(2,1)S(1)} %project.1.token_ref.rest_0_), channel_id=1, source_target_pairs={{0,6},{1,7},{2,4},{3,5},{4,2},{5,3},{6,0},{7,1},{8,14},{9,15},{10,... | collective-permute-start | bytes 503816 | tf_op jit(solution)/shard_map/ppermute | solution.py:487
  34.0 1.4 %merge_tail.1 = (bf16[640,1024]{1,0:T(8,128)(2,1)S(1)}, f32[640,1]{1,0:T(8,128)S(1)}) custom-call(bf16[640,5120]{1,0:T(8,128)(2,1)S(1)} %bitcast.1, f32[640]{0:T(1024)} %bias_hbm.1, bf16[656,128]{1,0:T(8,128)(2,1)S(1)} %project.1.token_ref.rest_0_), custom_call_target="tpu_custom_call" | custom-call | bytes 4194304 | tf_op jit(solution)/shard_map/merge_tail/pallas_call | solution.py:588
  35.4 1.4 %collective-permute-done.17.rest_1_ = bf16[656,128]{1,0:T(8,128)(2,1)S(1)} collective-permute-done((bf16[656,128]{1,0:T(8,128)(2,1)S(1)}, bf16[656,128]{1,0:T(8,128)(2,1)S(1)}, u32[]{:S(2)}, u32[]{:S(2)}) %collective-permute-start.17) | collective-permute-done | bytes 167968 | tf_op jit(solution)/shard_map/ppermute | solution.py:487
  36.8 1.5 %collective-permute-done.18.rest_2_ = bf16[656,128]{1,0:T(8,128)(2,1)S(1)} collective-permute-done((bf16[656,128]{1,0:T(8,128)(2,1)S(1)}, bf16[656,128]{1,0:T(8,128)(2,1)S(1)}, u32[]{:S(2)}, u32[]{:S(2)}) %collective-permute-start.18) | collective-permute-done | bytes 167968 | tf_op jit(solution)/shard_map/ppermute | solution.py:487
  38.3 1.3 %merge_first.1.rest_3_ = f32[4,640,128]{2,1,0:T(8,128)S(1)} custom-call(bf16[656,128]{1,0:T(8,128)(2,1)S(1)} %project.1.token_ref.rest_0_, bf16[656,128]{1,0:T(8,128)(2,1)S(1)} %collective-permute-done.17.rest_1_, bf16[656,128]{1,0:T(8,128)(2,1)S(1)} %collective-permute-done.18.rest_2_, bf16[640,5120]{1,0:T(8,128)(2,1)S(1)} %bitcast.1, ...), custom_call_target="tpu_custom_call" | custom-call | flops 1 | bytes 1 | tf_op jit(solution)/shard_map/merge_first/pallas_call | solution.py:599
  39.6 2.0 %collective-permute-done.22.rest_6_ = bf16[656,128]{1,0:T(8,128)(2,1)S(1)} collective-permute-done((bf16[656,128]{1,0:T(8,128)(2,1)S(1)}, bf16[656,128]{1,0:T(8,128)(2,1)S(1)}, u32[]{:S(2)}, u32[]{:S(2)}) %collective-permute-start.22) | collective-permute-done | bytes 167968 | tf_op jit(solution)/shard_map/ppermute | solution.py:487
  41.6 1.3 %merge_second.1.rest_8_ = f32[4,640,128]{2,1,0:T(8,128)S(1)} custom-call(bf16[656,128]{1,0:T(8,128)(2,1)S(1)} %collective-permute-done.19.rest_0_.rest_3_, bf16[656,128]{1,0:T(8,128)(2,1)S(1)} %collective-permute-done.20.rest_1_.rest_4_, bf16[656,128]{1,0:T(8,128)(2,1)S(1)} %collective-permute-done.21.rest_2_.rest_5_, ...), custom_call_target="tpu_custom_call" | custom-call | flops 1 | bytes 1 | tf_op jit(solution)/shard_map/merge_second/pallas_call | solution.py:603
  43.0 1.4 %merge.1 = bf16[1,640,128]{2,1,0:T(8,128)(2,1)} custom-call(bf16[656,128]{1,0:T(8,128)(2,1)S(1)} %project.1.token_ref.rest_0_, bf16[656,128]{1,0:T(8,128)(2,1)S(1)} %collective-permute-done.17.rest_1_, bf16[656,128]{1,0:T(8,128)(2,1)S(1)} %collective-permute-done.18.rest_2_, bf16[656,128]{1,0:T(8,128)(2,1)S(1)} %collective-permute-done.19.rest_0_.rest_3_, ...), custom_call_target="tpu_custom_call" | custom-call | flops 335544320 | bytes 8388608 | tf_op jit(solution)/shard_map/merge/pallas_call | solution.py:606
  (44 shorter events, 5.2 us)
Async XLA Ops:
  1.5 7.7 %collective-permute-start = (bf16[64,640]{1,0:T(8,128)(2,1)S(1)}, bf16[64,640]{1,0:T(8,128)(2,1)S(1)}, u32[]{:S(2)}, u32[]{:S(2)}) collective-permute-start(bf16[64,640]{1,0:T(8,128)(2,1)S(1)} %get-tuple-element.32), channel_id=1, source_target_pairs={{0,4},{1,3},{2,6},{3,1},{4,0},{5,7},{6,2},{7,5},{8,12},{9,11},{10,... | collective-permute-start | bytes 245768 | tf_op jit(solution)/shard_map/ppermute | solution.py:487
  4.6 5.1 %collective-permute-start.1 = (bf16[64,640]{1,0:T(8,128)(2,1)S(1)}, bf16[64,640]{1,0:T(8,128)(2,1)S(1)}, u32[]{:S(2)}, u32[]{:S(2)}) collective-permute-start(bf16[64,640]{1,0:T(8,128)(2,1)S(1)} %get-tuple-element.33), channel_id=1, source_target_pairs={{0,2},{1,5},{2,0},{3,7},{4,6},{5,1},{6,4},{7,3},{8,10},{9,13},{10,... | collective-permute-start | bytes 245768 | tf_op jit(solution)/shard_map/ppermute | solution.py:487
  6.1 6.2 %collective-permute-start.2 = (bf16[64,640]{1,0:T(8,128)(2,1)S(1)}, bf16[64,640]{1,0:T(8,128)(2,1)S(1)}, u32[]{:S(2)}, u32[]{:S(2)}) collective-permute-start(bf16[64,640]{1,0:T(8,128)(2,1)S(1)} %get-tuple-element.34), channel_id=1, source_target_pairs={{0,6},{1,7},{2,4},{3,5},{4,2},{5,3},{6,0},{7,1},{8,14},{9,15},{10,... | collective-permute-start | bytes 245768 | tf_op jit(solution)/shard_map/ppermute | solution.py:487
  6.1 7.9 %collective-permute-start.3 = (bf16[64,640]{1,0:T(8,128)(2,1)S(1)}, bf16[64,640]{1,0:T(8,128)(2,1)S(1)}, u32[]{:S(2)}, u32[]{:S(2)}) collective-permute-start(bf16[64,640]{1,0:T(8,128)(2,1)S(1)} %get-tuple-element.38), channel_id=1, source_target_pairs={{0,7},{1,6},{2,5},{3,4},{4,3},{5,2},{6,1},{7,0},{8,15},{9,14},{10,... | collective-permute-start | bytes 245768 | tf_op jit(solution)/shard_map/ppermute | solution.py:487
  7.6 6.7 %collective-permute-start.4 = (bf16[64,640]{1,0:T(8,128)(2,1)S(1)}, bf16[64,640]{1,0:T(8,128)(2,1)S(1)}, u32[]{:S(2)}, u32[]{:S(2)}) collective-permute-start(bf16[64,640]{1,0:T(8,128)(2,1)S(1)} %get-tuple-element.39), channel_id=1, source_target_pairs={{0,3},{1,4},{2,1},{3,6},{4,7},{5,0},{6,5},{7,2},{8,11},{9,12},{10,... | collective-permute-start | bytes 245768 | tf_op jit(solution)/shard_map/ppermute | solution.py:487
  9.3 5.0 %collective-permute-start.5 = (bf16[64,640]{1,0:T(8,128)(2,1)S(1)}, bf16[64,640]{1,0:T(8,128)(2,1)S(1)}, u32[]{:S(2)}, u32[]{:S(2)}) collective-permute-start(bf16[64,640]{1,0:T(8,128)(2,1)S(1)} %get-tuple-element.40), channel_id=1, source_target_pairs={{0,5},{1,2},{2,7},{3,0},{4,1},{5,6},{6,3},{7,4},{8,13},{9,10},{10,... | collective-permute-start | bytes 245768 | tf_op jit(solution)/shard_map/ppermute | solution.py:487
  9.6 4.7 %collective-permute-start.6 = (bf16[64,640]{1,0:T(8,128)(2,1)S(1)}, bf16[64,640]{1,0:T(8,128)(2,1)S(1)}, u32[]{:S(2)}, u32[]{:S(2)}) collective-permute-start(bf16[64,640]{1,0:T(8,128)(2,1)S(1)} %get-tuple-element.41), channel_id=1, source_target_pairs={{0,1},{1,0},{2,3},{3,2},{4,5},{5,4},{6,7},{7,6},{8,9},{9,8},{10,11... | collective-permute-start | bytes 245768 | tf_op jit(solution)/shard_map/ppermute | solution.py:487
  12.2 10.0 %collective-permute-start.10 = (bf16[800,128]{1,0:T(8,128)(2,1)S(1)}, bf16[800,128]{1,0:T(8,128)(2,1)S(1)}, u32[]{:S(2)}, u32[]{:S(2)}) collective-permute-start(bf16[800,128]{1,0:T(8,128)(2,1)S(1)} %get-tuple-element.44), channel_id=1, source_target_pairs={{0,8},{1,25},{2,10},{3,27},{4,12},{5,29},{6,14},{7,31},{8,16},{9,1... | collective-permute-start | bytes 614408 | tf_op jit(solution)/shard_map/ppermute | solution.py:496
  15.6 7.8 %collective-permute-start.13 = (bf16[640,128]{1,0:T(8,128)(2,1)S(1)}, bf16[640,128]{1,0:T(8,128)(2,1)S(1)}, u32[]{:S(2)}, u32[]{:S(2)}) collective-permute-start(bf16[640,128]{1,0:T(8,128)(2,1)S(1)} %attend.1.token_ref.rest_0_), channel_id=1, source_target_pairs={{0,4},{1,5},{2,6},{3,7},{4,0},{5,1},{6,2},{7,3},{8,12},{9,13},{10,... | collective-permute-start | bytes 491528 | tf_op jit(solution)/shard_map/ppermute | solution.py:487
  16.9 7.2 %collective-permute-start.15 = (bf16[640,128]{1,0:T(8,128)(2,1)S(1)}, bf16[640,128]{1,0:T(8,128)(2,1)S(1)}, u32[]{:S(2)}, u32[]{:S(2)}) collective-permute-start(bf16[640,128]{1,0:T(8,128)(2,1)S(1)} %attend.1.token_ref.rest_0_), channel_id=1, source_target_pairs={{0,2},{1,3},{2,0},{3,1},{4,6},{5,7},{6,4},{7,5},{8,10},{9,11},{10,... | collective-permute-start | bytes 491528 | tf_op jit(solution)/shard_map/ppermute | solution.py:487
  17.7 10.4 %collective-permute-start.7 = (bf16[640,128]{1,0:T(8,128)(2,1)S(1)}, bf16[640,128]{1,0:T(8,128)(2,1)S(1)}, u32[]{:S(2)}, u32[]{:S(2)}) collective-permute-start(bf16[640,128]{1,0:T(8,128)(2,1)S(1)} %attend.1.token_ref.rest_0_), channel_id=1, source_target_pairs={{0,6},{1,7},{2,4},{3,5},{4,2},{5,3},{6,0},{7,1},{8,14},{9,15},{10,... | collective-permute-start | bytes 491528 | tf_op jit(solution)/shard_map/ppermute | solution.py:487
  19.2 8.6 %collective-permute-start.9 = (bf16[400,128]{1,0:T(8,128)(2,1)S(1)}, bf16[400,128]{1,0:T(8,128)(2,1)S(1)}, u32[]{:S(2)}, u32[]{:S(2)}) collective-permute-start(bf16[400,128]{1,0:T(8,128)(2,1)S(1)} %get-tuple-element.43.rest_8_), channel_id=1, source_target_pairs={{0,16},{1,17},{2,18},{3,19},{4,20},{5,21},{6,22},{7,23},{8,24},{9,... | collective-permute-start | bytes 307208 | tf_op jit(solution)/shard_map/ppermute | solution.py:496
  22.2 5.5 %collective-permute-start.11 = (bf16[800,128]{1,0:T(8,128)(2,1)S(1)}, bf16[800,128]{1,0:T(8,128)(2,1)S(1)}, u32[]{:S(2)}, u32[]{:S(2)}) collective-permute-start(bf16[800,128]{1,0:T(8,128)(2,1)S(1)} %collective-permute-done.10.rest_9_), channel_id=1, source_target_pairs={{0,1},{1,0},{2,3},{3,2},{4,5},{5,4},{6,7},{7,6},{8,9},{9,8},{10,11... | collective-permute-start | bytes 614408 | tf_op jit(solution)/shard_map/ppermute | solution.py:487
  23.5 5.6 %collective-permute-start.14 = (bf16[640,128]{1,0:T(8,128)(2,1)S(1)}, bf16[640,128]{1,0:T(8,128)(2,1)S(1)}, u32[]{:S(2)}, u32[]{:S(2)}) collective-permute-start(bf16[640,128]{1,0:T(8,128)(2,1)S(1)} %collective-permute-done.13.rest_1_), channel_id=1, source_target_pairs={{0,1},{1,0},{2,3},{3,2},{4,5},{5,4},{6,7},{7,6},{8,9},{9,8},{10,11... | collective-permute-start | bytes 491528 | tf_op jit(solution)/shard_map/ppermute | solution.py:487
  24.1 5.0 %collective-permute-start.16 = (bf16[640,128]{1,0:T(8,128)(2,1)S(1)}, bf16[640,128]{1,0:T(8,128)(2,1)S(1)}, u32[]{:S(2)}, u32[]{:S(2)}) collective-permute-start(bf16[640,128]{1,0:T(8,128)(2,1)S(1)} %collective-permute-done.15.rest_2_), channel_id=1, source_target_pairs={{0,1},{1,0},{2,3},{3,2},{4,5},{5,4},{6,7},{7,6},{8,9},{9,8},{10,11... | collective-permute-start | bytes 491528 | tf_op jit(solution)/shard_map/ppermute | solution.py:487
  28.0 1.5 %collective-permute-start.12 = (bf16[640,128]{1,0:T(8,128)(2,1)S(1)}, bf16[640,128]{1,0:T(8,128)(2,1)S(1)}, u32[]{:S(2)}, u32[]{:S(2)}) collective-permute-start(bf16[640,128]{1,0:T(8,128)(2,1)S(1)} %attend.1.token_ref.rest_0_), channel_id=1, source_target_pairs={{0,1},{1,0},{2,3},{3,2},{4,5},{5,4},{6,7},{7,6},{8,9},{9,8},{10,11... | collective-permute-start | bytes 491528 | tf_op jit(solution)/shard_map/ppermute | solution.py:487
  28.1 1.8 %collective-permute-start.8 = (bf16[640,128]{1,0:T(8,128)(2,1)S(1)}, bf16[640,128]{1,0:T(8,128)(2,1)S(1)}, u32[]{:S(2)}, u32[]{:S(2)}) collective-permute-start(bf16[640,128]{1,0:T(8,128)(2,1)S(1)} %collective-permute-done.7.rest_0_), channel_id=1, source_target_pairs={{0,1},{1,0},{2,3},{3,2},{4,5},{5,4},{6,7},{7,6},{8,9},{9,8},{10,11... | collective-permute-start | bytes 491528 | tf_op jit(solution)/shard_map/ppermute | solution.py:487
  30.4 6.4 %collective-permute-start.17 = (bf16[656,128]{1,0:T(8,128)(2,1)S(1)}, bf16[656,128]{1,0:T(8,128)(2,1)S(1)}, u32[]{:S(2)}, u32[]{:S(2)}) collective-permute-start(bf16[656,128]{1,0:T(8,128)(2,1)S(1)} %project.1.token_ref.rest_0_), channel_id=1, source_target_pairs={{0,4},{1,5},{2,6},{3,7},{4,0},{5,1},{6,2},{7,3},{8,12},{9,13},{10,... | collective-permute-start | bytes 503816 | tf_op jit(solution)/shard_map/ppermute | solution.py:487
  31.1 7.2 %collective-permute-start.18 = (bf16[656,128]{1,0:T(8,128)(2,1)S(1)}, bf16[656,128]{1,0:T(8,128)(2,1)S(1)}, u32[]{:S(2)}, u32[]{:S(2)}) collective-permute-start(bf16[656,128]{1,0:T(8,128)(2,1)S(1)} %project.1.token_ref.rest_0_), channel_id=1, source_target_pairs={{0,2},{1,3},{2,0},{3,1},{4,6},{5,7},{6,4},{7,5},{8,10},{9,11},{10,... | collective-permute-start | bytes 503816 | tf_op jit(solution)/shard_map/ppermute | solution.py:487
  32.0 9.6 %collective-permute-start.22 = (bf16[656,128]{1,0:T(8,128)(2,1)S(1)}, bf16[656,128]{1,0:T(8,128)(2,1)S(1)}, u32[]{:S(2)}, u32[]{:S(2)}) collective-permute-start(bf16[656,128]{1,0:T(8,128)(2,1)S(1)} %project.1.token_ref.rest_0_), channel_id=1, source_target_pairs={{0,6},{1,7},{2,4},{3,5},{4,2},{5,3},{6,0},{7,1},{8,14},{9,15},{10,... | collective-permute-start | bytes 503816 | tf_op jit(solution)/shard_map/ppermute | solution.py:487
  35.4 4.2 %collective-permute-start.19 = (bf16[656,128]{1,0:T(8,128)(2,1)S(1)}, bf16[656,128]{1,0:T(8,128)(2,1)S(1)}, u32[]{:S(2)}, u32[]{:S(2)}) collective-permute-start(bf16[656,128]{1,0:T(8,128)(2,1)S(1)} %project.1.token_ref.rest_0_), channel_id=1, source_target_pairs={{0,1},{1,0},{2,3},{3,2},{4,5},{5,4},{6,7},{7,6},{8,9},{9,8},{10,11... | collective-permute-start | bytes 503816 | tf_op jit(solution)/shard_map/ppermute | solution.py:487
  36.8 4.8 %collective-permute-start.20 = (bf16[656,128]{1,0:T(8,128)(2,1)S(1)}, bf16[656,128]{1,0:T(8,128)(2,1)S(1)}, u32[]{:S(2)}, u32[]{:S(2)}) collective-permute-start(bf16[656,128]{1,0:T(8,128)(2,1)S(1)} %collective-permute-done.17.rest_1_), channel_id=1, source_target_pairs={{0,1},{1,0},{2,3},{3,2},{4,5},{5,4},{6,7},{7,6},{8,9},{9,8},{10,11... | collective-permute-start | bytes 503816 | tf_op jit(solution)/shard_map/ppermute | solution.py:487
  38.3 3.3 %collective-permute-start.21 = (bf16[656,128]{1,0:T(8,128)(2,1)S(1)}, bf16[656,128]{1,0:T(8,128)(2,1)S(1)}, u32[]{:S(2)}, u32[]{:S(2)}) collective-permute-start(bf16[656,128]{1,0:T(8,128)(2,1)S(1)} %collective-permute-done.18.rest_2_), channel_id=1, source_target_pairs={{0,1},{1,0},{2,3},{3,2},{4,5},{5,4},{6,7},{7,6},{8,9},{9,8},{10,11... | collective-permute-start | bytes 503816 | tf_op jit(solution)/shard_map/ppermute | solution.py:487
  41.6 1.4 %collective-permute-start.23 = (bf16[656,128]{1,0:T(8,128)(2,1)S(1)}, bf16[656,128]{1,0:T(8,128)(2,1)S(1)}, u32[]{:S(2)}, u32[]{:S(2)}) collective-permute-start(bf16[656,128]{1,0:T(8,128)(2,1)S(1)} %collective-permute-done.22.rest_6_), channel_id=1, source_target_pairs={{0,1},{1,0},{2,3},{3,2},{4,5},{5,4},{6,7},{7,6},{8,9},{9,8},{10,11... | collective-permute-start | bytes 503816 | tf_op jit(solution)/shard_map/ppermute | solution.py:487
  (3 other events, 11.4 us)

commit v20 on v19

--- a/solution.py
+++ b/solution.py
@@ -122,8 +122,8 @@
 REST = HPAIR - WIDE
 MAIN = ROWS * WIDE
 NOTES = 16
-RECEIVERS = ((0, 0), (4, 2), (2, 4), (6, 6), (7, 7), (3, 5), (5, 3), (1, 1))
-SENDERS = ((0, 0), (4, 2), (2, 4), (6, 6), (7, 7), (5, 3), (3, 5), (1, 1))
+RECEIVERS = ((0, 0), (6, 6), (7, 7), (4, 2), (2, 4), (3, 5), (5, 3), (1, 1))
+SENDERS = ((0, 0), (6, 6), (7, 7), (4, 2), (2, 4), (5, 3), (3, 5), (1, 1))
 OWNERS = (0, 4, 2, 1, 5, 3, 6, 7)
 ROOT = math.log2(math.e) / math.sqrt(HDIM)
 BF16 = jnp.bfloat16
@@ -144,19 +144,23 @@
     return jnp.concatenate([wide[at * groups : (at + 1) * groups] for at in range(4)], axis=1)
 
 
-def spread_kernel(qkv_hbm, resid_hbm, grid_hbm, *rest):
+def spread_kernel(qkv_hbm, resid_hbm, weight_hbm, grid_hbm, *rest):
     outs = rest[:ROWS]
-    grid_out, qkv, resid, held, grid, sems = rest[ROWS:]
-    me = row_index()
-    copies = [
-        pltpu.make_async_copy(grid_hbm, grid, sems.at[0]),
-        pltpu.make_async_copy(resid_hbm.at[0], resid, sems.at[1]),
-    ]
+    chip_ref, slice_ref, grid_out, qkv, resid, main, tile, held, grid, sems = rest[ROWS:]
+    me = row_index()
+    depth = weight_hbm.shape[0]
+    chip = pl.ds(pl.multiple_of(me // 2 * 2 * WIDE, 2 * WIDE), 2 * WIDE)
+    ends = pl.ds(pl.multiple_of(MAIN + me // 4 * WIDE, WIDE), WIDE)
     part = qkv.shape[0] // 4
+    copies = []
     for at in range(4):
         rows = pl.ds(at * part, part)
-        copies.append(pltpu.make_async_copy(qkv_hbm.at[0, rows], qkv.at[rows], sems.at[2 + at]))
-    for copy in reversed(copies):
+        copies.append(pltpu.make_async_copy(qkv_hbm.at[0, rows], qkv.at[rows], sems.at[at]))
+    copies.append(pltpu.make_async_copy(resid_hbm.at[0], resid, sems.at[4]))
+    copies.append(pltpu.make_async_copy(weight_hbm.at[:, chip], main, sems.at[5]))
+    copies.append(pltpu.make_async_copy(weight_hbm.at[:, ends], tile, sems.at[6]))
+    copies.append(pltpu.make_async_copy(grid_hbm, grid, sems.at[7]))
+    for copy in copies:
         copy.start()
     for copy in copies:
         copy.wait()
@@ -168,16 +172,6 @@
         held[dest] = jnp.concatenate(parts, axis=1)
     for step, out in zip(steps(RECEIVERS), outs):
         out[...] = held[me ^ step]
-    row = lax.broadcasted_iota(jnp.int32, grid_out.shape, 0)
-    grid_out[...] = jnp.where(row == 0, grid[0, 0], grid[0, 1])
-
-
-def slice_kernel(weight_ref, *rest):
-    chip_ref, slice_ref = rest[-2:]
-    me = row_index()
-    depth = weight_ref.shape[0]
-    main = weight_ref[:, pl.ds(pl.multiple_of(me // 2 * 2 * WIDE, 2 * WIDE), 2 * WIDE)]
-    tile = weight_ref[:, pl.ds(pl.multiple_of(MAIN + me // 4 * WIDE, WIDE), WIDE)]
     low = me // 2 % 2 == 0
     size = depth + depth // 4
     for core in range(2):
@@ -185,6 +179,8 @@
         chip_ref[core * size : core * size + depth, :] = main[:, core * WIDE : (core + 1) * WIDE]
         chip_ref[core * size + depth : (core + 1) * size, :] = pack_tail(tail)
     slice_ref[...] = chip_ref[pl.ds(pl.multiple_of(me % 2 * size, 16), size), :]
+    row = lax.broadcasted_iota(jnp.int32, grid_out.shape, 0)
+    grid_out[...] = jnp.where(row == 0, grid[0, 0], grid[0, 1])
 
 
 def layout_kernel(grid_ref, *rest):
@@ -254,7 +250,7 @@
 def ready_kernel(select_ref, gain_hbm, token_ref, *rest):
     del token_ref
     blocks = rest[:ROWS]
-    own_ref, near_ref = rest[ROWS : ROWS + 2]
+    own_ref, across_ref, near_ref = rest[ROWS : ROWS + 3]
     resid_ref, gain_out, main_ref, tail_ref, held, line, sem = rest[-7:]
     fetch = pltpu.make_async_copy(gain_hbm, line, sem)
     fetch.start()
@@ -269,7 +265,8 @@
     half = pl.ds(pl.multiple_of(core * size, 16), size)
     main_ref[...] = jnp.zeros_like(main_ref)
     tail_ref[...] = jnp.zeros_like(tail_ref)
-    place_slices([(0, own_ref[...]), (3 - 2 * core, near_ref[half, :])], main_ref, tail_ref)
+    cuts = [(0, own_ref[...]), (2, across_ref[...]), (3 - 2 * core, near_ref[half, :])]
+    place_slices(cuts, main_ref, tail_ref)
     fetch.wait()
     whole = line[...].reshape(1, D)
     gain = jnp.zeros(gain_out.shape, F32)
@@ -285,13 +282,13 @@
         place_rows(weight_rows(cut), 2 * lax.rem(lax.axis_index("page") + step, PAGES), main_ref, tail_ref)
 
 
-def last_kernel(across_ref, swapped_ref, main_before_ref, tail_before_ref, main_ref, tail_ref):
+def last_kernel(swapped_ref, main_before_ref, tail_before_ref, main_ref, tail_ref):
     main_ref[...] = main_before_ref[...]
     tail_ref[...] = tail_before_ref[...]
     core = row_index() % 2
-    size = across_ref.shape[0]
+    size = swapped_ref.shape[0] // 2
     half = pl.ds(pl.multiple_of(core * size, 16), size)
-    place_slices([(2, across_ref[...]), (1 + 2 * core, swapped_ref[half, :])], main_ref, tail_ref)
+    place_slices([(1 + 2 * core, swapped_ref[half, :])], main_ref, tail_ref)
 
 
 def far_block():
@@ -509,38 +506,33 @@
     piece = patches + groups
     size = depth + depth // 4
 
-    *sends, grid = kernel(
+    *sends, chip, own, grid = kernel(
         spread_kernel,
         "spread",
-        [shape(band, 4 * HPAIR)] * ROWS + [shape(8, WIDE, dtype=jnp.int32)],
+        [shape(band, 4 * HPAIR)] * ROWS
+        + [shape(2 * size, WIDE), shape(size, WIDE), shape(8, WIDE, dtype=jnp.int32)],
         [
             pltpu.VMEM((band, 3 * D), BF16),
             pltpu.VMEM((band, D), BF16),
+            pltpu.VMEM((depth, 2 * WIDE), BF16),
+            pltpu.VMEM((depth, WIDE), BF16),
             pltpu.VMEM((ROWS, band, 4 * HPAIR), BF16),
             pltpu.SMEM(page_grid.shape, jnp.int32),
-            pltpu.SemaphoreType.DMA((6,)),
+            pltpu.SemaphoreType.DMA((8,)),
         ],
-        fetched=range(3),
-        count=3,
+        fetched=range(4),
+        count=4,
         moved=1 << 20,
-    )(in_hbm(qkv_rows), in_hbm(residual), in_hbm(page_grid))
+    )(in_hbm(qkv_rows), in_hbm(residual), in_hbm(out_weight), in_hbm(page_grid))
     blocks = [sends[0]] + [swap(send, *pair) for send, pair in zip(sends[1:], RECEIVERS[1:])]
     select, dead, live = kernel(
         layout_kernel,
         "layout",
         [shape(patches, patches), shape(1, patches, dtype=F32), shape(1, groups, dtype=F32)],
-        fetched=range(1, 1 + 3),
-        count=1 + 3,
+        fetched=range(1, 1 + 2),
+        count=1 + 2,
         moved=1 << 20,
-    )(grid, *blocks[1:4])
-    chip, own = kernel(
-        slice_kernel,
-        "out_weight_slices",
-        [shape(2 * size, WIDE), shape(size, WIDE)],
-        fetched=(1,),
-        count=2,
-        moved=1 << 20,
-    )(out_weight, sends[0])
+    )(grid, *blocks[1:3])
     near = turn(after(chip, *()), 1, PAGES - 1)
     swapped = swap(near, 1)
     attn = kernel(
@@ -552,30 +544,30 @@
         flops=20 * patches * patches * 4096,
         moved=1 << 20,
     )(select, dead, *blocks)
-    across = turn(after(own, attn), 2, 2)
+    across = turn(own, 2, 2)
     resid, own_gain, main, tail = kernel(
         ready_kernel,
         "ready",
         [shape(patches, HPAIR, dtype=F32), shape(1, HPAIR, dtype=F32), shape(MAIN, HPAIR), shape(4, MAIN, HPAIR)],
         [pltpu.VMEM((patches, HPAIR), BF16), pltpu.VMEM((D,), F32), pltpu.SemaphoreType.DMA],
         fetched=(1, 2),
-        count=3 + ROWS + 2,
+        count=3 + ROWS + 3,
         flops=10 * patches * patches * 4096,
         moved=4 << 20,
-    )(select, in_hbm(norm_gain), attn, *blocks, own, near)
+    )(select, in_hbm(norm_gain), attn, *blocks, own, across, near)
+    one, two, far = swap(attn, 4), swap(attn, 2), swap(attn, 6)
     last = kernel(
         last_kernel,
         "ready_last",
         [shape(MAIN, HPAIR), shape(4, MAIN, HPAIR)],
-        count=4,
+        count=3,
         flops=1,
         moved=1,
-    )(across, swapped, main, tail)
-    one, two, far = swap(attn, 4), swap(attn, 2), swap(attn, 6)
+    )(swapped, main, tail)
+    near = [swap(after(attn, main), 1), swap(after(one, last[0]), 1), swap(two, 1)]
     weights = tuple(last)
     rows = shape(patches, HPAIR, dtype=F32)
     first = kernel(project_first_kernel, "project_first", rows, count=6, flops=1, moved=1)(attn, one, two, *weights, resid)
-    near = [swap(after(attn, last[0]), 1), swap(one, 1), swap(two, 1)]
     second = kernel(project_second_kernel, "project_second", rows, count=6, flops=1, moved=1)(*near, *weights, first)
     hidden = kernel(
         project_kernel,
@@ -584,7 +576,7 @@
         count=2 + 4,
         flops=patches * MAIN * 256,
         moved=4 << 20,
-    )(far, swap(far, 1), second, *weights, own_gain)
+    )(far, swap(after(far, first), 1), second, *weights, own_gain)
     ends, bias = kernel(
         tail_kernel,
         "merge_tail",

time: 44.6 us -> 43.8 us (0.982)
  waiting for transfers between devices: 9.55 us -> 11.6 us
  starting transfers between devices: 22.1 us -> 20.5 us
  local copies, waits for them, and re-layouts: 1.16 us -> 0.01 us
    ppermute x22, waiting for transfers between devices: 5.92 us -> 8.59 us  [swap(): lax.ppermute(value, 'row', [(row, row ^ (odd if row % 2 else even)) for r...]
    unnamed x6 -> x4, local copies, waits for them, and re-layouts: 1.16 us -> 0.01 us
    ppermute x22, starting transfers between devices: 17.4 us -> 16.3 us  [swap(): lax.ppermute(value, 'row', [(row, row ^ (odd if row % 2 else even)) for r...]
    ppermute x2, waiting for transfers between devices: 3.63 us -> 3 us  [turn(): return lax.ppermute(value, ('page', 'row'), pairs)]
    ppermute x2, starting transfers between devices: 4.66 us -> 4.17 us  [turn(): return lax.ppermute(value, ('page', 'row'), pairs)]
  transfers between devices with their start and end apart: 24 -> 24, of which waited for: 8 -> 12; matrix products, arithmetic and copies ran while one was open for 0% -> 0% of each run, Pallas kernels for 18% -> 18%
where the time goes in v20:
time: 43.8 us; the launch traced here: 43.6 us
  starting transfers between devices  20.5 us (47%)
  waiting for transfers between devices  11.6 us (26%)
  Pallas kernels  11.4 us (26%)
    ppermute x22, starting transfers between devices, swap(): lax.ppermute(value, 'row', [(row, row ^ (odd if row % 2 else even)) for r...  16.3 us
    ppermute x22, waiting for transfers between devices, swap(): lax.ppermute(value, 'row', [(row, row ^ (odd if row % 2 else even)) for r...  8.59 us
    ppermute x2, starting transfers between devices, turn(): return lax.ppermute(value, ('page', 'row'), pairs)  4.17 us
    ppermute x2, waiting for transfers between devices, turn(): return lax.ppermute(value, ('page', 'row'), pairs)  3 us
    pallas_call x1, Pallas kernels, local_eight(): kernel(spread_kernel, 'spread', [shape(band, 4 * HPAIR)] * ROWS + [shape(...  1.77 us
    pallas_call x1, Pallas kernels, local_eight(): kernel(tail_kernel, 'merge_tail', [shape(units, MAIN), shape(units, 1, dt...  1.39 us
    pallas_call x1, Pallas kernels, local_eight(): kernel(merge_kernel, 'merge', shape(1, units, groups), [pltpu.VMEM((units...  1.36 us
    pallas_call x1, Pallas kernels, local_eight(): kernel(attend_kernel, 'attend', shape(piece, WIDE), [pltpu.VMEM((patches,...  1.35 us
  transfers between devices with their start and end apart: 24, of which 12 were waited for; matrix products, arithmetic and copies ran while one was open for 0% of the time, Pallas kernels for 18%

profile of v20, /device:TPU:0, one launch (start us, length us, event | category | flops | bytes accessed | tf_op | source)
XLA Modules:
  0.0 43.6 jit_solution(2586232584127516269)
XLA Ops:
  0.0 1.8 %spread.1 = (bf16[64,640]{1,0:T(8,128)(2,1)S(1)}, bf16[64,640]{1,0:T(8,128)(2,1)S(1)}, bf16[64,640]{1,0:T(8,128)(2,1)S(1)}, bf16[64,640]{1,0:T(8,128)(2,1)S(1)},...) custom-call(bf16[1,64,3840]{2,1,0:T(8,128)(2,1)} %qkv_hbm.1, ...), custom_call_target="tpu_custom_call" | custom-call | bytes 1048576 | tf_op jit(solution)/shard_map/spread/pallas_call | solution.py:509
  1.8 4.0 %collective-permute-start = (bf16[64,640]{1,0:T(8,128)(2,1)S(1)}, bf16[64,640]{1,0:T(8,128)(2,1)S(1)}, u32[]{:S(2)}, u32[]{:S(2)}) collective-permute-start(bf16[64,640]{1,0:T(8,128)(2,1)S(1)} %get-tuple-element.33), channel_id=1, source_target_pairs={{0,6},{1,7},{2,4},{3,5},{4,2},{5,3},{6,0},{7,1},{8,14},{9,15},{10,... | collective-permute-start | bytes 245768 | tf_op jit(solution)/shard_map/ppermute | solution.py:484
  5.7 1.2 %collective-permute-start.2 = (bf16[64,640]{1,0:T(8,128)(2,1)S(1)}, bf16[64,640]{1,0:T(8,128)(2,1)S(1)}, u32[]{:S(2)}, u32[]{:S(2)}) collective-permute-start(bf16[64,640]{1,0:T(8,128)(2,1)S(1)} %get-tuple-element.38), channel_id=1, source_target_pairs={{0,4},{1,3},{2,6},{3,1},{4,0},{5,7},{6,2},{7,5},{8,12},{9,11},{10,... | collective-permute-start | bytes 245768 | tf_op jit(solution)/shard_map/ppermute | solution.py:484
  6.9 1.5 %collective-permute-start.3 = (bf16[64,640]{1,0:T(8,128)(2,1)S(1)}, bf16[64,640]{1,0:T(8,128)(2,1)S(1)}, u32[]{:S(2)}, u32[]{:S(2)}) collective-permute-start(bf16[64,640]{1,0:T(8,128)(2,1)S(1)} %get-tuple-element.39), channel_id=1, source_target_pairs={{0,2},{1,5},{2,0},{3,7},{4,6},{5,1},{6,4},{7,3},{8,10},{9,13},{10,... | collective-permute-start | bytes 245768 | tf_op jit(solution)/shard_map/ppermute | solution.py:484
  8.9 1.2 %collective-permute-start.5 = (bf16[64,640]{1,0:T(8,128)(2,1)S(1)}, bf16[64,640]{1,0:T(8,128)(2,1)S(1)}, u32[]{:S(2)}, u32[]{:S(2)}) collective-permute-start(bf16[64,640]{1,0:T(8,128)(2,1)S(1)} %get-tuple-element.41), channel_id=1, source_target_pairs={{0,5},{1,2},{2,7},{3,0},{4,1},{5,6},{6,3},{7,4},{8,13},{9,10},{10,... | collective-permute-start | bytes 245768 | tf_op jit(solution)/shard_map/ppermute | solution.py:484
  10.1 1.3 %collective-permute-done.1.rest_1_.rest_2_ = bf16[64,640]{1,0:T(8,128)(2,1)S(1)} collective-permute-done((bf16[64,640]{1,0:T(8,128)(2,1)S(1)}, bf16[64,640]{1,0:T(8,128)(2,1)S(1)}, u32[]{:S(2)}, u32[]{:S(2)}) %collective-permute-start.1) | collective-permute-done | bytes 81952 | tf_op jit(solution)/shard_map/ppermute | solution.py:484
  11.6 1.0 %collective-permute-done.2.rest_3_ = bf16[64,640]{1,0:T(8,128)(2,1)S(1)} collective-permute-done((bf16[64,640]{1,0:T(8,128)(2,1)S(1)}, bf16[64,640]{1,0:T(8,128)(2,1)S(1)}, u32[]{:S(2)}, u32[]{:S(2)}) %collective-permute-start.2) | collective-permute-done | bytes 81952 | tf_op jit(solution)/shard_map/ppermute | solution.py:484
  12.7 1.6 %collective-permute-start.10 = (bf16[800,128]{1,0:T(8,128)(2,1)S(1)}, bf16[800,128]{1,0:T(8,128)(2,1)S(1)}, u32[]{:S(2)}, u32[]{:S(2)}) collective-permute-start(bf16[800,128]{1,0:T(8,128)(2,1)S(1)} %get-tuple-element.43), channel_id=1, source_target_pairs={{0,8},{1,25},{2,10},{3,27},{4,12},{5,29},{6,14},{7,31},{8,16},{9,1... | collective-permute-start | bytes 614408 | tf_op jit(solution)/shard_map/ppermute | solution.py:493
  14.2 2.6 %collective-permute-start.12 = (bf16[400,128]{1,0:T(8,128)(2,1)S(1)}, bf16[400,128]{1,0:T(8,128)(2,1)S(1)}, u32[]{:S(2)}, u32[]{:S(2)}) collective-permute-start(bf16[400,128]{1,0:T(8,128)(2,1)S(1)} %get-tuple-element.44.rest_8_), channel_id=1, source_target_pairs={{0,16},{1,17},{2,18},{3,19},{4,20},{5,21},{6,22},{7,23},{8,24},{9,... | collective-permute-start | bytes 307208 | tf_op jit(solution)/shard_map/ppermute | solution.py:493
  16.8 1.3 %attend.1.token_ref.rest_0_ = bf16[640,128]{1,0:T(8,128)(2,1)S(1)} custom-call(bf16[512,512]{1,0:T(8,128)(2,1)S(1)} %get-tuple-element.35.select_ref, f32[1,512]{1,0:T(1,128)S(1)} %get-tuple-element.36.dead_ref, bf16[64,640]{1,0:T(8,128)(2,1)S(1)} %get-tuple-element.37.rest_0_, bf16[64,640]{1,0:T(8,128)(2,1)S(1)} %collective-permute-done.rest_0_.rest_1_, ...), custom_call_target="tpu_custom_call" | custom-call | flops 21474836480 | bytes 1048576 | tf_op jit(solution)/shard_map/attend/pallas_call | solution.py:538
  18.2 1.0 %collective-permute-start.8 = (bf16[640,128]{1,0:T(8,128)(2,1)S(1)}, bf16[640,128]{1,0:T(8,128)(2,1)S(1)}, u32[]{:S(2)}, u32[]{:S(2)}) collective-permute-start(bf16[640,128]{1,0:T(8,128)(2,1)S(1)} %attend.1.token_ref.rest_0_), channel_id=1, source_target_pairs={{0,4},{1,5},{2,6},{3,7},{4,0},{5,1},{6,2},{7,3},{8,12},{9,13},{10,... | collective-permute-start | bytes 491528 | tf_op jit(solution)/shard_map/ppermute | solution.py:484
  19.2 1.5 %collective-permute-start.9 = (bf16[640,128]{1,0:T(8,128)(2,1)S(1)}, bf16[640,128]{1,0:T(8,128)(2,1)S(1)}, u32[]{:S(2)}, u32[]{:S(2)}) collective-permute-start(bf16[640,128]{1,0:T(8,128)(2,1)S(1)} %attend.1.token_ref.rest_0_), channel_id=1, source_target_pairs={{0,2},{1,3},{2,0},{3,1},{4,6},{5,7},{6,4},{7,5},{8,10},{9,11},{10,... | collective-permute-start | bytes 491528 | tf_op jit(solution)/shard_map/ppermute | solution.py:484
  20.6 1.1 %collective-permute-start.7 = (bf16[640,128]{1,0:T(8,128)(2,1)S(1)}, bf16[640,128]{1,0:T(8,128)(2,1)S(1)}, u32[]{:S(2)}, u32[]{:S(2)}) collective-permute-start(bf16[640,128]{1,0:T(8,128)(2,1)S(1)} %attend.1.token_ref.rest_0_), channel_id=1, source_target_pairs={{0,6},{1,7},{2,4},{3,5},{4,2},{5,3},{6,0},{7,1},{8,14},{9,15},{10,... | collective-permute-start | bytes 491528 | tf_op jit(solution)/shard_map/ppermute | solution.py:484
  22.5 2.3 %collective-permute-done.12.rest_9_ = bf16[400,128]{1,0:T(8,128)(2,1)S(1)} collective-permute-done((bf16[400,128]{1,0:T(8,128)(2,1)S(1)}, bf16[400,128]{1,0:T(8,128)(2,1)S(1)}, u32[]{:S(2)}, u32[]{:S(2)}) %collective-permute-start.12) | collective-permute-done | bytes 102432 | tf_op jit(solution)/shard_map/ppermute | solution.py:493
  24.7 1.2 %ready.1 = (f32[512,160]{1,0:T(8,128)S(1)}, f32[1,160]{1,0:T(1,128)S(1)}, bf16[1024,160]{1,0:T(8,128)(2,1)S(1)}, bf16[4,1024,160]{2,1,0:T(8,128)(2,1)S(1)}) custom-call(bf16[512,512]{1,0:T(8,128)(2,1)S(1)} %get-tuple-element.35.select_ref, f32[1280]{0:T(1024)} %gain_hbm.1, bf16[640,128]{1,0:T(8,128)(2,1)S(1)} %attend.1.token_ref.rest_0_, ...), custom_call_target="tpu_custom_call" | custom-call | flops 10737418240 | bytes 4194304 | tf_op jit(solution)/shard_map/ready/pallas_call | solution.py:548
  29.7 1.6 %collective-permute-start.17 = (bf16[656,128]{1,0:T(8,128)(2,1)S(1)}, bf16[656,128]{1,0:T(8,128)(2,1)S(1)}, u32[]{:S(2)}, u32[]{:S(2)}) collective-permute-start(bf16[656,128]{1,0:T(8,128)(2,1)S(1)} %project.1.token_ref.rest_0_), channel_id=1, source_target_pairs={{0,4},{1,5},{2,6},{3,7},{4,0},{5,1},{6,2},{7,3},{8,12},{9,13},{10,... | collective-permute-start | bytes 503816 | tf_op jit(solution)/shard_map/ppermute | solution.py:484
  31.9 1.3 %collective-permute-start.22 = (bf16[656,128]{1,0:T(8,128)(2,1)S(1)}, bf16[656,128]{1,0:T(8,128)(2,1)S(1)}, u32[]{:S(2)}, u32[]{:S(2)}) collective-permute-start(bf16[656,128]{1,0:T(8,128)(2,1)S(1)} %project.1.token_ref.rest_0_), channel_id=1, source_target_pairs={{0,6},{1,7},{2,4},{3,5},{4,2},{5,3},{6,0},{7,1},{8,14},{9,15},{10,... | collective-permute-start | bytes 503816 | tf_op jit(solution)/shard_map/ppermute | solution.py:484
  33.2 1.4 %merge_tail.1 = (bf16[640,1024]{1,0:T(8,128)(2,1)S(1)}, f32[640,1]{1,0:T(8,128)S(1)}) custom-call(bf16[640,5120]{1,0:T(8,128)(2,1)S(1)} %bitcast.1, f32[640]{0:T(1024)} %bias_hbm.1, bf16[656,128]{1,0:T(8,128)(2,1)S(1)} %project.1.token_ref.rest_0_), custom_call_target="tpu_custom_call" | custom-call | bytes 4194304 | tf_op jit(solution)/shard_map/merge_tail/pallas_call | solution.py:580
  34.7 1.4 %collective-permute-done.17.rest_1_ = bf16[656,128]{1,0:T(8,128)(2,1)S(1)} collective-permute-done((bf16[656,128]{1,0:T(8,128)(2,1)S(1)}, bf16[656,128]{1,0:T(8,128)(2,1)S(1)}, u32[]{:S(2)}, u32[]{:S(2)}) %collective-permute-start.17) | collective-permute-done | bytes 167968 | tf_op jit(solution)/shard_map/ppermute | solution.py:484
  36.1 2.4 %collective-permute-done.18.rest_2_ = bf16[656,128]{1,0:T(8,128)(2,1)S(1)} collective-permute-done((bf16[656,128]{1,0:T(8,128)(2,1)S(1)}, bf16[656,128]{1,0:T(8,128)(2,1)S(1)}, u32[]{:S(2)}, u32[]{:S(2)}) %collective-permute-start.18) | collective-permute-done | bytes 167968 | tf_op jit(solution)/shard_map/ppermute | solution.py:484
  38.5 1.2 %merge_first.1.rest_3_ = f32[4,640,128]{2,1,0:T(8,128)S(1)} custom-call(bf16[656,128]{1,0:T(8,128)(2,1)S(1)} %project.1.token_ref.rest_0_, bf16[656,128]{1,0:T(8,128)(2,1)S(1)} %collective-permute-done.17.rest_1_, bf16[656,128]{1,0:T(8,128)(2,1)S(1)} %collective-permute-done.18.rest_2_, bf16[640,5120]{1,0:T(8,128)(2,1)S(1)} %bitcast.1, ...), custom_call_target="tpu_custom_call" | custom-call | flops 1 | bytes 1 | tf_op jit(solution)/shard_map/merge_first/pallas_call | solution.py:591
  39.8 1.1 %collective-permute-done.22.rest_6_ = bf16[656,128]{1,0:T(8,128)(2,1)S(1)} collective-permute-done((bf16[656,128]{1,0:T(8,128)(2,1)S(1)}, bf16[656,128]{1,0:T(8,128)(2,1)S(1)}, u32[]{:S(2)}, u32[]{:S(2)}) %collective-permute-start.22) | collective-permute-done | bytes 167968 | tf_op jit(solution)/shard_map/ppermute | solution.py:484
  40.9 1.3 %merge_second.1.rest_8_ = f32[4,640,128]{2,1,0:T(8,128)S(1)} custom-call(bf16[656,128]{1,0:T(8,128)(2,1)S(1)} %collective-permute-done.19.rest_0_.rest_3_, bf16[656,128]{1,0:T(8,128)(2,1)S(1)} %collective-permute-done.20.rest_1_.rest_4_, bf16[656,128]{1,0:T(8,128)(2,1)S(1)} %collective-permute-done.21.rest_2_.rest_5_, ...), custom_call_target="tpu_custom_call" | custom-call | flops 1 | bytes 1 | tf_op jit(solution)/shard_map/merge_second/pallas_call | solution.py:595
  42.3 1.4 %merge.1 = bf16[1,640,128]{2,1,0:T(8,128)(2,1)} custom-call(bf16[656,128]{1,0:T(8,128)(2,1)S(1)} %project.1.token_ref.rest_0_, bf16[656,128]{1,0:T(8,128)(2,1)S(1)} %collective-permute-done.17.rest_1_, bf16[656,128]{1,0:T(8,128)(2,1)S(1)} %collective-permute-done.18.rest_2_, bf16[656,128]{1,0:T(8,128)(2,1)S(1)} %collective-permute-done.19.rest_0_.rest_3_, ...), custom_call_target="tpu_custom_call" | custom-call | flops 335544320 | bytes 8388608 | tf_op jit(solution)/shard_map/merge/pallas_call | solution.py:598
  (41 shorter events, 5.9 us)
Async XLA Ops:
  1.8 7.1 %collective-permute-start = (bf16[64,640]{1,0:T(8,128)(2,1)S(1)}, bf16[64,640]{1,0:T(8,128)(2,1)S(1)}, u32[]{:S(2)}, u32[]{:S(2)}) collective-permute-start(bf16[64,640]{1,0:T(8,128)(2,1)S(1)} %get-tuple-element.33), channel_id=1, source_target_pairs={{0,6},{1,7},{2,4},{3,5},{4,2},{5,3},{6,0},{7,1},{8,14},{9,15},{10,... | collective-permute-start | bytes 245768 | tf_op jit(solution)/shard_map/ppermute | solution.py:484
  5.7 5.7 %collective-permute-start.1 = (bf16[64,640]{1,0:T(8,128)(2,1)S(1)}, bf16[64,640]{1,0:T(8,128)(2,1)S(1)}, u32[]{:S(2)}, u32[]{:S(2)}) collective-permute-start(bf16[64,640]{1,0:T(8,128)(2,1)S(1)} %get-tuple-element.34), channel_id=1, source_target_pairs={{0,7},{1,6},{2,5},{3,4},{4,3},{5,2},{6,1},{7,0},{8,15},{9,14},{10,... | collective-permute-start | bytes 245768 | tf_op jit(solution)/shard_map/ppermute | solution.py:484
  5.7 6.9 %collective-permute-start.2 = (bf16[64,640]{1,0:T(8,128)(2,1)S(1)}, bf16[64,640]{1,0:T(8,128)(2,1)S(1)}, u32[]{:S(2)}, u32[]{:S(2)}) collective-permute-start(bf16[64,640]{1,0:T(8,128)(2,1)S(1)} %get-tuple-element.38), channel_id=1, source_target_pairs={{0,4},{1,3},{2,6},{3,1},{4,0},{5,7},{6,2},{7,5},{8,12},{9,11},{10,... | collective-permute-start | bytes 245768 | tf_op jit(solution)/shard_map/ppermute | solution.py:484
  6.9 7.3 %collective-permute-start.3 = (bf16[64,640]{1,0:T(8,128)(2,1)S(1)}, bf16[64,640]{1,0:T(8,128)(2,1)S(1)}, u32[]{:S(2)}, u32[]{:S(2)}) collective-permute-start(bf16[64,640]{1,0:T(8,128)(2,1)S(1)} %get-tuple-element.39), channel_id=1, source_target_pairs={{0,2},{1,5},{2,0},{3,7},{4,6},{5,1},{6,4},{7,3},{8,10},{9,13},{10,... | collective-permute-start | bytes 245768 | tf_op jit(solution)/shard_map/ppermute | solution.py:484
  8.4 8.4 %collective-permute-start.4 = (bf16[64,640]{1,0:T(8,128)(2,1)S(1)}, bf16[64,640]{1,0:T(8,128)(2,1)S(1)}, u32[]{:S(2)}, u32[]{:S(2)}) collective-permute-start(bf16[64,640]{1,0:T(8,128)(2,1)S(1)} %get-tuple-element.40), channel_id=1, source_target_pairs={{0,3},{1,4},{2,1},{3,6},{4,7},{5,0},{6,5},{7,2},{8,11},{9,12},{10,... | collective-permute-start | bytes 245768 | tf_op jit(solution)/shard_map/ppermute | solution.py:484
  8.9 7.9 %collective-permute-start.5 = (bf16[64,640]{1,0:T(8,128)(2,1)S(1)}, bf16[64,640]{1,0:T(8,128)(2,1)S(1)}, u32[]{:S(2)}, u32[]{:S(2)}) collective-permute-start(bf16[64,640]{1,0:T(8,128)(2,1)S(1)} %get-tuple-element.41), channel_id=1, source_target_pairs={{0,5},{1,2},{2,7},{3,0},{4,1},{5,6},{6,3},{7,4},{8,13},{9,10},{10,... | collective-permute-start | bytes 245768 | tf_op jit(solution)/shard_map/ppermute | solution.py:484
  11.4 5.4 %collective-permute-start.6 = (bf16[64,640]{1,0:T(8,128)(2,1)S(1)}, bf16[64,640]{1,0:T(8,128)(2,1)S(1)}, u32[]{:S(2)}, u32[]{:S(2)}) collective-permute-start(bf16[64,640]{1,0:T(8,128)(2,1)S(1)} %get-tuple-element.42), channel_id=1, source_target_pairs={{0,1},{1,0},{2,3},{3,2},{4,5},{5,4},{6,7},{7,6},{8,9},{9,8},{10,11... | collective-permute-start | bytes 245768 | tf_op jit(solution)/shard_map/ppermute | solution.py:484
  12.7 9.8 %collective-permute-start.10 = (bf16[800,128]{1,0:T(8,128)(2,1)S(1)}, bf16[800,128]{1,0:T(8,128)(2,1)S(1)}, u32[]{:S(2)}, u32[]{:S(2)}) collective-permute-start(bf16[800,128]{1,0:T(8,128)(2,1)S(1)} %get-tuple-element.43), channel_id=1, source_target_pairs={{0,8},{1,25},{2,10},{3,27},{4,12},{5,29},{6,14},{7,31},{8,16},{9,1... | collective-permute-start | bytes 614408 | tf_op jit(solution)/shard_map/ppermute | solution.py:493
  14.2 10.5 %collective-permute-start.12 = (bf16[400,128]{1,0:T(8,128)(2,1)S(1)}, bf16[400,128]{1,0:T(8,128)(2,1)S(1)}, u32[]{:S(2)}, u32[]{:S(2)}) collective-permute-start(bf16[400,128]{1,0:T(8,128)(2,1)S(1)} %get-tuple-element.44.rest_8_), channel_id=1, source_target_pairs={{0,16},{1,17},{2,18},{3,19},{4,20},{5,21},{6,22},{7,23},{8,24},{9,... | collective-permute-start | bytes 307208 | tf_op jit(solution)/shard_map/ppermute | solution.py:493
  18.2 8.6 %collective-permute-start.8 = (bf16[640,128]{1,0:T(8,128)(2,1)S(1)}, bf16[640,128]{1,0:T(8,128)(2,1)S(1)}, u32[]{:S(2)}, u32[]{:S(2)}) collective-permute-start(bf16[640,128]{1,0:T(8,128)(2,1)S(1)} %attend.1.token_ref.rest_0_), channel_id=1, source_target_pairs={{0,4},{1,5},{2,6},{3,7},{4,0},{5,1},{6,2},{7,3},{8,12},{9,13},{10,... | collective-permute-start | bytes 491528 | tf_op jit(solution)/shard_map/ppermute | solution.py:484
  19.2 7.1 %collective-permute-start.9 = (bf16[640,128]{1,0:T(8,128)(2,1)S(1)}, bf16[640,128]{1,0:T(8,128)(2,1)S(1)}, u32[]{:S(2)}, u32[]{:S(2)}) collective-permute-start(bf16[640,128]{1,0:T(8,128)(2,1)S(1)} %attend.1.token_ref.rest_0_), channel_id=1, source_target_pairs={{0,2},{1,3},{2,0},{3,1},{4,6},{5,7},{6,4},{7,5},{8,10},{9,11},{10,... | collective-permute-start | bytes 491528 | tf_op jit(solution)/shard_map/ppermute | solution.py:484
  20.6 7.2 %collective-permute-start.7 = (bf16[640,128]{1,0:T(8,128)(2,1)S(1)}, bf16[640,128]{1,0:T(8,128)(2,1)S(1)}, u32[]{:S(2)}, u32[]{:S(2)}) collective-permute-start(bf16[640,128]{1,0:T(8,128)(2,1)S(1)} %attend.1.token_ref.rest_0_), channel_id=1, source_target_pairs={{0,6},{1,7},{2,4},{3,5},{4,2},{5,3},{6,0},{7,1},{8,14},{9,15},{10,... | collective-permute-start | bytes 491528 | tf_op jit(solution)/shard_map/ppermute | solution.py:484
  22.5 4.1 %collective-permute-start.11 = (bf16[800,128]{1,0:T(8,128)(2,1)S(1)}, bf16[800,128]{1,0:T(8,128)(2,1)S(1)}, u32[]{:S(2)}, u32[]{:S(2)}) collective-permute-start(bf16[800,128]{1,0:T(8,128)(2,1)S(1)} %collective-permute-done.10.rest_10_), channel_id=1, source_target_pairs={{0,1},{1,0},{2,3},{3,2},{4,5},{5,4},{6,7},{7,6},{8,9},{9,8},{10,11... | collective-permute-start | bytes 614408 | tf_op jit(solution)/shard_map/ppermute | solution.py:484
  26.0 1.9 %collective-permute-start.14 = (bf16[640,128]{1,0:T(8,128)(2,1)S(1)}, bf16[640,128]{1,0:T(8,128)(2,1)S(1)}, u32[]{:S(2)}, u32[]{:S(2)}) collective-permute-start(bf16[640,128]{1,0:T(8,128)(2,1)S(1)} %attend.1.token_ref.rest_0_), channel_id=1, source_target_pairs={{0,1},{1,0},{2,3},{3,2},{4,5},{5,4},{6,7},{7,6},{8,9},{9,8},{10,11... | collective-permute-start | bytes 491528 | tf_op jit(solution)/shard_map/ppermute | solution.py:484
  26.2 1.7 %collective-permute-start.16 = (bf16[640,128]{1,0:T(8,128)(2,1)S(1)}, bf16[640,128]{1,0:T(8,128)(2,1)S(1)}, u32[]{:S(2)}, u32[]{:S(2)}) collective-permute-start(bf16[640,128]{1,0:T(8,128)(2,1)S(1)} %collective-permute-done.9.rest_2_), channel_id=1, source_target_pairs={{0,1},{1,0},{2,3},{3,2},{4,5},{5,4},{6,7},{7,6},{8,9},{9,8},{10,11... | collective-permute-start | bytes 491528 | tf_op jit(solution)/shard_map/ppermute | solution.py:484
  26.8 1.5 %collective-permute-start.15 = (bf16[640,128]{1,0:T(8,128)(2,1)S(1)}, bf16[640,128]{1,0:T(8,128)(2,1)S(1)}, u32[]{:S(2)}, u32[]{:S(2)}) collective-permute-start(bf16[640,128]{1,0:T(8,128)(2,1)S(1)} %collective-permute-done.8.rest_1_), channel_id=1, source_target_pairs={{0,1},{1,0},{2,3},{3,2},{4,5},{5,4},{6,7},{7,6},{8,9},{9,8},{10,11... | collective-permute-start | bytes 491528 | tf_op jit(solution)/shard_map/ppermute | solution.py:484
  27.8 1.4 %collective-permute-start.13 = (bf16[640,128]{1,0:T(8,128)(2,1)S(1)}, bf16[640,128]{1,0:T(8,128)(2,1)S(1)}, u32[]{:S(2)}, u32[]{:S(2)}) collective-permute-start(bf16[640,128]{1,0:T(8,128)(2,1)S(1)} %collective-permute-done.7.rest_0_), channel_id=1, source_target_pairs={{0,1},{1,0},{2,3},{3,2},{4,5},{5,4},{6,7},{7,6},{8,9},{9,8},{10,11... | collective-permute-start | bytes 491528 | tf_op jit(solution)/shard_map/ppermute | solution.py:484
  29.7 6.4 %collective-permute-start.17 = (bf16[656,128]{1,0:T(8,128)(2,1)S(1)}, bf16[656,128]{1,0:T(8,128)(2,1)S(1)}, u32[]{:S(2)}, u32[]{:S(2)}) collective-permute-start(bf16[656,128]{1,0:T(8,128)(2,1)S(1)} %project.1.token_ref.rest_0_), channel_id=1, source_target_pairs={{0,4},{1,5},{2,6},{3,7},{4,0},{5,1},{6,2},{7,3},{8,12},{9,13},{10,... | collective-permute-start | bytes 503816 | tf_op jit(solution)/shard_map/ppermute | solution.py:484
  31.3 7.2 %collective-permute-start.18 = (bf16[656,128]{1,0:T(8,128)(2,1)S(1)}, bf16[656,128]{1,0:T(8,128)(2,1)S(1)}, u32[]{:S(2)}, u32[]{:S(2)}) collective-permute-start(bf16[656,128]{1,0:T(8,128)(2,1)S(1)} %project.1.token_ref.rest_0_), channel_id=1, source_target_pairs={{0,2},{1,3},{2,0},{3,1},{4,6},{5,7},{6,4},{7,5},{8,10},{9,11},{10,... | collective-permute-start | bytes 503816 | tf_op jit(solution)/shard_map/ppermute | solution.py:484
  31.9 8.9 %collective-permute-start.22 = (bf16[656,128]{1,0:T(8,128)(2,1)S(1)}, bf16[656,128]{1,0:T(8,128)(2,1)S(1)}, u32[]{:S(2)}, u32[]{:S(2)}) collective-permute-start(bf16[656,128]{1,0:T(8,128)(2,1)S(1)} %project.1.token_ref.rest_0_), channel_id=1, source_target_pairs={{0,6},{1,7},{2,4},{3,5},{4,2},{5,3},{6,0},{7,1},{8,14},{9,15},{10,... | collective-permute-start | bytes 503816 | tf_op jit(solution)/shard_map/ppermute | solution.py:484
  34.6 5.1 %collective-permute-start.19 = (bf16[656,128]{1,0:T(8,128)(2,1)S(1)}, bf16[656,128]{1,0:T(8,128)(2,1)S(1)}, u32[]{:S(2)}, u32[]{:S(2)}) collective-permute-start(bf16[656,128]{1,0:T(8,128)(2,1)S(1)} %project.1.token_ref.rest_0_), channel_id=1, source_target_pairs={{0,1},{1,0},{2,3},{3,2},{4,5},{5,4},{6,7},{7,6},{8,9},{9,8},{10,11... | collective-permute-start | bytes 503816 | tf_op jit(solution)/shard_map/ppermute | solution.py:484
  36.1 4.8 %collective-permute-start.20 = (bf16[656,128]{1,0:T(8,128)(2,1)S(1)}, bf16[656,128]{1,0:T(8,128)(2,1)S(1)}, u32[]{:S(2)}, u32[]{:S(2)}) collective-permute-start(bf16[656,128]{1,0:T(8,128)(2,1)S(1)} %collective-permute-done.17.rest_1_), channel_id=1, source_target_pairs={{0,1},{1,0},{2,3},{3,2},{4,5},{5,4},{6,7},{7,6},{8,9},{9,8},{10,11... | collective-permute-start | bytes 503816 | tf_op jit(solution)/shard_map/ppermute | solution.py:484
  38.5 2.4 %collective-permute-start.21 = (bf16[656,128]{1,0:T(8,128)(2,1)S(1)}, bf16[656,128]{1,0:T(8,128)(2,1)S(1)}, u32[]{:S(2)}, u32[]{:S(2)}) collective-permute-start(bf16[656,128]{1,0:T(8,128)(2,1)S(1)} %collective-permute-done.18.rest_2_), channel_id=1, source_target_pairs={{0,1},{1,0},{2,3},{3,2},{4,5},{5,4},{6,7},{7,6},{8,9},{9,8},{10,11... | collective-permute-start | bytes 503816 | tf_op jit(solution)/shard_map/ppermute | solution.py:484
  40.9 1.4 %collective-permute-start.23 = (bf16[656,128]{1,0:T(8,128)(2,1)S(1)}, bf16[656,128]{1,0:T(8,128)(2,1)S(1)}, u32[]{:S(2)}, u32[]{:S(2)}) collective-permute-start(bf16[656,128]{1,0:T(8,128)(2,1)S(1)} %collective-permute-done.22.rest_6_), channel_id=1, source_target_pairs={{0,1},{1,0},{2,3},{3,2},{4,5},{5,4},{6,7},{7,6},{8,9},{9,8},{10,11... | collective-permute-start | bytes 503816 | tf_op jit(solution)/shard_map/ppermute | solution.py:484
  (2 other events, 12.0 us)

commit v21 on v20

--- a/solution.py
+++ b/solution.py
@@ -122,8 +122,8 @@
 REST = HPAIR - WIDE
 MAIN = ROWS * WIDE
 NOTES = 16
-RECEIVERS = ((0, 0), (6, 6), (7, 7), (4, 2), (2, 4), (3, 5), (5, 3), (1, 1))
-SENDERS = ((0, 0), (6, 6), (7, 7), (4, 2), (2, 4), (5, 3), (3, 5), (1, 1))
+RECEIVERS = ((0, 0), (4, 2), (2, 4), (6, 6), (7, 7), (3, 5), (5, 3), (1, 1))
+SENDERS = ((0, 0), (4, 2), (2, 4), (6, 6), (7, 7), (5, 3), (3, 5), (1, 1))
 OWNERS = (0, 4, 2, 1, 5, 3, 6, 7)
 ROOT = math.log2(math.e) / math.sqrt(HDIM)
 BF16 = jnp.bfloat16

time: 43.8 us -> 43.8 us (level)
  starting transfers between devices: 20.5 us -> 21.5 us
  waiting for transfers between devices: 11.6 us -> 10.6 us
    ppermute x22, waiting for transfers between devices: 8.59 us -> 7.64 us  [swap(): lax.ppermute(value, 'row', [(row, row ^ (odd if row % 2 else even)) for r...]
    ppermute x22, starting transfers between devices: 16.3 us -> 16.9 us  [swap(): lax.ppermute(value, 'row', [(row, row ^ (odd if row % 2 else even)) for r...]
  transfers between devices with their start and end apart: 24 -> 24, of which waited for: 12 -> 10; matrix products, arithmetic and copies ran while one was open for 0% -> 0% of each run, Pallas kernels for 18% -> 18%
where the time goes in v21:
time: 43.8 us; the launch traced here: 43.6 us
  starting transfers between devices  21.5 us (49%)
  Pallas kernels  11.4 us (26%)
  waiting for transfers between devices  10.6 us (24%)
    ppermute x22, starting transfers between devices, swap(): lax.ppermute(value, 'row', [(row, row ^ (odd if row % 2 else even)) for r...  16.9 us
    ppermute x22, waiting for transfers between devices, swap(): lax.ppermute(value, 'row', [(row, row ^ (odd if row % 2 else even)) for r...  7.64 us
    ppermute x2, starting transfers between devices, turn(): return lax.ppermute(value, ('page', 'row'), pairs)  4.59 us
    ppermute x2, waiting for transfers between devices, turn(): return lax.ppermute(value, ('page', 'row'), pairs)  2.93 us
    pallas_call x1, Pallas kernels, local_eight(): kernel(spread_kernel, 'spread', [shape(band, 4 * HPAIR)] * ROWS + [shape(...  1.77 us
    pallas_call x1, Pallas kernels, local_eight(): kernel(tail_kernel, 'merge_tail', [shape(units, MAIN), shape(units, 1, dt...  1.39 us
    pallas_call x1, Pallas kernels, local_eight(): kernel(merge_kernel, 'merge', shape(1, units, groups), [pltpu.VMEM((units...  1.36 us
    pallas_call x1, Pallas kernels, local_eight(): kernel(attend_kernel, 'attend', shape(piece, WIDE), [pltpu.VMEM((patches,...  1.34 us
  transfers between devices with their start and end apart: 24, of which 10 were waited for; matrix products, arithmetic and copies ran while one was open for 0% of the time, Pallas kernels for 18%

profile of v21, /device:TPU:0, one launch (start us, length us, event | category | flops | bytes accessed | tf_op | source)
XLA Modules:
  0.0 43.6 jit_solution(11628124730042851794)
XLA Ops:
  0.0 1.8 %spread.1 = (bf16[64,640]{1,0:T(8,128)(2,1)S(1)}, bf16[64,640]{1,0:T(8,128)(2,1)S(1)}, bf16[64,640]{1,0:T(8,128)(2,1)S(1)}, bf16[64,640]{1,0:T(8,128)(2,1)S(1)},...) custom-call(bf16[1,64,3840]{2,1,0:T(8,128)(2,1)} %qkv_hbm.1, ...), custom_call_target="tpu_custom_call" | custom-call | bytes 1048576 | tf_op jit(solution)/shard_map/spread/pallas_call | solution.py:509
  1.8 3.0 %collective-permute-start = (bf16[64,640]{1,0:T(8,128)(2,1)S(1)}, bf16[64,640]{1,0:T(8,128)(2,1)S(1)}, u32[]{:S(2)}, u32[]{:S(2)}) collective-permute-start(bf16[64,640]{1,0:T(8,128)(2,1)S(1)} %get-tuple-element.33), channel_id=1, source_target_pairs={{0,4},{1,3},{2,6},{3,1},{4,0},{5,7},{6,2},{7,5},{8,12},{9,11},{10,... | collective-permute-start | bytes 245768 | tf_op jit(solution)/shard_map/ppermute | solution.py:484
  4.8 1.5 %collective-permute-start.1 = (bf16[64,640]{1,0:T(8,128)(2,1)S(1)}, bf16[64,640]{1,0:T(8,128)(2,1)S(1)}, u32[]{:S(2)}, u32[]{:S(2)}) collective-permute-start(bf16[64,640]{1,0:T(8,128)(2,1)S(1)} %get-tuple-element.34), channel_id=1, source_target_pairs={{0,2},{1,5},{2,0},{3,7},{4,6},{5,1},{6,4},{7,3},{8,10},{9,13},{10,... | collective-permute-start | bytes 245768 | tf_op jit(solution)/shard_map/ppermute | solution.py:484
  6.4 1.5 %collective-permute-start.3 = (bf16[64,640]{1,0:T(8,128)(2,1)S(1)}, bf16[64,640]{1,0:T(8,128)(2,1)S(1)}, u32[]{:S(2)}, u32[]{:S(2)}) collective-permute-start(bf16[64,640]{1,0:T(8,128)(2,1)S(1)} %get-tuple-element.39), channel_id=1, source_target_pairs={{0,7},{1,6},{2,5},{3,4},{4,3},{5,2},{6,1},{7,0},{8,15},{9,14},{10,... | collective-permute-start | bytes 245768 | tf_op jit(solution)/shard_map/ppermute | solution.py:484
  7.8 1.6 %collective-permute-start.4 = (bf16[64,640]{1,0:T(8,128)(2,1)S(1)}, bf16[64,640]{1,0:T(8,128)(2,1)S(1)}, u32[]{:S(2)}, u32[]{:S(2)}) collective-permute-start(bf16[64,640]{1,0:T(8,128)(2,1)S(1)} %get-tuple-element.40), channel_id=1, source_target_pairs={{0,3},{1,4},{2,1},{3,6},{4,7},{5,0},{6,5},{7,2},{8,11},{9,12},{10,... | collective-permute-start | bytes 245768 | tf_op jit(solution)/shard_map/ppermute | solution.py:484
  9.9 1.2 %collective-permute-start.6 = (bf16[64,640]{1,0:T(8,128)(2,1)S(1)}, bf16[64,640]{1,0:T(8,128)(2,1)S(1)}, u32[]{:S(2)}, u32[]{:S(2)}) collective-permute-start(bf16[64,640]{1,0:T(8,128)(2,1)S(1)} %get-tuple-element.42), channel_id=1, source_target_pairs={{0,1},{1,0},{2,3},{3,2},{4,5},{5,4},{6,7},{7,6},{8,9},{9,8},{10,11... | collective-permute-start | bytes 245768 | tf_op jit(solution)/shard_map/ppermute | solution.py:484
  11.3 0.8 %collective-permute-done.2.rest_3_ = bf16[64,640]{1,0:T(8,128)(2,1)S(1)} collective-permute-done((bf16[64,640]{1,0:T(8,128)(2,1)S(1)}, bf16[64,640]{1,0:T(8,128)(2,1)S(1)}, u32[]{:S(2)}, u32[]{:S(2)}) %collective-permute-start.2) | collective-permute-done | bytes 81952 | tf_op jit(solution)/shard_map/ppermute | solution.py:484
  12.1 2.0 %collective-permute-start.10 = (bf16[800,128]{1,0:T(8,128)(2,1)S(1)}, bf16[800,128]{1,0:T(8,128)(2,1)S(1)}, u32[]{:S(2)}, u32[]{:S(2)}) collective-permute-start(bf16[800,128]{1,0:T(8,128)(2,1)S(1)} %get-tuple-element.43), channel_id=1, source_target_pairs={{0,8},{1,25},{2,10},{3,27},{4,12},{5,29},{6,14},{7,31},{8,16},{9,1... | collective-permute-start | bytes 614408 | tf_op jit(solution)/shard_map/ppermute | solution.py:493
  14.1 2.6 %collective-permute-start.12 = (bf16[400,128]{1,0:T(8,128)(2,1)S(1)}, bf16[400,128]{1,0:T(8,128)(2,1)S(1)}, u32[]{:S(2)}, u32[]{:S(2)}) collective-permute-start(bf16[400,128]{1,0:T(8,128)(2,1)S(1)} %get-tuple-element.44.rest_8_), channel_id=1, source_target_pairs={{0,16},{1,17},{2,18},{3,19},{4,20},{5,21},{6,22},{7,23},{8,24},{9,... | collective-permute-start | bytes 307208 | tf_op jit(solution)/shard_map/ppermute | solution.py:493
  16.7 1.3 %attend.1.token_ref.rest_0_ = bf16[640,128]{1,0:T(8,128)(2,1)S(1)} custom-call(bf16[512,512]{1,0:T(8,128)(2,1)S(1)} %get-tuple-element.35.select_ref, f32[1,512]{1,0:T(1,128)S(1)} %get-tuple-element.36.dead_ref, bf16[64,640]{1,0:T(8,128)(2,1)S(1)} %get-tuple-element.37.rest_0_, bf16[64,640]{1,0:T(8,128)(2,1)S(1)} %collective-permute-done.rest_0_.rest_1_, ...), custom_call_target="tpu_custom_call" | custom-call | flops 21474836480 | bytes 1048576 | tf_op jit(solution)/shard_map/attend/pallas_call | solution.py:538
  18.1 1.1 %collective-permute-start.9 = (bf16[640,128]{1,0:T(8,128)(2,1)S(1)}, bf16[640,128]{1,0:T(8,128)(2,1)S(1)}, u32[]{:S(2)}, u32[]{:S(2)}) collective-permute-start(bf16[640,128]{1,0:T(8,128)(2,1)S(1)} %attend.1.token_ref.rest_0_), channel_id=1, source_target_pairs={{0,2},{1,3},{2,0},{3,1},{4,6},{5,7},{6,4},{7,5},{8,10},{9,11},{10,... | collective-permute-start | bytes 491528 | tf_op jit(solution)/shard_map/ppermute | solution.py:484
  19.3 2.3 %collective-permute-start.7 = (bf16[640,128]{1,0:T(8,128)(2,1)S(1)}, bf16[640,128]{1,0:T(8,128)(2,1)S(1)}, u32[]{:S(2)}, u32[]{:S(2)}) collective-permute-start(bf16[640,128]{1,0:T(8,128)(2,1)S(1)} %attend.1.token_ref.rest_0_), channel_id=1, source_target_pairs={{0,6},{1,7},{2,4},{3,5},{4,2},{5,3},{6,0},{7,1},{8,14},{9,15},{10,... | collective-permute-start | bytes 491528 | tf_op jit(solution)/shard_map/ppermute | solution.py:484
  21.6 2.9 %collective-permute-done.12.rest_9_ = bf16[400,128]{1,0:T(8,128)(2,1)S(1)} collective-permute-done((bf16[400,128]{1,0:T(8,128)(2,1)S(1)}, bf16[400,128]{1,0:T(8,128)(2,1)S(1)}, u32[]{:S(2)}, u32[]{:S(2)}) %collective-permute-start.12) | collective-permute-done | bytes 102432 | tf_op jit(solution)/shard_map/ppermute | solution.py:493
  24.5 1.2 %ready.1 = (f32[512,160]{1,0:T(8,128)S(1)}, f32[1,160]{1,0:T(1,128)S(1)}, bf16[1024,160]{1,0:T(8,128)(2,1)S(1)}, bf16[4,1024,160]{2,1,0:T(8,128)(2,1)S(1)}) custom-call(bf16[512,512]{1,0:T(8,128)(2,1)S(1)} %get-tuple-element.35.select_ref, f32[1280]{0:T(1024)} %gain_hbm.1, bf16[640,128]{1,0:T(8,128)(2,1)S(1)} %attend.1.token_ref.rest_0_, ...), custom_call_target="tpu_custom_call" | custom-call | flops 10737418240 | bytes 4194304 | tf_op jit(solution)/shard_map/ready/pallas_call | solution.py:548
  28.5 0.7 %collective-permute-done.13.rest_1_ = bf16[640,128]{1,0:T(8,128)(2,1)S(1)} collective-permute-done((bf16[640,128]{1,0:T(8,128)(2,1)S(1)}, bf16[640,128]{1,0:T(8,128)(2,1)S(1)}, u32[]{:S(2)}, u32[]{:S(2)}) %collective-permute-start.13) | collective-permute-done | bytes 163872 | tf_op jit(solution)/shard_map/ppermute | solution.py:484
  29.7 0.8 %collective-permute-start.17 = (bf16[656,128]{1,0:T(8,128)(2,1)S(1)}, bf16[656,128]{1,0:T(8,128)(2,1)S(1)}, u32[]{:S(2)}, u32[]{:S(2)}) collective-permute-start(bf16[656,128]{1,0:T(8,128)(2,1)S(1)} %project.1.token_ref.rest_0_), channel_id=1, source_target_pairs={{0,4},{1,5},{2,6},{3,7},{4,0},{5,1},{6,2},{7,3},{8,12},{9,13},{10,... | collective-permute-start | bytes 503816 | tf_op jit(solution)/shard_map/ppermute | solution.py:484
  31.2 2.0 %collective-permute-start.22 = (bf16[656,128]{1,0:T(8,128)(2,1)S(1)}, bf16[656,128]{1,0:T(8,128)(2,1)S(1)}, u32[]{:S(2)}, u32[]{:S(2)}) collective-permute-start(bf16[656,128]{1,0:T(8,128)(2,1)S(1)} %project.1.token_ref.rest_0_), channel_id=1, source_target_pairs={{0,6},{1,7},{2,4},{3,5},{4,2},{5,3},{6,0},{7,1},{8,14},{9,15},{10,... | collective-permute-start | bytes 503816 | tf_op jit(solution)/shard_map/ppermute | solution.py:484
  33.2 1.4 %merge_tail.1 = (bf16[640,1024]{1,0:T(8,128)(2,1)S(1)}, f32[640,1]{1,0:T(8,128)S(1)}) custom-call(bf16[640,5120]{1,0:T(8,128)(2,1)S(1)} %bitcast.1, f32[640]{0:T(1024)} %bias_hbm.1, bf16[656,128]{1,0:T(8,128)(2,1)S(1)} %project.1.token_ref.rest_0_), custom_call_target="tpu_custom_call" | custom-call | bytes 4194304 | tf_op jit(solution)/shard_map/merge_tail/pallas_call | solution.py:580
  34.7 1.4 %collective-permute-done.17.rest_1_ = bf16[656,128]{1,0:T(8,128)(2,1)S(1)} collective-permute-done((bf16[656,128]{1,0:T(8,128)(2,1)S(1)}, bf16[656,128]{1,0:T(8,128)(2,1)S(1)}, u32[]{:S(2)}, u32[]{:S(2)}) %collective-permute-start.17) | collective-permute-done | bytes 167968 | tf_op jit(solution)/shard_map/ppermute | solution.py:484
  36.0 1.6 %collective-permute-done.18.rest_2_ = bf16[656,128]{1,0:T(8,128)(2,1)S(1)} collective-permute-done((bf16[656,128]{1,0:T(8,128)(2,1)S(1)}, bf16[656,128]{1,0:T(8,128)(2,1)S(1)}, u32[]{:S(2)}, u32[]{:S(2)}) %collective-permute-start.18) | collective-permute-done | bytes 167968 | tf_op jit(solution)/shard_map/ppermute | solution.py:484
  37.6 1.2 %merge_first.1.rest_3_ = f32[4,640,128]{2,1,0:T(8,128)S(1)} custom-call(bf16[656,128]{1,0:T(8,128)(2,1)S(1)} %project.1.token_ref.rest_0_, bf16[656,128]{1,0:T(8,128)(2,1)S(1)} %collective-permute-done.17.rest_1_, bf16[656,128]{1,0:T(8,128)(2,1)S(1)} %collective-permute-done.18.rest_2_, bf16[640,5120]{1,0:T(8,128)(2,1)S(1)} %bitcast.1, ...), custom_call_target="tpu_custom_call" | custom-call | flops 1 | bytes 1 | tf_op jit(solution)/shard_map/merge_first/pallas_call | solution.py:591
  38.9 1.9 %collective-permute-done.22.rest_6_ = bf16[656,128]{1,0:T(8,128)(2,1)S(1)} collective-permute-done((bf16[656,128]{1,0:T(8,128)(2,1)S(1)}, bf16[656,128]{1,0:T(8,128)(2,1)S(1)}, u32[]{:S(2)}, u32[]{:S(2)}) %collective-permute-start.22) | collective-permute-done | bytes 167968 | tf_op jit(solution)/shard_map/ppermute | solution.py:484
  40.8 1.3 %merge_second.1.rest_8_ = f32[4,640,128]{2,1,0:T(8,128)S(1)} custom-call(bf16[656,128]{1,0:T(8,128)(2,1)S(1)} %collective-permute-done.19.rest_0_.rest_3_, bf16[656,128]{1,0:T(8,128)(2,1)S(1)} %collective-permute-done.20.rest_1_.rest_4_, bf16[656,128]{1,0:T(8,128)(2,1)S(1)} %collective-permute-done.21.rest_2_.rest_5_, ...), custom_call_target="tpu_custom_call" | custom-call | flops 1 | bytes 1 | tf_op jit(solution)/shard_map/merge_second/pallas_call | solution.py:595
  42.2 1.4 %merge.1 = bf16[1,640,128]{2,1,0:T(8,128)(2,1)} custom-call(bf16[656,128]{1,0:T(8,128)(2,1)S(1)} %project.1.token_ref.rest_0_, bf16[656,128]{1,0:T(8,128)(2,1)S(1)} %collective-permute-done.17.rest_1_, bf16[656,128]{1,0:T(8,128)(2,1)S(1)} %collective-permute-done.18.rest_2_, bf16[656,128]{1,0:T(8,128)(2,1)S(1)} %collective-permute-done.19.rest_0_.rest_3_, ...), custom_call_target="tpu_custom_call" | custom-call | flops 335544320 | bytes 8388608 | tf_op jit(solution)/shard_map/merge/pallas_call | solution.py:598
  (41 shorter events, 4.7 us)
Async XLA Ops:
  1.8 7.7 %collective-permute-start = (bf16[64,640]{1,0:T(8,128)(2,1)S(1)}, bf16[64,640]{1,0:T(8,128)(2,1)S(1)}, u32[]{:S(2)}, u32[]{:S(2)}) collective-permute-start(bf16[64,640]{1,0:T(8,128)(2,1)S(1)} %get-tuple-element.33), channel_id=1, source_target_pairs={{0,4},{1,3},{2,6},{3,1},{4,0},{5,7},{6,2},{7,5},{8,12},{9,11},{10,... | collective-permute-start | bytes 245768 | tf_op jit(solution)/shard_map/ppermute | solution.py:484
  4.8 5.1 %collective-permute-start.1 = (bf16[64,640]{1,0:T(8,128)(2,1)S(1)}, bf16[64,640]{1,0:T(8,128)(2,1)S(1)}, u32[]{:S(2)}, u32[]{:S(2)}) collective-permute-start(bf16[64,640]{1,0:T(8,128)(2,1)S(1)} %get-tuple-element.34), channel_id=1, source_target_pairs={{0,2},{1,5},{2,0},{3,7},{4,6},{5,1},{6,4},{7,3},{8,10},{9,13},{10,... | collective-permute-start | bytes 245768 | tf_op jit(solution)/shard_map/ppermute | solution.py:484
  6.3 5.8 %collective-permute-start.2 = (bf16[64,640]{1,0:T(8,128)(2,1)S(1)}, bf16[64,640]{1,0:T(8,128)(2,1)S(1)}, u32[]{:S(2)}, u32[]{:S(2)}) collective-permute-start(bf16[64,640]{1,0:T(8,128)(2,1)S(1)} %get-tuple-element.38), channel_id=1, source_target_pairs={{0,6},{1,7},{2,4},{3,5},{4,2},{5,3},{6,0},{7,1},{8,14},{9,15},{10,... | collective-permute-start | bytes 245768 | tf_op jit(solution)/shard_map/ppermute | solution.py:484
  6.4 7.8 %collective-permute-start.3 = (bf16[64,640]{1,0:T(8,128)(2,1)S(1)}, bf16[64,640]{1,0:T(8,128)(2,1)S(1)}, u32[]{:S(2)}, u32[]{:S(2)}) collective-permute-start(bf16[64,640]{1,0:T(8,128)(2,1)S(1)} %get-tuple-element.39), channel_id=1, source_target_pairs={{0,7},{1,6},{2,5},{3,4},{4,3},{5,2},{6,1},{7,0},{8,15},{9,14},{10,... | collective-permute-start | bytes 245768 | tf_op jit(solution)/shard_map/ppermute | solution.py:484
  7.8 8.9 %collective-permute-start.4 = (bf16[64,640]{1,0:T(8,128)(2,1)S(1)}, bf16[64,640]{1,0:T(8,128)(2,1)S(1)}, u32[]{:S(2)}, u32[]{:S(2)}) collective-permute-start(bf16[64,640]{1,0:T(8,128)(2,1)S(1)} %get-tuple-element.40), channel_id=1, source_target_pairs={{0,3},{1,4},{2,1},{3,6},{4,7},{5,0},{6,5},{7,2},{8,11},{9,12},{10,... | collective-permute-start | bytes 245768 | tf_op jit(solution)/shard_map/ppermute | solution.py:484
  9.5 7.2 %collective-permute-start.5 = (bf16[64,640]{1,0:T(8,128)(2,1)S(1)}, bf16[64,640]{1,0:T(8,128)(2,1)S(1)}, u32[]{:S(2)}, u32[]{:S(2)}) collective-permute-start(bf16[64,640]{1,0:T(8,128)(2,1)S(1)} %get-tuple-element.41), channel_id=1, source_target_pairs={{0,5},{1,2},{2,7},{3,0},{4,1},{5,6},{6,3},{7,4},{8,13},{9,10},{10,... | collective-permute-start | bytes 245768 | tf_op jit(solution)/shard_map/ppermute | solution.py:484
  9.9 6.8 %collective-permute-start.6 = (bf16[64,640]{1,0:T(8,128)(2,1)S(1)}, bf16[64,640]{1,0:T(8,128)(2,1)S(1)}, u32[]{:S(2)}, u32[]{:S(2)}) collective-permute-start(bf16[64,640]{1,0:T(8,128)(2,1)S(1)} %get-tuple-element.42), channel_id=1, source_target_pairs={{0,1},{1,0},{2,3},{3,2},{4,5},{5,4},{6,7},{7,6},{8,9},{9,8},{10,11... | collective-permute-start | bytes 245768 | tf_op jit(solution)/shard_map/ppermute | solution.py:484
  12.1 9.5 %collective-permute-start.10 = (bf16[800,128]{1,0:T(8,128)(2,1)S(1)}, bf16[800,128]{1,0:T(8,128)(2,1)S(1)}, u32[]{:S(2)}, u32[]{:S(2)}) collective-permute-start(bf16[800,128]{1,0:T(8,128)(2,1)S(1)} %get-tuple-element.43), channel_id=1, source_target_pairs={{0,8},{1,25},{2,10},{3,27},{4,12},{5,29},{6,14},{7,31},{8,16},{9,1... | collective-permute-start | bytes 614408 | tf_op jit(solution)/shard_map/ppermute | solution.py:493
  14.1 10.4 %collective-permute-start.12 = (bf16[400,128]{1,0:T(8,128)(2,1)S(1)}, bf16[400,128]{1,0:T(8,128)(2,1)S(1)}, u32[]{:S(2)}, u32[]{:S(2)}) collective-permute-start(bf16[400,128]{1,0:T(8,128)(2,1)S(1)} %get-tuple-element.44.rest_8_), channel_id=1, source_target_pairs={{0,16},{1,17},{2,18},{3,19},{4,20},{5,21},{6,22},{7,23},{8,24},{9,... | collective-permute-start | bytes 307208 | tf_op jit(solution)/shard_map/ppermute | solution.py:493
  18.0 8.5 %collective-permute-start.8 = (bf16[640,128]{1,0:T(8,128)(2,1)S(1)}, bf16[640,128]{1,0:T(8,128)(2,1)S(1)}, u32[]{:S(2)}, u32[]{:S(2)}) collective-permute-start(bf16[640,128]{1,0:T(8,128)(2,1)S(1)} %attend.1.token_ref.rest_0_), channel_id=1, source_target_pairs={{0,4},{1,5},{2,6},{3,7},{4,0},{5,1},{6,2},{7,3},{8,12},{9,13},{10,... | collective-permute-start | bytes 491528 | tf_op jit(solution)/shard_map/ppermute | solution.py:484
  18.1 7.7 %collective-permute-start.9 = (bf16[640,128]{1,0:T(8,128)(2,1)S(1)}, bf16[640,128]{1,0:T(8,128)(2,1)S(1)}, u32[]{:S(2)}, u32[]{:S(2)}) collective-permute-start(bf16[640,128]{1,0:T(8,128)(2,1)S(1)} %attend.1.token_ref.rest_0_), channel_id=1, source_target_pairs={{0,2},{1,3},{2,0},{3,1},{4,6},{5,7},{6,4},{7,5},{8,10},{9,11},{10,... | collective-permute-start | bytes 491528 | tf_op jit(solution)/shard_map/ppermute | solution.py:484
  19.3 8.5 %collective-permute-start.7 = (bf16[640,128]{1,0:T(8,128)(2,1)S(1)}, bf16[640,128]{1,0:T(8,128)(2,1)S(1)}, u32[]{:S(2)}, u32[]{:S(2)}) collective-permute-start(bf16[640,128]{1,0:T(8,128)(2,1)S(1)} %attend.1.token_ref.rest_0_), channel_id=1, source_target_pairs={{0,6},{1,7},{2,4},{3,5},{4,2},{5,3},{6,0},{7,1},{8,14},{9,15},{10,... | collective-permute-start | bytes 491528 | tf_op jit(solution)/shard_map/ppermute | solution.py:484
  21.6 4.7 %collective-permute-start.11 = (bf16[800,128]{1,0:T(8,128)(2,1)S(1)}, bf16[800,128]{1,0:T(8,128)(2,1)S(1)}, u32[]{:S(2)}, u32[]{:S(2)}) collective-permute-start(bf16[800,128]{1,0:T(8,128)(2,1)S(1)} %collective-permute-done.10.rest_10_), channel_id=1, source_target_pairs={{0,1},{1,0},{2,3},{3,2},{4,5},{5,4},{6,7},{7,6},{8,9},{9,8},{10,11... | collective-permute-start | bytes 614408 | tf_op jit(solution)/shard_map/ppermute | solution.py:484
  25.8 2.0 %collective-permute-start.14 = (bf16[640,128]{1,0:T(8,128)(2,1)S(1)}, bf16[640,128]{1,0:T(8,128)(2,1)S(1)}, u32[]{:S(2)}, u32[]{:S(2)}) collective-permute-start(bf16[640,128]{1,0:T(8,128)(2,1)S(1)} %attend.1.token_ref.rest_0_), channel_id=1, source_target_pairs={{0,1},{1,0},{2,3},{3,2},{4,5},{5,4},{6,7},{7,6},{8,9},{9,8},{10,11... | collective-permute-start | bytes 491528 | tf_op jit(solution)/shard_map/ppermute | solution.py:484
  25.8 2.0 %collective-permute-start.16 = (bf16[640,128]{1,0:T(8,128)(2,1)S(1)}, bf16[640,128]{1,0:T(8,128)(2,1)S(1)}, u32[]{:S(2)}, u32[]{:S(2)}) collective-permute-start(bf16[640,128]{1,0:T(8,128)(2,1)S(1)} %collective-permute-done.9.rest_2_), channel_id=1, source_target_pairs={{0,1},{1,0},{2,3},{3,2},{4,5},{5,4},{6,7},{7,6},{8,9},{9,8},{10,11... | collective-permute-start | bytes 491528 | tf_op jit(solution)/shard_map/ppermute | solution.py:484
  26.6 1.5 %collective-permute-start.15 = (bf16[640,128]{1,0:T(8,128)(2,1)S(1)}, bf16[640,128]{1,0:T(8,128)(2,1)S(1)}, u32[]{:S(2)}, u32[]{:S(2)}) collective-permute-start(bf16[640,128]{1,0:T(8,128)(2,1)S(1)} %collective-permute-done.8.rest_1_), channel_id=1, source_target_pairs={{0,1},{1,0},{2,3},{3,2},{4,5},{5,4},{6,7},{7,6},{8,9},{9,8},{10,11... | collective-permute-start | bytes 491528 | tf_op jit(solution)/shard_map/ppermute | solution.py:484
  27.8 1.4 %collective-permute-start.13 = (bf16[640,128]{1,0:T(8,128)(2,1)S(1)}, bf16[640,128]{1,0:T(8,128)(2,1)S(1)}, u32[]{:S(2)}, u32[]{:S(2)}) collective-permute-start(bf16[640,128]{1,0:T(8,128)(2,1)S(1)} %collective-permute-done.7.rest_0_), channel_id=1, source_target_pairs={{0,1},{1,0},{2,3},{3,2},{4,5},{5,4},{6,7},{7,6},{8,9},{9,8},{10,11... | collective-permute-start | bytes 491528 | tf_op jit(solution)/shard_map/ppermute | solution.py:484
  29.7 6.4 %collective-permute-start.17 = (bf16[656,128]{1,0:T(8,128)(2,1)S(1)}, bf16[656,128]{1,0:T(8,128)(2,1)S(1)}, u32[]{:S(2)}, u32[]{:S(2)}) collective-permute-start(bf16[656,128]{1,0:T(8,128)(2,1)S(1)} %project.1.token_ref.rest_0_), channel_id=1, source_target_pairs={{0,4},{1,5},{2,6},{3,7},{4,0},{5,1},{6,2},{7,3},{8,12},{9,13},{10,... | collective-permute-start | bytes 503816 | tf_op jit(solution)/shard_map/ppermute | solution.py:484
  30.5 7.2 %collective-permute-start.18 = (bf16[656,128]{1,0:T(8,128)(2,1)S(1)}, bf16[656,128]{1,0:T(8,128)(2,1)S(1)}, u32[]{:S(2)}, u32[]{:S(2)}) collective-permute-start(bf16[656,128]{1,0:T(8,128)(2,1)S(1)} %project.1.token_ref.rest_0_), channel_id=1, source_target_pairs={{0,2},{1,3},{2,0},{3,1},{4,6},{5,7},{6,4},{7,5},{8,10},{9,11},{10,... | collective-permute-start | bytes 503816 | tf_op jit(solution)/shard_map/ppermute | solution.py:484
  31.2 9.7 %collective-permute-start.22 = (bf16[656,128]{1,0:T(8,128)(2,1)S(1)}, bf16[656,128]{1,0:T(8,128)(2,1)S(1)}, u32[]{:S(2)}, u32[]{:S(2)}) collective-permute-start(bf16[656,128]{1,0:T(8,128)(2,1)S(1)} %project.1.token_ref.rest_0_), channel_id=1, source_target_pairs={{0,6},{1,7},{2,4},{3,5},{4,2},{5,3},{6,0},{7,1},{8,14},{9,15},{10,... | collective-permute-start | bytes 503816 | tf_op jit(solution)/shard_map/ppermute | solution.py:484
  34.6 4.3 %collective-permute-start.19 = (bf16[656,128]{1,0:T(8,128)(2,1)S(1)}, bf16[656,128]{1,0:T(8,128)(2,1)S(1)}, u32[]{:S(2)}, u32[]{:S(2)}) collective-permute-start(bf16[656,128]{1,0:T(8,128)(2,1)S(1)} %project.1.token_ref.rest_0_), channel_id=1, source_target_pairs={{0,1},{1,0},{2,3},{3,2},{4,5},{5,4},{6,7},{7,6},{8,9},{9,8},{10,11... | collective-permute-start | bytes 503816 | tf_op jit(solution)/shard_map/ppermute | solution.py:484
  36.0 4.8 %collective-permute-start.20 = (bf16[656,128]{1,0:T(8,128)(2,1)S(1)}, bf16[656,128]{1,0:T(8,128)(2,1)S(1)}, u32[]{:S(2)}, u32[]{:S(2)}) collective-permute-start(bf16[656,128]{1,0:T(8,128)(2,1)S(1)} %collective-permute-done.17.rest_1_), channel_id=1, source_target_pairs={{0,1},{1,0},{2,3},{3,2},{4,5},{5,4},{6,7},{7,6},{8,9},{9,8},{10,11... | collective-permute-start | bytes 503816 | tf_op jit(solution)/shard_map/ppermute | solution.py:484
  37.6 3.2 %collective-permute-start.21 = (bf16[656,128]{1,0:T(8,128)(2,1)S(1)}, bf16[656,128]{1,0:T(8,128)(2,1)S(1)}, u32[]{:S(2)}, u32[]{:S(2)}) collective-permute-start(bf16[656,128]{1,0:T(8,128)(2,1)S(1)} %collective-permute-done.18.rest_2_), channel_id=1, source_target_pairs={{0,1},{1,0},{2,3},{3,2},{4,5},{5,4},{6,7},{7,6},{8,9},{9,8},{10,11... | collective-permute-start | bytes 503816 | tf_op jit(solution)/shard_map/ppermute | solution.py:484
  40.8 1.4 %collective-permute-start.23 = (bf16[656,128]{1,0:T(8,128)(2,1)S(1)}, bf16[656,128]{1,0:T(8,128)(2,1)S(1)}, u32[]{:S(2)}, u32[]{:S(2)}) collective-permute-start(bf16[656,128]{1,0:T(8,128)(2,1)S(1)} %collective-permute-done.22.rest_6_), channel_id=1, source_target_pairs={{0,1},{1,0},{2,3},{3,2},{4,5},{5,4},{6,7},{7,6},{8,9},{9,8},{10,11... | collective-permute-start | bytes 503816 | tf_op jit(solution)/shard_map/ppermute | solution.py:484
  (2 other events, 12.5 us)

commit v22 on v21

--- a/solution.py
+++ b/solution.py
@@ -162,7 +162,7 @@
     copies.append(pltpu.make_async_copy(grid_hbm, grid, sems.at[7]))
     for copy in copies:
         copy.start()
-    for copy in copies:
+    for copy in copies[:5]:
         copy.wait()
     for dest in range(ROWS):
         at = dest * HPAIR
@@ -172,6 +172,8 @@
         held[dest] = jnp.concatenate(parts, axis=1)
     for step, out in zip(steps(RECEIVERS), outs):
         out[...] = held[me ^ step]
+    for copy in copies[5:]:
+        copy.wait()
     low = me // 2 % 2 == 0
     size = depth + depth // 4
     for core in range(2):

time: 43.8 us -> 43.8 us (level)
  no operation moved by 1% of the time
where the time goes in v22:
time: 43.8 us; the launch traced here: 43.6 us
  starting transfers between devices  21.5 us (49%)
  Pallas kernels  11.4 us (26%)
  waiting for transfers between devices  10.5 us (24%)
    ppermute x22, starting transfers between devices, swap(): lax.ppermute(value, 'row', [(row, row ^ (odd if row % 2 else even)) for r...  16.9 us
    ppermute x22, waiting for transfers between devices, swap(): lax.ppermute(value, 'row', [(row, row ^ (odd if row % 2 else even)) for r...  7.62 us
    ppermute x2, starting transfers between devices, turn(): return lax.ppermute(value, ('page', 'row'), pairs)  4.59 us
    ppermute x2, waiting for transfers between devices, turn(): return lax.ppermute(value, ('page', 'row'), pairs)  2.92 us
    pallas_call x1, Pallas kernels, local_eight(): kernel(spread_kernel, 'spread', [shape(band, 4 * HPAIR)] * ROWS + [shape(...  1.78 us
    pallas_call x1, Pallas kernels, local_eight(): kernel(tail_kernel, 'merge_tail', [shape(units, MAIN), shape(units, 1, dt...  1.39 us
    pallas_call x1, Pallas kernels, local_eight(): kernel(merge_kernel, 'merge', shape(1, units, groups), [pltpu.VMEM((units...  1.36 us
    pallas_call x1, Pallas kernels, local_eight(): kernel(attend_kernel, 'attend', shape(piece, WIDE), [pltpu.VMEM((patches,...  1.34 us
  transfers between devices with their start and end apart: 24, of which 10 were waited for; matrix products, arithmetic and copies ran while one was open for 0% of the time, Pallas kernels for 18%

profile of v22, /device:TPU:0, one launch (start us, length us, event | category | flops | bytes accessed | tf_op | source)
XLA Modules:
  0.0 43.6 jit_solution(17232970090604756203)
XLA Ops:
  0.0 1.8 %spread.1 = (bf16[64,640]{1,0:T(8,128)(2,1)S(1)}, bf16[64,640]{1,0:T(8,128)(2,1)S(1)}, bf16[64,640]{1,0:T(8,128)(2,1)S(1)}, bf16[64,640]{1,0:T(8,128)(2,1)S(1)},...) custom-call(bf16[1,64,3840]{2,1,0:T(8,128)(2,1)} %qkv_hbm.1, ...), custom_call_target="tpu_custom_call" | custom-call | bytes 1048576 | tf_op jit(solution)/shard_map/spread/pallas_call | solution.py:511
  1.8 3.0 %collective-permute-start = (bf16[64,640]{1,0:T(8,128)(2,1)S(1)}, bf16[64,640]{1,0:T(8,128)(2,1)S(1)}, u32[]{:S(2)}, u32[]{:S(2)}) collective-permute-start(bf16[64,640]{1,0:T(8,128)(2,1)S(1)} %get-tuple-element.33), channel_id=1, source_target_pairs={{0,4},{1,3},{2,6},{3,1},{4,0},{5,7},{6,2},{7,5},{8,12},{9,11},{10,... | collective-permute-start | bytes 245768 | tf_op jit(solution)/shard_map/ppermute | solution.py:486
  4.8 1.5 %collective-permute-start.1 = (bf16[64,640]{1,0:T(8,128)(2,1)S(1)}, bf16[64,640]{1,0:T(8,128)(2,1)S(1)}, u32[]{:S(2)}, u32[]{:S(2)}) collective-permute-start(bf16[64,640]{1,0:T(8,128)(2,1)S(1)} %get-tuple-element.34), channel_id=1, source_target_pairs={{0,2},{1,5},{2,0},{3,7},{4,6},{5,1},{6,4},{7,3},{8,10},{9,13},{10,... | collective-permute-start | bytes 245768 | tf_op jit(solution)/shard_map/ppermute | solution.py:486
  6.4 1.5 %collective-permute-start.3 = (bf16[64,640]{1,0:T(8,128)(2,1)S(1)}, bf16[64,640]{1,0:T(8,128)(2,1)S(1)}, u32[]{:S(2)}, u32[]{:S(2)}) collective-permute-start(bf16[64,640]{1,0:T(8,128)(2,1)S(1)} %get-tuple-element.39), channel_id=1, source_target_pairs={{0,7},{1,6},{2,5},{3,4},{4,3},{5,2},{6,1},{7,0},{8,15},{9,14},{10,... | collective-permute-start | bytes 245768 | tf_op jit(solution)/shard_map/ppermute | solution.py:486
  7.8 1.6 %collective-permute-start.4 = (bf16[64,640]{1,0:T(8,128)(2,1)S(1)}, bf16[64,640]{1,0:T(8,128)(2,1)S(1)}, u32[]{:S(2)}, u32[]{:S(2)}) collective-permute-start(bf16[64,640]{1,0:T(8,128)(2,1)S(1)} %get-tuple-element.40), channel_id=1, source_target_pairs={{0,3},{1,4},{2,1},{3,6},{4,7},{5,0},{6,5},{7,2},{8,11},{9,12},{10,... | collective-permute-start | bytes 245768 | tf_op jit(solution)/shard_map/ppermute | solution.py:486
  9.9 1.2 %collective-permute-start.6 = (bf16[64,640]{1,0:T(8,128)(2,1)S(1)}, bf16[64,640]{1,0:T(8,128)(2,1)S(1)}, u32[]{:S(2)}, u32[]{:S(2)}) collective-permute-start(bf16[64,640]{1,0:T(8,128)(2,1)S(1)} %get-tuple-element.42), channel_id=1, source_target_pairs={{0,1},{1,0},{2,3},{3,2},{4,5},{5,4},{6,7},{7,6},{8,9},{9,8},{10,11... | collective-permute-start | bytes 245768 | tf_op jit(solution)/shard_map/ppermute | solution.py:486
  11.3 0.8 %collective-permute-done.2.rest_3_ = bf16[64,640]{1,0:T(8,128)(2,1)S(1)} collective-permute-done((bf16[64,640]{1,0:T(8,128)(2,1)S(1)}, bf16[64,640]{1,0:T(8,128)(2,1)S(1)}, u32[]{:S(2)}, u32[]{:S(2)}) %collective-permute-start.2) | collective-permute-done | bytes 81952 | tf_op jit(solution)/shard_map/ppermute | solution.py:486
  12.1 2.0 %collective-permute-start.10 = (bf16[800,128]{1,0:T(8,128)(2,1)S(1)}, bf16[800,128]{1,0:T(8,128)(2,1)S(1)}, u32[]{:S(2)}, u32[]{:S(2)}) collective-permute-start(bf16[800,128]{1,0:T(8,128)(2,1)S(1)} %get-tuple-element.43), channel_id=1, source_target_pairs={{0,8},{1,25},{2,10},{3,27},{4,12},{5,29},{6,14},{7,31},{8,16},{9,1... | collective-permute-start | bytes 614408 | tf_op jit(solution)/shard_map/ppermute | solution.py:495
  14.1 2.6 %collective-permute-start.12 = (bf16[400,128]{1,0:T(8,128)(2,1)S(1)}, bf16[400,128]{1,0:T(8,128)(2,1)S(1)}, u32[]{:S(2)}, u32[]{:S(2)}) collective-permute-start(bf16[400,128]{1,0:T(8,128)(2,1)S(1)} %get-tuple-element.44.rest_8_), channel_id=1, source_target_pairs={{0,16},{1,17},{2,18},{3,19},{4,20},{5,21},{6,22},{7,23},{8,24},{9,... | collective-permute-start | bytes 307208 | tf_op jit(solution)/shard_map/ppermute | solution.py:495
  16.7 1.3 %attend.1.token_ref.rest_0_ = bf16[640,128]{1,0:T(8,128)(2,1)S(1)} custom-call(bf16[512,512]{1,0:T(8,128)(2,1)S(1)} %get-tuple-element.35.select_ref, f32[1,512]{1,0:T(1,128)S(1)} %get-tuple-element.36.dead_ref, bf16[64,640]{1,0:T(8,128)(2,1)S(1)} %get-tuple-element.37.rest_0_, bf16[64,640]{1,0:T(8,128)(2,1)S(1)} %collective-permute-done.rest_0_.rest_1_, ...), custom_call_target="tpu_custom_call" | custom-call | flops 21474836480 | bytes 1048576 | tf_op jit(solution)/shard_map/attend/pallas_call | solution.py:540
  18.1 1.1 %collective-permute-start.9 = (bf16[640,128]{1,0:T(8,128)(2,1)S(1)}, bf16[640,128]{1,0:T(8,128)(2,1)S(1)}, u32[]{:S(2)}, u32[]{:S(2)}) collective-permute-start(bf16[640,128]{1,0:T(8,128)(2,1)S(1)} %attend.1.token_ref.rest_0_), channel_id=1, source_target_pairs={{0,2},{1,3},{2,0},{3,1},{4,6},{5,7},{6,4},{7,5},{8,10},{9,11},{10,... | collective-permute-start | bytes 491528 | tf_op jit(solution)/shard_map/ppermute | solution.py:486
  19.3 2.4 %collective-permute-start.7 = (bf16[640,128]{1,0:T(8,128)(2,1)S(1)}, bf16[640,128]{1,0:T(8,128)(2,1)S(1)}, u32[]{:S(2)}, u32[]{:S(2)}) collective-permute-start(bf16[640,128]{1,0:T(8,128)(2,1)S(1)} %attend.1.token_ref.rest_0_), channel_id=1, source_target_pairs={{0,6},{1,7},{2,4},{3,5},{4,2},{5,3},{6,0},{7,1},{8,14},{9,15},{10,... | collective-permute-start | bytes 491528 | tf_op jit(solution)/shard_map/ppermute | solution.py:486
  21.6 2.9 %collective-permute-done.12.rest_9_ = bf16[400,128]{1,0:T(8,128)(2,1)S(1)} collective-permute-done((bf16[400,128]{1,0:T(8,128)(2,1)S(1)}, bf16[400,128]{1,0:T(8,128)(2,1)S(1)}, u32[]{:S(2)}, u32[]{:S(2)}) %collective-permute-start.12) | collective-permute-done | bytes 102432 | tf_op jit(solution)/shard_map/ppermute | solution.py:495
  24.5 1.2 %ready.1 = (f32[512,160]{1,0:T(8,128)S(1)}, f32[1,160]{1,0:T(1,128)S(1)}, bf16[1024,160]{1,0:T(8,128)(2,1)S(1)}, bf16[4,1024,160]{2,1,0:T(8,128)(2,1)S(1)}) custom-call(bf16[512,512]{1,0:T(8,128)(2,1)S(1)} %get-tuple-element.35.select_ref, f32[1280]{0:T(1024)} %gain_hbm.1, bf16[640,128]{1,0:T(8,128)(2,1)S(1)} %attend.1.token_ref.rest_0_, ...), custom_call_target="tpu_custom_call" | custom-call | flops 10737418240 | bytes 4194304 | tf_op jit(solution)/shard_map/ready/pallas_call | solution.py:550
  28.5 0.7 %collective-permute-done.13.rest_1_ = bf16[640,128]{1,0:T(8,128)(2,1)S(1)} collective-permute-done((bf16[640,128]{1,0:T(8,128)(2,1)S(1)}, bf16[640,128]{1,0:T(8,128)(2,1)S(1)}, u32[]{:S(2)}, u32[]{:S(2)}) %collective-permute-start.13) | collective-permute-done | bytes 163872 | tf_op jit(solution)/shard_map/ppermute | solution.py:486
  29.7 0.8 %collective-permute-start.17 = (bf16[656,128]{1,0:T(8,128)(2,1)S(1)}, bf16[656,128]{1,0:T(8,128)(2,1)S(1)}, u32[]{:S(2)}, u32[]{:S(2)}) collective-permute-start(bf16[656,128]{1,0:T(8,128)(2,1)S(1)} %project.1.token_ref.rest_0_), channel_id=1, source_target_pairs={{0,4},{1,5},{2,6},{3,7},{4,0},{5,1},{6,2},{7,3},{8,12},{9,13},{10,... | collective-permute-start | bytes 503816 | tf_op jit(solution)/shard_map/ppermute | solution.py:486
  31.2 2.0 %collective-permute-start.22 = (bf16[656,128]{1,0:T(8,128)(2,1)S(1)}, bf16[656,128]{1,0:T(8,128)(2,1)S(1)}, u32[]{:S(2)}, u32[]{:S(2)}) collective-permute-start(bf16[656,128]{1,0:T(8,128)(2,1)S(1)} %project.1.token_ref.rest_0_), channel_id=1, source_target_pairs={{0,6},{1,7},{2,4},{3,5},{4,2},{5,3},{6,0},{7,1},{8,14},{9,15},{10,... | collective-permute-start | bytes 503816 | tf_op jit(solution)/shard_map/ppermute | solution.py:486
  33.2 1.4 %merge_tail.1 = (bf16[640,1024]{1,0:T(8,128)(2,1)S(1)}, f32[640,1]{1,0:T(8,128)S(1)}) custom-call(bf16[640,5120]{1,0:T(8,128)(2,1)S(1)} %bitcast.1, f32[640]{0:T(1024)} %bias_hbm.1, bf16[656,128]{1,0:T(8,128)(2,1)S(1)} %project.1.token_ref.rest_0_), custom_call_target="tpu_custom_call" | custom-call | bytes 4194304 | tf_op jit(solution)/shard_map/merge_tail/pallas_call | solution.py:582
  34.7 1.4 %collective-permute-done.17.rest_1_ = bf16[656,128]{1,0:T(8,128)(2,1)S(1)} collective-permute-done((bf16[656,128]{1,0:T(8,128)(2,1)S(1)}, bf16[656,128]{1,0:T(8,128)(2,1)S(1)}, u32[]{:S(2)}, u32[]{:S(2)}) %collective-permute-start.17) | collective-permute-done | bytes 167968 | tf_op jit(solution)/shard_map/ppermute | solution.py:486
  36.0 1.6 %collective-permute-done.18.rest_2_ = bf16[656,128]{1,0:T(8,128)(2,1)S(1)} collective-permute-done((bf16[656,128]{1,0:T(8,128)(2,1)S(1)}, bf16[656,128]{1,0:T(8,128)(2,1)S(1)}, u32[]{:S(2)}, u32[]{:S(2)}) %collective-permute-start.18) | collective-permute-done | bytes 167968 | tf_op jit(solution)/shard_map/ppermute | solution.py:486
  37.7 1.3 %merge_first.1.rest_3_ = f32[4,640,128]{2,1,0:T(8,128)S(1)} custom-call(bf16[656,128]{1,0:T(8,128)(2,1)S(1)} %project.1.token_ref.rest_0_, bf16[656,128]{1,0:T(8,128)(2,1)S(1)} %collective-permute-done.17.rest_1_, bf16[656,128]{1,0:T(8,128)(2,1)S(1)} %collective-permute-done.18.rest_2_, bf16[640,5120]{1,0:T(8,128)(2,1)S(1)} %bitcast.1, ...), custom_call_target="tpu_custom_call" | custom-call | flops 1 | bytes 1 | tf_op jit(solution)/shard_map/merge_first/pallas_call | solution.py:593
  38.9 1.9 %collective-permute-done.22.rest_6_ = bf16[656,128]{1,0:T(8,128)(2,1)S(1)} collective-permute-done((bf16[656,128]{1,0:T(8,128)(2,1)S(1)}, bf16[656,128]{1,0:T(8,128)(2,1)S(1)}, u32[]{:S(2)}, u32[]{:S(2)}) %collective-permute-start.22) | collective-permute-done | bytes 167968 | tf_op jit(solution)/shard_map/ppermute | solution.py:486
  40.8 1.3 %merge_second.1.rest_8_ = f32[4,640,128]{2,1,0:T(8,128)S(1)} custom-call(bf16[656,128]{1,0:T(8,128)(2,1)S(1)} %collective-permute-done.19.rest_0_.rest_3_, bf16[656,128]{1,0:T(8,128)(2,1)S(1)} %collective-permute-done.20.rest_1_.rest_4_, bf16[656,128]{1,0:T(8,128)(2,1)S(1)} %collective-permute-done.21.rest_2_.rest_5_, ...), custom_call_target="tpu_custom_call" | custom-call | flops 1 | bytes 1 | tf_op jit(solution)/shard_map/merge_second/pallas_call | solution.py:597
  42.2 1.4 %merge.1 = bf16[1,640,128]{2,1,0:T(8,128)(2,1)} custom-call(bf16[656,128]{1,0:T(8,128)(2,1)S(1)} %project.1.token_ref.rest_0_, bf16[656,128]{1,0:T(8,128)(2,1)S(1)} %collective-permute-done.17.rest_1_, bf16[656,128]{1,0:T(8,128)(2,1)S(1)} %collective-permute-done.18.rest_2_, bf16[656,128]{1,0:T(8,128)(2,1)S(1)} %collective-permute-done.19.rest_0_.rest_3_, ...), custom_call_target="tpu_custom_call" | custom-call | flops 335544320 | bytes 8388608 | tf_op jit(solution)/shard_map/merge/pallas_call | solution.py:600
  (41 shorter events, 4.7 us)
Async XLA Ops:
  1.8 7.7 %collective-permute-start = (bf16[64,640]{1,0:T(8,128)(2,1)S(1)}, bf16[64,640]{1,0:T(8,128)(2,1)S(1)}, u32[]{:S(2)}, u32[]{:S(2)}) collective-permute-start(bf16[64,640]{1,0:T(8,128)(2,1)S(1)} %get-tuple-element.33), channel_id=1, source_target_pairs={{0,4},{1,3},{2,6},{3,1},{4,0},{5,7},{6,2},{7,5},{8,12},{9,11},{10,... | collective-permute-start | bytes 245768 | tf_op jit(solution)/shard_map/ppermute | solution.py:486
  4.8 5.1 %collective-permute-start.1 = (bf16[64,640]{1,0:T(8,128)(2,1)S(1)}, bf16[64,640]{1,0:T(8,128)(2,1)S(1)}, u32[]{:S(2)}, u32[]{:S(2)}) collective-permute-start(bf16[64,640]{1,0:T(8,128)(2,1)S(1)} %get-tuple-element.34), channel_id=1, source_target_pairs={{0,2},{1,5},{2,0},{3,7},{4,6},{5,1},{6,4},{7,3},{8,10},{9,13},{10,... | collective-permute-start | bytes 245768 | tf_op jit(solution)/shard_map/ppermute | solution.py:486
  6.3 5.8 %collective-permute-start.2 = (bf16[64,640]{1,0:T(8,128)(2,1)S(1)}, bf16[64,640]{1,0:T(8,128)(2,1)S(1)}, u32[]{:S(2)}, u32[]{:S(2)}) collective-permute-start(bf16[64,640]{1,0:T(8,128)(2,1)S(1)} %get-tuple-element.38), channel_id=1, source_target_pairs={{0,6},{1,7},{2,4},{3,5},{4,2},{5,3},{6,0},{7,1},{8,14},{9,15},{10,... | collective-permute-start | bytes 245768 | tf_op jit(solution)/shard_map/ppermute | solution.py:486
  6.4 7.8 %collective-permute-start.3 = (bf16[64,640]{1,0:T(8,128)(2,1)S(1)}, bf16[64,640]{1,0:T(8,128)(2,1)S(1)}, u32[]{:S(2)}, u32[]{:S(2)}) collective-permute-start(bf16[64,640]{1,0:T(8,128)(2,1)S(1)} %get-tuple-element.39), channel_id=1, source_target_pairs={{0,7},{1,6},{2,5},{3,4},{4,3},{5,2},{6,1},{7,0},{8,15},{9,14},{10,... | collective-permute-start | bytes 245768 | tf_op jit(solution)/shard_map/ppermute | solution.py:486
  7.8 8.9 %collective-permute-start.4 = (bf16[64,640]{1,0:T(8,128)(2,1)S(1)}, bf16[64,640]{1,0:T(8,128)(2,1)S(1)}, u32[]{:S(2)}, u32[]{:S(2)}) collective-permute-start(bf16[64,640]{1,0:T(8,128)(2,1)S(1)} %get-tuple-element.40), channel_id=1, source_target_pairs={{0,3},{1,4},{2,1},{3,6},{4,7},{5,0},{6,5},{7,2},{8,11},{9,12},{10,... | collective-permute-start | bytes 245768 | tf_op jit(solution)/shard_map/ppermute | solution.py:486
  9.5 7.2 %collective-permute-start.5 = (bf16[64,640]{1,0:T(8,128)(2,1)S(1)}, bf16[64,640]{1,0:T(8,128)(2,1)S(1)}, u32[]{:S(2)}, u32[]{:S(2)}) collective-permute-start(bf16[64,640]{1,0:T(8,128)(2,1)S(1)} %get-tuple-element.41), channel_id=1, source_target_pairs={{0,5},{1,2},{2,7},{3,0},{4,1},{5,6},{6,3},{7,4},{8,13},{9,10},{10,... | collective-permute-start | bytes 245768 | tf_op jit(solution)/shard_map/ppermute | solution.py:486
  9.9 6.8 %collective-permute-start.6 = (bf16[64,640]{1,0:T(8,128)(2,1)S(1)}, bf16[64,640]{1,0:T(8,128)(2,1)S(1)}, u32[]{:S(2)}, u32[]{:S(2)}) collective-permute-start(bf16[64,640]{1,0:T(8,128)(2,1)S(1)} %get-tuple-element.42), channel_id=1, source_target_pairs={{0,1},{1,0},{2,3},{3,2},{4,5},{5,4},{6,7},{7,6},{8,9},{9,8},{10,11... | collective-permute-start | bytes 245768 | tf_op jit(solution)/shard_map/ppermute | solution.py:486
  12.1 9.5 %collective-permute-start.10 = (bf16[800,128]{1,0:T(8,128)(2,1)S(1)}, bf16[800,128]{1,0:T(8,128)(2,1)S(1)}, u32[]{:S(2)}, u32[]{:S(2)}) collective-permute-start(bf16[800,128]{1,0:T(8,128)(2,1)S(1)} %get-tuple-element.43), channel_id=1, source_target_pairs={{0,8},{1,25},{2,10},{3,27},{4,12},{5,29},{6,14},{7,31},{8,16},{9,1... | collective-permute-start | bytes 614408 | tf_op jit(solution)/shard_map/ppermute | solution.py:495
  14.1 10.4 %collective-permute-start.12 = (bf16[400,128]{1,0:T(8,128)(2,1)S(1)}, bf16[400,128]{1,0:T(8,128)(2,1)S(1)}, u32[]{:S(2)}, u32[]{:S(2)}) collective-permute-start(bf16[400,128]{1,0:T(8,128)(2,1)S(1)} %get-tuple-element.44.rest_8_), channel_id=1, source_target_pairs={{0,16},{1,17},{2,18},{3,19},{4,20},{5,21},{6,22},{7,23},{8,24},{9,... | collective-permute-start | bytes 307208 | tf_op jit(solution)/shard_map/ppermute | solution.py:495
  18.1 8.5 %collective-permute-start.8 = (bf16[640,128]{1,0:T(8,128)(2,1)S(1)}, bf16[640,128]{1,0:T(8,128)(2,1)S(1)}, u32[]{:S(2)}, u32[]{:S(2)}) collective-permute-start(bf16[640,128]{1,0:T(8,128)(2,1)S(1)} %attend.1.token_ref.rest_0_), channel_id=1, source_target_pairs={{0,4},{1,5},{2,6},{3,7},{4,0},{5,1},{6,2},{7,3},{8,12},{9,13},{10,... | collective-permute-start | bytes 491528 | tf_op jit(solution)/shard_map/ppermute | solution.py:486
  18.1 7.7 %collective-permute-start.9 = (bf16[640,128]{1,0:T(8,128)(2,1)S(1)}, bf16[640,128]{1,0:T(8,128)(2,1)S(1)}, u32[]{:S(2)}, u32[]{:S(2)}) collective-permute-start(bf16[640,128]{1,0:T(8,128)(2,1)S(1)} %attend.1.token_ref.rest_0_), channel_id=1, source_target_pairs={{0,2},{1,3},{2,0},{3,1},{4,6},{5,7},{6,4},{7,5},{8,10},{9,11},{10,... | collective-permute-start | bytes 491528 | tf_op jit(solution)/shard_map/ppermute | solution.py:486
  19.3 8.5 %collective-permute-start.7 = (bf16[640,128]{1,0:T(8,128)(2,1)S(1)}, bf16[640,128]{1,0:T(8,128)(2,1)S(1)}, u32[]{:S(2)}, u32[]{:S(2)}) collective-permute-start(bf16[640,128]{1,0:T(8,128)(2,1)S(1)} %attend.1.token_ref.rest_0_), channel_id=1, source_target_pairs={{0,6},{1,7},{2,4},{3,5},{4,2},{5,3},{6,0},{7,1},{8,14},{9,15},{10,... | collective-permute-start | bytes 491528 | tf_op jit(solution)/shard_map/ppermute | solution.py:486
  21.6 4.7 %collective-permute-start.11 = (bf16[800,128]{1,0:T(8,128)(2,1)S(1)}, bf16[800,128]{1,0:T(8,128)(2,1)S(1)}, u32[]{:S(2)}, u32[]{:S(2)}) collective-permute-start(bf16[800,128]{1,0:T(8,128)(2,1)S(1)} %collective-permute-done.10.rest_10_), channel_id=1, source_target_pairs={{0,1},{1,0},{2,3},{3,2},{4,5},{5,4},{6,7},{7,6},{8,9},{9,8},{10,11... | collective-permute-start | bytes 614408 | tf_op jit(solution)/shard_map/ppermute | solution.py:486
  25.8 2.0 %collective-permute-start.14 = (bf16[640,128]{1,0:T(8,128)(2,1)S(1)}, bf16[640,128]{1,0:T(8,128)(2,1)S(1)}, u32[]{:S(2)}, u32[]{:S(2)}) collective-permute-start(bf16[640,128]{1,0:T(8,128)(2,1)S(1)} %attend.1.token_ref.rest_0_), channel_id=1, source_target_pairs={{0,1},{1,0},{2,3},{3,2},{4,5},{5,4},{6,7},{7,6},{8,9},{9,8},{10,11... | collective-permute-start | bytes 491528 | tf_op jit(solution)/shard_map/ppermute | solution.py:486
  25.9 2.0 %collective-permute-start.16 = (bf16[640,128]{1,0:T(8,128)(2,1)S(1)}, bf16[640,128]{1,0:T(8,128)(2,1)S(1)}, u32[]{:S(2)}, u32[]{:S(2)}) collective-permute-start(bf16[640,128]{1,0:T(8,128)(2,1)S(1)} %collective-permute-done.9.rest_2_), channel_id=1, source_target_pairs={{0,1},{1,0},{2,3},{3,2},{4,5},{5,4},{6,7},{7,6},{8,9},{9,8},{10,11... | collective-permute-start | bytes 491528 | tf_op jit(solution)/shard_map/ppermute | solution.py:486
  26.6 1.5 %collective-permute-start.15 = (bf16[640,128]{1,0:T(8,128)(2,1)S(1)}, bf16[640,128]{1,0:T(8,128)(2,1)S(1)}, u32[]{:S(2)}, u32[]{:S(2)}) collective-permute-start(bf16[640,128]{1,0:T(8,128)(2,1)S(1)} %collective-permute-done.8.rest_1_), channel_id=1, source_target_pairs={{0,1},{1,0},{2,3},{3,2},{4,5},{5,4},{6,7},{7,6},{8,9},{9,8},{10,11... | collective-permute-start | bytes 491528 | tf_op jit(solution)/shard_map/ppermute | solution.py:486
  27.8 1.4 %collective-permute-start.13 = (bf16[640,128]{1,0:T(8,128)(2,1)S(1)}, bf16[640,128]{1,0:T(8,128)(2,1)S(1)}, u32[]{:S(2)}, u32[]{:S(2)}) collective-permute-start(bf16[640,128]{1,0:T(8,128)(2,1)S(1)} %collective-permute-done.7.rest_0_), channel_id=1, source_target_pairs={{0,1},{1,0},{2,3},{3,2},{4,5},{5,4},{6,7},{7,6},{8,9},{9,8},{10,11... | collective-permute-start | bytes 491528 | tf_op jit(solution)/shard_map/ppermute | solution.py:486
  29.7 6.4 %collective-permute-start.17 = (bf16[656,128]{1,0:T(8,128)(2,1)S(1)}, bf16[656,128]{1,0:T(8,128)(2,1)S(1)}, u32[]{:S(2)}, u32[]{:S(2)}) collective-permute-start(bf16[656,128]{1,0:T(8,128)(2,1)S(1)} %project.1.token_ref.rest_0_), channel_id=1, source_target_pairs={{0,4},{1,5},{2,6},{3,7},{4,0},{5,1},{6,2},{7,3},{8,12},{9,13},{10,... | collective-permute-start | bytes 503816 | tf_op jit(solution)/shard_map/ppermute | solution.py:486
  30.5 7.2 %collective-permute-start.18 = (bf16[656,128]{1,0:T(8,128)(2,1)S(1)}, bf16[656,128]{1,0:T(8,128)(2,1)S(1)}, u32[]{:S(2)}, u32[]{:S(2)}) collective-permute-start(bf16[656,128]{1,0:T(8,128)(2,1)S(1)} %project.1.token_ref.rest_0_), channel_id=1, source_target_pairs={{0,2},{1,3},{2,0},{3,1},{4,6},{5,7},{6,4},{7,5},{8,10},{9,11},{10,... | collective-permute-start | bytes 503816 | tf_op jit(solution)/shard_map/ppermute | solution.py:486
  31.2 9.7 %collective-permute-start.22 = (bf16[656,128]{1,0:T(8,128)(2,1)S(1)}, bf16[656,128]{1,0:T(8,128)(2,1)S(1)}, u32[]{:S(2)}, u32[]{:S(2)}) collective-permute-start(bf16[656,128]{1,0:T(8,128)(2,1)S(1)} %project.1.token_ref.rest_0_), channel_id=1, source_target_pairs={{0,6},{1,7},{2,4},{3,5},{4,2},{5,3},{6,0},{7,1},{8,14},{9,15},{10,... | collective-permute-start | bytes 503816 | tf_op jit(solution)/shard_map/ppermute | solution.py:486
  34.6 4.3 %collective-permute-start.19 = (bf16[656,128]{1,0:T(8,128)(2,1)S(1)}, bf16[656,128]{1,0:T(8,128)(2,1)S(1)}, u32[]{:S(2)}, u32[]{:S(2)}) collective-permute-start(bf16[656,128]{1,0:T(8,128)(2,1)S(1)} %project.1.token_ref.rest_0_), channel_id=1, source_target_pairs={{0,1},{1,0},{2,3},{3,2},{4,5},{5,4},{6,7},{7,6},{8,9},{9,8},{10,11... | collective-permute-start | bytes 503816 | tf_op jit(solution)/shard_map/ppermute | solution.py:486
  36.0 4.8 %collective-permute-start.20 = (bf16[656,128]{1,0:T(8,128)(2,1)S(1)}, bf16[656,128]{1,0:T(8,128)(2,1)S(1)}, u32[]{:S(2)}, u32[]{:S(2)}) collective-permute-start(bf16[656,128]{1,0:T(8,128)(2,1)S(1)} %collective-permute-done.17.rest_1_), channel_id=1, source_target_pairs={{0,1},{1,0},{2,3},{3,2},{4,5},{5,4},{6,7},{7,6},{8,9},{9,8},{10,11... | collective-permute-start | bytes 503816 | tf_op jit(solution)/shard_map/ppermute | solution.py:486
  37.6 3.2 %collective-permute-start.21 = (bf16[656,128]{1,0:T(8,128)(2,1)S(1)}, bf16[656,128]{1,0:T(8,128)(2,1)S(1)}, u32[]{:S(2)}, u32[]{:S(2)}) collective-permute-start(bf16[656,128]{1,0:T(8,128)(2,1)S(1)} %collective-permute-done.18.rest_2_), channel_id=1, source_target_pairs={{0,1},{1,0},{2,3},{3,2},{4,5},{5,4},{6,7},{7,6},{8,9},{9,8},{10,11... | collective-permute-start | bytes 503816 | tf_op jit(solution)/shard_map/ppermute | solution.py:486
  40.8 1.4 %collective-permute-start.23 = (bf16[656,128]{1,0:T(8,128)(2,1)S(1)}, bf16[656,128]{1,0:T(8,128)(2,1)S(1)}, u32[]{:S(2)}, u32[]{:S(2)}) collective-permute-start(bf16[656,128]{1,0:T(8,128)(2,1)S(1)} %collective-permute-done.22.rest_6_), channel_id=1, source_target_pairs={{0,1},{1,0},{2,3},{3,2},{4,5},{5,4},{6,7},{7,6},{8,9},{9,8},{10,11... | collective-permute-start | bytes 503816 | tf_op jit(solution)/shard_map/ppermute | solution.py:486
  (2 other events, 12.5 us)

commit v23 on v21

--- a/solution.py
+++ b/solution.py
@@ -122,8 +122,8 @@
 REST = HPAIR - WIDE
 MAIN = ROWS * WIDE
 NOTES = 16
-RECEIVERS = ((0, 0), (4, 2), (2, 4), (6, 6), (7, 7), (3, 5), (5, 3), (1, 1))
-SENDERS = ((0, 0), (4, 2), (2, 4), (6, 6), (7, 7), (5, 3), (3, 5), (1, 1))
+RECEIVERS = ((0, 0), (4, 2), (1, 1), (2, 4), (6, 6), (7, 7), (3, 5), (5, 3))
+SENDERS = ((0, 0), (4, 2), (1, 1), (2, 4), (6, 6), (7, 7), (5, 3), (3, 5))
 OWNERS = (0, 4, 2, 1, 5, 3, 6, 7)
 ROOT = math.log2(math.e) / math.sqrt(HDIM)
 BF16 = jnp.bfloat16

time: 43.8 us -> 43.3 us (0.989)
    ppermute x2, waiting for transfers between devices: 2.93 us -> 2.33 us  [turn(): return lax.ppermute(value, ('page', 'row'), pairs)]
  transfers between devices with their start and end apart: 24 -> 24, of which waited for: 10 -> 9; matrix products, arithmetic and copies ran while one was open for 0% -> 0% of each run, Pallas kernels for 18% -> 18%
where the time goes in v23:
time: 43.3 us; the launch traced here: 43.1 us
  starting transfers between devices  21.1 us (49%)
  Pallas kernels  11.4 us (26%)
  waiting for transfers between devices  10.4 us (24%)
    ppermute x22, starting transfers between devices, swap(): lax.ppermute(value, 'row', [(row, row ^ (odd if row % 2 else even)) for r...  16.9 us
    ppermute x22, waiting for transfers between devices, swap(): lax.ppermute(value, 'row', [(row, row ^ (odd if row % 2 else even)) for r...  8.06 us
    ppermute x2, starting transfers between devices, turn(): return lax.ppermute(value, ('page', 'row'), pairs)  4.22 us
    ppermute x2, waiting for transfers between devices, turn(): return lax.ppermute(value, ('page', 'row'), pairs)  2.33 us
    pallas_call x1, Pallas kernels, local_eight(): kernel(spread_kernel, 'spread', [shape(band, 4 * HPAIR)] * ROWS + [shape(...  1.77 us
    pallas_call x1, Pallas kernels, local_eight(): kernel(tail_kernel, 'merge_tail', [shape(units, MAIN), shape(units, 1, dt...  1.39 us
    pallas_call x1, Pallas kernels, local_eight(): kernel(merge_kernel, 'merge', shape(1, units, groups), [pltpu.VMEM((units...  1.36 us
    pallas_call x1, Pallas kernels, local_eight(): kernel(attend_kernel, 'attend', shape(piece, WIDE), [pltpu.VMEM((patches,...  1.34 us
  transfers between devices with their start and end apart: 24, of which 9 were waited for; matrix products, arithmetic and copies ran while one was open for 0% of the time, Pallas kernels for 18%

profile of v23, /device:TPU:0, one launch (start us, length us, event | category | flops | bytes accessed | tf_op | source)
XLA Modules:
  0.0 43.1 jit_solution(5516708205031956371)
XLA Ops:
  0.0 1.8 %spread.1 = (bf16[64,640]{1,0:T(8,128)(2,1)S(1)}, bf16[64,640]{1,0:T(8,128)(2,1)S(1)}, bf16[64,640]{1,0:T(8,128)(2,1)S(1)}, bf16[64,640]{1,0:T(8,128)(2,1)S(1)},...) custom-call(bf16[1,64,3840]{2,1,0:T(8,128)(2,1)} %qkv_hbm.1, ...), custom_call_target="tpu_custom_call" | custom-call | bytes 1048576 | tf_op jit(solution)/shard_map/spread/pallas_call | solution.py:509
  1.8 3.0 %collective-permute-start = (bf16[64,640]{1,0:T(8,128)(2,1)S(1)}, bf16[64,640]{1,0:T(8,128)(2,1)S(1)}, u32[]{:S(2)}, u32[]{:S(2)}) collective-permute-start(bf16[64,640]{1,0:T(8,128)(2,1)S(1)} %get-tuple-element.33), channel_id=1, source_target_pairs={{0,4},{1,3},{2,6},{3,1},{4,0},{5,7},{6,2},{7,5},{8,12},{9,11},{10,... | collective-permute-start | bytes 245768 | tf_op jit(solution)/shard_map/ppermute | solution.py:484
  4.8 1.5 %collective-permute-start.2 = (bf16[64,640]{1,0:T(8,128)(2,1)S(1)}, bf16[64,640]{1,0:T(8,128)(2,1)S(1)}, u32[]{:S(2)}, u32[]{:S(2)}) collective-permute-start(bf16[64,640]{1,0:T(8,128)(2,1)S(1)} %get-tuple-element.38), channel_id=1, source_target_pairs={{0,2},{1,5},{2,0},{3,7},{4,6},{5,1},{6,4},{7,3},{8,10},{9,13},{10,... | collective-permute-start | bytes 245768 | tf_op jit(solution)/shard_map/ppermute | solution.py:484
  6.3 1.0 %collective-permute-start.3 = (bf16[64,640]{1,0:T(8,128)(2,1)S(1)}, bf16[64,640]{1,0:T(8,128)(2,1)S(1)}, u32[]{:S(2)}, u32[]{:S(2)}) collective-permute-start(bf16[64,640]{1,0:T(8,128)(2,1)S(1)} %get-tuple-element.39), channel_id=1, source_target_pairs={{0,6},{1,7},{2,4},{3,5},{4,2},{5,3},{6,0},{7,1},{8,14},{9,15},{10,... | collective-permute-start | bytes 245768 | tf_op jit(solution)/shard_map/ppermute | solution.py:484
  7.8 1.6 %collective-permute-start.5 = (bf16[64,640]{1,0:T(8,128)(2,1)S(1)}, bf16[64,640]{1,0:T(8,128)(2,1)S(1)}, u32[]{:S(2)}, u32[]{:S(2)}) collective-permute-start(bf16[64,640]{1,0:T(8,128)(2,1)S(1)} %get-tuple-element.41), channel_id=1, source_target_pairs={{0,3},{1,4},{2,1},{3,6},{4,7},{5,0},{6,5},{7,2},{8,11},{9,12},{10,... | collective-permute-start | bytes 245768 | tf_op jit(solution)/shard_map/ppermute | solution.py:484
  9.8 1.6 %collective-permute-start.10 = (bf16[800,128]{1,0:T(8,128)(2,1)S(1)}, bf16[800,128]{1,0:T(8,128)(2,1)S(1)}, u32[]{:S(2)}, u32[]{:S(2)}) collective-permute-start(bf16[800,128]{1,0:T(8,128)(2,1)S(1)} %get-tuple-element.43), channel_id=1, source_target_pairs={{0,8},{1,25},{2,10},{3,27},{4,12},{5,29},{6,14},{7,31},{8,16},{9,1... | collective-permute-start | bytes 614408 | tf_op jit(solution)/shard_map/ppermute | solution.py:493
  12.2 2.6 %collective-permute-start.12 = (bf16[400,128]{1,0:T(8,128)(2,1)S(1)}, bf16[400,128]{1,0:T(8,128)(2,1)S(1)}, u32[]{:S(2)}, u32[]{:S(2)}) collective-permute-start(bf16[400,128]{1,0:T(8,128)(2,1)S(1)} %get-tuple-element.44.rest_8_), channel_id=1, source_target_pairs={{0,16},{1,17},{2,18},{3,19},{4,20},{5,21},{6,22},{7,23},{8,24},{9,... | collective-permute-start | bytes 307208 | tf_op jit(solution)/shard_map/ppermute | solution.py:493
  15.0 1.3 %attend.1.token_ref.rest_0_ = bf16[640,128]{1,0:T(8,128)(2,1)S(1)} custom-call(bf16[512,512]{1,0:T(8,128)(2,1)S(1)} %get-tuple-element.35.select_ref, f32[1,512]{1,0:T(1,128)S(1)} %get-tuple-element.36.dead_ref, bf16[64,640]{1,0:T(8,128)(2,1)S(1)} %get-tuple-element.37.rest_0_, bf16[64,640]{1,0:T(8,128)(2,1)S(1)} %collective-permute-done.rest_0_.rest_1_, ...), custom_call_target="tpu_custom_call" | custom-call | flops 21474836480 | bytes 1048576 | tf_op jit(solution)/shard_map/attend/pallas_call | solution.py:538
  16.3 1.3 %collective-permute-start.8 = (bf16[640,128]{1,0:T(8,128)(2,1)S(1)}, bf16[640,128]{1,0:T(8,128)(2,1)S(1)}, u32[]{:S(2)}, u32[]{:S(2)}) collective-permute-start(bf16[640,128]{1,0:T(8,128)(2,1)S(1)} %attend.1.token_ref.rest_0_), channel_id=1, source_target_pairs={{0,4},{1,5},{2,6},{3,7},{4,0},{5,1},{6,2},{7,3},{8,12},{9,13},{10,... | collective-permute-start | bytes 491528 | tf_op jit(solution)/shard_map/ppermute | solution.py:484
  17.6 1.5 %collective-permute-start.9 = (bf16[640,128]{1,0:T(8,128)(2,1)S(1)}, bf16[640,128]{1,0:T(8,128)(2,1)S(1)}, u32[]{:S(2)}, u32[]{:S(2)}) collective-permute-start(bf16[640,128]{1,0:T(8,128)(2,1)S(1)} %attend.1.token_ref.rest_0_), channel_id=1, source_target_pairs={{0,2},{1,3},{2,0},{3,1},{4,6},{5,7},{6,4},{7,5},{8,10},{9,11},{10,... | collective-permute-start | bytes 491528 | tf_op jit(solution)/shard_map/ppermute | solution.py:484
  19.9 2.3 %collective-permute-done.12.rest_9_ = bf16[400,128]{1,0:T(8,128)(2,1)S(1)} collective-permute-done((bf16[400,128]{1,0:T(8,128)(2,1)S(1)}, bf16[400,128]{1,0:T(8,128)(2,1)S(1)}, u32[]{:S(2)}, u32[]{:S(2)}) %collective-permute-start.12) | collective-permute-done | bytes 102432 | tf_op jit(solution)/shard_map/ppermute | solution.py:493
  22.2 1.2 %ready.1 = (f32[512,160]{1,0:T(8,128)S(1)}, f32[1,160]{1,0:T(1,128)S(1)}, bf16[1024,160]{1,0:T(8,128)(2,1)S(1)}, bf16[4,1024,160]{2,1,0:T(8,128)(2,1)S(1)}) custom-call(bf16[512,512]{1,0:T(8,128)(2,1)S(1)} %get-tuple-element.35.select_ref, f32[1280]{0:T(1024)} %gain_hbm.1, bf16[640,128]{1,0:T(8,128)(2,1)S(1)} %attend.1.token_ref.rest_0_, ...), custom_call_target="tpu_custom_call" | custom-call | flops 10737418240 | bytes 4194304 | tf_op jit(solution)/shard_map/ready/pallas_call | solution.py:548
  23.5 1.4 %collective-permute-start.14 = (bf16[640,128]{1,0:T(8,128)(2,1)S(1)}, bf16[640,128]{1,0:T(8,128)(2,1)S(1)}, u32[]{:S(2)}, u32[]{:S(2)}) collective-permute-start(bf16[640,128]{1,0:T(8,128)(2,1)S(1)} %attend.1.token_ref.rest_0_), channel_id=1, source_target_pairs={{0,1},{1,0},{2,3},{3,2},{4,5},{5,4},{6,7},{7,6},{8,9},{9,8},{10,11... | collective-permute-start | bytes 491528 | tf_op jit(solution)/shard_map/ppermute | solution.py:484
  26.1 1.2 %collective-permute-done.7.rest_0_ = bf16[640,128]{1,0:T(8,128)(2,1)S(1)} collective-permute-done((bf16[640,128]{1,0:T(8,128)(2,1)S(1)}, bf16[640,128]{1,0:T(8,128)(2,1)S(1)}, u32[]{:S(2)}, u32[]{:S(2)}) %collective-permute-start.7) | collective-permute-done | bytes 163872 | tf_op jit(solution)/shard_map/ppermute | solution.py:484
  29.2 1.0 %collective-permute-start.17 = (bf16[656,128]{1,0:T(8,128)(2,1)S(1)}, bf16[656,128]{1,0:T(8,128)(2,1)S(1)}, u32[]{:S(2)}, u32[]{:S(2)}) collective-permute-start(bf16[656,128]{1,0:T(8,128)(2,1)S(1)} %project.1.token_ref.rest_0_), channel_id=1, source_target_pairs={{0,4},{1,5},{2,6},{3,7},{4,0},{5,1},{6,2},{7,3},{8,12},{9,13},{10,... | collective-permute-start | bytes 503816 | tf_op jit(solution)/shard_map/ppermute | solution.py:484
  30.2 1.5 %collective-permute-start.18 = (bf16[656,128]{1,0:T(8,128)(2,1)S(1)}, bf16[656,128]{1,0:T(8,128)(2,1)S(1)}, u32[]{:S(2)}, u32[]{:S(2)}) collective-permute-start(bf16[656,128]{1,0:T(8,128)(2,1)S(1)} %project.1.token_ref.rest_0_), channel_id=1, source_target_pairs={{0,2},{1,3},{2,0},{3,1},{4,6},{5,7},{6,4},{7,5},{8,10},{9,11},{10,... | collective-permute-start | bytes 503816 | tf_op jit(solution)/shard_map/ppermute | solution.py:484
  31.7 1.0 %collective-permute-start.22 = (bf16[656,128]{1,0:T(8,128)(2,1)S(1)}, bf16[656,128]{1,0:T(8,128)(2,1)S(1)}, u32[]{:S(2)}, u32[]{:S(2)}) collective-permute-start(bf16[656,128]{1,0:T(8,128)(2,1)S(1)} %project.1.token_ref.rest_0_), channel_id=1, source_target_pairs={{0,6},{1,7},{2,4},{3,5},{4,2},{5,3},{6,0},{7,1},{8,14},{9,15},{10,... | collective-permute-start | bytes 503816 | tf_op jit(solution)/shard_map/ppermute | solution.py:484
  32.7 1.4 %merge_tail.1 = (bf16[640,1024]{1,0:T(8,128)(2,1)S(1)}, f32[640,1]{1,0:T(8,128)S(1)}) custom-call(bf16[640,5120]{1,0:T(8,128)(2,1)S(1)} %bitcast.1, f32[640]{0:T(1024)} %bias_hbm.1, bf16[656,128]{1,0:T(8,128)(2,1)S(1)} %project.1.token_ref.rest_0_), custom_call_target="tpu_custom_call" | custom-call | bytes 4194304 | tf_op jit(solution)/shard_map/merge_tail/pallas_call | solution.py:580
  34.2 1.4 %collective-permute-done.17.rest_1_ = bf16[656,128]{1,0:T(8,128)(2,1)S(1)} collective-permute-done((bf16[656,128]{1,0:T(8,128)(2,1)S(1)}, bf16[656,128]{1,0:T(8,128)(2,1)S(1)}, u32[]{:S(2)}, u32[]{:S(2)}) %collective-permute-start.17) | collective-permute-done | bytes 167968 | tf_op jit(solution)/shard_map/ppermute | solution.py:484
  35.5 1.8 %collective-permute-done.18.rest_2_ = bf16[656,128]{1,0:T(8,128)(2,1)S(1)} collective-permute-done((bf16[656,128]{1,0:T(8,128)(2,1)S(1)}, bf16[656,128]{1,0:T(8,128)(2,1)S(1)}, u32[]{:S(2)}, u32[]{:S(2)}) %collective-permute-start.18) | collective-permute-done | bytes 167968 | tf_op jit(solution)/shard_map/ppermute | solution.py:484
  37.4 1.3 %merge_first.1.rest_3_ = f32[4,640,128]{2,1,0:T(8,128)S(1)} custom-call(bf16[656,128]{1,0:T(8,128)(2,1)S(1)} %project.1.token_ref.rest_0_, bf16[656,128]{1,0:T(8,128)(2,1)S(1)} %collective-permute-done.17.rest_1_, bf16[656,128]{1,0:T(8,128)(2,1)S(1)} %collective-permute-done.18.rest_2_, bf16[640,5120]{1,0:T(8,128)(2,1)S(1)} %bitcast.1, ...), custom_call_target="tpu_custom_call" | custom-call | flops 1 | bytes 1 | tf_op jit(solution)/shard_map/merge_first/pallas_call | solution.py:591
  38.7 1.7 %collective-permute-done.22.rest_6_ = bf16[656,128]{1,0:T(8,128)(2,1)S(1)} collective-permute-done((bf16[656,128]{1,0:T(8,128)(2,1)S(1)}, bf16[656,128]{1,0:T(8,128)(2,1)S(1)}, u32[]{:S(2)}, u32[]{:S(2)}) %collective-permute-start.22) | collective-permute-done | bytes 167968 | tf_op jit(solution)/shard_map/ppermute | solution.py:484
  40.3 1.3 %merge_second.1.rest_8_ = f32[4,640,128]{2,1,0:T(8,128)S(1)} custom-call(bf16[656,128]{1,0:T(8,128)(2,1)S(1)} %collective-permute-done.19.rest_0_.rest_3_, bf16[656,128]{1,0:T(8,128)(2,1)S(1)} %collective-permute-done.20.rest_1_.rest_4_, bf16[656,128]{1,0:T(8,128)(2,1)S(1)} %collective-permute-done.21.rest_2_.rest_5_, ...), custom_call_target="tpu_custom_call" | custom-call | flops 1 | bytes 1 | tf_op jit(solution)/shard_map/merge_second/pallas_call | solution.py:595
  41.7 1.4 %merge.1 = bf16[1,640,128]{2,1,0:T(8,128)(2,1)} custom-call(bf16[656,128]{1,0:T(8,128)(2,1)S(1)} %project.1.token_ref.rest_0_, bf16[656,128]{1,0:T(8,128)(2,1)S(1)} %collective-permute-done.17.rest_1_, bf16[656,128]{1,0:T(8,128)(2,1)S(1)} %collective-permute-done.18.rest_2_, bf16[656,128]{1,0:T(8,128)(2,1)S(1)} %collective-permute-done.19.rest_0_.rest_3_, ...), custom_call_target="tpu_custom_call" | custom-call | flops 335544320 | bytes 8388608 | tf_op jit(solution)/shard_map/merge/pallas_call | solution.py:598
  (41 shorter events, 5.8 us)
Async XLA Ops:
  1.8 6.1 %collective-permute-start = (bf16[64,640]{1,0:T(8,128)(2,1)S(1)}, bf16[64,640]{1,0:T(8,128)(2,1)S(1)}, u32[]{:S(2)}, u32[]{:S(2)}) collective-permute-start(bf16[64,640]{1,0:T(8,128)(2,1)S(1)} %get-tuple-element.33), channel_id=1, source_target_pairs={{0,4},{1,3},{2,6},{3,1},{4,0},{5,7},{6,2},{7,5},{8,12},{9,11},{10,... | collective-permute-start | bytes 245768 | tf_op jit(solution)/shard_map/ppermute | solution.py:484
  4.8 4.7 %collective-permute-start.1 = (bf16[64,640]{1,0:T(8,128)(2,1)S(1)}, bf16[64,640]{1,0:T(8,128)(2,1)S(1)}, u32[]{:S(2)}, u32[]{:S(2)}) collective-permute-start(bf16[64,640]{1,0:T(8,128)(2,1)S(1)} %get-tuple-element.34), channel_id=1, source_target_pairs={{0,1},{1,0},{2,3},{3,2},{4,5},{5,4},{6,7},{7,6},{8,9},{9,8},{10,11... | collective-permute-start | bytes 245768 | tf_op jit(solution)/shard_map/ppermute | solution.py:484
  4.8 5.0 %collective-permute-start.2 = (bf16[64,640]{1,0:T(8,128)(2,1)S(1)}, bf16[64,640]{1,0:T(8,128)(2,1)S(1)}, u32[]{:S(2)}, u32[]{:S(2)}) collective-permute-start(bf16[64,640]{1,0:T(8,128)(2,1)S(1)} %get-tuple-element.38), channel_id=1, source_target_pairs={{0,2},{1,5},{2,0},{3,7},{4,6},{5,1},{6,4},{7,3},{8,10},{9,13},{10,... | collective-permute-start | bytes 245768 | tf_op jit(solution)/shard_map/ppermute | solution.py:484
  6.3 5.9 %collective-permute-start.3 = (bf16[64,640]{1,0:T(8,128)(2,1)S(1)}, bf16[64,640]{1,0:T(8,128)(2,1)S(1)}, u32[]{:S(2)}, u32[]{:S(2)}) collective-permute-start(bf16[64,640]{1,0:T(8,128)(2,1)S(1)} %get-tuple-element.39), channel_id=1, source_target_pairs={{0,6},{1,7},{2,4},{3,5},{4,2},{5,3},{6,0},{7,1},{8,14},{9,15},{10,... | collective-permute-start | bytes 245768 | tf_op jit(solution)/shard_map/ppermute | solution.py:484
  7.3 7.5 %collective-permute-start.4 = (bf16[64,640]{1,0:T(8,128)(2,1)S(1)}, bf16[64,640]{1,0:T(8,128)(2,1)S(1)}, u32[]{:S(2)}, u32[]{:S(2)}) collective-permute-start(bf16[64,640]{1,0:T(8,128)(2,1)S(1)} %get-tuple-element.40), channel_id=1, source_target_pairs={{0,7},{1,6},{2,5},{3,4},{4,3},{5,2},{6,1},{7,0},{8,15},{9,14},{10,... | collective-permute-start | bytes 245768 | tf_op jit(solution)/shard_map/ppermute | solution.py:484
  7.8 7.1 %collective-permute-start.5 = (bf16[64,640]{1,0:T(8,128)(2,1)S(1)}, bf16[64,640]{1,0:T(8,128)(2,1)S(1)}, u32[]{:S(2)}, u32[]{:S(2)}) collective-permute-start(bf16[64,640]{1,0:T(8,128)(2,1)S(1)} %get-tuple-element.41), channel_id=1, source_target_pairs={{0,3},{1,4},{2,1},{3,6},{4,7},{5,0},{6,5},{7,2},{8,11},{9,12},{10,... | collective-permute-start | bytes 245768 | tf_op jit(solution)/shard_map/ppermute | solution.py:484
  9.5 5.5 %collective-permute-start.6 = (bf16[64,640]{1,0:T(8,128)(2,1)S(1)}, bf16[64,640]{1,0:T(8,128)(2,1)S(1)}, u32[]{:S(2)}, u32[]{:S(2)}) collective-permute-start(bf16[64,640]{1,0:T(8,128)(2,1)S(1)} %get-tuple-element.42), channel_id=1, source_target_pairs={{0,5},{1,2},{2,7},{3,0},{4,1},{5,6},{6,3},{7,4},{8,13},{9,10},{10,... | collective-permute-start | bytes 245768 | tf_op jit(solution)/shard_map/ppermute | solution.py:484
  9.8 10.1 %collective-permute-start.10 = (bf16[800,128]{1,0:T(8,128)(2,1)S(1)}, bf16[800,128]{1,0:T(8,128)(2,1)S(1)}, u32[]{:S(2)}, u32[]{:S(2)}) collective-permute-start(bf16[800,128]{1,0:T(8,128)(2,1)S(1)} %get-tuple-element.43), channel_id=1, source_target_pairs={{0,8},{1,25},{2,10},{3,27},{4,12},{5,29},{6,14},{7,31},{8,16},{9,1... | collective-permute-start | bytes 614408 | tf_op jit(solution)/shard_map/ppermute | solution.py:493
  12.2 10.0 %collective-permute-start.12 = (bf16[400,128]{1,0:T(8,128)(2,1)S(1)}, bf16[400,128]{1,0:T(8,128)(2,1)S(1)}, u32[]{:S(2)}, u32[]{:S(2)}) collective-permute-start(bf16[400,128]{1,0:T(8,128)(2,1)S(1)} %get-tuple-element.44.rest_8_), channel_id=1, source_target_pairs={{0,16},{1,17},{2,18},{3,19},{4,20},{5,21},{6,22},{7,23},{8,24},{9,... | collective-permute-start | bytes 307208 | tf_op jit(solution)/shard_map/ppermute | solution.py:493
  16.3 8.8 %collective-permute-start.8 = (bf16[640,128]{1,0:T(8,128)(2,1)S(1)}, bf16[640,128]{1,0:T(8,128)(2,1)S(1)}, u32[]{:S(2)}, u32[]{:S(2)}) collective-permute-start(bf16[640,128]{1,0:T(8,128)(2,1)S(1)} %attend.1.token_ref.rest_0_), channel_id=1, source_target_pairs={{0,4},{1,5},{2,6},{3,7},{4,0},{5,1},{6,2},{7,3},{8,12},{9,13},{10,... | collective-permute-start | bytes 491528 | tf_op jit(solution)/shard_map/ppermute | solution.py:484
  17.6 7.2 %collective-permute-start.9 = (bf16[640,128]{1,0:T(8,128)(2,1)S(1)}, bf16[640,128]{1,0:T(8,128)(2,1)S(1)}, u32[]{:S(2)}, u32[]{:S(2)}) collective-permute-start(bf16[640,128]{1,0:T(8,128)(2,1)S(1)} %attend.1.token_ref.rest_0_), channel_id=1, source_target_pairs={{0,2},{1,3},{2,0},{3,1},{4,6},{5,7},{6,4},{7,5},{8,10},{9,11},{10,... | collective-permute-start | bytes 491528 | tf_op jit(solution)/shard_map/ppermute | solution.py:484
  19.2 8.1 %collective-permute-start.7 = (bf16[640,128]{1,0:T(8,128)(2,1)S(1)}, bf16[640,128]{1,0:T(8,128)(2,1)S(1)}, u32[]{:S(2)}, u32[]{:S(2)}) collective-permute-start(bf16[640,128]{1,0:T(8,128)(2,1)S(1)} %attend.1.token_ref.rest_0_), channel_id=1, source_target_pairs={{0,6},{1,7},{2,4},{3,5},{4,2},{5,3},{6,0},{7,1},{8,14},{9,15},{10,... | collective-permute-start | bytes 491528 | tf_op jit(solution)/shard_map/ppermute | solution.py:484
  19.9 5.0 %collective-permute-start.11 = (bf16[800,128]{1,0:T(8,128)(2,1)S(1)}, bf16[800,128]{1,0:T(8,128)(2,1)S(1)}, u32[]{:S(2)}, u32[]{:S(2)}) collective-permute-start(bf16[800,128]{1,0:T(8,128)(2,1)S(1)} %collective-permute-done.10.rest_10_), channel_id=1, source_target_pairs={{0,1},{1,0},{2,3},{3,2},{4,5},{5,4},{6,7},{7,6},{8,9},{9,8},{10,11... | collective-permute-start | bytes 614408 | tf_op jit(solution)/shard_map/ppermute | solution.py:484
  23.5 3.9 %collective-permute-start.14 = (bf16[640,128]{1,0:T(8,128)(2,1)S(1)}, bf16[640,128]{1,0:T(8,128)(2,1)S(1)}, u32[]{:S(2)}, u32[]{:S(2)}) collective-permute-start(bf16[640,128]{1,0:T(8,128)(2,1)S(1)} %attend.1.token_ref.rest_0_), channel_id=1, source_target_pairs={{0,1},{1,0},{2,3},{3,2},{4,5},{5,4},{6,7},{7,6},{8,9},{9,8},{10,11... | collective-permute-start | bytes 491528 | tf_op jit(solution)/shard_map/ppermute | solution.py:484
  24.8 2.5 %collective-permute-start.16 = (bf16[640,128]{1,0:T(8,128)(2,1)S(1)}, bf16[640,128]{1,0:T(8,128)(2,1)S(1)}, u32[]{:S(2)}, u32[]{:S(2)}) collective-permute-start(bf16[640,128]{1,0:T(8,128)(2,1)S(1)} %collective-permute-done.9.rest_2_), channel_id=1, source_target_pairs={{0,1},{1,0},{2,3},{3,2},{4,5},{5,4},{6,7},{7,6},{8,9},{9,8},{10,11... | collective-permute-start | bytes 491528 | tf_op jit(solution)/shard_map/ppermute | solution.py:484
  25.2 2.2 %collective-permute-start.15 = (bf16[640,128]{1,0:T(8,128)(2,1)S(1)}, bf16[640,128]{1,0:T(8,128)(2,1)S(1)}, u32[]{:S(2)}, u32[]{:S(2)}) collective-permute-start(bf16[640,128]{1,0:T(8,128)(2,1)S(1)} %collective-permute-done.8.rest_1_), channel_id=1, source_target_pairs={{0,1},{1,0},{2,3},{3,2},{4,5},{5,4},{6,7},{7,6},{8,9},{9,8},{10,11... | collective-permute-start | bytes 491528 | tf_op jit(solution)/shard_map/ppermute | solution.py:484
  27.3 1.4 %collective-permute-start.13 = (bf16[640,128]{1,0:T(8,128)(2,1)S(1)}, bf16[640,128]{1,0:T(8,128)(2,1)S(1)}, u32[]{:S(2)}, u32[]{:S(2)}) collective-permute-start(bf16[640,128]{1,0:T(8,128)(2,1)S(1)} %collective-permute-done.7.rest_0_), channel_id=1, source_target_pairs={{0,1},{1,0},{2,3},{3,2},{4,5},{5,4},{6,7},{7,6},{8,9},{9,8},{10,11... | collective-permute-start | bytes 491528 | tf_op jit(solution)/shard_map/ppermute | solution.py:484
  29.2 6.4 %collective-permute-start.17 = (bf16[656,128]{1,0:T(8,128)(2,1)S(1)}, bf16[656,128]{1,0:T(8,128)(2,1)S(1)}, u32[]{:S(2)}, u32[]{:S(2)}) collective-permute-start(bf16[656,128]{1,0:T(8,128)(2,1)S(1)} %project.1.token_ref.rest_0_), channel_id=1, source_target_pairs={{0,4},{1,5},{2,6},{3,7},{4,0},{5,1},{6,2},{7,3},{8,12},{9,13},{10,... | collective-permute-start | bytes 503816 | tf_op jit(solution)/shard_map/ppermute | solution.py:484
  30.2 7.2 %collective-permute-start.18 = (bf16[656,128]{1,0:T(8,128)(2,1)S(1)}, bf16[656,128]{1,0:T(8,128)(2,1)S(1)}, u32[]{:S(2)}, u32[]{:S(2)}) collective-permute-start(bf16[656,128]{1,0:T(8,128)(2,1)S(1)} %project.1.token_ref.rest_0_), channel_id=1, source_target_pairs={{0,2},{1,3},{2,0},{3,1},{4,6},{5,7},{6,4},{7,5},{8,10},{9,11},{10,... | collective-permute-start | bytes 503816 | tf_op jit(solution)/shard_map/ppermute | solution.py:484
  31.7 8.6 %collective-permute-start.22 = (bf16[656,128]{1,0:T(8,128)(2,1)S(1)}, bf16[656,128]{1,0:T(8,128)(2,1)S(1)}, u32[]{:S(2)}, u32[]{:S(2)}) collective-permute-start(bf16[656,128]{1,0:T(8,128)(2,1)S(1)} %project.1.token_ref.rest_0_), channel_id=1, source_target_pairs={{0,6},{1,7},{2,4},{3,5},{4,2},{5,3},{6,0},{7,1},{8,14},{9,15},{10,... | collective-permute-start | bytes 503816 | tf_op jit(solution)/shard_map/ppermute | solution.py:484
  34.1 4.5 %collective-permute-start.19 = (bf16[656,128]{1,0:T(8,128)(2,1)S(1)}, bf16[656,128]{1,0:T(8,128)(2,1)S(1)}, u32[]{:S(2)}, u32[]{:S(2)}) collective-permute-start(bf16[656,128]{1,0:T(8,128)(2,1)S(1)} %project.1.token_ref.rest_0_), channel_id=1, source_target_pairs={{0,1},{1,0},{2,3},{3,2},{4,5},{5,4},{6,7},{7,6},{8,9},{9,8},{10,11... | collective-permute-start | bytes 503816 | tf_op jit(solution)/shard_map/ppermute | solution.py:484
  35.5 4.8 %collective-permute-start.20 = (bf16[656,128]{1,0:T(8,128)(2,1)S(1)}, bf16[656,128]{1,0:T(8,128)(2,1)S(1)}, u32[]{:S(2)}, u32[]{:S(2)}) collective-permute-start(bf16[656,128]{1,0:T(8,128)(2,1)S(1)} %collective-permute-done.17.rest_1_), channel_id=1, source_target_pairs={{0,1},{1,0},{2,3},{3,2},{4,5},{5,4},{6,7},{7,6},{8,9},{9,8},{10,11... | collective-permute-start | bytes 503816 | tf_op jit(solution)/shard_map/ppermute | solution.py:484
  37.4 3.0 %collective-permute-start.21 = (bf16[656,128]{1,0:T(8,128)(2,1)S(1)}, bf16[656,128]{1,0:T(8,128)(2,1)S(1)}, u32[]{:S(2)}, u32[]{:S(2)}) collective-permute-start(bf16[656,128]{1,0:T(8,128)(2,1)S(1)} %collective-permute-done.18.rest_2_), channel_id=1, source_target_pairs={{0,1},{1,0},{2,3},{3,2},{4,5},{5,4},{6,7},{7,6},{8,9},{9,8},{10,11... | collective-permute-start | bytes 503816 | tf_op jit(solution)/shard_map/ppermute | solution.py:484
  40.3 1.4 %collective-permute-start.23 = (bf16[656,128]{1,0:T(8,128)(2,1)S(1)}, bf16[656,128]{1,0:T(8,128)(2,1)S(1)}, u32[]{:S(2)}, u32[]{:S(2)}) collective-permute-start(bf16[656,128]{1,0:T(8,128)(2,1)S(1)} %collective-permute-done.22.rest_6_), channel_id=1, source_target_pairs={{0,1},{1,0},{2,3},{3,2},{4,5},{5,4},{6,7},{7,6},{8,9},{9,8},{10,11... | collective-permute-start | bytes 503816 | tf_op jit(solution)/shard_map/ppermute | solution.py:484
  (2 other events, 13.6 us)

commit v24 on v23

--- a/solution.py
+++ b/solution.py
@@ -122,8 +122,8 @@
 REST = HPAIR - WIDE
 MAIN = ROWS * WIDE
 NOTES = 16
-RECEIVERS = ((0, 0), (4, 2), (1, 1), (2, 4), (6, 6), (7, 7), (3, 5), (5, 3))
-SENDERS = ((0, 0), (4, 2), (1, 1), (2, 4), (6, 6), (7, 7), (5, 3), (3, 5))
+RECEIVERS = ((0, 0), (4, 2), (2, 4), (1, 1), (6, 6), (7, 7), (3, 5), (5, 3))
+SENDERS = ((0, 0), (4, 2), (2, 4), (1, 1), (6, 6), (7, 7), (5, 3), (3, 5))
 OWNERS = (0, 4, 2, 1, 5, 3, 6, 7)
 ROOT = math.log2(math.e) / math.sqrt(HDIM)
 BF16 = jnp.bfloat16

time: 43.3 us -> 43.8 us (1.012)
  starting transfers between devices: 21.1 us -> 21.9 us
    ppermute x22, waiting for transfers between devices: 8.06 us -> 7.19 us  [swap(): lax.ppermute(value, 'row', [(row, row ^ (odd if row % 2 else even)) for r...]
    ppermute x22, starting transfers between devices: 16.9 us -> 17.7 us  [swap(): lax.ppermute(value, 'row', [(row, row ^ (odd if row % 2 else even)) for r...]
    ppermute x2, waiting for transfers between devices: 2.33 us -> 2.95 us  [turn(): return lax.ppermute(value, ('page', 'row'), pairs)]
where the time goes in v24:
time: 43.8 us; the launch traced here: 43.6 us
  starting transfers between devices  21.9 us (50%)
  Pallas kernels  11.4 us (26%)
  waiting for transfers between devices  10.1 us (23%)
    ppermute x22, starting transfers between devices, swap(): lax.ppermute(value, 'row', [(row, row ^ (odd if row % 2 else even)) for r...  17.7 us
    ppermute x22, waiting for transfers between devices, swap(): lax.ppermute(value, 'row', [(row, row ^ (odd if row % 2 else even)) for r...  7.19 us
    ppermute x2, starting transfers between devices, turn(): return lax.ppermute(value, ('page', 'row'), pairs)  4.22 us
    ppermute x2, waiting for transfers between devices, turn(): return lax.ppermute(value, ('page', 'row'), pairs)  2.95 us
    pallas_call x1, Pallas kernels, local_eight(): kernel(spread_kernel, 'spread', [shape(band, 4 * HPAIR)] * ROWS + [shape(...  1.77 us
    pallas_call x1, Pallas kernels, local_eight(): kernel(tail_kernel, 'merge_tail', [shape(units, MAIN), shape(units, 1, dt...  1.39 us
    pallas_call x1, Pallas kernels, local_eight(): kernel(merge_kernel, 'merge', shape(1, units, groups), [pltpu.VMEM((units...  1.36 us
    pallas_call x1, Pallas kernels, local_eight(): kernel(attend_kernel, 'attend', shape(piece, WIDE), [pltpu.VMEM((patches,...  1.34 us
  transfers between devices with their start and end apart: 24, of which 9 were waited for; matrix products, arithmetic and copies ran while one was open for 0% of the time, Pallas kernels for 18%

profile of v24, /device:TPU:0, one launch (start us, length us, event | category | flops | bytes accessed | tf_op | source)
XLA Modules:
  0.0 43.6 jit_solution(13507705821193854231)
XLA Ops:
  0.0 1.8 %spread.1 = (bf16[64,640]{1,0:T(8,128)(2,1)S(1)}, bf16[64,640]{1,0:T(8,128)(2,1)S(1)}, bf16[64,640]{1,0:T(8,128)(2,1)S(1)}, bf16[64,640]{1,0:T(8,128)(2,1)S(1)},...) custom-call(bf16[1,64,3840]{2,1,0:T(8,128)(2,1)} %qkv_hbm.1, ...), custom_call_target="tpu_custom_call" | custom-call | bytes 1048576 | tf_op jit(solution)/shard_map/spread/pallas_call | solution.py:509
  1.8 3.0 %collective-permute-start = (bf16[64,640]{1,0:T(8,128)(2,1)S(1)}, bf16[64,640]{1,0:T(8,128)(2,1)S(1)}, u32[]{:S(2)}, u32[]{:S(2)}) collective-permute-start(bf16[64,640]{1,0:T(8,128)(2,1)S(1)} %get-tuple-element.33), channel_id=1, source_target_pairs={{0,4},{1,3},{2,6},{3,1},{4,0},{5,7},{6,2},{7,5},{8,12},{9,11},{10,... | collective-permute-start | bytes 245768 | tf_op jit(solution)/shard_map/ppermute | solution.py:484
  4.8 1.5 %collective-permute-start.1 = (bf16[64,640]{1,0:T(8,128)(2,1)S(1)}, bf16[64,640]{1,0:T(8,128)(2,1)S(1)}, u32[]{:S(2)}, u32[]{:S(2)}) collective-permute-start(bf16[64,640]{1,0:T(8,128)(2,1)S(1)} %get-tuple-element.34), channel_id=1, source_target_pairs={{0,2},{1,5},{2,0},{3,7},{4,6},{5,1},{6,4},{7,3},{8,10},{9,13},{10,... | collective-permute-start | bytes 245768 | tf_op jit(solution)/shard_map/ppermute | solution.py:484
  6.4 2.7 %collective-permute-start.4 = (bf16[64,640]{1,0:T(8,128)(2,1)S(1)}, bf16[64,640]{1,0:T(8,128)(2,1)S(1)}, u32[]{:S(2)}, u32[]{:S(2)}) collective-permute-start(bf16[64,640]{1,0:T(8,128)(2,1)S(1)} %get-tuple-element.40), channel_id=1, source_target_pairs={{0,7},{1,6},{2,5},{3,4},{4,3},{5,2},{6,1},{7,0},{8,15},{9,14},{10,... | collective-permute-start | bytes 245768 | tf_op jit(solution)/shard_map/ppermute | solution.py:484
  9.5 1.3 %collective-permute-start.6 = (bf16[64,640]{1,0:T(8,128)(2,1)S(1)}, bf16[64,640]{1,0:T(8,128)(2,1)S(1)}, u32[]{:S(2)}, u32[]{:S(2)}) collective-permute-start(bf16[64,640]{1,0:T(8,128)(2,1)S(1)} %get-tuple-element.42), channel_id=1, source_target_pairs={{0,5},{1,2},{2,7},{3,0},{4,1},{5,6},{6,3},{7,4},{8,13},{9,10},{10,... | collective-permute-start | bytes 245768 | tf_op jit(solution)/shard_map/ppermute | solution.py:484
  11.0 1.6 %collective-permute-start.10 = (bf16[800,128]{1,0:T(8,128)(2,1)S(1)}, bf16[800,128]{1,0:T(8,128)(2,1)S(1)}, u32[]{:S(2)}, u32[]{:S(2)}) collective-permute-start(bf16[800,128]{1,0:T(8,128)(2,1)S(1)} %get-tuple-element.43), channel_id=1, source_target_pairs={{0,8},{1,25},{2,10},{3,27},{4,12},{5,29},{6,14},{7,31},{8,16},{9,1... | collective-permute-start | bytes 614408 | tf_op jit(solution)/shard_map/ppermute | solution.py:493
  12.6 2.6 %collective-permute-start.12 = (bf16[400,128]{1,0:T(8,128)(2,1)S(1)}, bf16[400,128]{1,0:T(8,128)(2,1)S(1)}, u32[]{:S(2)}, u32[]{:S(2)}) collective-permute-start(bf16[400,128]{1,0:T(8,128)(2,1)S(1)} %get-tuple-element.44.rest_8_), channel_id=1, source_target_pairs={{0,16},{1,17},{2,18},{3,19},{4,20},{5,21},{6,22},{7,23},{8,24},{9,... | collective-permute-start | bytes 307208 | tf_op jit(solution)/shard_map/ppermute | solution.py:493
  15.5 1.3 %attend.1.token_ref.rest_0_ = bf16[640,128]{1,0:T(8,128)(2,1)S(1)} custom-call(bf16[512,512]{1,0:T(8,128)(2,1)S(1)} %get-tuple-element.35.select_ref, f32[1,512]{1,0:T(1,128)S(1)} %get-tuple-element.36.dead_ref, bf16[64,640]{1,0:T(8,128)(2,1)S(1)} %get-tuple-element.37.rest_0_, bf16[64,640]{1,0:T(8,128)(2,1)S(1)} %collective-permute-done.rest_0_.rest_1_, ...), custom_call_target="tpu_custom_call" | custom-call | flops 21474836480 | bytes 1048576 | tf_op jit(solution)/shard_map/attend/pallas_call | solution.py:538
  17.6 1.0 %collective-permute-start.9 = (bf16[640,128]{1,0:T(8,128)(2,1)S(1)}, bf16[640,128]{1,0:T(8,128)(2,1)S(1)}, u32[]{:S(2)}, u32[]{:S(2)}) collective-permute-start(bf16[640,128]{1,0:T(8,128)(2,1)S(1)} %attend.1.token_ref.rest_0_), channel_id=1, source_target_pairs={{0,2},{1,3},{2,0},{3,1},{4,6},{5,7},{6,4},{7,5},{8,10},{9,11},{10,... | collective-permute-start | bytes 491528 | tf_op jit(solution)/shard_map/ppermute | solution.py:484
  18.6 1.8 %collective-permute-start.7 = (bf16[640,128]{1,0:T(8,128)(2,1)S(1)}, bf16[640,128]{1,0:T(8,128)(2,1)S(1)}, u32[]{:S(2)}, u32[]{:S(2)}) collective-permute-start(bf16[640,128]{1,0:T(8,128)(2,1)S(1)} %attend.1.token_ref.rest_0_), channel_id=1, source_target_pairs={{0,6},{1,7},{2,4},{3,5},{4,2},{5,3},{6,0},{7,1},{8,14},{9,15},{10,... | collective-permute-start | bytes 491528 | tf_op jit(solution)/shard_map/ppermute | solution.py:484
  20.7 2.7 %collective-permute-done.12.rest_9_ = bf16[400,128]{1,0:T(8,128)(2,1)S(1)} collective-permute-done((bf16[400,128]{1,0:T(8,128)(2,1)S(1)}, bf16[400,128]{1,0:T(8,128)(2,1)S(1)}, u32[]{:S(2)}, u32[]{:S(2)}) %collective-permute-start.12) | collective-permute-done | bytes 102432 | tf_op jit(solution)/shard_map/ppermute | solution.py:493
  23.3 1.2 %ready.1 = (f32[512,160]{1,0:T(8,128)S(1)}, f32[1,160]{1,0:T(1,128)S(1)}, bf16[1024,160]{1,0:T(8,128)(2,1)S(1)}, bf16[4,1024,160]{2,1,0:T(8,128)(2,1)S(1)}) custom-call(bf16[512,512]{1,0:T(8,128)(2,1)S(1)} %get-tuple-element.35.select_ref, f32[1280]{0:T(1024)} %gain_hbm.1, bf16[640,128]{1,0:T(8,128)(2,1)S(1)} %attend.1.token_ref.rest_0_, ...), custom_call_target="tpu_custom_call" | custom-call | flops 10737418240 | bytes 4194304 | tf_op jit(solution)/shard_map/ready/pallas_call | solution.py:548
  24.6 0.9 %collective-permute-start.14 = (bf16[640,128]{1,0:T(8,128)(2,1)S(1)}, bf16[640,128]{1,0:T(8,128)(2,1)S(1)}, u32[]{:S(2)}, u32[]{:S(2)}) collective-permute-start(bf16[640,128]{1,0:T(8,128)(2,1)S(1)} %attend.1.token_ref.rest_0_), channel_id=1, source_target_pairs={{0,1},{1,0},{2,3},{3,2},{4,5},{5,4},{6,7},{7,6},{8,9},{9,8},{10,11... | collective-permute-start | bytes 491528 | tf_op jit(solution)/shard_map/ppermute | solution.py:484
  26.7 1.0 %collective-permute-done.7.rest_0_ = bf16[640,128]{1,0:T(8,128)(2,1)S(1)} collective-permute-done((bf16[640,128]{1,0:T(8,128)(2,1)S(1)}, bf16[640,128]{1,0:T(8,128)(2,1)S(1)}, u32[]{:S(2)}, u32[]{:S(2)}) %collective-permute-start.7) | collective-permute-done | bytes 163872 | tf_op jit(solution)/shard_map/ppermute | solution.py:484
  28.3 0.9 %collective-permute-done.13.rest_1_ = bf16[640,128]{1,0:T(8,128)(2,1)S(1)} collective-permute-done((bf16[640,128]{1,0:T(8,128)(2,1)S(1)}, bf16[640,128]{1,0:T(8,128)(2,1)S(1)}, u32[]{:S(2)}, u32[]{:S(2)}) %collective-permute-start.13) | collective-permute-done | bytes 163872 | tf_op jit(solution)/shard_map/ppermute | solution.py:484
  30.1 1.3 %collective-permute-start.18 = (bf16[656,128]{1,0:T(8,128)(2,1)S(1)}, bf16[656,128]{1,0:T(8,128)(2,1)S(1)}, u32[]{:S(2)}, u32[]{:S(2)}) collective-permute-start(bf16[656,128]{1,0:T(8,128)(2,1)S(1)} %project.1.token_ref.rest_0_), channel_id=1, source_target_pairs={{0,2},{1,3},{2,0},{3,1},{4,6},{5,7},{6,4},{7,5},{8,10},{9,11},{10,... | collective-permute-start | bytes 503816 | tf_op jit(solution)/shard_map/ppermute | solution.py:484
  31.4 1.8 %collective-permute-start.22 = (bf16[656,128]{1,0:T(8,128)(2,1)S(1)}, bf16[656,128]{1,0:T(8,128)(2,1)S(1)}, u32[]{:S(2)}, u32[]{:S(2)}) collective-permute-start(bf16[656,128]{1,0:T(8,128)(2,1)S(1)} %project.1.token_ref.rest_0_), channel_id=1, source_target_pairs={{0,6},{1,7},{2,4},{3,5},{4,2},{5,3},{6,0},{7,1},{8,14},{9,15},{10,... | collective-permute-start | bytes 503816 | tf_op jit(solution)/shard_map/ppermute | solution.py:484
  33.2 1.4 %merge_tail.1 = (bf16[640,1024]{1,0:T(8,128)(2,1)S(1)}, f32[640,1]{1,0:T(8,128)S(1)}) custom-call(bf16[640,5120]{1,0:T(8,128)(2,1)S(1)} %bitcast.1, f32[640]{0:T(1024)} %bias_hbm.1, bf16[656,128]{1,0:T(8,128)(2,1)S(1)} %project.1.token_ref.rest_0_), custom_call_target="tpu_custom_call" | custom-call | bytes 4194304 | tf_op jit(solution)/shard_map/merge_tail/pallas_call | solution.py:580
  34.7 1.4 %collective-permute-done.17.rest_1_ = bf16[656,128]{1,0:T(8,128)(2,1)S(1)} collective-permute-done((bf16[656,128]{1,0:T(8,128)(2,1)S(1)}, bf16[656,128]{1,0:T(8,128)(2,1)S(1)}, u32[]{:S(2)}, u32[]{:S(2)}) %collective-permute-start.17) | collective-permute-done | bytes 167968 | tf_op jit(solution)/shard_map/ppermute | solution.py:484
  36.0 1.3 %collective-permute-done.18.rest_2_ = bf16[656,128]{1,0:T(8,128)(2,1)S(1)} collective-permute-done((bf16[656,128]{1,0:T(8,128)(2,1)S(1)}, bf16[656,128]{1,0:T(8,128)(2,1)S(1)}, u32[]{:S(2)}, u32[]{:S(2)}) %collective-permute-start.18) | collective-permute-done | bytes 167968 | tf_op jit(solution)/shard_map/ppermute | solution.py:484
  37.3 1.2 %merge_first.1.rest_3_ = f32[4,640,128]{2,1,0:T(8,128)S(1)} custom-call(bf16[656,128]{1,0:T(8,128)(2,1)S(1)} %project.1.token_ref.rest_0_, bf16[656,128]{1,0:T(8,128)(2,1)S(1)} %collective-permute-done.17.rest_1_, bf16[656,128]{1,0:T(8,128)(2,1)S(1)} %collective-permute-done.18.rest_2_, bf16[640,5120]{1,0:T(8,128)(2,1)S(1)} %bitcast.1, ...), custom_call_target="tpu_custom_call" | custom-call | flops 1 | bytes 1 | tf_op jit(solution)/shard_map/merge_first/pallas_call | solution.py:591
  38.6 2.3 %collective-permute-done.22.rest_6_ = bf16[656,128]{1,0:T(8,128)(2,1)S(1)} collective-permute-done((bf16[656,128]{1,0:T(8,128)(2,1)S(1)}, bf16[656,128]{1,0:T(8,128)(2,1)S(1)}, u32[]{:S(2)}, u32[]{:S(2)}) %collective-permute-start.22) | collective-permute-done | bytes 167968 | tf_op jit(solution)/shard_map/ppermute | solution.py:484
  40.8 1.3 %merge_second.1.rest_8_ = f32[4,640,128]{2,1,0:T(8,128)S(1)} custom-call(bf16[656,128]{1,0:T(8,128)(2,1)S(1)} %collective-permute-done.19.rest_0_.rest_3_, bf16[656,128]{1,0:T(8,128)(2,1)S(1)} %collective-permute-done.20.rest_1_.rest_4_, bf16[656,128]{1,0:T(8,128)(2,1)S(1)} %collective-permute-done.21.rest_2_.rest_5_, ...), custom_call_target="tpu_custom_call" | custom-call | flops 1 | bytes 1 | tf_op jit(solution)/shard_map/merge_second/pallas_call | solution.py:595
  42.2 1.4 %merge.1 = bf16[1,640,128]{2,1,0:T(8,128)(2,1)} custom-call(bf16[656,128]{1,0:T(8,128)(2,1)S(1)} %project.1.token_ref.rest_0_, bf16[656,128]{1,0:T(8,128)(2,1)S(1)} %collective-permute-done.17.rest_1_, bf16[656,128]{1,0:T(8,128)(2,1)S(1)} %collective-permute-done.18.rest_2_, bf16[656,128]{1,0:T(8,128)(2,1)S(1)} %collective-permute-done.19.rest_0_.rest_3_, ...), custom_call_target="tpu_custom_call" | custom-call | flops 335544320 | bytes 8388608 | tf_op jit(solution)/shard_map/merge/pallas_call | solution.py:598
  (41 shorter events, 4.8 us)
Async XLA Ops:
  1.8 7.3 %collective-permute-start = (bf16[64,640]{1,0:T(8,128)(2,1)S(1)}, bf16[64,640]{1,0:T(8,128)(2,1)S(1)}, u32[]{:S(2)}, u32[]{:S(2)}) collective-permute-start(bf16[64,640]{1,0:T(8,128)(2,1)S(1)} %get-tuple-element.33), channel_id=1, source_target_pairs={{0,4},{1,3},{2,6},{3,1},{4,0},{5,7},{6,2},{7,5},{8,12},{9,11},{10,... | collective-permute-start | bytes 245768 | tf_op jit(solution)/shard_map/ppermute | solution.py:484
  4.8 4.7 %collective-permute-start.1 = (bf16[64,640]{1,0:T(8,128)(2,1)S(1)}, bf16[64,640]{1,0:T(8,128)(2,1)S(1)}, u32[]{:S(2)}, u32[]{:S(2)}) collective-permute-start(bf16[64,640]{1,0:T(8,128)(2,1)S(1)} %get-tuple-element.34), channel_id=1, source_target_pairs={{0,2},{1,5},{2,0},{3,7},{4,6},{5,1},{6,4},{7,3},{8,10},{9,13},{10,... | collective-permute-start | bytes 245768 | tf_op jit(solution)/shard_map/ppermute | solution.py:484
  6.3 4.7 %collective-permute-start.2 = (bf16[64,640]{1,0:T(8,128)(2,1)S(1)}, bf16[64,640]{1,0:T(8,128)(2,1)S(1)}, u32[]{:S(2)}, u32[]{:S(2)}) collective-permute-start(bf16[64,640]{1,0:T(8,128)(2,1)S(1)} %get-tuple-element.38), channel_id=1, source_target_pairs={{0,1},{1,0},{2,3},{3,2},{4,5},{5,4},{6,7},{7,6},{8,9},{9,8},{10,11... | collective-permute-start | bytes 245768 | tf_op jit(solution)/shard_map/ppermute | solution.py:484
  6.3 6.3 %collective-permute-start.3 = (bf16[64,640]{1,0:T(8,128)(2,1)S(1)}, bf16[64,640]{1,0:T(8,128)(2,1)S(1)}, u32[]{:S(2)}, u32[]{:S(2)}) collective-permute-start(bf16[64,640]{1,0:T(8,128)(2,1)S(1)} %get-tuple-element.39), channel_id=1, source_target_pairs={{0,6},{1,7},{2,4},{3,5},{4,2},{5,3},{6,0},{7,1},{8,14},{9,15},{10,... | collective-permute-start | bytes 245768 | tf_op jit(solution)/shard_map/ppermute | solution.py:484
  6.4 8.9 %collective-permute-start.4 = (bf16[64,640]{1,0:T(8,128)(2,1)S(1)}, bf16[64,640]{1,0:T(8,128)(2,1)S(1)}, u32[]{:S(2)}, u32[]{:S(2)}) collective-permute-start(bf16[64,640]{1,0:T(8,128)(2,1)S(1)} %get-tuple-element.40), channel_id=1, source_target_pairs={{0,7},{1,6},{2,5},{3,4},{4,3},{5,2},{6,1},{7,0},{8,15},{9,14},{10,... | collective-permute-start | bytes 245768 | tf_op jit(solution)/shard_map/ppermute | solution.py:484
  9.1 6.4 %collective-permute-start.5 = (bf16[64,640]{1,0:T(8,128)(2,1)S(1)}, bf16[64,640]{1,0:T(8,128)(2,1)S(1)}, u32[]{:S(2)}, u32[]{:S(2)}) collective-permute-start(bf16[64,640]{1,0:T(8,128)(2,1)S(1)} %get-tuple-element.41), channel_id=1, source_target_pairs={{0,3},{1,4},{2,1},{3,6},{4,7},{5,0},{6,5},{7,2},{8,11},{9,12},{10,... | collective-permute-start | bytes 245768 | tf_op jit(solution)/shard_map/ppermute | solution.py:484
  9.5 6.0 %collective-permute-start.6 = (bf16[64,640]{1,0:T(8,128)(2,1)S(1)}, bf16[64,640]{1,0:T(8,128)(2,1)S(1)}, u32[]{:S(2)}, u32[]{:S(2)}) collective-permute-start(bf16[64,640]{1,0:T(8,128)(2,1)S(1)} %get-tuple-element.42), channel_id=1, source_target_pairs={{0,5},{1,2},{2,7},{3,0},{4,1},{5,6},{6,3},{7,4},{8,13},{9,10},{10,... | collective-permute-start | bytes 245768 | tf_op jit(solution)/shard_map/ppermute | solution.py:484
  11.0 9.6 %collective-permute-start.10 = (bf16[800,128]{1,0:T(8,128)(2,1)S(1)}, bf16[800,128]{1,0:T(8,128)(2,1)S(1)}, u32[]{:S(2)}, u32[]{:S(2)}) collective-permute-start(bf16[800,128]{1,0:T(8,128)(2,1)S(1)} %get-tuple-element.43), channel_id=1, source_target_pairs={{0,8},{1,25},{2,10},{3,27},{4,12},{5,29},{6,14},{7,31},{8,16},{9,1... | collective-permute-start | bytes 614408 | tf_op jit(solution)/shard_map/ppermute | solution.py:493
  12.6 10.7 %collective-permute-start.12 = (bf16[400,128]{1,0:T(8,128)(2,1)S(1)}, bf16[400,128]{1,0:T(8,128)(2,1)S(1)}, u32[]{:S(2)}, u32[]{:S(2)}) collective-permute-start(bf16[400,128]{1,0:T(8,128)(2,1)S(1)} %get-tuple-element.44.rest_8_), channel_id=1, source_target_pairs={{0,16},{1,17},{2,18},{3,19},{4,20},{5,21},{6,22},{7,23},{8,24},{9,... | collective-permute-start | bytes 307208 | tf_op jit(solution)/shard_map/ppermute | solution.py:493
  16.8 9.0 %collective-permute-start.8 = (bf16[640,128]{1,0:T(8,128)(2,1)S(1)}, bf16[640,128]{1,0:T(8,128)(2,1)S(1)}, u32[]{:S(2)}, u32[]{:S(2)}) collective-permute-start(bf16[640,128]{1,0:T(8,128)(2,1)S(1)} %attend.1.token_ref.rest_0_), channel_id=1, source_target_pairs={{0,4},{1,5},{2,6},{3,7},{4,0},{5,1},{6,2},{7,3},{8,12},{9,13},{10,... | collective-permute-start | bytes 491528 | tf_op jit(solution)/shard_map/ppermute | solution.py:484
  17.6 7.8 %collective-permute-start.9 = (bf16[640,128]{1,0:T(8,128)(2,1)S(1)}, bf16[640,128]{1,0:T(8,128)(2,1)S(1)}, u32[]{:S(2)}, u32[]{:S(2)}) collective-permute-start(bf16[640,128]{1,0:T(8,128)(2,1)S(1)} %attend.1.token_ref.rest_0_), channel_id=1, source_target_pairs={{0,2},{1,3},{2,0},{3,1},{4,6},{5,7},{6,4},{7,5},{8,10},{9,11},{10,... | collective-permute-start | bytes 491528 | tf_op jit(solution)/shard_map/ppermute | solution.py:484
  18.6 9.2 %collective-permute-start.7 = (bf16[640,128]{1,0:T(8,128)(2,1)S(1)}, bf16[640,128]{1,0:T(8,128)(2,1)S(1)}, u32[]{:S(2)}, u32[]{:S(2)}) collective-permute-start(bf16[640,128]{1,0:T(8,128)(2,1)S(1)} %attend.1.token_ref.rest_0_), channel_id=1, source_target_pairs={{0,6},{1,7},{2,4},{3,5},{4,2},{5,3},{6,0},{7,1},{8,14},{9,15},{10,... | collective-permute-start | bytes 491528 | tf_op jit(solution)/shard_map/ppermute | solution.py:484
  20.7 4.9 %collective-permute-start.11 = (bf16[800,128]{1,0:T(8,128)(2,1)S(1)}, bf16[800,128]{1,0:T(8,128)(2,1)S(1)}, u32[]{:S(2)}, u32[]{:S(2)}) collective-permute-start(bf16[800,128]{1,0:T(8,128)(2,1)S(1)} %collective-permute-done.10.rest_10_), channel_id=1, source_target_pairs={{0,1},{1,0},{2,3},{3,2},{4,5},{5,4},{6,7},{7,6},{8,9},{9,8},{10,11... | collective-permute-start | bytes 614408 | tf_op jit(solution)/shard_map/ppermute | solution.py:484
  24.6 3.2 %collective-permute-start.14 = (bf16[640,128]{1,0:T(8,128)(2,1)S(1)}, bf16[640,128]{1,0:T(8,128)(2,1)S(1)}, u32[]{:S(2)}, u32[]{:S(2)}) collective-permute-start(bf16[640,128]{1,0:T(8,128)(2,1)S(1)} %attend.1.token_ref.rest_0_), channel_id=1, source_target_pairs={{0,1},{1,0},{2,3},{3,2},{4,5},{5,4},{6,7},{7,6},{8,9},{9,8},{10,11... | collective-permute-start | bytes 491528 | tf_op jit(solution)/shard_map/ppermute | solution.py:484
  25.5 2.3 %collective-permute-start.16 = (bf16[640,128]{1,0:T(8,128)(2,1)S(1)}, bf16[640,128]{1,0:T(8,128)(2,1)S(1)}, u32[]{:S(2)}, u32[]{:S(2)}) collective-permute-start(bf16[640,128]{1,0:T(8,128)(2,1)S(1)} %collective-permute-done.9.rest_2_), channel_id=1, source_target_pairs={{0,1},{1,0},{2,3},{3,2},{4,5},{5,4},{6,7},{7,6},{8,9},{9,8},{10,11... | collective-permute-start | bytes 491528 | tf_op jit(solution)/shard_map/ppermute | solution.py:484
  25.8 2.0 %collective-permute-start.15 = (bf16[640,128]{1,0:T(8,128)(2,1)S(1)}, bf16[640,128]{1,0:T(8,128)(2,1)S(1)}, u32[]{:S(2)}, u32[]{:S(2)}) collective-permute-start(bf16[640,128]{1,0:T(8,128)(2,1)S(1)} %collective-permute-done.8.rest_1_), channel_id=1, source_target_pairs={{0,1},{1,0},{2,3},{3,2},{4,5},{5,4},{6,7},{7,6},{8,9},{9,8},{10,11... | collective-permute-start | bytes 491528 | tf_op jit(solution)/shard_map/ppermute | solution.py:484
  27.8 1.4 %collective-permute-start.13 = (bf16[640,128]{1,0:T(8,128)(2,1)S(1)}, bf16[640,128]{1,0:T(8,128)(2,1)S(1)}, u32[]{:S(2)}, u32[]{:S(2)}) collective-permute-start(bf16[640,128]{1,0:T(8,128)(2,1)S(1)} %collective-permute-done.7.rest_0_), channel_id=1, source_target_pairs={{0,1},{1,0},{2,3},{3,2},{4,5},{5,4},{6,7},{7,6},{8,9},{9,8},{10,11... | collective-permute-start | bytes 491528 | tf_op jit(solution)/shard_map/ppermute | solution.py:484
  29.7 6.4 %collective-permute-start.17 = (bf16[656,128]{1,0:T(8,128)(2,1)S(1)}, bf16[656,128]{1,0:T(8,128)(2,1)S(1)}, u32[]{:S(2)}, u32[]{:S(2)}) collective-permute-start(bf16[656,128]{1,0:T(8,128)(2,1)S(1)} %project.1.token_ref.rest_0_), channel_id=1, source_target_pairs={{0,4},{1,5},{2,6},{3,7},{4,0},{5,1},{6,2},{7,3},{8,12},{9,13},{10,... | collective-permute-start | bytes 503816 | tf_op jit(solution)/shard_map/ppermute | solution.py:484
  30.1 7.2 %collective-permute-start.18 = (bf16[656,128]{1,0:T(8,128)(2,1)S(1)}, bf16[656,128]{1,0:T(8,128)(2,1)S(1)}, u32[]{:S(2)}, u32[]{:S(2)}) collective-permute-start(bf16[656,128]{1,0:T(8,128)(2,1)S(1)} %project.1.token_ref.rest_0_), channel_id=1, source_target_pairs={{0,2},{1,3},{2,0},{3,1},{4,6},{5,7},{6,4},{7,5},{8,10},{9,11},{10,... | collective-permute-start | bytes 503816 | tf_op jit(solution)/shard_map/ppermute | solution.py:484
  31.4 9.4 %collective-permute-start.22 = (bf16[656,128]{1,0:T(8,128)(2,1)S(1)}, bf16[656,128]{1,0:T(8,128)(2,1)S(1)}, u32[]{:S(2)}, u32[]{:S(2)}) collective-permute-start(bf16[656,128]{1,0:T(8,128)(2,1)S(1)} %project.1.token_ref.rest_0_), channel_id=1, source_target_pairs={{0,6},{1,7},{2,4},{3,5},{4,2},{5,3},{6,0},{7,1},{8,14},{9,15},{10,... | collective-permute-start | bytes 503816 | tf_op jit(solution)/shard_map/ppermute | solution.py:484
  34.6 4.0 %collective-permute-start.19 = (bf16[656,128]{1,0:T(8,128)(2,1)S(1)}, bf16[656,128]{1,0:T(8,128)(2,1)S(1)}, u32[]{:S(2)}, u32[]{:S(2)}) collective-permute-start(bf16[656,128]{1,0:T(8,128)(2,1)S(1)} %project.1.token_ref.rest_0_), channel_id=1, source_target_pairs={{0,1},{1,0},{2,3},{3,2},{4,5},{5,4},{6,7},{7,6},{8,9},{9,8},{10,11... | collective-permute-start | bytes 503816 | tf_op jit(solution)/shard_map/ppermute | solution.py:484
  36.0 4.8 %collective-permute-start.20 = (bf16[656,128]{1,0:T(8,128)(2,1)S(1)}, bf16[656,128]{1,0:T(8,128)(2,1)S(1)}, u32[]{:S(2)}, u32[]{:S(2)}) collective-permute-start(bf16[656,128]{1,0:T(8,128)(2,1)S(1)} %collective-permute-done.17.rest_1_), channel_id=1, source_target_pairs={{0,1},{1,0},{2,3},{3,2},{4,5},{5,4},{6,7},{7,6},{8,9},{9,8},{10,11... | collective-permute-start | bytes 503816 | tf_op jit(solution)/shard_map/ppermute | solution.py:484
  37.3 3.5 %collective-permute-start.21 = (bf16[656,128]{1,0:T(8,128)(2,1)S(1)}, bf16[656,128]{1,0:T(8,128)(2,1)S(1)}, u32[]{:S(2)}, u32[]{:S(2)}) collective-permute-start(bf16[656,128]{1,0:T(8,128)(2,1)S(1)} %collective-permute-done.18.rest_2_), channel_id=1, source_target_pairs={{0,1},{1,0},{2,3},{3,2},{4,5},{5,4},{6,7},{7,6},{8,9},{9,8},{10,11... | collective-permute-start | bytes 503816 | tf_op jit(solution)/shard_map/ppermute | solution.py:484
  40.8 1.4 %collective-permute-start.23 = (bf16[656,128]{1,0:T(8,128)(2,1)S(1)}, bf16[656,128]{1,0:T(8,128)(2,1)S(1)}, u32[]{:S(2)}, u32[]{:S(2)}) collective-permute-start(bf16[656,128]{1,0:T(8,128)(2,1)S(1)} %collective-permute-done.22.rest_6_), channel_id=1, source_target_pairs={{0,1},{1,0},{2,3},{3,2},{4,5},{5,4},{6,7},{7,6},{8,9},{9,8},{10,11... | collective-permute-start | bytes 503816 | tf_op jit(solution)/shard_map/ppermute | solution.py:484
  (2 other events, 13.4 us)

commit v25 on v24

--- a/solution.py
+++ b/solution.py
@@ -122,8 +122,8 @@
 REST = HPAIR - WIDE
 MAIN = ROWS * WIDE
 NOTES = 16
-RECEIVERS = ((0, 0), (4, 2), (2, 4), (1, 1), (6, 6), (7, 7), (3, 5), (5, 3))
-SENDERS = ((0, 0), (4, 2), (2, 4), (1, 1), (6, 6), (7, 7), (5, 3), (3, 5))
+RECEIVERS = ((0, 0), (1, 1), (4, 2), (2, 4), (6, 6), (7, 7), (3, 5), (5, 3))
+SENDERS = ((0, 0), (1, 1), (4, 2), (2, 4), (6, 6), (7, 7), (5, 3), (3, 5))
 OWNERS = (0, 4, 2, 1, 5, 3, 6, 7)
 ROOT = math.log2(math.e) / math.sqrt(HDIM)
 BF16 = jnp.bfloat16

time: 43.8 us -> 43.1 us (0.984)
  starting transfers between devices: 21.9 us -> 21.1 us
    ppermute x22, starting transfers between devices: 17.7 us -> 16.9 us  [swap(): lax.ppermute(value, 'row', [(row, row ^ (odd if row % 2 else even)) for r...]
  transfers between devices with their start and end apart: 24 -> 24, of which waited for: 9 -> 8; matrix products, arithmetic and copies ran while one was open for 0% -> 0% of each run, Pallas kernels for 18% -> 18%
where the time goes in v25:
time: 43.1 us; the launch traced here: 42.9 us
  starting transfers between devices  21.1 us (49%)
  Pallas kernels  11.4 us (26%)
  waiting for transfers between devices  10.2 us (24%)
    ppermute x22, starting transfers between devices, swap(): lax.ppermute(value, 'row', [(row, row ^ (odd if row % 2 else even)) for r...  16.9 us
    ppermute x22, waiting for transfers between devices, swap(): lax.ppermute(value, 'row', [(row, row ^ (odd if row % 2 else even)) for r...  7.33 us
    ppermute x2, starting transfers between devices, turn(): return lax.ppermute(value, ('page', 'row'), pairs)  4.21 us
    ppermute x2, waiting for transfers between devices, turn(): return lax.ppermute(value, ('page', 'row'), pairs)  2.91 us
    pallas_call x1, Pallas kernels, local_eight(): kernel(spread_kernel, 'spread', [shape(band, 4 * HPAIR)] * ROWS + [shape(...  1.77 us
    pallas_call x1, Pallas kernels, local_eight(): kernel(tail_kernel, 'merge_tail', [shape(units, MAIN), shape(units, 1, dt...  1.4 us
    pallas_call x1, Pallas kernels, local_eight(): kernel(merge_kernel, 'merge', shape(1, units, groups), [pltpu.VMEM((units...  1.36 us
    pallas_call x1, Pallas kernels, local_eight(): kernel(attend_kernel, 'attend', shape(piece, WIDE), [pltpu.VMEM((patches,...  1.35 us
  transfers between devices with their start and end apart: 24, of which 8 were waited for; matrix products, arithmetic and copies ran while one was open for 0% of the time, Pallas kernels for 18%

profile of v25, /device:TPU:0, one launch (start us, length us, event | category | flops | bytes accessed | tf_op | source)
XLA Modules:
  0.0 42.9 jit_solution(6640519302296782074)
XLA Ops:
  0.0 1.8 %spread.1 = (bf16[64,640]{1,0:T(8,128)(2,1)S(1)}, bf16[64,640]{1,0:T(8,128)(2,1)S(1)}, bf16[64,640]{1,0:T(8,128)(2,1)S(1)}, bf16[64,640]{1,0:T(8,128)(2,1)S(1)},...) custom-call(bf16[1,64,3840]{2,1,0:T(8,128)(2,1)} %qkv_hbm.1, ...), custom_call_target="tpu_custom_call" | custom-call | bytes 1048576 | tf_op jit(solution)/shard_map/spread/pallas_call | solution.py:509
  2.3 2.6 %collective-permute-start.1 = (bf16[64,640]{1,0:T(8,128)(2,1)S(1)}, bf16[64,640]{1,0:T(8,128)(2,1)S(1)}, u32[]{:S(2)}, u32[]{:S(2)}) collective-permute-start(bf16[64,640]{1,0:T(8,128)(2,1)S(1)} %get-tuple-element.34), channel_id=1, source_target_pairs={{0,4},{1,3},{2,6},{3,1},{4,0},{5,7},{6,2},{7,5},{8,12},{9,11},{10,... | collective-permute-start | bytes 245768 | tf_op jit(solution)/shard_map/ppermute | solution.py:484
  4.9 1.5 %collective-permute-start.2 = (bf16[64,640]{1,0:T(8,128)(2,1)S(1)}, bf16[64,640]{1,0:T(8,128)(2,1)S(1)}, u32[]{:S(2)}, u32[]{:S(2)}) collective-permute-start(bf16[64,640]{1,0:T(8,128)(2,1)S(1)} %get-tuple-element.38), channel_id=1, source_target_pairs={{0,2},{1,5},{2,0},{3,7},{4,6},{5,1},{6,4},{7,3},{8,10},{9,13},{10,... | collective-permute-start | bytes 245768 | tf_op jit(solution)/shard_map/ppermute | solution.py:484
  6.4 2.1 %collective-permute-start.4 = (bf16[64,640]{1,0:T(8,128)(2,1)S(1)}, bf16[64,640]{1,0:T(8,128)(2,1)S(1)}, u32[]{:S(2)}, u32[]{:S(2)}) collective-permute-start(bf16[64,640]{1,0:T(8,128)(2,1)S(1)} %get-tuple-element.40), channel_id=1, source_target_pairs={{0,7},{1,6},{2,5},{3,4},{4,3},{5,2},{6,1},{7,0},{8,15},{9,14},{10,... | collective-permute-start | bytes 245768 | tf_op jit(solution)/shard_map/ppermute | solution.py:484
  8.5 1.1 %collective-permute-start.5 = (bf16[64,640]{1,0:T(8,128)(2,1)S(1)}, bf16[64,640]{1,0:T(8,128)(2,1)S(1)}, u32[]{:S(2)}, u32[]{:S(2)}) collective-permute-start(bf16[64,640]{1,0:T(8,128)(2,1)S(1)} %get-tuple-element.41), channel_id=1, source_target_pairs={{0,3},{1,4},{2,1},{3,6},{4,7},{5,0},{6,5},{7,2},{8,11},{9,12},{10,... | collective-permute-start | bytes 245768 | tf_op jit(solution)/shard_map/ppermute | solution.py:484
  10.4 1.6 %collective-permute-start.10 = (bf16[800,128]{1,0:T(8,128)(2,1)S(1)}, bf16[800,128]{1,0:T(8,128)(2,1)S(1)}, u32[]{:S(2)}, u32[]{:S(2)}) collective-permute-start(bf16[800,128]{1,0:T(8,128)(2,1)S(1)} %get-tuple-element.43), channel_id=1, source_target_pairs={{0,8},{1,25},{2,10},{3,27},{4,12},{5,29},{6,14},{7,31},{8,16},{9,1... | collective-permute-start | bytes 614408 | tf_op jit(solution)/shard_map/ppermute | solution.py:493
  12.6 2.6 %collective-permute-start.12 = (bf16[400,128]{1,0:T(8,128)(2,1)S(1)}, bf16[400,128]{1,0:T(8,128)(2,1)S(1)}, u32[]{:S(2)}, u32[]{:S(2)}) collective-permute-start(bf16[400,128]{1,0:T(8,128)(2,1)S(1)} %get-tuple-element.44.rest_8_), channel_id=1, source_target_pairs={{0,16},{1,17},{2,18},{3,19},{4,20},{5,21},{6,22},{7,23},{8,24},{9,... | collective-permute-start | bytes 307208 | tf_op jit(solution)/shard_map/ppermute | solution.py:493
  15.2 1.4 %attend.1.token_ref.rest_0_ = bf16[640,128]{1,0:T(8,128)(2,1)S(1)} custom-call(bf16[512,512]{1,0:T(8,128)(2,1)S(1)} %get-tuple-element.35.select_ref, f32[1,512]{1,0:T(1,128)S(1)} %get-tuple-element.36.dead_ref, bf16[64,640]{1,0:T(8,128)(2,1)S(1)} %get-tuple-element.37.rest_0_, bf16[64,640]{1,0:T(8,128)(2,1)S(1)} %collective-permute-done.rest_0_.rest_1_, ...), custom_call_target="tpu_custom_call" | custom-call | flops 21474836480 | bytes 1048576 | tf_op jit(solution)/shard_map/attend/pallas_call | solution.py:538
  16.6 0.8 %collective-permute-start.8 = (bf16[640,128]{1,0:T(8,128)(2,1)S(1)}, bf16[640,128]{1,0:T(8,128)(2,1)S(1)}, u32[]{:S(2)}, u32[]{:S(2)}) collective-permute-start(bf16[640,128]{1,0:T(8,128)(2,1)S(1)} %attend.1.token_ref.rest_0_), channel_id=1, source_target_pairs={{0,4},{1,5},{2,6},{3,7},{4,0},{5,1},{6,2},{7,3},{8,12},{9,13},{10,... | collective-permute-start | bytes 491528 | tf_op jit(solution)/shard_map/ppermute | solution.py:484
  17.4 0.8 %collective-permute-start.9 = (bf16[640,128]{1,0:T(8,128)(2,1)S(1)}, bf16[640,128]{1,0:T(8,128)(2,1)S(1)}, u32[]{:S(2)}, u32[]{:S(2)}) collective-permute-start(bf16[640,128]{1,0:T(8,128)(2,1)S(1)} %attend.1.token_ref.rest_0_), channel_id=1, source_target_pairs={{0,2},{1,3},{2,0},{3,1},{4,6},{5,7},{6,4},{7,5},{8,10},{9,11},{10,... | collective-permute-start | bytes 491528 | tf_op jit(solution)/shard_map/ppermute | solution.py:484
  18.1 2.0 %collective-permute-start.7 = (bf16[640,128]{1,0:T(8,128)(2,1)S(1)}, bf16[640,128]{1,0:T(8,128)(2,1)S(1)}, u32[]{:S(2)}, u32[]{:S(2)}) collective-permute-start(bf16[640,128]{1,0:T(8,128)(2,1)S(1)} %attend.1.token_ref.rest_0_), channel_id=1, source_target_pairs={{0,6},{1,7},{2,4},{3,5},{4,2},{5,3},{6,0},{7,1},{8,14},{9,15},{10,... | collective-permute-start | bytes 491528 | tf_op jit(solution)/shard_map/ppermute | solution.py:484
  20.1 2.9 %collective-permute-done.12.rest_9_ = bf16[400,128]{1,0:T(8,128)(2,1)S(1)} collective-permute-done((bf16[400,128]{1,0:T(8,128)(2,1)S(1)}, bf16[400,128]{1,0:T(8,128)(2,1)S(1)}, u32[]{:S(2)}, u32[]{:S(2)}) %collective-permute-start.12) | collective-permute-done | bytes 102432 | tf_op jit(solution)/shard_map/ppermute | solution.py:493
  23.0 1.2 %ready.1 = (f32[512,160]{1,0:T(8,128)S(1)}, f32[1,160]{1,0:T(1,128)S(1)}, bf16[1024,160]{1,0:T(8,128)(2,1)S(1)}, bf16[4,1024,160]{2,1,0:T(8,128)(2,1)S(1)}) custom-call(bf16[512,512]{1,0:T(8,128)(2,1)S(1)} %get-tuple-element.35.select_ref, f32[1280]{0:T(1024)} %gain_hbm.1, bf16[640,128]{1,0:T(8,128)(2,1)S(1)} %attend.1.token_ref.rest_0_, ...), custom_call_target="tpu_custom_call" | custom-call | flops 10737418240 | bytes 4194304 | tf_op jit(solution)/shard_map/ready/pallas_call | solution.py:548
  26.2 0.9 %collective-permute-done.7.rest_0_ = bf16[640,128]{1,0:T(8,128)(2,1)S(1)} collective-permute-done((bf16[640,128]{1,0:T(8,128)(2,1)S(1)}, bf16[640,128]{1,0:T(8,128)(2,1)S(1)}, u32[]{:S(2)}, u32[]{:S(2)}) %collective-permute-start.7) | collective-permute-done | bytes 163872 | tf_op jit(solution)/shard_map/ppermute | solution.py:484
  27.6 0.9 %collective-permute-done.13.rest_1_ = bf16[640,128]{1,0:T(8,128)(2,1)S(1)} collective-permute-done((bf16[640,128]{1,0:T(8,128)(2,1)S(1)}, bf16[640,128]{1,0:T(8,128)(2,1)S(1)}, u32[]{:S(2)}, u32[]{:S(2)}) %collective-permute-start.13) | collective-permute-done | bytes 163872 | tf_op jit(solution)/shard_map/ppermute | solution.py:484
  28.9 1.2 %collective-permute-start.17 = (bf16[656,128]{1,0:T(8,128)(2,1)S(1)}, bf16[656,128]{1,0:T(8,128)(2,1)S(1)}, u32[]{:S(2)}, u32[]{:S(2)}) collective-permute-start(bf16[656,128]{1,0:T(8,128)(2,1)S(1)} %project.1.token_ref.rest_0_), channel_id=1, source_target_pairs={{0,4},{1,5},{2,6},{3,7},{4,0},{5,1},{6,2},{7,3},{8,12},{9,13},{10,... | collective-permute-start | bytes 503816 | tf_op jit(solution)/shard_map/ppermute | solution.py:484
  30.9 1.6 %collective-permute-start.22 = (bf16[656,128]{1,0:T(8,128)(2,1)S(1)}, bf16[656,128]{1,0:T(8,128)(2,1)S(1)}, u32[]{:S(2)}, u32[]{:S(2)}) collective-permute-start(bf16[656,128]{1,0:T(8,128)(2,1)S(1)} %project.1.token_ref.rest_0_), channel_id=1, source_target_pairs={{0,6},{1,7},{2,4},{3,5},{4,2},{5,3},{6,0},{7,1},{8,14},{9,15},{10,... | collective-permute-start | bytes 503816 | tf_op jit(solution)/shard_map/ppermute | solution.py:484
  32.5 1.4 %merge_tail.1 = (bf16[640,1024]{1,0:T(8,128)(2,1)S(1)}, f32[640,1]{1,0:T(8,128)S(1)}) custom-call(bf16[640,5120]{1,0:T(8,128)(2,1)S(1)} %bitcast.1, f32[640]{0:T(1024)} %bias_hbm.1, bf16[656,128]{1,0:T(8,128)(2,1)S(1)} %project.1.token_ref.rest_0_), custom_call_target="tpu_custom_call" | custom-call | bytes 4194304 | tf_op jit(solution)/shard_map/merge_tail/pallas_call | solution.py:580
  34.0 1.4 %collective-permute-done.17.rest_1_ = bf16[656,128]{1,0:T(8,128)(2,1)S(1)} collective-permute-done((bf16[656,128]{1,0:T(8,128)(2,1)S(1)}, bf16[656,128]{1,0:T(8,128)(2,1)S(1)}, u32[]{:S(2)}, u32[]{:S(2)}) %collective-permute-start.17) | collective-permute-done | bytes 167968 | tf_op jit(solution)/shard_map/ppermute | solution.py:484
  35.3 2.0 %collective-permute-done.18.rest_2_ = bf16[656,128]{1,0:T(8,128)(2,1)S(1)} collective-permute-done((bf16[656,128]{1,0:T(8,128)(2,1)S(1)}, bf16[656,128]{1,0:T(8,128)(2,1)S(1)}, u32[]{:S(2)}, u32[]{:S(2)}) %collective-permute-start.18) | collective-permute-done | bytes 167968 | tf_op jit(solution)/shard_map/ppermute | solution.py:484
  37.4 1.2 %merge_first.1.rest_3_ = f32[4,640,128]{2,1,0:T(8,128)S(1)} custom-call(bf16[656,128]{1,0:T(8,128)(2,1)S(1)} %project.1.token_ref.rest_0_, bf16[656,128]{1,0:T(8,128)(2,1)S(1)} %collective-permute-done.17.rest_1_, bf16[656,128]{1,0:T(8,128)(2,1)S(1)} %collective-permute-done.18.rest_2_, bf16[640,5120]{1,0:T(8,128)(2,1)S(1)} %bitcast.1, ...), custom_call_target="tpu_custom_call" | custom-call | flops 1 | bytes 1 | tf_op jit(solution)/shard_map/merge_first/pallas_call | solution.py:591
  38.6 1.5 %collective-permute-done.22.rest_6_ = bf16[656,128]{1,0:T(8,128)(2,1)S(1)} collective-permute-done((bf16[656,128]{1,0:T(8,128)(2,1)S(1)}, bf16[656,128]{1,0:T(8,128)(2,1)S(1)}, u32[]{:S(2)}, u32[]{:S(2)}) %collective-permute-start.22) | collective-permute-done | bytes 167968 | tf_op jit(solution)/shard_map/ppermute | solution.py:484
  40.1 1.3 %merge_second.1.rest_8_ = f32[4,640,128]{2,1,0:T(8,128)S(1)} custom-call(bf16[656,128]{1,0:T(8,128)(2,1)S(1)} %collective-permute-done.19.rest_0_.rest_3_, bf16[656,128]{1,0:T(8,128)(2,1)S(1)} %collective-permute-done.20.rest_1_.rest_4_, bf16[656,128]{1,0:T(8,128)(2,1)S(1)} %collective-permute-done.21.rest_2_.rest_5_, ...), custom_call_target="tpu_custom_call" | custom-call | flops 1 | bytes 1 | tf_op jit(solution)/shard_map/merge_second/pallas_call | solution.py:595
  41.5 1.4 %merge.1 = bf16[1,640,128]{2,1,0:T(8,128)(2,1)} custom-call(bf16[656,128]{1,0:T(8,128)(2,1)S(1)} %project.1.token_ref.rest_0_, bf16[656,128]{1,0:T(8,128)(2,1)S(1)} %collective-permute-done.17.rest_1_, bf16[656,128]{1,0:T(8,128)(2,1)S(1)} %collective-permute-done.18.rest_2_, bf16[656,128]{1,0:T(8,128)(2,1)S(1)} %collective-permute-done.19.rest_0_.rest_3_, ...), custom_call_target="tpu_custom_call" | custom-call | flops 335544320 | bytes 8388608 | tf_op jit(solution)/shard_map/merge/pallas_call | solution.py:598
  (41 shorter events, 5.7 us)
Async XLA Ops:
  1.8 6.7 %collective-permute-start = (bf16[64,640]{1,0:T(8,128)(2,1)S(1)}, bf16[64,640]{1,0:T(8,128)(2,1)S(1)}, u32[]{:S(2)}, u32[]{:S(2)}) collective-permute-start(bf16[64,640]{1,0:T(8,128)(2,1)S(1)} %get-tuple-element.33), channel_id=1, source_target_pairs={{0,1},{1,0},{2,3},{3,2},{4,5},{5,4},{6,7},{7,6},{8,9},{9,8},{10,11... | collective-permute-start | bytes 245768 | tf_op jit(solution)/shard_map/ppermute | solution.py:484
  2.3 7.3 %collective-permute-start.1 = (bf16[64,640]{1,0:T(8,128)(2,1)S(1)}, bf16[64,640]{1,0:T(8,128)(2,1)S(1)}, u32[]{:S(2)}, u32[]{:S(2)}) collective-permute-start(bf16[64,640]{1,0:T(8,128)(2,1)S(1)} %get-tuple-element.34), channel_id=1, source_target_pairs={{0,4},{1,3},{2,6},{3,1},{4,0},{5,7},{6,2},{7,5},{8,12},{9,11},{10,... | collective-permute-start | bytes 245768 | tf_op jit(solution)/shard_map/ppermute | solution.py:484
  4.9 5.5 %collective-permute-start.2 = (bf16[64,640]{1,0:T(8,128)(2,1)S(1)}, bf16[64,640]{1,0:T(8,128)(2,1)S(1)}, u32[]{:S(2)}, u32[]{:S(2)}) collective-permute-start(bf16[64,640]{1,0:T(8,128)(2,1)S(1)} %get-tuple-element.38), channel_id=1, source_target_pairs={{0,2},{1,5},{2,0},{3,7},{4,6},{5,1},{6,4},{7,3},{8,10},{9,13},{10,... | collective-permute-start | bytes 245768 | tf_op jit(solution)/shard_map/ppermute | solution.py:484
  6.4 6.2 %collective-permute-start.3 = (bf16[64,640]{1,0:T(8,128)(2,1)S(1)}, bf16[64,640]{1,0:T(8,128)(2,1)S(1)}, u32[]{:S(2)}, u32[]{:S(2)}) collective-permute-start(bf16[64,640]{1,0:T(8,128)(2,1)S(1)} %get-tuple-element.39), channel_id=1, source_target_pairs={{0,6},{1,7},{2,4},{3,5},{4,2},{5,3},{6,0},{7,1},{8,14},{9,15},{10,... | collective-permute-start | bytes 245768 | tf_op jit(solution)/shard_map/ppermute | solution.py:484
  6.4 8.8 %collective-permute-start.4 = (bf16[64,640]{1,0:T(8,128)(2,1)S(1)}, bf16[64,640]{1,0:T(8,128)(2,1)S(1)}, u32[]{:S(2)}, u32[]{:S(2)}) collective-permute-start(bf16[64,640]{1,0:T(8,128)(2,1)S(1)} %get-tuple-element.40), channel_id=1, source_target_pairs={{0,7},{1,6},{2,5},{3,4},{4,3},{5,2},{6,1},{7,0},{8,15},{9,14},{10,... | collective-permute-start | bytes 245768 | tf_op jit(solution)/shard_map/ppermute | solution.py:484
  8.5 6.7 %collective-permute-start.5 = (bf16[64,640]{1,0:T(8,128)(2,1)S(1)}, bf16[64,640]{1,0:T(8,128)(2,1)S(1)}, u32[]{:S(2)}, u32[]{:S(2)}) collective-permute-start(bf16[64,640]{1,0:T(8,128)(2,1)S(1)} %get-tuple-element.41), channel_id=1, source_target_pairs={{0,3},{1,4},{2,1},{3,6},{4,7},{5,0},{6,5},{7,2},{8,11},{9,12},{10,... | collective-permute-start | bytes 245768 | tf_op jit(solution)/shard_map/ppermute | solution.py:484
  9.6 5.6 %collective-permute-start.6 = (bf16[64,640]{1,0:T(8,128)(2,1)S(1)}, bf16[64,640]{1,0:T(8,128)(2,1)S(1)}, u32[]{:S(2)}, u32[]{:S(2)}) collective-permute-start(bf16[64,640]{1,0:T(8,128)(2,1)S(1)} %get-tuple-element.42), channel_id=1, source_target_pairs={{0,5},{1,2},{2,7},{3,0},{4,1},{5,6},{6,3},{7,4},{8,13},{9,10},{10,... | collective-permute-start | bytes 245768 | tf_op jit(solution)/shard_map/ppermute | solution.py:484
  10.4 9.7 %collective-permute-start.10 = (bf16[800,128]{1,0:T(8,128)(2,1)S(1)}, bf16[800,128]{1,0:T(8,128)(2,1)S(1)}, u32[]{:S(2)}, u32[]{:S(2)}) collective-permute-start(bf16[800,128]{1,0:T(8,128)(2,1)S(1)} %get-tuple-element.43), channel_id=1, source_target_pairs={{0,8},{1,25},{2,10},{3,27},{4,12},{5,29},{6,14},{7,31},{8,16},{9,1... | collective-permute-start | bytes 614408 | tf_op jit(solution)/shard_map/ppermute | solution.py:493
  12.6 10.4 %collective-permute-start.12 = (bf16[400,128]{1,0:T(8,128)(2,1)S(1)}, bf16[400,128]{1,0:T(8,128)(2,1)S(1)}, u32[]{:S(2)}, u32[]{:S(2)}) collective-permute-start(bf16[400,128]{1,0:T(8,128)(2,1)S(1)} %get-tuple-element.44.rest_8_), channel_id=1, source_target_pairs={{0,16},{1,17},{2,18},{3,19},{4,20},{5,21},{6,22},{7,23},{8,24},{9,... | collective-permute-start | bytes 307208 | tf_op jit(solution)/shard_map/ppermute | solution.py:493
  16.6 8.7 %collective-permute-start.8 = (bf16[640,128]{1,0:T(8,128)(2,1)S(1)}, bf16[640,128]{1,0:T(8,128)(2,1)S(1)}, u32[]{:S(2)}, u32[]{:S(2)}) collective-permute-start(bf16[640,128]{1,0:T(8,128)(2,1)S(1)} %attend.1.token_ref.rest_0_), channel_id=1, source_target_pairs={{0,4},{1,5},{2,6},{3,7},{4,0},{5,1},{6,2},{7,3},{8,12},{9,13},{10,... | collective-permute-start | bytes 491528 | tf_op jit(solution)/shard_map/ppermute | solution.py:484
  17.4 7.5 %collective-permute-start.9 = (bf16[640,128]{1,0:T(8,128)(2,1)S(1)}, bf16[640,128]{1,0:T(8,128)(2,1)S(1)}, u32[]{:S(2)}, u32[]{:S(2)}) collective-permute-start(bf16[640,128]{1,0:T(8,128)(2,1)S(1)} %attend.1.token_ref.rest_0_), channel_id=1, source_target_pairs={{0,2},{1,3},{2,0},{3,1},{4,6},{5,7},{6,4},{7,5},{8,10},{9,11},{10,... | collective-permute-start | bytes 491528 | tf_op jit(solution)/shard_map/ppermute | solution.py:484
  18.1 8.9 %collective-permute-start.7 = (bf16[640,128]{1,0:T(8,128)(2,1)S(1)}, bf16[640,128]{1,0:T(8,128)(2,1)S(1)}, u32[]{:S(2)}, u32[]{:S(2)}) collective-permute-start(bf16[640,128]{1,0:T(8,128)(2,1)S(1)} %attend.1.token_ref.rest_0_), channel_id=1, source_target_pairs={{0,6},{1,7},{2,4},{3,5},{4,2},{5,3},{6,0},{7,1},{8,14},{9,15},{10,... | collective-permute-start | bytes 491528 | tf_op jit(solution)/shard_map/ppermute | solution.py:484
  20.1 4.9 %collective-permute-start.11 = (bf16[800,128]{1,0:T(8,128)(2,1)S(1)}, bf16[800,128]{1,0:T(8,128)(2,1)S(1)}, u32[]{:S(2)}, u32[]{:S(2)}) collective-permute-start(bf16[800,128]{1,0:T(8,128)(2,1)S(1)} %collective-permute-done.10.rest_10_), channel_id=1, source_target_pairs={{0,1},{1,0},{2,3},{3,2},{4,5},{5,4},{6,7},{7,6},{8,9},{9,8},{10,11... | collective-permute-start | bytes 614408 | tf_op jit(solution)/shard_map/ppermute | solution.py:484
  24.2 2.8 %collective-permute-start.14 = (bf16[640,128]{1,0:T(8,128)(2,1)S(1)}, bf16[640,128]{1,0:T(8,128)(2,1)S(1)}, u32[]{:S(2)}, u32[]{:S(2)}) collective-permute-start(bf16[640,128]{1,0:T(8,128)(2,1)S(1)} %attend.1.token_ref.rest_0_), channel_id=1, source_target_pairs={{0,1},{1,0},{2,3},{3,2},{4,5},{5,4},{6,7},{7,6},{8,9},{9,8},{10,11... | collective-permute-start | bytes 491528 | tf_op jit(solution)/shard_map/ppermute | solution.py:484
  24.9 2.2 %collective-permute-start.16 = (bf16[640,128]{1,0:T(8,128)(2,1)S(1)}, bf16[640,128]{1,0:T(8,128)(2,1)S(1)}, u32[]{:S(2)}, u32[]{:S(2)}) collective-permute-start(bf16[640,128]{1,0:T(8,128)(2,1)S(1)} %collective-permute-done.9.rest_2_), channel_id=1, source_target_pairs={{0,1},{1,0},{2,3},{3,2},{4,5},{5,4},{6,7},{7,6},{8,9},{9,8},{10,11... | collective-permute-start | bytes 491528 | tf_op jit(solution)/shard_map/ppermute | solution.py:484
  25.2 1.9 %collective-permute-start.15 = (bf16[640,128]{1,0:T(8,128)(2,1)S(1)}, bf16[640,128]{1,0:T(8,128)(2,1)S(1)}, u32[]{:S(2)}, u32[]{:S(2)}) collective-permute-start(bf16[640,128]{1,0:T(8,128)(2,1)S(1)} %collective-permute-done.8.rest_1_), channel_id=1, source_target_pairs={{0,1},{1,0},{2,3},{3,2},{4,5},{5,4},{6,7},{7,6},{8,9},{9,8},{10,11... | collective-permute-start | bytes 491528 | tf_op jit(solution)/shard_map/ppermute | solution.py:484
  27.1 1.4 %collective-permute-start.13 = (bf16[640,128]{1,0:T(8,128)(2,1)S(1)}, bf16[640,128]{1,0:T(8,128)(2,1)S(1)}, u32[]{:S(2)}, u32[]{:S(2)}) collective-permute-start(bf16[640,128]{1,0:T(8,128)(2,1)S(1)} %collective-permute-done.7.rest_0_), channel_id=1, source_target_pairs={{0,1},{1,0},{2,3},{3,2},{4,5},{5,4},{6,7},{7,6},{8,9},{9,8},{10,11... | collective-permute-start | bytes 491528 | tf_op jit(solution)/shard_map/ppermute | solution.py:484
  28.9 6.4 %collective-permute-start.17 = (bf16[656,128]{1,0:T(8,128)(2,1)S(1)}, bf16[656,128]{1,0:T(8,128)(2,1)S(1)}, u32[]{:S(2)}, u32[]{:S(2)}) collective-permute-start(bf16[656,128]{1,0:T(8,128)(2,1)S(1)} %project.1.token_ref.rest_0_), channel_id=1, source_target_pairs={{0,4},{1,5},{2,6},{3,7},{4,0},{5,1},{6,2},{7,3},{8,12},{9,13},{10,... | collective-permute-start | bytes 503816 | tf_op jit(solution)/shard_map/ppermute | solution.py:484
  30.2 7.2 %collective-permute-start.18 = (bf16[656,128]{1,0:T(8,128)(2,1)S(1)}, bf16[656,128]{1,0:T(8,128)(2,1)S(1)}, u32[]{:S(2)}, u32[]{:S(2)}) collective-permute-start(bf16[656,128]{1,0:T(8,128)(2,1)S(1)} %project.1.token_ref.rest_0_), channel_id=1, source_target_pairs={{0,2},{1,3},{2,0},{3,1},{4,6},{5,7},{6,4},{7,5},{8,10},{9,11},{10,... | collective-permute-start | bytes 503816 | tf_op jit(solution)/shard_map/ppermute | solution.py:484
  30.9 9.2 %collective-permute-start.22 = (bf16[656,128]{1,0:T(8,128)(2,1)S(1)}, bf16[656,128]{1,0:T(8,128)(2,1)S(1)}, u32[]{:S(2)}, u32[]{:S(2)}) collective-permute-start(bf16[656,128]{1,0:T(8,128)(2,1)S(1)} %project.1.token_ref.rest_0_), channel_id=1, source_target_pairs={{0,6},{1,7},{2,4},{3,5},{4,2},{5,3},{6,0},{7,1},{8,14},{9,15},{10,... | collective-permute-start | bytes 503816 | tf_op jit(solution)/shard_map/ppermute | solution.py:484
  33.9 4.7 %collective-permute-start.19 = (bf16[656,128]{1,0:T(8,128)(2,1)S(1)}, bf16[656,128]{1,0:T(8,128)(2,1)S(1)}, u32[]{:S(2)}, u32[]{:S(2)}) collective-permute-start(bf16[656,128]{1,0:T(8,128)(2,1)S(1)} %project.1.token_ref.rest_0_), channel_id=1, source_target_pairs={{0,1},{1,0},{2,3},{3,2},{4,5},{5,4},{6,7},{7,6},{8,9},{9,8},{10,11... | collective-permute-start | bytes 503816 | tf_op jit(solution)/shard_map/ppermute | solution.py:484
  35.3 4.8 %collective-permute-start.20 = (bf16[656,128]{1,0:T(8,128)(2,1)S(1)}, bf16[656,128]{1,0:T(8,128)(2,1)S(1)}, u32[]{:S(2)}, u32[]{:S(2)}) collective-permute-start(bf16[656,128]{1,0:T(8,128)(2,1)S(1)} %collective-permute-done.17.rest_1_), channel_id=1, source_target_pairs={{0,1},{1,0},{2,3},{3,2},{4,5},{5,4},{6,7},{7,6},{8,9},{9,8},{10,11... | collective-permute-start | bytes 503816 | tf_op jit(solution)/shard_map/ppermute | solution.py:484
  37.4 2.7 %collective-permute-start.21 = (bf16[656,128]{1,0:T(8,128)(2,1)S(1)}, bf16[656,128]{1,0:T(8,128)(2,1)S(1)}, u32[]{:S(2)}, u32[]{:S(2)}) collective-permute-start(bf16[656,128]{1,0:T(8,128)(2,1)S(1)} %collective-permute-done.18.rest_2_), channel_id=1, source_target_pairs={{0,1},{1,0},{2,3},{3,2},{4,5},{5,4},{6,7},{7,6},{8,9},{9,8},{10,11... | collective-permute-start | bytes 503816 | tf_op jit(solution)/shard_map/ppermute | solution.py:484
  40.1 1.4 %collective-permute-start.23 = (bf16[656,128]{1,0:T(8,128)(2,1)S(1)}, bf16[656,128]{1,0:T(8,128)(2,1)S(1)}, u32[]{:S(2)}, u32[]{:S(2)}) collective-permute-start(bf16[656,128]{1,0:T(8,128)(2,1)S(1)} %collective-permute-done.22.rest_6_), channel_id=1, source_target_pairs={{0,1},{1,0},{2,3},{3,2},{4,5},{5,4},{6,7},{7,6},{8,9},{9,8},{10,11... | collective-permute-start | bytes 503816 | tf_op jit(solution)/shard_map/ppermute | solution.py:484
  (2 other events, 13.1 us)

commit v26 on v25

--- a/solution.py
+++ b/solution.py
@@ -122,8 +122,8 @@
 REST = HPAIR - WIDE
 MAIN = ROWS * WIDE
 NOTES = 16
-RECEIVERS = ((0, 0), (1, 1), (4, 2), (2, 4), (6, 6), (7, 7), (3, 5), (5, 3))
-SENDERS = ((0, 0), (1, 1), (4, 2), (2, 4), (6, 6), (7, 7), (5, 3), (3, 5))
+RECEIVERS = ((0, 0), (1, 1), (4, 2), (6, 6), (2, 4), (7, 7), (3, 5), (5, 3))
+SENDERS = ((0, 0), (1, 1), (4, 2), (6, 6), (2, 4), (7, 7), (5, 3), (3, 5))
 OWNERS = (0, 4, 2, 1, 5, 3, 6, 7)
 ROOT = math.log2(math.e) / math.sqrt(HDIM)
 BF16 = jnp.bfloat16

time: 43.1 us -> 43 us (level)
    ppermute x22, waiting for transfers between devices: 7.33 us -> 6.72 us  [swap(): lax.ppermute(value, 'row', [(row, row ^ (odd if row % 2 else even)) for r...]
where the time goes in v26:
time: 43 us; the launch traced here: 42.8 us
  starting transfers between devices  21.4 us (50%)
  Pallas kernels  11.4 us (27%)
  waiting for transfers between devices  9.89 us (23%)
    ppermute x22, starting transfers between devices, swap(): lax.ppermute(value, 'row', [(row, row ^ (odd if row % 2 else even)) for r...  17.2 us
    ppermute x22, waiting for transfers between devices, swap(): lax.ppermute(value, 'row', [(row, row ^ (odd if row % 2 else even)) for r...  6.72 us
    ppermute x2, starting transfers between devices, turn(): return lax.ppermute(value, ('page', 'row'), pairs)  4.22 us
    ppermute x2, waiting for transfers between devices, turn(): return lax.ppermute(value, ('page', 'row'), pairs)  3.17 us
    pallas_call x1, Pallas kernels, local_eight(): kernel(spread_kernel, 'spread', [shape(band, 4 * HPAIR)] * ROWS + [shape(...  1.77 us
    pallas_call x1, Pallas kernels, local_eight(): kernel(tail_kernel, 'merge_tail', [shape(units, MAIN), shape(units, 1, dt...  1.4 us
    pallas_call x1, Pallas kernels, local_eight(): kernel(merge_kernel, 'merge', shape(1, units, groups), [pltpu.VMEM((units...  1.36 us
    pallas_call x1, Pallas kernels, local_eight(): kernel(attend_kernel, 'attend', shape(piece, WIDE), [pltpu.VMEM((patches,...  1.35 us
  transfers between devices with their start and end apart: 24, of which 8 were waited for; matrix products, arithmetic and copies ran while one was open for 0% of the time, Pallas kernels for 18%

profile of v26, /device:TPU:0, one launch (start us, length us, event | category | flops | bytes accessed | tf_op | source)
XLA Modules:
  0.0 42.8 jit_solution(10413303046142370024)
XLA Ops:
  0.0 1.8 %spread.1 = (bf16[64,640]{1,0:T(8,128)(2,1)S(1)}, bf16[64,640]{1,0:T(8,128)(2,1)S(1)}, bf16[64,640]{1,0:T(8,128)(2,1)S(1)}, bf16[64,640]{1,0:T(8,128)(2,1)S(1)},...) custom-call(bf16[1,64,3840]{2,1,0:T(8,128)(2,1)} %qkv_hbm.1, ...), custom_call_target="tpu_custom_call" | custom-call | bytes 1048576 | tf_op jit(solution)/shard_map/spread/pallas_call | solution.py:509
  2.3 2.6 %collective-permute-start.1 = (bf16[64,640]{1,0:T(8,128)(2,1)S(1)}, bf16[64,640]{1,0:T(8,128)(2,1)S(1)}, u32[]{:S(2)}, u32[]{:S(2)}) collective-permute-start(bf16[64,640]{1,0:T(8,128)(2,1)S(1)} %get-tuple-element.34), channel_id=1, source_target_pairs={{0,4},{1,3},{2,6},{3,1},{4,0},{5,7},{6,2},{7,5},{8,12},{9,11},{10,... | collective-permute-start | bytes 245768 | tf_op jit(solution)/shard_map/ppermute | solution.py:484
  4.9 1.4 %collective-permute-start.2 = (bf16[64,640]{1,0:T(8,128)(2,1)S(1)}, bf16[64,640]{1,0:T(8,128)(2,1)S(1)}, u32[]{:S(2)}, u32[]{:S(2)}) collective-permute-start(bf16[64,640]{1,0:T(8,128)(2,1)S(1)} %get-tuple-element.38), channel_id=1, source_target_pairs={{0,6},{1,7},{2,4},{3,5},{4,2},{5,3},{6,0},{7,1},{8,14},{9,15},{10,... | collective-permute-start | bytes 245768 | tf_op jit(solution)/shard_map/ppermute | solution.py:484
  6.4 2.1 %collective-permute-start.4 = (bf16[64,640]{1,0:T(8,128)(2,1)S(1)}, bf16[64,640]{1,0:T(8,128)(2,1)S(1)}, u32[]{:S(2)}, u32[]{:S(2)}) collective-permute-start(bf16[64,640]{1,0:T(8,128)(2,1)S(1)} %get-tuple-element.40), channel_id=1, source_target_pairs={{0,7},{1,6},{2,5},{3,4},{4,3},{5,2},{6,1},{7,0},{8,15},{9,14},{10,... | collective-permute-start | bytes 245768 | tf_op jit(solution)/shard_map/ppermute | solution.py:484
  8.5 1.1 %collective-permute-start.5 = (bf16[64,640]{1,0:T(8,128)(2,1)S(1)}, bf16[64,640]{1,0:T(8,128)(2,1)S(1)}, u32[]{:S(2)}, u32[]{:S(2)}) collective-permute-start(bf16[64,640]{1,0:T(8,128)(2,1)S(1)} %get-tuple-element.41), channel_id=1, source_target_pairs={{0,3},{1,4},{2,1},{3,6},{4,7},{5,0},{6,5},{7,2},{8,11},{9,12},{10,... | collective-permute-start | bytes 245768 | tf_op jit(solution)/shard_map/ppermute | solution.py:484
  10.4 1.6 %collective-permute-start.10 = (bf16[800,128]{1,0:T(8,128)(2,1)S(1)}, bf16[800,128]{1,0:T(8,128)(2,1)S(1)}, u32[]{:S(2)}, u32[]{:S(2)}) collective-permute-start(bf16[800,128]{1,0:T(8,128)(2,1)S(1)} %get-tuple-element.43), channel_id=1, source_target_pairs={{0,8},{1,25},{2,10},{3,27},{4,12},{5,29},{6,14},{7,31},{8,16},{9,1... | collective-permute-start | bytes 614408 | tf_op jit(solution)/shard_map/ppermute | solution.py:493
  12.1 2.6 %collective-permute-start.12 = (bf16[400,128]{1,0:T(8,128)(2,1)S(1)}, bf16[400,128]{1,0:T(8,128)(2,1)S(1)}, u32[]{:S(2)}, u32[]{:S(2)}) collective-permute-start(bf16[400,128]{1,0:T(8,128)(2,1)S(1)} %get-tuple-element.44.rest_8_), channel_id=1, source_target_pairs={{0,16},{1,17},{2,18},{3,19},{4,20},{5,21},{6,22},{7,23},{8,24},{9,... | collective-permute-start | bytes 307208 | tf_op jit(solution)/shard_map/ppermute | solution.py:493
  14.7 1.3 %attend.1.token_ref.rest_0_ = bf16[640,128]{1,0:T(8,128)(2,1)S(1)} custom-call(bf16[512,512]{1,0:T(8,128)(2,1)S(1)} %get-tuple-element.35.select_ref, f32[1,512]{1,0:T(1,128)S(1)} %get-tuple-element.36.dead_ref, bf16[64,640]{1,0:T(8,128)(2,1)S(1)} %get-tuple-element.37.rest_0_, bf16[64,640]{1,0:T(8,128)(2,1)S(1)} %collective-permute-done.rest_0_.rest_1_, ...), custom_call_target="tpu_custom_call" | custom-call | flops 21474836480 | bytes 1048576 | tf_op jit(solution)/shard_map/attend/pallas_call | solution.py:538
  16.0 1.1 %collective-permute-start.8 = (bf16[640,128]{1,0:T(8,128)(2,1)S(1)}, bf16[640,128]{1,0:T(8,128)(2,1)S(1)}, u32[]{:S(2)}, u32[]{:S(2)}) collective-permute-start(bf16[640,128]{1,0:T(8,128)(2,1)S(1)} %attend.1.token_ref.rest_0_), channel_id=1, source_target_pairs={{0,4},{1,5},{2,6},{3,7},{4,0},{5,1},{6,2},{7,3},{8,12},{9,13},{10,... | collective-permute-start | bytes 491528 | tf_op jit(solution)/shard_map/ppermute | solution.py:484
  17.1 1.5 %collective-permute-start.9 = (bf16[640,128]{1,0:T(8,128)(2,1)S(1)}, bf16[640,128]{1,0:T(8,128)(2,1)S(1)}, u32[]{:S(2)}, u32[]{:S(2)}) collective-permute-start(bf16[640,128]{1,0:T(8,128)(2,1)S(1)} %attend.1.token_ref.rest_0_), channel_id=1, source_target_pairs={{0,2},{1,3},{2,0},{3,1},{4,6},{5,7},{6,4},{7,5},{8,10},{9,11},{10,... | collective-permute-start | bytes 491528 | tf_op jit(solution)/shard_map/ppermute | solution.py:484
  18.6 1.0 %collective-permute-start.7 = (bf16[640,128]{1,0:T(8,128)(2,1)S(1)}, bf16[640,128]{1,0:T(8,128)(2,1)S(1)}, u32[]{:S(2)}, u32[]{:S(2)}) collective-permute-start(bf16[640,128]{1,0:T(8,128)(2,1)S(1)} %attend.1.token_ref.rest_0_), channel_id=1, source_target_pairs={{0,6},{1,7},{2,4},{3,5},{4,2},{5,3},{6,0},{7,1},{8,14},{9,15},{10,... | collective-permute-start | bytes 491528 | tf_op jit(solution)/shard_map/ppermute | solution.py:484
  20.1 2.7 %collective-permute-done.12.rest_9_ = bf16[400,128]{1,0:T(8,128)(2,1)S(1)} collective-permute-done((bf16[400,128]{1,0:T(8,128)(2,1)S(1)}, bf16[400,128]{1,0:T(8,128)(2,1)S(1)}, u32[]{:S(2)}, u32[]{:S(2)}) %collective-permute-start.12) | collective-permute-done | bytes 102432 | tf_op jit(solution)/shard_map/ppermute | solution.py:493
  22.8 1.2 %ready.1 = (f32[512,160]{1,0:T(8,128)S(1)}, f32[1,160]{1,0:T(1,128)S(1)}, bf16[1024,160]{1,0:T(8,128)(2,1)S(1)}, bf16[4,1024,160]{2,1,0:T(8,128)(2,1)S(1)}) custom-call(bf16[512,512]{1,0:T(8,128)(2,1)S(1)} %get-tuple-element.35.select_ref, f32[1280]{0:T(1024)} %gain_hbm.1, bf16[640,128]{1,0:T(8,128)(2,1)S(1)} %attend.1.token_ref.rest_0_, ...), custom_call_target="tpu_custom_call" | custom-call | flops 10737418240 | bytes 4194304 | tf_op jit(solution)/shard_map/ready/pallas_call | solution.py:548
  24.0 0.9 %collective-permute-start.14 = (bf16[640,128]{1,0:T(8,128)(2,1)S(1)}, bf16[640,128]{1,0:T(8,128)(2,1)S(1)}, u32[]{:S(2)}, u32[]{:S(2)}) collective-permute-start(bf16[640,128]{1,0:T(8,128)(2,1)S(1)} %attend.1.token_ref.rest_0_), channel_id=1, source_target_pairs={{0,1},{1,0},{2,3},{3,2},{4,5},{5,4},{6,7},{7,6},{8,9},{9,8},{10,11... | collective-permute-start | bytes 491528 | tf_op jit(solution)/shard_map/ppermute | solution.py:484
  27.5 0.9 %collective-permute-done.13.rest_1_ = bf16[640,128]{1,0:T(8,128)(2,1)S(1)} collective-permute-done((bf16[640,128]{1,0:T(8,128)(2,1)S(1)}, bf16[640,128]{1,0:T(8,128)(2,1)S(1)}, u32[]{:S(2)}, u32[]{:S(2)}) %collective-permute-start.13) | collective-permute-done | bytes 163872 | tf_op jit(solution)/shard_map/ppermute | solution.py:484
  28.9 1.7 %collective-permute-start.17 = (bf16[656,128]{1,0:T(8,128)(2,1)S(1)}, bf16[656,128]{1,0:T(8,128)(2,1)S(1)}, u32[]{:S(2)}, u32[]{:S(2)}) collective-permute-start(bf16[656,128]{1,0:T(8,128)(2,1)S(1)} %project.1.token_ref.rest_0_), channel_id=1, source_target_pairs={{0,4},{1,5},{2,6},{3,7},{4,0},{5,1},{6,2},{7,3},{8,12},{9,13},{10,... | collective-permute-start | bytes 503816 | tf_op jit(solution)/shard_map/ppermute | solution.py:484
  31.0 1.5 %collective-permute-start.22 = (bf16[656,128]{1,0:T(8,128)(2,1)S(1)}, bf16[656,128]{1,0:T(8,128)(2,1)S(1)}, u32[]{:S(2)}, u32[]{:S(2)}) collective-permute-start(bf16[656,128]{1,0:T(8,128)(2,1)S(1)} %project.1.token_ref.rest_0_), channel_id=1, source_target_pairs={{0,6},{1,7},{2,4},{3,5},{4,2},{5,3},{6,0},{7,1},{8,14},{9,15},{10,... | collective-permute-start | bytes 503816 | tf_op jit(solution)/shard_map/ppermute | solution.py:484
  32.4 1.4 %merge_tail.1 = (bf16[640,1024]{1,0:T(8,128)(2,1)S(1)}, f32[640,1]{1,0:T(8,128)S(1)}) custom-call(bf16[640,5120]{1,0:T(8,128)(2,1)S(1)} %bitcast.1, f32[640]{0:T(1024)} %bias_hbm.1, bf16[656,128]{1,0:T(8,128)(2,1)S(1)} %project.1.token_ref.rest_0_), custom_call_target="tpu_custom_call" | custom-call | bytes 4194304 | tf_op jit(solution)/shard_map/merge_tail/pallas_call | solution.py:580
  33.9 1.4 %collective-permute-done.17.rest_1_ = bf16[656,128]{1,0:T(8,128)(2,1)S(1)} collective-permute-done((bf16[656,128]{1,0:T(8,128)(2,1)S(1)}, bf16[656,128]{1,0:T(8,128)(2,1)S(1)}, u32[]{:S(2)}, u32[]{:S(2)}) %collective-permute-start.17) | collective-permute-done | bytes 167968 | tf_op jit(solution)/shard_map/ppermute | solution.py:484
  35.3 2.5 %collective-permute-done.18.rest_2_ = bf16[656,128]{1,0:T(8,128)(2,1)S(1)} collective-permute-done((bf16[656,128]{1,0:T(8,128)(2,1)S(1)}, bf16[656,128]{1,0:T(8,128)(2,1)S(1)}, u32[]{:S(2)}, u32[]{:S(2)}) %collective-permute-start.18) | collective-permute-done | bytes 167968 | tf_op jit(solution)/shard_map/ppermute | solution.py:484
  37.8 1.2 %merge_first.1.rest_3_ = f32[4,640,128]{2,1,0:T(8,128)S(1)} custom-call(bf16[656,128]{1,0:T(8,128)(2,1)S(1)} %project.1.token_ref.rest_0_, bf16[656,128]{1,0:T(8,128)(2,1)S(1)} %collective-permute-done.17.rest_1_, bf16[656,128]{1,0:T(8,128)(2,1)S(1)} %collective-permute-done.18.rest_2_, bf16[640,5120]{1,0:T(8,128)(2,1)S(1)} %bitcast.1, ...), custom_call_target="tpu_custom_call" | custom-call | flops 1 | bytes 1 | tf_op jit(solution)/shard_map/merge_first/pallas_call | solution.py:591
  39.0 1.0 %collective-permute-done.22.rest_6_ = bf16[656,128]{1,0:T(8,128)(2,1)S(1)} collective-permute-done((bf16[656,128]{1,0:T(8,128)(2,1)S(1)}, bf16[656,128]{1,0:T(8,128)(2,1)S(1)}, u32[]{:S(2)}, u32[]{:S(2)}) %collective-permute-start.22) | collective-permute-done | bytes 167968 | tf_op jit(solution)/shard_map/ppermute | solution.py:484
  40.1 1.3 %merge_second.1.rest_8_ = f32[4,640,128]{2,1,0:T(8,128)S(1)} custom-call(bf16[656,128]{1,0:T(8,128)(2,1)S(1)} %collective-permute-done.19.rest_0_.rest_3_, bf16[656,128]{1,0:T(8,128)(2,1)S(1)} %collective-permute-done.20.rest_1_.rest_4_, bf16[656,128]{1,0:T(8,128)(2,1)S(1)} %collective-permute-done.21.rest_2_.rest_5_, ...), custom_call_target="tpu_custom_call" | custom-call | flops 1 | bytes 1 | tf_op jit(solution)/shard_map/merge_second/pallas_call | solution.py:595
  41.5 1.4 %merge.1 = bf16[1,640,128]{2,1,0:T(8,128)(2,1)} custom-call(bf16[656,128]{1,0:T(8,128)(2,1)S(1)} %project.1.token_ref.rest_0_, bf16[656,128]{1,0:T(8,128)(2,1)S(1)} %collective-permute-done.17.rest_1_, bf16[656,128]{1,0:T(8,128)(2,1)S(1)} %collective-permute-done.18.rest_2_, bf16[656,128]{1,0:T(8,128)(2,1)S(1)} %collective-permute-done.19.rest_0_.rest_3_, ...), custom_call_target="tpu_custom_call" | custom-call | flops 335544320 | bytes 8388608 | tf_op jit(solution)/shard_map/merge/pallas_call | solution.py:598
  (41 shorter events, 5.5 us)
Async XLA Ops:
  1.8 6.7 %collective-permute-start = (bf16[64,640]{1,0:T(8,128)(2,1)S(1)}, bf16[64,640]{1,0:T(8,128)(2,1)S(1)}, u32[]{:S(2)}, u32[]{:S(2)}) collective-permute-start(bf16[64,640]{1,0:T(8,128)(2,1)S(1)} %get-tuple-element.33), channel_id=1, source_target_pairs={{0,1},{1,0},{2,3},{3,2},{4,5},{5,4},{6,7},{7,6},{8,9},{9,8},{10,11... | collective-permute-start | bytes 245768 | tf_op jit(solution)/shard_map/ppermute | solution.py:484
  2.3 7.3 %collective-permute-start.1 = (bf16[64,640]{1,0:T(8,128)(2,1)S(1)}, bf16[64,640]{1,0:T(8,128)(2,1)S(1)}, u32[]{:S(2)}, u32[]{:S(2)}) collective-permute-start(bf16[64,640]{1,0:T(8,128)(2,1)S(1)} %get-tuple-element.34), channel_id=1, source_target_pairs={{0,4},{1,3},{2,6},{3,1},{4,0},{5,7},{6,2},{7,5},{8,12},{9,11},{10,... | collective-permute-start | bytes 245768 | tf_op jit(solution)/shard_map/ppermute | solution.py:484
  4.9 5.5 %collective-permute-start.2 = (bf16[64,640]{1,0:T(8,128)(2,1)S(1)}, bf16[64,640]{1,0:T(8,128)(2,1)S(1)}, u32[]{:S(2)}, u32[]{:S(2)}) collective-permute-start(bf16[64,640]{1,0:T(8,128)(2,1)S(1)} %get-tuple-element.38), channel_id=1, source_target_pairs={{0,6},{1,7},{2,4},{3,5},{4,2},{5,3},{6,0},{7,1},{8,14},{9,15},{10,... | collective-permute-start | bytes 245768 | tf_op jit(solution)/shard_map/ppermute | solution.py:484
  6.3 5.8 %collective-permute-start.3 = (bf16[64,640]{1,0:T(8,128)(2,1)S(1)}, bf16[64,640]{1,0:T(8,128)(2,1)S(1)}, u32[]{:S(2)}, u32[]{:S(2)}) collective-permute-start(bf16[64,640]{1,0:T(8,128)(2,1)S(1)} %get-tuple-element.39), channel_id=1, source_target_pairs={{0,2},{1,5},{2,0},{3,7},{4,6},{5,1},{6,4},{7,3},{8,10},{9,13},{10,... | collective-permute-start | bytes 245768 | tf_op jit(solution)/shard_map/ppermute | solution.py:484
  6.4 8.2 %collective-permute-start.4 = (bf16[64,640]{1,0:T(8,128)(2,1)S(1)}, bf16[64,640]{1,0:T(8,128)(2,1)S(1)}, u32[]{:S(2)}, u32[]{:S(2)}) collective-permute-start(bf16[64,640]{1,0:T(8,128)(2,1)S(1)} %get-tuple-element.40), channel_id=1, source_target_pairs={{0,7},{1,6},{2,5},{3,4},{4,3},{5,2},{6,1},{7,0},{8,15},{9,14},{10,... | collective-permute-start | bytes 245768 | tf_op jit(solution)/shard_map/ppermute | solution.py:484
  8.5 6.2 %collective-permute-start.5 = (bf16[64,640]{1,0:T(8,128)(2,1)S(1)}, bf16[64,640]{1,0:T(8,128)(2,1)S(1)}, u32[]{:S(2)}, u32[]{:S(2)}) collective-permute-start(bf16[64,640]{1,0:T(8,128)(2,1)S(1)} %get-tuple-element.41), channel_id=1, source_target_pairs={{0,3},{1,4},{2,1},{3,6},{4,7},{5,0},{6,5},{7,2},{8,11},{9,12},{10,... | collective-permute-start | bytes 245768 | tf_op jit(solution)/shard_map/ppermute | solution.py:484
  9.6 5.1 %collective-permute-start.6 = (bf16[64,640]{1,0:T(8,128)(2,1)S(1)}, bf16[64,640]{1,0:T(8,128)(2,1)S(1)}, u32[]{:S(2)}, u32[]{:S(2)}) collective-permute-start(bf16[64,640]{1,0:T(8,128)(2,1)S(1)} %get-tuple-element.42), channel_id=1, source_target_pairs={{0,5},{1,2},{2,7},{3,0},{4,1},{5,6},{6,3},{7,4},{8,13},{9,10},{10,... | collective-permute-start | bytes 245768 | tf_op jit(solution)/shard_map/ppermute | solution.py:484
  10.4 9.6 %collective-permute-start.10 = (bf16[800,128]{1,0:T(8,128)(2,1)S(1)}, bf16[800,128]{1,0:T(8,128)(2,1)S(1)}, u32[]{:S(2)}, u32[]{:S(2)}) collective-permute-start(bf16[800,128]{1,0:T(8,128)(2,1)S(1)} %get-tuple-element.43), channel_id=1, source_target_pairs={{0,8},{1,25},{2,10},{3,27},{4,12},{5,29},{6,14},{7,31},{8,16},{9,1... | collective-permute-start | bytes 614408 | tf_op jit(solution)/shard_map/ppermute | solution.py:493
  12.1 10.7 %collective-permute-start.12 = (bf16[400,128]{1,0:T(8,128)(2,1)S(1)}, bf16[400,128]{1,0:T(8,128)(2,1)S(1)}, u32[]{:S(2)}, u32[]{:S(2)}) collective-permute-start(bf16[400,128]{1,0:T(8,128)(2,1)S(1)} %get-tuple-element.44.rest_8_), channel_id=1, source_target_pairs={{0,16},{1,17},{2,18},{3,19},{4,20},{5,21},{6,22},{7,23},{8,24},{9,... | collective-permute-start | bytes 307208 | tf_op jit(solution)/shard_map/ppermute | solution.py:493
  16.0 9.2 %collective-permute-start.8 = (bf16[640,128]{1,0:T(8,128)(2,1)S(1)}, bf16[640,128]{1,0:T(8,128)(2,1)S(1)}, u32[]{:S(2)}, u32[]{:S(2)}) collective-permute-start(bf16[640,128]{1,0:T(8,128)(2,1)S(1)} %attend.1.token_ref.rest_0_), channel_id=1, source_target_pairs={{0,4},{1,5},{2,6},{3,7},{4,0},{5,1},{6,2},{7,3},{8,12},{9,13},{10,... | collective-permute-start | bytes 491528 | tf_op jit(solution)/shard_map/ppermute | solution.py:484
  17.1 7.8 %collective-permute-start.9 = (bf16[640,128]{1,0:T(8,128)(2,1)S(1)}, bf16[640,128]{1,0:T(8,128)(2,1)S(1)}, u32[]{:S(2)}, u32[]{:S(2)}) collective-permute-start(bf16[640,128]{1,0:T(8,128)(2,1)S(1)} %attend.1.token_ref.rest_0_), channel_id=1, source_target_pairs={{0,2},{1,3},{2,0},{3,1},{4,6},{5,7},{6,4},{7,5},{8,10},{9,11},{10,... | collective-permute-start | bytes 491528 | tf_op jit(solution)/shard_map/ppermute | solution.py:484
  18.6 8.4 %collective-permute-start.7 = (bf16[640,128]{1,0:T(8,128)(2,1)S(1)}, bf16[640,128]{1,0:T(8,128)(2,1)S(1)}, u32[]{:S(2)}, u32[]{:S(2)}) collective-permute-start(bf16[640,128]{1,0:T(8,128)(2,1)S(1)} %attend.1.token_ref.rest_0_), channel_id=1, source_target_pairs={{0,6},{1,7},{2,4},{3,5},{4,2},{5,3},{6,0},{7,1},{8,14},{9,15},{10,... | collective-permute-start | bytes 491528 | tf_op jit(solution)/shard_map/ppermute | solution.py:484
  20.1 5.0 %collective-permute-start.11 = (bf16[800,128]{1,0:T(8,128)(2,1)S(1)}, bf16[800,128]{1,0:T(8,128)(2,1)S(1)}, u32[]{:S(2)}, u32[]{:S(2)}) collective-permute-start(bf16[800,128]{1,0:T(8,128)(2,1)S(1)} %collective-permute-done.10.rest_10_), channel_id=1, source_target_pairs={{0,1},{1,0},{2,3},{3,2},{4,5},{5,4},{6,7},{7,6},{8,9},{9,8},{10,11... | collective-permute-start | bytes 614408 | tf_op jit(solution)/shard_map/ppermute | solution.py:484
  24.0 3.0 %collective-permute-start.14 = (bf16[640,128]{1,0:T(8,128)(2,1)S(1)}, bf16[640,128]{1,0:T(8,128)(2,1)S(1)}, u32[]{:S(2)}, u32[]{:S(2)}) collective-permute-start(bf16[640,128]{1,0:T(8,128)(2,1)S(1)} %attend.1.token_ref.rest_0_), channel_id=1, source_target_pairs={{0,1},{1,0},{2,3},{3,2},{4,5},{5,4},{6,7},{7,6},{8,9},{9,8},{10,11... | collective-permute-start | bytes 491528 | tf_op jit(solution)/shard_map/ppermute | solution.py:484
  24.9 2.1 %collective-permute-start.16 = (bf16[640,128]{1,0:T(8,128)(2,1)S(1)}, bf16[640,128]{1,0:T(8,128)(2,1)S(1)}, u32[]{:S(2)}, u32[]{:S(2)}) collective-permute-start(bf16[640,128]{1,0:T(8,128)(2,1)S(1)} %collective-permute-done.9.rest_2_), channel_id=1, source_target_pairs={{0,1},{1,0},{2,3},{3,2},{4,5},{5,4},{6,7},{7,6},{8,9},{9,8},{10,11... | collective-permute-start | bytes 491528 | tf_op jit(solution)/shard_map/ppermute | solution.py:484
  25.3 1.8 %collective-permute-start.15 = (bf16[640,128]{1,0:T(8,128)(2,1)S(1)}, bf16[640,128]{1,0:T(8,128)(2,1)S(1)}, u32[]{:S(2)}, u32[]{:S(2)}) collective-permute-start(bf16[640,128]{1,0:T(8,128)(2,1)S(1)} %collective-permute-done.8.rest_1_), channel_id=1, source_target_pairs={{0,1},{1,0},{2,3},{3,2},{4,5},{5,4},{6,7},{7,6},{8,9},{9,8},{10,11... | collective-permute-start | bytes 491528 | tf_op jit(solution)/shard_map/ppermute | solution.py:484
  27.0 1.4 %collective-permute-start.13 = (bf16[640,128]{1,0:T(8,128)(2,1)S(1)}, bf16[640,128]{1,0:T(8,128)(2,1)S(1)}, u32[]{:S(2)}, u32[]{:S(2)}) collective-permute-start(bf16[640,128]{1,0:T(8,128)(2,1)S(1)} %collective-permute-done.7.rest_0_), channel_id=1, source_target_pairs={{0,1},{1,0},{2,3},{3,2},{4,5},{5,4},{6,7},{7,6},{8,9},{9,8},{10,11... | collective-permute-start | bytes 491528 | tf_op jit(solution)/shard_map/ppermute | solution.py:484
  28.9 6.4 %collective-permute-start.17 = (bf16[656,128]{1,0:T(8,128)(2,1)S(1)}, bf16[656,128]{1,0:T(8,128)(2,1)S(1)}, u32[]{:S(2)}, u32[]{:S(2)}) collective-permute-start(bf16[656,128]{1,0:T(8,128)(2,1)S(1)} %project.1.token_ref.rest_0_), channel_id=1, source_target_pairs={{0,4},{1,5},{2,6},{3,7},{4,0},{5,1},{6,2},{7,3},{8,12},{9,13},{10,... | collective-permute-start | bytes 503816 | tf_op jit(solution)/shard_map/ppermute | solution.py:484
  30.6 7.2 %collective-permute-start.18 = (bf16[656,128]{1,0:T(8,128)(2,1)S(1)}, bf16[656,128]{1,0:T(8,128)(2,1)S(1)}, u32[]{:S(2)}, u32[]{:S(2)}) collective-permute-start(bf16[656,128]{1,0:T(8,128)(2,1)S(1)} %project.1.token_ref.rest_0_), channel_id=1, source_target_pairs={{0,2},{1,3},{2,0},{3,1},{4,6},{5,7},{6,4},{7,5},{8,10},{9,11},{10,... | collective-permute-start | bytes 503816 | tf_op jit(solution)/shard_map/ppermute | solution.py:484
  31.0 9.1 %collective-permute-start.22 = (bf16[656,128]{1,0:T(8,128)(2,1)S(1)}, bf16[656,128]{1,0:T(8,128)(2,1)S(1)}, u32[]{:S(2)}, u32[]{:S(2)}) collective-permute-start(bf16[656,128]{1,0:T(8,128)(2,1)S(1)} %project.1.token_ref.rest_0_), channel_id=1, source_target_pairs={{0,6},{1,7},{2,4},{3,5},{4,2},{5,3},{6,0},{7,1},{8,14},{9,15},{10,... | collective-permute-start | bytes 503816 | tf_op jit(solution)/shard_map/ppermute | solution.py:484
  33.8 5.2 %collective-permute-start.19 = (bf16[656,128]{1,0:T(8,128)(2,1)S(1)}, bf16[656,128]{1,0:T(8,128)(2,1)S(1)}, u32[]{:S(2)}, u32[]{:S(2)}) collective-permute-start(bf16[656,128]{1,0:T(8,128)(2,1)S(1)} %project.1.token_ref.rest_0_), channel_id=1, source_target_pairs={{0,1},{1,0},{2,3},{3,2},{4,5},{5,4},{6,7},{7,6},{8,9},{9,8},{10,11... | collective-permute-start | bytes 503816 | tf_op jit(solution)/shard_map/ppermute | solution.py:484
  35.3 4.8 %collective-permute-start.20 = (bf16[656,128]{1,0:T(8,128)(2,1)S(1)}, bf16[656,128]{1,0:T(8,128)(2,1)S(1)}, u32[]{:S(2)}, u32[]{:S(2)}) collective-permute-start(bf16[656,128]{1,0:T(8,128)(2,1)S(1)} %collective-permute-done.17.rest_1_), channel_id=1, source_target_pairs={{0,1},{1,0},{2,3},{3,2},{4,5},{5,4},{6,7},{7,6},{8,9},{9,8},{10,11... | collective-permute-start | bytes 503816 | tf_op jit(solution)/shard_map/ppermute | solution.py:484
  37.8 2.3 %collective-permute-start.21 = (bf16[656,128]{1,0:T(8,128)(2,1)S(1)}, bf16[656,128]{1,0:T(8,128)(2,1)S(1)}, u32[]{:S(2)}, u32[]{:S(2)}) collective-permute-start(bf16[656,128]{1,0:T(8,128)(2,1)S(1)} %collective-permute-done.18.rest_2_), channel_id=1, source_target_pairs={{0,1},{1,0},{2,3},{3,2},{4,5},{5,4},{6,7},{7,6},{8,9},{9,8},{10,11... | collective-permute-start | bytes 503816 | tf_op jit(solution)/shard_map/ppermute | solution.py:484
  40.0 1.4 %collective-permute-start.23 = (bf16[656,128]{1,0:T(8,128)(2,1)S(1)}, bf16[656,128]{1,0:T(8,128)(2,1)S(1)}, u32[]{:S(2)}, u32[]{:S(2)}) collective-permute-start(bf16[656,128]{1,0:T(8,128)(2,1)S(1)} %collective-permute-done.22.rest_6_), channel_id=1, source_target_pairs={{0,1},{1,0},{2,3},{3,2},{4,5},{5,4},{6,7},{7,6},{8,9},{9,8},{10,11... | collective-permute-start | bytes 503816 | tf_op jit(solution)/shard_map/ppermute | solution.py:484
  (2 other events, 12.9 us)
